TPU v7x, 32 devices: a whole 2x2x4 slice. The times are simulated.
32 devices in a mesh: group: 2 (over x), span: 4 (over y, core), tensor: 4 (over z).
Axes of the slice: x: 2, y: 2, z: 4, core: 2. Of those that a mesh axis runs over, the one named last changes fastest.
Arguments:
- queries: bfloat16 [3072, 3072], P(('group', 'span'), 'tensor'), parts along dimension 0, may hold values from -96 to 96
- keys: bfloat16 [3072, 3072], P(('group', 'span'), 'tensor'), parts along dimension 0, may hold values from -4 to 4
- values: bfloat16 [3072, 3072], P(('group', 'span'), 'tensor'), parts along dimension 0, may hold values from -6 to 6
- out_weight: bfloat16 [3072, 6144], P('tensor'), may hold values from -2 to 2
- gate_table: float32 [64, 6144], replicated, may hold values from 0.5 to 1.5
- levels: int32 [8], P('group'), parts along dimension 0, may hold values from 0 to 63
- visible: int32 [8, 4], P('group'), parts along dimension 0, may hold values from 0 to 1, as said below
Outputs:
- gated_output: bfloat16 [3072, 6144], P(('group', 'span', 'tensor')), parts along dimension 0
There are 2 independent parts, one for each index of `group`. A program takes and returns all parts, laid end to end along the dimension named above; an argument that names none is the same for every part. Nothing has to cross between parts.
Inputs may be any that keep to these rules, and one draw needn't show every extreme that they name: visible[c, c] = 1 and visible[c, j] = 0 for j > c.
All inputs are finite; a program needn't handle non-finite values.
Results may differ from a plain program's by a relative error of at most 0.013.
Values may be sent and summed in bfloat16 or wider, within the bound.
No kernel may reach another device: no remote copies, remote signals or barrier semaphores. Data moves between devices by JAX's collectives and lax.ppermute only.
A program may use at most 64 MiB of HBM per device.

v0:
```python
import jax
import jax.numpy as jnp
from jax import lax
from jax.sharding import PartitionSpec as P

HD = 128


def passed_along(block, axis, distance):
    devices = range(lax.axis_size(axis))
    route = [(i - distance, i) for i in devices if i - distance in devices]
    return lax.ppermute(block, axis, route)


def body(queries, keys, values, out_weight, gate_table, levels, visible):
    rows, width = queries.shape
    heads = width // HD
    scale = HD ** (-0.5)
    span_index = lax.axis_index("span")
    span_count = lax.axis_size("span")
    numbers = jnp.arange(visible.shape[0], dtype=jnp.int32)
    vis_row = jnp.sum(jnp.where(numbers[:, None] == span_index, visible, 0), axis=0)
    level = jnp.sum(jnp.where(numbers == span_index, levels, 0))
    level_hot = (jnp.arange(gate_table.shape[0], dtype=jnp.int32) == level).astype(jnp.float32)
    gate_row = jnp.dot(level_hot, gate_table, precision=lax.Precision.HIGHEST)
    query_heads = queries.reshape(rows, heads, HD)

    def attend(state, stacked, allowed):
        running, total, accum = state
        key_heads = stacked[0].reshape(-1, heads, HD)
        value_heads = stacked[1].reshape(-1, heads, HD)
        scores = (
            jnp.einsum("qhd,khd->hqk", query_heads, key_heads, preferred_element_type=jnp.float32)
            * scale
        )
        scores = jnp.where(allowed[None, None, :], scores, -jnp.inf)
        top = jnp.maximum(running, jnp.max(scores, axis=-1))
        safe_top = jnp.where(jnp.isfinite(top), top, 0.0)
        shrink = jnp.exp(running - safe_top)
        probs = jnp.exp(scores - safe_top[:, :, None])
        total = total * shrink + jnp.sum(probs, axis=-1)
        product = jnp.einsum(
            "hqk,khd->qhd",
            probs.astype(jnp.bfloat16),
            value_heads,
            preferred_element_type=jnp.float32,
        )
        accum = accum * jnp.transpose(shrink)[:, :, None] + product
        return (top, total, accum)

    start_state = (
        jnp.full((heads, rows), -jnp.inf, jnp.float32),
        jnp.zeros((heads, rows), jnp.float32),
        jnp.zeros((rows, heads, HD), jnp.float32),
    )
    stacked_own = jnp.stack([keys, values])
    every_row = jnp.ones((rows,), jnp.bool_)
    first_state = attend(start_state, stacked_own, every_row)

    def step_body(step, carry):
        held, state = carry
        held = passed_along(held, "span", 1)
        source = span_index - step
        seen = jnp.sum(jnp.where(numbers == source, vis_row, 0)) > 0
        flag = jnp.logical_and(source >= 0, seen)
        state = lax.cond(flag, lambda st: attend(st, held, every_row), lambda st: st, state)
        return (held, state)

    final_held, final_state = lax.fori_loop(1, span_count, step_body, (stacked_own, first_state))
    running, total, accum = final_state
    attended = (accum / jnp.transpose(total)[:, :, None]).astype(jnp.bfloat16).reshape(rows, width)
    summed = lax.psum_scatter(
        jnp.dot(attended, out_weight, preferred_element_type=jnp.float32).astype(jnp.bfloat16),
        "tensor",
        scatter_dimension=0,
        tiled=True,
    ).astype(jnp.float32)
    return (summed * gate_row[None, :]).astype(jnp.bfloat16)


def solution(mesh):
    return jax.shard_map(
        body,
        mesh=mesh,
        in_specs=(
            P(("group", "span"), "tensor"),
            P(("group", "span"), "tensor"),
            P(("group", "span"), "tensor"),
            P("tensor", None),
            P(),
            P("group"),
            P("group", None),
        ),
        out_specs=P(("group", "span", "tensor"), None),
        check_vma=False,
    )
```

profile of v0, /device:TPU:14, one launch (start us, length us, event | category | flops | bytes accessed | tf_op | source)
XLA Modules:
  0.0 193.2 jit_solution(4619279401151702539)
XLA Ops:
  6.5 0.0 copy-start
  6.5 1.5 copy.17
  8.0 1.4 copy.15
  9.4 2.4 %multiply_reduce_fusion.1 = (f32[6,384]{1,0:T(8,128)S(1)}, f32[6,384,384]{1,2,0:T(8,128)}) fusion(bf16[384,6,128]{0,2,1:T(8,128)(2,1)S(1)} %bitcast.36, bf16[384,6,128]{0,2,1:T(8,128)(2,1)S(1)} %bitcast.38), kind=kOutput, calls=%fused_computation.19 | convolution fusion | flops 228259584 | bytes 4727808 | tf_op jit(solution)/shard_map/qhd,khd->hqk/dot_general | solution.py:33
  11.9 0.3 copy.24
  12.2 1.4 copy.16
  13.6 2.6 %fusion.18 = f32[6,384]{1,0:T(8,128)S(1)} fusion(f32[6,384,384]{1,2,0:T(8,128)} %get-tuple-element.244, f32[6,384]{1,0:T(8,128)S(1)} %is-finite_select_fusion.2), kind=kLoop, calls=%fused_computation.21 | loop fusion | flops 2651904 | bytes 3557376 | tf_op jit(solution)/shard_map/reduce_sum | solution.py:41
  16.2 4.1 %fusion.26 = f32[384,6,128]{2,0,1:T(8,128)} fusion(bf16[384,6,128]{0,2,1:T(8,128)(2,1)S(1)} %bitcast.40, f32[6,384,384]{1,2,0:T(8,128)} %get-tuple-element.244, f32[6,384]{1,0:T(8,128)S(1)} %is-finite_select_fusion.2, f32[384,6]{0,1:T(8,128)S(1)} %fusion.31), kind=kOutput, calls=%fused_computation.27 | convolution fusion | flops 229441536 | bytes 5326848 | tf_op jit(solution)/shard_map/hqk,khd->qhd/dot_general | solution.py:42
  20.3 1.1 pad_maximum_fusion
  21.4 0.1 select_reduce_fusion
  21.5 64.9 %while.20 = (s32[]{:T(128)}, bf16[2,384,768]{1,2,0:T(8,128)(2,1)}, f32[6,384]{1,0:T(8,128)S(1)}, f32[6,384]{1,0:T(8,128)S(1)}, f32[384,6,128]{2,0,1:T(8,128)}, /...) while((s32[]{:T(128)}, bf16[2,384,768]{1,2,0:T(8,128)(2,1)}, ...), condition=%wide.region_9.10_spmd.clone, body=%wide.region_3.9_spmd.clone.sunk | while | flops 460673312 | bytes 33786208 | solution.py:69
  21.5 1.9 collective-permute-start
  23.5 0.6 fusion.49
  24.6 14.6 %collective-permute-done = bf16[2,384,768]{1,2,0:T(8,128)(2,1)S(1)} collective-permute-done((bf16[2,384,768]{1,2,0:T(8,128)(2,1)}, bf16[2,384,768]{1,2,0:T(8,128)(2,1)S(1)}, u32[]{:S(2)}, u32[]{:S(2)}) %collective-permute-start) | collective-permute-done | bytes 1179680 | tf_op jit(solution)/shard_map/while/body/eval_jaxpr/ppermute | solution.py:12
  39.3 4.3 %conditional.3 = ((f32[6,384]{1,0:T(8,128)S(1)}, f32[6,384]{1,0:T(8,128)S(1)}, f32[384,6,128]{2,0,1:T(8,128)})) conditional(s32[]{:T(128)} %convert_element_type.49, (f32[6,384]{1,0:T(8,128)S(1)}, f32[6,384]{1,0:T(8,128)S(1)}, f32[384,6,128]{2,0,1:T(8,128)}) %tuple.47, (bf16[2,384,768]{1,2,0:T(8,128)(2,1)S(1)}, bf16[384,6,128]{2,0,1:T(8,128)(2,1)S(1)}, ...), branch_computations={%region_5.5_spmd, %region_6.8_spmd} | conditional | flops 460673280 | bytes 26708056 | solution.py:66
  39.3 0.1 fusion.38
  39.4 0.7 multiply_reduce_fusion
  40.1 0.0 copy-start.1
  40.1 0.6 fusion.3
  40.7 0.6 copy-done.1
  41.3 1.2 fusion.11
  42.6 1.0 copy-done.2
  43.6 1.0 copy.50
  44.6 1.9 collective-permute-start
  46.5 0.6 fusion.49
  47.7 14.6 %collective-permute-done = bf16[2,384,768]{1,2,0:T(8,128)(2,1)S(1)} collective-permute-done((bf16[2,384,768]{1,2,0:T(8,128)(2,1)}, bf16[2,384,768]{1,2,0:T(8,128)(2,1)S(1)}, u32[]{:S(2)}, u32[]{:S(2)}) %collective-permute-start) | collective-permute-done | bytes 1179680 | tf_op jit(solution)/shard_map/while/body/eval_jaxpr/ppermute | solution.py:12
  62.3 4.3 %conditional.3 = ((f32[6,384]{1,0:T(8,128)S(1)}, f32[6,384]{1,0:T(8,128)S(1)}, f32[384,6,128]{2,0,1:T(8,128)})) conditional(s32[]{:T(128)} %convert_element_type.49, (f32[6,384]{1,0:T(8,128)S(1)}, f32[6,384]{1,0:T(8,128)S(1)}, f32[384,6,128]{2,0,1:T(8,128)}) %tuple.47, (bf16[2,384,768]{1,2,0:T(8,128)(2,1)S(1)}, bf16[384,6,128]{2,0,1:T(8,128)(2,1)S(1)}, ...), branch_computations={%region_5.5_spmd, %region_6.8_spmd} | conditional | flops 460673280 | bytes 26708056 | solution.py:66
  62.3 0.1 fusion.38
  62.4 0.7 multiply_reduce_fusion
  63.1 0.0 copy-start.1
  63.2 0.6 fusion.3
  63.8 0.6 copy-done.1
  64.4 1.2 fusion.11
  65.7 1.0 copy-done.2
  66.6 1.0 copy.50
  67.7 1.9 collective-permute-start
  69.6 0.6 fusion.49
  70.7 14.6 %collective-permute-done = bf16[2,384,768]{1,2,0:T(8,128)(2,1)S(1)} collective-permute-done((bf16[2,384,768]{1,2,0:T(8,128)(2,1)}, bf16[2,384,768]{1,2,0:T(8,128)(2,1)S(1)}, u32[]{:S(2)}, u32[]{:S(2)}) %collective-permute-start) | collective-permute-done | bytes 1179680 | tf_op jit(solution)/shard_map/while/body/eval_jaxpr/ppermute | solution.py:12
  85.4 1.0 copy.50
  86.4 1.6 copy.25
  88.0 0.1 divide_convert_fusion
  88.1 9.2 %convolution_convert_fusion = bf16[384,6144]{1,0:T(8,128)(2,1)} fusion(bf16[384,768]{0,1:T(8,128)(2,1)S(1)} %bitcast.42, bf16[768,6144]{1,0:T(8,128)(2,1)} %param.14), kind=kOutput, calls=%fused_computation.17 | convolution fusion | flops 3626237952 | bytes 14745600 | tf_op jit(solution)/shard_map/dot_general | solution.py:73
  97.4 0.0 reduce-scatter.2.cloned.1.call-update
  97.4 0.6 copy-done.4
  98.0 0.6 select_reduce_fusion.1
  98.7 1.3 fusion.32
  99.9 84.0 %reduce-scatter.2.cloned.1.call-done = bf16[96,6144]{1,0:T(8,128)(2,1)} async-done(((bf16[384,6144]{1,0:T(8,128)(2,1)}), bf16[96,6144]{1,0:T(8,128)(2,1)}) %reduce-scatter.2.cloned.1.call-update) | async-done | bytes 1179664 | tf_op jit(solution)/shard_map/reduce_scatter | solution.py:72
  183.9 2.5 %multiply_convert_fusion = bf16[96,6144]{1,0:T(8,128)(2,1)} fusion(bf16[96,6144]{1,0:T(8,128)(2,1)} %reduce-scatter.2.cloned.1.call-done, f32[6144]{0:T(1024)S(1)} %bitcast.44), kind=kLoop, calls=%fused_computation.22 | loop fusion | flops 1769472 | bytes 2383872 | tf_op jit(solution)/shard_map/convert_element_type | solution.py:78
  (20 shorter events, 0.1 us)
Async XLA Ops:
  6.5 92.1 %copy-start = (f32[64,6144]{1,0:T(8,128)S(1)}, f32[64,6144]{1,0:T(8,128)}, u32[]{:S(2)}) copy-start(f32[64,6144]{1,0:T(8,128)} %param.15) | copy-start | bytes 4718596
  6.5 177.4 %reduce-scatter.2.cloned.1.call-start = ((), (), s32[]{:S(2)}) async-start(), calls=%async_computation.1 | async-start | bytes 5898240 | tf_op jit(solution)/shard_map/reduce_scatter | solution.py:72
  20.3 1.2 copy-start.3
  21.5 17.7 %collective-permute-start = (bf16[2,384,768]{1,2,0:T(8,128)(2,1)}, bf16[2,384,768]{1,2,0:T(8,128)(2,1)S(1)}, u32[]{:S(2)}, u32[]{:S(2)}) collective-permute-start(bf16[2,384,768]{1,2,0:T(8,128)(2,1)} %get-tuple-element.317), channel_id=1, source_target_pairs={{0,4},{4,8},{8,12},{1,5},{5,9},{9,13},{2,6},{6,10},{10,14},{3,7},{... | collective-permute-start | bytes 3538952 | tf_op jit(solution)/shard_map/while/body/eval_jaxpr/ppermute | solution.py:12
  40.1 1.3 copy-start.1
  42.6 1.0 copy-start.2
  44.6 17.7 %collective-permute-start = (bf16[2,384,768]{1,2,0:T(8,128)(2,1)}, bf16[2,384,768]{1,2,0:T(8,128)(2,1)S(1)}, u32[]{:S(2)}, u32[]{:S(2)}) collective-permute-start(bf16[2,384,768]{1,2,0:T(8,128)(2,1)} %get-tuple-element.317), channel_id=1, source_target_pairs={{0,4},{4,8},{8,12},{1,5},{5,9},{9,13},{2,6},{6,10},{10,14},{3,7},{... | collective-permute-start | bytes 3538952 | tf_op jit(solution)/shard_map/while/body/eval_jaxpr/ppermute | solution.py:12
  63.1 1.3 copy-start.1
  65.6 1.0 copy-start.2
  67.7 17.7 %collective-permute-start = (bf16[2,384,768]{1,2,0:T(8,128)(2,1)}, bf16[2,384,768]{1,2,0:T(8,128)(2,1)S(1)}, u32[]{:S(2)}, u32[]{:S(2)}) collective-permute-start(bf16[2,384,768]{1,2,0:T(8,128)(2,1)} %get-tuple-element.317), channel_id=1, source_target_pairs={{0,4},{4,8},{8,12},{1,5},{5,9},{9,13},{2,6},{6,10},{10,14},{3,7},{... | collective-permute-start | bytes 3538952 | tf_op jit(solution)/shard_map/while/body/eval_jaxpr/ppermute | solution.py:12
  97.4 0.7 copy-start.4
Sparse Core Ops, SparseCore 0:
  97.5 86.3 reduce-scatter.1
where the time goes:
time: 195 us; the launch traced here: 193 us
  waiting for transfers between devices  128 us (66%)
  matrix products  20.8 us (11%)
  between operations  13.5 us (7%)
  local copies, waits for them, and re-layouts  13.3 us (7%)
  other arithmetic  10.1 us (5%)
  starting transfers between devices  5.73 us (3%)
    reduce_scatter x1, waiting for transfers between devices, body(): lax.psum_scatter(jnp.dot(attended, out_weight, preferred_element_type=jnp...  84 us
    ppermute x3, waiting for transfers between devices, passed_along(): return lax.ppermute(block, axis, route)  43.9 us
    dot_general x1, matrix products, body(): jnp.dot(attended, out_weight, preferred_element_type=jnp.float32)  9.22 us
    dot_general x3, matrix products, attend(): jnp.einsum('hqk,khd->qhd', probs.astype(jnp.bfloat16), value_heads, prefe...  6.55 us
    ppermute x3, starting transfers between devices, passed_along(): return lax.ppermute(block, axis, route)  5.72 us
    unnamed x10, local copies, waits for them, and re-layouts  5.22 us
  transfers between devices with their start and end apart: 4, of which 4 were waited for; matrix products, arithmetic and copies ran while one was open for 2% of the time, Pallas kernels for 0%

commit v1 on v0

v1 whole, which is shorter than its diff:
```python
import functools

import jax
import jax.numpy as jnp
from jax import lax
from jax.experimental import pallas as pl
from jax.experimental.pallas import tpu as pltpu
from jax.sharding import PartitionSpec as P

HD = 128
LANES = 128
HIDDEN = -1e30
LOG2E = 1.4426950408889634
VMEM_BYTES = 48 * 1024 * 1024
PARAMS = pltpu.CompilerParams(vmem_limit_bytes=VMEM_BYTES)
SMEM = pl.BlockSpec(memory_space=pltpu.SMEM)
VMEM = pl.BlockSpec(memory_space=pltpu.VMEM)


def cost(flops, moved, exps=0):
    return pl.CostEstimate(flops=int(flops), bytes_accessed=int(moved), transcendentals=int(exps))


def shifted(block, axis, distance):
    count = lax.axis_size(axis)
    return lax.ppermute(block, axis, [(i, i + distance) for i in range(count) if 0 <= i + distance < count])


def head_columns(head):
    return slice(head * HD, (head + 1) * HD)


def attend_head(query, keys, values, biases):
    scale = LOG2E * HD ** (-0.5)
    scores = [
        lax.dot_general(query, key, (((1,), (1,)), ((), ())), preferred_element_type=jnp.float32) * scale + bias
        for key, bias in zip(keys, biases)
    ]
    tops = [jnp.max(block, axis=-1, keepdims=True) for block in scores]
    top = functools.reduce(jnp.maximum, tops)
    probs = [jnp.exp2(block - top) for block in scores]
    total = sum(jnp.sum(block, axis=-1, keepdims=True) for block in probs)
    product = sum(
        jnp.dot(block.astype(jnp.bfloat16), value, preferred_element_type=jnp.float32)
        for block, value in zip(probs, values)
    )
    return product / total, top + jnp.log2(total)


def bias_of(flag):
    return jnp.where(flag, 0.0, HIDDEN).astype(jnp.float32)


def local_kernel(place, visible, query_outer, query_inner, key, value, key_beside, value_beside,
                 outer, outer_sum, inner, inner_sum):
    span = place[0]
    beside = span + 1 - 2 * lax.rem(span, 2)
    biases = [jnp.float32(0.0), bias_of(visible[span, beside] > 0)]
    for query, result, sums in ((query_outer, outer, outer_sum), (query_inner, inner, inner_sum)):
        rows, width = query.shape
        lane = lax.broadcasted_iota(jnp.int32, (rows, LANES), 1)
        packed = jnp.zeros((rows, LANES), jnp.float32)
        for head in range(width // HD):
            columns = head_columns(head)
            product, logsum = attend_head(
                query[:, columns],
                [key[:, columns], key_beside[:, columns]],
                [value[:, columns], value_beside[:, columns]],
                biases,
            )
            result[:, columns] = product
            packed = jnp.where(lane == head, logsum, packed)
        sums[...] = packed


def served_kernel(distance, place, visible, query, key, value, key_beside, value_beside, result):
    span = place[0]
    beside = span + 1 - 2 * lax.rem(span, 2)
    asker = jnp.minimum(span + distance, visible.shape[0] - 1)
    biases = [bias_of(visible[asker, span] > 0), bias_of(visible[asker, beside] > 0)]
    rows, width = query.shape
    lane = lax.broadcasted_iota(jnp.int32, (rows, LANES), 1)
    packed = jnp.zeros((rows, LANES), jnp.float32)
    for head in range(width // HD):
        columns = head_columns(head)
        product, logsum = attend_head(
            query[:, columns],
            [key[:, columns], key_beside[:, columns]],
            [value[:, columns], value_beside[:, columns]],
            biases,
        )
        result[:, columns] = product.astype(jnp.bfloat16)
        for piece in range(3):
            part = logsum.astype(jnp.bfloat16).astype(jnp.float32)
            packed = jnp.where(lane == 3 * head + piece, part, packed)
            logsum = logsum - part
    result[:, width:] = packed.astype(jnp.bfloat16)


def merge_kernel(distances, place, own, own_sum, *refs):
    served, result = refs[:-1], refs[-1]
    width = own.shape[1]
    span = place[0]
    logs = own_sum[...]
    away = [ref[:, width:].astype(jnp.float32) for ref in served]
    for head in range(width // HD):
        columns = head_columns(head)
        sums = [logs[:, head:head + 1]]
        for distance, pieces in zip(distances, away):
            at = 3 * head
            joined = pieces[:, at:at + 1] + pieces[:, at + 1:at + 2] + pieces[:, at + 2:at + 3]
            sums.append(jnp.where(span >= distance, joined, HIDDEN))
        top = functools.reduce(jnp.maximum, sums)
        shares = [jnp.exp2(one - top) for one in sums]
        total = sum(shares)
        merged = own[:, columns] * (shares[0] / total)
        for share, ref in zip(shares[1:], served):
            merged = merged + ref[:, columns].astype(jnp.float32) * (share / total)
        result[:, columns] = merged.astype(jnp.bfloat16)


def message_kernel(blocks, up_rows, down_rows, weight, *refs):
    ups, downs = refs[-2:]
    rows = up_rows.shape[0]
    both = jnp.concatenate([up_rows[...], down_rows[...]], axis=0)
    product = jnp.dot(both, weight[...], preferred_element_type=jnp.float32)
    up, down = product[:rows], product[rows:]
    if len(refs) == 4:
        up = up + refs[0][...].astype(jnp.float32)
        down = down + refs[1][...].astype(jnp.float32)
    ups[...] = up.astype(jnp.bfloat16)
    downs[...] = down.astype(jnp.bfloat16)


def message(blocks, attended, weight, arrived, first, columns, rows, tile):
    width = attended.shape[1]
    start = first // tile
    piece = pl.BlockSpec((rows, tile), lambda j, b: (0, j))
    return pl.pallas_call(
        message_kernel,
        grid_spec=pltpu.PrefetchScalarGridSpec(
            num_scalar_prefetch=1,
            grid=(columns // tile,),
            in_specs=[
                pl.BlockSpec((rows, width), lambda j, b: (b[0], 0)),
                pl.BlockSpec((rows, width), lambda j, b: (b[1], 0)),
                pl.BlockSpec((width, tile), lambda j, b: (0, start + j)),
            ] + [piece] * len(arrived),
            out_specs=[piece, piece],
        ),
        out_shape=[jax.ShapeDtypeStruct((rows, columns), jnp.bfloat16)] * 2,
        compiler_params=PARAMS,
        cost_estimate=cost(4 * rows * width * columns, 2 * width * columns + 8 * rows * columns),
        name="message",
    )(blocks, attended, attended, weight, *arrived)


def final_kernel(blocks, own_rows, weight, gate, up, down, result):
    product = jnp.dot(own_rows[...], weight[...], preferred_element_type=jnp.float32)
    summed = product + up[...].astype(jnp.float32) + down[...].astype(jnp.float32)
    result[...] = (summed * gate[pl.ds(lax.rem(blocks[1], 8), 1), :]).astype(jnp.bfloat16)


def final(blocks, attended, weight, gate_table, up, down, first, columns, rows, tile):
    width = attended.shape[1]
    start = first // tile
    piece = pl.BlockSpec((rows, tile), lambda j, b: (0, j))
    return pl.pallas_call(
        final_kernel,
        grid_spec=pltpu.PrefetchScalarGridSpec(
            num_scalar_prefetch=1,
            grid=(columns // tile,),
            in_specs=[
                pl.BlockSpec((rows, width), lambda j, b: (b[0], 0)),
                pl.BlockSpec((width, tile), lambda j, b: (0, start + j)),
                pl.BlockSpec((8, tile), lambda j, b: (b[1] // 8, start + j)),
                piece,
                piece,
            ],
            out_specs=piece,
        ),
        out_shape=jax.ShapeDtypeStruct((rows, columns), jnp.bfloat16),
        compiler_params=PARAMS,
        cost_estimate=cost(2 * rows * width * columns, 2 * width * columns + 10 * rows * columns),
        name="final",
    )(blocks, attended, weight, gate_table, up, down)


def body(queries, keys, values, out_weight, gate_table, levels, visible):
    rows, width = queries.shape
    model = out_weight.shape[1]
    spans = lax.axis_size("span")
    ranks = lax.axis_size("tensor")
    span = lax.axis_index("span")
    rank = lax.axis_index("tensor")
    block = rows // ranks
    quarter = rows // 4
    half = 2 * quarter
    place = jnp.stack([span, rank]).astype(jnp.int32)
    level = levels[span]

    query_outer = jnp.concatenate([queries[:quarter], queries[rows - quarter:]])
    query_inner = queries[quarter:rows - quarter]
    distances = list(range(2, spans, 2))
    asked_outer = [shifted(query_outer, "span", -distance) for distance in distances]
    swap = [(i, i + 1 - 2 * (i % 2)) for i in range(spans)]
    key_beside = lax.ppermute(keys, "span", swap)
    value_beside = lax.ppermute(values, "span", swap)
    asked_inner = [shifted(query_inner, "span", -distance) for distance in distances]

    def served(asked, distance):
        return pl.pallas_call(
            functools.partial(served_kernel, distance),
            in_specs=[SMEM, SMEM] + [VMEM] * 5,
            out_specs=VMEM,
            out_shape=jax.ShapeDtypeStruct((half, width + LANES), jnp.bfloat16),
            compiler_params=PARAMS,
            cost_estimate=cost(8 * half * rows * width, 12 * rows * width, 2 * half * rows * width // HD),
            name="served",
        )(place, visible, asked, keys, values, key_beside, value_beside)

    back_outer = [shifted(served(q, d), "span", d) for q, d in zip(asked_outer, distances)]
    local_shapes = [
        jax.ShapeDtypeStruct((half, width), jnp.float32),
        jax.ShapeDtypeStruct((half, LANES), jnp.float32),
    ] * 2
    outer, outer_sum, inner, inner_sum = pl.pallas_call(
        local_kernel,
        in_specs=[SMEM, SMEM] + [VMEM] * 6,
        out_specs=[VMEM] * 4,
        out_shape=local_shapes,
        compiler_params=PARAMS,
        cost_estimate=cost(16 * half * rows * width, 14 * rows * width, 4 * half * rows * width // HD),
        name="local",
    )(place, visible, query_outer, query_inner, keys, values, key_beside, value_beside)
    back_inner = [shifted(served(q, d), "span", d) for q, d in zip(asked_inner, distances)]

    def merge(own, own_sum, back):
        return pl.pallas_call(
            functools.partial(merge_kernel, distances),
            in_specs=[SMEM] + [VMEM] * (2 + len(back)),
            out_specs=VMEM,
            out_shape=jax.ShapeDtypeStruct((half, width), jnp.bfloat16),
            compiler_params=PARAMS,
            cost_estimate=cost(8 * half * width, 10 * half * width),
            name="merge",
        )(place, own, own_sum, *back)

    attended_outer = merge(outer, outer_sum, back_outer)
    attended_inner = merge(inner, inner_sum, back_inner)
    attended = jnp.concatenate([attended_outer[:quarter], attended_inner, attended_outer[quarter:]])

    chunks = 2
    columns = model // chunks
    tile = 512 if columns % 512 == 0 else columns
    last = ranks - 1
    arrived = [()] * chunks
    for step in range(last):
        if step == 0:
            source, blocks = attended_outer, jnp.array([half // block - 1, 0], jnp.int32)
        else:
            source = attended
            blocks = jnp.stack([jnp.minimum(last - step + rank, last), jnp.maximum(step + rank - last, 0)])
        for chunk in range(chunks):
            up, down = message(
                blocks, source, out_weight, arrived[chunk], chunk * columns, columns, block, tile
            )
            up = lax.ppermute(up, "tensor", [(i, i + 1) for i in range(step + 1)])
            down = lax.ppermute(down, "tensor", [(last - i, last - i - 1) for i in range(step + 1)])
            arrived[chunk] = (up, down)
    blocks = jnp.stack([rank, level])
    return jnp.concatenate([
        final(blocks, attended, out_weight, gate_table, *arrived[chunk], chunk * columns, columns, block, tile)
        for chunk in range(chunks)
    ], axis=1)


def solution(mesh):
    return jax.shard_map(
        body,
        mesh=mesh,
        in_specs=(
            P(("group", "span"), "tensor"),
            P(("group", "span"), "tensor"),
            P(("group", "span"), "tensor"),
            P("tensor", None),
            P(),
            P("group"),
            P("group", None),
        ),
        out_specs=P(("group", "span", "tensor"), None),
        check_vma=False,
    )
```

time: 195 us -> 128 us (0.66)
  the two profiles are of different devices: /device:TPU:14 before, /device:TPU:0 now
where the time goes in v1:
time: 128 us; the launch traced here: 126 us
  Pallas kernels  66.5 us (52%)
  starting transfers between devices  36.6 us (29%)
  waiting for transfers between devices  18.1 us (14%)
  local copies, waits for them, and re-layouts  2.67 us (2%)
  other arithmetic  2.08 us (2%)
    pallas_call x6, Pallas kernels, message(): pl.pallas_call(message_kernel, grid_spec=pltpu.PrefetchScalarGridSpec(num...  38.7 us
    ppermute x6, starting transfers between devices, body(): up = lax.ppermute(up, 'tensor', [(i, i + 1) for i in range(step + 1)])  23.1 us
    pallas_call x2, Pallas kernels, final(): pl.pallas_call(final_kernel, grid_spec=pltpu.PrefetchScalarGridSpec(num_s...  10.5 us
    ppermute x4, waiting for transfers between devices, shifted(): lax.ppermute(block, axis, [(i, i + distance) for i in range(count) if 0 <...  9.15 us
    ppermute x6, waiting for transfers between devices, body(): up = lax.ppermute(up, 'tensor', [(i, i + 1) for i in range(step + 1)])  8.03 us
    pallas_call x2, Pallas kernels, served(): pl.pallas_call(functools.partial(served_kernel, distance), in_specs=[SMEM...  7.11 us
    ppermute x6, starting transfers between devices, body(): lax.ppermute(down, 'tensor', [(last - i, last - i - 1) for i in range(ste...  6.6 us
    ppermute x4, starting transfers between devices, shifted(): lax.ppermute(block, axis, [(i, i + distance) for i in range(count) if 0 <...  6.25 us
  transfers between devices with their start and end apart: 18, of which 8 were waited for; matrix products, arithmetic and copies ran while one was open for 3% of the time, Pallas kernels for 48%

profile of v1, /device:TPU:0, one launch (start us, length us, event | category | flops | bytes accessed | tf_op | source)
XLA Modules:
  0.0 126.4 jit_solution(10444403504868901631)
XLA Ops:
  0.0 0.5 collective-permute-start
  0.5 0.1 collective-permute-start.1
  0.6 1.0 fusion
  1.7 1.3 %collective-permute-start.2 = (bf16[192,768]{1,0:T(8,128)(2,1)S(1)}, bf16[192,768]{1,0:T(8,128)(2,1)}, u32[]{:S(2)}, u32[]{:S(2)}) collective-permute-start(bf16[192,768]{1,0:T(8,128)(2,1)S(1)} %pad_maximum_fusion.2.query_outer), channel_id=1, source_target_pairs={{8,0},{12,4},{9,1},{13,5},{10,2},{14,6},{11,3},{15,7},{24,16},{28,... | collective-permute-start | bytes 884744 | tf_op jit(solution)/shard_map/ppermute | solution.py:26
  3.0 1.0 slice.17.query_inner
  3.9 1.3 %collective-permute-start.4 = (bf16[192,768]{1,0:T(8,128)(2,1)S(1)}, bf16[192,768]{1,0:T(8,128)(2,1)S(1)}, u32[]{:S(2)}, u32[]{:S(2)}) collective-permute-start(bf16[192,768]{1,0:T(8,128)(2,1)S(1)} %slice.17.query_inner), channel_id=1, source_target_pairs={{8,0},{12,4},{9,1},{13,5},{10,2},{14,6},{11,3},{15,7},{24,16},{28,... | collective-permute-start | bytes 884744 | tf_op jit(solution)/shard_map/ppermute | solution.py:26
  5.3 0.1 pad_add_fusion.1.place
  5.3 8.5 %collective-permute-done.2.query = bf16[192,768]{1,0:T(8,128)(2,1)} collective-permute-done((bf16[192,768]{1,0:T(8,128)(2,1)S(1)}, bf16[192,768]{1,0:T(8,128)(2,1)}, u32[]{:S(2)}, u32[]{:S(2)}) %collective-permute-start.2) | collective-permute-done | bytes 294944 | tf_op jit(solution)/shard_map/ppermute | solution.py:26
  13.8 3.4 %served.2 = bf16[192,896]{1,0:T(8,128)(2,1)S(1)} custom-call(s32[2]{0:T(128)S(1)} %pad_add_fusion.1.place, s32[4,4]{1,0:T(4,128)S(1)} %copy-done.9, bf16[192,768]{1,0:T(8,128)(2,1)} %collective-permute-done.2.query, bf16[384,768]{1,0:T(8,128)(2,1)S(1)} %copy-done.1, bf16[384,768]{1,0:T(8,128)(2,1)S(1)} %copy-done.2, ...), custom_call_target="tpu_custom_call" | custom-call | flops 452984832 | bytes 3538944 | tf_op jit(solution)/shard_map/served/pallas_call | solution.py:212
  17.2 1.5 %collective-permute-start.3 = (bf16[192,896]{1,0:T(8,128)(2,1)S(1)}, bf16[192,896]{1,0:T(8,128)(2,1)S(1)}, u32[]{:S(2)}, u32[]{:S(2)}) collective-permute-start(bf16[192,896]{1,0:T(8,128)(2,1)S(1)} %served.2), channel_id=1, source_target_pairs={{0,8},{4,12},{1,9},{5,13},{2,10},{6,14},{3,11},{7,15},{16,24},{20,... | collective-permute-start | bytes 1032200 | tf_op jit(solution)/shard_map/ppermute | solution.py:26
  18.7 0.7 collective-permute-done.4.query
  19.4 3.7 %served.3 = bf16[192,896]{1,0:T(8,128)(2,1)} custom-call(s32[2]{0:T(128)S(1)} %pad_add_fusion.1.place, s32[4,4]{1,0:T(4,128)S(1)} %copy-done.9, bf16[192,768]{1,0:T(8,128)(2,1)S(1)} %collective-permute-done.4.query, bf16[384,768]{1,0:T(8,128)(2,1)S(1)} %copy-done.1, bf16[384,768]{1,0:T(8,128)(2,1)S(1)} %copy-done.2, ...), custom_call_target="tpu_custom_call" | custom-call | flops 452984832 | bytes 3538944 | tf_op jit(solution)/shard_map/served/pallas_call | solution.py:212
  23.2 2.2 %collective-permute-start.5 = (bf16[192,896]{1,0:T(8,128)(2,1)}, bf16[192,896]{1,0:T(8,128)(2,1)}, u32[]{:S(2)}, u32[]{:S(2)}) collective-permute-start(bf16[192,896]{1,0:T(8,128)(2,1)} %served.3), channel_id=1, source_target_pairs={{0,8},{4,12},{1,9},{5,13},{2,10},{6,14},{3,11},{7,15},{16,24},{20,... | collective-permute-start | bytes 1032200 | tf_op jit(solution)/shard_map/ppermute | solution.py:26
  25.3 5.3 %local.1 = (f32[192,768]{1,0:T(8,128)S(1)}, f32[192,128]{1,0:T(8,128)S(1)}, f32[192,768]{1,0:T(8,128)S(1)}, f32[192,128]{1,0:T(8,128)S(1)}) custom-call(s32[2]{0:T(128)S(1)} %pad_add_fusion.1.place, s32[4,4]{1,0:T(4,128)S(1)} %copy-done.9, bf16[192,768]{1,0:T(8,128)(2,1)S(1)} %copy-done.4, bf16[192,768]{1,0:T(8,128)(2,1)S(1)} %copy-done.6, ...), custom_call_target="tpu_custom_call" | custom-call | flops 905969664 | bytes 4128768 | tf_op jit(solution)/shard_map/local/pallas_call | solution.py:227
  30.6 0.0 copy-start.10
  30.6 2.3 %merge.2.up_rows.down_rows = bf16[192,768]{1,0:T(8,128)(2,1)S(1)} custom-call(s32[2]{0:T(128)S(1)} %pad_add_fusion.1.place, f32[192,768]{1,0:T(8,128)S(1)} %get-tuple-element.21.own, f32[192,128]{1,0:T(8,128)S(1)} %get-tuple-element.22.own_sum, bf16[192,896]{1,0:T(8,128)(2,1)S(1)} %collective-permute-done.3.refs_0_), custom_call_target="tpu_custom_call" | custom-call | flops 1179648 | bytes 1474560 | tf_op jit(solution)/shard_map/merge/pallas_call | solution.py:239
  32.9 6.5 %message.6 = (bf16[96,3072]{1,0:T(8,128)(2,1)}, bf16[96,3072]{1,0:T(8,128)(2,1)}) custom-call(s32[2]{0:T(128)S(1)} %copy-done.10, bf16[192,768]{1,0:T(8,128)(2,1)S(1)} %merge.2.up_rows.down_rows, bf16[192,768]{1,0:T(8,128)(2,1)S(1)} %merge.2.up_rows.down_rows, bf16[768,6144]{1,0:T(8,128)(2,1)} %weight.15), custom_call_target="tpu_custom_call" | custom-call | flops 905969664 | bytes 7077888 | tf_op jit(solution)/shard_map/message/pallas_call | solution.py:139
  39.4 4.3 %collective-permute-start.6 = (bf16[96,3072]{1,0:T(8,128)(2,1)}, bf16[96,3072]{1,0:T(8,128)(2,1)S(1)}, u32[]{:S(2)}, u32[]{:S(2)}) collective-permute-start(bf16[96,3072]{1,0:T(8,128)(2,1)} %get-tuple-element.25), channel_id=1, source_target_pairs={{0,1},{4,5},{8,9},{12,13},{16,17},{20,21},{24,25},{28,29}} | collective-permute-start | bytes 1769480 | tf_op jit(solution)/shard_map/ppermute | solution.py:268
  43.7 0.8 collective-permute-start.7
  44.6 6.4 %message.9 = (bf16[96,3072]{1,0:T(8,128)(2,1)}, bf16[96,3072]{1,0:T(8,128)(2,1)}) custom-call(s32[2]{0:T(128)S(1)} %copy-done.10, bf16[192,768]{1,0:T(8,128)(2,1)S(1)} %merge.2.up_rows.down_rows, bf16[192,768]{1,0:T(8,128)(2,1)S(1)} %merge.2.up_rows.down_rows, bf16[768,6144]{1,0:T(8,128)(2,1)} %weight.15), custom_call_target="tpu_custom_call" | custom-call | flops 905969664 | bytes 7077888 | tf_op jit(solution)/shard_map/message/pallas_call | solution.py:139
  51.0 1.3 %collective-permute-start.12 = (bf16[96,3072]{1,0:T(8,128)(2,1)}, bf16[96,3072]{1,0:T(8,128)(2,1)S(1)}, u32[]{:S(2)}, u32[]{:S(2)}) collective-permute-start(bf16[96,3072]{1,0:T(8,128)(2,1)} %get-tuple-element.31), channel_id=1, source_target_pairs={{0,1},{4,5},{8,9},{12,13},{16,17},{20,21},{24,25},{28,29}} | collective-permute-start | bytes 1769480 | tf_op jit(solution)/shard_map/ppermute | solution.py:268
  52.3 0.9 collective-permute-start.13
  53.2 0.1 pad_add_fusion.3.blocks
  53.3 2.7 %merge.3 = bf16[192,768]{1,0:T(8,128)(2,1)S(1)} custom-call(s32[2]{0:T(128)S(1)} %pad_add_fusion.1.place, f32[192,768]{1,0:T(8,128)S(1)} %get-tuple-element.23.own, f32[192,128]{1,0:T(8,128)S(1)} %copy-done.8, bf16[192,896]{1,0:T(8,128)(2,1)} %collective-permute-done.5.refs_0_), custom_call_target="tpu_custom_call" | custom-call | flops 1179648 | bytes 1474560 | tf_op jit(solution)/shard_map/merge/pallas_call | solution.py:239
  56.1 1.7 %collective-permute-done.6.refs_0_ = bf16[96,3072]{1,0:T(8,128)(2,1)S(1)} collective-permute-done((bf16[96,3072]{1,0:T(8,128)(2,1)}, bf16[96,3072]{1,0:T(8,128)(2,1)S(1)}, u32[]{:S(2)}, u32[]{:S(2)}) %collective-permute-start.6) | collective-permute-done | bytes 589856 | tf_op jit(solution)/shard_map/ppermute | solution.py:268
  57.8 6.4 %message.7 = (bf16[96,3072]{1,0:T(8,128)(2,1)}, bf16[96,3072]{1,0:T(8,128)(2,1)}) custom-call(s32[2]{0:T(128)S(1)} %pad_add_fusion.3.blocks, bf16[384,768]{1,0:T(8,128)(2,1)S(1)} %pad_maximum_fusion.1.up_rows.down_rows.own_rows, bf16[384,768]{1,0:T(8,128)(2,1)S(1)} %pad_maximum_fusion.1.up_rows.down_rows.own_rows, bf16[768,6144]{1,0:T(8,128)(2,1)} %weight.15, ...), custom_call_target="tpu_custom_call" | custom-call | flops 905969664 | bytes 7077888 | tf_op jit(solution)/shard_map/message/pallas_call | solution.py:139
  64.2 4.3 %collective-permute-start.8 = (bf16[96,3072]{1,0:T(8,128)(2,1)}, bf16[96,3072]{1,0:T(8,128)(2,1)S(1)}, u32[]{:S(2)}, u32[]{:S(2)}) collective-permute-start(bf16[96,3072]{1,0:T(8,128)(2,1)} %get-tuple-element.27), channel_id=1, source_target_pairs={{0,1},{1,2},{4,5},{5,6},{8,9},{9,10},{12,13},{13,14},{16,17},{17,1... | collective-permute-start | bytes 1769480 | tf_op jit(solution)/shard_map/ppermute | solution.py:268
  68.5 0.7 collective-permute-start.9
  69.2 1.2 collective-permute-done.12.refs_0_
  70.4 6.4 %message.10 = (bf16[96,3072]{1,0:T(8,128)(2,1)}, bf16[96,3072]{1,0:T(8,128)(2,1)}) custom-call(s32[2]{0:T(128)S(1)} %pad_add_fusion.3.blocks, bf16[384,768]{1,0:T(8,128)(2,1)S(1)} %pad_maximum_fusion.1.up_rows.down_rows.own_rows, bf16[384,768]{1,0:T(8,128)(2,1)S(1)} %pad_maximum_fusion.1.up_rows.down_rows.own_rows, bf16[768,6144]{1,0:T(8,128)(2,1)} %weight.15, ...), custom_call_target="tpu_custom_call" | custom-call | flops 905969664 | bytes 7077888 | tf_op jit(solution)/shard_map/message/pallas_call | solution.py:139
  76.9 4.3 %collective-permute-start.14 = (bf16[96,3072]{1,0:T(8,128)(2,1)}, bf16[96,3072]{1,0:T(8,128)(2,1)S(1)}, u32[]{:S(2)}, u32[]{:S(2)}) collective-permute-start(bf16[96,3072]{1,0:T(8,128)(2,1)} %get-tuple-element.33), channel_id=1, source_target_pairs={{0,1},{1,2},{4,5},{5,6},{8,9},{9,10},{12,13},{13,14},{16,17},{17,1... | collective-permute-start | bytes 1769480 | tf_op jit(solution)/shard_map/ppermute | solution.py:268
  81.2 1.5 %collective-permute-start.15 = (bf16[96,3072]{1,0:T(8,128)(2,1)}, bf16[96,3072]{1,0:T(8,128)(2,1)}, u32[]{:S(2)}, u32[]{:S(2)}) collective-permute-start(bf16[96,3072]{1,0:T(8,128)(2,1)} %get-tuple-element.34), channel_id=1, source_target_pairs={{3,2},{2,1},{7,6},{6,5},{11,10},{10,9},{15,14},{14,13},{19,18},{18... | collective-permute-start | bytes 1769480 | tf_op jit(solution)/shard_map/ppermute | solution.py:269
  82.7 0.1 pad_add_fusion.2.blocks
  82.7 0.3 collective-permute-done.8.refs_0_
  83.1 6.4 %message.8 = (bf16[96,3072]{1,0:T(8,128)(2,1)}, bf16[96,3072]{1,0:T(8,128)(2,1)}) custom-call(s32[2]{0:T(128)S(1)} %pad_add_fusion.2.blocks, bf16[384,768]{1,0:T(8,128)(2,1)S(1)} %pad_maximum_fusion.1.up_rows.down_rows.own_rows, bf16[384,768]{1,0:T(8,128)(2,1)S(1)} %pad_maximum_fusion.1.up_rows.down_rows.own_rows, bf16[768,6144]{1,0:T(8,128)(2,1)} %weight.15, ...), custom_call_target="tpu_custom_call" | custom-call | flops 905969664 | bytes 7077888 | tf_op jit(solution)/shard_map/message/pallas_call | solution.py:139
  89.5 4.3 %collective-permute-start.10 = (bf16[96,3072]{1,0:T(8,128)(2,1)}, bf16[96,3072]{1,0:T(8,128)(2,1)S(1)}, u32[]{:S(2)}, u32[]{:S(2)}) collective-permute-start(bf16[96,3072]{1,0:T(8,128)(2,1)} %get-tuple-element.29), channel_id=1, source_target_pairs={{0,1},{1,2},{2,3},{4,5},{5,6},{6,7},{8,9},{9,10},{10,11},{12,13},{... | collective-permute-start | bytes 1769480 | tf_op jit(solution)/shard_map/ppermute | solution.py:268
  93.8 1.4 %collective-permute-start.11 = (bf16[96,3072]{1,0:T(8,128)(2,1)}, bf16[96,3072]{1,0:T(8,128)(2,1)}, u32[]{:S(2)}, u32[]{:S(2)}) collective-permute-start(bf16[96,3072]{1,0:T(8,128)(2,1)} %get-tuple-element.30), channel_id=1, source_target_pairs={{3,2},{2,1},{1,0},{7,6},{6,5},{5,4},{11,10},{10,9},{9,8},{15,14},{... | collective-permute-start | bytes 1769480 | tf_op jit(solution)/shard_map/ppermute | solution.py:269
  95.3 0.4 collective-permute-done.14.refs_0_
  95.7 6.5 %message.11 = (bf16[96,3072]{1,0:T(8,128)(2,1)}, bf16[96,3072]{1,0:T(8,128)(2,1)}) custom-call(s32[2]{0:T(128)S(1)} %pad_add_fusion.2.blocks, bf16[384,768]{1,0:T(8,128)(2,1)S(1)} %pad_maximum_fusion.1.up_rows.down_rows.own_rows, bf16[384,768]{1,0:T(8,128)(2,1)S(1)} %pad_maximum_fusion.1.up_rows.down_rows.own_rows, bf16[768,6144]{1,0:T(8,128)(2,1)} %weight.15, ...), custom_call_target="tpu_custom_call" | custom-call | flops 905969664 | bytes 7077888 | tf_op jit(solution)/shard_map/message/pallas_call | solution.py:139
  102.2 4.6 %collective-permute-start.16 = (bf16[96,3072]{1,0:T(8,128)(2,1)}, bf16[96,3072]{1,0:T(8,128)(2,1)S(1)}, u32[]{:S(2)}, u32[]{:S(2)}) collective-permute-start(bf16[96,3072]{1,0:T(8,128)(2,1)} %get-tuple-element.35), channel_id=1, source_target_pairs={{0,1},{1,2},{2,3},{4,5},{5,6},{6,7},{8,9},{9,10},{10,11},{12,13},{... | collective-permute-start | bytes 1769480 | tf_op jit(solution)/shard_map/ppermute | solution.py:268
  106.7 1.3 %collective-permute-start.17 = (bf16[96,3072]{1,0:T(8,128)(2,1)}, bf16[96,3072]{1,0:T(8,128)(2,1)}, u32[]{:S(2)}, u32[]{:S(2)}) collective-permute-start(bf16[96,3072]{1,0:T(8,128)(2,1)} %get-tuple-element.36), channel_id=1, source_target_pairs={{3,2},{2,1},{1,0},{7,6},{6,5},{5,4},{11,10},{10,9},{9,8},{15,14},{... | collective-permute-start | bytes 1769480 | tf_op jit(solution)/shard_map/ppermute | solution.py:269
  108.0 0.6 dynamic_slice.3
  108.6 0.7 pad_add_fusion.blocks
  109.4 5.3 %final.2 = bf16[96,3072]{1,0:T(8,128)(2,1)S(1)} custom-call(s32[2]{0:T(128)S(1)} %pad_add_fusion.blocks, bf16[384,768]{1,0:T(8,128)(2,1)S(1)} %pad_maximum_fusion.1.up_rows.down_rows.own_rows, bf16[768,6144]{1,0:T(8,128)(2,1)} %weight.15, f32[64,6144]{1,0:T(8,128)S(1)} %copy-done, bf16[96,3072]{1,0:T(8,128)(2,1)S(1)} %collective-permute-done.10.up, ...), custom_call_target="tpu_custom_call" | custom-call | flops 452984832 | bytes 7667712 | tf_op jit(solution)/shard_map/final/pallas_call | solution.py:168
  114.6 4.4 %collective-permute-done.16.up = bf16[96,3072]{1,0:T(8,128)(2,1)S(1)} collective-permute-done((bf16[96,3072]{1,0:T(8,128)(2,1)}, bf16[96,3072]{1,0:T(8,128)(2,1)S(1)}, u32[]{:S(2)}, u32[]{:S(2)}) %collective-permute-start.16) | collective-permute-done | bytes 589856 | tf_op jit(solution)/shard_map/ppermute | solution.py:268
  119.0 0.9 collective-permute-done.17.down
  120.0 5.3 %final.3 = bf16[96,3072]{1,0:T(8,128)(2,1)S(1)} custom-call(s32[2]{0:T(128)S(1)} %pad_add_fusion.blocks, bf16[384,768]{1,0:T(8,128)(2,1)S(1)} %pad_maximum_fusion.1.up_rows.down_rows.own_rows, bf16[768,6144]{1,0:T(8,128)(2,1)} %weight.15, f32[64,6144]{1,0:T(8,128)S(1)} %copy-done, bf16[96,3072]{1,0:T(8,128)(2,1)S(1)} %collective-permute-done.16.up, ...), custom_call_target="tpu_custom_call" | custom-call | flops 452984832 | bytes 7667712 | tf_op jit(solution)/shard_map/final/pallas_call | solution.py:168
  125.3 1.1 pad_maximum_fusion
  (36 shorter events, 0.2 us)
Async XLA Ops:
  0.0 13.8 %copy-start.1 = (bf16[384,768]{1,0:T(8,128)(2,1)S(1)}, bf16[384,768]{1,0:T(8,128)(2,1)}, u32[]{:S(2)}) copy-start(bf16[384,768]{1,0:T(8,128)(2,1)} %key.5) | copy-start | bytes 1769476
  0.0 13.8 %copy-start.2 = (bf16[384,768]{1,0:T(8,128)(2,1)S(1)}, bf16[384,768]{1,0:T(8,128)(2,1)}, u32[]{:S(2)}) copy-start(bf16[384,768]{1,0:T(8,128)(2,1)} %value.5) | copy-start | bytes 1769476
  0.0 13.8 %copy-start.9 = (s32[4,4]{1,0:T(4,128)S(1)}, s32[4,4]{1,0:T(4,128)}, u32[]{:S(2)}) copy-start(s32[4,4]{1,0:T(4,128)} %visible.5) | copy-start | bytes 196
  0.0 13.8 %collective-permute-start = (bf16[384,768]{1,0:T(8,128)(2,1)}, bf16[384,768]{1,0:T(8,128)(2,1)S(1)}, u32[]{:S(2)}, u32[]{:S(2)}) collective-permute-start(bf16[384,768]{1,0:T(8,128)(2,1)} %key.5), channel_id=1, source_target_pairs={{0,4},{4,0},{8,12},{12,8},{1,5},{5,1},{9,13},{13,9},{2,6},{6,2},{1... | collective-permute-start | bytes 1769480 | tf_op jit(solution)/shard_map/ppermute | solution.py:207
  0.5 13.3 %collective-permute-start.1 = (bf16[384,768]{1,0:T(8,128)(2,1)}, bf16[384,768]{1,0:T(8,128)(2,1)S(1)}, u32[]{:S(2)}, u32[]{:S(2)}) collective-permute-start(bf16[384,768]{1,0:T(8,128)(2,1)} %value.5), channel_id=1, source_target_pairs={{0,4},{4,0},{8,12},{12,8},{1,5},{5,1},{9,13},{13,9},{2,6},{6,2},{1... | collective-permute-start | bytes 1769480 | tf_op jit(solution)/shard_map/ppermute | solution.py:208
  1.6 12.1 %copy-start.3 = (bf16[192,768]{1,0:T(8,128)(2,1)}, bf16[192,768]{1,0:T(8,128)(2,1)S(1)}, u32[]{:S(2)}) copy-start(bf16[192,768]{1,0:T(8,128)(2,1)S(1)} %pad_maximum_fusion.2.query_outer) | copy-start | bytes 884740
  1.7 12.1 %collective-permute-start.2 = (bf16[192,768]{1,0:T(8,128)(2,1)S(1)}, bf16[192,768]{1,0:T(8,128)(2,1)}, u32[]{:S(2)}, u32[]{:S(2)}) collective-permute-start(bf16[192,768]{1,0:T(8,128)(2,1)S(1)} %pad_maximum_fusion.2.query_outer), channel_id=1, source_target_pairs={{8,0},{12,4},{9,1},{13,5},{10,2},{14,6},{11,3},{15,7},{24,16},{28,... | collective-permute-start | bytes 884744 | tf_op jit(solution)/shard_map/ppermute | solution.py:26
  3.9 13.3 %copy-start.5 = (bf16[192,768]{1,0:T(8,128)(2,1)}, bf16[192,768]{1,0:T(8,128)(2,1)S(1)}, u32[]{:S(2)}) copy-start(bf16[192,768]{1,0:T(8,128)(2,1)S(1)} %slice.17.query_inner) | copy-start | bytes 884740
  3.9 15.5 %collective-permute-start.4 = (bf16[192,768]{1,0:T(8,128)(2,1)S(1)}, bf16[192,768]{1,0:T(8,128)(2,1)S(1)}, u32[]{:S(2)}, u32[]{:S(2)}) collective-permute-start(bf16[192,768]{1,0:T(8,128)(2,1)S(1)} %slice.17.query_inner), channel_id=1, source_target_pairs={{8,0},{12,4},{9,1},{13,5},{10,2},{14,6},{11,3},{15,7},{24,16},{28,... | collective-permute-start | bytes 884744 | tf_op jit(solution)/shard_map/ppermute | solution.py:26
  17.2 8.1 %copy-start.4 = (bf16[192,768]{1,0:T(8,128)(2,1)S(1)}, bf16[192,768]{1,0:T(8,128)(2,1)}, u32[]{:S(2)}) copy-start(bf16[192,768]{1,0:T(8,128)(2,1)} %copy-done.3) | copy-start | bytes 884740
  17.2 13.4 %collective-permute-start.3 = (bf16[192,896]{1,0:T(8,128)(2,1)S(1)}, bf16[192,896]{1,0:T(8,128)(2,1)S(1)}, u32[]{:S(2)}, u32[]{:S(2)}) collective-permute-start(bf16[192,896]{1,0:T(8,128)(2,1)S(1)} %served.2), channel_id=1, source_target_pairs={{0,8},{4,12},{1,9},{5,13},{2,10},{6,14},{3,11},{7,15},{16,24},{20,... | collective-permute-start | bytes 1032200 | tf_op jit(solution)/shard_map/ppermute | solution.py:26
  18.7 6.6 %copy-start.6 = (bf16[192,768]{1,0:T(8,128)(2,1)S(1)}, bf16[192,768]{1,0:T(8,128)(2,1)}, u32[]{:S(2)}) copy-start(bf16[192,768]{1,0:T(8,128)(2,1)} %copy-done.5) | copy-start | bytes 884740
  23.2 30.1 %collective-permute-start.5 = (bf16[192,896]{1,0:T(8,128)(2,1)}, bf16[192,896]{1,0:T(8,128)(2,1)}, u32[]{:S(2)}, u32[]{:S(2)}) collective-permute-start(bf16[192,896]{1,0:T(8,128)(2,1)} %served.3), channel_id=1, source_target_pairs={{0,8},{4,12},{1,9},{5,13},{2,10},{6,14},{3,11},{7,15},{16,24},{20,... | collective-permute-start | bytes 1032200 | tf_op jit(solution)/shard_map/ppermute | solution.py:26
  30.6 8.8 %copy-start.7 = (f32[192,128]{1,0:T(8,128)}, f32[192,128]{1,0:T(8,128)S(1)}, u32[]{:S(2)}) copy-start(f32[192,128]{1,0:T(8,128)S(1)} %get-tuple-element.24.own_sum) | copy-start | bytes 294916
  30.6 2.3 %copy-start.10 = (s32[2]{0:T(128)S(1)}, s32[2]{0:T(128)}, u32[]{:S(2)}) copy-start(s32[2]{0:T(128)} %constant.25.clone.blocks) | copy-start | bytes 28
  39.4 18.4 %collective-permute-start.6 = (bf16[96,3072]{1,0:T(8,128)(2,1)}, bf16[96,3072]{1,0:T(8,128)(2,1)S(1)}, u32[]{:S(2)}, u32[]{:S(2)}) collective-permute-start(bf16[96,3072]{1,0:T(8,128)(2,1)} %get-tuple-element.25), channel_id=1, source_target_pairs={{0,1},{4,5},{8,9},{12,13},{16,17},{20,21},{24,25},{28,29}} | collective-permute-start | bytes 1769480 | tf_op jit(solution)/shard_map/ppermute | solution.py:268
  43.7 9.6 %copy-start.8 = (f32[192,128]{1,0:T(8,128)S(1)}, f32[192,128]{1,0:T(8,128)}, u32[]{:S(2)}) copy-start(f32[192,128]{1,0:T(8,128)} %copy-done.7) | copy-start | bytes 294916
  43.7 14.0 %collective-permute-start.7 = (bf16[96,3072]{1,0:T(8,128)(2,1)}, bf16[96,3072]{1,0:T(8,128)(2,1)S(1)}, u32[]{:S(2)}, u32[]{:S(2)}) collective-permute-start(bf16[96,3072]{1,0:T(8,128)(2,1)} %get-tuple-element.26), channel_id=1, source_target_pairs={{3,2},{7,6},{11,10},{15,14},{19,18},{23,22},{27,26},{31,30}} | collective-permute-start | bytes 1769480 | tf_op jit(solution)/shard_map/ppermute | solution.py:269
  51.0 19.4 %collective-permute-start.12 = (bf16[96,3072]{1,0:T(8,128)(2,1)}, bf16[96,3072]{1,0:T(8,128)(2,1)S(1)}, u32[]{:S(2)}, u32[]{:S(2)}) collective-permute-start(bf16[96,3072]{1,0:T(8,128)(2,1)} %get-tuple-element.31), channel_id=1, source_target_pairs={{0,1},{4,5},{8,9},{12,13},{16,17},{20,21},{24,25},{28,29}} | collective-permute-start | bytes 1769480 | tf_op jit(solution)/shard_map/ppermute | solution.py:268
  52.3 18.1 %collective-permute-start.13 = (bf16[96,3072]{1,0:T(8,128)(2,1)}, bf16[96,3072]{1,0:T(8,128)(2,1)S(1)}, u32[]{:S(2)}, u32[]{:S(2)}) collective-permute-start(bf16[96,3072]{1,0:T(8,128)(2,1)} %get-tuple-element.32), channel_id=1, source_target_pairs={{3,2},{7,6},{11,10},{15,14},{19,18},{23,22},{27,26},{31,30}} | collective-permute-start | bytes 1769480 | tf_op jit(solution)/shard_map/ppermute | solution.py:269
  64.2 18.8 %collective-permute-start.8 = (bf16[96,3072]{1,0:T(8,128)(2,1)}, bf16[96,3072]{1,0:T(8,128)(2,1)S(1)}, u32[]{:S(2)}, u32[]{:S(2)}) collective-permute-start(bf16[96,3072]{1,0:T(8,128)(2,1)} %get-tuple-element.27), channel_id=1, source_target_pairs={{0,1},{1,2},{4,5},{5,6},{8,9},{9,10},{12,13},{13,14},{16,17},{17,1... | collective-permute-start | bytes 1769480 | tf_op jit(solution)/shard_map/ppermute | solution.py:268
  68.5 14.5 %collective-permute-start.9 = (bf16[96,3072]{1,0:T(8,128)(2,1)}, bf16[96,3072]{1,0:T(8,128)(2,1)S(1)}, u32[]{:S(2)}, u32[]{:S(2)}) collective-permute-start(bf16[96,3072]{1,0:T(8,128)(2,1)} %get-tuple-element.28), channel_id=1, source_target_pairs={{3,2},{2,1},{7,6},{6,5},{11,10},{10,9},{15,14},{14,13},{19,18},{18... | collective-permute-start | bytes 1769480 | tf_op jit(solution)/shard_map/ppermute | solution.py:269
  76.9 18.8 %collective-permute-start.14 = (bf16[96,3072]{1,0:T(8,128)(2,1)}, bf16[96,3072]{1,0:T(8,128)(2,1)S(1)}, u32[]{:S(2)}, u32[]{:S(2)}) collective-permute-start(bf16[96,3072]{1,0:T(8,128)(2,1)} %get-tuple-element.33), channel_id=1, source_target_pairs={{0,1},{1,2},{4,5},{5,6},{8,9},{9,10},{12,13},{13,14},{16,17},{17,1... | collective-permute-start | bytes 1769480 | tf_op jit(solution)/shard_map/ppermute | solution.py:268
  81.2 14.5 %collective-permute-start.15 = (bf16[96,3072]{1,0:T(8,128)(2,1)}, bf16[96,3072]{1,0:T(8,128)(2,1)}, u32[]{:S(2)}, u32[]{:S(2)}) collective-permute-start(bf16[96,3072]{1,0:T(8,128)(2,1)} %get-tuple-element.34), channel_id=1, source_target_pairs={{3,2},{2,1},{7,6},{6,5},{11,10},{10,9},{15,14},{14,13},{19,18},{18... | collective-permute-start | bytes 1769480 | tf_op jit(solution)/shard_map/ppermute | solution.py:269
  89.5 19.9 %collective-permute-start.10 = (bf16[96,3072]{1,0:T(8,128)(2,1)}, bf16[96,3072]{1,0:T(8,128)(2,1)S(1)}, u32[]{:S(2)}, u32[]{:S(2)}) collective-permute-start(bf16[96,3072]{1,0:T(8,128)(2,1)} %get-tuple-element.29), channel_id=1, source_target_pairs={{0,1},{1,2},{2,3},{4,5},{5,6},{6,7},{8,9},{9,10},{10,11},{12,13},{... | collective-permute-start | bytes 1769480 | tf_op jit(solution)/shard_map/ppermute | solution.py:268
  93.8 14.2 %copy-start.11 = (s32[4]{0:T(128)S(1)}, s32[4]{0:T(128)}, u32[]{:S(2)}) copy-start(s32[4]{0:T(128)} %param.13) | copy-start | bytes 52
  93.8 15.5 %copy-start = (f32[64,6144]{1,0:T(8,128)S(1)}, f32[64,6144]{1,0:T(8,128)}, u32[]{:S(2)}) copy-start(f32[64,6144]{1,0:T(8,128)} %gate.3) | copy-start | bytes 4718596
  93.8 15.5 %collective-permute-start.11 = (bf16[96,3072]{1,0:T(8,128)(2,1)}, bf16[96,3072]{1,0:T(8,128)(2,1)}, u32[]{:S(2)}, u32[]{:S(2)}) collective-permute-start(bf16[96,3072]{1,0:T(8,128)(2,1)} %get-tuple-element.30), channel_id=1, source_target_pairs={{3,2},{2,1},{1,0},{7,6},{6,5},{5,4},{11,10},{10,9},{9,8},{15,14},{... | collective-permute-start | bytes 1769480 | tf_op jit(solution)/shard_map/ppermute | solution.py:269
  102.2 16.9 %collective-permute-start.16 = (bf16[96,3072]{1,0:T(8,128)(2,1)}, bf16[96,3072]{1,0:T(8,128)(2,1)S(1)}, u32[]{:S(2)}, u32[]{:S(2)}) collective-permute-start(bf16[96,3072]{1,0:T(8,128)(2,1)} %get-tuple-element.35), channel_id=1, source_target_pairs={{0,1},{1,2},{2,3},{4,5},{5,6},{6,7},{8,9},{9,10},{10,11},{12,13},{... | collective-permute-start | bytes 1769480 | tf_op jit(solution)/shard_map/ppermute | solution.py:268
  106.7 13.2 %collective-permute-start.17 = (bf16[96,3072]{1,0:T(8,128)(2,1)}, bf16[96,3072]{1,0:T(8,128)(2,1)}, u32[]{:S(2)}, u32[]{:S(2)}) collective-permute-start(bf16[96,3072]{1,0:T(8,128)(2,1)} %get-tuple-element.36), channel_id=1, source_target_pairs={{3,2},{2,1},{1,0},{7,6},{6,5},{5,4},{11,10},{10,9},{9,8},{15,14},{... | collective-permute-start | bytes 1769480 | tf_op jit(solution)/shard_map/ppermute | solution.py:269

commit v2 on v1

v2 whole, which is shorter than its diff:
```python
import functools

import jax
import jax.numpy as jnp
from jax import lax
from jax.experimental import pallas as pl
from jax.experimental.pallas import tpu as pltpu
from jax.sharding import PartitionSpec as P

HD = 128
LANES = 128
HIDDEN = -1e30
LOG2E = 1.4426950408889634
PARAMS = pltpu.CompilerParams(vmem_limit_bytes=20 * 1024 * 1024)
SMEM = pl.BlockSpec(memory_space=pltpu.SMEM)
VMEM = pl.BlockSpec(memory_space=pltpu.VMEM)
PIECE_LANES = 32


def cost(flops, moved, exps=0):
    return pl.CostEstimate(flops=int(flops), bytes_accessed=int(moved), transcendentals=int(exps))


def shifted(block, axis, distance):
    count = lax.axis_size(axis)
    return lax.ppermute(block, axis, [(i, i + distance) for i in range(count) if 0 <= i + distance < count])


def head_columns(head):
    return slice(head * HD, (head + 1) * HD)


def attend(query, keys, values, flags, write):
    rows, width = query.shape
    scale = LOG2E * HD ** (-0.5)
    lane = lax.broadcasted_iota(jnp.int32, (rows, LANES), 1)
    packed = jnp.zeros((rows, LANES), jnp.float32)
    for head in range(width // HD):
        columns = head_columns(head)
        mine = query[:, columns]
        scores = [
            lax.dot_general(mine, key[:, columns], (((1,), (1,)), ((), ())), preferred_element_type=jnp.float32)
            for key in keys
        ]
        tops = [jnp.max(block, axis=-1, keepdims=True) * scale for block in scores]
        top = functools.reduce(
            jnp.maximum, [one if flag is None else jnp.where(flag, one, HIDDEN) for one, flag in zip(tops, flags)]
        )
        total, product = None, None
        for block, value, flag in zip(scores, values, flags):
            above = top if flag is None else jnp.where(flag, top, -HIDDEN)
            probs = jnp.exp2(block * scale - above)
            part = jnp.sum(probs, axis=-1, keepdims=True)
            part_product = jnp.dot(
                probs.astype(jnp.bfloat16), value[:, columns], preferred_element_type=jnp.float32
            )
            total = part if total is None else total + part
            product = part_product if product is None else product + part_product
        total = jnp.where(total > 0.0, total, 1.0)
        write(columns, product * (1.0 / total))
        packed = jnp.where(lane == head, top + jnp.log2(total), packed)
    return packed


def beside_of(span):
    return span + 1 - 2 * lax.rem(span, 2)


def local_kernel(place, visible, query, key, value, key_beside, value_beside, result, sums):
    span = place[0]

    def write(columns, block):
        result[:, columns] = block

    sums[...] = attend(
        query, [key, key_beside], [value, value_beside], [None, visible[span, beside_of(span)] > 0], write
    )


def served_kernel(distance, place, visible, query, key, value, key_beside, value_beside, result):
    span = place[0]
    asker = jnp.minimum(span + distance, visible.shape[0] - 1)
    flags = [visible[asker, span] > 0, visible[asker, beside_of(span)] > 0]

    def write(columns, block):
        result[:, columns] = block.astype(jnp.bfloat16)

    width = query.shape[1]
    rest = attend(query, [key, key_beside], [value, value_beside], flags, write)
    sent = jnp.zeros_like(rest)
    for piece in range(3):
        part = rest.astype(jnp.bfloat16).astype(jnp.float32)
        sent = sent + (part if piece == 0 else pltpu.roll(part, piece * PIECE_LANES, 1))
        rest = rest - part
    result[:, width:] = sent.astype(jnp.bfloat16)


def merge_kernel(distances, pieces, place, own, own_sum, *refs):
    served, result = refs[:-1], refs[-1]
    width = own.shape[1]
    span = place[0]
    at = 0
    for start, rows in pieces:
        there, here = slice(start, start + rows), slice(at, at + rows)
        sums = [own_sum[there, :]]
        for distance, ref in zip(distances, served):
            sent = ref[here, width:].astype(jnp.float32)
            joined = sent
            for piece in (1, 2):
                joined = joined + pltpu.roll(sent, LANES - piece * PIECE_LANES, 1)
            sums.append(jnp.where(span >= distance, joined, HIDDEN))
        top = functools.reduce(jnp.maximum, sums)
        shares = [jnp.exp2(one - top) for one in sums]
        over = 1.0 / sum(shares)
        shares = [share * over for share in shares]
        for head in range(width // HD):
            columns = head_columns(head)
            merged = own[there, columns] * shares[0][:, head:head + 1]
            for share, ref in zip(shares[1:], served):
                merged = merged + ref[here, columns].astype(jnp.float32) * share[:, head:head + 1]
            result[here, columns] = merged.astype(jnp.bfloat16)
        at += rows


def rows_at(attended, index, rows):
    return attended[pl.ds(pl.multiple_of(index * rows, rows), rows), :]


def message_kernel(first, tile, blocks, attended, weight, *refs):
    ups, downs = refs[-2:]
    rows, columns = ups.shape
    both = jnp.concatenate([rows_at(attended, blocks[0], rows), rows_at(attended, blocks[1], rows)], axis=0)
    for at in range(0, columns, tile):
        here = slice(at, at + tile)
        product = jnp.dot(both, weight[:, first + at:first + at + tile], preferred_element_type=jnp.float32)
        up, down = product[:rows], product[rows:]
        if len(refs) == 4:
            up = up + refs[0][:, here].astype(jnp.float32)
            down = down + refs[1][:, here].astype(jnp.float32)
        ups[:, here] = up.astype(jnp.bfloat16)
        downs[:, here] = down.astype(jnp.bfloat16)


def message(blocks, attended, weight, arrived, first, columns, rows, tile):
    width = attended.shape[1]
    return pl.pallas_call(
        functools.partial(message_kernel, first, tile),
        in_specs=[SMEM] + [VMEM] * (2 + len(arrived)),
        out_specs=[VMEM, VMEM],
        out_shape=[jax.ShapeDtypeStruct((rows, columns), jnp.bfloat16)] * 2,
        compiler_params=PARAMS,
        cost_estimate=cost(4 * rows * width * columns, 2 * width * columns + 8 * rows * columns),
        name="message",
    )(blocks, attended, weight, *arrived)


def own_kernel(tile, blocks, attended, weight, result):
    rows, columns = result.shape
    mine = rows_at(attended, blocks[0], rows)
    for at in range(0, columns, tile):
        here = slice(at, at + tile)
        result[:, here] = jnp.dot(mine, weight[:, here], preferred_element_type=jnp.float32)


def own_projection(blocks, attended, weight, rows, tile):
    width, columns = weight.shape
    return pl.pallas_call(
        functools.partial(own_kernel, tile),
        in_specs=[SMEM, VMEM, VMEM],
        out_specs=VMEM,
        out_shape=jax.ShapeDtypeStruct((rows, columns), jnp.float32),
        compiler_params=PARAMS,
        cost_estimate=cost(2 * rows * width * columns, 2 * width * columns + 4 * rows * columns),
        name="own",
    )(blocks, attended, weight)


def final_kernel(blocks, own, gate, up, down, *refs):
    result = refs[-1]
    summed = own[...] + up[...].astype(jnp.float32) + down[...].astype(jnp.float32)
    result[...] = (summed * gate[pl.ds(lax.rem(blocks[1], 8), 1), :]).astype(jnp.bfloat16)


def final(blocks, own, gate_table, up, down, first, tile, before):
    rows, columns = up.shape
    start = first // tile
    there = pl.BlockSpec((rows, tile), lambda j, b: (0, start + j))
    piece = pl.BlockSpec((rows, tile), lambda j, b: (0, j))
    return pl.pallas_call(
        final_kernel,
        grid_spec=pltpu.PrefetchScalarGridSpec(
            num_scalar_prefetch=1,
            grid=(columns // tile,),
            in_specs=[
                there,
                pl.BlockSpec((8, tile), lambda j, b: (b[1] // 8, start + j)),
                piece,
                piece,
            ] + [pl.BlockSpec(memory_space=pl.ANY)] * len(before),
            out_specs=there,
        ),
        out_shape=jax.ShapeDtypeStruct(own.shape, jnp.bfloat16),
        input_output_aliases={5: 0} if before else {},
        compiler_params=PARAMS,
        cost_estimate=cost(4 * rows * columns, 10 * rows * columns),
        name="final",
    )(blocks, own, gate_table, up, down, *before)


def body(queries, keys, values, out_weight, gate_table, levels, visible):
    rows, width = queries.shape
    model = out_weight.shape[1]
    spans = lax.axis_size("span")
    ranks = lax.axis_size("tensor")
    span = lax.axis_index("span")
    rank = lax.axis_index("tensor")
    block = rows // ranks
    quarter = rows // 4
    half = 2 * quarter
    place = jnp.stack([span, rank]).astype(jnp.int32)
    level = levels[span]

    query_outer = jnp.concatenate([queries[:quarter], queries[rows - quarter:]])
    query_inner = queries[quarter:rows - quarter]
    distances = list(range(2, spans, 2))
    asked_outer = [shifted(query_outer, "span", -distance) for distance in distances]
    swap = [(i, i + 1 - 2 * (i % 2)) for i in range(spans)]
    key_beside = lax.ppermute(keys, "span", swap)
    value_beside = lax.ppermute(values, "span", swap)
    asked_inner = [shifted(query_inner, "span", -distance) for distance in distances]

    own, own_sum = pl.pallas_call(
        local_kernel,
        in_specs=[SMEM, SMEM] + [VMEM] * 5,
        out_specs=[VMEM] * 2,
        out_shape=[
            jax.ShapeDtypeStruct((rows, width), jnp.float32),
            jax.ShapeDtypeStruct((rows, LANES), jnp.float32),
        ],
        compiler_params=PARAMS,
        cost_estimate=cost(8 * rows * rows * width, 14 * rows * width, 2 * rows * rows * width // HD),
        name="local",
    )(place, visible, queries, keys, values, key_beside, value_beside)

    def served(asked, distance):
        return pl.pallas_call(
            functools.partial(served_kernel, distance),
            in_specs=[SMEM, SMEM] + [VMEM] * 5,
            out_specs=VMEM,
            out_shape=jax.ShapeDtypeStruct((half, width + LANES), jnp.bfloat16),
            compiler_params=PARAMS,
            cost_estimate=cost(8 * half * rows * width, 12 * rows * width, 2 * half * rows * width // HD),
            name="served",
        )(place, visible, asked, keys, values, key_beside, value_beside)

    asked_outer, asked_inner, own_sum = lax.optimization_barrier((asked_outer, asked_inner, own_sum))
    back_outer = [shifted(served(q, d), "span", d) for q, d in zip(asked_outer, distances)]
    back_inner = [shifted(served(q, d), "span", d) for q, d in zip(asked_inner, distances)]

    def merge(back, pieces):
        return pl.pallas_call(
            functools.partial(merge_kernel, distances, pieces),
            in_specs=[SMEM] + [VMEM] * (2 + len(back)),
            out_specs=VMEM,
            out_shape=jax.ShapeDtypeStruct((half, width), jnp.bfloat16),
            compiler_params=PARAMS,
            cost_estimate=cost(8 * half * width, 10 * half * width),
            name="merge",
        )(place, own, own_sum, *back)

    attended_outer = merge(back_outer, [(0, quarter), (rows - quarter, quarter)])
    attended_inner = merge(back_inner, [(quarter, half)])
    attended = jnp.concatenate([attended_outer[:quarter], attended_inner, attended_outer[quarter:]])

    chunks = 2
    columns = model // chunks
    tile = 512 if columns % 512 == 0 else columns
    last = ranks - 1
    arrived = [()] * chunks
    for step in range(last):
        if step == 0:
            source, blocks = attended_outer, jnp.array([half // block - 1, 0], jnp.int32)
        else:
            source = attended
            blocks = jnp.stack([jnp.minimum(last - step + rank, last), jnp.maximum(step + rank - last, 0)])
        for chunk in range(chunks):
            up, down = message(
                blocks, source, out_weight, arrived[chunk], chunk * columns, columns, block, tile
            )
            up = lax.ppermute(up, "tensor", [(i, i + 1) for i in range(step + 1)])
            down = lax.ppermute(down, "tensor", [(last - i, last - i - 1) for i in range(step + 1)])
            arrived[chunk] = (up, down)
    blocks = jnp.stack([rank, level])
    projected = own_projection(blocks, attended, out_weight, block, tile)
    result = ()
    for chunk in range(chunks):
        result = (final(blocks, projected, gate_table, *arrived[chunk], chunk * columns, columns // 2, result),)
    return result[0]


def solution(mesh):
    return jax.shard_map(
        body,
        mesh=mesh,
        in_specs=(
            P(("group", "span"), "tensor"),
            P(("group", "span"), "tensor"),
            P(("group", "span"), "tensor"),
            P("tensor", None),
            P(),
            P("group"),
            P("group", None),
        ),
        out_specs=P(("group", "span", "tensor"), None),
        check_vma=False,
    )
```

time: 128 us -> 120 us (0.938)
  the two profiles are of different devices: /device:TPU:0 before, /device:TPU:14 now
where the time goes in v2:
time: 120 us; the launch traced here: 118 us
  Pallas kernels  37.2 us (31%)
  starting transfers between devices  36.3 us (30%)
  waiting for transfers between devices  25.5 us (21%)
  local copies, waits for them, and re-layouts  17.3 us (14%)
  other arithmetic  1.73 us (1%)
    pallas_call x6, Pallas kernels, message(): pl.pallas_call(functools.partial(message_kernel, first, tile), in_specs=[...  16.8 us
    ppermute x6, starting transfers between devices, body(): up = lax.ppermute(up, 'tensor', [(i, i + 1) for i in range(step + 1)])  15.2 us
    unnamed x26, local copies, waits for them, and re-layouts  14 us
    ppermute x6, waiting for transfers between devices, body(): up = lax.ppermute(up, 'tensor', [(i, i + 1) for i in range(step + 1)])  13.9 us
    ppermute x6, starting transfers between devices, body(): lax.ppermute(down, 'tensor', [(last - i, last - i - 1) for i in range(ste...  12.7 us
    pallas_call x2, Pallas kernels, served(): pl.pallas_call(functools.partial(served_kernel, distance), in_specs=[SMEM...  7.91 us
    ppermute x4, starting transfers between devices, shifted(): lax.ppermute(block, axis, [(i, i + distance) for i in range(count) if 0 <...  7.82 us
    ppermute x4, waiting for transfers between devices, shifted(): lax.ppermute(block, axis, [(i, i + distance) for i in range(count) if 0 <...  6.95 us
  transfers between devices with their start and end apart: 18, of which 8 were waited for; matrix products, arithmetic and copies ran while one was open for 4% of the time, Pallas kernels for 27%

profile of v2, /device:TPU:14, one launch (start us, length us, event | category | flops | bytes accessed | tf_op | source)
XLA Modules:
  0.0 118.3 jit_solution(4723405851869554288)
XLA Ops:
  0.1 0.5 collective-permute-start.1
  0.6 1.0 fusion
  1.6 0.7 pad_maximum_fusion.1
  2.3 3.1 %collective-permute-start.2 = (bf16[192,768]{1,0:T(8,128)(2,1)}, bf16[192,768]{1,0:T(8,128)(2,1)}, u32[]{:S(2)}, u32[]{:S(2)}) collective-permute-start(bf16[192,768]{1,0:T(8,128)(2,1)} %pad_maximum_fusion.1), channel_id=1, source_target_pairs={{8,0},{12,4},{9,1},{13,5},{10,2},{14,6},{11,3},{15,7},{24,16},{28,... | collective-permute-start | bytes 884744 | tf_op jit(solution)/shard_map/ppermute | solution.py:26
  5.5 1.7 %slice.17 = bf16[192,768]{1,0:T(8,128)(2,1)} slice(bf16[384,768]{1,0:T(8,128)(2,1)} %query.1), slice={[96:288], [0:768]} | slice | bytes 589824 | tf_op jit(solution)/shard_map/slice | solution.py:224
  7.1 2.0 %collective-permute-start.3 = (bf16[192,768]{1,0:T(8,128)(2,1)}, bf16[192,768]{1,0:T(8,128)(2,1)}, u32[]{:S(2)}, u32[]{:S(2)}) collective-permute-start(bf16[192,768]{1,0:T(8,128)(2,1)} %slice.17), channel_id=1, source_target_pairs={{8,0},{12,4},{9,1},{13,5},{10,2},{14,6},{11,3},{15,7},{24,16},{28,... | collective-permute-start | bytes 884744 | tf_op jit(solution)/shard_map/ppermute | solution.py:26
  9.2 0.8 copy-done.7
  10.1 1.1 copy-done.8
  11.1 1.1 copy-done.9
  12.2 4.2 %local.1 = (f32[384,768]{1,0:T(8,128)S(1)}, f32[384,128]{1,0:T(8,128)S(1)}) custom-call(s32[2]{0:T(128)S(1)} %pad_add_fusion.1.place, s32[4,4]{1,0:T(4,128)S(1)} %copy-done.10, bf16[384,768]{1,0:T(8,128)(2,1)S(1)} %copy-done.9, bf16[384,768]{1,0:T(8,128)(2,1)S(1)} %copy-done.5, bf16[384,768]{1,0:T(8,128)(2,1)S(1)} %copy-done.6, ...), custom_call_target="tpu_custom_call" | custom-call | flops 905969664 | bytes 4128768 | tf_op jit(solution)/shard_map/local/pallas_call | solution.py:232
  16.4 1.5 %collective-permute-done.3.query = bf16[192,768]{1,0:T(8,128)(2,1)} collective-permute-done((bf16[192,768]{1,0:T(8,128)(2,1)}, bf16[192,768]{1,0:T(8,128)(2,1)}, u32[]{:S(2)}, u32[]{:S(2)}) %collective-permute-start.3) | collective-permute-done | bytes 294944 | tf_op jit(solution)/shard_map/ppermute | solution.py:26
  17.9 3.6 %served.2 = bf16[192,896]{1,0:T(8,128)(2,1)S(1)} custom-call(s32[2]{0:T(128)S(1)} %pad_add_fusion.1.place, s32[4,4]{1,0:T(4,128)S(1)} %copy-done.10, bf16[192,768]{1,0:T(8,128)(2,1)} %collective-permute-done.2.query, bf16[384,768]{1,0:T(8,128)(2,1)S(1)} %copy-done.5, bf16[384,768]{1,0:T(8,128)(2,1)S(1)} %copy-done.6, ...), custom_call_target="tpu_custom_call" | custom-call | flops 452984832 | bytes 3538944 | tf_op jit(solution)/shard_map/served/pallas_call | solution.py:246
  21.4 1.3 %collective-permute-start.4 = (bf16[192,896]{1,0:T(8,128)(2,1)S(1)}, bf16[192,896]{1,0:T(8,128)(2,1)S(1)}, u32[]{:S(2)}, u32[]{:S(2)}) collective-permute-start(bf16[192,896]{1,0:T(8,128)(2,1)S(1)} %served.2), channel_id=1, source_target_pairs={{0,8},{4,12},{1,9},{5,13},{2,10},{6,14},{3,11},{7,15},{16,24},{20,... | collective-permute-start | bytes 1032200 | tf_op jit(solution)/shard_map/ppermute | solution.py:26
  22.7 4.3 %served.3 = bf16[192,896]{1,0:T(8,128)(2,1)} custom-call(s32[2]{0:T(128)S(1)} %pad_add_fusion.1.place, s32[4,4]{1,0:T(4,128)S(1)} %copy-done.10, bf16[192,768]{1,0:T(8,128)(2,1)} %collective-permute-done.3.query, bf16[384,768]{1,0:T(8,128)(2,1)S(1)} %copy-done.5, bf16[384,768]{1,0:T(8,128)(2,1)S(1)} %copy-done.6, ...), custom_call_target="tpu_custom_call" | custom-call | flops 452984832 | bytes 3538944 | tf_op jit(solution)/shard_map/served/pallas_call | solution.py:246
  27.1 1.4 %collective-permute-start.5 = (bf16[192,896]{1,0:T(8,128)(2,1)}, bf16[192,896]{1,0:T(8,128)(2,1)}, u32[]{:S(2)}, u32[]{:S(2)}) collective-permute-start(bf16[192,896]{1,0:T(8,128)(2,1)} %served.3), channel_id=1, source_target_pairs={{0,8},{4,12},{1,9},{5,13},{2,10},{6,14},{3,11},{7,15},{16,24},{20,... | collective-permute-start | bytes 1032200 | tf_op jit(solution)/shard_map/ppermute | solution.py:26
  28.5 5.5 %collective-permute-done.4.refs_0_ = bf16[192,896]{1,0:T(8,128)(2,1)S(1)} collective-permute-done((bf16[192,896]{1,0:T(8,128)(2,1)S(1)}, bf16[192,896]{1,0:T(8,128)(2,1)S(1)}, u32[]{:S(2)}, u32[]{:S(2)}) %collective-permute-start.4) | collective-permute-done | bytes 344096 | tf_op jit(solution)/shard_map/ppermute | solution.py:26
  34.0 1.2 %merge.2.attended = bf16[192,768]{1,0:T(8,128)(2,1)S(1)} custom-call(s32[2]{0:T(128)S(1)} %pad_add_fusion.1.place, f32[384,768]{1,0:T(8,128)S(1)} %get-tuple-element.22.own, f32[384,128]{1,0:T(8,128)S(1)} %get-tuple-element.24.own_sum, bf16[192,896]{1,0:T(8,128)(2,1)S(1)} %collective-permute-done.4.refs_0_), custom_call_target="tpu_custom_call" | custom-call | flops 1179648 | bytes 1474560 | tf_op jit(solution)/shard_map/merge/pallas_call | solution.py:261
  35.2 2.6 %message.9 = (bf16[96,3072]{1,0:T(8,128)(2,1)}, bf16[96,3072]{1,0:T(8,128)(2,1)}) custom-call(s32[2]{0:T(128)S(1)} %copy-done.11, bf16[192,768]{1,0:T(8,128)(2,1)S(1)} %merge.2.attended, bf16[768,6144]{1,0:T(8,128)(2,1)S(1)} %copy-done), custom_call_target="tpu_custom_call" | custom-call | flops 905969664 | bytes 7077888 | tf_op jit(solution)/shard_map/message/pallas_call | solution.py:146
  37.9 1.3 %collective-permute-start.12 = (bf16[96,3072]{1,0:T(8,128)(2,1)}, bf16[96,3072]{1,0:T(8,128)(2,1)S(1)}, u32[]{:S(2)}, u32[]{:S(2)}) collective-permute-start(bf16[96,3072]{1,0:T(8,128)(2,1)} %get-tuple-element.33), channel_id=1, source_target_pairs={{0,1},{4,5},{8,9},{12,13},{16,17},{20,21},{24,25},{28,29}} | collective-permute-start | bytes 1769480 | tf_op jit(solution)/shard_map/ppermute | solution.py:290
  39.2 1.5 %collective-permute-start.13 = (bf16[96,3072]{1,0:T(8,128)(2,1)}, bf16[96,3072]{1,0:T(8,128)(2,1)}, u32[]{:S(2)}, u32[]{:S(2)}) collective-permute-start(bf16[96,3072]{1,0:T(8,128)(2,1)} %get-tuple-element.34), channel_id=1, source_target_pairs={{3,2},{7,6},{11,10},{15,14},{19,18},{23,22},{27,26},{31,30}} | collective-permute-start | bytes 1769480 | tf_op jit(solution)/shard_map/ppermute | solution.py:291
  40.7 2.6 %message.6 = (bf16[96,3072]{1,0:T(8,128)(2,1)}, bf16[96,3072]{1,0:T(8,128)(2,1)}) custom-call(s32[2]{0:T(128)S(1)} %copy-done.11, bf16[192,768]{1,0:T(8,128)(2,1)S(1)} %merge.2.attended, bf16[768,6144]{1,0:T(8,128)(2,1)S(1)} %copy-done), custom_call_target="tpu_custom_call" | custom-call | flops 905969664 | bytes 7077888 | tf_op jit(solution)/shard_map/message/pallas_call | solution.py:146
  43.3 1.3 %collective-permute-start.6 = (bf16[96,3072]{1,0:T(8,128)(2,1)}, bf16[96,3072]{1,0:T(8,128)(2,1)S(1)}, u32[]{:S(2)}, u32[]{:S(2)}) collective-permute-start(bf16[96,3072]{1,0:T(8,128)(2,1)} %get-tuple-element.27), channel_id=1, source_target_pairs={{0,1},{4,5},{8,9},{12,13},{16,17},{20,21},{24,25},{28,29}} | collective-permute-start | bytes 1769480 | tf_op jit(solution)/shard_map/ppermute | solution.py:290
  44.6 0.9 collective-permute-start.7
  45.6 1.5 %merge.3 = bf16[192,768]{1,0:T(8,128)(2,1)S(1)} custom-call(s32[2]{0:T(128)S(1)} %pad_add_fusion.1.place, f32[384,768]{1,0:T(8,128)S(1)} %get-tuple-element.22.own, f32[384,128]{1,0:T(8,128)S(1)} %get-tuple-element.24.own_sum, bf16[192,896]{1,0:T(8,128)(2,1)} %collective-permute-done.5.refs_0_), custom_call_target="tpu_custom_call" | custom-call | flops 1179648 | bytes 1474560 | tf_op jit(solution)/shard_map/merge/pallas_call | solution.py:261
  47.2 9.1 %collective-permute-done.12.refs_0_ = bf16[96,3072]{1,0:T(8,128)(2,1)S(1)} collective-permute-done((bf16[96,3072]{1,0:T(8,128)(2,1)}, bf16[96,3072]{1,0:T(8,128)(2,1)S(1)}, u32[]{:S(2)}, u32[]{:S(2)}) %collective-permute-start.12) | collective-permute-done | bytes 589856 | tf_op jit(solution)/shard_map/ppermute | solution.py:290
  56.2 3.7 %copy-done.1 = bf16[768,6144]{1,0:T(8,128)(2,1)S(1)} copy-done((bf16[768,6144]{1,0:T(8,128)(2,1)S(1)}, bf16[768,6144]{1,0:T(8,128)(2,1)}, u32[]{:S(2)}) %copy-start.1) | copy-done | bytes 9437208
  59.9 3.2 %message.10 = (bf16[96,3072]{1,0:T(8,128)(2,1)}, bf16[96,3072]{1,0:T(8,128)(2,1)}) custom-call(s32[2]{0:T(128)S(1)} %pad_add_fusion.3.blocks, bf16[384,768]{1,0:T(8,128)(2,1)S(1)} %pad_maximum_fusion.attended, bf16[768,6144]{1,0:T(8,128)(2,1)S(1)} %copy-done.1, bf16[96,3072]{1,0:T(8,128)(2,1)S(1)} %collective-permute-done.12.refs_0_, ...), custom_call_target="tpu_custom_call" | custom-call | flops 905969664 | bytes 7077888 | tf_op jit(solution)/shard_map/message/pallas_call | solution.py:146
  63.1 4.3 %collective-permute-start.14 = (bf16[96,3072]{1,0:T(8,128)(2,1)}, bf16[96,3072]{1,0:T(8,128)(2,1)S(1)}, u32[]{:S(2)}, u32[]{:S(2)}) collective-permute-start(bf16[96,3072]{1,0:T(8,128)(2,1)} %get-tuple-element.35), channel_id=1, source_target_pairs={{0,1},{1,2},{4,5},{5,6},{8,9},{9,10},{12,13},{13,14},{16,17},{17,1... | collective-permute-start | bytes 1769480 | tf_op jit(solution)/shard_map/ppermute | solution.py:290
  67.4 1.3 %collective-permute-start.15 = (bf16[96,3072]{1,0:T(8,128)(2,1)}, bf16[96,3072]{1,0:T(8,128)(2,1)S(1)}, u32[]{:S(2)}, u32[]{:S(2)}) collective-permute-start(bf16[96,3072]{1,0:T(8,128)(2,1)} %get-tuple-element.36), channel_id=1, source_target_pairs={{3,2},{2,1},{7,6},{6,5},{11,10},{10,9},{15,14},{14,13},{19,18},{18... | collective-permute-start | bytes 1769480 | tf_op jit(solution)/shard_map/ppermute | solution.py:291
  68.9 2.7 %message.7 = (bf16[96,3072]{1,0:T(8,128)(2,1)}, bf16[96,3072]{1,0:T(8,128)(2,1)}) custom-call(s32[2]{0:T(128)S(1)} %pad_add_fusion.3.blocks, bf16[384,768]{1,0:T(8,128)(2,1)S(1)} %pad_maximum_fusion.attended, bf16[768,6144]{1,0:T(8,128)(2,1)S(1)} %copy-done.1, bf16[96,3072]{1,0:T(8,128)(2,1)S(1)} %collective-permute-done.6.refs_0_, ...), custom_call_target="tpu_custom_call" | custom-call | flops 905969664 | bytes 7077888 | tf_op jit(solution)/shard_map/message/pallas_call | solution.py:146
  71.6 4.4 %collective-permute-start.8 = (bf16[96,3072]{1,0:T(8,128)(2,1)}, bf16[96,3072]{1,0:T(8,128)(2,1)S(1)}, u32[]{:S(2)}, u32[]{:S(2)}) collective-permute-start(bf16[96,3072]{1,0:T(8,128)(2,1)} %get-tuple-element.29), channel_id=1, source_target_pairs={{0,1},{1,2},{4,5},{5,6},{8,9},{9,10},{12,13},{13,14},{16,17},{17,1... | collective-permute-start | bytes 1769480 | tf_op jit(solution)/shard_map/ppermute | solution.py:290
  75.9 1.3 %collective-permute-start.9 = (bf16[96,3072]{1,0:T(8,128)(2,1)}, bf16[96,3072]{1,0:T(8,128)(2,1)}, u32[]{:S(2)}, u32[]{:S(2)}) collective-permute-start(bf16[96,3072]{1,0:T(8,128)(2,1)} %get-tuple-element.30), channel_id=1, source_target_pairs={{3,2},{2,1},{7,6},{6,5},{11,10},{10,9},{15,14},{14,13},{19,18},{18... | collective-permute-start | bytes 1769480 | tf_op jit(solution)/shard_map/ppermute | solution.py:291
  77.3 4.2 %collective-permute-done.14.refs_0_ = bf16[96,3072]{1,0:T(8,128)(2,1)S(1)} collective-permute-done((bf16[96,3072]{1,0:T(8,128)(2,1)}, bf16[96,3072]{1,0:T(8,128)(2,1)S(1)}, u32[]{:S(2)}, u32[]{:S(2)}) %collective-permute-start.14) | collective-permute-done | bytes 589856 | tf_op jit(solution)/shard_map/ppermute | solution.py:290
  81.5 3.5 %collective-permute-done.15.refs_1_ = bf16[96,3072]{1,0:T(8,128)(2,1)S(1)} collective-permute-done((bf16[96,3072]{1,0:T(8,128)(2,1)}, bf16[96,3072]{1,0:T(8,128)(2,1)S(1)}, u32[]{:S(2)}, u32[]{:S(2)}) %collective-permute-start.15) | collective-permute-done | bytes 589856 | tf_op jit(solution)/shard_map/ppermute | solution.py:291
  85.0 3.7 %copy-done.2 = bf16[768,6144]{1,0:T(8,128)(2,1)S(1)} copy-done((bf16[768,6144]{1,0:T(8,128)(2,1)S(1)}, bf16[768,6144]{1,0:T(8,128)(2,1)}, u32[]{:S(2)}) %copy-start.2) | copy-done | bytes 9437208
  88.7 2.6 %message.11 = (bf16[96,3072]{1,0:T(8,128)(2,1)}, bf16[96,3072]{1,0:T(8,128)(2,1)}) custom-call(s32[2]{0:T(128)S(1)} %pad_add_fusion.2.blocks, bf16[384,768]{1,0:T(8,128)(2,1)S(1)} %pad_maximum_fusion.attended, bf16[768,6144]{1,0:T(8,128)(2,1)S(1)} %copy-done.2, bf16[96,3072]{1,0:T(8,128)(2,1)S(1)} %collective-permute-done.14.refs_0_, ...), custom_call_target="tpu_custom_call" | custom-call | flops 905969664 | bytes 7077888 | tf_op jit(solution)/shard_map/message/pallas_call | solution.py:146
  91.3 2.0 %collective-permute-start.16 = (bf16[96,3072]{1,0:T(8,128)(2,1)}, bf16[96,3072]{1,0:T(8,128)(2,1)S(1)}, u32[]{:S(2)}, u32[]{:S(2)}) collective-permute-start(bf16[96,3072]{1,0:T(8,128)(2,1)} %get-tuple-element.37), channel_id=1, source_target_pairs={{0,1},{1,2},{2,3},{4,5},{5,6},{6,7},{8,9},{9,10},{10,11},{12,13},{... | collective-permute-start | bytes 1769480 | tf_op jit(solution)/shard_map/ppermute | solution.py:290
  93.4 3.9 %collective-permute-start.17 = (bf16[96,3072]{1,0:T(8,128)(2,1)}, bf16[96,3072]{1,0:T(8,128)(2,1)S(1)}, u32[]{:S(2)}, u32[]{:S(2)}) collective-permute-start(bf16[96,3072]{1,0:T(8,128)(2,1)} %get-tuple-element.38), channel_id=1, source_target_pairs={{3,2},{2,1},{1,0},{7,6},{6,5},{5,4},{11,10},{10,9},{9,8},{15,14},{... | collective-permute-start | bytes 1769480 | tf_op jit(solution)/shard_map/ppermute | solution.py:291
  97.3 3.0 %message.8 = (bf16[96,3072]{1,0:T(8,128)(2,1)}, bf16[96,3072]{1,0:T(8,128)(2,1)S(1)}) custom-call(s32[2]{0:T(128)S(1)} %pad_add_fusion.2.blocks, bf16[384,768]{1,0:T(8,128)(2,1)S(1)} %pad_maximum_fusion.attended, bf16[768,6144]{1,0:T(8,128)(2,1)S(1)} %copy-done.2, bf16[96,3072]{1,0:T(8,128)(2,1)S(1)} %collective-permute-done.8.refs_0_, ...), custom_call_target="tpu_custom_call" | custom-call | flops 905969664 | bytes 7077888 | tf_op jit(solution)/shard_map/message/pallas_call | solution.py:146
  100.3 2.1 %collective-permute-start.10 = (bf16[96,3072]{1,0:T(8,128)(2,1)}, bf16[96,3072]{1,0:T(8,128)(2,1)S(1)}, u32[]{:S(2)}, u32[]{:S(2)}) collective-permute-start(bf16[96,3072]{1,0:T(8,128)(2,1)} %get-tuple-element.31), channel_id=1, source_target_pairs={{0,1},{1,2},{2,3},{4,5},{5,6},{6,7},{8,9},{9,10},{10,11},{12,13},{... | collective-permute-start | bytes 1769480 | tf_op jit(solution)/shard_map/ppermute | solution.py:290
  102.3 3.8 %collective-permute-start.11 = (bf16[96,3072]{1,0:T(8,128)(2,1)S(1)}, bf16[96,3072]{1,0:T(8,128)(2,1)S(1)}, u32[]{:S(2)}, u32[]{:S(2)}) collective-permute-start(bf16[96,3072]{1,0:T(8,128)(2,1)S(1)} %get-tuple-element.32), channel_id=1, source_target_pairs={{3,2},{2,1},{1,0},{7,6},{6,5},{5,4},{11,10},{10,9},{9,8},{15,14},{... | collective-permute-start | bytes 1769480 | tf_op jit(solution)/shard_map/ppermute | solution.py:291
  106.2 0.6 dynamic_slice.3
  106.7 0.7 pad_add_fusion.blocks
  107.5 3.7 %copy-done.3 = bf16[768,6144]{1,0:T(8,128)(2,1)S(1)} copy-done((bf16[768,6144]{1,0:T(8,128)(2,1)S(1)}, bf16[768,6144]{1,0:T(8,128)(2,1)}, u32[]{:S(2)}) %copy-start.3) | copy-done | bytes 9437208
  111.1 2.2 %own.1 = f32[96,6144]{1,0:T(8,128)S(1)} custom-call(s32[2]{0:T(128)S(1)} %pad_add_fusion.blocks, bf16[384,768]{1,0:T(8,128)(2,1)S(1)} %pad_maximum_fusion.attended, bf16[768,6144]{1,0:T(8,128)(2,1)S(1)} %copy-done.3), custom_call_target="tpu_custom_call" | custom-call | flops 905969664 | bytes 11796480 | tf_op jit(solution)/shard_map/own/pallas_call | solution.py:167
  113.4 1.7 %final.2.refs_0_ = bf16[96,6144]{1,0:T(8,128)(2,1)} custom-call(s32[2]{0:T(128)S(1)} %pad_add_fusion.blocks, f32[96,6144]{1,0:T(8,128)S(1)} %own.1, f32[64,6144]{1,0:T(8,128)S(1)} %copy-done.4, bf16[96,3072]{1,0:T(8,128)(2,1)S(1)} %collective-permute-done.16.up, bf16[96,3072]{1,0:T(8,128)(2,1)S(1)} %collective-permute-done.17.down), custom_call_target="tpu_custom_call" | custom-call | flops 1179648 | bytes 2949120 | tf_op jit(solution)/shard_map/final/pallas_call | solution.py:189
  115.5 1.1 collective-permute-done.11.down
  116.6 1.7 %final.3 = bf16[96,6144]{1,0:T(8,128)(2,1)} custom-call(s32[2]{0:T(128)S(1)} %pad_add_fusion.blocks, f32[96,6144]{1,0:T(8,128)S(1)} %own.1, f32[64,6144]{1,0:T(8,128)S(1)} %copy-done.4, bf16[96,3072]{1,0:T(8,128)(2,1)S(1)} %collective-permute-done.10.up, bf16[96,3072]{1,0:T(8,128)(2,1)S(1)} %collective-permute-done.11.down, ...), custom_call_target="tpu_custom_call", output_to_operand_aliasing={{}: (5, {})} | custom-call | flops 1179648 | bytes 2949120 | tf_op jit(solution)/shard_map/final/pallas_call | solution.py:189
  (38 shorter events, 1.0 us)
Async XLA Ops:
  0.0 10.0 %copy-start.5 = (bf16[384,768]{1,0:T(8,128)(2,1)S(1)}, bf16[384,768]{1,0:T(8,128)(2,1)}, u32[]{:S(2)}) copy-start(bf16[384,768]{1,0:T(8,128)(2,1)} %key.5) | copy-start | bytes 1769476
  0.0 10.0 %copy-start.6 = (bf16[384,768]{1,0:T(8,128)(2,1)S(1)}, bf16[384,768]{1,0:T(8,128)(2,1)}, u32[]{:S(2)}) copy-start(bf16[384,768]{1,0:T(8,128)(2,1)} %value.5) | copy-start | bytes 1769476
  0.0 10.0 %copy-start.10 = (s32[4,4]{1,0:T(4,128)S(1)}, s32[4,4]{1,0:T(4,128)}, u32[]{:S(2)}) copy-start(s32[4,4]{1,0:T(4,128)} %visible.5) | copy-start | bytes 196
  0.0 9.2 %collective-permute-start = (bf16[384,768]{1,0:T(8,128)(2,1)}, bf16[384,768]{1,0:T(8,128)(2,1)S(1)}, u32[]{:S(2)}, u32[]{:S(2)}) collective-permute-start(bf16[384,768]{1,0:T(8,128)(2,1)} %key.5), channel_id=1, source_target_pairs={{0,4},{4,0},{8,12},{12,8},{1,5},{5,1},{9,13},{13,9},{2,6},{6,2},{1... | collective-permute-start | bytes 1769480 | tf_op jit(solution)/shard_map/ppermute | solution.py:228
  0.1 9.1 %collective-permute-start.1 = (bf16[384,768]{1,0:T(8,128)(2,1)}, bf16[384,768]{1,0:T(8,128)(2,1)S(1)}, u32[]{:S(2)}, u32[]{:S(2)}) collective-permute-start(bf16[384,768]{1,0:T(8,128)(2,1)} %value.5), channel_id=1, source_target_pairs={{0,4},{4,0},{8,12},{12,8},{1,5},{5,1},{9,13},{13,9},{2,6},{6,2},{1... | collective-permute-start | bytes 1769480 | tf_op jit(solution)/shard_map/ppermute | solution.py:229
  2.3 14.1 %collective-permute-start.2 = (bf16[192,768]{1,0:T(8,128)(2,1)}, bf16[192,768]{1,0:T(8,128)(2,1)}, u32[]{:S(2)}, u32[]{:S(2)}) collective-permute-start(bf16[192,768]{1,0:T(8,128)(2,1)} %pad_maximum_fusion.1), channel_id=1, source_target_pairs={{8,0},{12,4},{9,1},{13,5},{10,2},{14,6},{11,3},{15,7},{24,16},{28,... | collective-permute-start | bytes 884744 | tf_op jit(solution)/shard_map/ppermute | solution.py:26
  7.1 10.7 %collective-permute-start.3 = (bf16[192,768]{1,0:T(8,128)(2,1)}, bf16[192,768]{1,0:T(8,128)(2,1)}, u32[]{:S(2)}, u32[]{:S(2)}) collective-permute-start(bf16[192,768]{1,0:T(8,128)(2,1)} %slice.17), channel_id=1, source_target_pairs={{8,0},{12,4},{9,1},{13,5},{10,2},{14,6},{11,3},{15,7},{24,16},{28,... | collective-permute-start | bytes 884744 | tf_op jit(solution)/shard_map/ppermute | solution.py:26
  9.2 0.8 copy-start.7
  10.1 1.1 copy-start.8
  11.1 1.1 copy-start.9
  12.2 23.0 %copy-start = (bf16[768,6144]{1,0:T(8,128)(2,1)S(1)}, bf16[768,6144]{1,0:T(8,128)(2,1)}, u32[]{:S(2)}) copy-start(bf16[768,6144]{1,0:T(8,128)(2,1)} %weight.13) | copy-start | bytes 28311556
  21.4 12.5 %collective-permute-start.4 = (bf16[192,896]{1,0:T(8,128)(2,1)S(1)}, bf16[192,896]{1,0:T(8,128)(2,1)S(1)}, u32[]{:S(2)}, u32[]{:S(2)}) collective-permute-start(bf16[192,896]{1,0:T(8,128)(2,1)S(1)} %served.2), channel_id=1, source_target_pairs={{0,8},{4,12},{1,9},{5,13},{2,10},{6,14},{3,11},{7,15},{16,24},{20,... | collective-permute-start | bytes 1032200 | tf_op jit(solution)/shard_map/ppermute | solution.py:26
  27.1 8.1 %copy-start.11 = (s32[2]{0:T(128)S(1)}, s32[2]{0:T(128)}, u32[]{:S(2)}) copy-start(s32[2]{0:T(128)} %constant.25.clone.blocks) | copy-start | bytes 28
  27.1 18.5 %collective-permute-start.5 = (bf16[192,896]{1,0:T(8,128)(2,1)}, bf16[192,896]{1,0:T(8,128)(2,1)}, u32[]{:S(2)}, u32[]{:S(2)}) collective-permute-start(bf16[192,896]{1,0:T(8,128)(2,1)} %served.3), channel_id=1, source_target_pairs={{0,8},{4,12},{1,9},{5,13},{2,10},{6,14},{3,11},{7,15},{16,24},{20,... | collective-permute-start | bytes 1032200 | tf_op jit(solution)/shard_map/ppermute | solution.py:26
  37.9 18.4 %collective-permute-start.12 = (bf16[96,3072]{1,0:T(8,128)(2,1)}, bf16[96,3072]{1,0:T(8,128)(2,1)S(1)}, u32[]{:S(2)}, u32[]{:S(2)}) collective-permute-start(bf16[96,3072]{1,0:T(8,128)(2,1)} %get-tuple-element.33), channel_id=1, source_target_pairs={{0,1},{4,5},{8,9},{12,13},{16,17},{20,21},{24,25},{28,29}} | collective-permute-start | bytes 1769480 | tf_op jit(solution)/shard_map/ppermute | solution.py:290
  39.2 17.1 %collective-permute-start.13 = (bf16[96,3072]{1,0:T(8,128)(2,1)}, bf16[96,3072]{1,0:T(8,128)(2,1)}, u32[]{:S(2)}, u32[]{:S(2)}) collective-permute-start(bf16[96,3072]{1,0:T(8,128)(2,1)} %get-tuple-element.34), channel_id=1, source_target_pairs={{3,2},{7,6},{11,10},{15,14},{19,18},{23,22},{27,26},{31,30}} | collective-permute-start | bytes 1769480 | tf_op jit(solution)/shard_map/ppermute | solution.py:291
  43.3 25.5 %collective-permute-start.6 = (bf16[96,3072]{1,0:T(8,128)(2,1)}, bf16[96,3072]{1,0:T(8,128)(2,1)S(1)}, u32[]{:S(2)}, u32[]{:S(2)}) collective-permute-start(bf16[96,3072]{1,0:T(8,128)(2,1)} %get-tuple-element.27), channel_id=1, source_target_pairs={{0,1},{4,5},{8,9},{12,13},{16,17},{20,21},{24,25},{28,29}} | collective-permute-start | bytes 1769480 | tf_op jit(solution)/shard_map/ppermute | solution.py:290
  44.6 24.3 %collective-permute-start.7 = (bf16[96,3072]{1,0:T(8,128)(2,1)}, bf16[96,3072]{1,0:T(8,128)(2,1)S(1)}, u32[]{:S(2)}, u32[]{:S(2)}) collective-permute-start(bf16[96,3072]{1,0:T(8,128)(2,1)} %get-tuple-element.28), channel_id=1, source_target_pairs={{3,2},{7,6},{11,10},{15,14},{19,18},{23,22},{27,26},{31,30}} | collective-permute-start | bytes 1769480 | tf_op jit(solution)/shard_map/ppermute | solution.py:291
  56.2 3.7 %copy-start.1 = (bf16[768,6144]{1,0:T(8,128)(2,1)S(1)}, bf16[768,6144]{1,0:T(8,128)(2,1)}, u32[]{:S(2)}) copy-start(bf16[768,6144]{1,0:T(8,128)(2,1)} %weight.13) | copy-start | bytes 28311556
  63.1 18.4 %collective-permute-start.14 = (bf16[96,3072]{1,0:T(8,128)(2,1)}, bf16[96,3072]{1,0:T(8,128)(2,1)S(1)}, u32[]{:S(2)}, u32[]{:S(2)}) collective-permute-start(bf16[96,3072]{1,0:T(8,128)(2,1)} %get-tuple-element.35), channel_id=1, source_target_pairs={{0,1},{1,2},{4,5},{5,6},{8,9},{9,10},{12,13},{13,14},{16,17},{17,1... | collective-permute-start | bytes 1769480 | tf_op jit(solution)/shard_map/ppermute | solution.py:290
  67.4 17.7 %collective-permute-start.15 = (bf16[96,3072]{1,0:T(8,128)(2,1)}, bf16[96,3072]{1,0:T(8,128)(2,1)S(1)}, u32[]{:S(2)}, u32[]{:S(2)}) collective-permute-start(bf16[96,3072]{1,0:T(8,128)(2,1)} %get-tuple-element.36), channel_id=1, source_target_pairs={{3,2},{2,1},{7,6},{6,5},{11,10},{10,9},{15,14},{14,13},{19,18},{18... | collective-permute-start | bytes 1769480 | tf_op jit(solution)/shard_map/ppermute | solution.py:291
  71.6 25.7 %collective-permute-start.8 = (bf16[96,3072]{1,0:T(8,128)(2,1)}, bf16[96,3072]{1,0:T(8,128)(2,1)S(1)}, u32[]{:S(2)}, u32[]{:S(2)}) collective-permute-start(bf16[96,3072]{1,0:T(8,128)(2,1)} %get-tuple-element.29), channel_id=1, source_target_pairs={{0,1},{1,2},{4,5},{5,6},{8,9},{9,10},{12,13},{13,14},{16,17},{17,1... | collective-permute-start | bytes 1769480 | tf_op jit(solution)/shard_map/ppermute | solution.py:290
  75.9 21.3 %collective-permute-start.9 = (bf16[96,3072]{1,0:T(8,128)(2,1)}, bf16[96,3072]{1,0:T(8,128)(2,1)}, u32[]{:S(2)}, u32[]{:S(2)}) collective-permute-start(bf16[96,3072]{1,0:T(8,128)(2,1)} %get-tuple-element.30), channel_id=1, source_target_pairs={{3,2},{2,1},{7,6},{6,5},{11,10},{10,9},{15,14},{14,13},{19,18},{18... | collective-permute-start | bytes 1769480 | tf_op jit(solution)/shard_map/ppermute | solution.py:291
  85.0 3.7 %copy-start.2 = (bf16[768,6144]{1,0:T(8,128)(2,1)S(1)}, bf16[768,6144]{1,0:T(8,128)(2,1)}, u32[]{:S(2)}) copy-start(bf16[768,6144]{1,0:T(8,128)(2,1)} %weight.13) | copy-start | bytes 28311556
  91.3 22.0 %collective-permute-start.16 = (bf16[96,3072]{1,0:T(8,128)(2,1)}, bf16[96,3072]{1,0:T(8,128)(2,1)S(1)}, u32[]{:S(2)}, u32[]{:S(2)}) collective-permute-start(bf16[96,3072]{1,0:T(8,128)(2,1)} %get-tuple-element.37), channel_id=1, source_target_pairs={{0,1},{1,2},{2,3},{4,5},{5,6},{6,7},{8,9},{9,10},{10,11},{12,13},{... | collective-permute-start | bytes 1769480 | tf_op jit(solution)/shard_map/ppermute | solution.py:290
  93.4 12.8 %copy-start.12 = (s32[4]{0:T(128)S(1)}, s32[4]{0:T(128)}, u32[]{:S(2)}) copy-start(s32[4]{0:T(128)} %param.13) | copy-start | bytes 52
  93.4 20.0 %collective-permute-start.17 = (bf16[96,3072]{1,0:T(8,128)(2,1)}, bf16[96,3072]{1,0:T(8,128)(2,1)S(1)}, u32[]{:S(2)}, u32[]{:S(2)}) collective-permute-start(bf16[96,3072]{1,0:T(8,128)(2,1)} %get-tuple-element.38), channel_id=1, source_target_pairs={{3,2},{2,1},{1,0},{7,6},{6,5},{5,4},{11,10},{10,9},{9,8},{15,14},{... | collective-permute-start | bytes 1769480 | tf_op jit(solution)/shard_map/ppermute | solution.py:291
  100.3 15.2 %collective-permute-start.10 = (bf16[96,3072]{1,0:T(8,128)(2,1)}, bf16[96,3072]{1,0:T(8,128)(2,1)S(1)}, u32[]{:S(2)}, u32[]{:S(2)}) collective-permute-start(bf16[96,3072]{1,0:T(8,128)(2,1)} %get-tuple-element.31), channel_id=1, source_target_pairs={{0,1},{1,2},{2,3},{4,5},{5,6},{6,7},{8,9},{9,10},{10,11},{12,13},{... | collective-permute-start | bytes 1769480 | tf_op jit(solution)/shard_map/ppermute | solution.py:290
  102.3 14.3 %collective-permute-start.11 = (bf16[96,3072]{1,0:T(8,128)(2,1)S(1)}, bf16[96,3072]{1,0:T(8,128)(2,1)S(1)}, u32[]{:S(2)}, u32[]{:S(2)}) collective-permute-start(bf16[96,3072]{1,0:T(8,128)(2,1)S(1)} %get-tuple-element.32), channel_id=1, source_target_pairs={{3,2},{2,1},{1,0},{7,6},{6,5},{5,4},{11,10},{10,9},{9,8},{15,14},{... | collective-permute-start | bytes 1769480 | tf_op jit(solution)/shard_map/ppermute | solution.py:291
  107.5 3.7 %copy-start.3 = (bf16[768,6144]{1,0:T(8,128)(2,1)S(1)}, bf16[768,6144]{1,0:T(8,128)(2,1)}, u32[]{:S(2)}) copy-start(bf16[768,6144]{1,0:T(8,128)(2,1)} %weight.13) | copy-start | bytes 28311556
  111.1 2.3 %copy-start.4 = (f32[64,6144]{1,0:T(8,128)S(1)}, f32[64,6144]{1,0:T(8,128)}, u32[]{:S(2)}) copy-start(f32[64,6144]{1,0:T(8,128)} %gate.3) | copy-start | bytes 4718596

commit v3 on v2

--- a/solution.py
+++ b/solution.py
@@ -11,7 +11,8 @@
 LANES = 128
 HIDDEN = -1e30
 LOG2E = 1.4426950408889634
-PARAMS = pltpu.CompilerParams(vmem_limit_bytes=20 * 1024 * 1024)
+PARAMS = pltpu.CompilerParams(vmem_limit_bytes=4 * 1024 * 1024)
+ATTEND_PARAMS = pltpu.CompilerParams(vmem_limit_bytes=8 * 1024 * 1024)
 SMEM = pl.BlockSpec(memory_space=pltpu.SMEM)
 VMEM = pl.BlockSpec(memory_space=pltpu.VMEM)
 PIECE_LANES = 32
@@ -66,6 +67,23 @@
     return span + 1 - 2 * lax.rem(span, 2)
 
 
+def split_kernel(query, outer, inner, semaphores):
+    rows = query.shape[0]
+    quarter = rows // 4
+    copies = [
+        pltpu.make_async_copy(query.at[pl.ds(start, size)], target.at[pl.ds(at, size)], semaphores.at[index])
+        for index, (start, size, target, at) in enumerate((
+            (0, quarter, outer, 0),
+            (rows - quarter, quarter, outer, quarter),
+            (quarter, rows - 2 * quarter, inner, 0),
+        ))
+    ]
+    for copy in copies:
+        copy.start()
+    for copy in copies:
+        copy.wait()
+
+
 def local_kernel(place, visible, query, key, value, key_beside, value_beside, result, sums):
     span = place[0]
 
@@ -126,30 +144,30 @@
     return attended[pl.ds(pl.multiple_of(index * rows, rows), rows), :]
 
 
-def message_kernel(first, tile, blocks, attended, weight, *refs):
-    ups, downs = refs[-2:]
-    rows, columns = ups.shape
-    both = jnp.concatenate([rows_at(attended, blocks[0], rows), rows_at(attended, blocks[1], rows)], axis=0)
-    for at in range(0, columns, tile):
-        here = slice(at, at + tile)
-        product = jnp.dot(both, weight[:, first + at:first + at + tile], preferred_element_type=jnp.float32)
-        up, down = product[:rows], product[rows:]
-        if len(refs) == 4:
-            up = up + refs[0][:, here].astype(jnp.float32)
-            down = down + refs[1][:, here].astype(jnp.float32)
-        ups[:, here] = up.astype(jnp.bfloat16)
-        downs[:, here] = down.astype(jnp.bfloat16)
-
-
-def message(blocks, attended, weight, arrived, first, columns, rows, tile):
+def message_kernel(hop, first, tile, blocks, attended, weight, *refs):
+    result = refs[-1]
+    rows, columns = result.shape
+
+    @pl.when(blocks[1] > 0)
+    def _():
+        mine = rows_at(attended, blocks[0], rows)
+        for at in range(0, columns, tile):
+            here = slice(at, at + tile)
+            product = jnp.dot(mine, weight[:, first + at:first + at + tile], preferred_element_type=jnp.float32)
+            if len(refs) == 2:
+                product = product + refs[0][:, here].astype(jnp.float32)
+            result[:, here] = product.astype(jnp.bfloat16)
+
+
+def message(hop, blocks, attended, weight, arrived, first, columns, rows, tile):
     width = attended.shape[1]
     return pl.pallas_call(
-        functools.partial(message_kernel, first, tile),
+        functools.partial(message_kernel, hop, first, tile),
         in_specs=[SMEM] + [VMEM] * (2 + len(arrived)),
-        out_specs=[VMEM, VMEM],
-        out_shape=[jax.ShapeDtypeStruct((rows, columns), jnp.bfloat16)] * 2,
+        out_specs=VMEM,
+        out_shape=jax.ShapeDtypeStruct((rows, columns), jnp.bfloat16),
         compiler_params=PARAMS,
-        cost_estimate=cost(4 * rows * width * columns, 2 * width * columns + 8 * rows * columns),
+        cost_estimate=cost(2 * rows * width * columns, 2 * width * columns + 4 * rows * columns),
         name="message",
     )(blocks, attended, weight, *arrived)
 
@@ -175,36 +193,33 @@
     )(blocks, attended, weight)
 
 
-def final_kernel(blocks, own, gate, up, down, *refs):
+def final_kernel(count, blocks, own, gate, *refs):
     result = refs[-1]
-    summed = own[...] + up[...].astype(jnp.float32) + down[...].astype(jnp.float32)
+    summed = own[...] + sum(ref[...].astype(jnp.float32) for ref in refs[:count])
     result[...] = (summed * gate[pl.ds(lax.rem(blocks[1], 8), 1), :]).astype(jnp.bfloat16)
 
 
-def final(blocks, own, gate_table, up, down, first, tile, before):
-    rows, columns = up.shape
+def final(blocks, own, gate_table, comes, first, tile, before):
+    rows, columns = comes[0].shape
     start = first // tile
     there = pl.BlockSpec((rows, tile), lambda j, b: (0, start + j))
     piece = pl.BlockSpec((rows, tile), lambda j, b: (0, j))
     return pl.pallas_call(
-        final_kernel,
+        functools.partial(final_kernel, len(comes)),
         grid_spec=pltpu.PrefetchScalarGridSpec(
             num_scalar_prefetch=1,
             grid=(columns // tile,),
-            in_specs=[
-                there,
-                pl.BlockSpec((8, tile), lambda j, b: (b[1] // 8, start + j)),
-                piece,
-                piece,
-            ] + [pl.BlockSpec(memory_space=pl.ANY)] * len(before),
+            in_specs=[there, pl.BlockSpec((8, tile), lambda j, b: (b[1] // 8, start + j))]
+            + [piece] * len(comes)
+            + [pl.BlockSpec(memory_space=pl.ANY)] * len(before),
             out_specs=there,
         ),
         out_shape=jax.ShapeDtypeStruct(own.shape, jnp.bfloat16),
-        input_output_aliases={5: 0} if before else {},
+        input_output_aliases={3 + len(comes): 0} if before else {},
         compiler_params=PARAMS,
         cost_estimate=cost(4 * rows * columns, 10 * rows * columns),
         name="final",
-    )(blocks, own, gate_table, up, down, *before)
+    )(blocks, own, gate_table, *comes, *before)
 
 
 def body(queries, keys, values, out_weight, gate_table, levels, visible):
@@ -220,14 +235,21 @@
     place = jnp.stack([span, rank]).astype(jnp.int32)
     level = levels[span]
 
-    query_outer = jnp.concatenate([queries[:quarter], queries[rows - quarter:]])
-    query_inner = queries[quarter:rows - quarter]
+    query_outer, query_inner = pl.pallas_call(
+        split_kernel,
+        in_specs=[pl.BlockSpec(memory_space=pl.ANY)],
+        out_specs=[VMEM, VMEM],
+        out_shape=[jax.ShapeDtypeStruct((half, width), queries.dtype)] * 2,
+        scratch_shapes=[pltpu.SemaphoreType.DMA((3,))],
+        compiler_params=PARAMS,
+        cost_estimate=cost(0, 4 * rows * width),
+        name="split",
+    )(queries)
     distances = list(range(2, spans, 2))
     asked_outer = [shifted(query_outer, "span", -distance) for distance in distances]
     swap = [(i, i + 1 - 2 * (i % 2)) for i in range(spans)]
     key_beside = lax.ppermute(keys, "span", swap)
     value_beside = lax.ppermute(values, "span", swap)
-    asked_inner = [shifted(query_inner, "span", -distance) for distance in distances]
 
     own, own_sum = pl.pallas_call(
         local_kernel,
@@ -237,7 +259,7 @@
             jax.ShapeDtypeStruct((rows, width), jnp.float32),
             jax.ShapeDtypeStruct((rows, LANES), jnp.float32),
         ],
-        compiler_params=PARAMS,
+        compiler_params=ATTEND_PARAMS,
         cost_estimate=cost(8 * rows * rows * width, 14 * rows * width, 2 * rows * rows * width // HD),
         name="local",
     )(place, visible, queries, keys, values, key_beside, value_beside)
@@ -248,13 +270,16 @@
             in_specs=[SMEM, SMEM] + [VMEM] * 5,
             out_specs=VMEM,
             out_shape=jax.ShapeDtypeStruct((half, width + LANES), jnp.bfloat16),
-            compiler_params=PARAMS,
+            compiler_params=ATTEND_PARAMS,
             cost_estimate=cost(8 * half * rows * width, 12 * rows * width, 2 * half * rows * width // HD),
             name="served",
         )(place, visible, asked, keys, values, key_beside, value_beside)
 
-    asked_outer, asked_inner, own_sum = lax.optimization_barrier((asked_outer, asked_inner, own_sum))
-    back_outer = [shifted(served(q, d), "span", d) for q, d in zip(asked_outer, distances)]
+    asked_outer, query_inner, own_sum = lax.optimization_barrier((asked_outer, query_inner, own_sum))
+    asked_inner = [shifted(query_inner, "span", -distance) for distance in distances]
+    out_outer = [served(q, d) for q, d in zip(asked_outer, distances)]
+    back_outer = [shifted(o, "span", d) for o, d in zip(out_outer, distances)]
+    asked_inner, out_outer = lax.optimization_barrier((asked_inner, out_outer))
     back_inner = [shifted(served(q, d), "span", d) for q, d in zip(asked_inner, distances)]
 
     def merge(back, pieces):
@@ -272,29 +297,39 @@
     attended_inner = merge(back_inner, [(quarter, half)])
     attended = jnp.concatenate([attended_outer[:quarter], attended_inner, attended_outer[quarter:]])
 
-    chunks = 2
+    chunks = 3 if model % (3 * 512) == 0 else 1
     columns = model // chunks
     tile = 512 if columns % 512 == 0 else columns
     last = ranks - 1
-    arrived = [()] * chunks
-    for step in range(last):
-        if step == 0:
-            source, blocks = attended_outer, jnp.array([half // block - 1, 0], jnp.int32)
-        else:
-            source = attended
-            blocks = jnp.stack([jnp.minimum(last - step + rank, last), jnp.maximum(step + rank - last, 0)])
-        for chunk in range(chunks):
-            up, down = message(
-                blocks, source, out_weight, arrived[chunk], chunk * columns, columns, block, tile
+    ahead = 2
+    arrived = {}
+    for slot in range(last * chunks):
+        for hop in range(last):
+            at = slot - hop * ahead
+            if not 0 <= at < (last - hop) * chunks:
+                continue
+            target, chunk = last - at // chunks, at % chunks
+            upward, downward = rank == hop, rank == last - hop
+            if target == last:
+                source, far, near = attended_outer, half // block - 1, 0
+            else:
+                source, far, near = attended, target, last - target
+            blocks = jnp.stack([jnp.where(upward, far, near), jnp.logical_or(upward, downward).astype(jnp.int32)])
+            before = [arrived[hop - 1, target, chunk]] if hop else []
+            sent = message(hop, blocks, source, out_weight, before, chunk * columns, columns, block, tile)
+            paced = slot - ahead
+            if hop == 0 and paced >= 0:
+                gone = (0, last - paced // chunks, paced % chunks)
+                sent, arrived[gone] = lax.optimization_barrier((sent, arrived[gone]))
+            arrived[hop, target, chunk] = lax.ppermute(
+                sent, "tensor", [(hop, hop + 1), (last - hop, last - hop - 1)]
             )
-            up = lax.ppermute(up, "tensor", [(i, i + 1) for i in range(step + 1)])
-            down = lax.ppermute(down, "tensor", [(last - i, last - i - 1) for i in range(step + 1)])
-            arrived[chunk] = (up, down)
     blocks = jnp.stack([rank, level])
     projected = own_projection(blocks, attended, out_weight, block, tile)
     result = ()
     for chunk in range(chunks):
-        result = (final(blocks, projected, gate_table, *arrived[chunk], chunk * columns, columns // 2, result),)
+        comes = [arrived[hop, hop + 1, chunk] for hop in range(last)]
+        result = (final(blocks, projected, gate_table, comes, chunk * columns, columns // 2, result),)
     return result[0]
 
 

time: 120 us -> 143 us (1.19)
  the two profiles are of different devices: /device:TPU:14 before, /device:TPU:0 now
where the time goes in v3:
time: 143 us; the launch traced here: 142 us
  starting transfers between devices  61.5 us (43%)
  Pallas kernels  48.3 us (34%)
  local copies, waits for them, and re-layouts  24.7 us (17%)
  waiting for transfers between devices  6.06 us (4%)
    ppermute x18, starting transfers between devices, body(): lax.ppermute(sent, 'tensor', [(hop, hop + 1), (last - hop, last - hop - 1)])  48.7 us
    unnamed x52, local copies, waits for them, and re-layouts  24.1 us
    pallas_call x18, Pallas kernels, message(): pl.pallas_call(functools.partial(message_kernel, hop, first, tile), in_sp...  22.8 us
    ppermute x4, starting transfers between devices, shifted(): lax.ppermute(block, axis, [(i, i + distance) for i in range(count) if 0 <...  12.3 us
    pallas_call x2, Pallas kernels, served(): pl.pallas_call(functools.partial(served_kernel, distance), in_specs=[SMEM...  8.29 us
    pallas_call x3, Pallas kernels, final(): pl.pallas_call(functools.partial(final_kernel, len(comes)), grid_spec=plt...  6.95 us
    ppermute x4, waiting for transfers between devices, shifted(): lax.ppermute(block, axis, [(i, i + distance) for i in range(count) if 0 <...  5.97 us
    pallas_call x1, Pallas kernels, body(): pl.pallas_call(local_kernel, in_specs=[SMEM, SMEM] + [VMEM] * 5, out_spec...  4.18 us
  transfers between devices with their start and end apart: 24, of which 2 were waited for; matrix products, arithmetic and copies ran while one was open for 1% of the time, Pallas kernels for 29%

profile of v3, /device:TPU:0, one launch (start us, length us, event | category | flops | bytes accessed | tf_op | source)
XLA Modules:
  0.0 142.3 jit_solution(11337811687313375502)
XLA Ops:
  0.5 1.1 copy-done.12
  1.6 1.2 split.1
  3.5 1.3 collective-permute-start.2
  5.7 1.1 copy-done.5
  10.6 4.2 %local.1 = (f32[384,768]{1,0:T(8,128)S(1)}, f32[384,128]{1,0:T(8,128)S(1)}) custom-call(s32[2]{0:T(128)S(1)} %pad_add_fusion.1.place, s32[4,4]{1,0:T(4,128)S(1)} %copy-done.16, bf16[384,768]{1,0:T(8,128)(2,1)S(1)} %copy-done.13, bf16[384,768]{1,0:T(8,128)(2,1)S(1)} %copy-done.5, bf16[384,768]{1,0:T(8,128)(2,1)S(1)} %copy-done.7, ...), custom_call_target="tpu_custom_call" | custom-call | flops 905969664 | bytes 4128768 | tf_op jit(solution)/shard_map/local/pallas_call | solution.py:254
  15.1 4.0 %served.2 = bf16[192,896]{1,0:T(8,128)(2,1)} custom-call(s32[2]{0:T(128)S(1)} %pad_add_fusion.1.place, s32[4,4]{1,0:T(4,128)S(1)} %copy-done.16, bf16[192,768]{1,0:T(8,128)(2,1)S(1)} %collective-permute-done.2.query, bf16[384,768]{1,0:T(8,128)(2,1)S(1)} %copy-done.6, bf16[384,768]{1,0:T(8,128)(2,1)S(1)} %copy-done.8, ...), custom_call_target="tpu_custom_call" | custom-call | flops 452984832 | bytes 3538944 | tf_op jit(solution)/shard_map/served/pallas_call | solution.py:268
  19.1 5.4 %collective-permute-start.3 = (bf16[192,896]{1,0:T(8,128)(2,1)}, bf16[192,896]{1,0:T(8,128)(2,1)}, u32[]{:S(2)}, u32[]{:S(2)}) collective-permute-start(bf16[192,896]{1,0:T(8,128)(2,1)} %served.2), channel_id=1, source_target_pairs={{0,8},{4,12},{1,9},{5,13},{2,10},{6,14},{3,11},{7,15},{16,24},{20,... | collective-permute-start | bytes 1032200 | tf_op jit(solution)/shard_map/ppermute | solution.py:27
  24.4 1.3 collective-permute-start.4
  25.8 5.7 %collective-permute-done.3.refs_0_ = bf16[192,896]{1,0:T(8,128)(2,1)} collective-permute-done((bf16[192,896]{1,0:T(8,128)(2,1)}, bf16[192,896]{1,0:T(8,128)(2,1)}, u32[]{:S(2)}, u32[]{:S(2)}) %collective-permute-start.3) | collective-permute-done | bytes 344096 | tf_op jit(solution)/shard_map/ppermute | solution.py:27
  31.5 1.7 %merge.2.attended = bf16[192,768]{1,0:T(8,128)(2,1)S(1)} custom-call(s32[2]{0:T(128)S(1)} %pad_add_fusion.1.place, f32[384,768]{1,0:T(8,128)S(1)} %get-tuple-element.27.own, f32[384,128]{1,0:T(8,128)S(1)} %get-tuple-element.31.own_sum, bf16[192,896]{1,0:T(8,128)(2,1)} %collective-permute-done.3.refs_0_), custom_call_target="tpu_custom_call" | custom-call | flops 1179648 | bytes 1474560 | tf_op jit(solution)/shard_map/merge/pallas_call | solution.py:286
  33.1 3.7 %copy-done = bf16[768,6144]{1,0:T(8,128)(2,1)S(1)} copy-done((bf16[768,6144]{1,0:T(8,128)(2,1)S(1)}, bf16[768,6144]{1,0:T(8,128)(2,1)}, u32[]{:S(2)}) %copy-start) | copy-done | bytes 9437208
  36.8 1.9 %message.22 = bf16[96,2048]{1,0:T(8,128)(2,1)} custom-call(s32[2]{0:T(128)S(1)} %pad_add_fusion.4.blocks, bf16[192,768]{1,0:T(8,128)(2,1)S(1)} %merge.2.attended, bf16[768,6144]{1,0:T(8,128)(2,1)S(1)} %copy-done), custom_call_target="tpu_custom_call" | custom-call | flops 301989888 | bytes 3932160 | tf_op jit(solution)/shard_map/message/pallas_call | solution.py:164
  38.8 4.4 %collective-permute-start.6 = (bf16[96,2048]{1,0:T(8,128)(2,1)}, bf16[96,2048]{1,0:T(8,128)(2,1)}, u32[]{:S(2)}, u32[]{:S(2)}) collective-permute-start(bf16[96,2048]{1,0:T(8,128)(2,1)} %message.22), channel_id=1, source_target_pairs={{0,1},{3,2},{4,5},{7,6},{8,9},{11,10},{12,13},{15,14},{16,17},{19,... | collective-permute-start | bytes 1179656 | tf_op jit(solution)/shard_map/ppermute | solution.py:324
  43.3 1.1 copy-done.11
  44.3 4.3 %served.3 = bf16[192,896]{1,0:T(8,128)(2,1)} custom-call(s32[2]{0:T(128)S(1)} %pad_add_fusion.1.place, s32[4,4]{1,0:T(4,128)S(1)} %copy-done.17, bf16[192,768]{1,0:T(8,128)(2,1)} %collective-permute-done.4.query, bf16[384,768]{1,0:T(8,128)(2,1)S(1)} %copy-done.6, bf16[384,768]{1,0:T(8,128)(2,1)S(1)} %copy-done.8, ...), custom_call_target="tpu_custom_call" | custom-call | flops 452984832 | bytes 3538944 | tf_op jit(solution)/shard_map/served/pallas_call | solution.py:268
  48.7 4.4 %collective-permute-start.5 = (bf16[192,896]{1,0:T(8,128)(2,1)}, bf16[192,896]{1,0:T(8,128)(2,1)S(1)}, u32[]{:S(2)}, u32[]{:S(2)}) collective-permute-start(bf16[192,896]{1,0:T(8,128)(2,1)} %served.3), channel_id=1, source_target_pairs={{0,8},{4,12},{1,9},{5,13},{2,10},{6,14},{3,11},{7,15},{16,24},{20,... | collective-permute-start | bytes 1032200 | tf_op jit(solution)/shard_map/ppermute | solution.py:27
  53.2 3.7 %copy-done.1 = bf16[768,6144]{1,0:T(8,128)(2,1)S(1)} copy-done((bf16[768,6144]{1,0:T(8,128)(2,1)S(1)}, bf16[768,6144]{1,0:T(8,128)(2,1)}, u32[]{:S(2)}) %copy-start.1) | copy-done | bytes 9437208
  56.8 1.2 message.26
  58.0 1.6 %collective-permute-start.11 = (bf16[96,2048]{1,0:T(8,128)(2,1)S(1)}, bf16[96,2048]{1,0:T(8,128)(2,1)S(1)}, u32[]{:S(2)}, u32[]{:S(2)}) collective-permute-start(bf16[96,2048]{1,0:T(8,128)(2,1)S(1)} %message.26), channel_id=1, source_target_pairs={{0,1},{3,2},{4,5},{7,6},{8,9},{11,10},{12,13},{15,14},{16,17},{19,... | collective-permute-start | bytes 1179656 | tf_op jit(solution)/shard_map/ppermute | solution.py:324
  59.6 1.2 message.21
  60.8 1.3 collective-permute-start.7
  63.3 2.0 %message.25 = bf16[96,2048]{1,0:T(8,128)(2,1)} custom-call(s32[2]{0:T(128)S(1)} %pad_add_fusion.3.blocks, bf16[384,768]{1,0:T(8,128)(2,1)S(1)} %pad_maximum_fusion.attended, bf16[768,6144]{1,0:T(8,128)(2,1)S(1)} %bitcast.11), custom_call_target="tpu_custom_call" | custom-call | flops 301989888 | bytes 3932160 | tf_op jit(solution)/shard_map/message/pallas_call | solution.py:164
  65.3 2.1 %message.20 = bf16[96,2048]{1,0:T(8,128)(2,1)} custom-call(s32[2]{0:T(128)S(1)} %pad_add_fusion.3.blocks, bf16[384,768]{1,0:T(8,128)(2,1)S(1)} %pad_maximum_fusion.attended, bf16[768,6144]{1,0:T(8,128)(2,1)S(1)} %bitcast.11), custom_call_target="tpu_custom_call" | custom-call | flops 301989888 | bytes 3932160 | tf_op jit(solution)/shard_map/message/pallas_call | solution.py:164
  69.2 1.3 message.31
  70.4 1.4 collective-permute-start.19
  71.8 7.1 %collective-permute-start.12 = (bf16[96,2048]{1,0:T(8,128)(2,1)}, bf16[96,2048]{1,0:T(8,128)(2,1)S(1)}, u32[]{:S(2)}, u32[]{:S(2)}) collective-permute-start(bf16[96,2048]{1,0:T(8,128)(2,1)} %message.25), channel_id=1, source_target_pairs={{0,1},{3,2},{4,5},{7,6},{8,9},{11,10},{12,13},{15,14},{16,17},{19,... | collective-permute-start | bytes 1179656 | tf_op jit(solution)/shard_map/ppermute | solution.py:324
  79.0 1.3 message.28
  81.0 5.7 %collective-permute-start.8 = (bf16[96,2048]{1,0:T(8,128)(2,1)}, bf16[96,2048]{1,0:T(8,128)(2,1)S(1)}, u32[]{:S(2)}, u32[]{:S(2)}) collective-permute-start(bf16[96,2048]{1,0:T(8,128)(2,1)} %message.20), channel_id=1, source_target_pairs={{0,1},{3,2},{4,5},{7,6},{8,9},{11,10},{12,13},{15,14},{16,17},{19,... | collective-permute-start | bytes 1179656 | tf_op jit(solution)/shard_map/ppermute | solution.py:324
  86.9 3.7 %copy-done.2 = bf16[768,6144]{1,0:T(8,128)(2,1)S(1)} copy-done((bf16[768,6144]{1,0:T(8,128)(2,1)S(1)}, bf16[768,6144]{1,0:T(8,128)(2,1)}, u32[]{:S(2)}) %copy-start.2) | copy-done | bytes 9437208
  90.6 1.2 message.24
  91.8 1.2 message.19
  93.1 1.4 %collective-permute-start.13 = (bf16[96,2048]{1,0:T(8,128)(2,1)S(1)}, bf16[96,2048]{1,0:T(8,128)(2,1)S(1)}, u32[]{:S(2)}, u32[]{:S(2)}) collective-permute-start(bf16[96,2048]{1,0:T(8,128)(2,1)S(1)} %message.24), channel_id=1, source_target_pairs={{0,1},{3,2},{4,5},{7,6},{8,9},{11,10},{12,13},{15,14},{16,17},{19,... | collective-permute-start | bytes 1179656 | tf_op jit(solution)/shard_map/ppermute | solution.py:324
  95.1 1.3 collective-permute-start.23
  97.5 1.3 collective-permute-start.20
  98.8 5.2 %collective-permute-start.9 = (bf16[96,2048]{1,0:T(8,128)(2,1)S(1)}, bf16[96,2048]{1,0:T(8,128)(2,1)S(1)}, u32[]{:S(2)}, u32[]{:S(2)}) collective-permute-start(bf16[96,2048]{1,0:T(8,128)(2,1)S(1)} %message.19), channel_id=1, source_target_pairs={{0,1},{3,2},{4,5},{7,6},{8,9},{11,10},{12,13},{15,14},{16,17},{19,... | collective-permute-start | bytes 1179656 | tf_op jit(solution)/shard_map/ppermute | solution.py:324
  106.0 1.9 %message.23 = bf16[96,2048]{1,0:T(8,128)(2,1)} custom-call(s32[2]{0:T(128)S(1)} %pad_add_fusion.2.blocks, bf16[384,768]{1,0:T(8,128)(2,1)S(1)} %pad_maximum_fusion.attended, bf16[768,6144]{1,0:T(8,128)(2,1)S(1)} %bitcast.13), custom_call_target="tpu_custom_call" | custom-call | flops 301989888 | bytes 3932160 | tf_op jit(solution)/shard_map/message/pallas_call | solution.py:164
  108.0 1.9 %message.18 = bf16[96,2048]{1,0:T(8,128)(2,1)} custom-call(s32[2]{0:T(128)S(1)} %pad_add_fusion.2.blocks, bf16[384,768]{1,0:T(8,128)(2,1)S(1)} %pad_maximum_fusion.attended, bf16[768,6144]{1,0:T(8,128)(2,1)S(1)} %bitcast.13), custom_call_target="tpu_custom_call" | custom-call | flops 301989888 | bytes 3932160 | tf_op jit(solution)/shard_map/message/pallas_call | solution.py:164
  109.9 1.3 message.29
  111.2 1.3 collective-permute-start.16
  113.6 1.4 %collective-permute-start.18 = (bf16[96,2048]{1,0:T(8,128)(2,1)S(1)}, bf16[96,2048]{1,0:T(8,128)(2,1)}, u32[]{:S(2)}, u32[]{:S(2)}) collective-permute-start(bf16[96,2048]{1,0:T(8,128)(2,1)S(1)} %message.30), channel_id=1, source_target_pairs={{1,2},{2,1},{5,6},{6,5},{9,10},{10,9},{13,14},{14,13},{17,18},{18,... | collective-permute-start | bytes 1179656 | tf_op jit(solution)/shard_map/ppermute | solution.py:324
  115.1 7.8 %collective-permute-start.17 = (bf16[96,2048]{1,0:T(8,128)(2,1)}, bf16[96,2048]{1,0:T(8,128)(2,1)}, u32[]{:S(2)}, u32[]{:S(2)}) collective-permute-start(bf16[96,2048]{1,0:T(8,128)(2,1)} %message.23), channel_id=1, source_target_pairs={{0,1},{3,2},{4,5},{7,6},{8,9},{11,10},{12,13},{15,14},{16,17},{19,... | collective-permute-start | bytes 1179656 | tf_op jit(solution)/shard_map/ppermute | solution.py:324
  122.9 1.4 collective-permute-start.14
  124.3 3.8 %collective-permute-start.10 = (bf16[96,2048]{1,0:T(8,128)(2,1)}, bf16[96,2048]{1,0:T(8,128)(2,1)}, u32[]{:S(2)}, u32[]{:S(2)}) collective-permute-start(bf16[96,2048]{1,0:T(8,128)(2,1)} %message.18), channel_id=1, source_target_pairs={{0,1},{3,2},{4,5},{7,6},{8,9},{11,10},{12,13},{15,14},{16,17},{19,... | collective-permute-start | bytes 1179656 | tf_op jit(solution)/shard_map/ppermute | solution.py:324
  129.5 3.7 %copy-done.3 = bf16[768,6144]{1,0:T(8,128)(2,1)S(1)} copy-done((bf16[768,6144]{1,0:T(8,128)(2,1)S(1)}, bf16[768,6144]{1,0:T(8,128)(2,1)}, u32[]{:S(2)}) %copy-start.3) | copy-done | bytes 9437208
  133.1 2.2 %own.1 = f32[96,6144]{1,0:T(8,128)S(1)} custom-call(s32[2]{0:T(128)S(1)} %pad_add_fusion.blocks, bf16[384,768]{1,0:T(8,128)(2,1)S(1)} %pad_maximum_fusion.attended, bf16[768,6144]{1,0:T(8,128)(2,1)S(1)} %copy-done.3), custom_call_target="tpu_custom_call" | custom-call | flops 905969664 | bytes 11796480 | tf_op jit(solution)/shard_map/own/pallas_call | solution.py:185
  135.3 1.6 %final.3.refs_3_ = bf16[96,6144]{1,0:T(8,128)(2,1)} custom-call(s32[2]{0:T(128)S(1)} %pad_add_fusion.blocks, f32[96,6144]{1,0:T(8,128)S(1)} %own.1, f32[64,6144]{1,0:T(8,128)S(1)} %copy-done.4, bf16[96,2048]{1,0:T(8,128)(2,1)S(1)} %collective-permute-done.9.refs_0_, bf16[96,2048]{1,0:T(8,128)(2,1)S(1)} %collective-permute-done.21.refs_1_, ...), custom_call_target="tpu_custom_call" | custom-call | flops 786432 | bytes 1966080 | tf_op jit(solution)/shard_map/final/pallas_call | solution.py:207
  136.9 2.6 %final.4.refs_3_ = bf16[96,6144]{1,0:T(8,128)(2,1)} custom-call(s32[2]{0:T(128)S(1)} %pad_add_fusion.blocks, f32[96,6144]{1,0:T(8,128)S(1)} %own.1, f32[64,6144]{1,0:T(8,128)S(1)} %copy-done.4, bf16[96,2048]{1,0:T(8,128)(2,1)} %collective-permute-done.17.refs_0_, bf16[96,2048]{1,0:T(8,128)(2,1)} %collective-permute-done.18.refs_1_, ...), custom_call_target="tpu_custom_call", output_to_operand_aliasing={{}: (6, {})} | custom-call | flops 786432 | bytes 1966080 | tf_op jit(solution)/shard_map/final/pallas_call | solution.py:207
  139.6 2.7 %final.5 = bf16[96,6144]{1,0:T(8,128)(2,1)} custom-call(s32[2]{0:T(128)S(1)} %pad_add_fusion.blocks, f32[96,6144]{1,0:T(8,128)S(1)} %own.1, f32[64,6144]{1,0:T(8,128)S(1)} %copy-done.4, bf16[96,2048]{1,0:T(8,128)(2,1)} %collective-permute-done.10.refs_0_, bf16[96,2048]{1,0:T(8,128)(2,1)} %collective-permute-done.14.refs_1_, ...), custom_call_target="tpu_custom_call", output_to_operand_aliasing={{}: (6, {})} | custom-call | flops 786432 | bytes 1966080 | tf_op jit(solution)/shard_map/final/pallas_call | solution.py:207
  (93 shorter events, 16.3 us)
Async XLA Ops:
  0.0 4.9 %collective-permute-start = (bf16[384,768]{1,0:T(8,128)(2,1)}, bf16[384,768]{1,0:T(8,128)(2,1)S(1)}, u32[]{:S(2)}, u32[]{:S(2)}) collective-permute-start(bf16[384,768]{1,0:T(8,128)(2,1)} %key.5), channel_id=1, source_target_pairs={{0,4},{4,0},{8,12},{12,8},{1,5},{5,1},{9,13},{13,9},{2,6},{6,2},{1... | collective-permute-start | bytes 1769480 | tf_op jit(solution)/shard_map/ppermute | solution.py:251
  0.5 4.4 %collective-permute-start.1 = (bf16[384,768]{1,0:T(8,128)(2,1)}, bf16[384,768]{1,0:T(8,128)(2,1)S(1)}, u32[]{:S(2)}, u32[]{:S(2)}) collective-permute-start(bf16[384,768]{1,0:T(8,128)(2,1)} %value.5), channel_id=1, source_target_pairs={{0,4},{4,0},{8,12},{12,8},{1,5},{5,1},{9,13},{13,9},{2,6},{6,2},{1... | collective-permute-start | bytes 1769480 | tf_op jit(solution)/shard_map/ppermute | solution.py:252
  0.5 1.1 copy-start.12
  3.5 11.6 %collective-permute-start.2 = (bf16[192,768]{1,0:T(8,128)(2,1)}, bf16[192,768]{1,0:T(8,128)(2,1)S(1)}, u32[]{:S(2)}, u32[]{:S(2)}) collective-permute-start(bf16[192,768]{1,0:T(8,128)(2,1)} %get-tuple-element.28), channel_id=1, source_target_pairs={{8,0},{12,4},{9,1},{13,5},{10,2},{14,6},{11,3},{15,7},{24,16},{28,... | collective-permute-start | bytes 884744 | tf_op jit(solution)/shard_map/ppermute | solution.py:27
  4.9 0.8 copy-start.9
  5.7 1.1 copy-start.5
  6.7 1.1 copy-start.7
  7.8 1.1 copy-start.10
  8.9 1.1 copy-start.13
  10.6 4.5 %copy-start.6 = (bf16[384,768]{1,0:T(8,128)(2,1)S(1)}, bf16[384,768]{1,0:T(8,128)(2,1)}, u32[]{:S(2)}) copy-start(bf16[384,768]{1,0:T(8,128)(2,1)} %key.5) | copy-start | bytes 1769476
  10.6 4.5 %copy-start.8 = (bf16[384,768]{1,0:T(8,128)(2,1)S(1)}, bf16[384,768]{1,0:T(8,128)(2,1)}, u32[]{:S(2)}) copy-start(bf16[384,768]{1,0:T(8,128)(2,1)} %value.5) | copy-start | bytes 1769476
  19.1 12.4 %collective-permute-start.3 = (bf16[192,896]{1,0:T(8,128)(2,1)}, bf16[192,896]{1,0:T(8,128)(2,1)}, u32[]{:S(2)}, u32[]{:S(2)}) collective-permute-start(bf16[192,896]{1,0:T(8,128)(2,1)} %served.2), channel_id=1, source_target_pairs={{0,8},{4,12},{1,9},{5,13},{2,10},{6,14},{3,11},{7,15},{16,24},{20,... | collective-permute-start | bytes 1032200 | tf_op jit(solution)/shard_map/ppermute | solution.py:27
  24.4 18.8 %collective-permute-start.4 = (bf16[192,768]{1,0:T(8,128)(2,1)}, bf16[192,768]{1,0:T(8,128)(2,1)}, u32[]{:S(2)}, u32[]{:S(2)}) collective-permute-start(bf16[192,768]{1,0:T(8,128)(2,1)} %copy-done.18), channel_id=1, source_target_pairs={{8,0},{12,4},{9,1},{13,5},{10,2},{14,6},{11,3},{15,7},{24,16},{28,... | collective-permute-start | bytes 884744 | tf_op jit(solution)/shard_map/ppermute | solution.py:27
  33.1 3.7 %copy-start = (bf16[768,6144]{1,0:T(8,128)(2,1)S(1)}, bf16[768,6144]{1,0:T(8,128)(2,1)}, u32[]{:S(2)}) copy-start(bf16[768,6144]{1,0:T(8,128)(2,1)} %weight.37) | copy-start | bytes 28311556
  36.8 6.4 %copy-start.17 = (s32[4,4]{1,0:T(4,128)S(1)}, s32[4,4]{1,0:T(4,128)}, u32[]{:S(2)}) copy-start(s32[4,4]{1,0:T(4,128)} %visible.5) | copy-start | bytes 196
  38.8 22.0 %collective-permute-start.6 = (bf16[96,2048]{1,0:T(8,128)(2,1)}, bf16[96,2048]{1,0:T(8,128)(2,1)}, u32[]{:S(2)}, u32[]{:S(2)}) collective-permute-start(bf16[96,2048]{1,0:T(8,128)(2,1)} %message.22), channel_id=1, source_target_pairs={{0,1},{3,2},{4,5},{7,6},{8,9},{11,10},{12,13},{15,14},{16,17},{19,... | collective-permute-start | bytes 1179656 | tf_op jit(solution)/shard_map/ppermute | solution.py:324
  43.3 1.1 copy-start.11
  48.7 13.5 %collective-permute-start.5 = (bf16[192,896]{1,0:T(8,128)(2,1)}, bf16[192,896]{1,0:T(8,128)(2,1)S(1)}, u32[]{:S(2)}, u32[]{:S(2)}) collective-permute-start(bf16[192,896]{1,0:T(8,128)(2,1)} %served.3), channel_id=1, source_target_pairs={{0,8},{4,12},{1,9},{5,13},{2,10},{6,14},{3,11},{7,15},{16,24},{20,... | collective-permute-start | bytes 1032200 | tf_op jit(solution)/shard_map/ppermute | solution.py:27
  53.2 3.7 %copy-start.1 = (bf16[768,6144]{1,0:T(8,128)(2,1)S(1)}, bf16[768,6144]{1,0:T(8,128)(2,1)}, u32[]{:S(2)}) copy-start(bf16[768,6144]{1,0:T(8,128)(2,1)} %weight.37) | copy-start | bytes 28311556
  56.8 6.4 %slice-start = ((s8[9437184]{0:T(1024)(128)(4,1)}), s8[4194304]{0:T(1024)(128)(4,1)S(1)}, s32[]{:S(2)}) async-start(s8[9437184]{0:T(1024)(128)(4,1)} %bitcast.10), calls=%async_computation | async-start | bytes 8388608
  56.8 6.4 %slice-start.1 = ((s8[9437184]{0:T(1024)(128)(4,1)}), s8[4194304]{0:T(1024)(128)(4,1)S(1)}, s32[]{:S(2)}) async-start(s8[9437184]{0:T(1024)(128)(4,1)} %bitcast.10), calls=%async_computation.1 | async-start | bytes 8388608
  58.0 5.3 %slice-start.2 = ((s8[9437184]{0:T(1024)(128)(4,1)}), s8[1048576]{0:T(1024)(128)(4,1)S(1)}, s32[]{:S(2)}) async-start(s8[9437184]{0:T(1024)(128)(4,1)} %bitcast.10), calls=%async_computation.2 | async-start | bytes 2097152
  58.0 11.1 %collective-permute-start.11 = (bf16[96,2048]{1,0:T(8,128)(2,1)S(1)}, bf16[96,2048]{1,0:T(8,128)(2,1)S(1)}, u32[]{:S(2)}, u32[]{:S(2)}) collective-permute-start(bf16[96,2048]{1,0:T(8,128)(2,1)S(1)} %message.26), channel_id=1, source_target_pairs={{0,1},{3,2},{4,5},{7,6},{8,9},{11,10},{12,13},{15,14},{16,17},{19,... | collective-permute-start | bytes 1179656 | tf_op jit(solution)/shard_map/ppermute | solution.py:324
  60.8 18.2 %collective-permute-start.7 = (bf16[96,2048]{1,0:T(8,128)(2,1)S(1)}, bf16[96,2048]{1,0:T(8,128)(2,1)S(1)}, u32[]{:S(2)}, u32[]{:S(2)}) collective-permute-start(bf16[96,2048]{1,0:T(8,128)(2,1)S(1)} %message.21), channel_id=1, source_target_pairs={{0,1},{3,2},{4,5},{7,6},{8,9},{11,10},{12,13},{15,14},{16,17},{19,... | collective-permute-start | bytes 1179656 | tf_op jit(solution)/shard_map/ppermute | solution.py:324
  68.4 26.1 %collective-permute-start.22 = (bf16[96,2048]{1,0:T(8,128)(2,1)S(1)}, bf16[96,2048]{1,0:T(8,128)(2,1)S(1)}, u32[]{:S(2)}, u32[]{:S(2)}) collective-permute-start(bf16[96,2048]{1,0:T(8,128)(2,1)S(1)} %message.34), channel_id=1, source_target_pairs={{1,2},{2,1},{5,6},{6,5},{9,10},{10,9},{13,14},{14,13},{17,18},{18,... | collective-permute-start | bytes 1179656 | tf_op jit(solution)/shard_map/ppermute | solution.py:324
  70.4 26.0 %collective-permute-start.19 = (bf16[96,2048]{1,0:T(8,128)(2,1)}, bf16[96,2048]{1,0:T(8,128)(2,1)}, u32[]{:S(2)}, u32[]{:S(2)}) collective-permute-start(bf16[96,2048]{1,0:T(8,128)(2,1)} %message.31), channel_id=1, source_target_pairs={{1,2},{2,1},{5,6},{6,5},{9,10},{10,9},{13,14},{14,13},{17,18},{18,... | collective-permute-start | bytes 1179656 | tf_op jit(solution)/shard_map/ppermute | solution.py:324
  71.8 21.2 %collective-permute-start.12 = (bf16[96,2048]{1,0:T(8,128)(2,1)}, bf16[96,2048]{1,0:T(8,128)(2,1)S(1)}, u32[]{:S(2)}, u32[]{:S(2)}) collective-permute-start(bf16[96,2048]{1,0:T(8,128)(2,1)} %message.25), channel_id=1, source_target_pairs={{0,1},{3,2},{4,5},{7,6},{8,9},{11,10},{12,13},{15,14},{16,17},{19,... | collective-permute-start | bytes 1179656 | tf_op jit(solution)/shard_map/ppermute | solution.py:324
  80.3 24.3 %collective-permute-start.15 = (bf16[96,2048]{1,0:T(8,128)(2,1)}, bf16[96,2048]{1,0:T(8,128)(2,1)S(1)}, u32[]{:S(2)}, u32[]{:S(2)}) collective-permute-start(bf16[96,2048]{1,0:T(8,128)(2,1)} %message.28), channel_id=1, source_target_pairs={{1,2},{2,1},{5,6},{6,5},{9,10},{10,9},{13,14},{14,13},{17,18},{18,... | collective-permute-start | bytes 1179656 | tf_op jit(solution)/shard_map/ppermute | solution.py:324
  81.0 17.8 %collective-permute-start.8 = (bf16[96,2048]{1,0:T(8,128)(2,1)}, bf16[96,2048]{1,0:T(8,128)(2,1)S(1)}, u32[]{:S(2)}, u32[]{:S(2)}) collective-permute-start(bf16[96,2048]{1,0:T(8,128)(2,1)} %message.20), channel_id=1, source_target_pairs={{0,1},{3,2},{4,5},{7,6},{8,9},{11,10},{12,13},{15,14},{16,17},{19,... | collective-permute-start | bytes 1179656 | tf_op jit(solution)/shard_map/ppermute | solution.py:324
  86.9 3.7 %copy-start.2 = (bf16[768,6144]{1,0:T(8,128)(2,1)S(1)}, bf16[768,6144]{1,0:T(8,128)(2,1)}, u32[]{:S(2)}) copy-start(bf16[768,6144]{1,0:T(8,128)(2,1)} %weight.37) | copy-start | bytes 28311556
  90.6 3.9 %slice-start.3 = ((s8[9437184]{0:T(1024)(128)(4,1)}), s8[4194304]{0:T(1024)(128)(4,1)S(1)}, s32[]{:S(2)}) async-start(s8[9437184]{0:T(1024)(128)(4,1)} %bitcast.12), calls=%async_computation.3 | async-start | bytes 8388608
  90.6 3.9 %slice-start.4 = ((s8[9437184]{0:T(1024)(128)(4,1)}), s8[4194304]{0:T(1024)(128)(4,1)S(1)}, s32[]{:S(2)}) async-start(s8[9437184]{0:T(1024)(128)(4,1)} %bitcast.12), calls=%async_computation.4 | async-start | bytes 8388608
  91.8 2.7 %slice-start.5 = ((s8[9437184]{0:T(1024)(128)(4,1)}), s8[1048576]{0:T(1024)(128)(4,1)S(1)}, s32[]{:S(2)}) async-start(s8[9437184]{0:T(1024)(128)(4,1)} %bitcast.12), calls=%async_computation.5 | async-start | bytes 2097152
  93.1 18.1 %collective-permute-start.13 = (bf16[96,2048]{1,0:T(8,128)(2,1)S(1)}, bf16[96,2048]{1,0:T(8,128)(2,1)S(1)}, u32[]{:S(2)}, u32[]{:S(2)}) collective-permute-start(bf16[96,2048]{1,0:T(8,128)(2,1)S(1)} %message.24), channel_id=1, source_target_pairs={{0,1},{3,2},{4,5},{7,6},{8,9},{11,10},{12,13},{15,14},{16,17},{19,... | collective-permute-start | bytes 1179656 | tf_op jit(solution)/shard_map/ppermute | solution.py:324
  95.1 19.9 %collective-permute-start.23 = (bf16[96,2048]{1,0:T(8,128)(2,1)S(1)}, bf16[96,2048]{1,0:T(8,128)(2,1)S(1)}, u32[]{:S(2)}, u32[]{:S(2)}) collective-permute-start(bf16[96,2048]{1,0:T(8,128)(2,1)S(1)} %message.35), channel_id=1, source_target_pairs={{2,3},{1,0},{6,7},{5,4},{10,11},{9,8},{14,15},{13,12},{18,19},{17,... | collective-permute-start | bytes 1179656 | tf_op jit(solution)/shard_map/ppermute | solution.py:324
  97.5 25.5 %collective-permute-start.20 = (bf16[96,2048]{1,0:T(8,128)(2,1)S(1)}, bf16[96,2048]{1,0:T(8,128)(2,1)S(1)}, u32[]{:S(2)}, u32[]{:S(2)}) collective-permute-start(bf16[96,2048]{1,0:T(8,128)(2,1)S(1)} %message.32), channel_id=1, source_target_pairs={{2,3},{1,0},{6,7},{5,4},{10,11},{9,8},{14,15},{13,12},{18,19},{17,... | collective-permute-start | bytes 1179656 | tf_op jit(solution)/shard_map/ppermute | solution.py:324
  98.8 14.9 %collective-permute-start.9 = (bf16[96,2048]{1,0:T(8,128)(2,1)S(1)}, bf16[96,2048]{1,0:T(8,128)(2,1)S(1)}, u32[]{:S(2)}, u32[]{:S(2)}) collective-permute-start(bf16[96,2048]{1,0:T(8,128)(2,1)S(1)} %message.19), channel_id=1, source_target_pairs={{0,1},{3,2},{4,5},{7,6},{8,9},{11,10},{12,13},{15,14},{16,17},{19,... | collective-permute-start | bytes 1179656 | tf_op jit(solution)/shard_map/ppermute | solution.py:324
  104.6 0.7 copy-start.14
  105.3 19.0 %collective-permute-start.21 = (bf16[96,2048]{1,0:T(8,128)(2,1)S(1)}, bf16[96,2048]{1,0:T(8,128)(2,1)S(1)}, u32[]{:S(2)}, u32[]{:S(2)}) collective-permute-start(bf16[96,2048]{1,0:T(8,128)(2,1)S(1)} %message.33), channel_id=1, source_target_pairs={{1,2},{2,1},{5,6},{6,5},{9,10},{10,9},{13,14},{14,13},{17,18},{18,... | collective-permute-start | bytes 1179656 | tf_op jit(solution)/shard_map/ppermute | solution.py:324
  108.0 1.9 %copy-start.15 = (bf16[96,2048]{1,0:T(8,128)(2,1)S(1)}, bf16[96,2048]{1,0:T(8,128)(2,1)}, u32[]{:S(2)}) copy-start(bf16[96,2048]{1,0:T(8,128)(2,1)} %copy-done.14) | copy-start | bytes 1179652
  111.2 28.3 %collective-permute-start.16 = (bf16[96,2048]{1,0:T(8,128)(2,1)}, bf16[96,2048]{1,0:T(8,128)(2,1)}, u32[]{:S(2)}, u32[]{:S(2)}) collective-permute-start(bf16[96,2048]{1,0:T(8,128)(2,1)} %message.29), channel_id=1, source_target_pairs={{2,3},{1,0},{6,7},{5,4},{10,11},{9,8},{14,15},{13,12},{18,19},{17,... | collective-permute-start | bytes 1179656 | tf_op jit(solution)/shard_map/ppermute | solution.py:324
  113.0 15.1 %copy-start.19 = (s32[4]{0:T(128)S(1)}, s32[4]{0:T(128)}, u32[]{:S(2)}) copy-start(s32[4]{0:T(128)} %param.12) | copy-start | bytes 52
  113.6 23.3 %collective-permute-start.18 = (bf16[96,2048]{1,0:T(8,128)(2,1)S(1)}, bf16[96,2048]{1,0:T(8,128)(2,1)}, u32[]{:S(2)}, u32[]{:S(2)}) collective-permute-start(bf16[96,2048]{1,0:T(8,128)(2,1)S(1)} %message.30), channel_id=1, source_target_pairs={{1,2},{2,1},{5,6},{6,5},{9,10},{10,9},{13,14},{14,13},{17,18},{18,... | collective-permute-start | bytes 1179656 | tf_op jit(solution)/shard_map/ppermute | solution.py:324
  115.1 21.9 %collective-permute-start.17 = (bf16[96,2048]{1,0:T(8,128)(2,1)}, bf16[96,2048]{1,0:T(8,128)(2,1)}, u32[]{:S(2)}, u32[]{:S(2)}) collective-permute-start(bf16[96,2048]{1,0:T(8,128)(2,1)} %message.23), channel_id=1, source_target_pairs={{0,1},{3,2},{4,5},{7,6},{8,9},{11,10},{12,13},{15,14},{16,17},{19,... | collective-permute-start | bytes 1179656 | tf_op jit(solution)/shard_map/ppermute | solution.py:324
  122.9 16.6 %collective-permute-start.14 = (bf16[96,2048]{1,0:T(8,128)(2,1)S(1)}, bf16[96,2048]{1,0:T(8,128)(2,1)}, u32[]{:S(2)}, u32[]{:S(2)}) collective-permute-start(bf16[96,2048]{1,0:T(8,128)(2,1)S(1)} %message.27), channel_id=1, source_target_pairs={{1,2},{2,1},{5,6},{6,5},{9,10},{10,9},{13,14},{14,13},{17,18},{18,... | collective-permute-start | bytes 1179656 | tf_op jit(solution)/shard_map/ppermute | solution.py:324
  124.3 15.2 %collective-permute-start.10 = (bf16[96,2048]{1,0:T(8,128)(2,1)}, bf16[96,2048]{1,0:T(8,128)(2,1)}, u32[]{:S(2)}, u32[]{:S(2)}) collective-permute-start(bf16[96,2048]{1,0:T(8,128)(2,1)} %message.18), channel_id=1, source_target_pairs={{0,1},{3,2},{4,5},{7,6},{8,9},{11,10},{12,13},{15,14},{16,17},{19,... | collective-permute-start | bytes 1179656 | tf_op jit(solution)/shard_map/ppermute | solution.py:324
  129.4 3.7 %copy-start.3 = (bf16[768,6144]{1,0:T(8,128)(2,1)S(1)}, bf16[768,6144]{1,0:T(8,128)(2,1)}, u32[]{:S(2)}) copy-start(bf16[768,6144]{1,0:T(8,128)(2,1)} %weight.37) | copy-start | bytes 28311556
  133.1 2.2 %copy-start.4 = (f32[64,6144]{1,0:T(8,128)S(1)}, f32[64,6144]{1,0:T(8,128)}, u32[]{:S(2)}) copy-start(f32[64,6144]{1,0:T(8,128)} %gate.5) | copy-start | bytes 4718596
  (2 other events, 1.4 us)

commit v4 on v2

--- a/solution.py
+++ b/solution.py
@@ -11,7 +11,8 @@
 LANES = 128
 HIDDEN = -1e30
 LOG2E = 1.4426950408889634
-PARAMS = pltpu.CompilerParams(vmem_limit_bytes=20 * 1024 * 1024)
+PARAMS = pltpu.CompilerParams(vmem_limit_bytes=24 * 1024 * 1024)
+ANY = pl.BlockSpec(memory_space=pl.ANY)
 SMEM = pl.BlockSpec(memory_space=pltpu.SMEM)
 VMEM = pl.BlockSpec(memory_space=pltpu.VMEM)
 PIECE_LANES = 32
@@ -122,69 +123,77 @@
         at += rows
 
 
-def rows_at(attended, index, rows):
-    return attended[pl.ds(pl.multiple_of(index * rows, rows), rows), :]
-
-
-def message_kernel(first, tile, blocks, attended, weight, *refs):
-    ups, downs = refs[-2:]
-    rows, columns = ups.shape
-    both = jnp.concatenate([rows_at(attended, blocks[0], rows), rows_at(attended, blocks[1], rows)], axis=0)
-    for at in range(0, columns, tile):
-        here = slice(at, at + tile)
-        product = jnp.dot(both, weight[:, first + at:first + at + tile], preferred_element_type=jnp.float32)
-        up, down = product[:rows], product[rows:]
-        if len(refs) == 4:
-            up = up + refs[0][:, here].astype(jnp.float32)
-            down = down + refs[1][:, here].astype(jnp.float32)
-        ups[:, here] = up.astype(jnp.bfloat16)
-        downs[:, here] = down.astype(jnp.bfloat16)
-
-
-def message(blocks, attended, weight, arrived, first, columns, rows, tile):
-    width = attended.shape[1]
+def project_kernel(first, attended, weight, *refs):
+    result = refs[-3] if first else refs[-1]
+    product = jnp.dot(attended[...], weight[...], preferred_element_type=jnp.float32).astype(jnp.bfloat16)
+    result[...] = product
+    if first:
+        up, down = refs[-2:]
+        rows = up.shape[0]
+        up[...] = product[product.shape[0] - rows:]
+        down[...] = product[:rows]
+
+
+def project(attended, weight, chunk, columns, rows, tile, before):
+    half, width = attended.shape
+    start = chunk * columns // tile
+    first = not before
+    place = 0 if first else 1
+    piece = pl.BlockSpec((rows, tile), lambda j: (0, j))
+    message = jax.ShapeDtypeStruct((rows, columns), jnp.bfloat16)
     return pl.pallas_call(
-        functools.partial(message_kernel, first, tile),
-        in_specs=[SMEM] + [VMEM] * (2 + len(arrived)),
-        out_specs=[VMEM, VMEM],
+        functools.partial(project_kernel, first),
+        grid=(columns // tile,),
+        in_specs=[
+            pl.BlockSpec((half, width), lambda j: (0, 0)),
+            pl.BlockSpec((width, tile), lambda j: (0, start + j)),
+        ] + [ANY] * len(before),
+        out_specs=[pl.BlockSpec((half, tile), lambda j: (place, j))] + [piece, piece] * first,
+        out_shape=[jax.ShapeDtypeStruct((2 * half, columns), jnp.bfloat16)] + [message, message] * first,
+        input_output_aliases={} if first else {2: 0},
+        compiler_params=PARAMS,
+        cost_estimate=cost(2 * half * width * columns, 2 * width * columns + 4 * half * columns),
+        name="project",
+    )(attended, weight, *before)
+
+
+def message_kernel(blocks, up_block, down_block, up_arrived, down_arrived, up, down):
+    up[...] = (up_block[...].astype(jnp.float32) + up_arrived[...].astype(jnp.float32)).astype(jnp.bfloat16)
+    down[...] = (down_block[...].astype(jnp.float32) + down_arrived[...].astype(jnp.float32)).astype(jnp.bfloat16)
+
+
+def message(blocks, projected, arrived, tile):
+    rows, columns = arrived[0].shape
+    piece = pl.BlockSpec((rows, tile), lambda j, b: (0, j))
+    return pl.pallas_call(
+        message_kernel,
+        grid_spec=pltpu.PrefetchScalarGridSpec(
+            num_scalar_prefetch=1,
+            grid=(columns // tile,),
+            in_specs=[
+                pl.BlockSpec((rows, tile), lambda j, b: (b[0], j)),
+                pl.BlockSpec((rows, tile), lambda j, b: (b[1], j)),
+                piece,
+                piece,
+            ],
+            out_specs=[piece, piece],
+        ),
         out_shape=[jax.ShapeDtypeStruct((rows, columns), jnp.bfloat16)] * 2,
         compiler_params=PARAMS,
-        cost_estimate=cost(4 * rows * width * columns, 2 * width * columns + 8 * rows * columns),
+        cost_estimate=cost(4 * rows * columns, 12 * rows * columns),
         name="message",
-    )(blocks, attended, weight, *arrived)
-
-
-def own_kernel(tile, blocks, attended, weight, result):
-    rows, columns = result.shape
-    mine = rows_at(attended, blocks[0], rows)
-    for at in range(0, columns, tile):
-        here = slice(at, at + tile)
-        result[:, here] = jnp.dot(mine, weight[:, here], preferred_element_type=jnp.float32)
-
-
-def own_projection(blocks, attended, weight, rows, tile):
-    width, columns = weight.shape
-    return pl.pallas_call(
-        functools.partial(own_kernel, tile),
-        in_specs=[SMEM, VMEM, VMEM],
-        out_specs=VMEM,
-        out_shape=jax.ShapeDtypeStruct((rows, columns), jnp.float32),
-        compiler_params=PARAMS,
-        cost_estimate=cost(2 * rows * width * columns, 2 * width * columns + 4 * rows * columns),
-        name="own",
-    )(blocks, attended, weight)
+    )(blocks, projected, projected, *arrived)
 
 
 def final_kernel(blocks, own, gate, up, down, *refs):
     result = refs[-1]
-    summed = own[...] + up[...].astype(jnp.float32) + down[...].astype(jnp.float32)
+    summed = own[...].astype(jnp.float32) + up[...].astype(jnp.float32) + down[...].astype(jnp.float32)
     result[...] = (summed * gate[pl.ds(lax.rem(blocks[1], 8), 1), :]).astype(jnp.bfloat16)
 
 
-def final(blocks, own, gate_table, up, down, first, tile, before):
-    rows, columns = up.shape
+def final(blocks, projected, gate_table, arrived, first, tile, before):
+    rows, columns = arrived[0].shape
     start = first // tile
-    there = pl.BlockSpec((rows, tile), lambda j, b: (0, start + j))
     piece = pl.BlockSpec((rows, tile), lambda j, b: (0, j))
     return pl.pallas_call(
         final_kernel,
@@ -192,19 +201,19 @@
             num_scalar_prefetch=1,
             grid=(columns // tile,),
             in_specs=[
-                there,
+                pl.BlockSpec((rows, tile), lambda j, b: (b[0], j)),
                 pl.BlockSpec((8, tile), lambda j, b: (b[1] // 8, start + j)),
                 piece,
                 piece,
-            ] + [pl.BlockSpec(memory_space=pl.ANY)] * len(before),
-            out_specs=there,
+            ] + [ANY] * len(before),
+            out_specs=pl.BlockSpec((rows, tile), lambda j, b: (0, start + j)),
         ),
-        out_shape=jax.ShapeDtypeStruct(own.shape, jnp.bfloat16),
+        out_shape=jax.ShapeDtypeStruct((rows, gate_table.shape[1]), jnp.bfloat16),
         input_output_aliases={5: 0} if before else {},
         compiler_params=PARAMS,
         cost_estimate=cost(4 * rows * columns, 10 * rows * columns),
         name="final",
-    )(blocks, own, gate_table, up, down, *before)
+    )(blocks, projected, gate_table, *arrived, *before)
 
 
 def body(queries, keys, values, out_weight, gate_table, levels, visible):
@@ -227,7 +236,6 @@
     swap = [(i, i + 1 - 2 * (i % 2)) for i in range(spans)]
     key_beside = lax.ppermute(keys, "span", swap)
     value_beside = lax.ppermute(values, "span", swap)
-    asked_inner = [shifted(query_inner, "span", -distance) for distance in distances]
 
     own, own_sum = pl.pallas_call(
         local_kernel,
@@ -253,8 +261,11 @@
             name="served",
         )(place, visible, asked, keys, values, key_beside, value_beside)
 
-    asked_outer, asked_inner, own_sum = lax.optimization_barrier((asked_outer, asked_inner, own_sum))
-    back_outer = [shifted(served(q, d), "span", d) for q, d in zip(asked_outer, distances)]
+    asked_outer, query_inner, own_sum = lax.optimization_barrier((asked_outer, query_inner, own_sum))
+    asked_inner = [shifted(query_inner, "span", -distance) for distance in distances]
+    out_outer = [served(q, d) for q, d in zip(asked_outer, distances)]
+    back_outer = [shifted(o, "span", d) for o, d in zip(out_outer, distances)]
+    asked_inner, out_outer = lax.optimization_barrier((asked_inner, out_outer))
     back_inner = [shifted(served(q, d), "span", d) for q, d in zip(asked_inner, distances)]
 
     def merge(back, pieces):
@@ -270,31 +281,43 @@
 
     attended_outer = merge(back_outer, [(0, quarter), (rows - quarter, quarter)])
     attended_inner = merge(back_inner, [(quarter, half)])
-    attended = jnp.concatenate([attended_outer[:quarter], attended_inner, attended_outer[quarter:]])
 
     chunks = 2
     columns = model // chunks
-    tile = 512 if columns % 512 == 0 else columns
+    wide = columns // 2
     last = ranks - 1
-    arrived = [()] * chunks
-    for step in range(last):
-        if step == 0:
-            source, blocks = attended_outer, jnp.array([half // block - 1, 0], jnp.int32)
-        else:
-            source = attended
-            blocks = jnp.stack([jnp.minimum(last - step + rank, last), jnp.maximum(step + rank - last, 0)])
+    corner = quarter // block
+
+    def stored(target):
+        late = target + 2 * corner - ranks
+        return jnp.where(target < corner, target, jnp.where(late >= corner, late, target + corner))
+
+    def exchanged(up, down, step):
+        return (
+            lax.ppermute(up, "tensor", [(i, i + 1) for i in range(step + 1)]),
+            lax.ppermute(down, "tensor", [(last - i, last - i - 1) for i in range(step + 1)]),
+        )
+
+    projected, arrived = [], []
+    for chunk in range(chunks):
+        upper, up, down = project(attended_outer, out_weight, chunk, columns, block, wide, ())
+        projected.append(upper)
+        arrived.append(exchanged(up, down, 0))
+    projected = [
+        project(attended_inner, out_weight, chunk, columns, block, wide, (projected[chunk],))[0]
+        for chunk in range(chunks)
+    ]
+    for step in range(1, last):
+        blocks = jnp.stack([
+            stored(jnp.minimum(last - step + rank, last)),
+            stored(jnp.maximum(step + rank - last, 0)),
+        ])
         for chunk in range(chunks):
-            up, down = message(
-                blocks, source, out_weight, arrived[chunk], chunk * columns, columns, block, tile
-            )
-            up = lax.ppermute(up, "tensor", [(i, i + 1) for i in range(step + 1)])
-            down = lax.ppermute(down, "tensor", [(last - i, last - i - 1) for i in range(step + 1)])
-            arrived[chunk] = (up, down)
-    blocks = jnp.stack([rank, level])
-    projected = own_projection(blocks, attended, out_weight, block, tile)
+            arrived[chunk] = exchanged(*message(blocks, projected[chunk], arrived[chunk], wide), step)
+    blocks = jnp.stack([stored(rank), level])
     result = ()
     for chunk in range(chunks):
-        result = (final(blocks, projected, gate_table, *arrived[chunk], chunk * columns, columns // 2, result),)
+        result = (final(blocks, projected[chunk], gate_table, arrived[chunk], chunk * columns, wide, result),)
     return result[0]
 
 

time: 120 us -> 135 us (1.12)
  waiting for transfers between devices: 25.5 us -> 35.6 us
  starting transfers between devices: 36.3 us -> 39 us
  Pallas kernels: 37.2 us -> 39.1 us
    ppermute x4, waiting for transfers between devices: 6.95 us -> 15.1 us  [shifted(): lax.ppermute(block, axis, [(i, i + distance) for i in range(count) if 0 <...]
    ppermute x4, starting transfers between devices: 7.82 us -> 10.5 us  [shifted(): lax.ppermute(block, axis, [(i, i + distance) for i in range(count) if 0 <...]
    ppermute x12, waiting for transfers between devices: 18.6 us -> 20.5 us  [the longest x6 11.6 us: exchanged(): lax.ppermute(up, 'tensor', [(i, i + 1) for i in range(step + 1)])]
    pallas_call x2, Pallas kernels: 3.39 us -> 5.12 us  [final(): pl.pallas_call(final_kernel, grid_spec=pltpu.PrefetchScalarGridSpec(num_s...]
    unnamed x26 -> x50, local copies, waits for them, and re-layouts: 14 us -> 15.3 us
    pallas_call x7 -> x8, Pallas kernels: 19 us -> 19.5 us  [the longest x4 11.1 us: message(): pl.pallas_call(message_kernel, grid_spec=pltpu.PrefetchScalarGridSpec(num...]
  transfers between devices with their start and end apart: 18 -> 18, of which waited for: 8 -> 10; matrix products, arithmetic and copies ran while one was open for 4% -> 4% of each run, Pallas kernels for 27% -> 24%
where the time goes in v4:
time: 135 us; the launch traced here: 134 us
  Pallas kernels  39.1 us (29%)
  starting transfers between devices  39 us (29%)
  waiting for transfers between devices  35.6 us (26%)
  local copies, waits for them, and re-layouts  18.5 us (14%)
  other arithmetic  1.68 us (1%)
    unnamed x50, local copies, waits for them, and re-layouts  15.3 us
    ppermute x4, waiting for transfers between devices, shifted(): lax.ppermute(block, axis, [(i, i + distance) for i in range(count) if 0 <...  15.1 us
    ppermute x6, starting transfers between devices, exchanged(): lax.ppermute(up, 'tensor', [(i, i + 1) for i in range(step + 1)])  14.6 us
    ppermute x6, starting transfers between devices, exchanged(): lax.ppermute(down, 'tensor', [(last - i, last - i - 1) for i in range(ste...  13.4 us
    ppermute x6, waiting for transfers between devices, exchanged(): lax.ppermute(up, 'tensor', [(i, i + 1) for i in range(step + 1)])  11.6 us
    pallas_call x4, Pallas kernels, message(): pl.pallas_call(message_kernel, grid_spec=pltpu.PrefetchScalarGridSpec(num...  11.1 us
    ppermute x4, starting transfers between devices, shifted(): lax.ppermute(block, axis, [(i, i + distance) for i in range(count) if 0 <...  10.5 us
    ppermute x6, waiting for transfers between devices, exchanged(): lax.ppermute(down, 'tensor', [(last - i, last - i - 1) for i in range(ste...  8.88 us
  transfers between devices with their start and end apart: 18, of which 10 were waited for; matrix products, arithmetic and copies ran while one was open for 4% of the time, Pallas kernels for 24%

profile of v4, /device:TPU:14, one launch (start us, length us, event | category | flops | bytes accessed | tf_op | source)
XLA Modules:
  0.0 134.4 jit_solution(16237933878208792778)
XLA Ops:
  2.3 3.1 %collective-permute-start.2 = (bf16[192,768]{1,0:T(8,128)(2,1)}, bf16[192,768]{1,0:T(8,128)(2,1)}, u32[]{:S(2)}, u32[]{:S(2)}) collective-permute-start(bf16[192,768]{1,0:T(8,128)(2,1)} %pad_maximum_fusion), channel_id=1, source_target_pairs={{8,0},{12,4},{9,1},{13,5},{10,2},{14,6},{11,3},{15,7},{24,16},{28,... | collective-permute-start | bytes 884744 | tf_op jit(solution)/shard_map/ppermute | solution.py:27
  5.4 1.7 %slice.11 = bf16[192,768]{1,0:T(8,128)(2,1)} slice(bf16[384,768]{1,0:T(8,128)(2,1)} %query.1), slice={[96:288], [0:768]} | slice | bytes 589824 | tf_op jit(solution)/shard_map/slice | solution.py:233
  7.2 1.3 copy-done.8
  8.5 1.1 copy-done.11
  9.5 1.1 copy-done.20
  11.3 4.3 %local.1 = (f32[384,768]{1,0:T(8,128)S(1)}, f32[384,128]{1,0:T(8,128)S(1)}) custom-call(s32[2]{0:T(128)S(1)} %pad_add_fusion.1.place, s32[4,4]{1,0:T(4,128)S(1)} %copy-done.21, bf16[384,768]{1,0:T(8,128)(2,1)S(1)} %copy-done.20, bf16[384,768]{1,0:T(8,128)(2,1)S(1)} %copy-done.8, bf16[384,768]{1,0:T(8,128)(2,1)S(1)} %copy-done.11, ...), custom_call_target="tpu_custom_call" | custom-call | flops 905969664 | bytes 4128768 | tf_op jit(solution)/shard_map/local/pallas_call | solution.py:240
  15.6 3.6 %served.2 = bf16[192,896]{1,0:T(8,128)(2,1)S(1)} custom-call(s32[2]{0:T(128)S(1)} %pad_add_fusion.1.place, s32[4,4]{1,0:T(4,128)S(1)} %copy-done.21, bf16[192,768]{1,0:T(8,128)(2,1)} %collective-permute-done.2.query, bf16[384,768]{1,0:T(8,128)(2,1)S(1)} %copy-done.9, bf16[384,768]{1,0:T(8,128)(2,1)S(1)} %copy-done.12, ...), custom_call_target="tpu_custom_call" | custom-call | flops 452984832 | bytes 3538944 | tf_op jit(solution)/shard_map/served/pallas_call | solution.py:254
  19.2 1.3 collective-permute-start.5
  20.5 4.6 %collective-permute-start.3 = (bf16[192,768]{1,0:T(8,128)(2,1)S(1)}, bf16[192,768]{1,0:T(8,128)(2,1)S(1)}, u32[]{:S(2)}, u32[]{:S(2)}) collective-permute-start(bf16[192,768]{1,0:T(8,128)(2,1)S(1)} %copy-done.23), channel_id=1, source_target_pairs={{8,0},{12,4},{9,1},{13,5},{10,2},{14,6},{11,3},{15,7},{24,16},{28,... | collective-permute-start | bytes 884744 | tf_op jit(solution)/shard_map/ppermute | solution.py:27
  25.1 5.7 %collective-permute-done.5.refs_0_ = bf16[192,896]{1,0:T(8,128)(2,1)S(1)} collective-permute-done((bf16[192,896]{1,0:T(8,128)(2,1)S(1)}, bf16[192,896]{1,0:T(8,128)(2,1)S(1)}, u32[]{:S(2)}, u32[]{:S(2)}) %collective-permute-start.5) | collective-permute-done | bytes 344096 | tf_op jit(solution)/shard_map/ppermute | solution.py:27
  30.8 1.2 merge.3.attended
  32.0 3.7 %copy-done = bf16[768,6144]{1,0:T(8,128)(2,1)S(1)} copy-done((bf16[768,6144]{1,0:T(8,128)(2,1)S(1)}, bf16[768,6144]{1,0:T(8,128)(2,1)}, u32[]{:S(2)}) %copy-start) | copy-done | bytes 9437208
  35.7 2.5 %project.6 = (bf16[384,3072]{1,0:T(8,128)(2,1)S(1)}, bf16[96,3072]{1,0:T(8,128)(2,1)}, bf16[96,3072]{1,0:T(8,128)(2,1)}) custom-call(bf16[192,768]{1,0:T(8,128)(2,1)S(1)} %merge.3.attended, bf16[768,6144]{1,0:T(8,128)(2,1)S(1)} %copy-done), custom_call_target="tpu_custom_call" | custom-call | flops 905969664 | bytes 7077888 | tf_op jit(solution)/shard_map/project/pallas_call | solution.py:144
  38.2 1.3 collective-permute-start.12
  39.6 1.6 %collective-permute-start.13 = (bf16[96,3072]{1,0:T(8,128)(2,1)}, bf16[96,3072]{1,0:T(8,128)(2,1)}, u32[]{:S(2)}, u32[]{:S(2)}) collective-permute-start(bf16[96,3072]{1,0:T(8,128)(2,1)} %get-tuple-element.40), channel_id=1, source_target_pairs={{3,2},{7,6},{11,10},{15,14},{19,18},{23,22},{27,26},{31,30}} | collective-permute-start | bytes 1769480 | tf_op jit(solution)/shard_map/ppermute | solution.py:298
  41.2 2.5 %project.4 = (bf16[384,3072]{1,0:T(8,128)(2,1)S(1)}, bf16[96,3072]{1,0:T(8,128)(2,1)}, bf16[96,3072]{1,0:T(8,128)(2,1)}) custom-call(bf16[192,768]{1,0:T(8,128)(2,1)S(1)} %merge.3.attended, bf16[768,6144]{1,0:T(8,128)(2,1)S(1)} %copy-done), custom_call_target="tpu_custom_call" | custom-call | flops 905969664 | bytes 7077888 | tf_op jit(solution)/shard_map/project/pallas_call | solution.py:144
  43.7 1.4 %copy-done.2 = bf16[384,3072]{1,0:T(8,128)(2,1)} copy-done((bf16[384,3072]{1,0:T(8,128)(2,1)}, bf16[384,3072]{1,0:T(8,128)(2,1)S(1)}, u32[]{:S(2)}) %copy-start.2) | copy-done | bytes 2359320
  45.1 1.3 collective-permute-start.6
  46.4 1.5 %collective-permute-start.7 = (bf16[96,3072]{1,0:T(8,128)(2,1)}, bf16[96,3072]{1,0:T(8,128)(2,1)}, u32[]{:S(2)}, u32[]{:S(2)}) collective-permute-start(bf16[96,3072]{1,0:T(8,128)(2,1)} %get-tuple-element.33), channel_id=1, source_target_pairs={{3,2},{7,6},{11,10},{15,14},{19,18},{23,22},{27,26},{31,30}} | collective-permute-start | bytes 1769480 | tf_op jit(solution)/shard_map/ppermute | solution.py:298
  48.0 3.9 %served.3 = bf16[192,896]{1,0:T(8,128)(2,1)} custom-call(s32[2]{0:T(128)S(1)} %pad_add_fusion.1.place, s32[4,4]{1,0:T(4,128)S(1)} %copy-done.22, bf16[192,768]{1,0:T(8,128)(2,1)S(1)} %collective-permute-done.3.query, bf16[384,768]{1,0:T(8,128)(2,1)S(1)} %copy-done.10, bf16[384,768]{1,0:T(8,128)(2,1)S(1)} %copy-done.13, bf16[384,768]{1,0:T(8,128)(2,1)S(1)} %copy-done.15, ...), custom_call_target="tpu_custom_call" | custom-call | flops 452984832 | bytes 3538944 | tf_op jit(solution)/shard_map/served/pallas_call | solution.py:254
  51.9 1.5 %collective-permute-start.4 = (bf16[192,896]{1,0:T(8,128)(2,1)}, bf16[192,896]{1,0:T(8,128)(2,1)}, u32[]{:S(2)}, u32[]{:S(2)}) collective-permute-start(bf16[192,896]{1,0:T(8,128)(2,1)} %served.3), channel_id=1, source_target_pairs={{0,8},{4,12},{1,9},{5,13},{2,10},{6,14},{3,11},{7,15},{16,24},{20,... | collective-permute-start | bytes 1032200 | tf_op jit(solution)/shard_map/ppermute | solution.py:27
  53.4 9.4 %collective-permute-done.4.refs_0_ = bf16[192,896]{1,0:T(8,128)(2,1)} collective-permute-done((bf16[192,896]{1,0:T(8,128)(2,1)}, bf16[192,896]{1,0:T(8,128)(2,1)}, u32[]{:S(2)}, u32[]{:S(2)}) %collective-permute-start.4) | collective-permute-done | bytes 344096 | tf_op jit(solution)/shard_map/ppermute | solution.py:27
  63.8 1.5 %merge.2.attended = bf16[192,768]{1,0:T(8,128)(2,1)S(1)} custom-call(s32[2]{0:T(128)S(1)} %pad_add_fusion.1.place, f32[384,768]{1,0:T(8,128)S(1)} %get-tuple-element.25.own, f32[384,128]{1,0:T(8,128)S(1)} %copy-done.19, bf16[192,896]{1,0:T(8,128)(2,1)} %collective-permute-done.4.refs_0_), custom_call_target="tpu_custom_call" | custom-call | flops 1179648 | bytes 1474560 | tf_op jit(solution)/shard_map/merge/pallas_call | solution.py:272
  65.3 3.7 %copy-done.1 = bf16[768,6144]{1,0:T(8,128)(2,1)S(1)} copy-done((bf16[768,6144]{1,0:T(8,128)(2,1)S(1)}, bf16[768,6144]{1,0:T(8,128)(2,1)}, u32[]{:S(2)}) %copy-start.1) | copy-done | bytes 9437208
  69.0 1.7 %project.7.up_block.down_block.own = bf16[384,3072]{1,0:T(8,128)(2,1)S(1)} custom-call(bf16[192,768]{1,0:T(8,128)(2,1)S(1)} %merge.2.attended, bf16[768,6144]{1,0:T(8,128)(2,1)S(1)} %copy-done.1, bf16[384,3072]{1,0:T(8,128)(2,1)S(1)} %get-tuple-element.38.refs_0_), custom_call_target="tpu_custom_call", output_to_operand_aliasing={{}: (2, {})} | custom-call | flops 905969664 | bytes 7077888 | tf_op jit(solution)/shard_map/project/pallas_call | solution.py:144
  70.6 1.7 %project.5.up_block.down_block.own = bf16[384,3072]{1,0:T(8,128)(2,1)S(1)} custom-call(bf16[192,768]{1,0:T(8,128)(2,1)S(1)} %merge.2.attended, bf16[768,6144]{1,0:T(8,128)(2,1)S(1)} %copy-done.1, bf16[384,3072]{1,0:T(8,128)(2,1)S(1)} %copy-done.3), custom_call_target="tpu_custom_call", output_to_operand_aliasing={{}: (2, {})} | custom-call | flops 905969664 | bytes 7077888 | tf_op jit(solution)/shard_map/project/pallas_call | solution.py:144
  72.4 2.9 %message.6 = (bf16[96,3072]{1,0:T(8,128)(2,1)}, bf16[96,3072]{1,0:T(8,128)(2,1)}) custom-call(s32[2]{0:T(128)S(1)} %pad_add_fusion.3.blocks, bf16[384,3072]{1,0:T(8,128)(2,1)S(1)} %project.7.up_block.down_block.own, bf16[384,3072]{1,0:T(8,128)(2,1)S(1)} %project.7.up_block.down_block.own, bf16[96,3072]{1,0:T(8,128)(2,1)} %collective-permute-done.12.up_arrived, ...), custom_call_target="tpu_custom_call" | custom-call | flops 1179648 | bytes 3538944 | tf_op jit(solution)/shard_map/message/pallas_call | solution.py:168
  75.3 3.5 %collective-permute-start.14 = (bf16[96,3072]{1,0:T(8,128)(2,1)}, bf16[96,3072]{1,0:T(8,128)(2,1)S(1)}, u32[]{:S(2)}, u32[]{:S(2)}) collective-permute-start(bf16[96,3072]{1,0:T(8,128)(2,1)} %get-tuple-element.41), channel_id=1, source_target_pairs={{0,1},{1,2},{4,5},{5,6},{8,9},{9,10},{12,13},{13,14},{16,17},{17,1... | collective-permute-start | bytes 1769480 | tf_op jit(solution)/shard_map/ppermute | solution.py:297
  78.8 1.3 collective-permute-start.15
  80.1 2.8 %message.4 = (bf16[96,3072]{1,0:T(8,128)(2,1)}, bf16[96,3072]{1,0:T(8,128)(2,1)}) custom-call(s32[2]{0:T(128)S(1)} %pad_add_fusion.3.blocks, bf16[384,3072]{1,0:T(8,128)(2,1)S(1)} %project.5.up_block.down_block.own, bf16[384,3072]{1,0:T(8,128)(2,1)S(1)} %project.5.up_block.down_block.own, bf16[96,3072]{1,0:T(8,128)(2,1)} %collective-permute-done.6.up_arrived, ...), custom_call_target="tpu_custom_call" | custom-call | flops 1179648 | bytes 3538944 | tf_op jit(solution)/shard_map/message/pallas_call | solution.py:168
  82.9 4.5 %collective-permute-start.8 = (bf16[96,3072]{1,0:T(8,128)(2,1)}, bf16[96,3072]{1,0:T(8,128)(2,1)S(1)}, u32[]{:S(2)}, u32[]{:S(2)}) collective-permute-start(bf16[96,3072]{1,0:T(8,128)(2,1)} %get-tuple-element.34), channel_id=1, source_target_pairs={{0,1},{1,2},{4,5},{5,6},{8,9},{9,10},{12,13},{13,14},{16,17},{17,1... | collective-permute-start | bytes 1769480 | tf_op jit(solution)/shard_map/ppermute | solution.py:297
  87.4 1.3 collective-permute-start.9
  88.8 6.2 %collective-permute-done.14.up_arrived = bf16[96,3072]{1,0:T(8,128)(2,1)S(1)} collective-permute-done((bf16[96,3072]{1,0:T(8,128)(2,1)}, bf16[96,3072]{1,0:T(8,128)(2,1)S(1)}, u32[]{:S(2)}, u32[]{:S(2)}) %collective-permute-start.14) | collective-permute-done | bytes 589856 | tf_op jit(solution)/shard_map/ppermute | solution.py:297
  95.0 2.3 %collective-permute-done.15.down_arrived = bf16[96,3072]{1,0:T(8,128)(2,1)} collective-permute-done((bf16[96,3072]{1,0:T(8,128)(2,1)}, bf16[96,3072]{1,0:T(8,128)(2,1)}, u32[]{:S(2)}, u32[]{:S(2)}) %collective-permute-start.15) | collective-permute-done | bytes 589856 | tf_op jit(solution)/shard_map/ppermute | solution.py:298
  97.3 2.7 %message.7 = (bf16[96,3072]{1,0:T(8,128)(2,1)}, bf16[96,3072]{1,0:T(8,128)(2,1)}) custom-call(s32[2]{0:T(128)S(1)} %pad_add_fusion.2.blocks, bf16[384,3072]{1,0:T(8,128)(2,1)S(1)} %project.7.up_block.down_block.own, bf16[384,3072]{1,0:T(8,128)(2,1)S(1)} %project.7.up_block.down_block.own, bf16[96,3072]{1,0:T(8,128)(2,1)S(1)} %collective-permute-done.14.up_arrived, ...), custom_call_target="tpu_custom_call" | custom-call | flops 1179648 | bytes 3538944 | tf_op jit(solution)/shard_map/message/pallas_call | solution.py:168
  100.0 2.0 %collective-permute-start.16 = (bf16[96,3072]{1,0:T(8,128)(2,1)}, bf16[96,3072]{1,0:T(8,128)(2,1)S(1)}, u32[]{:S(2)}, u32[]{:S(2)}) collective-permute-start(bf16[96,3072]{1,0:T(8,128)(2,1)} %get-tuple-element.43), channel_id=1, source_target_pairs={{0,1},{1,2},{2,3},{4,5},{5,6},{6,7},{8,9},{9,10},{10,11},{12,13},{... | collective-permute-start | bytes 1769480 | tf_op jit(solution)/shard_map/ppermute | solution.py:297
  102.0 3.9 %collective-permute-start.17 = (bf16[96,3072]{1,0:T(8,128)(2,1)}, bf16[96,3072]{1,0:T(8,128)(2,1)}, u32[]{:S(2)}, u32[]{:S(2)}) collective-permute-start(bf16[96,3072]{1,0:T(8,128)(2,1)} %get-tuple-element.44), channel_id=1, source_target_pairs={{3,2},{2,1},{1,0},{7,6},{6,5},{5,4},{11,10},{10,9},{9,8},{15,14},{... | collective-permute-start | bytes 1769480 | tf_op jit(solution)/shard_map/ppermute | solution.py:298
  105.9 1.8 %collective-permute-done.8.up_arrived = bf16[96,3072]{1,0:T(8,128)(2,1)S(1)} collective-permute-done((bf16[96,3072]{1,0:T(8,128)(2,1)}, bf16[96,3072]{1,0:T(8,128)(2,1)S(1)}, u32[]{:S(2)}, u32[]{:S(2)}) %collective-permute-start.8) | collective-permute-done | bytes 589856 | tf_op jit(solution)/shard_map/ppermute | solution.py:297
  107.6 2.3 %collective-permute-done.9.down_arrived = bf16[96,3072]{1,0:T(8,128)(2,1)} collective-permute-done((bf16[96,3072]{1,0:T(8,128)(2,1)}, bf16[96,3072]{1,0:T(8,128)(2,1)}, u32[]{:S(2)}, u32[]{:S(2)}) %collective-permute-start.9) | collective-permute-done | bytes 589856 | tf_op jit(solution)/shard_map/ppermute | solution.py:298
  109.9 2.7 %message.5 = (bf16[96,3072]{1,0:T(8,128)(2,1)}, bf16[96,3072]{1,0:T(8,128)(2,1)}) custom-call(s32[2]{0:T(128)S(1)} %pad_add_fusion.2.blocks, bf16[384,3072]{1,0:T(8,128)(2,1)S(1)} %copy-done.5, bf16[384,3072]{1,0:T(8,128)(2,1)S(1)} %copy-done.5, bf16[96,3072]{1,0:T(8,128)(2,1)S(1)} %collective-permute-done.8.up_arrived, ...), custom_call_target="tpu_custom_call" | custom-call | flops 1179648 | bytes 3538944 | tf_op jit(solution)/shard_map/message/pallas_call | solution.py:168
  112.6 2.0 %collective-permute-start.10 = (bf16[96,3072]{1,0:T(8,128)(2,1)}, bf16[96,3072]{1,0:T(8,128)(2,1)S(1)}, u32[]{:S(2)}, u32[]{:S(2)}) collective-permute-start(bf16[96,3072]{1,0:T(8,128)(2,1)} %get-tuple-element.36), channel_id=1, source_target_pairs={{0,1},{1,2},{2,3},{4,5},{5,6},{6,7},{8,9},{9,10},{10,11},{12,13},{... | collective-permute-start | bytes 1769480 | tf_op jit(solution)/shard_map/ppermute | solution.py:297
  114.6 3.9 %collective-permute-start.11 = (bf16[96,3072]{1,0:T(8,128)(2,1)}, bf16[96,3072]{1,0:T(8,128)(2,1)}, u32[]{:S(2)}, u32[]{:S(2)}) collective-permute-start(bf16[96,3072]{1,0:T(8,128)(2,1)} %get-tuple-element.37), channel_id=1, source_target_pairs={{3,2},{2,1},{1,0},{7,6},{6,5},{5,4},{11,10},{10,9},{9,8},{15,14},{... | collective-permute-start | bytes 1769480 | tf_op jit(solution)/shard_map/ppermute | solution.py:298
  120.3 2.3 %collective-permute-done.17.down = bf16[96,3072]{1,0:T(8,128)(2,1)} collective-permute-done((bf16[96,3072]{1,0:T(8,128)(2,1)}, bf16[96,3072]{1,0:T(8,128)(2,1)}, u32[]{:S(2)}, u32[]{:S(2)}) %collective-permute-start.17) | collective-permute-done | bytes 589856 | tf_op jit(solution)/shard_map/ppermute | solution.py:298
  122.6 1.4 %copy-done.7 = f32[64,6144]{1,0:T(8,128)S(1)} copy-done((f32[64,6144]{1,0:T(8,128)S(1)}, f32[64,6144]{1,0:T(8,128)}, u32[]{:S(2)}) %copy-start.7) | copy-done | bytes 1572888
  124.0 2.6 %final.2.refs_0_ = bf16[96,6144]{1,0:T(8,128)(2,1)} custom-call(s32[2]{0:T(128)S(1)} %pad_add_fusion.blocks, bf16[384,3072]{1,0:T(8,128)(2,1)S(1)} %project.7.up_block.down_block.own, f32[64,6144]{1,0:T(8,128)S(1)} %copy-done.7, bf16[96,3072]{1,0:T(8,128)(2,1)S(1)} %collective-permute-done.16.up, bf16[96,3072]{1,0:T(8,128)(2,1)} %collective-permute-done.17.down), custom_call_target="tpu_custom_call" | custom-call | flops 1179648 | bytes 2949120 | tf_op jit(solution)/shard_map/final/pallas_call | solution.py:198
  126.5 3.3 %collective-permute-done.10.up = bf16[96,3072]{1,0:T(8,128)(2,1)S(1)} collective-permute-done((bf16[96,3072]{1,0:T(8,128)(2,1)}, bf16[96,3072]{1,0:T(8,128)(2,1)S(1)}, u32[]{:S(2)}, u32[]{:S(2)}) %collective-permute-start.10) | collective-permute-done | bytes 589856 | tf_op jit(solution)/shard_map/ppermute | solution.py:297
  129.8 2.0 %collective-permute-done.11.down = bf16[96,3072]{1,0:T(8,128)(2,1)} collective-permute-done((bf16[96,3072]{1,0:T(8,128)(2,1)}, bf16[96,3072]{1,0:T(8,128)(2,1)}, u32[]{:S(2)}, u32[]{:S(2)}) %collective-permute-start.11) | collective-permute-done | bytes 589856 | tf_op jit(solution)/shard_map/ppermute | solution.py:298
  131.8 2.6 %final.3 = bf16[96,6144]{1,0:T(8,128)(2,1)} custom-call(s32[2]{0:T(128)S(1)} %pad_add_fusion.blocks, bf16[384,3072]{1,0:T(8,128)(2,1)S(1)} %copy-done.6, f32[64,6144]{1,0:T(8,128)S(1)} %copy-done.7, bf16[96,3072]{1,0:T(8,128)(2,1)S(1)} %collective-permute-done.10.up, bf16[96,3072]{1,0:T(8,128)(2,1)} %collective-permute-done.11.down, ...), custom_call_target="tpu_custom_call", output_to_operand_aliasing={{}: (5, {})} | custom-call | flops 1179648 | bytes 2949120 | tf_op jit(solution)/shard_map/final/pallas_call | solution.py:198
  (61 shorter events, 5.9 us)
Async XLA Ops:
  0.0 7.2 %collective-permute-start = (bf16[384,768]{1,0:T(8,128)(2,1)}, bf16[384,768]{1,0:T(8,128)(2,1)S(1)}, u32[]{:S(2)}, u32[]{:S(2)}) collective-permute-start(bf16[384,768]{1,0:T(8,128)(2,1)} %key.5), channel_id=1, source_target_pairs={{0,4},{4,0},{8,12},{12,8},{1,5},{5,1},{9,13},{13,9},{2,6},{6,2},{1... | collective-permute-start | bytes 1769480 | tf_op jit(solution)/shard_map/ppermute | solution.py:237
  0.0 7.2 %collective-permute-start.1 = (bf16[384,768]{1,0:T(8,128)(2,1)}, bf16[384,768]{1,0:T(8,128)(2,1)S(1)}, u32[]{:S(2)}, u32[]{:S(2)}) collective-permute-start(bf16[384,768]{1,0:T(8,128)(2,1)} %value.5), channel_id=1, source_target_pairs={{0,4},{4,0},{8,12},{12,8},{1,5},{5,1},{9,13},{13,9},{2,6},{6,2},{1... | collective-permute-start | bytes 1769480 | tf_op jit(solution)/shard_map/ppermute | solution.py:238
  1.5 14.0 %copy-start.9 = (bf16[384,768]{1,0:T(8,128)(2,1)S(1)}, bf16[384,768]{1,0:T(8,128)(2,1)}, u32[]{:S(2)}) copy-start(bf16[384,768]{1,0:T(8,128)(2,1)} %key.5) | copy-start | bytes 1769476
  1.5 14.0 %copy-start.12 = (bf16[384,768]{1,0:T(8,128)(2,1)S(1)}, bf16[384,768]{1,0:T(8,128)(2,1)}, u32[]{:S(2)}) copy-start(bf16[384,768]{1,0:T(8,128)(2,1)} %value.5) | copy-start | bytes 1769476
  2.3 13.3 %collective-permute-start.2 = (bf16[192,768]{1,0:T(8,128)(2,1)}, bf16[192,768]{1,0:T(8,128)(2,1)}, u32[]{:S(2)}, u32[]{:S(2)}) collective-permute-start(bf16[192,768]{1,0:T(8,128)(2,1)} %pad_maximum_fusion), channel_id=1, source_target_pairs={{8,0},{12,4},{9,1},{13,5},{10,2},{14,6},{11,3},{15,7},{24,16},{28,... | collective-permute-start | bytes 884744 | tf_op jit(solution)/shard_map/ppermute | solution.py:27
  7.2 12.0 %copy-start.14 = (bf16[384,768]{1,0:T(8,128)(2,1)}, bf16[384,768]{1,0:T(8,128)(2,1)S(1)}, u32[]{:S(2)}) copy-start(bf16[384,768]{1,0:T(8,128)(2,1)S(1)} %collective-permute-done.key_beside) | copy-start | bytes 1769476
  7.2 1.3 copy-start.8
  8.5 1.1 copy-start.11
  9.5 1.1 copy-start.20
  10.6 0.7 copy-start.21
  11.3 7.9 %copy-start.16 = (bf16[384,768]{1,0:T(8,128)(2,1)}, bf16[384,768]{1,0:T(8,128)(2,1)S(1)}, u32[]{:S(2)}) copy-start(bf16[384,768]{1,0:T(8,128)(2,1)S(1)} %collective-permute-done.1.value_beside) | copy-start | bytes 1769476
  11.3 9.2 %copy-start.23 = (bf16[192,768]{1,0:T(8,128)(2,1)S(1)}, bf16[192,768]{1,0:T(8,128)(2,1)}, u32[]{:S(2)}) copy-start(bf16[192,768]{1,0:T(8,128)(2,1)} %slice.11) | copy-start | bytes 884740
  15.5 15.3 %copy-start.18 = (f32[384,128]{1,0:T(8,128)}, f32[384,128]{1,0:T(8,128)S(1)}, u32[]{:S(2)}) copy-start(f32[384,128]{1,0:T(8,128)S(1)} %get-tuple-element.27.own_sum) | copy-start | bytes 589828
  19.2 11.6 %collective-permute-start.5 = (bf16[192,896]{1,0:T(8,128)(2,1)S(1)}, bf16[192,896]{1,0:T(8,128)(2,1)S(1)}, u32[]{:S(2)}, u32[]{:S(2)}) collective-permute-start(bf16[192,896]{1,0:T(8,128)(2,1)S(1)} %served.2), channel_id=1, source_target_pairs={{0,8},{4,12},{1,9},{5,13},{2,10},{6,14},{3,11},{7,15},{16,24},{20,... | collective-permute-start | bytes 1032200 | tf_op jit(solution)/shard_map/ppermute | solution.py:27
  20.5 27.4 %collective-permute-start.3 = (bf16[192,768]{1,0:T(8,128)(2,1)S(1)}, bf16[192,768]{1,0:T(8,128)(2,1)S(1)}, u32[]{:S(2)}, u32[]{:S(2)}) collective-permute-start(bf16[192,768]{1,0:T(8,128)(2,1)S(1)} %copy-done.23), channel_id=1, source_target_pairs={{8,0},{12,4},{9,1},{13,5},{10,2},{14,6},{11,3},{15,7},{24,16},{28,... | collective-permute-start | bytes 884744 | tf_op jit(solution)/shard_map/ppermute | solution.py:27
  32.0 3.7 %copy-start = (bf16[768,6144]{1,0:T(8,128)(2,1)S(1)}, bf16[768,6144]{1,0:T(8,128)(2,1)}, u32[]{:S(2)}) copy-start(bf16[768,6144]{1,0:T(8,128)(2,1)} %weight.7) | copy-start | bytes 28311556
  38.2 34.1 %collective-permute-start.12 = (bf16[96,3072]{1,0:T(8,128)(2,1)}, bf16[96,3072]{1,0:T(8,128)(2,1)}, u32[]{:S(2)}, u32[]{:S(2)}) collective-permute-start(bf16[96,3072]{1,0:T(8,128)(2,1)} %get-tuple-element.39), channel_id=1, source_target_pairs={{0,1},{4,5},{8,9},{12,13},{16,17},{20,21},{24,25},{28,29}} | collective-permute-start | bytes 1769480 | tf_op jit(solution)/shard_map/ppermute | solution.py:297
  39.5 8.4 %copy-start.10 = (bf16[384,768]{1,0:T(8,128)(2,1)S(1)}, bf16[384,768]{1,0:T(8,128)(2,1)}, u32[]{:S(2)}) copy-start(bf16[384,768]{1,0:T(8,128)(2,1)} %key.5) | copy-start | bytes 1769476
  39.5 8.4 %copy-start.13 = (bf16[384,768]{1,0:T(8,128)(2,1)S(1)}, bf16[384,768]{1,0:T(8,128)(2,1)}, u32[]{:S(2)}) copy-start(bf16[384,768]{1,0:T(8,128)(2,1)} %value.5) | copy-start | bytes 1769476
  39.5 8.4 %copy-start.15 = (bf16[384,768]{1,0:T(8,128)(2,1)S(1)}, bf16[384,768]{1,0:T(8,128)(2,1)}, u32[]{:S(2)}) copy-start(bf16[384,768]{1,0:T(8,128)(2,1)} %copy-done.14) | copy-start | bytes 1769476
  39.5 8.4 %copy-start.17 = (bf16[384,768]{1,0:T(8,128)(2,1)S(1)}, bf16[384,768]{1,0:T(8,128)(2,1)}, u32[]{:S(2)}) copy-start(bf16[384,768]{1,0:T(8,128)(2,1)} %copy-done.16) | copy-start | bytes 1769476
  39.6 8.4 %copy-start.22 = (s32[4,4]{1,0:T(4,128)S(1)}, s32[4,4]{1,0:T(4,128)}, u32[]{:S(2)}) copy-start(s32[4,4]{1,0:T(4,128)} %visible.5) | copy-start | bytes 196
  39.6 32.8 %collective-permute-start.13 = (bf16[96,3072]{1,0:T(8,128)(2,1)}, bf16[96,3072]{1,0:T(8,128)(2,1)}, u32[]{:S(2)}, u32[]{:S(2)}) collective-permute-start(bf16[96,3072]{1,0:T(8,128)(2,1)} %get-tuple-element.40), channel_id=1, source_target_pairs={{3,2},{7,6},{11,10},{15,14},{19,18},{23,22},{27,26},{31,30}} | collective-permute-start | bytes 1769480 | tf_op jit(solution)/shard_map/ppermute | solution.py:298
  43.7 1.4 %copy-start.2 = (bf16[384,3072]{1,0:T(8,128)(2,1)}, bf16[384,3072]{1,0:T(8,128)(2,1)S(1)}, u32[]{:S(2)}) copy-start(bf16[384,3072]{1,0:T(8,128)(2,1)S(1)} %get-tuple-element.31.refs_0_) | copy-start | bytes 7077892
  45.1 35.0 %collective-permute-start.6 = (bf16[96,3072]{1,0:T(8,128)(2,1)}, bf16[96,3072]{1,0:T(8,128)(2,1)}, u32[]{:S(2)}, u32[]{:S(2)}) collective-permute-start(bf16[96,3072]{1,0:T(8,128)(2,1)} %get-tuple-element.32), channel_id=1, source_target_pairs={{0,1},{4,5},{8,9},{12,13},{16,17},{20,21},{24,25},{28,29}} | collective-permute-start | bytes 1769480 | tf_op jit(solution)/shard_map/ppermute | solution.py:297
  46.4 33.7 %collective-permute-start.7 = (bf16[96,3072]{1,0:T(8,128)(2,1)}, bf16[96,3072]{1,0:T(8,128)(2,1)}, u32[]{:S(2)}, u32[]{:S(2)}) collective-permute-start(bf16[96,3072]{1,0:T(8,128)(2,1)} %get-tuple-element.33), channel_id=1, source_target_pairs={{3,2},{7,6},{11,10},{15,14},{19,18},{23,22},{27,26},{31,30}} | collective-permute-start | bytes 1769480 | tf_op jit(solution)/shard_map/ppermute | solution.py:298
  51.9 11.0 %collective-permute-start.4 = (bf16[192,896]{1,0:T(8,128)(2,1)}, bf16[192,896]{1,0:T(8,128)(2,1)}, u32[]{:S(2)}, u32[]{:S(2)}) collective-permute-start(bf16[192,896]{1,0:T(8,128)(2,1)} %served.3), channel_id=1, source_target_pairs={{0,8},{4,12},{1,9},{5,13},{2,10},{6,14},{3,11},{7,15},{16,24},{20,... | collective-permute-start | bytes 1032200 | tf_op jit(solution)/shard_map/ppermute | solution.py:27
  62.9 0.9 copy-start.19
  65.3 3.7 %copy-start.1 = (bf16[768,6144]{1,0:T(8,128)(2,1)S(1)}, bf16[768,6144]{1,0:T(8,128)(2,1)}, u32[]{:S(2)}) copy-start(bf16[768,6144]{1,0:T(8,128)(2,1)} %weight.7) | copy-start | bytes 28311556
  68.9 1.7 %copy-start.3 = (bf16[384,3072]{1,0:T(8,128)(2,1)S(1)}, bf16[384,3072]{1,0:T(8,128)(2,1)}, u32[]{:S(2)}) copy-start(bf16[384,3072]{1,0:T(8,128)(2,1)} %copy-done.2) | copy-start | bytes 7077892
  72.3 7.8 %copy-start.4 = (bf16[384,3072]{1,0:T(8,128)(2,1)}, bf16[384,3072]{1,0:T(8,128)(2,1)S(1)}, u32[]{:S(2)}) copy-start(bf16[384,3072]{1,0:T(8,128)(2,1)S(1)} %project.5.up_block.down_block.own) | copy-start | bytes 7077892
  75.3 19.7 %collective-permute-start.14 = (bf16[96,3072]{1,0:T(8,128)(2,1)}, bf16[96,3072]{1,0:T(8,128)(2,1)S(1)}, u32[]{:S(2)}, u32[]{:S(2)}) collective-permute-start(bf16[96,3072]{1,0:T(8,128)(2,1)} %get-tuple-element.41), channel_id=1, source_target_pairs={{0,1},{1,2},{4,5},{5,6},{8,9},{9,10},{12,13},{13,14},{16,17},{17,1... | collective-permute-start | bytes 1769480 | tf_op jit(solution)/shard_map/ppermute | solution.py:297
  78.8 18.5 %collective-permute-start.15 = (bf16[96,3072]{1,0:T(8,128)(2,1)}, bf16[96,3072]{1,0:T(8,128)(2,1)}, u32[]{:S(2)}, u32[]{:S(2)}) collective-permute-start(bf16[96,3072]{1,0:T(8,128)(2,1)} %get-tuple-element.42), channel_id=1, source_target_pairs={{3,2},{2,1},{7,6},{6,5},{11,10},{10,9},{15,14},{14,13},{19,18},{18... | collective-permute-start | bytes 1769480 | tf_op jit(solution)/shard_map/ppermute | solution.py:298
  82.9 24.7 %collective-permute-start.8 = (bf16[96,3072]{1,0:T(8,128)(2,1)}, bf16[96,3072]{1,0:T(8,128)(2,1)S(1)}, u32[]{:S(2)}, u32[]{:S(2)}) collective-permute-start(bf16[96,3072]{1,0:T(8,128)(2,1)} %get-tuple-element.34), channel_id=1, source_target_pairs={{0,1},{1,2},{4,5},{5,6},{8,9},{9,10},{12,13},{13,14},{16,17},{17,1... | collective-permute-start | bytes 1769480 | tf_op jit(solution)/shard_map/ppermute | solution.py:297
  87.4 22.5 %collective-permute-start.9 = (bf16[96,3072]{1,0:T(8,128)(2,1)}, bf16[96,3072]{1,0:T(8,128)(2,1)}, u32[]{:S(2)}, u32[]{:S(2)}) collective-permute-start(bf16[96,3072]{1,0:T(8,128)(2,1)} %get-tuple-element.35), channel_id=1, source_target_pairs={{3,2},{2,1},{7,6},{6,5},{11,10},{10,9},{15,14},{14,13},{19,18},{18... | collective-permute-start | bytes 1769480 | tf_op jit(solution)/shard_map/ppermute | solution.py:298
  88.8 21.1 %copy-start.5 = (bf16[384,3072]{1,0:T(8,128)(2,1)S(1)}, bf16[384,3072]{1,0:T(8,128)(2,1)}, u32[]{:S(2)}) copy-start(bf16[384,3072]{1,0:T(8,128)(2,1)} %copy-done.4) | copy-start | bytes 7077892
  100.0 20.3 %collective-permute-start.16 = (bf16[96,3072]{1,0:T(8,128)(2,1)}, bf16[96,3072]{1,0:T(8,128)(2,1)S(1)}, u32[]{:S(2)}, u32[]{:S(2)}) collective-permute-start(bf16[96,3072]{1,0:T(8,128)(2,1)} %get-tuple-element.43), channel_id=1, source_target_pairs={{0,1},{1,2},{2,3},{4,5},{5,6},{6,7},{8,9},{9,10},{10,11},{12,13},{... | collective-permute-start | bytes 1769480 | tf_op jit(solution)/shard_map/ppermute | solution.py:297
  102.0 16.5 %copy-start.24 = (s32[4]{0:T(128)S(1)}, s32[4]{0:T(128)}, u32[]{:S(2)}) copy-start(s32[4]{0:T(128)} %param.12) | copy-start | bytes 52
  102.0 20.6 %collective-permute-start.17 = (bf16[96,3072]{1,0:T(8,128)(2,1)}, bf16[96,3072]{1,0:T(8,128)(2,1)}, u32[]{:S(2)}, u32[]{:S(2)}) collective-permute-start(bf16[96,3072]{1,0:T(8,128)(2,1)} %get-tuple-element.44), channel_id=1, source_target_pairs={{3,2},{2,1},{1,0},{7,6},{6,5},{5,4},{11,10},{10,9},{9,8},{15,14},{... | collective-permute-start | bytes 1769480 | tf_op jit(solution)/shard_map/ppermute | solution.py:298
  112.6 17.1 %collective-permute-start.10 = (bf16[96,3072]{1,0:T(8,128)(2,1)}, bf16[96,3072]{1,0:T(8,128)(2,1)S(1)}, u32[]{:S(2)}, u32[]{:S(2)}) collective-permute-start(bf16[96,3072]{1,0:T(8,128)(2,1)} %get-tuple-element.36), channel_id=1, source_target_pairs={{0,1},{1,2},{2,3},{4,5},{5,6},{6,7},{8,9},{9,10},{10,11},{12,13},{... | collective-permute-start | bytes 1769480 | tf_op jit(solution)/shard_map/ppermute | solution.py:297
  114.6 17.2 %collective-permute-start.11 = (bf16[96,3072]{1,0:T(8,128)(2,1)}, bf16[96,3072]{1,0:T(8,128)(2,1)}, u32[]{:S(2)}, u32[]{:S(2)}) collective-permute-start(bf16[96,3072]{1,0:T(8,128)(2,1)} %get-tuple-element.37), channel_id=1, source_target_pairs={{3,2},{2,1},{1,0},{7,6},{6,5},{5,4},{11,10},{10,9},{9,8},{15,14},{... | collective-permute-start | bytes 1769480 | tf_op jit(solution)/shard_map/ppermute | solution.py:298
  119.8 12.0 %copy-start.6 = (bf16[384,3072]{1,0:T(8,128)(2,1)S(1)}, bf16[384,3072]{1,0:T(8,128)(2,1)}, u32[]{:S(2)}) copy-start(bf16[384,3072]{1,0:T(8,128)(2,1)} %copy-done.4) | copy-start | bytes 7077892
  122.6 1.4 %copy-start.7 = (f32[64,6144]{1,0:T(8,128)S(1)}, f32[64,6144]{1,0:T(8,128)}, u32[]{:S(2)}) copy-start(f32[64,6144]{1,0:T(8,128)} %gate.3) | copy-start | bytes 4718596

commit v5 on v4

--- a/solution.py
+++ b/solution.py
@@ -13,6 +13,7 @@
 LOG2E = 1.4426950408889634
 PARAMS = pltpu.CompilerParams(vmem_limit_bytes=24 * 1024 * 1024)
 ANY = pl.BlockSpec(memory_space=pl.ANY)
+HBM = pl.BlockSpec(memory_space=pltpu.HBM)
 SMEM = pl.BlockSpec(memory_space=pltpu.SMEM)
 VMEM = pl.BlockSpec(memory_space=pltpu.VMEM)
 PIECE_LANES = 32
@@ -67,6 +68,24 @@
     return span + 1 - 2 * lax.rem(span, 2)
 
 
+def split_kernel(place, query, outer, semaphores):
+    rows = query.shape[0]
+    quarter = rows // 4
+
+    @pl.when(place[0] > 1)
+    def _():
+        copies = [
+            pltpu.make_async_copy(
+                query.at[pl.ds(start, quarter)], outer.at[pl.ds(index * quarter, quarter)], semaphores.at[index]
+            )
+            for index, start in enumerate((0, rows - quarter))
+        ]
+        for copy in copies:
+            copy.start()
+        for copy in copies:
+            copy.wait()
+
+
 def local_kernel(place, visible, query, key, value, key_beside, value_beside, result, sums):
     span = place[0]
 
@@ -78,22 +97,25 @@
     )
 
 
-def served_kernel(distance, place, visible, query, key, value, key_beside, value_beside, result):
+def served_kernel(distance, spans, place, visible, query, key, value, key_beside, value_beside, result):
     span = place[0]
-    asker = jnp.minimum(span + distance, visible.shape[0] - 1)
-    flags = [visible[asker, span] > 0, visible[asker, beside_of(span)] > 0]
-
-    def write(columns, block):
-        result[:, columns] = block.astype(jnp.bfloat16)
-
-    width = query.shape[1]
-    rest = attend(query, [key, key_beside], [value, value_beside], flags, write)
-    sent = jnp.zeros_like(rest)
-    for piece in range(3):
-        part = rest.astype(jnp.bfloat16).astype(jnp.float32)
-        sent = sent + (part if piece == 0 else pltpu.roll(part, piece * PIECE_LANES, 1))
-        rest = rest - part
-    result[:, width:] = sent.astype(jnp.bfloat16)
+
+    @pl.when(span + distance < spans)
+    def _():
+        asker = jnp.minimum(span + distance, spans - 1)
+        flags = [visible[asker, span] > 0, visible[asker, beside_of(span)] > 0]
+
+        def write(columns, block):
+            result[:, columns] = block.astype(jnp.bfloat16)
+
+        width = query.shape[1]
+        rest = attend(query, [key, key_beside], [value, value_beside], flags, write)
+        sent = jnp.zeros_like(rest)
+        for piece in range(3):
+            part = rest.astype(jnp.bfloat16).astype(jnp.float32)
+            sent = sent + (part if piece == 0 else pltpu.roll(part, piece * PIECE_LANES, 1))
+            rest = rest - part
+        result[:, width:] = sent.astype(jnp.bfloat16)
 
 
 def merge_kernel(distances, pieces, place, own, own_sum, *refs):
@@ -229,7 +251,16 @@
     place = jnp.stack([span, rank]).astype(jnp.int32)
     level = levels[span]
 
-    query_outer = jnp.concatenate([queries[:quarter], queries[rows - quarter:]])
+    query_outer = pl.pallas_call(
+        split_kernel,
+        in_specs=[SMEM, HBM],
+        out_specs=VMEM,
+        out_shape=jax.ShapeDtypeStruct((half, width), queries.dtype),
+        scratch_shapes=[pltpu.SemaphoreType.DMA((2,))],
+        compiler_params=PARAMS,
+        cost_estimate=cost(0, 2 * rows * width),
+        name="split",
+    )(place, pltpu.with_memory_space_constraint(queries, pltpu.HBM))
     query_inner = queries[quarter:rows - quarter]
     distances = list(range(2, spans, 2))
     asked_outer = [shifted(query_outer, "span", -distance) for distance in distances]
@@ -252,7 +283,7 @@
 
     def served(asked, distance):
         return pl.pallas_call(
-            functools.partial(served_kernel, distance),
+            functools.partial(served_kernel, distance, spans),
             in_specs=[SMEM, SMEM] + [VMEM] * 5,
             out_specs=VMEM,
             out_shape=jax.ShapeDtypeStruct((half, width + LANES), jnp.bfloat16),
@@ -261,12 +292,12 @@
             name="served",
         )(place, visible, asked, keys, values, key_beside, value_beside)
 
-    asked_outer, query_inner, own_sum = lax.optimization_barrier((asked_outer, query_inner, own_sum))
     asked_inner = [shifted(query_inner, "span", -distance) for distance in distances]
-    out_outer = [served(q, d) for q, d in zip(asked_outer, distances)]
-    back_outer = [shifted(o, "span", d) for o, d in zip(out_outer, distances)]
-    asked_inner, out_outer = lax.optimization_barrier((asked_inner, out_outer))
-    back_inner = [shifted(served(q, d), "span", d) for q, d in zip(asked_inner, distances)]
+    asked_outer, own_sum = lax.optimization_barrier((asked_outer, own_sum))
+    back_outer = [shifted(served(q, d), "span", d) for q, d in zip(asked_outer, distances)]
+    out_inner = [served(q, d) for q, d in zip(asked_inner, distances)]
+    back_outer, out_inner = lax.optimization_barrier((back_outer, out_inner))
+    back_inner = [shifted(o, "span", d) for o, d in zip(out_inner, distances)]
 
     def merge(back, pieces):
         return pl.pallas_call(
@@ -284,7 +315,8 @@
 
     chunks = 2
     columns = model // chunks
-    wide = columns // 2
+    tile = columns // 4
+    wide = columns // 3
     last = ranks - 1
     corner = quarter // block
 
@@ -298,13 +330,14 @@
             lax.ppermute(down, "tensor", [(last - i, last - i - 1) for i in range(step + 1)]),
         )
 
+    out_weight = pltpu.with_memory_space_constraint(out_weight, pltpu.HBM)
     projected, arrived = [], []
     for chunk in range(chunks):
-        upper, up, down = project(attended_outer, out_weight, chunk, columns, block, wide, ())
+        upper, up, down = project(attended_outer, out_weight, chunk, columns, block, tile, ())
         projected.append(upper)
         arrived.append(exchanged(up, down, 0))
     projected = [
-        project(attended_inner, out_weight, chunk, columns, block, wide, (projected[chunk],))[0]
+        project(attended_inner, out_weight, chunk, columns, block, tile, (projected[chunk],))[0]
         for chunk in range(chunks)
     ]
     for step in range(1, last):

time: 135 us -> 133 us (0.985)
  Pallas kernels: 39.1 us -> 50.3 us
  local copies, waits for them, and re-layouts: 18.5 us -> 8.26 us
    pallas_call x4, Pallas kernels: 8.4 us -> 18 us  [project(): pl.pallas_call(functools.partial(project_kernel, first), grid=(columns //...]
    unnamed x50 -> x30, local copies, waits for them, and re-layouts: 15.3 us -> 7.65 us
    pallas_call x2 -> x3, Pallas kernels: 7.52 us -> 3.44 us  [the longest x2 1.9 us: served(): pl.pallas_call(functools.partial(served_kernel, distance, spans), in_spec...]
    pallas_call x4, Pallas kernels: 11.1 us -> 15.1 us  [message(): pl.pallas_call(message_kernel, grid_spec=pltpu.PrefetchScalarGridSpec(num...]
    ppermute x6, waiting for transfers between devices: 11.6 us -> 8.38 us  [exchanged(): lax.ppermute(up, 'tensor', [(i, i + 1) for i in range(step + 1)])]
    ppermute x4, waiting for transfers between devices: 15.1 us -> 17.8 us  [shifted(): lax.ppermute(block, axis, [(i, i + distance) for i in range(count) if 0 <...]
    pallas_call x2, Pallas kernels: 5.12 us -> 6.86 us  [final(): pl.pallas_call(final_kernel, grid_spec=pltpu.PrefetchScalarGridSpec(num_s...]
    slice x1, local copies, waits for them, and re-layouts: 1.69 us -> 0.02 us  [body(): query_inner = queries[quarter:rows - quarter]]
  transfers between devices with their start and end apart: 18 -> 18, of which waited for: 10 -> 9; matrix products, arithmetic and copies ran while one was open for 4% -> 1% of each run, Pallas kernels for 24% -> 30%
where the time goes in v5:
time: 133 us; the launch traced here: 132 us
  Pallas kernels  50.3 us (38%)
  starting transfers between devices  37.9 us (28%)
  waiting for transfers between devices  34.4 us (26%)
  local copies, waits for them, and re-layouts  8.26 us (6%)
    pallas_call x4, Pallas kernels, project(): pl.pallas_call(functools.partial(project_kernel, first), grid=(columns //...  18 us
    ppermute x4, waiting for transfers between devices, shifted(): lax.ppermute(block, axis, [(i, i + distance) for i in range(count) if 0 <...  17.8 us
    pallas_call x4, Pallas kernels, message(): pl.pallas_call(message_kernel, grid_spec=pltpu.PrefetchScalarGridSpec(num...  15.1 us
    ppermute x6, starting transfers between devices, exchanged(): lax.ppermute(up, 'tensor', [(i, i + 1) for i in range(step + 1)])  14.7 us
    ppermute x6, starting transfers between devices, exchanged(): lax.ppermute(down, 'tensor', [(last - i, last - i - 1) for i in range(ste...  13.2 us
    ppermute x4, starting transfers between devices, shifted(): lax.ppermute(block, axis, [(i, i + distance) for i in range(count) if 0 <...  9.45 us
    ppermute x6, waiting for transfers between devices, exchanged(): lax.ppermute(up, 'tensor', [(i, i + 1) for i in range(step + 1)])  8.38 us
    ppermute x6, waiting for transfers between devices, exchanged(): lax.ppermute(down, 'tensor', [(last - i, last - i - 1) for i in range(ste...  8.23 us
  transfers between devices with their start and end apart: 18, of which 9 were waited for; matrix products, arithmetic and copies ran while one was open for 1% of the time, Pallas kernels for 30%

profile of v5, /device:TPU:14, one launch (start us, length us, event | category | flops | bytes accessed | tf_op | source)
XLA Modules:
  0.0 132.1 jit_solution(11811826294375073559)
XLA Ops:
  0.6 1.5 %split.1 = bf16[192,768]{1,0:T(8,128)(2,1)S(1)} custom-call(s32[2]{0:T(128)S(1)} %pad_add_fusion.1.place, bf16[384,768]{1,0:T(8,128)(2,1)} %query.3), custom_call_target="tpu_custom_call" | custom-call | bytes 589824 | tf_op jit(solution)/shard_map/split/pallas_call | solution.py:254
  2.1 1.5 %collective-permute-start.2 = (bf16[192,768]{1,0:T(8,128)(2,1)S(1)}, bf16[192,768]{1,0:T(8,128)(2,1)S(1)}, u32[]{:S(2)}, u32[]{:S(2)}) collective-permute-start(bf16[192,768]{1,0:T(8,128)(2,1)S(1)} %split.1), channel_id=1, source_target_pairs={{8,0},{12,4},{9,1},{13,5},{10,2},{14,6},{11,3},{15,7},{24,16},{28,... | collective-permute-start | bytes 884744 | tf_op jit(solution)/shard_map/ppermute | solution.py:28
  3.6 1.1 copy-done.6
  4.7 1.1 copy-done.8
  5.8 1.1 copy-done.10
  6.8 0.7 copy-done.13
  7.5 4.3 %local.1 = (f32[384,768]{1,0:T(8,128)S(1)}, f32[384,128]{1,0:T(8,128)S(1)}) custom-call(s32[2]{0:T(128)S(1)} %pad_add_fusion.1.place, s32[4,4]{1,0:T(4,128)S(1)} %copy-done.13, bf16[384,768]{1,0:T(8,128)(2,1)S(1)} %copy-done.10, bf16[384,768]{1,0:T(8,128)(2,1)S(1)} %copy-done.6, bf16[384,768]{1,0:T(8,128)(2,1)S(1)} %copy-done.8, ...), custom_call_target="tpu_custom_call" | custom-call | flops 905969664 | bytes 4128768 | tf_op jit(solution)/shard_map/local/pallas_call | solution.py:271
  12.4 1.3 collective-permute-start.3
  13.7 5.4 %collective-permute-start.4 = (bf16[192,768]{1,0:T(8,128)(2,1)S(1)}, bf16[192,768]{1,0:T(8,128)(2,1)S(1)}, u32[]{:S(2)}, u32[]{:S(2)}) collective-permute-start(bf16[192,768]{1,0:T(8,128)(2,1)S(1)} %slice.3), channel_id=1, source_target_pairs={{8,0},{12,4},{9,1},{13,5},{10,2},{14,6},{11,3},{15,7},{24,16},{28,... | collective-permute-start | bytes 884744 | tf_op jit(solution)/shard_map/ppermute | solution.py:28
  19.2 5.8 %collective-permute-done.4.query = bf16[192,768]{1,0:T(8,128)(2,1)S(1)} collective-permute-done((bf16[192,768]{1,0:T(8,128)(2,1)S(1)}, bf16[192,768]{1,0:T(8,128)(2,1)S(1)}, u32[]{:S(2)}, u32[]{:S(2)}) %collective-permute-start.4) | collective-permute-done | bytes 294944 | tf_op jit(solution)/shard_map/ppermute | solution.py:28
  24.9 1.3 %served.3 = bf16[192,896]{1,0:T(8,128)(2,1)} custom-call(s32[2]{0:T(128)S(1)} %pad_add_fusion.1.place, s32[4,4]{1,0:T(4,128)S(1)} %copy-done.13, bf16[192,768]{1,0:T(8,128)(2,1)S(1)} %collective-permute-done.4.query, bf16[384,768]{1,0:T(8,128)(2,1)S(1)} %copy-done.7, bf16[384,768]{1,0:T(8,128)(2,1)S(1)} %copy-done.9, ...), custom_call_target="tpu_custom_call" | custom-call | flops 452984832 | bytes 3538944 | tf_op jit(solution)/shard_map/served/pallas_call | solution.py:285
  26.2 1.2 merge.3.attended
  27.5 5.0 %project.6 = (bf16[384,3072]{1,0:T(8,128)(2,1)S(1)}, bf16[96,3072]{1,0:T(8,128)(2,1)}, bf16[96,3072]{1,0:T(8,128)(2,1)}) custom-call(bf16[192,768]{1,0:T(8,128)(2,1)S(1)} %merge.3.attended, bf16[768,6144]{1,0:T(8,128)(2,1)} %weight.7), custom_call_target="tpu_custom_call" | custom-call | flops 905969664 | bytes 7077888 | tf_op jit(solution)/shard_map/project/pallas_call | solution.py:166
  32.5 1.3 collective-permute-start.12
  33.8 1.5 %collective-permute-start.13 = (bf16[96,3072]{1,0:T(8,128)(2,1)}, bf16[96,3072]{1,0:T(8,128)(2,1)}, u32[]{:S(2)}, u32[]{:S(2)}) collective-permute-start(bf16[96,3072]{1,0:T(8,128)(2,1)} %get-tuple-element.40), channel_id=1, source_target_pairs={{3,2},{7,6},{11,10},{15,14},{19,18},{23,22},{27,26},{31,30}} | collective-permute-start | bytes 1769480 | tf_op jit(solution)/shard_map/ppermute | solution.py:330
  35.3 4.9 %project.4 = (bf16[384,3072]{1,0:T(8,128)(2,1)S(1)}, bf16[96,3072]{1,0:T(8,128)(2,1)}, bf16[96,3072]{1,0:T(8,128)(2,1)}) custom-call(bf16[192,768]{1,0:T(8,128)(2,1)S(1)} %merge.3.attended, bf16[768,6144]{1,0:T(8,128)(2,1)} %weight.7), custom_call_target="tpu_custom_call" | custom-call | flops 905969664 | bytes 7077888 | tf_op jit(solution)/shard_map/project/pallas_call | solution.py:166
  40.2 1.4 %copy-done = bf16[384,3072]{1,0:T(8,128)(2,1)} copy-done((bf16[384,3072]{1,0:T(8,128)(2,1)}, bf16[384,3072]{1,0:T(8,128)(2,1)S(1)}, u32[]{:S(2)}) %copy-start) | copy-done | bytes 2359320
  41.6 1.3 collective-permute-start.6
  42.9 1.5 %collective-permute-start.7 = (bf16[96,3072]{1,0:T(8,128)(2,1)}, bf16[96,3072]{1,0:T(8,128)(2,1)}, u32[]{:S(2)}, u32[]{:S(2)}) collective-permute-start(bf16[96,3072]{1,0:T(8,128)(2,1)} %get-tuple-element.33), channel_id=1, source_target_pairs={{3,2},{7,6},{11,10},{15,14},{19,18},{23,22},{27,26},{31,30}} | collective-permute-start | bytes 1769480 | tf_op jit(solution)/shard_map/ppermute | solution.py:330
  44.4 1.3 collective-permute-start.5
  45.8 12.0 %collective-permute-done.5.refs_0_ = bf16[192,896]{1,0:T(8,128)(2,1)} collective-permute-done((bf16[192,896]{1,0:T(8,128)(2,1)}, bf16[192,896]{1,0:T(8,128)(2,1)}, u32[]{:S(2)}, u32[]{:S(2)}) %collective-permute-start.5) | collective-permute-done | bytes 344096 | tf_op jit(solution)/shard_map/ppermute | solution.py:28
  57.8 0.9 copy-done.12
  58.7 1.5 %merge.2.attended = bf16[192,768]{1,0:T(8,128)(2,1)S(1)} custom-call(s32[2]{0:T(128)S(1)} %pad_add_fusion.1.place, f32[384,768]{1,0:T(8,128)S(1)} %get-tuple-element.25.own, f32[384,128]{1,0:T(8,128)S(1)} %copy-done.12, bf16[192,896]{1,0:T(8,128)(2,1)} %collective-permute-done.5.refs_0_), custom_call_target="tpu_custom_call" | custom-call | flops 1179648 | bytes 1474560 | tf_op jit(solution)/shard_map/merge/pallas_call | solution.py:303
  60.2 4.1 %project.7.up_block.down_block.own = bf16[384,3072]{1,0:T(8,128)(2,1)S(1)} custom-call(bf16[192,768]{1,0:T(8,128)(2,1)S(1)} %merge.2.attended, bf16[768,6144]{1,0:T(8,128)(2,1)} %weight.7, bf16[384,3072]{1,0:T(8,128)(2,1)S(1)} %get-tuple-element.38.refs_0_), custom_call_target="tpu_custom_call", output_to_operand_aliasing={{}: (2, {})} | custom-call | flops 905969664 | bytes 7077888 | tf_op jit(solution)/shard_map/project/pallas_call | solution.py:166
  64.3 3.9 %project.5.up_block.down_block.own = bf16[384,3072]{1,0:T(8,128)(2,1)S(1)} custom-call(bf16[192,768]{1,0:T(8,128)(2,1)S(1)} %merge.2.attended, bf16[768,6144]{1,0:T(8,128)(2,1)} %weight.7, bf16[384,3072]{1,0:T(8,128)(2,1)S(1)} %copy-done.1), custom_call_target="tpu_custom_call", output_to_operand_aliasing={{}: (2, {})} | custom-call | flops 905969664 | bytes 7077888 | tf_op jit(solution)/shard_map/project/pallas_call | solution.py:166
  68.3 4.0 %message.6 = (bf16[96,3072]{1,0:T(8,128)(2,1)}, bf16[96,3072]{1,0:T(8,128)(2,1)}) custom-call(s32[2]{0:T(128)S(1)} %pad_add_fusion.3.blocks, bf16[384,3072]{1,0:T(8,128)(2,1)S(1)} %project.7.up_block.down_block.own, bf16[384,3072]{1,0:T(8,128)(2,1)S(1)} %project.7.up_block.down_block.own, bf16[96,3072]{1,0:T(8,128)(2,1)} %collective-permute-done.12.up_arrived, ...), custom_call_target="tpu_custom_call" | custom-call | flops 1179648 | bytes 3538944 | tf_op jit(solution)/shard_map/message/pallas_call | solution.py:190
  72.3 3.5 %collective-permute-start.14 = (bf16[96,3072]{1,0:T(8,128)(2,1)}, bf16[96,3072]{1,0:T(8,128)(2,1)S(1)}, u32[]{:S(2)}, u32[]{:S(2)}) collective-permute-start(bf16[96,3072]{1,0:T(8,128)(2,1)} %get-tuple-element.41), channel_id=1, source_target_pairs={{0,1},{1,2},{4,5},{5,6},{8,9},{9,10},{12,13},{13,14},{16,17},{17,1... | collective-permute-start | bytes 1769480 | tf_op jit(solution)/shard_map/ppermute | solution.py:329
  75.8 1.3 collective-permute-start.15
  77.1 3.8 %message.4 = (bf16[96,3072]{1,0:T(8,128)(2,1)}, bf16[96,3072]{1,0:T(8,128)(2,1)}) custom-call(s32[2]{0:T(128)S(1)} %pad_add_fusion.3.blocks, bf16[384,3072]{1,0:T(8,128)(2,1)S(1)} %project.5.up_block.down_block.own, bf16[384,3072]{1,0:T(8,128)(2,1)S(1)} %project.5.up_block.down_block.own, bf16[96,3072]{1,0:T(8,128)(2,1)} %collective-permute-done.6.up_arrived, ...), custom_call_target="tpu_custom_call" | custom-call | flops 1179648 | bytes 3538944 | tf_op jit(solution)/shard_map/message/pallas_call | solution.py:190
  80.9 4.5 %collective-permute-start.8 = (bf16[96,3072]{1,0:T(8,128)(2,1)}, bf16[96,3072]{1,0:T(8,128)(2,1)S(1)}, u32[]{:S(2)}, u32[]{:S(2)}) collective-permute-start(bf16[96,3072]{1,0:T(8,128)(2,1)} %get-tuple-element.34), channel_id=1, source_target_pairs={{0,1},{1,2},{4,5},{5,6},{8,9},{9,10},{12,13},{13,14},{16,17},{17,1... | collective-permute-start | bytes 1769480 | tf_op jit(solution)/shard_map/ppermute | solution.py:329
  85.5 1.3 collective-permute-start.9
  86.9 5.2 %collective-permute-done.14.up_arrived = bf16[96,3072]{1,0:T(8,128)(2,1)S(1)} collective-permute-done((bf16[96,3072]{1,0:T(8,128)(2,1)}, bf16[96,3072]{1,0:T(8,128)(2,1)S(1)}, u32[]{:S(2)}, u32[]{:S(2)}) %collective-permute-start.14) | collective-permute-done | bytes 589856 | tf_op jit(solution)/shard_map/ppermute | solution.py:329
  92.0 2.2 %collective-permute-done.15.down_arrived = bf16[96,3072]{1,0:T(8,128)(2,1)} collective-permute-done((bf16[96,3072]{1,0:T(8,128)(2,1)}, bf16[96,3072]{1,0:T(8,128)(2,1)}, u32[]{:S(2)}, u32[]{:S(2)}) %collective-permute-start.15) | collective-permute-done | bytes 589856 | tf_op jit(solution)/shard_map/ppermute | solution.py:330
  94.2 3.6 %message.7 = (bf16[96,3072]{1,0:T(8,128)(2,1)}, bf16[96,3072]{1,0:T(8,128)(2,1)}) custom-call(s32[2]{0:T(128)S(1)} %pad_add_fusion.2.blocks, bf16[384,3072]{1,0:T(8,128)(2,1)S(1)} %project.7.up_block.down_block.own, bf16[384,3072]{1,0:T(8,128)(2,1)S(1)} %project.7.up_block.down_block.own, bf16[96,3072]{1,0:T(8,128)(2,1)S(1)} %collective-permute-done.14.up_arrived, ...), custom_call_target="tpu_custom_call" | custom-call | flops 1179648 | bytes 3538944 | tf_op jit(solution)/shard_map/message/pallas_call | solution.py:190
  97.9 2.0 %collective-permute-start.16 = (bf16[96,3072]{1,0:T(8,128)(2,1)}, bf16[96,3072]{1,0:T(8,128)(2,1)S(1)}, u32[]{:S(2)}, u32[]{:S(2)}) collective-permute-start(bf16[96,3072]{1,0:T(8,128)(2,1)} %get-tuple-element.43), channel_id=1, source_target_pairs={{0,1},{1,2},{2,3},{4,5},{5,6},{6,7},{8,9},{9,10},{10,11},{12,13},{... | collective-permute-start | bytes 1769480 | tf_op jit(solution)/shard_map/ppermute | solution.py:329
  99.9 3.8 %collective-permute-start.17 = (bf16[96,3072]{1,0:T(8,128)(2,1)}, bf16[96,3072]{1,0:T(8,128)(2,1)}, u32[]{:S(2)}, u32[]{:S(2)}) collective-permute-start(bf16[96,3072]{1,0:T(8,128)(2,1)} %get-tuple-element.44), channel_id=1, source_target_pairs={{3,2},{2,1},{1,0},{7,6},{6,5},{5,4},{11,10},{10,9},{9,8},{15,14},{... | collective-permute-start | bytes 1769480 | tf_op jit(solution)/shard_map/ppermute | solution.py:330
  103.8 0.9 collective-permute-done.8.up_arrived
  104.6 2.2 %collective-permute-done.9.down_arrived = bf16[96,3072]{1,0:T(8,128)(2,1)} collective-permute-done((bf16[96,3072]{1,0:T(8,128)(2,1)}, bf16[96,3072]{1,0:T(8,128)(2,1)}, u32[]{:S(2)}, u32[]{:S(2)}) %collective-permute-start.9) | collective-permute-done | bytes 589856 | tf_op jit(solution)/shard_map/ppermute | solution.py:330
  106.9 3.6 %message.5 = (bf16[96,3072]{1,0:T(8,128)(2,1)}, bf16[96,3072]{1,0:T(8,128)(2,1)}) custom-call(s32[2]{0:T(128)S(1)} %pad_add_fusion.2.blocks, bf16[384,3072]{1,0:T(8,128)(2,1)S(1)} %copy-done.3, bf16[384,3072]{1,0:T(8,128)(2,1)S(1)} %copy-done.3, bf16[96,3072]{1,0:T(8,128)(2,1)S(1)} %collective-permute-done.8.up_arrived, ...), custom_call_target="tpu_custom_call" | custom-call | flops 1179648 | bytes 3538944 | tf_op jit(solution)/shard_map/message/pallas_call | solution.py:190
  110.5 2.0 %collective-permute-start.10 = (bf16[96,3072]{1,0:T(8,128)(2,1)}, bf16[96,3072]{1,0:T(8,128)(2,1)S(1)}, u32[]{:S(2)}, u32[]{:S(2)}) collective-permute-start(bf16[96,3072]{1,0:T(8,128)(2,1)} %get-tuple-element.36), channel_id=1, source_target_pairs={{0,1},{1,2},{2,3},{4,5},{5,6},{6,7},{8,9},{9,10},{10,11},{12,13},{... | collective-permute-start | bytes 1769480 | tf_op jit(solution)/shard_map/ppermute | solution.py:329
  112.6 3.8 %collective-permute-start.11 = (bf16[96,3072]{1,0:T(8,128)(2,1)}, bf16[96,3072]{1,0:T(8,128)(2,1)}, u32[]{:S(2)}, u32[]{:S(2)}) collective-permute-start(bf16[96,3072]{1,0:T(8,128)(2,1)} %get-tuple-element.37), channel_id=1, source_target_pairs={{3,2},{2,1},{1,0},{7,6},{6,5},{5,4},{11,10},{10,9},{9,8},{15,14},{... | collective-permute-start | bytes 1769480 | tf_op jit(solution)/shard_map/ppermute | solution.py:330
  117.0 0.7 pad_add_fusion.blocks
  117.7 1.8 %collective-permute-done.17.down = bf16[96,3072]{1,0:T(8,128)(2,1)} collective-permute-done((bf16[96,3072]{1,0:T(8,128)(2,1)}, bf16[96,3072]{1,0:T(8,128)(2,1)}, u32[]{:S(2)}, u32[]{:S(2)}) %collective-permute-start.17) | collective-permute-done | bytes 589856 | tf_op jit(solution)/shard_map/ppermute | solution.py:330
  119.5 1.4 %copy-done.5 = f32[64,6144]{1,0:T(8,128)S(1)} copy-done((f32[64,6144]{1,0:T(8,128)S(1)}, f32[64,6144]{1,0:T(8,128)}, u32[]{:S(2)}) %copy-start.5) | copy-done | bytes 1572888
  120.9 3.4 %final.2.refs_0_ = bf16[96,6144]{1,0:T(8,128)(2,1)} custom-call(s32[2]{0:T(128)S(1)} %pad_add_fusion.blocks, bf16[384,3072]{1,0:T(8,128)(2,1)S(1)} %project.7.up_block.down_block.own, f32[64,6144]{1,0:T(8,128)S(1)} %copy-done.5, bf16[96,3072]{1,0:T(8,128)(2,1)S(1)} %collective-permute-done.16.up, bf16[96,3072]{1,0:T(8,128)(2,1)} %collective-permute-done.17.down), custom_call_target="tpu_custom_call" | custom-call | flops 1179648 | bytes 2949120 | tf_op jit(solution)/shard_map/final/pallas_call | solution.py:220
  124.4 2.3 %collective-permute-done.10.up = bf16[96,3072]{1,0:T(8,128)(2,1)S(1)} collective-permute-done((bf16[96,3072]{1,0:T(8,128)(2,1)}, bf16[96,3072]{1,0:T(8,128)(2,1)S(1)}, u32[]{:S(2)}, u32[]{:S(2)}) %collective-permute-start.10) | collective-permute-done | bytes 589856 | tf_op jit(solution)/shard_map/ppermute | solution.py:329
  126.7 2.0 %collective-permute-done.11.down = bf16[96,3072]{1,0:T(8,128)(2,1)} collective-permute-done((bf16[96,3072]{1,0:T(8,128)(2,1)}, bf16[96,3072]{1,0:T(8,128)(2,1)}, u32[]{:S(2)}, u32[]{:S(2)}) %collective-permute-start.11) | collective-permute-done | bytes 589856 | tf_op jit(solution)/shard_map/ppermute | solution.py:330
  128.7 3.4 %final.3 = bf16[96,6144]{1,0:T(8,128)(2,1)} custom-call(s32[2]{0:T(128)S(1)} %pad_add_fusion.blocks, bf16[384,3072]{1,0:T(8,128)(2,1)S(1)} %copy-done.4, f32[64,6144]{1,0:T(8,128)S(1)} %copy-done.5, bf16[96,3072]{1,0:T(8,128)(2,1)S(1)} %collective-permute-done.10.up, bf16[96,3072]{1,0:T(8,128)(2,1)} %collective-permute-done.11.down, ...), custom_call_target="tpu_custom_call", output_to_operand_aliasing={{}: (5, {})} | custom-call | flops 1179648 | bytes 2949120 | tf_op jit(solution)/shard_map/final/pallas_call | solution.py:220
  (40 shorter events, 2.0 us)
Async XLA Ops:
  0.0 11.8 %copy-start.7 = (bf16[384,768]{1,0:T(8,128)(2,1)S(1)}, bf16[384,768]{1,0:T(8,128)(2,1)}, u32[]{:S(2)}) copy-start(bf16[384,768]{1,0:T(8,128)(2,1)} %key.5) | copy-start | bytes 1769476
  0.0 3.6 %collective-permute-start = (bf16[384,768]{1,0:T(8,128)(2,1)}, bf16[384,768]{1,0:T(8,128)(2,1)S(1)}, u32[]{:S(2)}, u32[]{:S(2)}) collective-permute-start(bf16[384,768]{1,0:T(8,128)(2,1)} %key.5), channel_id=1, source_target_pairs={{0,4},{4,0},{8,12},{12,8},{1,5},{5,1},{9,13},{13,9},{2,6},{6,2},{1... | collective-permute-start | bytes 1769480 | tf_op jit(solution)/shard_map/ppermute | solution.py:268
  0.0 3.6 %collective-permute-start.1 = (bf16[384,768]{1,0:T(8,128)(2,1)}, bf16[384,768]{1,0:T(8,128)(2,1)S(1)}, u32[]{:S(2)}, u32[]{:S(2)}) collective-permute-start(bf16[384,768]{1,0:T(8,128)(2,1)} %value.5), channel_id=1, source_target_pairs={{0,4},{4,0},{8,12},{12,8},{1,5},{5,1},{9,13},{13,9},{2,6},{6,2},{1... | collective-permute-start | bytes 1769480 | tf_op jit(solution)/shard_map/ppermute | solution.py:269
  2.1 9.6 %collective-permute-start.2 = (bf16[192,768]{1,0:T(8,128)(2,1)S(1)}, bf16[192,768]{1,0:T(8,128)(2,1)S(1)}, u32[]{:S(2)}, u32[]{:S(2)}) collective-permute-start(bf16[192,768]{1,0:T(8,128)(2,1)S(1)} %split.1), channel_id=1, source_target_pairs={{8,0},{12,4},{9,1},{13,5},{10,2},{14,6},{11,3},{15,7},{24,16},{28,... | collective-permute-start | bytes 884744 | tf_op jit(solution)/shard_map/ppermute | solution.py:28
  3.6 1.1 copy-start.6
  4.7 1.1 copy-start.8
  5.8 1.1 copy-start.10
  6.8 0.7 copy-start.13
  7.5 4.3 %copy-start.9 = (bf16[384,768]{1,0:T(8,128)(2,1)S(1)}, bf16[384,768]{1,0:T(8,128)(2,1)}, u32[]{:S(2)}) copy-start(bf16[384,768]{1,0:T(8,128)(2,1)} %value.5) | copy-start | bytes 1769476
  11.8 14.5 %copy-start.11 = (f32[384,128]{1,0:T(8,128)}, f32[384,128]{1,0:T(8,128)S(1)}, u32[]{:S(2)}) copy-start(f32[384,128]{1,0:T(8,128)S(1)} %get-tuple-element.27.own_sum) | copy-start | bytes 589828
  12.4 13.9 %collective-permute-start.3 = (bf16[192,896]{1,0:T(8,128)(2,1)S(1)}, bf16[192,896]{1,0:T(8,128)(2,1)S(1)}, u32[]{:S(2)}, u32[]{:S(2)}) collective-permute-start(bf16[192,896]{1,0:T(8,128)(2,1)S(1)} %served.2), channel_id=1, source_target_pairs={{0,8},{4,12},{1,9},{5,13},{2,10},{6,14},{3,11},{7,15},{16,24},{20,... | collective-permute-start | bytes 1032200 | tf_op jit(solution)/shard_map/ppermute | solution.py:28
  13.7 11.2 %collective-permute-start.4 = (bf16[192,768]{1,0:T(8,128)(2,1)S(1)}, bf16[192,768]{1,0:T(8,128)(2,1)S(1)}, u32[]{:S(2)}, u32[]{:S(2)}) collective-permute-start(bf16[192,768]{1,0:T(8,128)(2,1)S(1)} %slice.3), channel_id=1, source_target_pairs={{8,0},{12,4},{9,1},{13,5},{10,2},{14,6},{11,3},{15,7},{24,16},{28,... | collective-permute-start | bytes 884744 | tf_op jit(solution)/shard_map/ppermute | solution.py:28
  32.5 35.8 %collective-permute-start.12 = (bf16[96,3072]{1,0:T(8,128)(2,1)}, bf16[96,3072]{1,0:T(8,128)(2,1)}, u32[]{:S(2)}, u32[]{:S(2)}) collective-permute-start(bf16[96,3072]{1,0:T(8,128)(2,1)} %get-tuple-element.39), channel_id=1, source_target_pairs={{0,1},{4,5},{8,9},{12,13},{16,17},{20,21},{24,25},{28,29}} | collective-permute-start | bytes 1769480 | tf_op jit(solution)/shard_map/ppermute | solution.py:329
  33.8 34.5 %collective-permute-start.13 = (bf16[96,3072]{1,0:T(8,128)(2,1)}, bf16[96,3072]{1,0:T(8,128)(2,1)}, u32[]{:S(2)}, u32[]{:S(2)}) collective-permute-start(bf16[96,3072]{1,0:T(8,128)(2,1)} %get-tuple-element.40), channel_id=1, source_target_pairs={{3,2},{7,6},{11,10},{15,14},{19,18},{23,22},{27,26},{31,30}} | collective-permute-start | bytes 1769480 | tf_op jit(solution)/shard_map/ppermute | solution.py:330
  40.2 1.4 %copy-start = (bf16[384,3072]{1,0:T(8,128)(2,1)}, bf16[384,3072]{1,0:T(8,128)(2,1)S(1)}, u32[]{:S(2)}) copy-start(bf16[384,3072]{1,0:T(8,128)(2,1)S(1)} %get-tuple-element.31.refs_0_) | copy-start | bytes 7077892
  41.6 35.4 %collective-permute-start.6 = (bf16[96,3072]{1,0:T(8,128)(2,1)}, bf16[96,3072]{1,0:T(8,128)(2,1)}, u32[]{:S(2)}, u32[]{:S(2)}) collective-permute-start(bf16[96,3072]{1,0:T(8,128)(2,1)} %get-tuple-element.32), channel_id=1, source_target_pairs={{0,1},{4,5},{8,9},{12,13},{16,17},{20,21},{24,25},{28,29}} | collective-permute-start | bytes 1769480 | tf_op jit(solution)/shard_map/ppermute | solution.py:329
  42.9 34.2 %collective-permute-start.7 = (bf16[96,3072]{1,0:T(8,128)(2,1)}, bf16[96,3072]{1,0:T(8,128)(2,1)}, u32[]{:S(2)}, u32[]{:S(2)}) collective-permute-start(bf16[96,3072]{1,0:T(8,128)(2,1)} %get-tuple-element.33), channel_id=1, source_target_pairs={{3,2},{7,6},{11,10},{15,14},{19,18},{23,22},{27,26},{31,30}} | collective-permute-start | bytes 1769480 | tf_op jit(solution)/shard_map/ppermute | solution.py:330
  44.4 13.4 %collective-permute-start.5 = (bf16[192,896]{1,0:T(8,128)(2,1)}, bf16[192,896]{1,0:T(8,128)(2,1)}, u32[]{:S(2)}, u32[]{:S(2)}) collective-permute-start(bf16[192,896]{1,0:T(8,128)(2,1)} %served.3), channel_id=1, source_target_pairs={{0,8},{4,12},{1,9},{5,13},{2,10},{6,14},{3,11},{7,15},{16,24},{20,... | collective-permute-start | bytes 1032200 | tf_op jit(solution)/shard_map/ppermute | solution.py:28
  57.8 0.9 copy-start.12
  60.2 4.1 %copy-start.1 = (bf16[384,3072]{1,0:T(8,128)(2,1)S(1)}, bf16[384,3072]{1,0:T(8,128)(2,1)}, u32[]{:S(2)}) copy-start(bf16[384,3072]{1,0:T(8,128)(2,1)} %copy-done) | copy-start | bytes 7077892
  68.3 8.8 %copy-start.2 = (bf16[384,3072]{1,0:T(8,128)(2,1)}, bf16[384,3072]{1,0:T(8,128)(2,1)S(1)}, u32[]{:S(2)}) copy-start(bf16[384,3072]{1,0:T(8,128)(2,1)S(1)} %project.5.up_block.down_block.own) | copy-start | bytes 7077892
  72.3 19.7 %collective-permute-start.14 = (bf16[96,3072]{1,0:T(8,128)(2,1)}, bf16[96,3072]{1,0:T(8,128)(2,1)S(1)}, u32[]{:S(2)}, u32[]{:S(2)}) collective-permute-start(bf16[96,3072]{1,0:T(8,128)(2,1)} %get-tuple-element.41), channel_id=1, source_target_pairs={{0,1},{1,2},{4,5},{5,6},{8,9},{9,10},{12,13},{13,14},{16,17},{17,1... | collective-permute-start | bytes 1769480 | tf_op jit(solution)/shard_map/ppermute | solution.py:329
  75.8 18.5 %collective-permute-start.15 = (bf16[96,3072]{1,0:T(8,128)(2,1)}, bf16[96,3072]{1,0:T(8,128)(2,1)}, u32[]{:S(2)}, u32[]{:S(2)}) collective-permute-start(bf16[96,3072]{1,0:T(8,128)(2,1)} %get-tuple-element.42), channel_id=1, source_target_pairs={{3,2},{2,1},{7,6},{6,5},{11,10},{10,9},{15,14},{14,13},{19,18},{18... | collective-permute-start | bytes 1769480 | tf_op jit(solution)/shard_map/ppermute | solution.py:330
  80.9 23.7 %collective-permute-start.8 = (bf16[96,3072]{1,0:T(8,128)(2,1)}, bf16[96,3072]{1,0:T(8,128)(2,1)S(1)}, u32[]{:S(2)}, u32[]{:S(2)}) collective-permute-start(bf16[96,3072]{1,0:T(8,128)(2,1)} %get-tuple-element.34), channel_id=1, source_target_pairs={{0,1},{1,2},{4,5},{5,6},{8,9},{9,10},{12,13},{13,14},{16,17},{17,1... | collective-permute-start | bytes 1769480 | tf_op jit(solution)/shard_map/ppermute | solution.py:329
  85.5 21.4 %collective-permute-start.9 = (bf16[96,3072]{1,0:T(8,128)(2,1)}, bf16[96,3072]{1,0:T(8,128)(2,1)}, u32[]{:S(2)}, u32[]{:S(2)}) collective-permute-start(bf16[96,3072]{1,0:T(8,128)(2,1)} %get-tuple-element.35), channel_id=1, source_target_pairs={{3,2},{2,1},{7,6},{6,5},{11,10},{10,9},{15,14},{14,13},{19,18},{18... | collective-permute-start | bytes 1769480 | tf_op jit(solution)/shard_map/ppermute | solution.py:330
  86.8 20.0 %copy-start.3 = (bf16[384,3072]{1,0:T(8,128)(2,1)S(1)}, bf16[384,3072]{1,0:T(8,128)(2,1)}, u32[]{:S(2)}) copy-start(bf16[384,3072]{1,0:T(8,128)(2,1)} %copy-done.2) | copy-start | bytes 7077892
  97.9 19.9 %collective-permute-start.16 = (bf16[96,3072]{1,0:T(8,128)(2,1)}, bf16[96,3072]{1,0:T(8,128)(2,1)S(1)}, u32[]{:S(2)}, u32[]{:S(2)}) collective-permute-start(bf16[96,3072]{1,0:T(8,128)(2,1)} %get-tuple-element.43), channel_id=1, source_target_pairs={{0,1},{1,2},{2,3},{4,5},{5,6},{6,7},{8,9},{9,10},{10,11},{12,13},{... | collective-permute-start | bytes 1769480 | tf_op jit(solution)/shard_map/ppermute | solution.py:329
  99.9 16.5 %copy-start.14 = (s32[4]{0:T(128)S(1)}, s32[4]{0:T(128)}, u32[]{:S(2)}) copy-start(s32[4]{0:T(128)} %param.12) | copy-start | bytes 52
  99.9 19.6 %collective-permute-start.17 = (bf16[96,3072]{1,0:T(8,128)(2,1)}, bf16[96,3072]{1,0:T(8,128)(2,1)}, u32[]{:S(2)}, u32[]{:S(2)}) collective-permute-start(bf16[96,3072]{1,0:T(8,128)(2,1)} %get-tuple-element.44), channel_id=1, source_target_pairs={{3,2},{2,1},{1,0},{7,6},{6,5},{5,4},{11,10},{10,9},{9,8},{15,14},{... | collective-permute-start | bytes 1769480 | tf_op jit(solution)/shard_map/ppermute | solution.py:330
  110.5 16.2 %collective-permute-start.10 = (bf16[96,3072]{1,0:T(8,128)(2,1)}, bf16[96,3072]{1,0:T(8,128)(2,1)S(1)}, u32[]{:S(2)}, u32[]{:S(2)}) collective-permute-start(bf16[96,3072]{1,0:T(8,128)(2,1)} %get-tuple-element.36), channel_id=1, source_target_pairs={{0,1},{1,2},{2,3},{4,5},{5,6},{6,7},{8,9},{9,10},{10,11},{12,13},{... | collective-permute-start | bytes 1769480 | tf_op jit(solution)/shard_map/ppermute | solution.py:329
  112.6 16.1 %collective-permute-start.11 = (bf16[96,3072]{1,0:T(8,128)(2,1)}, bf16[96,3072]{1,0:T(8,128)(2,1)}, u32[]{:S(2)}, u32[]{:S(2)}) collective-permute-start(bf16[96,3072]{1,0:T(8,128)(2,1)} %get-tuple-element.37), channel_id=1, source_target_pairs={{3,2},{2,1},{1,0},{7,6},{6,5},{5,4},{11,10},{10,9},{9,8},{15,14},{... | collective-permute-start | bytes 1769480 | tf_op jit(solution)/shard_map/ppermute | solution.py:330
  117.7 10.9 %copy-start.4 = (bf16[384,3072]{1,0:T(8,128)(2,1)S(1)}, bf16[384,3072]{1,0:T(8,128)(2,1)}, u32[]{:S(2)}) copy-start(bf16[384,3072]{1,0:T(8,128)(2,1)} %copy-done.2) | copy-start | bytes 7077892
  119.5 1.4 %copy-start.5 = (f32[64,6144]{1,0:T(8,128)S(1)}, f32[64,6144]{1,0:T(8,128)}, u32[]{:S(2)}) copy-start(f32[64,6144]{1,0:T(8,128)} %gate.3) | copy-start | bytes 4718596

commit v6 on v0

v6 whole, which is shorter than its diff:
```python
import functools

import jax
import jax.numpy as jnp
from jax import lax
from jax.experimental import pallas as pl
from jax.experimental.pallas import tpu as pltpu
from jax.sharding import PartitionSpec as P

HD = 128
LANES = 128
HIDDEN = -1e30
LOG2E = 1.4426950408889634
PARAMS = pltpu.CompilerParams(vmem_limit_bytes=24 * 1024 * 1024)
SMEM = pl.BlockSpec(memory_space=pltpu.SMEM)
VMEM = pl.BlockSpec(memory_space=pltpu.VMEM)
ANY = pl.BlockSpec(memory_space=pl.ANY)
HBM = pl.BlockSpec(memory_space=pltpu.HBM)
PIECE_LANES = 32
SHORT = pl.CostEstimate(flops=1, bytes_accessed=1, transcendentals=0)


def in_hbm(array):
    return pltpu.with_memory_space_constraint(array, pltpu.HBM)


def shifted(block, axis, distance):
    count = lax.axis_size(axis)
    return lax.ppermute(block, axis, [(i, i + distance) for i in range(count) if 0 <= i + distance < count])


def head_columns(head):
    return slice(head * HD, (head + 1) * HD)


def attend(query, keys, values, flags, write):
    rows, width = query.shape
    scale = LOG2E * HD ** (-0.5)
    lane = lax.broadcasted_iota(jnp.int32, (rows, LANES), 1)
    packed = jnp.zeros((rows, LANES), jnp.float32)
    for head in range(width // HD):
        columns = head_columns(head)
        mine = query[:, columns]
        scores = [
            lax.dot_general(mine, key[:, columns], (((1,), (1,)), ((), ())), preferred_element_type=jnp.float32)
            for key in keys
        ]
        tops = [jnp.max(block, axis=-1, keepdims=True) * scale for block in scores]
        top = functools.reduce(
            jnp.maximum, [one if flag is None else jnp.where(flag, one, HIDDEN) for one, flag in zip(tops, flags)]
        )
        total, product = None, None
        for block, value, flag in zip(scores, values, flags):
            above = top if flag is None else jnp.where(flag, top, -HIDDEN)
            probs = jnp.exp2(block * scale - above)
            part = jnp.sum(probs, axis=-1, keepdims=True)
            part_product = jnp.dot(
                probs.astype(jnp.bfloat16), value[:, columns], preferred_element_type=jnp.float32
            )
            total = part if total is None else total + part
            product = part_product if product is None else product + part_product
        total = jnp.where(total > 0.0, total, 1.0)
        write(columns, product * (1.0 / total))
        packed = jnp.where(lane == head, top + jnp.log2(total), packed)
    return packed


class Facts:
    def __init__(self, ref, spans):
        self.ref, self.spans = ref, spans
        self.span, self.rank = ref[spans, 0], ref[spans, 1]
        self.beside = self.span + 1 - 2 * lax.rem(self.span, 2)

    def sees(self, asker, span):
        return self.ref[asker, span] > 0

    def level(self):
        return self.ref[self.spans + 1, self.span]


def copied(source, target, semaphore):
    copy = pltpu.make_async_copy(source, target, semaphore)
    copy.start()
    return copy


def split_kernel(spans, facts, query, outer, inner, semaphores):
    rows = query.shape[0]
    quarter = rows // 4

    @pl.when(Facts(facts, spans).span > 1)
    def _():
        copies = [
            copied(query.at[pl.ds(0, quarter)], outer.at[pl.ds(0, quarter)], semaphores.at[0]),
            copied(query.at[pl.ds(rows - quarter, quarter)], outer.at[pl.ds(quarter, quarter)], semaphores.at[1]),
            copied(query.at[pl.ds(quarter, 2 * quarter)], inner, semaphores.at[2]),
        ]
        for copy in copies:
            copy.wait()


def local_kernel(spans, facts, query, key, value, key_beside, value_beside, result, sums, *scratch):
    here = Facts(facts, spans)
    query_, key_, value_, key_beside_, value_beside_, semaphores = scratch
    copies = [
        copied(source, target, semaphores.at[index])
        for index, (source, target) in enumerate((
            (query, query_), (key, key_), (key_beside, key_beside_), (value, value_), (value_beside, value_beside_),
        ))
    ]
    for copy in copies:
        copy.wait()

    def write(columns, block):
        result[:, columns] = block

    flags = [None, here.sees(here.span, here.beside)]
    sums[...] = attend(query_, [key_, key_beside_], [value_, value_beside_], flags, write)


def served_kernel(distance, spans, facts, query, key, value, key_beside, value_beside, result):
    here = Facts(facts, spans)

    @pl.when(here.span + distance < spans)
    def _():
        asker = jnp.minimum(here.span + distance, spans - 1)
        flags = [here.sees(asker, here.span), here.sees(asker, here.beside)]

        def write(columns, block):
            result[:, columns] = block.astype(jnp.bfloat16)

        width = query.shape[1]
        rest = attend(query, [key, key_beside], [value, value_beside], flags, write)
        sent = jnp.zeros_like(rest)
        for piece in range(3):
            part = rest.astype(jnp.bfloat16).astype(jnp.float32)
            sent = sent + (part if piece == 0 else pltpu.roll(part, piece * PIECE_LANES, 1))
            rest = rest - part
        result[:, width:] = sent.astype(jnp.bfloat16)


def merge(span, distances, own, own_sum, there, served, here, write):
    width = own.shape[1]
    sums = [own_sum[there, :]]
    for distance, ref in zip(distances, served):
        sent = ref[here, width:].astype(jnp.float32)
        joined = sent
        for piece in (1, 2):
            joined = joined + pltpu.roll(sent, LANES - piece * PIECE_LANES, 1)
        sums.append(jnp.where(span >= distance, joined, HIDDEN))
    top = functools.reduce(jnp.maximum, sums)
    shares = [jnp.exp2(one - top) for one in sums]
    over = 1.0 / sum(shares)
    shares = [share * over for share in shares]
    for head in range(width // HD):
        columns = head_columns(head)
        merged = own[there, columns] * shares[0][:, head:head + 1]
        for distance, share, ref in zip(distances, shares[1:], served):
            away = jnp.where(span >= distance, ref[here, columns].astype(jnp.float32), 0.0)
            merged = merged + away * share[:, head:head + 1]
        write(columns, merged.astype(jnp.bfloat16))


def opening_kernel(spans, ranks, distances, first, facts, own, own_sum, *refs):
    served = refs[:len(distances)]
    weight, result, tiles, rows, semaphores = refs[len(distances):]
    here = Facts(facts, spans)
    block, width = rows.shape
    count, _, tile = tiles.shape

    @pl.when(jnp.logical_or(here.rank == 0, here.rank == ranks - 1))
    def _():
        copies = [
            copied(weight.at[:, pl.ds(first + index * tile, tile)], tiles.at[index], semaphores.at[index])
            for index in range(count)
        ]
        lowest = here.rank == 0
        there = pl.ds(pl.multiple_of(jnp.where(lowest, own.shape[0] - block, 0), block), block)
        back = pl.ds(pl.multiple_of(jnp.where(lowest, own.shape[0] // 2 - block, 0), block), block)

        def write(columns, part):
            rows[:, columns] = part

        merge(here.span, distances, own, own_sum, there, served, back, write)
        for index, copy in enumerate(copies):
            copy.wait()
            product = jnp.dot(rows[...], tiles[index], preferred_element_type=jnp.float32)
            result[:, index * tile:(index + 1) * tile] = product.astype(jnp.bfloat16)


def project_kernel(spans, distances, facts, own, own_sum, *refs):
    count = len(distances)
    outer, inner = refs[:count], refs[count:2 * count]
    weight, result, tiles, products, attended, semaphores, out_semaphores = refs[2 * count:]
    here = Facts(facts, spans)
    total = own.shape[0]
    quarter = total // 4
    copies = [
        copied(weight.at[:, pl.ds(index * tiles.shape[2], tiles.shape[2])], tiles.at[index], semaphores.at[index])
        for index in range(tiles.shape[0])
    ]
    for served, pieces in (
        (outer, ((0, 0, quarter), (total - quarter, quarter, quarter))),
        (inner, ((quarter, 0, 2 * quarter),)),
    ):
        for start, at, size in pieces:
            there, back = slice(start, start + size), slice(at, at + size)

            def write(columns, part):
                attended[there, columns] = part

            merge(here.span, distances, own, own_sum, there, served, back, write)
    sent = []
    for index, copy in enumerate(copies):
        copy.wait()
        product = jnp.dot(attended[...], tiles[index], preferred_element_type=jnp.float32)
        products[index] = product.astype(jnp.bfloat16)
        columns = pl.ds(index * tiles.shape[2], tiles.shape[2])
        sent.append(copied(products.at[index], result.at[:, columns], out_semaphores.at[index]))
    for copy in sent:
        copy.wait()


def final_kernel(count, facts, row, own, gate, *refs):
    result = refs[-1]
    summed = own[...].astype(jnp.float32) + sum(ref[...].astype(jnp.float32) for ref in refs[:count])
    result[...] = (summed * gate[pl.ds(row[1], 1), :]).astype(jnp.bfloat16)


def final(facts, row, projected, gate_table, comes, first, tile, before):
    rows, columns = comes[0].shape
    start = first // tile
    piece = pl.BlockSpec((rows, tile), lambda j, f, r: (0, j))
    return pl.pallas_call(
        functools.partial(final_kernel, len(comes)),
        grid_spec=pltpu.PrefetchScalarGridSpec(
            num_scalar_prefetch=2,
            grid=(columns // tile,),
            in_specs=[
                pl.BlockSpec((rows, tile), lambda j, f, r: (r[2], start + j)),
                pl.BlockSpec((8, tile), lambda j, f, r: (r[0], start + j)),
            ] + [piece] * len(comes) + [ANY] * len(before),
            out_specs=pl.BlockSpec((rows, tile), lambda j, f, r: (0, start + j)),
        ),
        out_shape=jax.ShapeDtypeStruct((rows, gate_table.shape[1]), jnp.bfloat16),
        input_output_aliases={4 + len(comes): 0} if before else {},
        compiler_params=PARAMS,
        cost_estimate=SHORT,
        name="final",
    )(facts, row, in_hbm(projected), in_hbm(gate_table), *comes, *before)


def body(queries, keys, values, out_weight, gate_table, levels, visible):
    rows, width = queries.shape
    model = out_weight.shape[1]
    spans = lax.axis_size("span")
    ranks = lax.axis_size("tensor")
    span = lax.axis_index("span")
    rank = lax.axis_index("tensor")
    block = rows // ranks
    half = rows // 2
    bf16, f32 = jnp.bfloat16, jnp.float32
    numbers = jnp.arange(spans, dtype=jnp.int32)
    place = jnp.where(numbers == 0, span, jnp.where(numbers == 1, rank, 0)).astype(jnp.int32)
    facts = jnp.concatenate([visible, place[None, :], levels[None, :]], axis=0)
    level = jnp.sum(jnp.where(numbers == span, levels, 0))
    row = jnp.stack([level // 8, level % 8, rank]).astype(jnp.int32)

    query_outer, query_inner = pl.pallas_call(
        functools.partial(split_kernel, spans),
        in_specs=[SMEM, HBM],
        out_specs=[VMEM, VMEM],
        out_shape=[jax.ShapeDtypeStruct((half, width), bf16)] * 2,
        scratch_shapes=[pltpu.SemaphoreType.DMA((3,))],
        compiler_params=PARAMS,
        cost_estimate=SHORT,
        name="split",
    )(facts, in_hbm(queries))
    distances = list(range(2, spans, 2))
    asked_outer = [shifted(query_outer, "span", -distance) for distance in distances]
    swap = [(i, i + 1 - 2 * (i % 2)) for i in range(spans)]
    key_beside = lax.ppermute(keys, "span", swap)
    value_beside = lax.ppermute(values, "span", swap)

    own, own_sum = pl.pallas_call(
        functools.partial(local_kernel, spans),
        in_specs=[SMEM, HBM, HBM, HBM, ANY, ANY],
        out_specs=[VMEM] * 2,
        out_shape=[jax.ShapeDtypeStruct((rows, width), f32), jax.ShapeDtypeStruct((rows, LANES), f32)],
        scratch_shapes=[pltpu.VMEM((rows, width), bf16)] * 5 + [pltpu.SemaphoreType.DMA((5,))],
        compiler_params=PARAMS,
        cost_estimate=SHORT,
        name="local",
    )(facts, in_hbm(queries), in_hbm(keys), in_hbm(values), key_beside, value_beside)

    def served(asked, distance):
        return pl.pallas_call(
            functools.partial(served_kernel, distance, spans),
            in_specs=[SMEM] + [VMEM] * 5,
            out_specs=VMEM,
            out_shape=jax.ShapeDtypeStruct((half, width + LANES), bf16),
            compiler_params=PARAMS,
            cost_estimate=SHORT,
            name="served",
        )(facts, asked, keys, values, key_beside, value_beside)

    asked_outer, query_inner, own_sum = lax.optimization_barrier((asked_outer, query_inner, own_sum))
    asked_inner = [shifted(query_inner, "span", -distance) for distance in distances]
    out_outer = [served(q, d) for q, d in zip(asked_outer, distances)]
    back_outer = [shifted(o, "span", d) for o, d in zip(out_outer, distances)]
    asked_inner, out_outer = lax.optimization_barrier((asked_inner, out_outer))
    out_inner = [served(q, d) for q, d in zip(asked_inner, distances)]
    back_outer, out_inner = lax.optimization_barrier((back_outer, out_inner))
    back_inner = [shifted(o, "span", d) for o, d in zip(out_inner, distances)]

    chunks = 2
    columns = model // chunks
    tile = columns // 4
    last = ranks - 1
    weight = in_hbm(out_weight)

    def opening(chunk):
        return pl.pallas_call(
            functools.partial(opening_kernel, spans, ranks, distances, chunk * columns),
            in_specs=[SMEM] + [VMEM] * (2 + len(distances)) + [HBM],
            out_specs=VMEM,
            out_shape=jax.ShapeDtypeStruct((block, columns), bf16),
            scratch_shapes=[
                pltpu.VMEM((4, width, tile), bf16),
                pltpu.VMEM((block, width), bf16),
                pltpu.SemaphoreType.DMA((4,)),
            ],
            compiler_params=PARAMS,
            cost_estimate=SHORT,
            name="opening",
        )(facts, own, own_sum, *back_outer, weight)

    def hopped(sent, hop):
        return lax.ppermute(sent, "tensor", [(hop, hop + 1), (last - hop, last - hop - 1)])

    openings = [opening(chunk) for chunk in range(chunks)]
    arrived = [[hopped(sent, 0)] for sent in openings]
    back_inner, openings = lax.optimization_barrier((back_inner, openings))
    projected = pl.pallas_call(
        functools.partial(project_kernel, spans, distances),
        in_specs=[SMEM] + [VMEM] * (2 + 2 * len(distances)) + [HBM],
        out_specs=HBM,
        out_shape=jax.ShapeDtypeStruct((rows, model), bf16),
        scratch_shapes=[
            pltpu.VMEM((8, width, model // 8), bf16),
            pltpu.VMEM((8, rows, model // 8), bf16),
            pltpu.VMEM((rows, width), bf16),
            pltpu.SemaphoreType.DMA((8,)),
            pltpu.SemaphoreType.DMA((8,)),
        ],
        compiler_params=PARAMS,
        cost_estimate=SHORT,
        name="project",
    )(facts, own, own_sum, *back_outer, *back_inner, weight)

    for step in range(1, last):
        for chunk in range(chunks):
            comes = arrived[chunk]
            leaves = []
            for hop in range(step + 1):
                target = last - (step - hop)
                index = jnp.where(rank == hop, target, last - target)
                sent = lax.dynamic_slice(projected, (index * block, chunk * columns), (block, columns))
                if hop:
                    sent = (sent.astype(f32) + comes[hop - 1].astype(f32)).astype(bf16)
                else:
                    sent, comes[0] = lax.optimization_barrier((sent, comes[0]))
                leaves.append(hopped(sent, hop))
            arrived[chunk] = leaves
    result = ()
    for chunk in range(chunks):
        result = (final(facts, row, projected, gate_table, arrived[chunk], chunk * columns, columns // 2, result),)
    return result[0]


def solution(mesh):
    return jax.shard_map(
        body,
        mesh=mesh,
        in_specs=(
            P(("group", "span"), "tensor"),
            P(("group", "span"), "tensor"),
            P(("group", "span"), "tensor"),
            P("tensor", None),
            P(),
            P("group"),
            P("group", None),
        ),
        out_specs=P(("group", "span", "tensor"), None),
        check_vma=False,
    )
```

time: 195 us -> 138 us (0.71)
  the two profiles are of different devices: /device:TPU:14 before, /device:TPU:18 now
where the time goes in v6:
time: 138 us
  waiting for transfers between devices  62.9 us (46%)
  starting transfers between devices  33.5 us (24%)
  Pallas kernels  29 us (21%)
  other arithmetic  8.31 us (6%)
  between operations  2.54 us (2%)
    ppermute x12, waiting for transfers between devices, hopped(): lax.ppermute(sent, 'tensor', [(hop, hop + 1), (last - hop, last - hop - 1)])  48.5 us
    ppermute x12, starting transfers between devices, hopped(): lax.ppermute(sent, 'tensor', [(hop, hop + 1), (last - hop, last - hop - 1)])  26.9 us
    ppermute x4, waiting for transfers between devices, shifted(): lax.ppermute(block, axis, [(i, i + distance) for i in range(count) if 0 <...  14.4 us
    pallas_call x1, Pallas kernels, body(): pl.pallas_call(functools.partial(project_kernel, spans, distances), in_sp...  9.61 us
    convert_element_type x3, other arithmetic, body(): sent = (sent.astype(f32) + comes[hop - 1].astype(f32)).astype(bf16)  6.89 us
    pallas_call x2, Pallas kernels, served(): pl.pallas_call(functools.partial(served_kernel, distance, spans), in_spec...  6.44 us
    ppermute x4, starting transfers between devices, shifted(): lax.ppermute(block, axis, [(i, i + distance) for i in range(count) if 0 <...  6.06 us
    pallas_call x1, Pallas kernels, body(): pl.pallas_call(functools.partial(local_kernel, spans), in_specs=[SMEM, HB...  5.71 us
  transfers between devices with their start and end apart: 18, of which 10 were waited for; matrix products, arithmetic and copies ran while one was open for 4% of the time, Pallas kernels for 17%

profile of v6, /device:TPU:18, one launch (start us, length us, event | category | flops | bytes accessed | tf_op | source)
XLA Modules:
  0.0 137.7 jit_solution(13324408850114150526)
XLA Ops:
  0.0 0.0 collective-permute-start
  0.0 0.5 collective-permute-start.1
  0.5 0.7 pad_add_fusion.facts
  1.2 0.6 split.1
  1.9 0.0 copy-start.1
  1.9 0.0 copy-start.2
  1.9 1.4 %collective-permute-start.2 = (bf16[192,768]{1,0:T(8,128)(2,1)S(1)}, bf16[192,768]{1,0:T(8,128)(2,1)S(1)}, u32[]{:S(2)}, u32[]{:S(2)}) collective-permute-start(bf16[192,768]{1,0:T(8,128)(2,1)S(1)} %get-tuple-element.25), channel_id=1, source_target_pairs={{8,0},{12,4},{9,1},{13,5},{10,2},{14,6},{11,3},{15,7},{24,16},{28,... | collective-permute-start | bytes 884744 | tf_op jit(solution)/shard_map/ppermute | solution.py:29
  3.3 0.0 collective-permute-done.key_beside
  3.3 5.7 %local.1 = (f32[384,768]{1,0:T(8,128)S(1)}, f32[384,128]{1,0:T(8,128)S(1)}) custom-call(s32[6,4]{1,0:T(8,128)S(1)} %pad_add_fusion.facts, bf16[384,768]{1,0:T(8,128)(2,1)} %query.3, bf16[384,768]{1,0:T(8,128)(2,1)} %key.5, bf16[384,768]{1,0:T(8,128)(2,1)} %value.5, bf16[384,768]{1,0:T(8,128)(2,1)S(1)} %collective-permute-done.key_beside, ...), custom_call_target="tpu_custom_call" | custom-call | flops 1 | bytes 1 | tf_op jit(solution)/shard_map/local/pallas_call | solution.py:285
  9.1 4.0 %collective-permute-done.2.query = bf16[192,768]{1,0:T(8,128)(2,1)S(1)} collective-permute-done((bf16[192,768]{1,0:T(8,128)(2,1)S(1)}, bf16[192,768]{1,0:T(8,128)(2,1)S(1)}, u32[]{:S(2)}, u32[]{:S(2)}) %collective-permute-start.2) | collective-permute-done | bytes 294944 | tf_op jit(solution)/shard_map/ppermute | solution.py:29
  13.1 3.2 %served.2 = bf16[192,896]{1,0:T(8,128)(2,1)S(1)} custom-call(s32[6,4]{1,0:T(8,128)S(1)} %pad_add_fusion.facts, bf16[192,768]{1,0:T(8,128)(2,1)S(1)} %collective-permute-done.2.query, bf16[384,768]{1,0:T(8,128)(2,1)S(1)} %copy-done.1, bf16[384,768]{1,0:T(8,128)(2,1)S(1)} %copy-done.2, bf16[384,768]{1,0:T(8,128)(2,1)S(1)} %collective-permute-done.key_beside, ...), custom_call_target="tpu_custom_call" | custom-call | flops 1 | bytes 1 | tf_op jit(solution)/shard_map/served/pallas_call | solution.py:297
  16.3 1.3 collective-permute-start.3
  17.7 1.3 collective-permute-start.4
  19.0 9.0 %collective-permute-done.4.query = bf16[192,768]{1,0:T(8,128)(2,1)S(1)} collective-permute-done((bf16[192,768]{1,0:T(8,128)(2,1)S(1)}, bf16[192,768]{1,0:T(8,128)(2,1)S(1)}, u32[]{:S(2)}, u32[]{:S(2)}) %collective-permute-start.4) | collective-permute-done | bytes 294944 | tf_op jit(solution)/shard_map/ppermute | solution.py:29
  27.9 3.2 %served.3 = bf16[192,896]{1,0:T(8,128)(2,1)S(1)} custom-call(s32[6,4]{1,0:T(8,128)S(1)} %pad_add_fusion.facts, bf16[192,768]{1,0:T(8,128)(2,1)S(1)} %collective-permute-done.4.query, bf16[384,768]{1,0:T(8,128)(2,1)S(1)} %copy-done.1, bf16[384,768]{1,0:T(8,128)(2,1)S(1)} %copy-done.2, bf16[384,768]{1,0:T(8,128)(2,1)S(1)} %collective-permute-done.key_beside, ...), custom_call_target="tpu_custom_call" | custom-call | flops 1 | bytes 1 | tf_op jit(solution)/shard_map/served/pallas_call | solution.py:297
  31.1 0.0 collective-permute-done.3.refs_0_
  31.1 2.0 %collective-permute-start.5 = (bf16[192,896]{1,0:T(8,128)(2,1)S(1)}, bf16[192,896]{1,0:T(8,128)(2,1)}, u32[]{:S(2)}, u32[]{:S(2)}) collective-permute-start(bf16[192,896]{1,0:T(8,128)(2,1)S(1)} %served.3), channel_id=1, source_target_pairs={{0,8},{4,12},{1,9},{5,13},{2,10},{6,14},{3,11},{7,15},{16,24},{20,... | collective-permute-start | bytes 1032200 | tf_op jit(solution)/shard_map/ppermute | solution.py:29
  33.2 0.6 opening.2
  33.8 1.3 collective-permute-start.12
  35.1 0.6 opening.3
  35.8 1.5 %collective-permute-start.6 = (bf16[96,3072]{1,0:T(8,128)(2,1)S(1)}, bf16[96,3072]{1,0:T(8,128)(2,1)}, u32[]{:S(2)}, u32[]{:S(2)}) collective-permute-start(bf16[96,3072]{1,0:T(8,128)(2,1)S(1)} %opening.3), channel_id=1, source_target_pairs={{0,1},{3,2},{4,5},{7,6},{8,9},{11,10},{12,13},{15,14},{16,17},{19,... | collective-permute-start | bytes 1769480 | tf_op jit(solution)/shard_map/ppermute | solution.py:339
  37.3 1.4 %collective-permute-done.5.refs_1_ = bf16[192,896]{1,0:T(8,128)(2,1)} collective-permute-done((bf16[192,896]{1,0:T(8,128)(2,1)S(1)}, bf16[192,896]{1,0:T(8,128)(2,1)}, u32[]{:S(2)}, u32[]{:S(2)}) %collective-permute-start.5) | collective-permute-done | bytes 344096 | tf_op jit(solution)/shard_map/ppermute | solution.py:29
  38.7 9.6 %project.1.own = bf16[384,6144]{1,0:T(8,128)(2,1)S(1)} custom-call(s32[6,4]{1,0:T(8,128)S(1)} %pad_add_fusion.facts, f32[384,768]{1,0:T(8,128)S(1)} %get-tuple-element.24.own, f32[384,128]{1,0:T(8,128)S(1)} %get-tuple-element.28.own_sum, bf16[192,896]{1,0:T(8,128)(2,1)S(1)} %collective-permute-done.3.refs_0_, ...), custom_call_target="tpu_custom_call" | custom-call | flops 1 | bytes 1 | tf_op jit(solution)/shard_map/project/pallas_call | solution.py:344
  48.3 1.4 constant_dynamic-slice_fusion.2
  49.7 4.1 %collective-permute-done.12 = bf16[96,3072]{1,0:T(8,128)(2,1)} collective-permute-done((bf16[96,3072]{1,0:T(8,128)(2,1)S(1)}, bf16[96,3072]{1,0:T(8,128)(2,1)}, u32[]{:S(2)}, u32[]{:S(2)}) %collective-permute-start.12) | collective-permute-done | bytes 589856 | tf_op jit(solution)/shard_map/ppermute | solution.py:339
  53.8 10.4 %collective-permute-done.6 = bf16[96,3072]{1,0:T(8,128)(2,1)} collective-permute-done((bf16[96,3072]{1,0:T(8,128)(2,1)S(1)}, bf16[96,3072]{1,0:T(8,128)(2,1)}, u32[]{:S(2)}, u32[]{:S(2)}) %collective-permute-start.6) | collective-permute-done | bytes 589856 | tf_op jit(solution)/shard_map/ppermute | solution.py:339
  64.2 1.3 collective-permute-start.7
  65.5 1.3 collective-permute-start.13
  66.8 1.2 add_convert_fusion.1
  68.0 1.9 %collective-permute-start.16 = (bf16[96,3072]{1,0:T(8,128)(2,1)S(1)}, bf16[96,3072]{1,0:T(8,128)(2,1)S(1)}, u32[]{:S(2)}, u32[]{:S(2)}) collective-permute-start(bf16[96,3072]{1,0:T(8,128)(2,1)S(1)} %add_convert_fusion.1), channel_id=1, source_target_pairs={{1,2},{2,1},{5,6},{6,5},{9,10},{10,9},{13,14},{14,13},{17,18},{18,... | collective-permute-start | bytes 1769480 | tf_op jit(solution)/shard_map/ppermute | solution.py:339
  70.0 12.4 %collective-permute-done.7 = bf16[96,3072]{1,0:T(8,128)(2,1)S(1)} collective-permute-done((bf16[96,3072]{1,0:T(8,128)(2,1)S(1)}, bf16[96,3072]{1,0:T(8,128)(2,1)S(1)}, u32[]{:S(2)}, u32[]{:S(2)}) %collective-permute-start.7) | collective-permute-done | bytes 589856 | tf_op jit(solution)/shard_map/ppermute | solution.py:339
  82.3 9.5 %collective-permute-done.13 = bf16[96,3072]{1,0:T(8,128)(2,1)S(1)} collective-permute-done((bf16[96,3072]{1,0:T(8,128)(2,1)S(1)}, bf16[96,3072]{1,0:T(8,128)(2,1)S(1)}, u32[]{:S(2)}, u32[]{:S(2)}) %collective-permute-start.13) | collective-permute-done | bytes 589856 | tf_op jit(solution)/shard_map/ppermute | solution.py:339
  91.8 3.6 %add_convert_fusion = (bf16[96,3072]{1,0:T(8,128)(2,1)S(1)}, bf16[96,3072]{1,0:T(8,128)(2,1)}, bf16[96,3072]{1,0:T(8,128)(2,1)S(1)}, bf16[96,3072]{1,0:T(8,128)(2,1)}) fusion(bf16[96,3072]{1,0:T(8,128)(2,1)S(1)} %collective-permute-done.16, bf16[384,6144]{1,0:T(8,128)(2,1)} %copy-done, s32[]{:T(128)S(6)} %select_n.90, ...), kind=kLoop, calls=%fused_computation | loop fusion | flops 4718592 | bytes 7077900 | tf_op jit(solution)/shard_map/convert_element_type | solution.py:370
  95.5 2.0 %collective-permute-start.10 = (bf16[96,3072]{1,0:T(8,128)(2,1)S(1)}, bf16[96,3072]{1,0:T(8,128)(2,1)S(1)}, u32[]{:S(2)}, u32[]{:S(2)}) collective-permute-start(bf16[96,3072]{1,0:T(8,128)(2,1)S(1)} %get-tuple-element.45), channel_id=1, source_target_pairs={{1,2},{2,1},{5,6},{6,5},{9,10},{10,9},{13,14},{14,13},{17,18},{18,... | collective-permute-start | bytes 1769480 | tf_op jit(solution)/shard_map/ppermute | solution.py:339
  97.5 1.3 collective-permute-start.8
  98.8 4.6 %collective-permute-start.17 = (bf16[96,3072]{1,0:T(8,128)(2,1)S(1)}, bf16[96,3072]{1,0:T(8,128)(2,1)S(1)}, u32[]{:S(2)}, u32[]{:S(2)}) collective-permute-start(bf16[96,3072]{1,0:T(8,128)(2,1)S(1)} %get-tuple-element.43), channel_id=1, source_target_pairs={{2,3},{1,0},{6,7},{5,4},{10,11},{9,8},{14,15},{13,12},{18,19},{17,... | collective-permute-start | bytes 1769480 | tf_op jit(solution)/shard_map/ppermute | solution.py:339
  103.5 3.9 %collective-permute-start.15 = (bf16[96,3072]{1,0:T(8,128)(2,1)}, bf16[96,3072]{1,0:T(8,128)(2,1)S(1)}, u32[]{:S(2)}, u32[]{:S(2)}) collective-permute-start(bf16[96,3072]{1,0:T(8,128)(2,1)} %get-tuple-element.44), channel_id=1, source_target_pairs={{1,2},{2,1},{5,6},{6,5},{9,10},{10,9},{13,14},{14,13},{17,18},{18,... | collective-permute-start | bytes 1769480 | tf_op jit(solution)/shard_map/ppermute | solution.py:339
  107.4 1.9 %collective-permute-start.9 = (bf16[96,3072]{1,0:T(8,128)(2,1)}, bf16[96,3072]{1,0:T(8,128)(2,1)S(1)}, u32[]{:S(2)}, u32[]{:S(2)}) collective-permute-start(bf16[96,3072]{1,0:T(8,128)(2,1)} %get-tuple-element.46), channel_id=1, source_target_pairs={{1,2},{2,1},{5,6},{6,5},{9,10},{10,9},{13,14},{14,13},{17,18},{18,... | collective-permute-start | bytes 1769480 | tf_op jit(solution)/shard_map/ppermute | solution.py:339
  109.3 4.4 %collective-permute-done.10 = bf16[96,3072]{1,0:T(8,128)(2,1)S(1)} collective-permute-done((bf16[96,3072]{1,0:T(8,128)(2,1)S(1)}, bf16[96,3072]{1,0:T(8,128)(2,1)S(1)}, u32[]{:S(2)}, u32[]{:S(2)}) %collective-permute-start.10) | collective-permute-done | bytes 589856 | tf_op jit(solution)/shard_map/ppermute | solution.py:339
  113.8 1.3 collective-permute-start.14
  115.0 2.0 %add_convert_fusion.3 = bf16[96,3072]{1,0:T(8,128)(2,1)} fusion(bf16[96,3072]{1,0:T(8,128)(2,1)S(1)} %collective-permute-done.10, bf16[384,6144]{1,0:T(8,128)(2,1)} %copy-done, s32[]{:T(128)S(6)} %select_n.90), kind=kLoop, calls=%fused_computation.3 | loop fusion | flops 1179648 | bytes 1769476 | tf_op jit(solution)/shard_map/convert_element_type | solution.py:370
  117.1 4.6 %collective-permute-start.11 = (bf16[96,3072]{1,0:T(8,128)(2,1)}, bf16[96,3072]{1,0:T(8,128)(2,1)S(1)}, u32[]{:S(2)}, u32[]{:S(2)}) collective-permute-start(bf16[96,3072]{1,0:T(8,128)(2,1)} %add_convert_fusion.3), channel_id=1, source_target_pairs={{2,3},{1,0},{6,7},{5,4},{10,11},{9,8},{14,15},{13,12},{18,19},{17,... | collective-permute-start | bytes 1769480 | tf_op jit(solution)/shard_map/ppermute | solution.py:339
  121.7 0.6 fusion
  124.6 0.1 pad_add_fusion.1.row
  124.7 1.7 %collective-permute-done.15.refs_1_ = bf16[96,3072]{1,0:T(8,128)(2,1)S(1)} collective-permute-done((bf16[96,3072]{1,0:T(8,128)(2,1)}, bf16[96,3072]{1,0:T(8,128)(2,1)S(1)}, u32[]{:S(2)}, u32[]{:S(2)}) %collective-permute-start.15) | collective-permute-done | bytes 589856 | tf_op jit(solution)/shard_map/ppermute | solution.py:339
  126.4 2.7 %final.2.refs_3_ = bf16[96,6144]{1,0:T(8,128)(2,1)} custom-call(s32[6,4]{1,0:T(8,128)S(1)} %pad_add_fusion.facts, s32[3]{0:T(128)S(1)} %pad_add_fusion.1.row, bf16[384,6144]{1,0:T(8,128)(2,1)} %copy-done, f32[64,6144]{1,0:T(8,128)} %gate.3, bf16[96,3072]{1,0:T(8,128)(2,1)S(1)} %collective-permute-done.14.refs_0_, ...), custom_call_target="tpu_custom_call" | custom-call | flops 1 | bytes 1 | tf_op jit(solution)/shard_map/final/pallas_call | solution.py:234
  129.1 5.9 %collective-permute-done.9.refs_1_ = bf16[96,3072]{1,0:T(8,128)(2,1)S(1)} collective-permute-done((bf16[96,3072]{1,0:T(8,128)(2,1)}, bf16[96,3072]{1,0:T(8,128)(2,1)S(1)}, u32[]{:S(2)}, u32[]{:S(2)}) %collective-permute-start.9) | collective-permute-done | bytes 589856 | tf_op jit(solution)/shard_map/ppermute | solution.py:339
  135.0 2.7 %final.3 = bf16[96,6144]{1,0:T(8,128)(2,1)} custom-call(s32[6,4]{1,0:T(8,128)S(1)} %pad_add_fusion.facts, s32[3]{0:T(128)S(1)} %pad_add_fusion.1.row, bf16[384,6144]{1,0:T(8,128)(2,1)} %copy-done, f32[64,6144]{1,0:T(8,128)} %gate.3, bf16[96,3072]{1,0:T(8,128)(2,1)S(1)} %collective-permute-done.8.refs_0_, ...), custom_call_target="tpu_custom_call", output_to_operand_aliasing={{}: (7, {})} | custom-call | flops 1 | bytes 1 | tf_op jit(solution)/shard_map/final/pallas_call | solution.py:234
  (13 shorter events, 0.0 us)
Async XLA Ops:
  0.0 3.3 %collective-permute-start = (bf16[384,768]{1,0:T(8,128)(2,1)}, bf16[384,768]{1,0:T(8,128)(2,1)S(1)}, u32[]{:S(2)}, u32[]{:S(2)}) collective-permute-start(bf16[384,768]{1,0:T(8,128)(2,1)} %key.5), channel_id=1, source_target_pairs={{0,4},{4,0},{8,12},{12,8},{1,5},{5,1},{9,13},{13,9},{2,6},{6,2},{1... | collective-permute-start | bytes 1769480 | tf_op jit(solution)/shard_map/ppermute | solution.py:282
  0.0 3.3 %collective-permute-start.1 = (bf16[384,768]{1,0:T(8,128)(2,1)}, bf16[384,768]{1,0:T(8,128)(2,1)S(1)}, u32[]{:S(2)}, u32[]{:S(2)}) collective-permute-start(bf16[384,768]{1,0:T(8,128)(2,1)} %value.5), channel_id=1, source_target_pairs={{0,4},{4,0},{8,12},{12,8},{1,5},{5,1},{9,13},{13,9},{2,6},{6,2},{1... | collective-permute-start | bytes 1769480 | tf_op jit(solution)/shard_map/ppermute | solution.py:283
  1.9 11.2 %copy-start.1 = (bf16[384,768]{1,0:T(8,128)(2,1)S(1)}, bf16[384,768]{1,0:T(8,128)(2,1)}, u32[]{:S(2)}) copy-start(bf16[384,768]{1,0:T(8,128)(2,1)} %key.5) | copy-start | bytes 1769476
  1.9 11.2 %copy-start.2 = (bf16[384,768]{1,0:T(8,128)(2,1)S(1)}, bf16[384,768]{1,0:T(8,128)(2,1)}, u32[]{:S(2)}) copy-start(bf16[384,768]{1,0:T(8,128)(2,1)} %value.5) | copy-start | bytes 1769476
  1.9 11.2 %collective-permute-start.2 = (bf16[192,768]{1,0:T(8,128)(2,1)S(1)}, bf16[192,768]{1,0:T(8,128)(2,1)S(1)}, u32[]{:S(2)}, u32[]{:S(2)}) collective-permute-start(bf16[192,768]{1,0:T(8,128)(2,1)S(1)} %get-tuple-element.25), channel_id=1, source_target_pairs={{8,0},{12,4},{9,1},{13,5},{10,2},{14,6},{11,3},{15,7},{24,16},{28,... | collective-permute-start | bytes 884744 | tf_op jit(solution)/shard_map/ppermute | solution.py:29
  16.3 14.8 %collective-permute-start.3 = (bf16[192,896]{1,0:T(8,128)(2,1)S(1)}, bf16[192,896]{1,0:T(8,128)(2,1)S(1)}, u32[]{:S(2)}, u32[]{:S(2)}) collective-permute-start(bf16[192,896]{1,0:T(8,128)(2,1)S(1)} %served.2), channel_id=1, source_target_pairs={{0,8},{4,12},{1,9},{5,13},{2,10},{6,14},{3,11},{7,15},{16,24},{20,... | collective-permute-start | bytes 1032200 | tf_op jit(solution)/shard_map/ppermute | solution.py:29
  17.7 10.3 %collective-permute-start.4 = (bf16[192,768]{1,0:T(8,128)(2,1)S(1)}, bf16[192,768]{1,0:T(8,128)(2,1)S(1)}, u32[]{:S(2)}, u32[]{:S(2)}) collective-permute-start(bf16[192,768]{1,0:T(8,128)(2,1)S(1)} %get-tuple-element.30), channel_id=1, source_target_pairs={{8,0},{12,4},{9,1},{13,5},{10,2},{14,6},{11,3},{15,7},{24,16},{28,... | collective-permute-start | bytes 884744 | tf_op jit(solution)/shard_map/ppermute | solution.py:29
  31.1 7.6 %collective-permute-start.5 = (bf16[192,896]{1,0:T(8,128)(2,1)S(1)}, bf16[192,896]{1,0:T(8,128)(2,1)}, u32[]{:S(2)}, u32[]{:S(2)}) collective-permute-start(bf16[192,896]{1,0:T(8,128)(2,1)S(1)} %served.3), channel_id=1, source_target_pairs={{0,8},{4,12},{1,9},{5,13},{2,10},{6,14},{3,11},{7,15},{16,24},{20,... | collective-permute-start | bytes 1032200 | tf_op jit(solution)/shard_map/ppermute | solution.py:29
  33.8 19.9 %collective-permute-start.12 = (bf16[96,3072]{1,0:T(8,128)(2,1)S(1)}, bf16[96,3072]{1,0:T(8,128)(2,1)}, u32[]{:S(2)}, u32[]{:S(2)}) collective-permute-start(bf16[96,3072]{1,0:T(8,128)(2,1)S(1)} %opening.2), channel_id=1, source_target_pairs={{0,1},{3,2},{4,5},{7,6},{8,9},{11,10},{12,13},{15,14},{16,17},{19,... | collective-permute-start | bytes 1769480 | tf_op jit(solution)/shard_map/ppermute | solution.py:339
  35.8 28.4 %collective-permute-start.6 = (bf16[96,3072]{1,0:T(8,128)(2,1)S(1)}, bf16[96,3072]{1,0:T(8,128)(2,1)}, u32[]{:S(2)}, u32[]{:S(2)}) collective-permute-start(bf16[96,3072]{1,0:T(8,128)(2,1)S(1)} %opening.3), channel_id=1, source_target_pairs={{0,1},{3,2},{4,5},{7,6},{8,9},{11,10},{12,13},{15,14},{16,17},{19,... | collective-permute-start | bytes 1769480 | tf_op jit(solution)/shard_map/ppermute | solution.py:339
  48.3 18.4 %copy-start = (bf16[384,6144]{1,0:T(8,128)(2,1)}, bf16[384,6144]{1,0:T(8,128)(2,1)S(1)}, u32[]{:S(2)}) copy-start(bf16[384,6144]{1,0:T(8,128)(2,1)S(1)} %project.1.own) | copy-start | bytes 14155780
  64.2 18.1 %collective-permute-start.7 = (bf16[96,3072]{1,0:T(8,128)(2,1)S(1)}, bf16[96,3072]{1,0:T(8,128)(2,1)S(1)}, u32[]{:S(2)}, u32[]{:S(2)}) collective-permute-start(bf16[96,3072]{1,0:T(8,128)(2,1)S(1)} %get-tuple-element.35), channel_id=1, source_target_pairs={{0,1},{3,2},{4,5},{7,6},{8,9},{11,10},{12,13},{15,14},{16,17},{19,... | collective-permute-start | bytes 1769480 | tf_op jit(solution)/shard_map/ppermute | solution.py:339
  65.5 26.4 %collective-permute-start.13 = (bf16[96,3072]{1,0:T(8,128)(2,1)S(1)}, bf16[96,3072]{1,0:T(8,128)(2,1)S(1)}, u32[]{:S(2)}, u32[]{:S(2)}) collective-permute-start(bf16[96,3072]{1,0:T(8,128)(2,1)S(1)} %get-tuple-element.39), channel_id=1, source_target_pairs={{0,1},{3,2},{4,5},{7,6},{8,9},{11,10},{12,13},{15,14},{16,17},{19,... | collective-permute-start | bytes 1769480 | tf_op jit(solution)/shard_map/ppermute | solution.py:339
  68.0 23.8 %collective-permute-start.16 = (bf16[96,3072]{1,0:T(8,128)(2,1)S(1)}, bf16[96,3072]{1,0:T(8,128)(2,1)S(1)}, u32[]{:S(2)}, u32[]{:S(2)}) collective-permute-start(bf16[96,3072]{1,0:T(8,128)(2,1)S(1)} %add_convert_fusion.1), channel_id=1, source_target_pairs={{1,2},{2,1},{5,6},{6,5},{9,10},{10,9},{13,14},{14,13},{17,18},{18,... | collective-permute-start | bytes 1769480 | tf_op jit(solution)/shard_map/ppermute | solution.py:339
  95.5 26.2 %copy-start.3 = (s32[4]{0:T(128)S(1)}, s32[4]{0:T(128)}, u32[]{:S(2)}) copy-start(s32[4]{0:T(128)} %param.12) | copy-start | bytes 52
  95.5 18.3 %collective-permute-start.10 = (bf16[96,3072]{1,0:T(8,128)(2,1)S(1)}, bf16[96,3072]{1,0:T(8,128)(2,1)S(1)}, u32[]{:S(2)}, u32[]{:S(2)}) collective-permute-start(bf16[96,3072]{1,0:T(8,128)(2,1)S(1)} %get-tuple-element.45), channel_id=1, source_target_pairs={{1,2},{2,1},{5,6},{6,5},{9,10},{10,9},{13,14},{14,13},{17,18},{18,... | collective-permute-start | bytes 1769480 | tf_op jit(solution)/shard_map/ppermute | solution.py:339
  97.5 31.6 %collective-permute-start.8 = (bf16[96,3072]{1,0:T(8,128)(2,1)}, bf16[96,3072]{1,0:T(8,128)(2,1)S(1)}, u32[]{:S(2)}, u32[]{:S(2)}) collective-permute-start(bf16[96,3072]{1,0:T(8,128)(2,1)} %get-tuple-element.36), channel_id=1, source_target_pairs={{0,1},{3,2},{4,5},{7,6},{8,9},{11,10},{12,13},{15,14},{16,17},{19,... | collective-permute-start | bytes 1769480 | tf_op jit(solution)/shard_map/ppermute | solution.py:339
  98.8 18.3 %collective-permute-start.17 = (bf16[96,3072]{1,0:T(8,128)(2,1)S(1)}, bf16[96,3072]{1,0:T(8,128)(2,1)S(1)}, u32[]{:S(2)}, u32[]{:S(2)}) collective-permute-start(bf16[96,3072]{1,0:T(8,128)(2,1)S(1)} %get-tuple-element.43), channel_id=1, source_target_pairs={{2,3},{1,0},{6,7},{5,4},{10,11},{9,8},{14,15},{13,12},{18,19},{17,... | collective-permute-start | bytes 1769480 | tf_op jit(solution)/shard_map/ppermute | solution.py:339
  103.5 22.9 %collective-permute-start.15 = (bf16[96,3072]{1,0:T(8,128)(2,1)}, bf16[96,3072]{1,0:T(8,128)(2,1)S(1)}, u32[]{:S(2)}, u32[]{:S(2)}) collective-permute-start(bf16[96,3072]{1,0:T(8,128)(2,1)} %get-tuple-element.44), channel_id=1, source_target_pairs={{1,2},{2,1},{5,6},{6,5},{9,10},{10,9},{13,14},{14,13},{17,18},{18,... | collective-permute-start | bytes 1769480 | tf_op jit(solution)/shard_map/ppermute | solution.py:339
  107.4 27.6 %collective-permute-start.9 = (bf16[96,3072]{1,0:T(8,128)(2,1)}, bf16[96,3072]{1,0:T(8,128)(2,1)S(1)}, u32[]{:S(2)}, u32[]{:S(2)}) collective-permute-start(bf16[96,3072]{1,0:T(8,128)(2,1)} %get-tuple-element.46), channel_id=1, source_target_pairs={{1,2},{2,1},{5,6},{6,5},{9,10},{10,9},{13,14},{14,13},{17,18},{18,... | collective-permute-start | bytes 1769480 | tf_op jit(solution)/shard_map/ppermute | solution.py:339
  113.8 12.6 %collective-permute-start.14 = (bf16[96,3072]{1,0:T(8,128)(2,1)}, bf16[96,3072]{1,0:T(8,128)(2,1)S(1)}, u32[]{:S(2)}, u32[]{:S(2)}) collective-permute-start(bf16[96,3072]{1,0:T(8,128)(2,1)} %get-tuple-element.40), channel_id=1, source_target_pairs={{0,1},{3,2},{4,5},{7,6},{8,9},{11,10},{12,13},{15,14},{16,17},{19,... | collective-permute-start | bytes 1769480 | tf_op jit(solution)/shard_map/ppermute | solution.py:339
  117.1 17.9 %collective-permute-start.11 = (bf16[96,3072]{1,0:T(8,128)(2,1)}, bf16[96,3072]{1,0:T(8,128)(2,1)S(1)}, u32[]{:S(2)}, u32[]{:S(2)}) collective-permute-start(bf16[96,3072]{1,0:T(8,128)(2,1)} %add_convert_fusion.3), channel_id=1, source_target_pairs={{2,3},{1,0},{6,7},{5,4},{10,11},{9,8},{14,15},{13,12},{18,19},{17,... | collective-permute-start | bytes 1769480 | tf_op jit(solution)/shard_map/ppermute | solution.py:339

commit v7 on v6

--- a/solution.py
+++ b/solution.py
@@ -84,16 +84,24 @@
     return copy
 
 
-def split_kernel(spans, facts, query, outer, inner, semaphores):
-    rows = query.shape[0]
-    quarter = rows // 4
-
-    @pl.when(Facts(facts, spans).span > 1)
+def parts_of(rank, ranks, rows):
+    block = rows // ranks
+    lower = rank < ranks // 2
+    early = pl.multiple_of(jnp.where(lower, rows - block, 0), block)
+    late = pl.multiple_of(jnp.where(lower, 0, block), block)
+    return (early, block), (late, rows - block)
+
+
+def split_kernel(spans, ranks, facts, query, early, late, semaphores):
+    here = Facts(facts, spans)
+
+    @pl.when(here.span > 1)
     def _():
         copies = [
-            copied(query.at[pl.ds(0, quarter)], outer.at[pl.ds(0, quarter)], semaphores.at[0]),
-            copied(query.at[pl.ds(rows - quarter, quarter)], outer.at[pl.ds(quarter, quarter)], semaphores.at[1]),
-            copied(query.at[pl.ds(quarter, 2 * quarter)], inner, semaphores.at[2]),
+            copied(query.at[pl.ds(start, size)], target, semaphores.at[index])
+            for index, ((start, size), target) in enumerate(
+                zip(parts_of(here.rank, ranks, query.shape[0]), (early, late))
+            )
         ]
         for copy in copies:
             copy.wait()
@@ -161,93 +169,119 @@
         write(columns, merged.astype(jnp.bfloat16))
 
 
+def streamed(weight, first, tiles, semaphores):
+    count, _, tile = tiles.shape
+    return [
+        copied(weight.at[:, pl.ds(first + index * tile, tile)], tiles.at[index], semaphores.at[index])
+        for index in range(count)
+    ]
+
+
 def opening_kernel(spans, ranks, distances, first, facts, own, own_sum, *refs):
     served = refs[:len(distances)]
     weight, result, tiles, rows, semaphores = refs[len(distances):]
     here = Facts(facts, spans)
-    block, width = rows.shape
-    count, _, tile = tiles.shape
+    tile = tiles.shape[2]
 
     @pl.when(jnp.logical_or(here.rank == 0, here.rank == ranks - 1))
     def _():
-        copies = [
-            copied(weight.at[:, pl.ds(first + index * tile, tile)], tiles.at[index], semaphores.at[index])
-            for index in range(count)
-        ]
-        lowest = here.rank == 0
-        there = pl.ds(pl.multiple_of(jnp.where(lowest, own.shape[0] - block, 0), block), block)
-        back = pl.ds(pl.multiple_of(jnp.where(lowest, own.shape[0] // 2 - block, 0), block), block)
+        copies = streamed(weight, first, tiles, semaphores)
+        (start, size), _ = parts_of(here.rank, ranks, own.shape[0])
 
         def write(columns, part):
             rows[:, columns] = part
 
-        merge(here.span, distances, own, own_sum, there, served, back, write)
+        merge(here.span, distances, own, own_sum, pl.ds(start, size), served, slice(0, size), write)
         for index, copy in enumerate(copies):
             copy.wait()
             product = jnp.dot(rows[...], tiles[index], preferred_element_type=jnp.float32)
             result[:, index * tile:(index + 1) * tile] = product.astype(jnp.bfloat16)
 
 
-def project_kernel(spans, distances, facts, own, own_sum, *refs):
-    count = len(distances)
-    outer, inner = refs[:count], refs[count:2 * count]
-    weight, result, tiles, products, attended, semaphores, out_semaphores = refs[2 * count:]
-    here = Facts(facts, spans)
-    total = own.shape[0]
-    quarter = total // 4
-    copies = [
-        copied(weight.at[:, pl.ds(index * tiles.shape[2], tiles.shape[2])], tiles.at[index], semaphores.at[index])
-        for index in range(tiles.shape[0])
-    ]
-    for served, pieces in (
-        (outer, ((0, 0, quarter), (total - quarter, quarter, quarter))),
-        (inner, ((quarter, 0, 2 * quarter),)),
-    ):
-        for start, at, size in pieces:
-            there, back = slice(start, start + size), slice(at, at + size)
-
-            def write(columns, part):
-                attended[there, columns] = part
-
-            merge(here.span, distances, own, own_sum, there, served, back, write)
+def project_rows(rank, ranks, first, attended, weight, result, leaving, tiles, products, semaphores, out_semaphores):
+    count, width, tile = tiles.shape
+    block = attended.shape[0] // ranks
+    last = ranks - 1
+    copies = streamed(weight, first, tiles, semaphores)
+    yield
     sent = []
     for index, copy in enumerate(copies):
         copy.wait()
         product = jnp.dot(attended[...], tiles[index], preferred_element_type=jnp.float32)
         products[index] = product.astype(jnp.bfloat16)
-        columns = pl.ds(index * tiles.shape[2], tiles.shape[2])
+        columns = pl.ds(index * tile, tile)
         sent.append(copied(products.at[index], result.at[:, columns], out_semaphores.at[index]))
+        for step, target in enumerate(leaving, start=1):
+            start = pl.multiple_of(jnp.where(rank == 0, last - step, step) * block, block)
+            sent.append(copied(
+                products.at[index, pl.ds(start, block)], target.at[:, columns], out_semaphores.at[step * count + index]
+            ))
     for copy in sent:
         copy.wait()
 
 
-def final_kernel(count, facts, row, own, gate, *refs):
-    result = refs[-1]
-    summed = own[...].astype(jnp.float32) + sum(ref[...].astype(jnp.float32) for ref in refs[:count])
-    result[...] = (summed * gate[pl.ds(row[1], 1), :]).astype(jnp.bfloat16)
-
-
-def final(facts, row, projected, gate_table, comes, first, tile, before):
-    rows, columns = comes[0].shape
-    start = first // tile
-    piece = pl.BlockSpec((rows, tile), lambda j, f, r: (0, j))
-    return pl.pallas_call(
-        functools.partial(final_kernel, len(comes)),
-        grid_spec=pltpu.PrefetchScalarGridSpec(
-            num_scalar_prefetch=2,
-            grid=(columns // tile,),
-            in_specs=[
-                pl.BlockSpec((rows, tile), lambda j, f, r: (r[2], start + j)),
-                pl.BlockSpec((8, tile), lambda j, f, r: (r[0], start + j)),
-            ] + [piece] * len(comes) + [ANY] * len(before),
-            out_specs=pl.BlockSpec((rows, tile), lambda j, f, r: (0, start + j)),
-        ),
-        out_shape=jax.ShapeDtypeStruct((rows, gate_table.shape[1]), jnp.bfloat16),
-        input_output_aliases={4 + len(comes): 0} if before else {},
-        compiler_params=PARAMS,
-        cost_estimate=SHORT,
-        name="final",
-    )(facts, row, in_hbm(projected), in_hbm(gate_table), *comes, *before)
+def project_first_kernel(spans, ranks, distances, facts, own, own_sum, *refs):
+    count = len(distances)
+    early, late = refs[:count], refs[count:2 * count]
+    weight, attended, result = refs[2 * count:2 * count + 3]
+    leaving, scratch = refs[2 * count + 3:-4], refs[-4:]
+    here = Facts(facts, spans)
+    work = project_rows(here.rank, ranks, 0, attended, weight, result, leaving, *scratch)
+    next(work)
+    for (start, size), served in zip(parts_of(here.rank, ranks, own.shape[0]), (early, late)):
+        there = pl.ds(start, size)
+
+        def write(columns, part):
+            attended[there, columns] = part
+
+        merge(here.span, distances, own, own_sum, there, served, slice(0, size), write)
+    for _ in work:
+        pass
+
+
+def project_next_kernel(spans, ranks, first, facts, attended, weight, result, *refs):
+    leaving, scratch = refs[:-4], refs[-4:]
+    here = Facts(facts, spans)
+    for _ in project_rows(here.rank, ranks, first, attended, weight, result, leaving, *scratch):
+        pass
+
+
+def message_kernel(spans, ranks, hop, target, facts, projected, arrived, result, own, semaphores):
+    here = Facts(facts, spans)
+    block = result.shape[0]
+    last = ranks - 1
+
+    @pl.when(jnp.logical_or(here.rank == hop, here.rank == last - hop))
+    def _():
+        start = pl.multiple_of(jnp.where(here.rank == hop, target, last - target) * block, block)
+        copied(projected.at[pl.ds(start, block)], own, semaphores.at[0]).wait()
+        result[...] = (own[...].astype(jnp.float32) + arrived[...].astype(jnp.float32)).astype(jnp.bfloat16)
+
+
+def final_kernel(spans, ranks, count, first, facts, projected, gate_table, *refs):
+    comes, (result, own, gate, gated, semaphores) = refs[:count], refs[-5:]
+    here = Facts(facts, spans)
+    block, columns = own.shape
+    pieces = gated.shape[0]
+    wide = columns // pieces
+    level = here.level()
+    above = pl.multiple_of(level // 8 * 8, 8)
+    copies = [
+        copied(projected.at[pl.ds(pl.multiple_of(here.rank * block, block), block)], own, semaphores.at[0]),
+        copied(gate_table.at[pl.ds(above, 8), pl.ds(first, columns)], gate, semaphores.at[1]),
+    ]
+    for copy in copies:
+        copy.wait()
+    sent = []
+    for piece in range(pieces):
+        there = slice(piece * wide, (piece + 1) * wide)
+        summed = own[:, there].astype(jnp.float32) + sum(ref[:, there].astype(jnp.float32) for ref in comes)
+        gated[piece] = (summed * gate[pl.ds(lax.rem(level, 8), 1), there]).astype(jnp.bfloat16)
+        sent.append(copied(
+            gated.at[piece], result.at[:, pl.ds(first + piece * wide, wide)], semaphores.at[2 + piece]
+        ))
+    for copy in sent:
+        copy.wait()
 
 
 def body(queries, keys, values, out_weight, gate_table, levels, visible):
@@ -258,26 +292,27 @@
     span = lax.axis_index("span")
     rank = lax.axis_index("tensor")
     block = rows // ranks
-    half = rows // 2
     bf16, f32 = jnp.bfloat16, jnp.float32
     numbers = jnp.arange(spans, dtype=jnp.int32)
     place = jnp.where(numbers == 0, span, jnp.where(numbers == 1, rank, 0)).astype(jnp.int32)
     facts = jnp.concatenate([visible, place[None, :], levels[None, :]], axis=0)
-    level = jnp.sum(jnp.where(numbers == span, levels, 0))
-    row = jnp.stack([level // 8, level % 8, rank]).astype(jnp.int32)
-
-    query_outer, query_inner = pl.pallas_call(
-        functools.partial(split_kernel, spans),
+
+    query_early, query_late = pl.pallas_call(
+        functools.partial(split_kernel, spans, ranks),
         in_specs=[SMEM, HBM],
         out_specs=[VMEM, VMEM],
-        out_shape=[jax.ShapeDtypeStruct((half, width), bf16)] * 2,
-        scratch_shapes=[pltpu.SemaphoreType.DMA((3,))],
+        out_shape=[
+            jax.ShapeDtypeStruct((block, width), bf16),
+            jax.ShapeDtypeStruct((rows - block, width), bf16),
+        ],
+        scratch_shapes=[pltpu.SemaphoreType.DMA((2,))],
         compiler_params=PARAMS,
         cost_estimate=SHORT,
         name="split",
     )(facts, in_hbm(queries))
     distances = list(range(2, spans, 2))
-    asked_outer = [shifted(query_outer, "span", -distance) for distance in distances]
+    asked_early = [shifted(query_early, "span", -distance) for distance in distances]
+    asked_late = [shifted(query_late, "span", -distance) for distance in distances]
     swap = [(i, i + 1 - 2 * (i % 2)) for i in range(spans)]
     key_beside = lax.ppermute(keys, "span", swap)
     value_beside = lax.ppermute(values, "span", swap)
@@ -298,24 +333,24 @@
             functools.partial(served_kernel, distance, spans),
             in_specs=[SMEM] + [VMEM] * 5,
             out_specs=VMEM,
-            out_shape=jax.ShapeDtypeStruct((half, width + LANES), bf16),
+            out_shape=jax.ShapeDtypeStruct((asked.shape[0], width + LANES), bf16),
             compiler_params=PARAMS,
             cost_estimate=SHORT,
             name="served",
         )(facts, asked, keys, values, key_beside, value_beside)
 
-    asked_outer, query_inner, own_sum = lax.optimization_barrier((asked_outer, query_inner, own_sum))
-    asked_inner = [shifted(query_inner, "span", -distance) for distance in distances]
-    out_outer = [served(q, d) for q, d in zip(asked_outer, distances)]
-    back_outer = [shifted(o, "span", d) for o, d in zip(out_outer, distances)]
-    asked_inner, out_outer = lax.optimization_barrier((asked_inner, out_outer))
-    out_inner = [served(q, d) for q, d in zip(asked_inner, distances)]
-    back_outer, out_inner = lax.optimization_barrier((back_outer, out_inner))
-    back_inner = [shifted(o, "span", d) for o, d in zip(out_inner, distances)]
+    asked_early, own_sum = lax.optimization_barrier((asked_early, own_sum))
+    out_early = [served(q, d) for q, d in zip(asked_early, distances)]
+    back_early = [shifted(o, "span", d) for o, d in zip(out_early, distances)]
+    asked_late, out_early = lax.optimization_barrier((asked_late, out_early))
+    out_late = [served(q, d) for q, d in zip(asked_late, distances)]
+    back_early, out_late = lax.optimization_barrier((back_early, out_late))
+    back_late = [shifted(o, "span", d) for o, d in zip(out_late, distances)]
 
     chunks = 2
     columns = model // chunks
-    tile = columns // 4
+    tiles = 4
+    tile = columns // tiles
     last = ranks - 1
     weight = in_hbm(out_weight)
 
@@ -326,55 +361,99 @@
             out_specs=VMEM,
             out_shape=jax.ShapeDtypeStruct((block, columns), bf16),
             scratch_shapes=[
-                pltpu.VMEM((4, width, tile), bf16),
+                pltpu.VMEM((tiles, width, tile), bf16),
                 pltpu.VMEM((block, width), bf16),
-                pltpu.SemaphoreType.DMA((4,)),
+                pltpu.SemaphoreType.DMA((tiles,)),
             ],
             compiler_params=PARAMS,
             cost_estimate=SHORT,
             name="opening",
-        )(facts, own, own_sum, *back_outer, weight)
+        )(facts, own, own_sum, *back_early, weight)
 
     def hopped(sent, hop):
         return lax.ppermute(sent, "tensor", [(hop, hop + 1), (last - hop, last - hop - 1)])
 
     openings = [opening(chunk) for chunk in range(chunks)]
     arrived = [[hopped(sent, 0)] for sent in openings]
-    back_inner, openings = lax.optimization_barrier((back_inner, openings))
-    projected = pl.pallas_call(
-        functools.partial(project_kernel, spans, distances),
-        in_specs=[SMEM] + [VMEM] * (2 + 2 * len(distances)) + [HBM],
-        out_specs=HBM,
-        out_shape=jax.ShapeDtypeStruct((rows, model), bf16),
+    back_late, openings = lax.optimization_barrier((back_late, openings))
+
+    message_shape = jax.ShapeDtypeStruct((block, columns), bf16)
+    stored_shape = pltpu.HBM((rows, columns), bf16)
+    projection = dict(
         scratch_shapes=[
-            pltpu.VMEM((8, width, model // 8), bf16),
-            pltpu.VMEM((8, rows, model // 8), bf16),
-            pltpu.VMEM((rows, width), bf16),
-            pltpu.SemaphoreType.DMA((8,)),
-            pltpu.SemaphoreType.DMA((8,)),
+            pltpu.VMEM((tiles, width, tile), bf16),
+            pltpu.VMEM((tiles, rows, tile), bf16),
+            pltpu.SemaphoreType.DMA((tiles,)),
+            pltpu.SemaphoreType.DMA((tiles * last,)),
         ],
         compiler_params=PARAMS,
         cost_estimate=SHORT,
         name="project",
-    )(facts, own, own_sum, *back_outer, *back_inner, weight)
-
+    )
+    stored = [HBM] + [HBM] * (last - 1)
+    shapes = [stored_shape] + [message_shape] * (last - 1)
+    attended, *first_outputs = pl.pallas_call(
+        functools.partial(project_first_kernel, spans, ranks, distances),
+        in_specs=[SMEM] + [VMEM] * (2 + 2 * len(distances)) + [HBM],
+        out_specs=[VMEM] + stored,
+        out_shape=[jax.ShapeDtypeStruct((rows, width), bf16)] + shapes,
+        **projection,
+    )(facts, own, own_sum, *back_early, *back_late, weight)
+    projected = [first_outputs] + [
+        pl.pallas_call(
+            functools.partial(project_next_kernel, spans, ranks, chunk * columns),
+            in_specs=[SMEM, VMEM, HBM],
+            out_specs=stored,
+            out_shape=shapes,
+            **projection,
+        )(facts, attended, weight)
+        for chunk in range(1, chunks)
+    ]
+
+    def message(hop, target, chunk, comes):
+        return pl.pallas_call(
+            functools.partial(message_kernel, spans, ranks, hop, target),
+            in_specs=[SMEM, HBM, VMEM],
+            out_specs=VMEM,
+            out_shape=message_shape,
+            scratch_shapes=[pltpu.VMEM((block, columns), bf16), pltpu.SemaphoreType.DMA((1,))],
+            compiler_params=PARAMS,
+            cost_estimate=SHORT,
+            name="message",
+        )(facts, in_hbm(projected[chunk][0]), comes)
+
+    before = projected[-1][0]
     for step in range(1, last):
         for chunk in range(chunks):
-            comes = arrived[chunk]
-            leaves = []
-            for hop in range(step + 1):
-                target = last - (step - hop)
-                index = jnp.where(rank == hop, target, last - target)
-                sent = lax.dynamic_slice(projected, (index * block, chunk * columns), (block, columns))
-                if hop:
-                    sent = (sent.astype(f32) + comes[hop - 1].astype(f32)).astype(bf16)
-                else:
-                    sent, comes[0] = lax.optimization_barrier((sent, comes[0]))
-                leaves.append(hopped(sent, hop))
+            comes, before = lax.optimization_barrier((arrived[chunk], before))
+            sent, comes = lax.optimization_barrier((projected[chunk][step], comes))
+            leaves = [hopped(sent, 0)]
+            for hop in range(1, step + 1):
+                before = message(hop, last - (step - hop), chunk, comes[hop - 1])
+                leaves.append(hopped(before, hop))
             arrived[chunk] = leaves
+
     result = ()
+    pieces = 2
     for chunk in range(chunks):
-        result = (final(facts, row, projected, gate_table, arrived[chunk], chunk * columns, columns // 2, result),)
+        result = (
+            pl.pallas_call(
+                functools.partial(final_kernel, spans, ranks, last, chunk * columns),
+                in_specs=[SMEM, HBM, HBM] + [VMEM] * last + [ANY] * len(result),
+                out_specs=HBM,
+                out_shape=jax.ShapeDtypeStruct((block, model), bf16),
+                input_output_aliases={3 + last: 0} if result else {},
+                scratch_shapes=[
+                    pltpu.VMEM((block, columns), bf16),
+                    pltpu.VMEM((8, columns), f32),
+                    pltpu.VMEM((pieces, block, columns // pieces), bf16),
+                    pltpu.SemaphoreType.DMA((2 + pieces,)),
+                ],
+                compiler_params=PARAMS,
+                cost_estimate=SHORT,
+                name="final",
+            )(facts, in_hbm(projected[chunk][0]), in_hbm(gate_table), *arrived[chunk], *result),
+        )
     return result[0]
 
 

time: 138 us -> 122 us (0.88)
  the two profiles are of different devices: /device:TPU:18 before, /device:TPU:14 now
where the time goes in v7:
time: 122 us; the launch traced here: 121 us
  waiting for transfers between devices  50.5 us (41%)
  Pallas kernels  39.6 us (32%)
  starting transfers between devices  30.1 us (25%)
    ppermute x12, waiting for transfers between devices, hopped(): lax.ppermute(sent, 'tensor', [(hop, hop + 1), (last - hop, last - hop - 1)])  25.6 us
    ppermute x4, waiting for transfers between devices, shifted(): lax.ppermute(block, axis, [(i, i + distance) for i in range(count) if 0 <...  24.9 us
    ppermute x12, starting transfers between devices, hopped(): lax.ppermute(sent, 'tensor', [(hop, hop + 1), (last - hop, last - hop - 1)])  24.3 us
    pallas_call x6, Pallas kernels, message(): pl.pallas_call(functools.partial(message_kernel, spans, ranks, hop, targe...  11 us
    pallas_call x1, Pallas kernels, body(): pl.pallas_call(functools.partial(project_first_kernel, spans, ranks, dist...  7.04 us
    pallas_call x1, Pallas kernels, body(): pl.pallas_call(functools.partial(project_next_kernel, spans, ranks, chunk...  6.11 us
    pallas_call x1, Pallas kernels, body(): pl.pallas_call(functools.partial(local_kernel, spans), in_specs=[SMEM, HB...  5.71 us
    pallas_call x2, Pallas kernels, body(): pl.pallas_call(functools.partial(final_kernel, spans, ranks, last, chunk...  5.55 us
  transfers between devices with their start and end apart: 18, of which 9 were waited for; matrix products, arithmetic and copies ran while one was open for 1% of the time, Pallas kernels for 30%

profile of v7, /device:TPU:14, one launch (start us, length us, event | category | flops | bytes accessed | tf_op | source)
XLA Modules:
  0.0 121.4 jit_solution(13753518342183780256)
XLA Ops:
  0.0 0.5 collective-permute-start.1
  0.5 0.7 pad_add_fusion.facts
  1.2 1.7 %split.1 = (bf16[96,768]{1,0:T(8,128)(2,1)S(1)}, bf16[288,768]{1,0:T(8,128)(2,1)S(1)}) custom-call(s32[6,4]{1,0:T(8,128)S(1)} %pad_add_fusion.facts, bf16[384,768]{1,0:T(8,128)(2,1)} %query.3), custom_call_target="tpu_custom_call" | custom-call | flops 1 | bytes 1 | tf_op jit(solution)/shard_map/split/pallas_call | solution.py:300
  2.9 0.0 copy-start
  3.0 0.0 copy-start.1
  3.0 1.5 %collective-permute-start.4 = (bf16[288,768]{1,0:T(8,128)(2,1)S(1)}, bf16[288,768]{1,0:T(8,128)(2,1)S(1)}, u32[]{:S(2)}, u32[]{:S(2)}) collective-permute-start(bf16[288,768]{1,0:T(8,128)(2,1)S(1)} %get-tuple-element.43), channel_id=1, source_target_pairs={{8,0},{12,4},{9,1},{13,5},{10,2},{14,6},{11,3},{15,7},{24,16},{28,... | collective-permute-start | bytes 1327112 | tf_op jit(solution)/shard_map/ppermute | solution.py:29
  4.5 1.3 %collective-permute-start.2 = (bf16[96,768]{1,0:T(8,128)(2,1)S(1)}, bf16[96,768]{1,0:T(8,128)(2,1)S(1)}, u32[]{:S(2)}, u32[]{:S(2)}) collective-permute-start(bf16[96,768]{1,0:T(8,128)(2,1)S(1)} %get-tuple-element.39), channel_id=1, source_target_pairs={{8,0},{12,4},{9,1},{13,5},{10,2},{14,6},{11,3},{15,7},{24,16},{28,... | collective-permute-start | bytes 442376 | tf_op jit(solution)/shard_map/ppermute | solution.py:29
  5.8 0.0 collective-permute-done.key_beside
  5.8 0.0 collective-permute-done.1.value_beside
  5.8 5.7 %local.1 = (f32[384,768]{1,0:T(8,128)S(1)}, f32[384,128]{1,0:T(8,128)S(1)}) custom-call(s32[6,4]{1,0:T(8,128)S(1)} %pad_add_fusion.facts, bf16[384,768]{1,0:T(8,128)(2,1)} %query.3, bf16[384,768]{1,0:T(8,128)(2,1)} %key.5, bf16[384,768]{1,0:T(8,128)(2,1)} %value.5, bf16[384,768]{1,0:T(8,128)(2,1)S(1)} %collective-permute-done.key_beside, ...), custom_call_target="tpu_custom_call" | custom-call | flops 1 | bytes 1 | tf_op jit(solution)/shard_map/local/pallas_call | solution.py:320
  11.5 5.9 %collective-permute-done.2.query = bf16[96,768]{1,0:T(8,128)(2,1)S(1)} collective-permute-done((bf16[96,768]{1,0:T(8,128)(2,1)S(1)}, bf16[96,768]{1,0:T(8,128)(2,1)S(1)}, u32[]{:S(2)}, u32[]{:S(2)}) %collective-permute-start.2) | collective-permute-done | bytes 147488 | tf_op jit(solution)/shard_map/ppermute | solution.py:29
  17.4 0.6 served.2
  18.0 1.3 %collective-permute-start.3 = (bf16[96,896]{1,0:T(8,128)(2,1)S(1)}, bf16[96,896]{1,0:T(8,128)(2,1)S(1)}, u32[]{:S(2)}, u32[]{:S(2)}) collective-permute-start(bf16[96,896]{1,0:T(8,128)(2,1)S(1)} %served.2), channel_id=1, source_target_pairs={{0,8},{4,12},{1,9},{5,13},{2,10},{6,14},{3,11},{7,15},{16,24},{20,... | collective-permute-start | bytes 516104 | tf_op jit(solution)/shard_map/ppermute | solution.py:29
  19.4 0.6 served.3
  20.0 8.0 %collective-permute-done.3.refs_0_ = bf16[96,896]{1,0:T(8,128)(2,1)S(1)} collective-permute-done((bf16[96,896]{1,0:T(8,128)(2,1)S(1)}, bf16[96,896]{1,0:T(8,128)(2,1)S(1)}, u32[]{:S(2)}, u32[]{:S(2)}) %collective-permute-start.3) | collective-permute-done | bytes 172064 | tf_op jit(solution)/shard_map/ppermute | solution.py:29
  28.0 0.6 opening.2
  28.6 1.3 %collective-permute-start.7 = (bf16[96,3072]{1,0:T(8,128)(2,1)S(1)}, bf16[96,3072]{1,0:T(8,128)(2,1)S(1)}, u32[]{:S(2)}, u32[]{:S(2)}) collective-permute-start(bf16[96,3072]{1,0:T(8,128)(2,1)S(1)} %opening.2), channel_id=1, source_target_pairs={{0,1},{3,2},{4,5},{7,6},{8,9},{11,10},{12,13},{15,14},{16,17},{19,... | collective-permute-start | bytes 1769480 | tf_op jit(solution)/shard_map/ppermute | solution.py:374
  29.9 1.3 %collective-permute-start.5 = (bf16[288,896]{1,0:T(8,128)(2,1)S(1)}, bf16[288,896]{1,0:T(8,128)(2,1)S(1)}, u32[]{:S(2)}, u32[]{:S(2)}) collective-permute-start(bf16[288,896]{1,0:T(8,128)(2,1)S(1)} %served.3), channel_id=1, source_target_pairs={{0,8},{4,12},{1,9},{5,13},{2,10},{6,14},{3,11},{7,15},{16,24},{20,... | collective-permute-start | bytes 1548296 | tf_op jit(solution)/shard_map/ppermute | solution.py:29
  31.2 0.6 opening.3
  31.9 1.5 %collective-permute-start.6 = (bf16[96,3072]{1,0:T(8,128)(2,1)S(1)}, bf16[96,3072]{1,0:T(8,128)(2,1)S(1)}, u32[]{:S(2)}, u32[]{:S(2)}) collective-permute-start(bf16[96,3072]{1,0:T(8,128)(2,1)S(1)} %opening.3), channel_id=1, source_target_pairs={{0,1},{3,2},{4,5},{7,6},{8,9},{11,10},{12,13},{15,14},{16,17},{19,... | collective-permute-start | bytes 1769480 | tf_op jit(solution)/shard_map/ppermute | solution.py:374
  33.3 10.9 %collective-permute-done.5.refs_1_ = bf16[288,896]{1,0:T(8,128)(2,1)S(1)} collective-permute-done((bf16[288,896]{1,0:T(8,128)(2,1)S(1)}, bf16[288,896]{1,0:T(8,128)(2,1)S(1)}, u32[]{:S(2)}, u32[]{:S(2)}) %collective-permute-start.5) | collective-permute-done | bytes 516128 | tf_op jit(solution)/shard_map/ppermute | solution.py:29
  44.3 7.0 %project.2 = (bf16[384,768]{1,0:T(8,128)(2,1)S(1)}, bf16[384,3072]{1,0:T(8,128)(2,1)}, bf16[96,3072]{1,0:T(8,128)(2,1)S(1)}, bf16[96,3072]{1,0:T(8,128)(2,1)S(1)}) custom-call(s32[6,4]{1,0:T(8,128)S(1)} %pad_add_fusion.facts, f32[384,768]{1,0:T(8,128)S(1)} %get-tuple-element.38.own, f32[384,128]{1,0:T(8,128)S(1)} %get-tuple-element.41.own_sum, ...), custom_call_target="tpu_custom_call" | custom-call | flops 1 | bytes 1 | tf_op jit(solution)/shard_map/project/pallas_call | solution.py:395
  51.3 6.1 %project.3 = (bf16[384,3072]{1,0:T(8,128)(2,1)}, bf16[96,3072]{1,0:T(8,128)(2,1)S(1)}, bf16[96,3072]{1,0:T(8,128)(2,1)S(1)}) custom-call(s32[6,4]{1,0:T(8,128)S(1)} %pad_add_fusion.facts, bf16[384,768]{1,0:T(8,128)(2,1)S(1)} %get-tuple-element.48.attended, bf16[768,6144]{1,0:T(8,128)(2,1)} %weight.1), custom_call_target="tpu_custom_call" | custom-call | flops 1 | bytes 1 | tf_op jit(solution)/shard_map/project/pallas_call | solution.py:403
  57.5 1.8 %message.6 = bf16[96,3072]{1,0:T(8,128)(2,1)S(1)} custom-call(s32[6,4]{1,0:T(8,128)S(1)} %pad_add_fusion.facts, bf16[384,3072]{1,0:T(8,128)(2,1)} %get-tuple-element.52.projected, bf16[96,3072]{1,0:T(8,128)(2,1)S(1)} %collective-permute-done.7.arrived), custom_call_target="tpu_custom_call" | custom-call | flops 1 | bytes 1 | tf_op jit(solution)/shard_map/message/pallas_call | solution.py:414
  59.3 3.5 %collective-permute-start.11 = (bf16[96,3072]{1,0:T(8,128)(2,1)S(1)}, bf16[96,3072]{1,0:T(8,128)(2,1)S(1)}, u32[]{:S(2)}, u32[]{:S(2)}) collective-permute-start(bf16[96,3072]{1,0:T(8,128)(2,1)S(1)} %message.6), channel_id=1, source_target_pairs={{1,2},{2,1},{5,6},{6,5},{9,10},{10,9},{13,14},{14,13},{17,18},{18,... | collective-permute-start | bytes 1769480 | tf_op jit(solution)/shard_map/ppermute | solution.py:374
  62.8 1.3 %collective-permute-start.10 = (bf16[96,3072]{1,0:T(8,128)(2,1)S(1)}, bf16[96,3072]{1,0:T(8,128)(2,1)S(1)}, u32[]{:S(2)}, u32[]{:S(2)}) collective-permute-start(bf16[96,3072]{1,0:T(8,128)(2,1)S(1)} %get-tuple-element.60), channel_id=1, source_target_pairs={{0,1},{3,2},{4,5},{7,6},{8,9},{11,10},{12,13},{15,14},{16,17},{19,... | collective-permute-start | bytes 1769480 | tf_op jit(solution)/shard_map/ppermute | solution.py:374
  64.1 1.8 %message.7 = bf16[96,3072]{1,0:T(8,128)(2,1)S(1)} custom-call(s32[6,4]{1,0:T(8,128)S(1)} %pad_add_fusion.facts, bf16[384,3072]{1,0:T(8,128)(2,1)} %get-tuple-element.49.projected, bf16[96,3072]{1,0:T(8,128)(2,1)S(1)} %collective-permute-done.6.arrived), custom_call_target="tpu_custom_call" | custom-call | flops 1 | bytes 1 | tf_op jit(solution)/shard_map/message/pallas_call | solution.py:414
  65.9 2.4 %collective-permute-start.9 = (bf16[96,3072]{1,0:T(8,128)(2,1)S(1)}, bf16[96,3072]{1,0:T(8,128)(2,1)S(1)}, u32[]{:S(2)}, u32[]{:S(2)}) collective-permute-start(bf16[96,3072]{1,0:T(8,128)(2,1)S(1)} %message.7), channel_id=1, source_target_pairs={{1,2},{2,1},{5,6},{6,5},{9,10},{10,9},{13,14},{14,13},{17,18},{18,... | collective-permute-start | bytes 1769480 | tf_op jit(solution)/shard_map/ppermute | solution.py:374
  68.3 1.3 %collective-permute-start.8 = (bf16[96,3072]{1,0:T(8,128)(2,1)S(1)}, bf16[96,3072]{1,0:T(8,128)(2,1)S(1)}, u32[]{:S(2)}, u32[]{:S(2)}) collective-permute-start(bf16[96,3072]{1,0:T(8,128)(2,1)S(1)} %get-tuple-element.57), channel_id=1, source_target_pairs={{0,1},{3,2},{4,5},{7,6},{8,9},{11,10},{12,13},{15,14},{16,17},{19,... | collective-permute-start | bytes 1769480 | tf_op jit(solution)/shard_map/ppermute | solution.py:374
  69.6 7.9 %collective-permute-done.11.arrived = bf16[96,3072]{1,0:T(8,128)(2,1)S(1)} collective-permute-done((bf16[96,3072]{1,0:T(8,128)(2,1)S(1)}, bf16[96,3072]{1,0:T(8,128)(2,1)S(1)}, u32[]{:S(2)}, u32[]{:S(2)}) %collective-permute-start.11) | collective-permute-done | bytes 589856 | tf_op jit(solution)/shard_map/ppermute | solution.py:374
  77.5 3.5 %collective-permute-done.10.arrived = bf16[96,3072]{1,0:T(8,128)(2,1)S(1)} collective-permute-done((bf16[96,3072]{1,0:T(8,128)(2,1)S(1)}, bf16[96,3072]{1,0:T(8,128)(2,1)S(1)}, u32[]{:S(2)}, u32[]{:S(2)}) %collective-permute-start.10) | collective-permute-done | bytes 589856 | tf_op jit(solution)/shard_map/ppermute | solution.py:374
  80.9 1.8 %message.11 = bf16[96,3072]{1,0:T(8,128)(2,1)S(1)} custom-call(s32[6,4]{1,0:T(8,128)S(1)} %pad_add_fusion.facts, bf16[384,3072]{1,0:T(8,128)(2,1)} %get-tuple-element.52.projected, bf16[96,3072]{1,0:T(8,128)(2,1)S(1)} %collective-permute-done.10.arrived), custom_call_target="tpu_custom_call" | custom-call | flops 1 | bytes 1 | tf_op jit(solution)/shard_map/message/pallas_call | solution.py:414
  82.8 2.4 %collective-permute-start.16 = (bf16[96,3072]{1,0:T(8,128)(2,1)S(1)}, bf16[96,3072]{1,0:T(8,128)(2,1)S(1)}, u32[]{:S(2)}, u32[]{:S(2)}) collective-permute-start(bf16[96,3072]{1,0:T(8,128)(2,1)S(1)} %message.11), channel_id=1, source_target_pairs={{1,2},{2,1},{5,6},{6,5},{9,10},{10,9},{13,14},{14,13},{17,18},{18,... | collective-permute-start | bytes 1769480 | tf_op jit(solution)/shard_map/ppermute | solution.py:374
  85.2 1.8 %message.8 = bf16[96,3072]{1,0:T(8,128)(2,1)S(1)} custom-call(s32[6,4]{1,0:T(8,128)S(1)} %pad_add_fusion.facts, bf16[384,3072]{1,0:T(8,128)(2,1)} %get-tuple-element.52.projected, bf16[96,3072]{1,0:T(8,128)(2,1)S(1)} %collective-permute-done.11.arrived), custom_call_target="tpu_custom_call" | custom-call | flops 1 | bytes 1 | tf_op jit(solution)/shard_map/message/pallas_call | solution.py:414
  87.0 1.3 %collective-permute-start.17 = (bf16[96,3072]{1,0:T(8,128)(2,1)S(1)}, bf16[96,3072]{1,0:T(8,128)(2,1)S(1)}, u32[]{:S(2)}, u32[]{:S(2)}) collective-permute-start(bf16[96,3072]{1,0:T(8,128)(2,1)S(1)} %message.8), channel_id=1, source_target_pairs={{2,3},{1,0},{6,7},{5,4},{10,11},{9,8},{14,15},{13,12},{18,19},{17,... | collective-permute-start | bytes 1769480 | tf_op jit(solution)/shard_map/ppermute | solution.py:374
  88.3 1.8 %collective-permute-done.9.arrived = bf16[96,3072]{1,0:T(8,128)(2,1)S(1)} collective-permute-done((bf16[96,3072]{1,0:T(8,128)(2,1)S(1)}, bf16[96,3072]{1,0:T(8,128)(2,1)S(1)}, u32[]{:S(2)}, u32[]{:S(2)}) %collective-permute-start.9) | collective-permute-done | bytes 589856 | tf_op jit(solution)/shard_map/ppermute | solution.py:374
  90.1 0.1 collective-permute-done.8.arrived
  90.2 1.8 %message.9 = bf16[96,3072]{1,0:T(8,128)(2,1)S(1)} custom-call(s32[6,4]{1,0:T(8,128)S(1)} %pad_add_fusion.facts, bf16[384,3072]{1,0:T(8,128)(2,1)} %get-tuple-element.49.projected, bf16[96,3072]{1,0:T(8,128)(2,1)S(1)} %collective-permute-done.8.arrived), custom_call_target="tpu_custom_call" | custom-call | flops 1 | bytes 1 | tf_op jit(solution)/shard_map/message/pallas_call | solution.py:414
  92.0 1.3 %collective-permute-start.15 = (bf16[96,3072]{1,0:T(8,128)(2,1)S(1)}, bf16[96,3072]{1,0:T(8,128)(2,1)S(1)}, u32[]{:S(2)}, u32[]{:S(2)}) collective-permute-start(bf16[96,3072]{1,0:T(8,128)(2,1)S(1)} %get-tuple-element.69), channel_id=1, source_target_pairs={{0,1},{3,2},{4,5},{7,6},{8,9},{11,10},{12,13},{15,14},{16,17},{19,... | collective-permute-start | bytes 1769480 | tf_op jit(solution)/shard_map/ppermute | solution.py:374
  93.3 1.8 %message.10 = bf16[96,3072]{1,0:T(8,128)(2,1)S(1)} custom-call(s32[6,4]{1,0:T(8,128)S(1)} %pad_add_fusion.facts, bf16[384,3072]{1,0:T(8,128)(2,1)} %get-tuple-element.49.projected, bf16[96,3072]{1,0:T(8,128)(2,1)S(1)} %collective-permute-done.9.arrived), custom_call_target="tpu_custom_call" | custom-call | flops 1 | bytes 1 | tf_op jit(solution)/shard_map/message/pallas_call | solution.py:414
  95.2 3.4 %collective-permute-start.14 = (bf16[96,3072]{1,0:T(8,128)(2,1)S(1)}, bf16[96,3072]{1,0:T(8,128)(2,1)S(1)}, u32[]{:S(2)}, u32[]{:S(2)}) collective-permute-start(bf16[96,3072]{1,0:T(8,128)(2,1)S(1)} %message.10), channel_id=1, source_target_pairs={{2,3},{1,0},{6,7},{5,4},{10,11},{9,8},{14,15},{13,12},{18,19},{17,... | collective-permute-start | bytes 1769480 | tf_op jit(solution)/shard_map/ppermute | solution.py:374
  98.6 3.4 %collective-permute-start.13 = (bf16[96,3072]{1,0:T(8,128)(2,1)S(1)}, bf16[96,3072]{1,0:T(8,128)(2,1)S(1)}, u32[]{:S(2)}, u32[]{:S(2)}) collective-permute-start(bf16[96,3072]{1,0:T(8,128)(2,1)S(1)} %message.9), channel_id=1, source_target_pairs={{1,2},{2,1},{5,6},{6,5},{9,10},{10,9},{13,14},{14,13},{17,18},{18,... | collective-permute-start | bytes 1769480 | tf_op jit(solution)/shard_map/ppermute | solution.py:374
  102.0 1.3 %collective-permute-start.12 = (bf16[96,3072]{1,0:T(8,128)(2,1)S(1)}, bf16[96,3072]{1,0:T(8,128)(2,1)S(1)}, u32[]{:S(2)}, u32[]{:S(2)}) collective-permute-start(bf16[96,3072]{1,0:T(8,128)(2,1)S(1)} %get-tuple-element.66), channel_id=1, source_target_pairs={{0,1},{3,2},{4,5},{7,6},{8,9},{11,10},{12,13},{15,14},{16,17},{19,... | collective-permute-start | bytes 1769480 | tf_op jit(solution)/shard_map/ppermute | solution.py:374
  103.3 0.0 collective-permute-done.17.refs_2_
  103.3 6.9 %collective-permute-done.15.refs_0_ = bf16[96,3072]{1,0:T(8,128)(2,1)S(1)} collective-permute-done((bf16[96,3072]{1,0:T(8,128)(2,1)S(1)}, bf16[96,3072]{1,0:T(8,128)(2,1)S(1)}, u32[]{:S(2)}, u32[]{:S(2)}) %collective-permute-start.15) | collective-permute-done | bytes 589856 | tf_op jit(solution)/shard_map/ppermute | solution.py:374
  110.2 2.8 %final.2.refs_3_ = bf16[96,6144]{1,0:T(8,128)(2,1)} custom-call(s32[6,4]{1,0:T(8,128)S(1)} %pad_add_fusion.facts, bf16[384,3072]{1,0:T(8,128)(2,1)} %get-tuple-element.52.projected, f32[64,6144]{1,0:T(8,128)} %gate_table.3, bf16[96,3072]{1,0:T(8,128)(2,1)S(1)} %collective-permute-done.15.refs_0_, bf16[96,3072]{1,0:T(8,128)(2,1)S(1)} %collective-permute-done.16.refs_1_, ...), custom_call_target="tpu_custom_call" | custom-call | flops 1 | bytes 1 | tf_op jit(solution)/shard_map/final/pallas_call | solution.py:440
  113.0 5.5 %collective-permute-done.12.refs_0_ = bf16[96,3072]{1,0:T(8,128)(2,1)S(1)} collective-permute-done((bf16[96,3072]{1,0:T(8,128)(2,1)S(1)}, bf16[96,3072]{1,0:T(8,128)(2,1)S(1)}, u32[]{:S(2)}, u32[]{:S(2)}) %collective-permute-start.12) | collective-permute-done | bytes 589856 | tf_op jit(solution)/shard_map/ppermute | solution.py:374
  118.5 2.8 %final.3 = bf16[96,6144]{1,0:T(8,128)(2,1)} custom-call(s32[6,4]{1,0:T(8,128)S(1)} %pad_add_fusion.facts, bf16[384,3072]{1,0:T(8,128)(2,1)} %get-tuple-element.49.projected, f32[64,6144]{1,0:T(8,128)} %gate_table.3, bf16[96,3072]{1,0:T(8,128)(2,1)S(1)} %collective-permute-done.12.refs_0_, ...), custom_call_target="tpu_custom_call", output_to_operand_aliasing={{}: (6, {})} | custom-call | flops 1 | bytes 1 | tf_op jit(solution)/shard_map/final/pallas_call | solution.py:440
  (10 shorter events, 0.0 us)
Async XLA Ops:
  0.0 5.8 %collective-permute-start = (bf16[384,768]{1,0:T(8,128)(2,1)}, bf16[384,768]{1,0:T(8,128)(2,1)S(1)}, u32[]{:S(2)}, u32[]{:S(2)}) collective-permute-start(bf16[384,768]{1,0:T(8,128)(2,1)} %key.5), channel_id=1, source_target_pairs={{0,4},{4,0},{8,12},{12,8},{1,5},{5,1},{9,13},{13,9},{2,6},{6,2},{1... | collective-permute-start | bytes 1769480 | tf_op jit(solution)/shard_map/ppermute | solution.py:317
  0.0 5.8 %collective-permute-start.1 = (bf16[384,768]{1,0:T(8,128)(2,1)}, bf16[384,768]{1,0:T(8,128)(2,1)S(1)}, u32[]{:S(2)}, u32[]{:S(2)}) collective-permute-start(bf16[384,768]{1,0:T(8,128)(2,1)} %value.5), channel_id=1, source_target_pairs={{0,4},{4,0},{8,12},{12,8},{1,5},{5,1},{9,13},{13,9},{2,6},{6,2},{1... | collective-permute-start | bytes 1769480 | tf_op jit(solution)/shard_map/ppermute | solution.py:318
  2.9 14.5 %copy-start = (bf16[384,768]{1,0:T(8,128)(2,1)S(1)}, bf16[384,768]{1,0:T(8,128)(2,1)}, u32[]{:S(2)}) copy-start(bf16[384,768]{1,0:T(8,128)(2,1)} %key.5) | copy-start | bytes 1769476
  3.0 14.5 %copy-start.1 = (bf16[384,768]{1,0:T(8,128)(2,1)S(1)}, bf16[384,768]{1,0:T(8,128)(2,1)}, u32[]{:S(2)}) copy-start(bf16[384,768]{1,0:T(8,128)(2,1)} %value.5) | copy-start | bytes 1769476
  3.0 16.4 %collective-permute-start.4 = (bf16[288,768]{1,0:T(8,128)(2,1)S(1)}, bf16[288,768]{1,0:T(8,128)(2,1)S(1)}, u32[]{:S(2)}, u32[]{:S(2)}) collective-permute-start(bf16[288,768]{1,0:T(8,128)(2,1)S(1)} %get-tuple-element.43), channel_id=1, source_target_pairs={{8,0},{12,4},{9,1},{13,5},{10,2},{14,6},{11,3},{15,7},{24,16},{28,... | collective-permute-start | bytes 1327112 | tf_op jit(solution)/shard_map/ppermute | solution.py:29
  4.5 13.0 %collective-permute-start.2 = (bf16[96,768]{1,0:T(8,128)(2,1)S(1)}, bf16[96,768]{1,0:T(8,128)(2,1)S(1)}, u32[]{:S(2)}, u32[]{:S(2)}) collective-permute-start(bf16[96,768]{1,0:T(8,128)(2,1)S(1)} %get-tuple-element.39), channel_id=1, source_target_pairs={{8,0},{12,4},{9,1},{13,5},{10,2},{14,6},{11,3},{15,7},{24,16},{28,... | collective-permute-start | bytes 442376 | tf_op jit(solution)/shard_map/ppermute | solution.py:29
  18.0 9.9 %collective-permute-start.3 = (bf16[96,896]{1,0:T(8,128)(2,1)S(1)}, bf16[96,896]{1,0:T(8,128)(2,1)S(1)}, u32[]{:S(2)}, u32[]{:S(2)}) collective-permute-start(bf16[96,896]{1,0:T(8,128)(2,1)S(1)} %served.2), channel_id=1, source_target_pairs={{0,8},{4,12},{1,9},{5,13},{2,10},{6,14},{3,11},{7,15},{16,24},{20,... | collective-permute-start | bytes 516104 | tf_op jit(solution)/shard_map/ppermute | solution.py:29
  28.6 28.8 %collective-permute-start.7 = (bf16[96,3072]{1,0:T(8,128)(2,1)S(1)}, bf16[96,3072]{1,0:T(8,128)(2,1)S(1)}, u32[]{:S(2)}, u32[]{:S(2)}) collective-permute-start(bf16[96,3072]{1,0:T(8,128)(2,1)S(1)} %opening.2), channel_id=1, source_target_pairs={{0,1},{3,2},{4,5},{7,6},{8,9},{11,10},{12,13},{15,14},{16,17},{19,... | collective-permute-start | bytes 1769480 | tf_op jit(solution)/shard_map/ppermute | solution.py:374
  29.9 14.4 %collective-permute-start.5 = (bf16[288,896]{1,0:T(8,128)(2,1)S(1)}, bf16[288,896]{1,0:T(8,128)(2,1)S(1)}, u32[]{:S(2)}, u32[]{:S(2)}) collective-permute-start(bf16[288,896]{1,0:T(8,128)(2,1)S(1)} %served.3), channel_id=1, source_target_pairs={{0,8},{4,12},{1,9},{5,13},{2,10},{6,14},{3,11},{7,15},{16,24},{20,... | collective-permute-start | bytes 1548296 | tf_op jit(solution)/shard_map/ppermute | solution.py:29
  31.9 32.2 %collective-permute-start.6 = (bf16[96,3072]{1,0:T(8,128)(2,1)S(1)}, bf16[96,3072]{1,0:T(8,128)(2,1)S(1)}, u32[]{:S(2)}, u32[]{:S(2)}) collective-permute-start(bf16[96,3072]{1,0:T(8,128)(2,1)S(1)} %opening.3), channel_id=1, source_target_pairs={{0,1},{3,2},{4,5},{7,6},{8,9},{11,10},{12,13},{15,14},{16,17},{19,... | collective-permute-start | bytes 1769480 | tf_op jit(solution)/shard_map/ppermute | solution.py:374
  59.3 18.2 %collective-permute-start.11 = (bf16[96,3072]{1,0:T(8,128)(2,1)S(1)}, bf16[96,3072]{1,0:T(8,128)(2,1)S(1)}, u32[]{:S(2)}, u32[]{:S(2)}) collective-permute-start(bf16[96,3072]{1,0:T(8,128)(2,1)S(1)} %message.6), channel_id=1, source_target_pairs={{1,2},{2,1},{5,6},{6,5},{9,10},{10,9},{13,14},{14,13},{17,18},{18,... | collective-permute-start | bytes 1769480 | tf_op jit(solution)/shard_map/ppermute | solution.py:374
  62.8 18.2 %collective-permute-start.10 = (bf16[96,3072]{1,0:T(8,128)(2,1)S(1)}, bf16[96,3072]{1,0:T(8,128)(2,1)S(1)}, u32[]{:S(2)}, u32[]{:S(2)}) collective-permute-start(bf16[96,3072]{1,0:T(8,128)(2,1)S(1)} %get-tuple-element.60), channel_id=1, source_target_pairs={{0,1},{3,2},{4,5},{7,6},{8,9},{11,10},{12,13},{15,14},{16,17},{19,... | collective-permute-start | bytes 1769480 | tf_op jit(solution)/shard_map/ppermute | solution.py:374
  65.9 24.2 %collective-permute-start.9 = (bf16[96,3072]{1,0:T(8,128)(2,1)S(1)}, bf16[96,3072]{1,0:T(8,128)(2,1)S(1)}, u32[]{:S(2)}, u32[]{:S(2)}) collective-permute-start(bf16[96,3072]{1,0:T(8,128)(2,1)S(1)} %message.7), channel_id=1, source_target_pairs={{1,2},{2,1},{5,6},{6,5},{9,10},{10,9},{13,14},{14,13},{17,18},{18,... | collective-permute-start | bytes 1769480 | tf_op jit(solution)/shard_map/ppermute | solution.py:374
  68.3 21.9 %collective-permute-start.8 = (bf16[96,3072]{1,0:T(8,128)(2,1)S(1)}, bf16[96,3072]{1,0:T(8,128)(2,1)S(1)}, u32[]{:S(2)}, u32[]{:S(2)}) collective-permute-start(bf16[96,3072]{1,0:T(8,128)(2,1)S(1)} %get-tuple-element.57), channel_id=1, source_target_pairs={{0,1},{3,2},{4,5},{7,6},{8,9},{11,10},{12,13},{15,14},{16,17},{19,... | collective-permute-start | bytes 1769480 | tf_op jit(solution)/shard_map/ppermute | solution.py:374
  82.8 19.2 %collective-permute-start.16 = (bf16[96,3072]{1,0:T(8,128)(2,1)S(1)}, bf16[96,3072]{1,0:T(8,128)(2,1)S(1)}, u32[]{:S(2)}, u32[]{:S(2)}) collective-permute-start(bf16[96,3072]{1,0:T(8,128)(2,1)S(1)} %message.11), channel_id=1, source_target_pairs={{1,2},{2,1},{5,6},{6,5},{9,10},{10,9},{13,14},{14,13},{17,18},{18,... | collective-permute-start | bytes 1769480 | tf_op jit(solution)/shard_map/ppermute | solution.py:374
  87.0 16.3 %collective-permute-start.17 = (bf16[96,3072]{1,0:T(8,128)(2,1)S(1)}, bf16[96,3072]{1,0:T(8,128)(2,1)S(1)}, u32[]{:S(2)}, u32[]{:S(2)}) collective-permute-start(bf16[96,3072]{1,0:T(8,128)(2,1)S(1)} %message.8), channel_id=1, source_target_pairs={{2,3},{1,0},{6,7},{5,4},{10,11},{9,8},{14,15},{13,12},{18,19},{17,... | collective-permute-start | bytes 1769480 | tf_op jit(solution)/shard_map/ppermute | solution.py:374
  92.0 18.2 %collective-permute-start.15 = (bf16[96,3072]{1,0:T(8,128)(2,1)S(1)}, bf16[96,3072]{1,0:T(8,128)(2,1)S(1)}, u32[]{:S(2)}, u32[]{:S(2)}) collective-permute-start(bf16[96,3072]{1,0:T(8,128)(2,1)S(1)} %get-tuple-element.69), channel_id=1, source_target_pairs={{0,1},{3,2},{4,5},{7,6},{8,9},{11,10},{12,13},{15,14},{16,17},{19,... | collective-permute-start | bytes 1769480 | tf_op jit(solution)/shard_map/ppermute | solution.py:374
  95.2 17.8 %collective-permute-start.14 = (bf16[96,3072]{1,0:T(8,128)(2,1)S(1)}, bf16[96,3072]{1,0:T(8,128)(2,1)S(1)}, u32[]{:S(2)}, u32[]{:S(2)}) collective-permute-start(bf16[96,3072]{1,0:T(8,128)(2,1)S(1)} %message.10), channel_id=1, source_target_pairs={{2,3},{1,0},{6,7},{5,4},{10,11},{9,8},{14,15},{13,12},{18,19},{17,... | collective-permute-start | bytes 1769480 | tf_op jit(solution)/shard_map/ppermute | solution.py:374
  98.6 14.4 %collective-permute-start.13 = (bf16[96,3072]{1,0:T(8,128)(2,1)S(1)}, bf16[96,3072]{1,0:T(8,128)(2,1)S(1)}, u32[]{:S(2)}, u32[]{:S(2)}) collective-permute-start(bf16[96,3072]{1,0:T(8,128)(2,1)S(1)} %message.9), channel_id=1, source_target_pairs={{1,2},{2,1},{5,6},{6,5},{9,10},{10,9},{13,14},{14,13},{17,18},{18,... | collective-permute-start | bytes 1769480 | tf_op jit(solution)/shard_map/ppermute | solution.py:374
  102.0 16.5 %collective-permute-start.12 = (bf16[96,3072]{1,0:T(8,128)(2,1)S(1)}, bf16[96,3072]{1,0:T(8,128)(2,1)S(1)}, u32[]{:S(2)}, u32[]{:S(2)}) collective-permute-start(bf16[96,3072]{1,0:T(8,128)(2,1)S(1)} %get-tuple-element.66), channel_id=1, source_target_pairs={{0,1},{3,2},{4,5},{7,6},{8,9},{11,10},{12,13},{15,14},{16,17},{19,... | collective-permute-start | bytes 1769480 | tf_op jit(solution)/shard_map/ppermute | solution.py:374

commit v8 on v7

v8 whole, which is shorter than its diff:
```python
import functools

import jax
import jax.numpy as jnp
from jax import lax
from jax.experimental import pallas as pl
from jax.experimental.pallas import tpu as pltpu
from jax.sharding import PartitionSpec as P

HD = 128
LANES = 128
HIDDEN = -1e30
LOG2E = 1.4426950408889634
PARAMS = pltpu.CompilerParams(vmem_limit_bytes=24 * 1024 * 1024)
SMEM = pl.BlockSpec(memory_space=pltpu.SMEM)
VMEM = pl.BlockSpec(memory_space=pltpu.VMEM)
ANY = pl.BlockSpec(memory_space=pl.ANY)
HBM = pl.BlockSpec(memory_space=pltpu.HBM)
PIECE_LANES = 32


def taking(microseconds):
    return pl.CostEstimate(flops=0, bytes_accessed=int(microseconds * 3.69e6), transcendentals=0)


def in_hbm(array):
    return pltpu.with_memory_space_constraint(array, pltpu.HBM)


def shifted(block, axis, distance):
    count = lax.axis_size(axis)
    return lax.ppermute(block, axis, [(i, i + distance) for i in range(count) if 0 <= i + distance < count])


def head_columns(head):
    return slice(head * HD, (head + 1) * HD)


def attend(query, keys, values, flags, write, lanes=0):
    rows, width = query.shape
    scale = LOG2E * HD ** (-0.5)
    lane = lax.broadcasted_iota(jnp.int32, (rows, LANES), 1)
    packed = jnp.zeros((rows, LANES), jnp.float32)
    for head in range(width // HD):
        columns = head_columns(head)
        mine = query[:, columns]
        scores = [
            lax.dot_general(mine, key[:, columns], (((1,), (1,)), ((), ())), preferred_element_type=jnp.float32)
            for key in keys
        ]
        tops = [jnp.max(block, axis=-1, keepdims=True) * scale for block in scores]
        top = functools.reduce(
            jnp.maximum, [one if flag is None else jnp.where(flag, one, HIDDEN) for one, flag in zip(tops, flags)]
        )
        total, product = None, None
        for block, value, flag in zip(scores, values, flags):
            above = top if flag is None else jnp.where(flag, top, -HIDDEN)
            probs = jnp.exp2(block * scale - above)
            part = jnp.sum(probs, axis=-1, keepdims=True)
            part_product = jnp.dot(
                probs.astype(jnp.bfloat16), value[:, columns], preferred_element_type=jnp.float32
            )
            total = part if total is None else total + part
            product = part_product if product is None else product + part_product
        total = jnp.where(total > 0.0, total, 1.0)
        write(columns, product * (1.0 / total))
        packed = jnp.where(lane == lanes + head, top + jnp.log2(total), packed)
    return packed


class Facts:
    def __init__(self, ref, spans):
        self.ref, self.spans = ref, spans
        self.span, self.rank = ref[spans, 0], ref[spans, 1]
        self.beside = self.span + 1 - 2 * lax.rem(self.span, 2)

    def sees(self, asker, span):
        return self.ref[asker, span] > 0

    def level(self):
        return self.ref[self.spans + 1, self.span]


def copied(source, target, semaphore):
    copy = pltpu.make_async_copy(source, target, semaphore)
    copy.start()
    return copy


def parts_of(rank, ranks, rows):
    block = rows // ranks
    lower = rank < ranks // 2
    early = pl.multiple_of(jnp.where(lower, rows - block, 0), block)
    late = pl.multiple_of(jnp.where(lower, 0, block), block)
    return (early, block), (late, rows - block)


def split_kernel(spans, ranks, facts, query, *refs):
    here = Facts(facts, spans)
    *targets, semaphores = refs

    @pl.when(here.span > 1)
    def _():
        (early, _), (late, rest) = parts_of(here.rank, ranks, query.shape[0])
        half = rest // 2
        copies = [
            copied(query.at[pl.ds(start, target.shape[0])], target, semaphores.at[index])
            for index, (start, target) in enumerate(zip((early, late, pl.multiple_of(late + half, 16)), targets))
        ]
        for copy in copies:
            copy.wait()


def local_kernel(spans, heads, facts, query, key, value, key_beside, value_beside, result, sums, *scratch):
    here = Facts(facts, spans)
    query_, key_, value_, key_beside_, value_beside_, semaphores = scratch
    columns = pl.ds(heads.start * HD, len(heads) * HD)
    copies = [
        copied(source.at[:, columns], target, semaphores.at[index])
        for index, (source, target) in enumerate((
            (query, query_), (key, key_), (key_beside, key_beside_), (value, value_), (value_beside, value_beside_),
        ))
    ]
    for copy in copies:
        copy.wait()

    def write(columns, block):
        result[:, columns] = block

    flags = [None, here.sees(here.span, here.beside)]
    sums[...] = attend(query_, [key_, key_beside_], [value_, value_beside_], flags, write, heads.start)


def served_kernel(distance, spans, facts, key, value, key_beside, value_beside, *refs):
    here = Facts(facts, spans)

    @pl.when(here.span + distance < spans)
    def _():
        asker = jnp.minimum(here.span + distance, spans - 1)
        flags = [here.sees(asker, here.span), here.sees(asker, here.beside)]
        *queries, result = refs
        at = 0
        for query in queries:
            rows, width = query.shape
            there = slice(at, at + rows)

            def write(columns, block):
                result[there, columns] = block.astype(jnp.bfloat16)

            rest = attend(query, [key, key_beside], [value, value_beside], flags, write)
            sent = jnp.zeros_like(rest)
            for piece in range(3):
                part = rest.astype(jnp.bfloat16).astype(jnp.float32)
                sent = sent + (part if piece == 0 else pltpu.roll(part, piece * PIECE_LANES, 1))
                rest = rest - part
            result[there, width:] = sent.astype(jnp.bfloat16)
            at += rows


def merge(span, distances, own, own_sum, there, served, here, write):
    width = served[0].shape[1] - LANES
    sums = [own_sum[0][there, :] + own_sum[1][there, :]]
    for distance, ref in zip(distances, served):
        sent = ref[here, width:].astype(jnp.float32)
        joined = sent
        for piece in (1, 2):
            joined = joined + pltpu.roll(sent, LANES - piece * PIECE_LANES, 1)
        sums.append(jnp.where(span >= distance, joined, HIDDEN))
    top = functools.reduce(jnp.maximum, sums)
    shares = [jnp.exp2(one - top) for one in sums]
    over = 1.0 / sum(shares)
    shares = [share * over for share in shares]
    for head in range(width // HD):
        columns = head_columns(head)
        split = own[0].shape[1]
        mine = own[0][there, columns] if columns.stop <= split else (
            own[1][there, columns.start - split:columns.stop - split])
        merged = mine * shares[0][:, head:head + 1]
        for distance, share, ref in zip(distances, shares[1:], served):
            away = jnp.where(span >= distance, ref[here, columns].astype(jnp.float32), 0.0)
            merged = merged + away * share[:, head:head + 1]
        write(columns, merged.astype(jnp.bfloat16))


def streamed(weight, first, tiles, semaphores):
    count, _, tile = tiles.shape
    return [
        copied(weight.at[:, pl.ds(first + index * tile, tile)], tiles.at[index], semaphores.at[index])
        for index in range(count)
    ]


def opening_kernel(spans, ranks, distances, first, facts, *refs):
    own, own_sum, served = refs[:2], refs[2:4], refs[4:4 + len(distances)]
    weight, result, tiles, rows, semaphores = refs[4 + len(distances):]
    here = Facts(facts, spans)
    tile = tiles.shape[2]

    @pl.when(jnp.logical_or(here.rank == 0, here.rank == ranks - 1))
    def _():
        copies = streamed(weight, first, tiles, semaphores)
        (start, size), _ = parts_of(here.rank, ranks, own[0].shape[0])

        def write(columns, part):
            rows[:, columns] = part

        merge(here.span, distances, own, own_sum, pl.ds(start, size), served, slice(0, size), write)
        for index, copy in enumerate(copies):
            copy.wait()
            product = jnp.dot(rows[...], tiles[index], preferred_element_type=jnp.float32)
            result[:, index * tile:(index + 1) * tile] = product.astype(jnp.bfloat16)


def project_blocks(ranks, facts, step, attended, weight, results, tiles, semaphores):
    rank = facts.rank
    last = ranks - 1
    count, _, tile = tiles.shape
    copies = streamed(weight, 0, tiles, semaphores)
    yield
    ups, downs = results[::2], results[1::2]
    block, columns = ups[0].shape
    each = columns // tile
    for index, copy in enumerate(copies):
        copy.wait()
        there = slice(index % each * tile, (index % each + 1) * tile)
        for sends, target, result in (
            (rank <= step, last - step + rank, ups[index // each]),
            (rank >= last - step, step + rank - last, downs[index // each]),
        ):

            @pl.when(sends)
            def _():
                start = pl.multiple_of(target * block, block)
                product = jnp.dot(
                    attended[pl.ds(start, block), :], tiles[index], preferred_element_type=jnp.float32
                )
                result[:, there] = product.astype(jnp.bfloat16)


def merged_blocks_kernel(spans, ranks, distances, facts, *refs):
    count = len(distances)
    own, own_sum, refs = refs[:2], refs[2:4], refs[4:]
    early, late = refs[:count], refs[count:2 * count]
    weight, attended, *results, tiles, semaphores = refs[2 * count:]
    here = Facts(facts, spans)
    work = project_blocks(ranks, here, 1, attended, weight, results, tiles, semaphores)
    next(work)
    for (start, size), served in zip(parts_of(here.rank, ranks, own[0].shape[0]), (early, late)):
        there = pl.ds(start, size)

        def write(columns, part):
            attended[there, columns] = part

        merge(here.span, distances, own, own_sum, there, served, slice(0, size), write)
    for _ in work:
        pass


def blocks_kernel(spans, ranks, step, facts, attended, weight, *refs):
    *results, tiles, semaphores = refs
    for _ in project_blocks(ranks, Facts(facts, spans), step, attended, weight, results, tiles, semaphores):
        pass


def own_kernel(spans, facts, attended, weight, result, tiles, semaphores):
    block = result.shape[0]
    count, _, tile = tiles.shape
    copies = streamed(weight, 0, tiles, semaphores)
    start = pl.multiple_of(Facts(facts, spans).rank * block, block)
    for index, copy in enumerate(copies):
        copy.wait()
        product = jnp.dot(attended[pl.ds(start, block), :], tiles[index], preferred_element_type=jnp.float32)
        result[:, index * tile:(index + 1) * tile] = product.astype(jnp.bfloat16)


def final_kernel(spans, facts, done, projected, gate_table, up, down, result, own, gate, gated, semaphores):
    here = Facts(facts, spans)
    first, (block, columns) = done.shape[1], own.shape
    pieces = gated.shape[0]
    wide = columns // pieces
    level = here.level()
    above = pl.multiple_of(level // 8 * 8, 8)
    copies = [
        copied(projected.at[:, pl.ds(first, columns)], own, semaphores.at[0]),
        copied(gate_table.at[pl.ds(above, 8), pl.ds(first, columns)], gate, semaphores.at[1]),
    ]
    sent = [copied(done, result.at[:, pl.ds(0, first)], semaphores.at[2])]
    for copy in copies:
        copy.wait()
    for piece in range(pieces):
        there = slice(piece * wide, (piece + 1) * wide)
        summed = own[:, there].astype(jnp.float32) + up[:, there].astype(jnp.float32)
        summed = summed + down[:, there].astype(jnp.float32)
        gated[piece] = (summed * gate[pl.ds(lax.rem(level, 8), 1), there]).astype(jnp.bfloat16)
        sent.append(copied(
            gated.at[piece], result.at[:, pl.ds(first + piece * wide, wide)], semaphores.at[3 + piece]
        ))
    for copy in sent:
        copy.wait()


def body(queries, keys, values, out_weight, gate_table, levels, visible):
    rows, width = queries.shape
    model = out_weight.shape[1]
    spans = lax.axis_size("span")
    ranks = lax.axis_size("tensor")
    span = lax.axis_index("span")
    rank = lax.axis_index("tensor")
    block = rows // ranks
    bf16, f32 = jnp.bfloat16, jnp.float32
    numbers = jnp.arange(spans, dtype=jnp.int32)
    place = jnp.where(numbers == 0, span, jnp.where(numbers == 1, rank, 0)).astype(jnp.int32)
    facts = jnp.concatenate([visible, place[None, :], levels[None, :]], axis=0)

    query_early, *query_late = pl.pallas_call(
        functools.partial(split_kernel, spans, ranks),
        in_specs=[SMEM, HBM],
        out_specs=[VMEM] * 3,
        out_shape=[
            jax.ShapeDtypeStruct((part, width), bf16) for part in (block, (rows - block) // 2, (rows - block) // 2)
        ],
        scratch_shapes=[pltpu.SemaphoreType.DMA((3,))],
        compiler_params=PARAMS,
        cost_estimate=taking(1.7),
        name="split",
    )(facts, in_hbm(queries))
    distances = list(range(2, spans, 2))
    asked_early = [shifted(query_early, "span", -distance) for distance in distances]
    swap = [(i, i + 1 - 2 * (i % 2)) for i in range(spans)]
    key_beside = lax.ppermute(keys, "span", swap)
    value_beside = lax.ppermute(values, "span", swap)

    def local(heads):
        wide = len(heads) * HD
        return pl.pallas_call(
            functools.partial(local_kernel, spans, heads),
            in_specs=[SMEM, HBM, HBM, HBM, ANY, ANY],
            out_specs=[VMEM] * 2,
            out_shape=[jax.ShapeDtypeStruct((rows, wide), f32), jax.ShapeDtypeStruct((rows, LANES), f32)],
            scratch_shapes=[pltpu.VMEM((rows, wide), bf16)] * 5 + [pltpu.SemaphoreType.DMA((5,))],
            compiler_params=PARAMS,
            cost_estimate=taking(1.0 + 0.8 * len(heads)),
            name="local",
        )(facts, in_hbm(queries), in_hbm(keys), in_hbm(values), key_beside, value_beside)

    heads = width // HD
    own, own_sum = local(range(heads // 3))
    query_late, own_sum = lax.optimization_barrier((query_late, own_sum))
    asked_late = [
        [shifted(query, "span", -distance) for query in query_late] for distance in distances
    ]
    own, own_sum = zip((own, own_sum), local(range(heads // 3, heads)))

    def served(asked, distance):
        return pl.pallas_call(
            functools.partial(served_kernel, distance, spans),
            in_specs=[SMEM] + [VMEM] * (4 + len(asked)),
            out_specs=VMEM,
            out_shape=jax.ShapeDtypeStruct((sum(part.shape[0] for part in asked), width + LANES), bf16),
            compiler_params=PARAMS,
            cost_estimate=taking(3.3),
            name="served",
        )(facts, keys, values, key_beside, value_beside, *asked)

    asked_early, own_sum = lax.optimization_barrier((asked_early, list(own_sum)))
    out_early = [served([q], d) for q, d in zip(asked_early, distances)]
    back_early = [shifted(o, "span", d) for o, d in zip(out_early, distances)]
    asked_late, out_early = lax.optimization_barrier((asked_late, out_early))
    out_late = [served(q, d) for q, d in zip(asked_late, distances)]
    back_early, out_late = lax.optimization_barrier((back_early, out_late))
    back_late = [shifted(o, "span", d) for o, d in zip(out_late, distances)]

    chunks = 2
    columns = model // chunks
    tiles = 4
    tile = columns // tiles
    last = ranks - 1
    weight = in_hbm(out_weight)

    def opening(chunk):
        return pl.pallas_call(
            functools.partial(opening_kernel, spans, ranks, distances, chunk * columns),
            in_specs=[SMEM] + [VMEM] * (4 + len(distances)) + [HBM],
            out_specs=VMEM,
            out_shape=jax.ShapeDtypeStruct((block, columns), bf16),
            scratch_shapes=[
                pltpu.VMEM((tiles, width, tile), bf16),
                pltpu.VMEM((block, width), bf16),
                pltpu.SemaphoreType.DMA((tiles,)),
            ],
            compiler_params=PARAMS,
            cost_estimate=taking(3.4),
            name="opening",
        )(facts, *own, *own_sum, *back_early, weight)

    openings = [opening(chunk) for chunk in range(chunks)]
    ends = [(0, 1), (last, last - 1)]
    arrived = [[lax.ppermute(sent, "tensor", ends)] for sent in openings]
    back_late, openings = lax.optimization_barrier((back_late, openings))

    streaming = dict(
        scratch_shapes=[
            pltpu.VMEM((chunks * tiles, width, tile), bf16), pltpu.SemaphoreType.DMA((chunks * tiles,))
        ],
        compiler_params=PARAMS,
    )
    attended_shape = jax.ShapeDtypeStruct((rows, width), bf16)
    block_shapes = [jax.ShapeDtypeStruct((block, columns), bf16)] * (2 * chunks)
    attended, *blocks = pl.pallas_call(
        functools.partial(merged_blocks_kernel, spans, ranks, distances),
        in_specs=[SMEM] + [VMEM] * (4 + 2 * len(distances)) + [HBM],
        out_specs=[VMEM] * (1 + 2 * chunks),
        out_shape=[attended_shape] + block_shapes,
        cost_estimate=taking(6.0),
        name="merged_blocks",
        **streaming,
    )(facts, *own, *own_sum, *back_early, *back_late, weight)

    before = attended
    for step in range(1, last):
        if step > 1:
            attended, before = lax.optimization_barrier((attended, before))
            blocks = pl.pallas_call(
                functools.partial(blocks_kernel, spans, ranks, step),
                in_specs=[SMEM, VMEM, HBM],
                out_specs=[VMEM] * (2 * chunks),
                out_shape=block_shapes,
                cost_estimate=taking(5.0),
                name="blocks",
                **streaming,
            )(facts, attended, weight)
        for chunk in range(chunks):
            comes, blocks, before = lax.optimization_barrier((arrived[chunk], blocks, before))
            up, down = [
                (mine.astype(f32) + come.astype(f32)).astype(bf16)
                for mine, come in zip(blocks[2 * chunk:2 * chunk + 2], (comes[0], comes[-1]))
            ]
            before = (up, down)
            arrived[chunk] = [
                lax.ppermute(up, "tensor", [(i, i + 1) for i in range(step + 1)]),
                lax.ppermute(down, "tensor", [(last - i, last - i - 1) for i in range(step + 1)]),
            ]
    attended, before = lax.optimization_barrier((attended, before))
    projected = pl.pallas_call(
        functools.partial(own_kernel, spans),
        in_specs=[SMEM, VMEM, HBM],
        out_specs=VMEM,
        out_shape=jax.ShapeDtypeStruct((block, model), bf16),
        cost_estimate=taking(5.0),
        name="own",
        **streaming,
    )(facts, attended, weight)
    level = jnp.sum(jnp.where(numbers == span, levels, 0))
    gate = lax.dynamic_slice(gate_table, (level, 0), (1, model))
    finished = []
    for chunk in range(chunks - 1):
        there = slice(chunk * columns, (chunk + 1) * columns)
        summed = sum(part.astype(f32) for part in (projected[:, there], *arrived[chunk]))
        finished.append((summed * gate[:, there]).astype(bf16))
    pieces = 2
    return pl.pallas_call(
        functools.partial(final_kernel, spans),
        in_specs=[SMEM, ANY, ANY, HBM, VMEM, VMEM],
        out_specs=HBM,
        out_shape=jax.ShapeDtypeStruct((block, model), bf16),
        scratch_shapes=[
            pltpu.VMEM((block, columns), bf16),
            pltpu.VMEM((8, columns), f32),
            pltpu.VMEM((pieces, block, columns // pieces), bf16),
            pltpu.SemaphoreType.DMA((3 + pieces,)),
        ],
        compiler_params=PARAMS,
        cost_estimate=taking(2.7),
        name="final",
    )(facts, jnp.concatenate(finished, axis=1), projected, in_hbm(gate_table), *arrived[-1])


def solution(mesh):
    return jax.shard_map(
        body,
        mesh=mesh,
        in_specs=(
            P(("group", "span"), "tensor"),
            P(("group", "span"), "tensor"),
            P(("group", "span"), "tensor"),
            P("tensor", None),
            P(),
            P("group"),
            P("group", None),
        ),
        out_specs=P(("group", "span", "tensor"), None),
        check_vma=False,
    )
```

time: 122 us -> 112 us (0.918)
  the two profiles are of different devices: /device:TPU:14 before, /device:TPU:18 now
where the time goes in v8:
time: 112 us; the launch traced here: 111 us
  Pallas kernels  38 us (34%)
  waiting for transfers between devices  34.3 us (31%)
  starting transfers between devices  31.8 us (28%)
  other arithmetic  3.84 us (3%)
  between operations  2.46 us (2%)
    ppermute x4, waiting for transfers between devices, body(): lax.ppermute(down, 'tensor', [(last - i, last - i - 1) for i in range(ste...  20.8 us
    ppermute x4, starting transfers between devices, body(): lax.ppermute(down, 'tensor', [(last - i, last - i - 1) for i in range(ste...  12.3 us
    ppermute x4, starting transfers between devices, body(): lax.ppermute(up, 'tensor', [(i, i + 1) for i in range(step + 1)])  8.46 us
    pallas_call x2, Pallas kernels, served(): pl.pallas_call(functools.partial(served_kernel, distance, spans), in_spec...  8.03 us
    ppermute x5, starting transfers between devices, shifted(): lax.ppermute(block, axis, [(i, i + distance) for i in range(count) if 0 <...  7.73 us
    pallas_call x2, Pallas kernels, local(): pl.pallas_call(functools.partial(local_kernel, spans, heads), in_specs=[S...  7.4 us
    pallas_call x1, Pallas kernels, body(): pl.pallas_call(functools.partial(blocks_kernel, spans, ranks, step), in_s...  7.36 us
    ppermute x5, waiting for transfers between devices, shifted(): lax.ppermute(block, axis, [(i, i + distance) for i in range(count) if 0 <...  7.25 us
  transfers between devices with their start and end apart: 17, of which 8 were waited for; matrix products, arithmetic and copies ran while one was open for 4% of the time, Pallas kernels for 31%

profile of v8, /device:TPU:18, one launch (start us, length us, event | category | flops | bytes accessed | tf_op | source)
XLA Modules:
  0.0 111.3 jit_solution(10069893773822464610)
XLA Ops:
  0.0 0.5 collective-permute-start.1
  0.5 0.7 pad_add_fusion.facts
  1.2 0.6 split.1
  1.9 1.3 %collective-permute-start.2 = (bf16[96,768]{1,0:T(8,128)(2,1)S(1)}, bf16[96,768]{1,0:T(8,128)(2,1)S(1)}, u32[]{:S(2)}, u32[]{:S(2)}) collective-permute-start(bf16[96,768]{1,0:T(8,128)(2,1)S(1)} %get-tuple-element.54), channel_id=1, source_target_pairs={{8,0},{12,4},{9,1},{13,5},{10,2},{14,6},{11,3},{15,7},{24,16},{28,... | collective-permute-start | bytes 442376 | tf_op jit(solution)/shard_map/ppermute | solution.py:32
  3.2 3.0 %local.2 = (f32[384,256]{1,0:T(8,128)S(1)}, f32[384,128]{1,0:T(8,128)S(1)}) custom-call(s32[6,4]{1,0:T(8,128)S(1)} %pad_add_fusion.facts, bf16[384,768]{1,0:T(8,128)(2,1)} %query.5, bf16[384,768]{1,0:T(8,128)(2,1)} %key.7, bf16[384,768]{1,0:T(8,128)(2,1)} %value.7, bf16[384,768]{1,0:T(8,128)(2,1)S(1)} %collective-permute-done.key_beside, ...), custom_call_target="tpu_custom_call" | custom-call | bytes 9594000 | tf_op jit(solution)/shard_map/local/pallas_call | solution.py:335
  6.2 0.0 copy-start
  6.3 0.0 copy-start.1
  6.3 1.4 %collective-permute-start.4 = (bf16[144,768]{1,0:T(8,128)(2,1)S(1)}, bf16[144,768]{1,0:T(8,128)(2,1)S(1)}, u32[]{:S(2)}, u32[]{:S(2)}) collective-permute-start(bf16[144,768]{1,0:T(8,128)(2,1)S(1)} %get-tuple-element.63), channel_id=1, source_target_pairs={{8,0},{12,4},{9,1},{13,5},{10,2},{14,6},{11,3},{15,7},{24,16},{28,... | collective-permute-start | bytes 663560 | tf_op jit(solution)/shard_map/ppermute | solution.py:32
  7.7 1.3 %collective-permute-start.5 = (bf16[144,768]{1,0:T(8,128)(2,1)S(1)}, bf16[144,768]{1,0:T(8,128)(2,1)S(1)}, u32[]{:S(2)}, u32[]{:S(2)}) collective-permute-start(bf16[144,768]{1,0:T(8,128)(2,1)S(1)} %get-tuple-element.64), channel_id=1, source_target_pairs={{8,0},{12,4},{9,1},{13,5},{10,2},{14,6},{11,3},{15,7},{24,16},{28,... | collective-permute-start | bytes 663560 | tf_op jit(solution)/shard_map/ppermute | solution.py:32
  9.0 4.4 %local.3 = (f32[384,512]{1,0:T(8,128)S(1)}, f32[384,128]{1,0:T(8,128)S(1)}) custom-call(s32[6,4]{1,0:T(8,128)S(1)} %pad_add_fusion.facts, bf16[384,768]{1,0:T(8,128)(2,1)} %query.5, bf16[384,768]{1,0:T(8,128)(2,1)} %key.7, bf16[384,768]{1,0:T(8,128)(2,1)} %value.7, bf16[384,768]{1,0:T(8,128)(2,1)S(1)} %collective-permute-done.key_beside, ...), custom_call_target="tpu_custom_call" | custom-call | bytes 15498000 | tf_op jit(solution)/shard_map/local/pallas_call | solution.py:335
  13.4 2.8 %served.2 = bf16[96,896]{1,0:T(8,128)(2,1)S(1)} custom-call(s32[6,4]{1,0:T(8,128)S(1)} %pad_add_fusion.facts, bf16[384,768]{1,0:T(8,128)(2,1)S(1)} %copy-done, bf16[384,768]{1,0:T(8,128)(2,1)S(1)} %copy-done.1, bf16[384,768]{1,0:T(8,128)(2,1)S(1)} %collective-permute-done.key_beside, bf16[384,768]{1,0:T(8,128)(2,1)S(1)} %collective-permute-done.1.value_beside, ...), custom_call_target="tpu_custom_call" | custom-call | bytes 12177000 | tf_op jit(solution)/shard_map/served/pallas_call | solution.py:355
  16.2 2.4 %collective-permute-start.3 = (bf16[96,896]{1,0:T(8,128)(2,1)S(1)}, bf16[96,896]{1,0:T(8,128)(2,1)S(1)}, u32[]{:S(2)}, u32[]{:S(2)}) collective-permute-start(bf16[96,896]{1,0:T(8,128)(2,1)S(1)} %served.2), channel_id=1, source_target_pairs={{0,8},{4,12},{1,9},{5,13},{2,10},{6,14},{3,11},{7,15},{16,24},{20,... | collective-permute-start | bytes 516104 | tf_op jit(solution)/shard_map/ppermute | solution.py:32
  18.6 2.0 %collective-permute-done.5.refs_1_ = bf16[144,768]{1,0:T(8,128)(2,1)S(1)} collective-permute-done((bf16[144,768]{1,0:T(8,128)(2,1)S(1)}, bf16[144,768]{1,0:T(8,128)(2,1)S(1)}, u32[]{:S(2)}, u32[]{:S(2)}) %collective-permute-start.5) | collective-permute-done | bytes 221216 | tf_op jit(solution)/shard_map/ppermute | solution.py:32
  20.6 5.2 %served.3 = bf16[288,896]{1,0:T(8,128)(2,1)S(1)} custom-call(s32[6,4]{1,0:T(8,128)S(1)} %pad_add_fusion.facts, bf16[384,768]{1,0:T(8,128)(2,1)S(1)} %copy-done, bf16[384,768]{1,0:T(8,128)(2,1)S(1)} %copy-done.1, bf16[384,768]{1,0:T(8,128)(2,1)S(1)} %collective-permute-done.key_beside, bf16[384,768]{1,0:T(8,128)(2,1)S(1)} %collective-permute-done.1.value_beside, ...), custom_call_target="tpu_custom_call" | custom-call | bytes 12177000 | tf_op jit(solution)/shard_map/served/pallas_call | solution.py:355
  25.9 0.0 copy-start.2
  25.9 0.6 opening.2
  26.6 1.3 %collective-permute-start.8 = (bf16[96,3072]{1,0:T(8,128)(2,1)S(1)}, bf16[96,3072]{1,0:T(8,128)(2,1)}, u32[]{:S(2)}, u32[]{:S(2)}) collective-permute-start(bf16[96,3072]{1,0:T(8,128)(2,1)S(1)} %opening.2), channel_id=1, source_target_pairs={{0,1},{3,2},{4,5},{7,6},{8,9},{11,10},{12,13},{15,14},{16,17},{19,... | collective-permute-start | bytes 1769480 | tf_op jit(solution)/shard_map/ppermute | solution.py:398
  27.9 1.3 %collective-permute-start.6 = (bf16[288,896]{1,0:T(8,128)(2,1)S(1)}, bf16[288,896]{1,0:T(8,128)(2,1)S(1)}, u32[]{:S(2)}, u32[]{:S(2)}) collective-permute-start(bf16[288,896]{1,0:T(8,128)(2,1)S(1)} %served.3), channel_id=1, source_target_pairs={{0,8},{4,12},{1,9},{5,13},{2,10},{6,14},{3,11},{7,15},{16,24},{20,... | collective-permute-start | bytes 1548296 | tf_op jit(solution)/shard_map/ppermute | solution.py:32
  29.2 0.6 fusion.4
  31.8 0.9 constant_dynamic-slice_fusion
  32.7 0.6 opening.3
  33.3 1.5 %collective-permute-start.7 = (bf16[96,3072]{1,0:T(8,128)(2,1)S(1)}, bf16[96,3072]{1,0:T(8,128)(2,1)S(1)}, u32[]{:S(2)}, u32[]{:S(2)}) collective-permute-start(bf16[96,3072]{1,0:T(8,128)(2,1)S(1)} %opening.3), channel_id=1, source_target_pairs={{0,1},{3,2},{4,5},{7,6},{8,9},{11,10},{12,13},{15,14},{16,17},{19,... | collective-permute-start | bytes 1769480 | tf_op jit(solution)/shard_map/ppermute | solution.py:398
  34.8 5.2 %collective-permute-done.6.refs_5_ = bf16[288,896]{1,0:T(8,128)(2,1)S(1)} collective-permute-done((bf16[288,896]{1,0:T(8,128)(2,1)S(1)}, bf16[288,896]{1,0:T(8,128)(2,1)S(1)}, u32[]{:S(2)}, u32[]{:S(2)}) %collective-permute-start.6) | collective-permute-done | bytes 516128 | tf_op jit(solution)/shard_map/ppermute | solution.py:32
  40.0 5.7 %merged_blocks.1 = (bf16[384,768]{1,0:T(8,128)(2,1)S(1)}, bf16[96,3072]{1,0:T(8,128)(2,1)S(1)}, bf16[96,3072]{1,0:T(8,128)(2,1)S(1)}, bf16[96,3072]{1,0:T(8,128)(2,1)S(1)}, bf16[96,3072]{1,0:T(8,128)(2,1)S(1)}) custom-call(s32[6,4]{1,0:T(8,128)S(1)} %pad_add_fusion.facts, f32[384,256]{1,0:T(8,128)S(1)} %get-tuple-element.52.refs_0_, ...), custom_call_target="tpu_custom_call" | custom-call | bytes 22140000 | tf_op jit(solution)/shard_map/merged_blocks/pallas_call | solution.py:409
  45.8 0.9 collective-permute-done.8
  46.7 1.4 %fusion.1 = (bf16[96,3072]{1,0:T(8,128)(2,1)S(1)}, bf16[96,3072]{1,0:T(8,128)(2,1)S(1)}) fusion(bf16[96,3072]{1,0:T(8,128)(2,1)} %collective-permute-done.8, bf16[96,3072]{1,0:T(8,128)(2,1)S(1)} %get-tuple-element.76, bf16[96,3072]{1,0:T(8,128)(2,1)S(1)} %get-tuple-element.75), kind=kLoop, calls=%fused_computation.5 | loop fusion | flops 2064384 | bytes 2949120 | tf_op jit(solution)/shard_map/convert_element_type | solution.py:435
  48.0 1.3 %collective-permute-start.11 = (bf16[96,3072]{1,0:T(8,128)(2,1)S(1)}, bf16[96,3072]{1,0:T(8,128)(2,1)S(1)}, u32[]{:S(2)}, u32[]{:S(2)}) collective-permute-start(bf16[96,3072]{1,0:T(8,128)(2,1)S(1)} %get-tuple-element.102), channel_id=1, source_target_pairs={{0,1},{1,2},{4,5},{5,6},{8,9},{9,10},{12,13},{13,14},{16,17},{17,1... | collective-permute-start | bytes 1769480 | tf_op jit(solution)/shard_map/ppermute | solution.py:440
  49.3 4.6 %collective-permute-start.12 = (bf16[96,3072]{1,0:T(8,128)(2,1)S(1)}, bf16[96,3072]{1,0:T(8,128)(2,1)S(1)}, u32[]{:S(2)}, u32[]{:S(2)}) collective-permute-start(bf16[96,3072]{1,0:T(8,128)(2,1)S(1)} %get-tuple-element.101), channel_id=1, source_target_pairs={{3,2},{2,1},{7,6},{6,5},{11,10},{10,9},{15,14},{14,13},{19,18},{18... | collective-permute-start | bytes 1769480 | tf_op jit(solution)/shard_map/ppermute | solution.py:441
  53.9 5.3 %collective-permute-done.7 = bf16[96,3072]{1,0:T(8,128)(2,1)S(1)} collective-permute-done((bf16[96,3072]{1,0:T(8,128)(2,1)S(1)}, bf16[96,3072]{1,0:T(8,128)(2,1)S(1)}, u32[]{:S(2)}, u32[]{:S(2)}) %collective-permute-start.7) | collective-permute-done | bytes 589856 | tf_op jit(solution)/shard_map/ppermute | solution.py:398
  59.2 0.3 fusion.3
  59.5 1.9 %collective-permute-start.10 = (bf16[96,3072]{1,0:T(8,128)(2,1)S(1)}, bf16[96,3072]{1,0:T(8,128)(2,1)S(1)}, u32[]{:S(2)}, u32[]{:S(2)}) collective-permute-start(bf16[96,3072]{1,0:T(8,128)(2,1)S(1)} %get-tuple-element.99), channel_id=1, source_target_pairs={{3,2},{2,1},{7,6},{6,5},{11,10},{10,9},{15,14},{14,13},{19,18},{18... | collective-permute-start | bytes 1769480 | tf_op jit(solution)/shard_map/ppermute | solution.py:441
  61.4 1.3 %collective-permute-start.9 = (bf16[96,3072]{1,0:T(8,128)(2,1)S(1)}, bf16[96,3072]{1,0:T(8,128)(2,1)S(1)}, u32[]{:S(2)}, u32[]{:S(2)}) collective-permute-start(bf16[96,3072]{1,0:T(8,128)(2,1)S(1)} %get-tuple-element.100), channel_id=1, source_target_pairs={{0,1},{1,2},{4,5},{5,6},{8,9},{9,10},{12,13},{13,14},{16,17},{17,1... | collective-permute-start | bytes 1769480 | tf_op jit(solution)/shard_map/ppermute | solution.py:440
  62.7 7.4 %blocks.1 = (bf16[96,3072]{1,0:T(8,128)(2,1)S(1)}, bf16[96,3072]{1,0:T(8,128)(2,1)S(1)}, bf16[96,3072]{1,0:T(8,128)(2,1)S(1)}, bf16[96,3072]{1,0:T(8,128)(2,1)S(1)}) custom-call(s32[6,4]{1,0:T(8,128)S(1)} %pad_add_fusion.facts, bf16[384,768]{1,0:T(8,128)(2,1)S(1)} %get-tuple-element.98.attended, bf16[768,6144]{1,0:T(8,128)(2,1)} %weight.3), custom_call_target="tpu_custom_call" | custom-call | bytes 18450000 | tf_op jit(solution)/shard_map/blocks/pallas_call | solution.py:423
  70.1 1.7 %collective-permute-done.12 = bf16[96,3072]{1,0:T(8,128)(2,1)S(1)} collective-permute-done((bf16[96,3072]{1,0:T(8,128)(2,1)S(1)}, bf16[96,3072]{1,0:T(8,128)(2,1)S(1)}, u32[]{:S(2)}, u32[]{:S(2)}) %collective-permute-start.12) | collective-permute-done | bytes 589856 | tf_op jit(solution)/shard_map/ppermute | solution.py:441
  71.8 0.1 add_convert_fusion.3
  72.0 1.9 %collective-permute-start.13 = (bf16[96,3072]{1,0:T(8,128)(2,1)S(1)}, bf16[96,3072]{1,0:T(8,128)(2,1)S(1)}, u32[]{:S(2)}, u32[]{:S(2)}) collective-permute-start(bf16[96,3072]{1,0:T(8,128)(2,1)S(1)} %add_convert_fusion.3), channel_id=1, source_target_pairs={{0,1},{1,2},{2,3},{4,5},{5,6},{6,7},{8,9},{9,10},{10,11},{12,13},{... | collective-permute-start | bytes 1769480 | tf_op jit(solution)/shard_map/ppermute | solution.py:440
  73.9 0.1 add_convert_fusion.2
  74.1 3.9 %collective-permute-start.14 = (bf16[96,3072]{1,0:T(8,128)(2,1)S(1)}, bf16[96,3072]{1,0:T(8,128)(2,1)S(1)}, u32[]{:S(2)}, u32[]{:S(2)}) collective-permute-start(bf16[96,3072]{1,0:T(8,128)(2,1)S(1)} %add_convert_fusion.2), channel_id=1, source_target_pairs={{3,2},{2,1},{1,0},{7,6},{6,5},{5,4},{11,10},{10,9},{9,8},{15,14},{... | collective-permute-start | bytes 1769480 | tf_op jit(solution)/shard_map/ppermute | solution.py:441
  78.0 6.5 %collective-permute-done.10 = bf16[96,3072]{1,0:T(8,128)(2,1)S(1)} collective-permute-done((bf16[96,3072]{1,0:T(8,128)(2,1)S(1)}, bf16[96,3072]{1,0:T(8,128)(2,1)S(1)}, u32[]{:S(2)}, u32[]{:S(2)}) %collective-permute-start.10) | collective-permute-done | bytes 589856 | tf_op jit(solution)/shard_map/ppermute | solution.py:441
  84.5 0.1 add_convert_fusion
  84.6 1.9 %collective-permute-start.16 = (bf16[96,3072]{1,0:T(8,128)(2,1)S(1)}, bf16[96,3072]{1,0:T(8,128)(2,1)S(1)}, u32[]{:S(2)}, u32[]{:S(2)}) collective-permute-start(bf16[96,3072]{1,0:T(8,128)(2,1)S(1)} %add_convert_fusion), channel_id=1, source_target_pairs={{3,2},{2,1},{1,0},{7,6},{6,5},{5,4},{11,10},{10,9},{9,8},{15,14},{... | collective-permute-start | bytes 1769480 | tf_op jit(solution)/shard_map/ppermute | solution.py:441
  86.6 0.1 add_convert_fusion.1
  86.7 4.0 %collective-permute-start.15 = (bf16[96,3072]{1,0:T(8,128)(2,1)S(1)}, bf16[96,3072]{1,0:T(8,128)(2,1)S(1)}, u32[]{:S(2)}, u32[]{:S(2)}) collective-permute-start(bf16[96,3072]{1,0:T(8,128)(2,1)S(1)} %add_convert_fusion.1), channel_id=1, source_target_pairs={{0,1},{1,2},{2,3},{4,5},{5,6},{6,7},{8,9},{9,10},{10,11},{12,13},{... | collective-permute-start | bytes 1769480 | tf_op jit(solution)/shard_map/ppermute | solution.py:440
  90.7 4.9 %own.1.projected = bf16[96,6144]{1,0:T(8,128)(2,1)S(1)} custom-call(s32[6,4]{1,0:T(8,128)S(1)} %pad_add_fusion.facts, bf16[384,768]{1,0:T(8,128)(2,1)S(1)} %get-tuple-element.98.attended, bf16[768,6144]{1,0:T(8,128)(2,1)} %weight.3), custom_call_target="tpu_custom_call" | custom-call | bytes 18450000 | tf_op jit(solution)/shard_map/own/pallas_call | solution.py:444
  95.6 1.5 %collective-permute-done.14 = bf16[96,3072]{1,0:T(8,128)(2,1)S(1)} collective-permute-done((bf16[96,3072]{1,0:T(8,128)(2,1)S(1)}, bf16[96,3072]{1,0:T(8,128)(2,1)S(1)}, u32[]{:S(2)}, u32[]{:S(2)}) %collective-permute-start.14) | collective-permute-done | bytes 589856 | tf_op jit(solution)/shard_map/ppermute | solution.py:441
  97.1 0.3 multiply_convert_fusion.done
  97.4 11.1 %collective-permute-done.16.down = bf16[96,3072]{1,0:T(8,128)(2,1)S(1)} collective-permute-done((bf16[96,3072]{1,0:T(8,128)(2,1)S(1)}, bf16[96,3072]{1,0:T(8,128)(2,1)S(1)}, u32[]{:S(2)}, u32[]{:S(2)}) %collective-permute-start.16) | collective-permute-done | bytes 589856 | tf_op jit(solution)/shard_map/ppermute | solution.py:441
  108.5 2.7 %final.1 = bf16[96,6144]{1,0:T(8,128)(2,1)} custom-call(s32[6,4]{1,0:T(8,128)S(1)} %pad_add_fusion.facts, bf16[96,3072]{1,0:T(8,128)(2,1)S(1)} %multiply_convert_fusion.done, bf16[96,6144]{1,0:T(8,128)(2,1)S(1)} %own.1.projected, f32[64,6144]{1,0:T(8,128)} %gate_table.1, bf16[96,3072]{1,0:T(8,128)(2,1)S(1)} %collective-permute-done.15.up, ...), custom_call_target="tpu_custom_call" | custom-call | bytes 9963000 | tf_op jit(solution)/shard_map/final/pallas_call | solution.py:461
  (14 shorter events, 0.0 us)
Async XLA Ops:
  0.0 3.2 %collective-permute-start = (bf16[384,768]{1,0:T(8,128)(2,1)}, bf16[384,768]{1,0:T(8,128)(2,1)S(1)}, u32[]{:S(2)}, u32[]{:S(2)}) collective-permute-start(bf16[384,768]{1,0:T(8,128)(2,1)} %key.7), channel_id=1, source_target_pairs={{0,4},{4,0},{8,12},{12,8},{1,5},{5,1},{9,13},{13,9},{2,6},{6,2},{1... | collective-permute-start | bytes 1769480 | tf_op jit(solution)/shard_map/ppermute | solution.py:330
  0.0 3.2 %collective-permute-start.1 = (bf16[384,768]{1,0:T(8,128)(2,1)}, bf16[384,768]{1,0:T(8,128)(2,1)S(1)}, u32[]{:S(2)}, u32[]{:S(2)}) collective-permute-start(bf16[384,768]{1,0:T(8,128)(2,1)} %value.7), channel_id=1, source_target_pairs={{0,4},{4,0},{8,12},{12,8},{1,5},{5,1},{9,13},{13,9},{2,6},{6,2},{1... | collective-permute-start | bytes 1769480 | tf_op jit(solution)/shard_map/ppermute | solution.py:331
  1.9 11.5 %collective-permute-start.2 = (bf16[96,768]{1,0:T(8,128)(2,1)S(1)}, bf16[96,768]{1,0:T(8,128)(2,1)S(1)}, u32[]{:S(2)}, u32[]{:S(2)}) collective-permute-start(bf16[96,768]{1,0:T(8,128)(2,1)S(1)} %get-tuple-element.54), channel_id=1, source_target_pairs={{8,0},{12,4},{9,1},{13,5},{10,2},{14,6},{11,3},{15,7},{24,16},{28,... | collective-permute-start | bytes 442376 | tf_op jit(solution)/shard_map/ppermute | solution.py:32
  6.2 7.1 %copy-start = (bf16[384,768]{1,0:T(8,128)(2,1)S(1)}, bf16[384,768]{1,0:T(8,128)(2,1)}, u32[]{:S(2)}) copy-start(bf16[384,768]{1,0:T(8,128)(2,1)} %key.7) | copy-start | bytes 1769476
  6.3 7.1 %copy-start.1 = (bf16[384,768]{1,0:T(8,128)(2,1)S(1)}, bf16[384,768]{1,0:T(8,128)(2,1)}, u32[]{:S(2)}) copy-start(bf16[384,768]{1,0:T(8,128)(2,1)} %value.7) | copy-start | bytes 1769476
  6.3 12.3 %collective-permute-start.4 = (bf16[144,768]{1,0:T(8,128)(2,1)S(1)}, bf16[144,768]{1,0:T(8,128)(2,1)S(1)}, u32[]{:S(2)}, u32[]{:S(2)}) collective-permute-start(bf16[144,768]{1,0:T(8,128)(2,1)S(1)} %get-tuple-element.63), channel_id=1, source_target_pairs={{8,0},{12,4},{9,1},{13,5},{10,2},{14,6},{11,3},{15,7},{24,16},{28,... | collective-permute-start | bytes 663560 | tf_op jit(solution)/shard_map/ppermute | solution.py:32
  7.7 12.9 %collective-permute-start.5 = (bf16[144,768]{1,0:T(8,128)(2,1)S(1)}, bf16[144,768]{1,0:T(8,128)(2,1)S(1)}, u32[]{:S(2)}, u32[]{:S(2)}) collective-permute-start(bf16[144,768]{1,0:T(8,128)(2,1)S(1)} %get-tuple-element.64), channel_id=1, source_target_pairs={{8,0},{12,4},{9,1},{13,5},{10,2},{14,6},{11,3},{15,7},{24,16},{28,... | collective-permute-start | bytes 663560 | tf_op jit(solution)/shard_map/ppermute | solution.py:32
  16.2 9.7 %collective-permute-start.3 = (bf16[96,896]{1,0:T(8,128)(2,1)S(1)}, bf16[96,896]{1,0:T(8,128)(2,1)S(1)}, u32[]{:S(2)}, u32[]{:S(2)}) collective-permute-start(bf16[96,896]{1,0:T(8,128)(2,1)S(1)} %served.2), channel_id=1, source_target_pairs={{0,8},{4,12},{1,9},{5,13},{2,10},{6,14},{3,11},{7,15},{16,24},{20,... | collective-permute-start | bytes 516104 | tf_op jit(solution)/shard_map/ppermute | solution.py:32
  25.9 3.3 %copy-start.2 = (s32[4]{0:T(128)S(1)}, s32[4]{0:T(128)}, u32[]{:S(2)}) copy-start(s32[4]{0:T(128)} %param.12) | copy-start | bytes 52
  26.6 20.1 %collective-permute-start.8 = (bf16[96,3072]{1,0:T(8,128)(2,1)S(1)}, bf16[96,3072]{1,0:T(8,128)(2,1)}, u32[]{:S(2)}, u32[]{:S(2)}) collective-permute-start(bf16[96,3072]{1,0:T(8,128)(2,1)S(1)} %opening.2), channel_id=1, source_target_pairs={{0,1},{3,2},{4,5},{7,6},{8,9},{11,10},{12,13},{15,14},{16,17},{19,... | collective-permute-start | bytes 1769480 | tf_op jit(solution)/shard_map/ppermute | solution.py:398
  27.9 12.2 %collective-permute-start.6 = (bf16[288,896]{1,0:T(8,128)(2,1)S(1)}, bf16[288,896]{1,0:T(8,128)(2,1)S(1)}, u32[]{:S(2)}, u32[]{:S(2)}) collective-permute-start(bf16[288,896]{1,0:T(8,128)(2,1)S(1)} %served.3), channel_id=1, source_target_pairs={{0,8},{4,12},{1,9},{5,13},{2,10},{6,14},{3,11},{7,15},{16,24},{20,... | collective-permute-start | bytes 1548296 | tf_op jit(solution)/shard_map/ppermute | solution.py:32
  33.3 25.9 %collective-permute-start.7 = (bf16[96,3072]{1,0:T(8,128)(2,1)S(1)}, bf16[96,3072]{1,0:T(8,128)(2,1)S(1)}, u32[]{:S(2)}, u32[]{:S(2)}) collective-permute-start(bf16[96,3072]{1,0:T(8,128)(2,1)S(1)} %opening.3), channel_id=1, source_target_pairs={{0,1},{3,2},{4,5},{7,6},{8,9},{11,10},{12,13},{15,14},{16,17},{19,... | collective-permute-start | bytes 1769480 | tf_op jit(solution)/shard_map/ppermute | solution.py:398
  48.0 22.1 %collective-permute-start.11 = (bf16[96,3072]{1,0:T(8,128)(2,1)S(1)}, bf16[96,3072]{1,0:T(8,128)(2,1)S(1)}, u32[]{:S(2)}, u32[]{:S(2)}) collective-permute-start(bf16[96,3072]{1,0:T(8,128)(2,1)S(1)} %get-tuple-element.102), channel_id=1, source_target_pairs={{0,1},{1,2},{4,5},{5,6},{8,9},{9,10},{12,13},{13,14},{16,17},{17,1... | collective-permute-start | bytes 1769480 | tf_op jit(solution)/shard_map/ppermute | solution.py:440
  49.3 22.5 %collective-permute-start.12 = (bf16[96,3072]{1,0:T(8,128)(2,1)S(1)}, bf16[96,3072]{1,0:T(8,128)(2,1)S(1)}, u32[]{:S(2)}, u32[]{:S(2)}) collective-permute-start(bf16[96,3072]{1,0:T(8,128)(2,1)S(1)} %get-tuple-element.101), channel_id=1, source_target_pairs={{3,2},{2,1},{7,6},{6,5},{11,10},{10,9},{15,14},{14,13},{19,18},{18... | collective-permute-start | bytes 1769480 | tf_op jit(solution)/shard_map/ppermute | solution.py:441
  59.5 25.0 %collective-permute-start.10 = (bf16[96,3072]{1,0:T(8,128)(2,1)S(1)}, bf16[96,3072]{1,0:T(8,128)(2,1)S(1)}, u32[]{:S(2)}, u32[]{:S(2)}) collective-permute-start(bf16[96,3072]{1,0:T(8,128)(2,1)S(1)} %get-tuple-element.99), channel_id=1, source_target_pairs={{3,2},{2,1},{7,6},{6,5},{11,10},{10,9},{15,14},{14,13},{19,18},{18... | collective-permute-start | bytes 1769480 | tf_op jit(solution)/shard_map/ppermute | solution.py:441
  61.4 23.1 %collective-permute-start.9 = (bf16[96,3072]{1,0:T(8,128)(2,1)S(1)}, bf16[96,3072]{1,0:T(8,128)(2,1)S(1)}, u32[]{:S(2)}, u32[]{:S(2)}) collective-permute-start(bf16[96,3072]{1,0:T(8,128)(2,1)S(1)} %get-tuple-element.100), channel_id=1, source_target_pairs={{0,1},{1,2},{4,5},{5,6},{8,9},{9,10},{12,13},{13,14},{16,17},{17,1... | collective-permute-start | bytes 1769480 | tf_op jit(solution)/shard_map/ppermute | solution.py:440
  72.0 23.6 %collective-permute-start.13 = (bf16[96,3072]{1,0:T(8,128)(2,1)S(1)}, bf16[96,3072]{1,0:T(8,128)(2,1)S(1)}, u32[]{:S(2)}, u32[]{:S(2)}) collective-permute-start(bf16[96,3072]{1,0:T(8,128)(2,1)S(1)} %add_convert_fusion.3), channel_id=1, source_target_pairs={{0,1},{1,2},{2,3},{4,5},{5,6},{6,7},{8,9},{9,10},{10,11},{12,13},{... | collective-permute-start | bytes 1769480 | tf_op jit(solution)/shard_map/ppermute | solution.py:440
  74.1 23.0 %collective-permute-start.14 = (bf16[96,3072]{1,0:T(8,128)(2,1)S(1)}, bf16[96,3072]{1,0:T(8,128)(2,1)S(1)}, u32[]{:S(2)}, u32[]{:S(2)}) collective-permute-start(bf16[96,3072]{1,0:T(8,128)(2,1)S(1)} %add_convert_fusion.2), channel_id=1, source_target_pairs={{3,2},{2,1},{1,0},{7,6},{6,5},{5,4},{11,10},{10,9},{9,8},{15,14},{... | collective-permute-start | bytes 1769480 | tf_op jit(solution)/shard_map/ppermute | solution.py:441
  84.6 23.9 %collective-permute-start.16 = (bf16[96,3072]{1,0:T(8,128)(2,1)S(1)}, bf16[96,3072]{1,0:T(8,128)(2,1)S(1)}, u32[]{:S(2)}, u32[]{:S(2)}) collective-permute-start(bf16[96,3072]{1,0:T(8,128)(2,1)S(1)} %add_convert_fusion), channel_id=1, source_target_pairs={{3,2},{2,1},{1,0},{7,6},{6,5},{5,4},{11,10},{10,9},{9,8},{15,14},{... | collective-permute-start | bytes 1769480 | tf_op jit(solution)/shard_map/ppermute | solution.py:441
  86.7 21.8 %collective-permute-start.15 = (bf16[96,3072]{1,0:T(8,128)(2,1)S(1)}, bf16[96,3072]{1,0:T(8,128)(2,1)S(1)}, u32[]{:S(2)}, u32[]{:S(2)}) collective-permute-start(bf16[96,3072]{1,0:T(8,128)(2,1)S(1)} %add_convert_fusion.1), channel_id=1, source_target_pairs={{0,1},{1,2},{2,3},{4,5},{5,6},{6,7},{8,9},{9,10},{10,11},{12,13},{... | collective-permute-start | bytes 1769480 | tf_op jit(solution)/shard_map/ppermute | solution.py:440

commit v9 on v8

--- a/solution.py
+++ b/solution.py
@@ -36,7 +36,7 @@
     return slice(head * HD, (head + 1) * HD)
 
 
-def attend(query, keys, values, flags, write, lanes=0):
+def attend(query, keys, values, flags, write):
     rows, width = query.shape
     scale = LOG2E * HD ** (-0.5)
     lane = lax.broadcasted_iota(jnp.int32, (rows, LANES), 1)
@@ -64,7 +64,7 @@
             product = part_product if product is None else product + part_product
         total = jnp.where(total > 0.0, total, 1.0)
         write(columns, product * (1.0 / total))
-        packed = jnp.where(lane == lanes + head, top + jnp.log2(total), packed)
+        packed = jnp.where(lane == head, top + jnp.log2(total), packed)
     return packed
 
 
@@ -101,24 +101,25 @@
 
     @pl.when(here.span > 1)
     def _():
-        (early, _), (late, rest) = parts_of(here.rank, ranks, query.shape[0])
-        half = rest // 2
+        (early, _), (late, _) = parts_of(here.rank, ranks, query.shape[0])
+        starts = (early, late, pl.multiple_of(late + targets[1].shape[0], 16))
         copies = [
             copied(query.at[pl.ds(start, target.shape[0])], target, semaphores.at[index])
-            for index, (start, target) in enumerate(zip((early, late, pl.multiple_of(late + half, 16)), targets))
+            for index, (start, target) in enumerate(zip(starts, targets))
         ]
         for copy in copies:
             copy.wait()
 
 
-def local_kernel(spans, heads, facts, query, key, value, key_beside, value_beside, result, sums, *scratch):
+def local_kernel(spans, ranks, part, facts, query, key, value, key_beside, value_beside, result, sums, *scratch):
     here = Facts(facts, spans)
     query_, key_, value_, key_beside_, value_beside_, semaphores = scratch
-    columns = pl.ds(heads.start * HD, len(heads) * HD)
+    start, size = parts_of(here.rank, ranks, query.shape[0])[part]
     copies = [
-        copied(source.at[:, columns], target, semaphores.at[index])
+        copied(source, target, semaphores.at[index])
         for index, (source, target) in enumerate((
-            (query, query_), (key, key_), (key_beside, key_beside_), (value, value_), (value_beside, value_beside_),
+            (query.at[pl.ds(start, size)], query_),
+            (key, key_), (key_beside, key_beside_), (value, value_), (value_beside, value_beside_),
         ))
     ]
     for copy in copies:
@@ -128,7 +129,7 @@
         result[:, columns] = block
 
     flags = [None, here.sees(here.span, here.beside)]
-    sums[...] = attend(query_, [key_, key_beside_], [value_, value_beside_], flags, write, heads.start)
+    sums[...] = attend(query_, [key_, key_beside_], [value_, value_beside_], flags, write)
 
 
 def served_kernel(distance, spans, facts, key, value, key_beside, value_beside, *refs):
@@ -138,30 +139,29 @@
     def _():
         asker = jnp.minimum(here.span + distance, spans - 1)
         flags = [here.sees(asker, here.span), here.sees(asker, here.beside)]
-        *queries, result = refs
+        *queries, result, query = refs
         at = 0
-        for query in queries:
-            rows, width = query.shape
-            there = slice(at, at + rows)
-
-            def write(columns, block):
-                result[there, columns] = block.astype(jnp.bfloat16)
-
-            rest = attend(query, [key, key_beside], [value, value_beside], flags, write)
-            sent = jnp.zeros_like(rest)
-            for piece in range(3):
-                part = rest.astype(jnp.bfloat16).astype(jnp.float32)
-                sent = sent + (part if piece == 0 else pltpu.roll(part, piece * PIECE_LANES, 1))
-                rest = rest - part
-            result[there, width:] = sent.astype(jnp.bfloat16)
-            at += rows
-
-
-def merge(span, distances, own, own_sum, there, served, here, write):
-    width = served[0].shape[1] - LANES
-    sums = [own_sum[0][there, :] + own_sum[1][there, :]]
+        for part in queries:
+            query[at:at + part.shape[0], :] = part[...]
+            at += part.shape[0]
+
+        def write(columns, block):
+            result[:, columns] = block.astype(jnp.bfloat16)
+
+        rest = attend(query, [key, key_beside], [value, value_beside], flags, write)
+        sent = jnp.zeros_like(rest)
+        for piece in range(3):
+            part = rest.astype(jnp.bfloat16).astype(jnp.float32)
+            sent = sent + (part if piece == 0 else pltpu.roll(part, piece * PIECE_LANES, 1))
+            rest = rest - part
+        result[:, query.shape[1]:] = sent.astype(jnp.bfloat16)
+
+
+def merge(span, distances, own, own_sum, served, write):
+    width = own.shape[1]
+    sums = [own_sum[...]]
     for distance, ref in zip(distances, served):
-        sent = ref[here, width:].astype(jnp.float32)
+        sent = ref[:, width:].astype(jnp.float32)
         joined = sent
         for piece in (1, 2):
             joined = joined + pltpu.roll(sent, LANES - piece * PIECE_LANES, 1)
@@ -172,12 +172,9 @@
     shares = [share * over for share in shares]
     for head in range(width // HD):
         columns = head_columns(head)
-        split = own[0].shape[1]
-        mine = own[0][there, columns] if columns.stop <= split else (
-            own[1][there, columns.start - split:columns.stop - split])
-        merged = mine * shares[0][:, head:head + 1]
+        merged = own[:, columns] * shares[0][:, head:head + 1]
         for distance, share, ref in zip(distances, shares[1:], served):
-            away = jnp.where(span >= distance, ref[here, columns].astype(jnp.float32), 0.0)
+            away = jnp.where(span >= distance, ref[:, columns].astype(jnp.float32), 0.0)
             merged = merged + away * share[:, head:head + 1]
         write(columns, merged.astype(jnp.bfloat16))
 
@@ -191,20 +188,19 @@
 
 
 def opening_kernel(spans, ranks, distances, first, facts, *refs):
-    own, own_sum, served = refs[:2], refs[2:4], refs[4:4 + len(distances)]
-    weight, result, tiles, rows, semaphores = refs[4 + len(distances):]
+    own, own_sum, *served = refs[:2 + len(distances)]
+    weight, result, tiles, rows, semaphores = refs[2 + len(distances):]
     here = Facts(facts, spans)
     tile = tiles.shape[2]
 
     @pl.when(jnp.logical_or(here.rank == 0, here.rank == ranks - 1))
     def _():
         copies = streamed(weight, first, tiles, semaphores)
-        (start, size), _ = parts_of(here.rank, ranks, own[0].shape[0])
 
         def write(columns, part):
             rows[:, columns] = part
 
-        merge(here.span, distances, own, own_sum, pl.ds(start, size), served, slice(0, size), write)
+        merge(here.span, distances, own, own_sum, served, write)
         for index, copy in enumerate(copies):
             copy.wait()
             product = jnp.dot(rows[...], tiles[index], preferred_element_type=jnp.float32)
@@ -238,20 +234,18 @@
 
 
 def merged_blocks_kernel(spans, ranks, distances, facts, *refs):
-    count = len(distances)
-    own, own_sum, refs = refs[:2], refs[2:4], refs[4:]
-    early, late = refs[:count], refs[count:2 * count]
-    weight, attended, *results, tiles, semaphores = refs[2 * count:]
+    each = 2 + len(distances)
+    parts, (weight, attended, *results, tiles, semaphores) = (refs[:each], refs[each:2 * each]), refs[2 * each:]
     here = Facts(facts, spans)
     work = project_blocks(ranks, here, 1, attended, weight, results, tiles, semaphores)
     next(work)
-    for (start, size), served in zip(parts_of(here.rank, ranks, own[0].shape[0]), (early, late)):
+    for (start, size), (own, own_sum, *served) in zip(parts_of(here.rank, ranks, attended.shape[0]), parts):
         there = pl.ds(start, size)
 
         def write(columns, part):
             attended[there, columns] = part
 
-        merge(here.span, distances, own, own_sum, there, served, slice(0, size), write)
+        merge(here.span, distances, own, own_sum, served, write)
     for _ in work:
         pass
 
@@ -312,13 +306,12 @@
     place = jnp.where(numbers == 0, span, jnp.where(numbers == 1, rank, 0)).astype(jnp.int32)
     facts = jnp.concatenate([visible, place[None, :], levels[None, :]], axis=0)
 
+    third = (rows - block) // 48 * 16
     query_early, *query_late = pl.pallas_call(
         functools.partial(split_kernel, spans, ranks),
         in_specs=[SMEM, HBM],
         out_specs=[VMEM] * 3,
-        out_shape=[
-            jax.ShapeDtypeStruct((part, width), bf16) for part in (block, (rows - block) // 2, (rows - block) // 2)
-        ],
+        out_shape=[jax.ShapeDtypeStruct((part, width), bf16) for part in (block, rows - block - third, third)],
         scratch_shapes=[pltpu.SemaphoreType.DMA((3,))],
         compiler_params=PARAMS,
         cost_estimate=taking(1.7),
@@ -330,26 +323,22 @@
     key_beside = lax.ppermute(keys, "span", swap)
     value_beside = lax.ppermute(values, "span", swap)
 
-    def local(heads):
-        wide = len(heads) * HD
+    def after(value, *others):
+        return lax.optimization_barrier((value, others))[0]
+
+    def local(part, facts):
+        size = (block, rows - block)[part]
         return pl.pallas_call(
-            functools.partial(local_kernel, spans, heads),
+            functools.partial(local_kernel, spans, ranks, part),
             in_specs=[SMEM, HBM, HBM, HBM, ANY, ANY],
             out_specs=[VMEM] * 2,
-            out_shape=[jax.ShapeDtypeStruct((rows, wide), f32), jax.ShapeDtypeStruct((rows, LANES), f32)],
-            scratch_shapes=[pltpu.VMEM((rows, wide), bf16)] * 5 + [pltpu.SemaphoreType.DMA((5,))],
+            out_shape=[jax.ShapeDtypeStruct((size, width), f32), jax.ShapeDtypeStruct((size, LANES), f32)],
+            scratch_shapes=[pltpu.VMEM((size, width), bf16)] + [pltpu.VMEM((rows, width), bf16)] * 4
+            + [pltpu.SemaphoreType.DMA((5,))],
             compiler_params=PARAMS,
-            cost_estimate=taking(1.0 + 0.8 * len(heads)),
+            cost_estimate=taking(4.0),
             name="local",
         )(facts, in_hbm(queries), in_hbm(keys), in_hbm(values), key_beside, value_beside)
-
-    heads = width // HD
-    own, own_sum = local(range(heads // 3))
-    query_late, own_sum = lax.optimization_barrier((query_late, own_sum))
-    asked_late = [
-        [shifted(query, "span", -distance) for query in query_late] for distance in distances
-    ]
-    own, own_sum = zip((own, own_sum), local(range(heads // 3, heads)))
 
     def served(asked, distance):
         return pl.pallas_call(
@@ -357,18 +346,17 @@
             in_specs=[SMEM] + [VMEM] * (4 + len(asked)),
             out_specs=VMEM,
             out_shape=jax.ShapeDtypeStruct((sum(part.shape[0] for part in asked), width + LANES), bf16),
+            scratch_shapes=[pltpu.VMEM((sum(part.shape[0] for part in asked), width), bf16)],
             compiler_params=PARAMS,
             cost_estimate=taking(3.3),
             name="served",
         )(facts, keys, values, key_beside, value_beside, *asked)
 
-    asked_early, own_sum = lax.optimization_barrier((asked_early, list(own_sum)))
-    out_early = [served([q], d) for q, d in zip(asked_early, distances)]
-    back_early = [shifted(o, "span", d) for o, d in zip(out_early, distances)]
-    asked_late, out_early = lax.optimization_barrier((asked_late, out_early))
-    out_late = [served(q, d) for q, d in zip(asked_late, distances)]
-    back_early, out_late = lax.optimization_barrier((back_early, out_late))
-    back_late = [shifted(o, "span", d) for o, d in zip(out_late, distances)]
+    early = list(local(0, facts))
+    query_late = after(query_late, early)
+    asked_early = after(asked_early, early)
+    asked_late = [[shifted(query, "span", -distance) for query in query_late] for distance in distances]
+    early += [shifted(served([q], d), "span", d) for q, d in zip(asked_early, distances)]
 
     chunks = 2
     columns = model // chunks
@@ -377,10 +365,10 @@
     last = ranks - 1
     weight = in_hbm(out_weight)
 
-    def opening(chunk):
+    def opening(chunk, facts):
         return pl.pallas_call(
             functools.partial(opening_kernel, spans, ranks, distances, chunk * columns),
-            in_specs=[SMEM] + [VMEM] * (4 + len(distances)) + [HBM],
+            in_specs=[SMEM] + [VMEM] * (2 + len(distances)) + [HBM],
             out_specs=VMEM,
             out_shape=jax.ShapeDtypeStruct((block, columns), bf16),
             scratch_shapes=[
@@ -391,12 +379,17 @@
             compiler_params=PARAMS,
             cost_estimate=taking(3.4),
             name="opening",
-        )(facts, *own, *own_sum, *back_early, weight)
-
-    openings = [opening(chunk) for chunk in range(chunks)]
+        )(facts, *early, weight)
+
     ends = [(0, 1), (last, last - 1)]
-    arrived = [[lax.ppermute(sent, "tensor", ends)] for sent in openings]
-    back_late, openings = lax.optimization_barrier((back_late, openings))
+    sent = opening(0, facts)
+    arrived = [[lax.ppermute(sent, "tensor", ends)]]
+    out_late = [served(q, d) for q, d in zip(after(asked_late, sent), distances)]
+    late = list(local(1, after(facts, out_late)))
+    for chunk in range(1, chunks):
+        sent = opening(chunk, after(facts, late))
+        arrived.append([lax.ppermute(sent, "tensor", ends)])
+    late += after([shifted(o, "span", d) for o, d in zip(out_late, distances)], sent)
 
     streaming = dict(
         scratch_shapes=[
@@ -414,7 +407,7 @@
         cost_estimate=taking(6.0),
         name="merged_blocks",
         **streaming,
-    )(facts, *own, *own_sum, *back_early, *back_late, weight)
+    )(facts, *early, *late, weight)
 
     before = attended
     for step in range(1, last):

time: 112 us -> 110 us (0.982)
  the two profiles are of different devices: /device:TPU:18 before, /device:TPU:16 now
where the time goes in v9:
time: 110 us; the launch traced here: 109 us
  Pallas kernels  39 us (35%)
  waiting for transfers between devices  33.2 us (30%)
  starting transfers between devices  30.7 us (28%)
  other arithmetic  2.77 us (3%)
  between operations  2.36 us (2%)
    ppermute x4, waiting for transfers between devices, body(): lax.ppermute(down, 'tensor', [(last - i, last - i - 1) for i in range(ste...  20.4 us
    ppermute x4, starting transfers between devices, body(): lax.ppermute(down, 'tensor', [(last - i, last - i - 1) for i in range(ste...  12.3 us
    pallas_call x2, Pallas kernels, local(): pl.pallas_call(functools.partial(local_kernel, spans, ranks, part), in_sp...  9.16 us
    ppermute x4, starting transfers between devices, body(): lax.ppermute(up, 'tensor', [(i, i + 1) for i in range(step + 1)])  8.46 us
    pallas_call x1, Pallas kernels, body(): pl.pallas_call(functools.partial(blocks_kernel, spans, ranks, step), in_s...  7.35 us
    pallas_call x2, Pallas kernels, served(): pl.pallas_call(functools.partial(served_kernel, distance, spans), in_spec...  7.3 us
    ppermute x1, waiting for transfers between devices, body(): arrived.append([lax.ppermute(sent, 'tensor', ends)])  7.24 us
    ppermute x5, starting transfers between devices, shifted(): lax.ppermute(block, axis, [(i, i + distance) for i in range(count) if 0 <...  6.62 us
  transfers between devices with their start and end apart: 17, of which 9 were waited for; matrix products, arithmetic and copies ran while one was open for 3% of the time, Pallas kernels for 33%

profile of v9, /device:TPU:16, one launch (start us, length us, event | category | flops | bytes accessed | tf_op | source)
XLA Modules:
  0.0 109.0 jit_solution(3586422403626917804)
XLA Ops:
  0.0 0.5 collective-permute-start.1
  0.5 0.7 pad_add_fusion.facts
  1.2 0.6 split.1
  1.9 0.0 copy-start
  1.9 1.4 %collective-permute-start.2 = (bf16[96,768]{1,0:T(8,128)(2,1)S(1)}, bf16[96,768]{1,0:T(8,128)(2,1)S(1)}, u32[]{:S(2)}, u32[]{:S(2)}) collective-permute-start(bf16[96,768]{1,0:T(8,128)(2,1)S(1)} %get-tuple-element.51), channel_id=1, source_target_pairs={{8,0},{12,4},{9,1},{13,5},{10,2},{14,6},{11,3},{15,7},{24,16},{28,... | collective-permute-start | bytes 442376 | tf_op jit(solution)/shard_map/ppermute | solution.py:32
  3.3 4.1 %local.2 = (f32[96,768]{1,0:T(8,128)S(1)}, f32[96,128]{1,0:T(8,128)S(1)}) custom-call(s32[6,4]{1,0:T(8,128)S(1)} %pad_add_fusion.facts, bf16[384,768]{1,0:T(8,128)(2,1)} %query.5, bf16[384,768]{1,0:T(8,128)(2,1)} %key.7, bf16[384,768]{1,0:T(8,128)(2,1)} %value.7, bf16[384,768]{1,0:T(8,128)(2,1)S(1)} %collective-permute-done.key_beside, ...), custom_call_target="tpu_custom_call" | custom-call | bytes 14760000 | tf_op jit(solution)/shard_map/local/pallas_call | solution.py:331
  7.4 1.3 %collective-permute-start.4 = (bf16[192,768]{1,0:T(8,128)(2,1)S(1)}, bf16[192,768]{1,0:T(8,128)(2,1)S(1)}, u32[]{:S(2)}, u32[]{:S(2)}) collective-permute-start(bf16[192,768]{1,0:T(8,128)(2,1)S(1)} %get-tuple-element.55), channel_id=1, source_target_pairs={{8,0},{12,4},{9,1},{13,5},{10,2},{14,6},{11,3},{15,7},{24,16},{28,... | collective-permute-start | bytes 884744 | tf_op jit(solution)/shard_map/ppermute | solution.py:32
  8.7 1.2 %collective-permute-done.2.refs_0_ = bf16[96,768]{1,0:T(8,128)(2,1)S(1)} collective-permute-done((bf16[96,768]{1,0:T(8,128)(2,1)S(1)}, bf16[96,768]{1,0:T(8,128)(2,1)S(1)}, u32[]{:S(2)}, u32[]{:S(2)}) %collective-permute-start.2) | collective-permute-done | bytes 147488 | tf_op jit(solution)/shard_map/ppermute | solution.py:32
  9.9 2.8 %served.2 = bf16[96,896]{1,0:T(8,128)(2,1)S(1)} custom-call(s32[6,4]{1,0:T(8,128)S(1)} %pad_add_fusion.facts, bf16[384,768]{1,0:T(8,128)(2,1)S(1)} %copy-done, bf16[384,768]{1,0:T(8,128)(2,1)S(1)} %copy-done.1, bf16[384,768]{1,0:T(8,128)(2,1)S(1)} %collective-permute-done.key_beside, bf16[384,768]{1,0:T(8,128)(2,1)S(1)} %collective-permute-done.1.value_beside, ...), custom_call_target="tpu_custom_call" | custom-call | bytes 12177000 | tf_op jit(solution)/shard_map/served/pallas_call | solution.py:344
  12.7 1.3 %collective-permute-start.3 = (bf16[96,896]{1,0:T(8,128)(2,1)S(1)}, bf16[96,896]{1,0:T(8,128)(2,1)S(1)}, u32[]{:S(2)}, u32[]{:S(2)}) collective-permute-start(bf16[96,896]{1,0:T(8,128)(2,1)S(1)} %served.2), channel_id=1, source_target_pairs={{0,8},{4,12},{1,9},{5,13},{2,10},{6,14},{3,11},{7,15},{16,24},{20,... | collective-permute-start | bytes 516104 | tf_op jit(solution)/shard_map/ppermute | solution.py:32
  14.0 1.3 %collective-permute-start.5 = (bf16[96,768]{1,0:T(8,128)(2,1)S(1)}, bf16[96,768]{1,0:T(8,128)(2,1)S(1)}, u32[]{:S(2)}, u32[]{:S(2)}) collective-permute-start(bf16[96,768]{1,0:T(8,128)(2,1)S(1)} %get-tuple-element.56), channel_id=1, source_target_pairs={{8,0},{12,4},{9,1},{13,5},{10,2},{14,6},{11,3},{15,7},{24,16},{28,... | collective-permute-start | bytes 442376 | tf_op jit(solution)/shard_map/ppermute | solution.py:32
  15.3 2.4 %collective-permute-done.3.refs_2_ = bf16[96,896]{1,0:T(8,128)(2,1)S(1)} collective-permute-done((bf16[96,896]{1,0:T(8,128)(2,1)S(1)}, bf16[96,896]{1,0:T(8,128)(2,1)S(1)}, u32[]{:S(2)}, u32[]{:S(2)}) %collective-permute-start.3) | collective-permute-done | bytes 172064 | tf_op jit(solution)/shard_map/ppermute | solution.py:32
  17.7 0.6 opening.2
  18.3 0.0 copy-start.2
  18.3 1.3 %collective-permute-start.8 = (bf16[96,3072]{1,0:T(8,128)(2,1)S(1)}, bf16[96,3072]{1,0:T(8,128)(2,1)S(1)}, u32[]{:S(2)}, u32[]{:S(2)}) collective-permute-start(bf16[96,3072]{1,0:T(8,128)(2,1)S(1)} %opening.2), channel_id=1, source_target_pairs={{0,1},{3,2},{4,5},{7,6},{8,9},{11,10},{12,13},{15,14},{16,17},{19,... | collective-permute-start | bytes 1769480 | tf_op jit(solution)/shard_map/ppermute | solution.py:386
  19.6 2.0 %collective-permute-done.5.refs_1_ = bf16[96,768]{1,0:T(8,128)(2,1)S(1)} collective-permute-done((bf16[96,768]{1,0:T(8,128)(2,1)S(1)}, bf16[96,768]{1,0:T(8,128)(2,1)S(1)}, u32[]{:S(2)}, u32[]{:S(2)}) %collective-permute-start.5) | collective-permute-done | bytes 147488 | tf_op jit(solution)/shard_map/ppermute | solution.py:32
  21.6 4.5 %served.3 = bf16[288,896]{1,0:T(8,128)(2,1)} custom-call(s32[6,4]{1,0:T(8,128)S(1)} %pad_add_fusion.facts, bf16[384,768]{1,0:T(8,128)(2,1)S(1)} %copy-done, bf16[384,768]{1,0:T(8,128)(2,1)S(1)} %copy-done.1, bf16[384,768]{1,0:T(8,128)(2,1)S(1)} %collective-permute-done.key_beside, bf16[384,768]{1,0:T(8,128)(2,1)S(1)} %collective-permute-done.1.value_beside, ...), custom_call_target="tpu_custom_call" | custom-call | bytes 12177000 | tf_op jit(solution)/shard_map/served/pallas_call | solution.py:344
  26.1 1.3 %collective-permute-start.6 = (bf16[288,896]{1,0:T(8,128)(2,1)}, bf16[288,896]{1,0:T(8,128)(2,1)S(1)}, u32[]{:S(2)}, u32[]{:S(2)}) collective-permute-start(bf16[288,896]{1,0:T(8,128)(2,1)} %served.3), channel_id=1, source_target_pairs={{0,8},{4,12},{1,9},{5,13},{2,10},{6,14},{3,11},{7,15},{16,24},{20,... | collective-permute-start | bytes 1548296 | tf_op jit(solution)/shard_map/ppermute | solution.py:32
  27.4 0.6 fusion.4
  30.0 0.9 constant_dynamic-slice_fusion
  30.9 5.1 %local.3 = (f32[288,768]{1,0:T(8,128)S(1)}, f32[288,128]{1,0:T(8,128)S(1)}) custom-call(s32[6,4]{1,0:T(8,128)S(1)} %pad_add_fusion.facts, bf16[384,768]{1,0:T(8,128)(2,1)} %query.5, bf16[384,768]{1,0:T(8,128)(2,1)} %key.7, bf16[384,768]{1,0:T(8,128)(2,1)} %value.7, bf16[384,768]{1,0:T(8,128)(2,1)S(1)} %collective-permute-done.key_beside, ...), custom_call_target="tpu_custom_call" | custom-call | bytes 14760000 | tf_op jit(solution)/shard_map/local/pallas_call | solution.py:331
  36.0 0.6 opening.3
  36.6 1.5 %collective-permute-start.7 = (bf16[96,3072]{1,0:T(8,128)(2,1)S(1)}, bf16[96,3072]{1,0:T(8,128)(2,1)S(1)}, u32[]{:S(2)}, u32[]{:S(2)}) collective-permute-start(bf16[96,3072]{1,0:T(8,128)(2,1)S(1)} %opening.3), channel_id=1, source_target_pairs={{0,1},{3,2},{4,5},{7,6},{8,9},{11,10},{12,13},{15,14},{16,17},{19,... | collective-permute-start | bytes 1769480 | tf_op jit(solution)/shard_map/ppermute | solution.py:391
  38.1 0.1 collective-permute-done.6.refs_5_
  38.2 5.7 %merged_blocks.1 = (bf16[384,768]{1,0:T(8,128)(2,1)S(1)}, bf16[96,3072]{1,0:T(8,128)(2,1)S(1)}, bf16[96,3072]{1,0:T(8,128)(2,1)S(1)}, bf16[96,3072]{1,0:T(8,128)(2,1)S(1)}, bf16[96,3072]{1,0:T(8,128)(2,1)S(1)}) custom-call(s32[6,4]{1,0:T(8,128)S(1)} %pad_add_fusion.facts, f32[96,768]{1,0:T(8,128)S(1)} %get-tuple-element.49.refs_0_, ...), custom_call_target="tpu_custom_call" | custom-call | bytes 22140000 | tf_op jit(solution)/shard_map/merged_blocks/pallas_call | solution.py:402
  43.9 0.3 fusion.1
  44.2 1.3 %collective-permute-start.11 = (bf16[96,3072]{1,0:T(8,128)(2,1)S(1)}, bf16[96,3072]{1,0:T(8,128)(2,1)S(1)}, u32[]{:S(2)}, u32[]{:S(2)}) collective-permute-start(bf16[96,3072]{1,0:T(8,128)(2,1)S(1)} %get-tuple-element.96), channel_id=1, source_target_pairs={{0,1},{1,2},{4,5},{5,6},{8,9},{9,10},{12,13},{13,14},{16,17},{17,1... | collective-permute-start | bytes 1769480 | tf_op jit(solution)/shard_map/ppermute | solution.py:433
  45.5 4.6 %collective-permute-start.12 = (bf16[96,3072]{1,0:T(8,128)(2,1)S(1)}, bf16[96,3072]{1,0:T(8,128)(2,1)S(1)}, u32[]{:S(2)}, u32[]{:S(2)}) collective-permute-start(bf16[96,3072]{1,0:T(8,128)(2,1)S(1)} %get-tuple-element.95), channel_id=1, source_target_pairs={{3,2},{2,1},{7,6},{6,5},{11,10},{10,9},{15,14},{14,13},{19,18},{18... | collective-permute-start | bytes 1769480 | tf_op jit(solution)/shard_map/ppermute | solution.py:434
  50.1 7.2 %collective-permute-done.7 = bf16[96,3072]{1,0:T(8,128)(2,1)S(1)} collective-permute-done((bf16[96,3072]{1,0:T(8,128)(2,1)S(1)}, bf16[96,3072]{1,0:T(8,128)(2,1)S(1)}, u32[]{:S(2)}, u32[]{:S(2)}) %collective-permute-start.7) | collective-permute-done | bytes 589856 | tf_op jit(solution)/shard_map/ppermute | solution.py:391
  57.3 0.3 fusion.3
  57.6 1.9 %collective-permute-start.10 = (bf16[96,3072]{1,0:T(8,128)(2,1)S(1)}, bf16[96,3072]{1,0:T(8,128)(2,1)S(1)}, u32[]{:S(2)}, u32[]{:S(2)}) collective-permute-start(bf16[96,3072]{1,0:T(8,128)(2,1)S(1)} %get-tuple-element.93), channel_id=1, source_target_pairs={{3,2},{2,1},{7,6},{6,5},{11,10},{10,9},{15,14},{14,13},{19,18},{18... | collective-permute-start | bytes 1769480 | tf_op jit(solution)/shard_map/ppermute | solution.py:434
  59.6 1.3 %collective-permute-start.9 = (bf16[96,3072]{1,0:T(8,128)(2,1)S(1)}, bf16[96,3072]{1,0:T(8,128)(2,1)S(1)}, u32[]{:S(2)}, u32[]{:S(2)}) collective-permute-start(bf16[96,3072]{1,0:T(8,128)(2,1)S(1)} %get-tuple-element.94), channel_id=1, source_target_pairs={{0,1},{1,2},{4,5},{5,6},{8,9},{9,10},{12,13},{13,14},{16,17},{17,1... | collective-permute-start | bytes 1769480 | tf_op jit(solution)/shard_map/ppermute | solution.py:433
  60.9 7.4 %blocks.1 = (bf16[96,3072]{1,0:T(8,128)(2,1)S(1)}, bf16[96,3072]{1,0:T(8,128)(2,1)S(1)}, bf16[96,3072]{1,0:T(8,128)(2,1)S(1)}, bf16[96,3072]{1,0:T(8,128)(2,1)S(1)}) custom-call(s32[6,4]{1,0:T(8,128)S(1)} %pad_add_fusion.facts, bf16[384,768]{1,0:T(8,128)(2,1)S(1)} %get-tuple-element.92.attended, bf16[768,6144]{1,0:T(8,128)(2,1)} %weight.3), custom_call_target="tpu_custom_call" | custom-call | bytes 18450000 | tf_op jit(solution)/shard_map/blocks/pallas_call | solution.py:416
  68.2 1.7 %collective-permute-done.12 = bf16[96,3072]{1,0:T(8,128)(2,1)S(1)} collective-permute-done((bf16[96,3072]{1,0:T(8,128)(2,1)S(1)}, bf16[96,3072]{1,0:T(8,128)(2,1)S(1)}, u32[]{:S(2)}, u32[]{:S(2)}) %collective-permute-start.12) | collective-permute-done | bytes 589856 | tf_op jit(solution)/shard_map/ppermute | solution.py:434
  70.0 0.1 add_convert_fusion.3
  70.1 1.9 %collective-permute-start.13 = (bf16[96,3072]{1,0:T(8,128)(2,1)S(1)}, bf16[96,3072]{1,0:T(8,128)(2,1)S(1)}, u32[]{:S(2)}, u32[]{:S(2)}) collective-permute-start(bf16[96,3072]{1,0:T(8,128)(2,1)S(1)} %add_convert_fusion.3), channel_id=1, source_target_pairs={{0,1},{1,2},{2,3},{4,5},{5,6},{6,7},{8,9},{9,10},{10,11},{12,13},{... | collective-permute-start | bytes 1769480 | tf_op jit(solution)/shard_map/ppermute | solution.py:433
  72.1 0.1 add_convert_fusion.2
  72.2 3.9 %collective-permute-start.14 = (bf16[96,3072]{1,0:T(8,128)(2,1)S(1)}, bf16[96,3072]{1,0:T(8,128)(2,1)S(1)}, u32[]{:S(2)}, u32[]{:S(2)}) collective-permute-start(bf16[96,3072]{1,0:T(8,128)(2,1)S(1)} %add_convert_fusion.2), channel_id=1, source_target_pairs={{3,2},{2,1},{1,0},{7,6},{6,5},{5,4},{11,10},{10,9},{9,8},{15,14},{... | collective-permute-start | bytes 1769480 | tf_op jit(solution)/shard_map/ppermute | solution.py:434
  76.1 6.5 %collective-permute-done.10 = bf16[96,3072]{1,0:T(8,128)(2,1)S(1)} collective-permute-done((bf16[96,3072]{1,0:T(8,128)(2,1)S(1)}, bf16[96,3072]{1,0:T(8,128)(2,1)S(1)}, u32[]{:S(2)}, u32[]{:S(2)}) %collective-permute-start.10) | collective-permute-done | bytes 589856 | tf_op jit(solution)/shard_map/ppermute | solution.py:434
  82.6 0.1 add_convert_fusion
  82.8 1.9 %collective-permute-start.16 = (bf16[96,3072]{1,0:T(8,128)(2,1)S(1)}, bf16[96,3072]{1,0:T(8,128)(2,1)S(1)}, u32[]{:S(2)}, u32[]{:S(2)}) collective-permute-start(bf16[96,3072]{1,0:T(8,128)(2,1)S(1)} %add_convert_fusion), channel_id=1, source_target_pairs={{3,2},{2,1},{1,0},{7,6},{6,5},{5,4},{11,10},{10,9},{9,8},{15,14},{... | collective-permute-start | bytes 1769480 | tf_op jit(solution)/shard_map/ppermute | solution.py:434
  84.7 0.1 add_convert_fusion.1
  84.9 4.0 %collective-permute-start.15 = (bf16[96,3072]{1,0:T(8,128)(2,1)S(1)}, bf16[96,3072]{1,0:T(8,128)(2,1)S(1)}, u32[]{:S(2)}, u32[]{:S(2)}) collective-permute-start(bf16[96,3072]{1,0:T(8,128)(2,1)S(1)} %add_convert_fusion.1), channel_id=1, source_target_pairs={{0,1},{1,2},{2,3},{4,5},{5,6},{6,7},{8,9},{9,10},{10,11},{12,13},{... | collective-permute-start | bytes 1769480 | tf_op jit(solution)/shard_map/ppermute | solution.py:433
  88.8 4.9 %own.1.projected = bf16[96,6144]{1,0:T(8,128)(2,1)S(1)} custom-call(s32[6,4]{1,0:T(8,128)S(1)} %pad_add_fusion.facts, bf16[384,768]{1,0:T(8,128)(2,1)S(1)} %get-tuple-element.92.attended, bf16[768,6144]{1,0:T(8,128)(2,1)} %weight.3), custom_call_target="tpu_custom_call" | custom-call | bytes 18450000 | tf_op jit(solution)/shard_map/own/pallas_call | solution.py:437
  93.8 1.5 %collective-permute-done.14 = bf16[96,3072]{1,0:T(8,128)(2,1)S(1)} collective-permute-done((bf16[96,3072]{1,0:T(8,128)(2,1)S(1)}, bf16[96,3072]{1,0:T(8,128)(2,1)S(1)}, u32[]{:S(2)}, u32[]{:S(2)}) %collective-permute-start.14) | collective-permute-done | bytes 589856 | tf_op jit(solution)/shard_map/ppermute | solution.py:434
  95.3 0.3 multiply_convert_fusion.done
  95.5 10.7 %collective-permute-done.16.down = bf16[96,3072]{1,0:T(8,128)(2,1)S(1)} collective-permute-done((bf16[96,3072]{1,0:T(8,128)(2,1)S(1)}, bf16[96,3072]{1,0:T(8,128)(2,1)S(1)}, u32[]{:S(2)}, u32[]{:S(2)}) %collective-permute-start.16) | collective-permute-done | bytes 589856 | tf_op jit(solution)/shard_map/ppermute | solution.py:434
  106.2 2.7 %final.1 = bf16[96,6144]{1,0:T(8,128)(2,1)} custom-call(s32[6,4]{1,0:T(8,128)S(1)} %pad_add_fusion.facts, bf16[96,3072]{1,0:T(8,128)(2,1)S(1)} %multiply_convert_fusion.done, bf16[96,6144]{1,0:T(8,128)(2,1)S(1)} %own.1.projected, f32[64,6144]{1,0:T(8,128)} %gate_table.1, bf16[96,3072]{1,0:T(8,128)(2,1)S(1)} %collective-permute-done.15.up, ...), custom_call_target="tpu_custom_call" | custom-call | bytes 9963000 | tf_op jit(solution)/shard_map/final/pallas_call | solution.py:454
  (14 shorter events, 0.0 us)
Async XLA Ops:
  0.0 3.3 %collective-permute-start = (bf16[384,768]{1,0:T(8,128)(2,1)}, bf16[384,768]{1,0:T(8,128)(2,1)S(1)}, u32[]{:S(2)}, u32[]{:S(2)}) collective-permute-start(bf16[384,768]{1,0:T(8,128)(2,1)} %key.7), channel_id=1, source_target_pairs={{0,4},{4,0},{8,12},{12,8},{1,5},{5,1},{9,13},{13,9},{2,6},{6,2},{1... | collective-permute-start | bytes 1769480 | tf_op jit(solution)/shard_map/ppermute | solution.py:323
  0.0 3.3 %collective-permute-start.1 = (bf16[384,768]{1,0:T(8,128)(2,1)}, bf16[384,768]{1,0:T(8,128)(2,1)S(1)}, u32[]{:S(2)}, u32[]{:S(2)}) collective-permute-start(bf16[384,768]{1,0:T(8,128)(2,1)} %value.7), channel_id=1, source_target_pairs={{0,4},{4,0},{8,12},{12,8},{1,5},{5,1},{9,13},{13,9},{2,6},{6,2},{1... | collective-permute-start | bytes 1769480 | tf_op jit(solution)/shard_map/ppermute | solution.py:324
  1.9 8.0 %copy-start = (bf16[384,768]{1,0:T(8,128)(2,1)S(1)}, bf16[384,768]{1,0:T(8,128)(2,1)}, u32[]{:S(2)}) copy-start(bf16[384,768]{1,0:T(8,128)(2,1)} %key.7) | copy-start | bytes 1769476
  1.9 8.0 %copy-start.1 = (bf16[384,768]{1,0:T(8,128)(2,1)S(1)}, bf16[384,768]{1,0:T(8,128)(2,1)}, u32[]{:S(2)}) copy-start(bf16[384,768]{1,0:T(8,128)(2,1)} %value.7) | copy-start | bytes 1769476
  1.9 8.0 %collective-permute-start.2 = (bf16[96,768]{1,0:T(8,128)(2,1)S(1)}, bf16[96,768]{1,0:T(8,128)(2,1)S(1)}, u32[]{:S(2)}, u32[]{:S(2)}) collective-permute-start(bf16[96,768]{1,0:T(8,128)(2,1)S(1)} %get-tuple-element.51), channel_id=1, source_target_pairs={{8,0},{12,4},{9,1},{13,5},{10,2},{14,6},{11,3},{15,7},{24,16},{28,... | collective-permute-start | bytes 442376 | tf_op jit(solution)/shard_map/ppermute | solution.py:32
  7.4 14.2 %collective-permute-start.4 = (bf16[192,768]{1,0:T(8,128)(2,1)S(1)}, bf16[192,768]{1,0:T(8,128)(2,1)S(1)}, u32[]{:S(2)}, u32[]{:S(2)}) collective-permute-start(bf16[192,768]{1,0:T(8,128)(2,1)S(1)} %get-tuple-element.55), channel_id=1, source_target_pairs={{8,0},{12,4},{9,1},{13,5},{10,2},{14,6},{11,3},{15,7},{24,16},{28,... | collective-permute-start | bytes 884744 | tf_op jit(solution)/shard_map/ppermute | solution.py:32
  12.7 5.0 %collective-permute-start.3 = (bf16[96,896]{1,0:T(8,128)(2,1)S(1)}, bf16[96,896]{1,0:T(8,128)(2,1)S(1)}, u32[]{:S(2)}, u32[]{:S(2)}) collective-permute-start(bf16[96,896]{1,0:T(8,128)(2,1)S(1)} %served.2), channel_id=1, source_target_pairs={{0,8},{4,12},{1,9},{5,13},{2,10},{6,14},{3,11},{7,15},{16,24},{20,... | collective-permute-start | bytes 516104 | tf_op jit(solution)/shard_map/ppermute | solution.py:32
  14.0 7.6 %collective-permute-start.5 = (bf16[96,768]{1,0:T(8,128)(2,1)S(1)}, bf16[96,768]{1,0:T(8,128)(2,1)S(1)}, u32[]{:S(2)}, u32[]{:S(2)}) collective-permute-start(bf16[96,768]{1,0:T(8,128)(2,1)S(1)} %get-tuple-element.56), channel_id=1, source_target_pairs={{8,0},{12,4},{9,1},{13,5},{10,2},{14,6},{11,3},{15,7},{24,16},{28,... | collective-permute-start | bytes 442376 | tf_op jit(solution)/shard_map/ppermute | solution.py:32
  18.3 9.1 %copy-start.2 = (s32[4]{0:T(128)S(1)}, s32[4]{0:T(128)}, u32[]{:S(2)}) copy-start(s32[4]{0:T(128)} %param.12) | copy-start | bytes 52
  18.3 25.6 %collective-permute-start.8 = (bf16[96,3072]{1,0:T(8,128)(2,1)S(1)}, bf16[96,3072]{1,0:T(8,128)(2,1)S(1)}, u32[]{:S(2)}, u32[]{:S(2)}) collective-permute-start(bf16[96,3072]{1,0:T(8,128)(2,1)S(1)} %opening.2), channel_id=1, source_target_pairs={{0,1},{3,2},{4,5},{7,6},{8,9},{11,10},{12,13},{15,14},{16,17},{19,... | collective-permute-start | bytes 1769480 | tf_op jit(solution)/shard_map/ppermute | solution.py:386
  26.1 12.1 %collective-permute-start.6 = (bf16[288,896]{1,0:T(8,128)(2,1)}, bf16[288,896]{1,0:T(8,128)(2,1)S(1)}, u32[]{:S(2)}, u32[]{:S(2)}) collective-permute-start(bf16[288,896]{1,0:T(8,128)(2,1)} %served.3), channel_id=1, source_target_pairs={{0,8},{4,12},{1,9},{5,13},{2,10},{6,14},{3,11},{7,15},{16,24},{20,... | collective-permute-start | bytes 1548296 | tf_op jit(solution)/shard_map/ppermute | solution.py:32
  36.6 20.7 %collective-permute-start.7 = (bf16[96,3072]{1,0:T(8,128)(2,1)S(1)}, bf16[96,3072]{1,0:T(8,128)(2,1)S(1)}, u32[]{:S(2)}, u32[]{:S(2)}) collective-permute-start(bf16[96,3072]{1,0:T(8,128)(2,1)S(1)} %opening.3), channel_id=1, source_target_pairs={{0,1},{3,2},{4,5},{7,6},{8,9},{11,10},{12,13},{15,14},{16,17},{19,... | collective-permute-start | bytes 1769480 | tf_op jit(solution)/shard_map/ppermute | solution.py:391
  44.2 24.0 %collective-permute-start.11 = (bf16[96,3072]{1,0:T(8,128)(2,1)S(1)}, bf16[96,3072]{1,0:T(8,128)(2,1)S(1)}, u32[]{:S(2)}, u32[]{:S(2)}) collective-permute-start(bf16[96,3072]{1,0:T(8,128)(2,1)S(1)} %get-tuple-element.96), channel_id=1, source_target_pairs={{0,1},{1,2},{4,5},{5,6},{8,9},{9,10},{12,13},{13,14},{16,17},{17,1... | collective-permute-start | bytes 1769480 | tf_op jit(solution)/shard_map/ppermute | solution.py:433
  45.5 24.4 %collective-permute-start.12 = (bf16[96,3072]{1,0:T(8,128)(2,1)S(1)}, bf16[96,3072]{1,0:T(8,128)(2,1)S(1)}, u32[]{:S(2)}, u32[]{:S(2)}) collective-permute-start(bf16[96,3072]{1,0:T(8,128)(2,1)S(1)} %get-tuple-element.95), channel_id=1, source_target_pairs={{3,2},{2,1},{7,6},{6,5},{11,10},{10,9},{15,14},{14,13},{19,18},{18... | collective-permute-start | bytes 1769480 | tf_op jit(solution)/shard_map/ppermute | solution.py:434
  57.6 25.0 %collective-permute-start.10 = (bf16[96,3072]{1,0:T(8,128)(2,1)S(1)}, bf16[96,3072]{1,0:T(8,128)(2,1)S(1)}, u32[]{:S(2)}, u32[]{:S(2)}) collective-permute-start(bf16[96,3072]{1,0:T(8,128)(2,1)S(1)} %get-tuple-element.93), channel_id=1, source_target_pairs={{3,2},{2,1},{7,6},{6,5},{11,10},{10,9},{15,14},{14,13},{19,18},{18... | collective-permute-start | bytes 1769480 | tf_op jit(solution)/shard_map/ppermute | solution.py:434
  59.6 23.1 %collective-permute-start.9 = (bf16[96,3072]{1,0:T(8,128)(2,1)S(1)}, bf16[96,3072]{1,0:T(8,128)(2,1)S(1)}, u32[]{:S(2)}, u32[]{:S(2)}) collective-permute-start(bf16[96,3072]{1,0:T(8,128)(2,1)S(1)} %get-tuple-element.94), channel_id=1, source_target_pairs={{0,1},{1,2},{4,5},{5,6},{8,9},{9,10},{12,13},{13,14},{16,17},{17,1... | collective-permute-start | bytes 1769480 | tf_op jit(solution)/shard_map/ppermute | solution.py:433
  70.1 23.6 %collective-permute-start.13 = (bf16[96,3072]{1,0:T(8,128)(2,1)S(1)}, bf16[96,3072]{1,0:T(8,128)(2,1)S(1)}, u32[]{:S(2)}, u32[]{:S(2)}) collective-permute-start(bf16[96,3072]{1,0:T(8,128)(2,1)S(1)} %add_convert_fusion.3), channel_id=1, source_target_pairs={{0,1},{1,2},{2,3},{4,5},{5,6},{6,7},{8,9},{9,10},{10,11},{12,13},{... | collective-permute-start | bytes 1769480 | tf_op jit(solution)/shard_map/ppermute | solution.py:433
  72.2 23.0 %collective-permute-start.14 = (bf16[96,3072]{1,0:T(8,128)(2,1)S(1)}, bf16[96,3072]{1,0:T(8,128)(2,1)S(1)}, u32[]{:S(2)}, u32[]{:S(2)}) collective-permute-start(bf16[96,3072]{1,0:T(8,128)(2,1)S(1)} %add_convert_fusion.2), channel_id=1, source_target_pairs={{3,2},{2,1},{1,0},{7,6},{6,5},{5,4},{11,10},{10,9},{9,8},{15,14},{... | collective-permute-start | bytes 1769480 | tf_op jit(solution)/shard_map/ppermute | solution.py:434
  82.8 23.4 %collective-permute-start.16 = (bf16[96,3072]{1,0:T(8,128)(2,1)S(1)}, bf16[96,3072]{1,0:T(8,128)(2,1)S(1)}, u32[]{:S(2)}, u32[]{:S(2)}) collective-permute-start(bf16[96,3072]{1,0:T(8,128)(2,1)S(1)} %add_convert_fusion), channel_id=1, source_target_pairs={{3,2},{2,1},{1,0},{7,6},{6,5},{5,4},{11,10},{10,9},{9,8},{15,14},{... | collective-permute-start | bytes 1769480 | tf_op jit(solution)/shard_map/ppermute | solution.py:434
  84.9 21.3 %collective-permute-start.15 = (bf16[96,3072]{1,0:T(8,128)(2,1)S(1)}, bf16[96,3072]{1,0:T(8,128)(2,1)S(1)}, u32[]{:S(2)}, u32[]{:S(2)}) collective-permute-start(bf16[96,3072]{1,0:T(8,128)(2,1)S(1)} %add_convert_fusion.1), channel_id=1, source_target_pairs={{0,1},{1,2},{2,3},{4,5},{5,6},{6,7},{8,9},{9,10},{10,11},{12,13},{... | collective-permute-start | bytes 1769480 | tf_op jit(solution)/shard_map/ppermute | solution.py:433

commit v10 on v9

--- a/solution.py
+++ b/solution.py
@@ -52,18 +52,15 @@
         top = functools.reduce(
             jnp.maximum, [one if flag is None else jnp.where(flag, one, HIDDEN) for one, flag in zip(tops, flags)]
         )
-        total, product = None, None
+        joined = None
         for block, value, flag in zip(scores, values, flags):
             above = top if flag is None else jnp.where(flag, top, -HIDDEN)
-            probs = jnp.exp2(block * scale - above)
-            part = jnp.sum(probs, axis=-1, keepdims=True)
-            part_product = jnp.dot(
-                probs.astype(jnp.bfloat16), value[:, columns], preferred_element_type=jnp.float32
-            )
-            total = part if total is None else total + part
-            product = part_product if product is None else product + part_product
-        total = jnp.where(total > 0.0, total, 1.0)
-        write(columns, product * (1.0 / total))
+            probs = jnp.exp2(block * scale - above).astype(jnp.bfloat16)
+            beside = jnp.concatenate([value[:, columns], jnp.ones((value.shape[0], HD), jnp.bfloat16)], axis=1)
+            part = jnp.dot(probs, beside, preferred_element_type=jnp.float32)
+            joined = part if joined is None else joined + part
+        product, total = joined[:, :HD], jnp.where(joined[:, HD:] > 0.0, joined[:, HD:], 1.0)
+        write(columns, product / total)
         packed = jnp.where(lane == head, top + jnp.log2(total), packed)
     return packed
 
@@ -207,37 +204,42 @@
             result[:, index * tile:(index + 1) * tile] = product.astype(jnp.bfloat16)
 
 
-def project_blocks(ranks, facts, step, attended, weight, results, tiles, semaphores):
+def project_blocks(ranks, first, facts, step, attended, weight, up, down, tiles, semaphores):
     rank = facts.rank
     last = ranks - 1
-    count, _, tile = tiles.shape
-    copies = streamed(weight, 0, tiles, semaphores)
+    tile = tiles.shape[2]
+    block = up.shape[0]
+    copies = streamed(weight, first, tiles, semaphores)
     yield
-    ups, downs = results[::2], results[1::2]
-    block, columns = ups[0].shape
-    each = columns // tile
+    sends = rank <= step, rank >= last - step
+    starts = [
+        pl.multiple_of(jnp.clip(target, 0, last) * block, block) for target in (last - step + rank, step + rank - last)
+    ]
+    rows = [attended[pl.ds(start, block), :] for start in starts]
     for index, copy in enumerate(copies):
         copy.wait()
-        there = slice(index % each * tile, (index % each + 1) * tile)
-        for sends, target, result in (
-            (rank <= step, last - step + rank, ups[index // each]),
-            (rank >= last - step, step + rank - last, downs[index // each]),
-        ):
-
-            @pl.when(sends)
-            def _():
-                start = pl.multiple_of(target * block, block)
-                product = jnp.dot(
-                    attended[pl.ds(start, block), :], tiles[index], preferred_element_type=jnp.float32
-                )
-                result[:, there] = product.astype(jnp.bfloat16)
+        there = slice(index * tile, (index + 1) * tile)
+
+        @pl.when(jnp.logical_and(*sends))
+        def _():
+            both = jnp.dot(jnp.concatenate(rows, axis=0), tiles[index], preferred_element_type=jnp.float32)
+            up[:, there] = both[:block].astype(jnp.bfloat16)
+            down[:, there] = both[block:].astype(jnp.bfloat16)
+
+        @pl.when(jnp.logical_not(jnp.logical_and(*sends)))
+        def _():
+            one = jnp.dot(
+                jnp.where(sends[0], rows[0], rows[1]), tiles[index], preferred_element_type=jnp.float32
+            ).astype(jnp.bfloat16)
+            up[:, there] = one
+            down[:, there] = one
 
 
 def merged_blocks_kernel(spans, ranks, distances, facts, *refs):
     each = 2 + len(distances)
-    parts, (weight, attended, *results, tiles, semaphores) = (refs[:each], refs[each:2 * each]), refs[2 * each:]
-    here = Facts(facts, spans)
-    work = project_blocks(ranks, here, 1, attended, weight, results, tiles, semaphores)
+    parts, (weight, attended, *results) = (refs[:each], refs[each:2 * each]), refs[2 * each:]
+    here = Facts(facts, spans)
+    work = project_blocks(ranks, 0, here, 1, attended, weight, *results)
     next(work)
     for (start, size), (own, own_sum, *served) in zip(parts_of(here.rank, ranks, attended.shape[0]), parts):
         there = pl.ds(start, size)
@@ -250,44 +252,42 @@
         pass
 
 
-def blocks_kernel(spans, ranks, step, facts, attended, weight, *refs):
-    *results, tiles, semaphores = refs
-    for _ in project_blocks(ranks, Facts(facts, spans), step, attended, weight, results, tiles, semaphores):
+def blocks_kernel(spans, ranks, first, step, facts, attended, weight, *results):
+    for _ in project_blocks(ranks, first, Facts(facts, spans), step, attended, weight, *results):
         pass
 
 
-def own_kernel(spans, facts, attended, weight, result, tiles, semaphores):
+def own_kernel(spans, facts, attended, weight, gate_table, result, gate, tiles, gates, semaphores):
+    here = Facts(facts, spans)
     block = result.shape[0]
     count, _, tile = tiles.shape
+    level = here.level()
+    above = pl.multiple_of(level // 8 * 8, 8)
+    gate_copy = copied(gate_table.at[pl.ds(above, 8)], gates, semaphores.at[count])
     copies = streamed(weight, 0, tiles, semaphores)
-    start = pl.multiple_of(Facts(facts, spans).rank * block, block)
+    start = pl.multiple_of(here.rank * block, block)
     for index, copy in enumerate(copies):
         copy.wait()
         product = jnp.dot(attended[pl.ds(start, block), :], tiles[index], preferred_element_type=jnp.float32)
         result[:, index * tile:(index + 1) * tile] = product.astype(jnp.bfloat16)
-
-
-def final_kernel(spans, facts, done, projected, gate_table, up, down, result, own, gate, gated, semaphores):
-    here = Facts(facts, spans)
+    gate_copy.wait()
+    gate[...] = gates[pl.ds(lax.rem(level, 8), 1), :]
+
+
+def final_kernel(done, projected, gate, up, down, result, own, gated, semaphores):
     first, (block, columns) = done.shape[1], own.shape
     pieces = gated.shape[0]
     wide = columns // pieces
-    level = here.level()
-    above = pl.multiple_of(level // 8 * 8, 8)
-    copies = [
-        copied(projected.at[:, pl.ds(first, columns)], own, semaphores.at[0]),
-        copied(gate_table.at[pl.ds(above, 8), pl.ds(first, columns)], gate, semaphores.at[1]),
-    ]
-    sent = [copied(done, result.at[:, pl.ds(0, first)], semaphores.at[2])]
-    for copy in copies:
-        copy.wait()
+    own_copy = copied(projected.at[:, pl.ds(first, columns)], own, semaphores.at[0])
+    sent = [copied(done, result.at[:, pl.ds(0, first)], semaphores.at[1])]
+    own_copy.wait()
     for piece in range(pieces):
         there = slice(piece * wide, (piece + 1) * wide)
         summed = own[:, there].astype(jnp.float32) + up[:, there].astype(jnp.float32)
         summed = summed + down[:, there].astype(jnp.float32)
-        gated[piece] = (summed * gate[pl.ds(lax.rem(level, 8), 1), there]).astype(jnp.bfloat16)
+        gated[piece] = (summed * gate[:, first + piece * wide:first + (piece + 1) * wide]).astype(jnp.bfloat16)
         sent.append(copied(
-            gated.at[piece], result.at[:, pl.ds(first + piece * wide, wide)], semaphores.at[3 + piece]
+            gated.at[piece], result.at[:, pl.ds(first + piece * wide, wide)], semaphores.at[2 + piece]
         ))
     for copy in sent:
         copy.wait()
@@ -385,66 +385,71 @@
     sent = opening(0, facts)
     arrived = [[lax.ppermute(sent, "tensor", ends)]]
     out_late = [served(q, d) for q, d in zip(after(asked_late, sent), distances)]
-    late = list(local(1, after(facts, out_late)))
     for chunk in range(1, chunks):
-        sent = opening(chunk, after(facts, late))
+        sent = opening(chunk, after(facts, out_late))
         arrived.append([lax.ppermute(sent, "tensor", ends)])
-    late += after([shifted(o, "span", d) for o, d in zip(out_late, distances)], sent)
+    late = list(local(1, after(facts, sent)))
+    late += [shifted(o, "span", d) for o, d in zip(out_late, distances)]
 
     streaming = dict(
-        scratch_shapes=[
-            pltpu.VMEM((chunks * tiles, width, tile), bf16), pltpu.SemaphoreType.DMA((chunks * tiles,))
-        ],
+        scratch_shapes=[pltpu.VMEM((tiles, width, tile), bf16), pltpu.SemaphoreType.DMA((tiles,))],
         compiler_params=PARAMS,
+        cost_estimate=taking(3.0),
     )
     attended_shape = jax.ShapeDtypeStruct((rows, width), bf16)
-    block_shapes = [jax.ShapeDtypeStruct((block, columns), bf16)] * (2 * chunks)
-    attended, *blocks = pl.pallas_call(
+    block_shapes = [jax.ShapeDtypeStruct((block, columns), bf16)] * 2
+    attended, *merged = pl.pallas_call(
         functools.partial(merged_blocks_kernel, spans, ranks, distances),
         in_specs=[SMEM] + [VMEM] * (4 + 2 * len(distances)) + [HBM],
-        out_specs=[VMEM] * (1 + 2 * chunks),
+        out_specs=[VMEM] * 3,
         out_shape=[attended_shape] + block_shapes,
-        cost_estimate=taking(6.0),
         name="merged_blocks",
         **streaming,
     )(facts, *early, *late, weight)
 
+    def blocks_of(step, chunk, attended):
+        return pl.pallas_call(
+            functools.partial(blocks_kernel, spans, ranks, chunk * columns, step),
+            in_specs=[SMEM, VMEM, HBM],
+            out_specs=[VMEM] * 2,
+            out_shape=block_shapes,
+            name="blocks",
+            **streaming,
+        )(facts, attended, weight)
+
     before = attended
     for step in range(1, last):
-        if step > 1:
-            attended, before = lax.optimization_barrier((attended, before))
-            blocks = pl.pallas_call(
-                functools.partial(blocks_kernel, spans, ranks, step),
-                in_specs=[SMEM, VMEM, HBM],
-                out_specs=[VMEM] * (2 * chunks),
-                out_shape=block_shapes,
-                cost_estimate=taking(5.0),
-                name="blocks",
-                **streaming,
-            )(facts, attended, weight)
         for chunk in range(chunks):
-            comes, blocks, before = lax.optimization_barrier((arrived[chunk], blocks, before))
+            if step == 1 and chunk == 0:
+                blocks = merged
+            else:
+                blocks = blocks_of(step, chunk, after(attended, before))
+            comes, blocks = lax.optimization_barrier((arrived[chunk], blocks))
             up, down = [
                 (mine.astype(f32) + come.astype(f32)).astype(bf16)
-                for mine, come in zip(blocks[2 * chunk:2 * chunk + 2], (comes[0], comes[-1]))
+                for mine, come in zip(blocks, (comes[0], comes[-1]))
             ]
             before = (up, down)
             arrived[chunk] = [
                 lax.ppermute(up, "tensor", [(i, i + 1) for i in range(step + 1)]),
                 lax.ppermute(down, "tensor", [(last - i, last - i - 1) for i in range(step + 1)]),
             ]
-    attended, before = lax.optimization_barrier((attended, before))
-    projected = pl.pallas_call(
+    everything = chunks * tiles
+    projected, gate = pl.pallas_call(
         functools.partial(own_kernel, spans),
-        in_specs=[SMEM, VMEM, HBM],
-        out_specs=VMEM,
-        out_shape=jax.ShapeDtypeStruct((block, model), bf16),
+        in_specs=[SMEM, VMEM, HBM, HBM],
+        out_specs=[VMEM, VMEM],
+        out_shape=[jax.ShapeDtypeStruct((block, model), bf16), jax.ShapeDtypeStruct((1, model), f32)],
+        scratch_shapes=[
+            pltpu.VMEM((everything, width, tile), bf16),
+            pltpu.VMEM((8, model), f32),
+            pltpu.SemaphoreType.DMA((everything + 1,)),
+        ],
+        compiler_params=PARAMS,
         cost_estimate=taking(5.0),
         name="own",
-        **streaming,
-    )(facts, attended, weight)
-    level = jnp.sum(jnp.where(numbers == span, levels, 0))
-    gate = lax.dynamic_slice(gate_table, (level, 0), (1, model))
+    )(facts, after(attended, before), weight, in_hbm(gate_table))
+
     finished = []
     for chunk in range(chunks - 1):
         there = slice(chunk * columns, (chunk + 1) * columns)
@@ -452,20 +457,19 @@
         finished.append((summed * gate[:, there]).astype(bf16))
     pieces = 2
     return pl.pallas_call(
-        functools.partial(final_kernel, spans),
-        in_specs=[SMEM, ANY, ANY, HBM, VMEM, VMEM],
+        final_kernel,
+        in_specs=[ANY, ANY, VMEM, VMEM, VMEM],
         out_specs=HBM,
         out_shape=jax.ShapeDtypeStruct((block, model), bf16),
         scratch_shapes=[
             pltpu.VMEM((block, columns), bf16),
-            pltpu.VMEM((8, columns), f32),
             pltpu.VMEM((pieces, block, columns // pieces), bf16),
-            pltpu.SemaphoreType.DMA((3 + pieces,)),
+            pltpu.SemaphoreType.DMA((2 + pieces,)),
         ],
         compiler_params=PARAMS,
         cost_estimate=taking(2.7),
         name="final",
-    )(facts, jnp.concatenate(finished, axis=1), projected, in_hbm(gate_table), *arrived[-1])
+    )(jnp.concatenate(finished, axis=1), projected, gate, *arrived[-1])
 
 
 def solution(mesh):

time: 110 us -> 103 us (0.936)
  the two profiles are of different devices: /device:TPU:16 before, /device:TPU:14 now
where the time goes in v10:
time: 103 us; the launch traced here: 101 us
  starting transfers between devices  38 us (37%)
  Pallas kernels  34.2 us (33%)
  waiting for transfers between devices  26 us (25%)
  other arithmetic  2.14 us (2%)
    ppermute x4, starting transfers between devices, body(): lax.ppermute(up, 'tensor', [(i, i + 1) for i in range(step + 1)])  18.3 us
    ppermute x5, waiting for transfers between devices, shifted(): lax.ppermute(block, axis, [(i, i + distance) for i in range(count) if 0 <...  10.8 us
    pallas_call x3, Pallas kernels, blocks_of(): pl.pallas_call(functools.partial(blocks_kernel, spans, ranks, chunk * col...  10.6 us
    ppermute x5, starting transfers between devices, shifted(): lax.ppermute(block, axis, [(i, i + distance) for i in range(count) if 0 <...  10 us
    pallas_call x2, Pallas kernels, local(): pl.pallas_call(functools.partial(local_kernel, spans, ranks, part), in_sp...  9.05 us
    ppermute x4, waiting for transfers between devices, body(): lax.ppermute(up, 'tensor', [(i, i + 1) for i in range(step + 1)])  7.98 us
    ppermute x4, waiting for transfers between devices, body(): lax.ppermute(down, 'tensor', [(last - i, last - i - 1) for i in range(ste...  7.21 us
    ppermute x4, starting transfers between devices, body(): lax.ppermute(down, 'tensor', [(last - i, last - i - 1) for i in range(ste...  6.43 us
  transfers between devices with their start and end apart: 17, of which 7 were waited for; matrix products, arithmetic and copies ran while one was open for 2% of the time, Pallas kernels for 33%

profile of v10, /device:TPU:14, one launch (start us, length us, event | category | flops | bytes accessed | tf_op | source)
XLA Modules:
  0.0 101.0 jit_solution(1463070316547270846)
XLA Ops:
  0.0 0.0 collective-permute-start
  0.0 0.5 collective-permute-start.1
  0.5 0.7 pad_add_fusion.facts
  1.2 1.7 %split.1 = (bf16[96,768]{1,0:T(8,128)(2,1)S(1)}, bf16[192,768]{1,0:T(8,128)(2,1)S(1)}, bf16[96,768]{1,0:T(8,128)(2,1)S(1)}) custom-call(s32[6,4]{1,0:T(8,128)S(1)} %pad_add_fusion.facts, bf16[384,768]{1,0:T(8,128)(2,1)} %query.5), custom_call_target="tpu_custom_call" | custom-call | bytes 6273000 | tf_op jit(solution)/shard_map/split/pallas_call | solution.py:310
  2.9 0.0 copy-start
  2.9 0.0 copy-start.1
  3.0 1.5 %collective-permute-start.2 = (bf16[96,768]{1,0:T(8,128)(2,1)S(1)}, bf16[96,768]{1,0:T(8,128)(2,1)S(1)}, u32[]{:S(2)}, u32[]{:S(2)}) collective-permute-start(bf16[96,768]{1,0:T(8,128)(2,1)S(1)} %get-tuple-element.50), channel_id=1, source_target_pairs={{8,0},{12,4},{9,1},{13,5},{10,2},{14,6},{11,3},{15,7},{24,16},{28,... | collective-permute-start | bytes 442376 | tf_op jit(solution)/shard_map/ppermute | solution.py:32
  4.5 0.0 collective-permute-done.1.value_beside
  4.5 4.2 %local.2 = (f32[96,768]{1,0:T(8,128)S(1)}, f32[96,128]{1,0:T(8,128)S(1)}) custom-call(s32[6,4]{1,0:T(8,128)S(1)} %pad_add_fusion.facts, bf16[384,768]{1,0:T(8,128)(2,1)} %query.5, bf16[384,768]{1,0:T(8,128)(2,1)} %key.7, bf16[384,768]{1,0:T(8,128)(2,1)} %value.7, bf16[384,768]{1,0:T(8,128)(2,1)S(1)} %collective-permute-done.key_beside, ...), custom_call_target="tpu_custom_call" | custom-call | bytes 14760000 | tf_op jit(solution)/shard_map/local/pallas_call | solution.py:331
  8.7 1.3 %collective-permute-start.4 = (bf16[192,768]{1,0:T(8,128)(2,1)S(1)}, bf16[192,768]{1,0:T(8,128)(2,1)S(1)}, u32[]{:S(2)}, u32[]{:S(2)}) collective-permute-start(bf16[192,768]{1,0:T(8,128)(2,1)S(1)} %get-tuple-element.54), channel_id=1, source_target_pairs={{8,0},{12,4},{9,1},{13,5},{10,2},{14,6},{11,3},{15,7},{24,16},{28,... | collective-permute-start | bytes 884744 | tf_op jit(solution)/shard_map/ppermute | solution.py:32
  10.1 0.6 served.2
  10.7 1.3 %collective-permute-start.3 = (bf16[96,896]{1,0:T(8,128)(2,1)S(1)}, bf16[96,896]{1,0:T(8,128)(2,1)S(1)}, u32[]{:S(2)}, u32[]{:S(2)}) collective-permute-start(bf16[96,896]{1,0:T(8,128)(2,1)S(1)} %served.2), channel_id=1, source_target_pairs={{0,8},{4,12},{1,9},{5,13},{2,10},{6,14},{3,11},{7,15},{16,24},{20,... | collective-permute-start | bytes 516104 | tf_op jit(solution)/shard_map/ppermute | solution.py:32
  12.0 4.6 %collective-permute-start.5 = (bf16[96,768]{1,0:T(8,128)(2,1)S(1)}, bf16[96,768]{1,0:T(8,128)(2,1)S(1)}, u32[]{:S(2)}, u32[]{:S(2)}) collective-permute-start(bf16[96,768]{1,0:T(8,128)(2,1)S(1)} %get-tuple-element.55), channel_id=1, source_target_pairs={{8,0},{12,4},{9,1},{13,5},{10,2},{14,6},{11,3},{15,7},{24,16},{28,... | collective-permute-start | bytes 442376 | tf_op jit(solution)/shard_map/ppermute | solution.py:32
  16.6 2.2 %collective-permute-done.3.refs_2_ = bf16[96,896]{1,0:T(8,128)(2,1)S(1)} collective-permute-done((bf16[96,896]{1,0:T(8,128)(2,1)S(1)}, bf16[96,896]{1,0:T(8,128)(2,1)S(1)}, u32[]{:S(2)}, u32[]{:S(2)}) %collective-permute-start.3) | collective-permute-done | bytes 172064 | tf_op jit(solution)/shard_map/ppermute | solution.py:32
  18.8 0.6 opening.2
  19.5 1.3 %collective-permute-start.8 = (bf16[96,3072]{1,0:T(8,128)(2,1)S(1)}, bf16[96,3072]{1,0:T(8,128)(2,1)S(1)}, u32[]{:S(2)}, u32[]{:S(2)}) collective-permute-start(bf16[96,3072]{1,0:T(8,128)(2,1)S(1)} %opening.2), channel_id=1, source_target_pairs={{0,1},{3,2},{4,5},{7,6},{8,9},{11,10},{12,13},{15,14},{16,17},{19,... | collective-permute-start | bytes 1769480 | tf_op jit(solution)/shard_map/ppermute | solution.py:386
  20.8 0.6 served.3
  21.4 1.3 %collective-permute-start.6 = (bf16[288,896]{1,0:T(8,128)(2,1)S(1)}, bf16[288,896]{1,0:T(8,128)(2,1)S(1)}, u32[]{:S(2)}, u32[]{:S(2)}) collective-permute-start(bf16[288,896]{1,0:T(8,128)(2,1)S(1)} %served.3), channel_id=1, source_target_pairs={{0,8},{4,12},{1,9},{5,13},{2,10},{6,14},{3,11},{7,15},{16,24},{20,... | collective-permute-start | bytes 1548296 | tf_op jit(solution)/shard_map/ppermute | solution.py:32
  22.7 0.6 opening.3
  23.4 1.5 %collective-permute-start.7 = (bf16[96,3072]{1,0:T(8,128)(2,1)S(1)}, bf16[96,3072]{1,0:T(8,128)(2,1)S(1)}, u32[]{:S(2)}, u32[]{:S(2)}) collective-permute-start(bf16[96,3072]{1,0:T(8,128)(2,1)S(1)} %opening.3), channel_id=1, source_target_pairs={{0,1},{3,2},{4,5},{7,6},{8,9},{11,10},{12,13},{15,14},{16,17},{19,... | collective-permute-start | bytes 1769480 | tf_op jit(solution)/shard_map/ppermute | solution.py:390
  24.8 4.8 %local.3 = (f32[288,768]{1,0:T(8,128)S(1)}, f32[288,128]{1,0:T(8,128)S(1)}) custom-call(s32[6,4]{1,0:T(8,128)S(1)} %pad_add_fusion.facts, bf16[384,768]{1,0:T(8,128)(2,1)} %query.5, bf16[384,768]{1,0:T(8,128)(2,1)} %key.7, bf16[384,768]{1,0:T(8,128)(2,1)} %value.7, bf16[384,768]{1,0:T(8,128)(2,1)S(1)} %collective-permute-done.key_beside, ...), custom_call_target="tpu_custom_call" | custom-call | bytes 14760000 | tf_op jit(solution)/shard_map/local/pallas_call | solution.py:331
  29.6 8.6 %collective-permute-done.6.refs_5_ = bf16[288,896]{1,0:T(8,128)(2,1)S(1)} collective-permute-done((bf16[288,896]{1,0:T(8,128)(2,1)S(1)}, bf16[288,896]{1,0:T(8,128)(2,1)S(1)}, u32[]{:S(2)}, u32[]{:S(2)}) %collective-permute-start.6) | collective-permute-done | bytes 516128 | tf_op jit(solution)/shard_map/ppermute | solution.py:32
  38.2 4.3 %merged_blocks.1 = (bf16[384,768]{1,0:T(8,128)(2,1)S(1)}, bf16[96,3072]{1,0:T(8,128)(2,1)S(1)}, bf16[96,3072]{1,0:T(8,128)(2,1)S(1)}) custom-call(s32[6,4]{1,0:T(8,128)S(1)} %pad_add_fusion.facts, f32[96,768]{1,0:T(8,128)S(1)} %get-tuple-element.48.refs_0_, f32[96,128]{1,0:T(8,128)S(1)} %get-tuple-element.49.refs_1_, ...), custom_call_target="tpu_custom_call" | custom-call | bytes 11070000 | tf_op jit(solution)/shard_map/merged_blocks/pallas_call | solution.py:401
  42.5 0.3 fusion.1
  42.8 1.3 %collective-permute-start.12 = (bf16[96,3072]{1,0:T(8,128)(2,1)S(1)}, bf16[96,3072]{1,0:T(8,128)(2,1)S(1)}, u32[]{:S(2)}, u32[]{:S(2)}) collective-permute-start(bf16[96,3072]{1,0:T(8,128)(2,1)S(1)} %get-tuple-element.93), channel_id=1, source_target_pairs={{3,2},{2,1},{7,6},{6,5},{11,10},{10,9},{15,14},{14,13},{19,18},{18... | collective-permute-start | bytes 1769480 | tf_op jit(solution)/shard_map/ppermute | solution.py:435
  44.1 4.6 %collective-permute-start.11 = (bf16[96,3072]{1,0:T(8,128)(2,1)S(1)}, bf16[96,3072]{1,0:T(8,128)(2,1)S(1)}, u32[]{:S(2)}, u32[]{:S(2)}) collective-permute-start(bf16[96,3072]{1,0:T(8,128)(2,1)S(1)} %get-tuple-element.94), channel_id=1, source_target_pairs={{0,1},{1,2},{4,5},{5,6},{8,9},{9,10},{12,13},{13,14},{16,17},{17,1... | collective-permute-start | bytes 1769480 | tf_op jit(solution)/shard_map/ppermute | solution.py:434
  48.7 3.3 %blocks.3 = (bf16[96,3072]{1,0:T(8,128)(2,1)S(1)}, bf16[96,3072]{1,0:T(8,128)(2,1)S(1)}) custom-call(s32[6,4]{1,0:T(8,128)S(1)} %pad_add_fusion.facts, bf16[384,768]{1,0:T(8,128)(2,1)S(1)} %get-tuple-element.88.attended, bf16[768,6144]{1,0:T(8,128)(2,1)} %weight.7), custom_call_target="tpu_custom_call" | custom-call | bytes 11070000 | tf_op jit(solution)/shard_map/blocks/pallas_call | solution.py:411
  52.0 0.3 fusion.3
  52.3 1.3 %collective-permute-start.10 = (bf16[96,3072]{1,0:T(8,128)(2,1)S(1)}, bf16[96,3072]{1,0:T(8,128)(2,1)S(1)}, u32[]{:S(2)}, u32[]{:S(2)}) collective-permute-start(bf16[96,3072]{1,0:T(8,128)(2,1)S(1)} %get-tuple-element.91), channel_id=1, source_target_pairs={{3,2},{2,1},{7,6},{6,5},{11,10},{10,9},{15,14},{14,13},{19,18},{18... | collective-permute-start | bytes 1769480 | tf_op jit(solution)/shard_map/ppermute | solution.py:435
  53.6 4.6 %collective-permute-start.9 = (bf16[96,3072]{1,0:T(8,128)(2,1)S(1)}, bf16[96,3072]{1,0:T(8,128)(2,1)S(1)}, u32[]{:S(2)}, u32[]{:S(2)}) collective-permute-start(bf16[96,3072]{1,0:T(8,128)(2,1)S(1)} %get-tuple-element.92), channel_id=1, source_target_pairs={{0,1},{1,2},{4,5},{5,6},{8,9},{9,10},{12,13},{13,14},{16,17},{17,1... | collective-permute-start | bytes 1769480 | tf_op jit(solution)/shard_map/ppermute | solution.py:434
  58.2 3.5 %blocks.4 = (bf16[96,3072]{1,0:T(8,128)(2,1)S(1)}, bf16[96,3072]{1,0:T(8,128)(2,1)S(1)}) custom-call(s32[6,4]{1,0:T(8,128)S(1)} %pad_add_fusion.facts, bf16[384,768]{1,0:T(8,128)(2,1)S(1)} %get-tuple-element.88.attended, bf16[768,6144]{1,0:T(8,128)(2,1)} %weight.7), custom_call_target="tpu_custom_call" | custom-call | bytes 11070000 | tf_op jit(solution)/shard_map/blocks/pallas_call | solution.py:411
  61.7 1.8 %collective-permute-done.11 = bf16[96,3072]{1,0:T(8,128)(2,1)S(1)} collective-permute-done((bf16[96,3072]{1,0:T(8,128)(2,1)S(1)}, bf16[96,3072]{1,0:T(8,128)(2,1)S(1)}, u32[]{:S(2)}, u32[]{:S(2)}) %collective-permute-start.11) | collective-permute-done | bytes 589856 | tf_op jit(solution)/shard_map/ppermute | solution.py:434
  63.5 0.1 add_convert_fusion.2
  63.7 1.9 %collective-permute-start.14 = (bf16[96,3072]{1,0:T(8,128)(2,1)S(1)}, bf16[96,3072]{1,0:T(8,128)(2,1)S(1)}, u32[]{:S(2)}, u32[]{:S(2)}) collective-permute-start(bf16[96,3072]{1,0:T(8,128)(2,1)S(1)} %add_convert_fusion.2), channel_id=1, source_target_pairs={{3,2},{2,1},{1,0},{7,6},{6,5},{5,4},{11,10},{10,9},{9,8},{15,14},{... | collective-permute-start | bytes 1769480 | tf_op jit(solution)/shard_map/ppermute | solution.py:435
  65.6 0.1 add_convert_fusion.3
  65.8 4.6 %collective-permute-start.13 = (bf16[96,3072]{1,0:T(8,128)(2,1)S(1)}, bf16[96,3072]{1,0:T(8,128)(2,1)S(1)}, u32[]{:S(2)}, u32[]{:S(2)}) collective-permute-start(bf16[96,3072]{1,0:T(8,128)(2,1)S(1)} %add_convert_fusion.3), channel_id=1, source_target_pairs={{0,1},{1,2},{2,3},{4,5},{5,6},{6,7},{8,9},{9,10},{10,11},{12,13},{... | collective-permute-start | bytes 1769480 | tf_op jit(solution)/shard_map/ppermute | solution.py:434
  70.4 3.7 %blocks.5 = (bf16[96,3072]{1,0:T(8,128)(2,1)S(1)}, bf16[96,3072]{1,0:T(8,128)(2,1)S(1)}) custom-call(s32[6,4]{1,0:T(8,128)S(1)} %pad_add_fusion.facts, bf16[384,768]{1,0:T(8,128)(2,1)S(1)} %get-tuple-element.88.attended, bf16[768,6144]{1,0:T(8,128)(2,1)} %weight.7), custom_call_target="tpu_custom_call" | custom-call | bytes 11070000 | tf_op jit(solution)/shard_map/blocks/pallas_call | solution.py:411
  74.1 2.0 %collective-permute-done.9 = bf16[96,3072]{1,0:T(8,128)(2,1)S(1)} collective-permute-done((bf16[96,3072]{1,0:T(8,128)(2,1)S(1)}, bf16[96,3072]{1,0:T(8,128)(2,1)S(1)}, u32[]{:S(2)}, u32[]{:S(2)}) %collective-permute-start.9) | collective-permute-done | bytes 589856 | tf_op jit(solution)/shard_map/ppermute | solution.py:434
  76.2 0.2 add_convert_fusion
  76.3 1.9 %collective-permute-start.16 = (bf16[96,3072]{1,0:T(8,128)(2,1)S(1)}, bf16[96,3072]{1,0:T(8,128)(2,1)S(1)}, u32[]{:S(2)}, u32[]{:S(2)}) collective-permute-start(bf16[96,3072]{1,0:T(8,128)(2,1)S(1)} %add_convert_fusion), channel_id=1, source_target_pairs={{3,2},{2,1},{1,0},{7,6},{6,5},{5,4},{11,10},{10,9},{9,8},{15,14},{... | collective-permute-start | bytes 1769480 | tf_op jit(solution)/shard_map/ppermute | solution.py:435
  78.2 0.1 add_convert_fusion.1
  78.4 4.6 %collective-permute-start.15 = (bf16[96,3072]{1,0:T(8,128)(2,1)S(1)}, bf16[96,3072]{1,0:T(8,128)(2,1)S(1)}, u32[]{:S(2)}, u32[]{:S(2)}) collective-permute-start(bf16[96,3072]{1,0:T(8,128)(2,1)S(1)} %add_convert_fusion.1), channel_id=1, source_target_pairs={{0,1},{1,2},{2,3},{4,5},{5,6},{6,7},{8,9},{9,10},{10,11},{12,13},{... | collective-permute-start | bytes 1769480 | tf_op jit(solution)/shard_map/ppermute | solution.py:434
  83.0 5.1 %own.1 = (bf16[96,6144]{1,0:T(8,128)(2,1)S(1)}, f32[1,6144]{1,0:T(1,128)S(1)}) custom-call(s32[6,4]{1,0:T(8,128)S(1)} %pad_add_fusion.facts, bf16[384,768]{1,0:T(8,128)(2,1)S(1)} %get-tuple-element.88.attended, bf16[768,6144]{1,0:T(8,128)(2,1)} %weight.7, f32[64,6144]{1,0:T(8,128)} %gate_table.1), custom_call_target="tpu_custom_call" | custom-call | bytes 18450000 | tf_op jit(solution)/shard_map/own/pallas_call | solution.py:438
  88.1 0.7 collective-permute-done.13
  88.8 0.3 multiply_convert_fusion.done
  89.1 7.2 %collective-permute-done.16.down = bf16[96,3072]{1,0:T(8,128)(2,1)S(1)} collective-permute-done((bf16[96,3072]{1,0:T(8,128)(2,1)S(1)}, bf16[96,3072]{1,0:T(8,128)(2,1)S(1)}, u32[]{:S(2)}, u32[]{:S(2)}) %collective-permute-start.16) | collective-permute-done | bytes 589856 | tf_op jit(solution)/shard_map/ppermute | solution.py:435
  96.3 3.4 %collective-permute-done.15.up = bf16[96,3072]{1,0:T(8,128)(2,1)S(1)} collective-permute-done((bf16[96,3072]{1,0:T(8,128)(2,1)S(1)}, bf16[96,3072]{1,0:T(8,128)(2,1)S(1)}, u32[]{:S(2)}, u32[]{:S(2)}) %collective-permute-start.15) | collective-permute-done | bytes 589856 | tf_op jit(solution)/shard_map/ppermute | solution.py:434
  99.7 1.1 %final.1 = bf16[96,6144]{1,0:T(8,128)(2,1)} custom-call(bf16[96,3072]{1,0:T(8,128)(2,1)S(1)} %multiply_convert_fusion.done, bf16[96,6144]{1,0:T(8,128)(2,1)S(1)} %get-tuple-element.89.projected, f32[1,6144]{1,0:T(1,128)S(1)} %get-tuple-element.90.gate, bf16[96,3072]{1,0:T(8,128)(2,1)S(1)} %collective-permute-done.15.up, ...), custom_call_target="tpu_custom_call" | custom-call | bytes 9963000 | tf_op jit(solution)/shard_map/final/pallas_call | solution.py:459
  (13 shorter events, 0.0 us)
Async XLA Ops:
  0.0 4.5 %collective-permute-start = (bf16[384,768]{1,0:T(8,128)(2,1)}, bf16[384,768]{1,0:T(8,128)(2,1)S(1)}, u32[]{:S(2)}, u32[]{:S(2)}) collective-permute-start(bf16[384,768]{1,0:T(8,128)(2,1)} %key.7), channel_id=1, source_target_pairs={{0,4},{4,0},{8,12},{12,8},{1,5},{5,1},{9,13},{13,9},{2,6},{6,2},{1... | collective-permute-start | bytes 1769480 | tf_op jit(solution)/shard_map/ppermute | solution.py:323
  0.0 4.5 %collective-permute-start.1 = (bf16[384,768]{1,0:T(8,128)(2,1)}, bf16[384,768]{1,0:T(8,128)(2,1)S(1)}, u32[]{:S(2)}, u32[]{:S(2)}) collective-permute-start(bf16[384,768]{1,0:T(8,128)(2,1)} %value.7), channel_id=1, source_target_pairs={{0,4},{4,0},{8,12},{12,8},{1,5},{5,1},{9,13},{13,9},{2,6},{6,2},{1... | collective-permute-start | bytes 1769480 | tf_op jit(solution)/shard_map/ppermute | solution.py:324
  2.9 7.1 %copy-start = (bf16[384,768]{1,0:T(8,128)(2,1)S(1)}, bf16[384,768]{1,0:T(8,128)(2,1)}, u32[]{:S(2)}) copy-start(bf16[384,768]{1,0:T(8,128)(2,1)} %key.7) | copy-start | bytes 1769476
  2.9 7.1 %copy-start.1 = (bf16[384,768]{1,0:T(8,128)(2,1)S(1)}, bf16[384,768]{1,0:T(8,128)(2,1)}, u32[]{:S(2)}) copy-start(bf16[384,768]{1,0:T(8,128)(2,1)} %value.7) | copy-start | bytes 1769476
  3.0 7.1 %collective-permute-start.2 = (bf16[96,768]{1,0:T(8,128)(2,1)S(1)}, bf16[96,768]{1,0:T(8,128)(2,1)S(1)}, u32[]{:S(2)}, u32[]{:S(2)}) collective-permute-start(bf16[96,768]{1,0:T(8,128)(2,1)S(1)} %get-tuple-element.50), channel_id=1, source_target_pairs={{8,0},{12,4},{9,1},{13,5},{10,2},{14,6},{11,3},{15,7},{24,16},{28,... | collective-permute-start | bytes 442376 | tf_op jit(solution)/shard_map/ppermute | solution.py:32
  8.7 12.0 %collective-permute-start.4 = (bf16[192,768]{1,0:T(8,128)(2,1)S(1)}, bf16[192,768]{1,0:T(8,128)(2,1)S(1)}, u32[]{:S(2)}, u32[]{:S(2)}) collective-permute-start(bf16[192,768]{1,0:T(8,128)(2,1)S(1)} %get-tuple-element.54), channel_id=1, source_target_pairs={{8,0},{12,4},{9,1},{13,5},{10,2},{14,6},{11,3},{15,7},{24,16},{28,... | collective-permute-start | bytes 884744 | tf_op jit(solution)/shard_map/ppermute | solution.py:32
  10.7 8.1 %collective-permute-start.3 = (bf16[96,896]{1,0:T(8,128)(2,1)S(1)}, bf16[96,896]{1,0:T(8,128)(2,1)S(1)}, u32[]{:S(2)}, u32[]{:S(2)}) collective-permute-start(bf16[96,896]{1,0:T(8,128)(2,1)S(1)} %served.2), channel_id=1, source_target_pairs={{0,8},{4,12},{1,9},{5,13},{2,10},{6,14},{3,11},{7,15},{16,24},{20,... | collective-permute-start | bytes 516104 | tf_op jit(solution)/shard_map/ppermute | solution.py:32
  12.0 8.8 %collective-permute-start.5 = (bf16[96,768]{1,0:T(8,128)(2,1)S(1)}, bf16[96,768]{1,0:T(8,128)(2,1)S(1)}, u32[]{:S(2)}, u32[]{:S(2)}) collective-permute-start(bf16[96,768]{1,0:T(8,128)(2,1)S(1)} %get-tuple-element.55), channel_id=1, source_target_pairs={{8,0},{12,4},{9,1},{13,5},{10,2},{14,6},{11,3},{15,7},{24,16},{28,... | collective-permute-start | bytes 442376 | tf_op jit(solution)/shard_map/ppermute | solution.py:32
  19.5 23.0 %collective-permute-start.8 = (bf16[96,3072]{1,0:T(8,128)(2,1)S(1)}, bf16[96,3072]{1,0:T(8,128)(2,1)S(1)}, u32[]{:S(2)}, u32[]{:S(2)}) collective-permute-start(bf16[96,3072]{1,0:T(8,128)(2,1)S(1)} %opening.2), channel_id=1, source_target_pairs={{0,1},{3,2},{4,5},{7,6},{8,9},{11,10},{12,13},{15,14},{16,17},{19,... | collective-permute-start | bytes 1769480 | tf_op jit(solution)/shard_map/ppermute | solution.py:386
  21.4 16.8 %collective-permute-start.6 = (bf16[288,896]{1,0:T(8,128)(2,1)S(1)}, bf16[288,896]{1,0:T(8,128)(2,1)S(1)}, u32[]{:S(2)}, u32[]{:S(2)}) collective-permute-start(bf16[288,896]{1,0:T(8,128)(2,1)S(1)} %served.3), channel_id=1, source_target_pairs={{0,8},{4,12},{1,9},{5,13},{2,10},{6,14},{3,11},{7,15},{16,24},{20,... | collective-permute-start | bytes 1548296 | tf_op jit(solution)/shard_map/ppermute | solution.py:32
  23.4 28.7 %collective-permute-start.7 = (bf16[96,3072]{1,0:T(8,128)(2,1)S(1)}, bf16[96,3072]{1,0:T(8,128)(2,1)S(1)}, u32[]{:S(2)}, u32[]{:S(2)}) collective-permute-start(bf16[96,3072]{1,0:T(8,128)(2,1)S(1)} %opening.3), channel_id=1, source_target_pairs={{0,1},{3,2},{4,5},{7,6},{8,9},{11,10},{12,13},{15,14},{16,17},{19,... | collective-permute-start | bytes 1769480 | tf_op jit(solution)/shard_map/ppermute | solution.py:390
  42.8 18.9 %collective-permute-start.12 = (bf16[96,3072]{1,0:T(8,128)(2,1)S(1)}, bf16[96,3072]{1,0:T(8,128)(2,1)S(1)}, u32[]{:S(2)}, u32[]{:S(2)}) collective-permute-start(bf16[96,3072]{1,0:T(8,128)(2,1)S(1)} %get-tuple-element.93), channel_id=1, source_target_pairs={{3,2},{2,1},{7,6},{6,5},{11,10},{10,9},{15,14},{14,13},{19,18},{18... | collective-permute-start | bytes 1769480 | tf_op jit(solution)/shard_map/ppermute | solution.py:435
  44.1 19.4 %collective-permute-start.11 = (bf16[96,3072]{1,0:T(8,128)(2,1)S(1)}, bf16[96,3072]{1,0:T(8,128)(2,1)S(1)}, u32[]{:S(2)}, u32[]{:S(2)}) collective-permute-start(bf16[96,3072]{1,0:T(8,128)(2,1)S(1)} %get-tuple-element.94), channel_id=1, source_target_pairs={{0,1},{1,2},{4,5},{5,6},{8,9},{9,10},{12,13},{13,14},{16,17},{17,1... | collective-permute-start | bytes 1769480 | tf_op jit(solution)/shard_map/ppermute | solution.py:434
  52.3 21.8 %collective-permute-start.10 = (bf16[96,3072]{1,0:T(8,128)(2,1)S(1)}, bf16[96,3072]{1,0:T(8,128)(2,1)S(1)}, u32[]{:S(2)}, u32[]{:S(2)}) collective-permute-start(bf16[96,3072]{1,0:T(8,128)(2,1)S(1)} %get-tuple-element.91), channel_id=1, source_target_pairs={{3,2},{2,1},{7,6},{6,5},{11,10},{10,9},{15,14},{14,13},{19,18},{18... | collective-permute-start | bytes 1769480 | tf_op jit(solution)/shard_map/ppermute | solution.py:435
  53.6 22.5 %collective-permute-start.9 = (bf16[96,3072]{1,0:T(8,128)(2,1)S(1)}, bf16[96,3072]{1,0:T(8,128)(2,1)S(1)}, u32[]{:S(2)}, u32[]{:S(2)}) collective-permute-start(bf16[96,3072]{1,0:T(8,128)(2,1)S(1)} %get-tuple-element.92), channel_id=1, source_target_pairs={{0,1},{1,2},{4,5},{5,6},{8,9},{9,10},{12,13},{13,14},{16,17},{17,1... | collective-permute-start | bytes 1769480 | tf_op jit(solution)/shard_map/ppermute | solution.py:434
  63.7 24.4 %collective-permute-start.14 = (bf16[96,3072]{1,0:T(8,128)(2,1)S(1)}, bf16[96,3072]{1,0:T(8,128)(2,1)S(1)}, u32[]{:S(2)}, u32[]{:S(2)}) collective-permute-start(bf16[96,3072]{1,0:T(8,128)(2,1)S(1)} %add_convert_fusion.2), channel_id=1, source_target_pairs={{3,2},{2,1},{1,0},{7,6},{6,5},{5,4},{11,10},{10,9},{9,8},{15,14},{... | collective-permute-start | bytes 1769480 | tf_op jit(solution)/shard_map/ppermute | solution.py:435
  65.8 23.0 %collective-permute-start.13 = (bf16[96,3072]{1,0:T(8,128)(2,1)S(1)}, bf16[96,3072]{1,0:T(8,128)(2,1)S(1)}, u32[]{:S(2)}, u32[]{:S(2)}) collective-permute-start(bf16[96,3072]{1,0:T(8,128)(2,1)S(1)} %add_convert_fusion.3), channel_id=1, source_target_pairs={{0,1},{1,2},{2,3},{4,5},{5,6},{6,7},{8,9},{9,10},{10,11},{12,13},{... | collective-permute-start | bytes 1769480 | tf_op jit(solution)/shard_map/ppermute | solution.py:434
  76.3 19.9 %collective-permute-start.16 = (bf16[96,3072]{1,0:T(8,128)(2,1)S(1)}, bf16[96,3072]{1,0:T(8,128)(2,1)S(1)}, u32[]{:S(2)}, u32[]{:S(2)}) collective-permute-start(bf16[96,3072]{1,0:T(8,128)(2,1)S(1)} %add_convert_fusion), channel_id=1, source_target_pairs={{3,2},{2,1},{1,0},{7,6},{6,5},{5,4},{11,10},{10,9},{9,8},{15,14},{... | collective-permute-start | bytes 1769480 | tf_op jit(solution)/shard_map/ppermute | solution.py:435
  78.4 21.3 %collective-permute-start.15 = (bf16[96,3072]{1,0:T(8,128)(2,1)S(1)}, bf16[96,3072]{1,0:T(8,128)(2,1)S(1)}, u32[]{:S(2)}, u32[]{:S(2)}) collective-permute-start(bf16[96,3072]{1,0:T(8,128)(2,1)S(1)} %add_convert_fusion.1), channel_id=1, source_target_pairs={{0,1},{1,2},{2,3},{4,5},{5,6},{6,7},{8,9},{9,10},{10,11},{12,13},{... | collective-permute-start | bytes 1769480 | tf_op jit(solution)/shard_map/ppermute | solution.py:434

commit v11 on v10

--- a/solution.py
+++ b/solution.py
@@ -92,20 +92,31 @@
     return (early, block), (late, rows - block)
 
 
-def split_kernel(spans, ranks, facts, query, *refs):
+def split_kernel(spans, ranks, facts, query, weight, *refs):
     here = Facts(facts, spans)
-    *targets, semaphores = refs
+    *targets, piece, semaphores = refs
+    (early, _), (late, _) = parts_of(here.rank, ranks, query.shape[0])
+    starts = (early, late, late + targets[1].shape[0])
+    copies = [
+        pltpu.make_async_copy(
+            query.at[pl.ds(pl.multiple_of(start, 16), target.shape[0])], target, semaphores.at[index]
+        )
+        for index, (start, target) in enumerate(zip(starts, targets))
+    ]
+    size, columns = piece.shape
+    first = pl.multiple_of(jnp.minimum(facts[spans, 2] * size, weight.shape[0] - size), 16)
+    taken = copied(
+        weight.at[pl.ds(first, size), pl.ds(weight.shape[1] - columns, columns)], piece, semaphores.at[len(copies)]
+    )
 
     @pl.when(here.span > 1)
     def _():
-        (early, _), (late, _) = parts_of(here.rank, ranks, query.shape[0])
-        starts = (early, late, pl.multiple_of(late + targets[1].shape[0], 16))
-        copies = [
-            copied(query.at[pl.ds(start, target.shape[0])], target, semaphores.at[index])
-            for index, (start, target) in enumerate(zip(starts, targets))
-        ]
+        for copy in copies:
+            copy.start()
         for copy in copies:
             copy.wait()
+
+    taken.wait()
 
 
 def local_kernel(spans, ranks, part, facts, query, key, value, key_beside, value_beside, result, sums, *scratch):
@@ -184,24 +195,31 @@
     ]
 
 
-def opening_kernel(spans, ranks, distances, first, facts, *refs):
+def opening_kernel(spans, ranks, distances, facts, *refs):
     own, own_sum, *served = refs[:2 + len(distances)]
-    weight, result, tiles, rows, semaphores = refs[2 + len(distances):]
+    weight, rows, result, tiles, semaphores = refs[2 + len(distances):]
     here = Facts(facts, spans)
     tile = tiles.shape[2]
-
-    @pl.when(jnp.logical_or(here.rank == 0, here.rank == ranks - 1))
-    def _():
-        copies = streamed(weight, first, tiles, semaphores)
-
+    is_end = jnp.logical_or(here.rank == 0, here.rank == ranks - 1)
+
+    def merged():
         def write(columns, part):
             rows[:, columns] = part
 
         merge(here.span, distances, own, own_sum, served, write)
+
+    @pl.when(is_end)
+    def _():
+        copies = streamed(weight, 0, tiles, semaphores)
+        merged()
         for index, copy in enumerate(copies):
             copy.wait()
             product = jnp.dot(rows[...], tiles[index], preferred_element_type=jnp.float32)
             result[:, index * tile:(index + 1) * tile] = product.astype(jnp.bfloat16)
+
+    @pl.when(jnp.logical_not(is_end))
+    def _():
+        merged()
 
 
 def project_blocks(ranks, first, facts, step, attended, weight, up, down, tiles, semaphores):
@@ -257,19 +275,101 @@
         pass
 
 
-def own_kernel(spans, facts, attended, weight, gate_table, result, gate, tiles, gates, semaphores):
+def is_inner(rank, ranks):
+    return jnp.logical_or(rank == 1, rank == ranks - 2)
+
+
+def streamed_pairs(weight, first, end_weight, tiles, semaphores):
+    count, depth, tile = tiles.shape
+    width = depth // 2
+    copies = []
+    for index in range(count):
+        columns = pl.ds(first + index * tile, tile)
+        copies.append((
+            copied(weight.at[:, columns], tiles.at[index, pl.ds(0, width)], semaphores.at[2 * index]),
+            copied(
+                end_weight.at[:, pl.ds(index * tile, tile)], tiles.at[index, pl.ds(width, width)],
+                semaphores.at[2 * index + 1],
+            ),
+        ))
+    return copies
+
+
+def joint_opening_kernel(spans, ranks, first, facts, rows, end_rows, weight, end_weight, result, tiles, semaphores):
+    tile = tiles.shape[2]
+
+    @pl.when(is_inner(Facts(facts, spans).rank, ranks))
+    def _():
+        copies = streamed_pairs(weight, first, end_weight, tiles, semaphores)
+        both = jnp.concatenate([rows[...], end_rows[...]], axis=1)
+        for index, pair in enumerate(copies):
+            for copy in pair:
+                copy.wait()
+            product = jnp.dot(both, tiles[index], preferred_element_type=jnp.float32)
+            result[:, index * tile:(index + 1) * tile] = product.astype(jnp.bfloat16)
+
+
+def joint_blocks_kernel(spans, ranks, first, step, facts, attended, end_rows, weight, end_weight,
+                        up, down, tiles, semaphores):
+    rank = Facts(facts, spans).rank
+    last = ranks - 1
+    block, tile = up.shape[0], tiles.shape[2]
+    width = attended.shape[1]
+    copies = streamed_pairs(weight, first, end_weight, tiles, semaphores)
+
+    def block_of(array, target, count):
+        return array[pl.ds(pl.multiple_of(jnp.clip(target, 0, count - 1) * block, block), block), :]
+
+    up_target, down_target = last - step + rank - 1, step - last + rank + 1
+    rows = jnp.concatenate([block_of(attended, target, ranks) for target in (up_target, down_target)], axis=0)
+    others = jnp.concatenate([
+        jnp.where(takes, block_of(end_rows, target - 1, ranks - 2), jnp.zeros((block, width), jnp.bfloat16))
+        for takes, target in ((rank == 1, up_target), (rank == last - 1, down_target))
+    ], axis=0)
+    for index, pair in enumerate(copies):
+        for copy in pair:
+            copy.wait()
+        there = slice(index * tile, (index + 1) * tile)
+
+        def write(product):
+            up[:, there] = product[:block].astype(jnp.bfloat16)
+            down[:, there] = product[block:].astype(jnp.bfloat16)
+
+        @pl.when(is_inner(rank, ranks))
+        def _():
+            both = jnp.concatenate([rows, others], axis=1)
+            write(jnp.dot(both, tiles[index], preferred_element_type=jnp.float32))
+
+        @pl.when(jnp.logical_not(is_inner(rank, ranks)))
+        def _():
+            write(jnp.dot(rows, tiles[index, :width], preferred_element_type=jnp.float32))
+
+
+def own_kernel(spans, ranks, facts, attended, end_rows, weight, end_weight, gate_table, result, gate,
+               tiles, pairs, gates, semaphores, pair_semaphores):
     here = Facts(facts, spans)
-    block = result.shape[0]
+    block, width = result.shape[0], attended.shape[1]
     count, _, tile = tiles.shape
+    columns = count * tile
     level = here.level()
     above = pl.multiple_of(level // 8 * 8, 8)
     gate_copy = copied(gate_table.at[pl.ds(above, 8)], gates, semaphores.at[count])
     copies = streamed(weight, 0, tiles, semaphores)
-    start = pl.multiple_of(here.rank * block, block)
+    pair_copies = streamed_pairs(weight, columns, end_weight, pairs, pair_semaphores)
+    mine = attended[pl.ds(pl.multiple_of(here.rank * block, block), block), :]
+    target = jnp.clip(here.rank - 1, 0, ranks - 3)
+    other = end_rows[pl.ds(pl.multiple_of(target * block, block), block), :]
+    other = jnp.where(is_inner(here.rank, ranks), other, jnp.zeros((block, width), jnp.bfloat16))
     for index, copy in enumerate(copies):
         copy.wait()
-        product = jnp.dot(attended[pl.ds(start, block), :], tiles[index], preferred_element_type=jnp.float32)
+        product = jnp.dot(mine, tiles[index], preferred_element_type=jnp.float32)
         result[:, index * tile:(index + 1) * tile] = product.astype(jnp.bfloat16)
+    both = jnp.concatenate([mine, other], axis=1)
+    for index, pair in enumerate(pair_copies):
+        for copy in pair:
+            copy.wait()
+        product = jnp.dot(both, pairs[index], preferred_element_type=jnp.float32)
+        result[:, columns + index * tile:columns + (index + 1) * tile] = product.astype(jnp.bfloat16)
     gate_copy.wait()
     gate[...] = gates[pl.ds(lax.rem(level, 8), 1), :]
 
@@ -303,20 +403,24 @@
     block = rows // ranks
     bf16, f32 = jnp.bfloat16, jnp.float32
     numbers = jnp.arange(spans, dtype=jnp.int32)
-    place = jnp.where(numbers == 0, span, jnp.where(numbers == 1, rank, 0)).astype(jnp.int32)
+    member = lax.axis_index("group") * spans + span
+    place = jnp.where(numbers == 0, span, jnp.where(numbers == 1, rank, member)).astype(jnp.int32)
     facts = jnp.concatenate([visible, place[None, :], levels[None, :]], axis=0)
 
     third = (rows - block) // 48 * 16
-    query_early, *query_late = pl.pallas_call(
+    columns = model // 2
+    pieces = -(-width // (16 * lax.axis_size("group") * spans)) * 16
+    query_early, *query_late, piece = pl.pallas_call(
         functools.partial(split_kernel, spans, ranks),
-        in_specs=[SMEM, HBM],
-        out_specs=[VMEM] * 3,
-        out_shape=[jax.ShapeDtypeStruct((part, width), bf16) for part in (block, rows - block - third, third)],
-        scratch_shapes=[pltpu.SemaphoreType.DMA((3,))],
+        in_specs=[SMEM, HBM, HBM],
+        out_specs=[VMEM] * 3 + [HBM],
+        out_shape=[jax.ShapeDtypeStruct((part, width), bf16) for part in (block, rows - block - third, third)]
+        + [pltpu.HBM((pieces, columns), bf16)],
+        scratch_shapes=[pltpu.SemaphoreType.DMA((4,))],
         compiler_params=PARAMS,
         cost_estimate=taking(1.7),
         name="split",
-    )(facts, in_hbm(queries))
+    )(facts, in_hbm(queries), in_hbm(out_weight))
     distances = list(range(2, spans, 2))
     asked_early = [shifted(query_early, "span", -distance) for distance in distances]
     swap = [(i, i + 1 - 2 * (i % 2)) for i in range(spans)]
@@ -352,52 +456,46 @@
             name="served",
         )(facts, keys, values, key_beside, value_beside, *asked)
 
-    early = list(local(0, facts))
-    query_late = after(query_late, early)
-    asked_early = after(asked_early, early)
+    ends = [(0, 1), (ranks - 1, ranks - 2)]
+    end_piece = lax.ppermute(after(piece, key_beside), "tensor", ends)
+
+    query_late = after(query_late, value_beside)
     asked_late = [[shifted(query, "span", -distance) for query in query_late] for distance in distances]
-    early += [shifted(served([q], d), "span", d) for q, d in zip(asked_early, distances)]
-
-    chunks = 2
-    columns = model // chunks
+    out_early = [served([q], d) for q, d in zip(asked_early, distances)]
+    early = list(local(0, after(facts, out_early)))
+    early += [shifted(o, "span", d) for o, d in zip(out_early, distances)]
+
     tiles = 4
     tile = columns // tiles
     last = ranks - 1
     weight = in_hbm(out_weight)
-
-    def opening(chunk, facts):
-        return pl.pallas_call(
-            functools.partial(opening_kernel, spans, ranks, distances, chunk * columns),
-            in_specs=[SMEM] + [VMEM] * (2 + len(distances)) + [HBM],
-            out_specs=VMEM,
-            out_shape=jax.ShapeDtypeStruct((block, columns), bf16),
-            scratch_shapes=[
-                pltpu.VMEM((tiles, width, tile), bf16),
-                pltpu.VMEM((block, width), bf16),
-                pltpu.SemaphoreType.DMA((tiles,)),
-            ],
-            compiler_params=PARAMS,
-            cost_estimate=taking(3.4),
-            name="opening",
-        )(facts, *early, weight)
-
-    ends = [(0, 1), (last, last - 1)]
-    sent = opening(0, facts)
-    arrived = [[lax.ppermute(sent, "tensor", ends)]]
-    out_late = [served(q, d) for q, d in zip(after(asked_late, sent), distances)]
-    for chunk in range(1, chunks):
-        sent = opening(chunk, after(facts, out_late))
-        arrived.append([lax.ppermute(sent, "tensor", ends)])
-    late = list(local(1, after(facts, sent)))
-    late += [shifted(o, "span", d) for o, d in zip(out_late, distances)]
-
+    message_shape = jax.ShapeDtypeStruct((block, columns), bf16)
     streaming = dict(
         scratch_shapes=[pltpu.VMEM((tiles, width, tile), bf16), pltpu.SemaphoreType.DMA((tiles,))],
         compiler_params=PARAMS,
         cost_estimate=taking(3.0),
     )
+    pair_streaming = dict(streaming, scratch_shapes=[
+        pltpu.VMEM((tiles, 2 * width, tile), bf16), pltpu.SemaphoreType.DMA((2 * tiles,))
+    ])
+
+    early_rows, sent = pl.pallas_call(
+        functools.partial(opening_kernel, spans, ranks, distances),
+        in_specs=[SMEM] + [VMEM] * (2 + len(distances)) + [HBM],
+        out_specs=[VMEM, VMEM],
+        out_shape=[jax.ShapeDtypeStruct((block, width), bf16), message_shape],
+        name="opening",
+        **streaming,
+    )(after(facts, asked_late), *early, weight)
+    arrived = [lax.ppermute(sent, "tensor", ends)]
+    end_early = lax.ppermute(early_rows, "tensor", ends)
+    end_weight = lax.all_gather(after(end_piece, sent), ("group", "span"), axis=0, tiled=True)[:width]
+    out_late = [served(q, d) for q, d in zip(after(asked_late, sent), distances)]
+    late = list(local(1, after(facts, out_late)))
+    late += [shifted(o, "span", d) for o, d in zip(out_late, distances)]
+
     attended_shape = jax.ShapeDtypeStruct((rows, width), bf16)
-    block_shapes = [jax.ShapeDtypeStruct((block, columns), bf16)] * 2
+    block_shapes = [message_shape] * 2
     attended, *merged = pl.pallas_call(
         functools.partial(merged_blocks_kernel, spans, ranks, distances),
         in_specs=[SMEM] + [VMEM] * (4 + 2 * len(distances)) + [HBM],
@@ -405,56 +503,80 @@
         out_shape=[attended_shape] + block_shapes,
         name="merged_blocks",
         **streaming,
-    )(facts, *early, *late, weight)
-
-    def blocks_of(step, chunk, attended):
-        return pl.pallas_call(
-            functools.partial(blocks_kernel, spans, ranks, chunk * columns, step),
-            in_specs=[SMEM, VMEM, HBM],
-            out_specs=[VMEM] * 2,
-            out_shape=block_shapes,
-            name="blocks",
-            **streaming,
-        )(facts, attended, weight)
+    )(after(facts, end_early), *early, *late, weight)
+
+    def exchanged(up, down, base, step):
+        reached = range(base, step + 1)
+        return [
+            lax.ppermute(up, "tensor", [(i, i + 1) for i in reached]),
+            lax.ppermute(down, "tensor", [(last - i, last - i - 1) for i in reached]),
+        ]
+
+    def added(blocks, comes):
+        return [
+            (mine.astype(f32) + come.astype(f32)).astype(bf16) for mine, come in zip(blocks, (comes[0], comes[-1]))
+        ]
 
     before = attended
     for step in range(1, last):
-        for chunk in range(chunks):
-            if step == 1 and chunk == 0:
-                blocks = merged
-            else:
-                blocks = blocks_of(step, chunk, after(attended, before))
-            comes, blocks = lax.optimization_barrier((arrived[chunk], blocks))
-            up, down = [
-                (mine.astype(f32) + come.astype(f32)).astype(bf16)
-                for mine, come in zip(blocks, (comes[0], comes[-1]))
-            ]
-            before = (up, down)
-            arrived[chunk] = [
-                lax.ppermute(up, "tensor", [(i, i + 1) for i in range(step + 1)]),
-                lax.ppermute(down, "tensor", [(last - i, last - i - 1) for i in range(step + 1)]),
-            ]
-    everything = chunks * tiles
+        if step == 1:
+            blocks = merged
+        else:
+            blocks = pl.pallas_call(
+                functools.partial(blocks_kernel, spans, ranks, 0, step),
+                in_specs=[SMEM, VMEM, HBM],
+                out_specs=[VMEM] * 2,
+                out_shape=block_shapes,
+                name="blocks",
+                **streaming,
+            )(facts, after(attended, before), weight)
+        comes, blocks = lax.optimization_barrier((arrived, blocks))
+        before = up, down = added(blocks, comes)
+        arrived = exchanged(up, down, 0, step)
+        if step == 1:
+            end_rows = lax.ppermute(attended[block:rows - block], "tensor", ends)
+            before = joint = pl.pallas_call(
+                functools.partial(joint_opening_kernel, spans, ranks, columns),
+                in_specs=[SMEM, VMEM, VMEM, HBM, HBM],
+                out_specs=VMEM,
+                out_shape=message_shape,
+                name="joint_opening",
+                **pair_streaming,
+            )(facts, after(early_rows, before), end_early, weight, in_hbm(end_weight))
+            come = lax.ppermute(joint, "tensor", [(1, 2), (last - 1, last - 2)])
+            joint_arrived = [jnp.where(rank == to, come, jnp.zeros_like(come)) for to in (2, last - 2)]
+        else:
+            blocks = pl.pallas_call(
+                functools.partial(joint_blocks_kernel, spans, ranks, columns, step - 1),
+                in_specs=[SMEM, VMEM, VMEM, HBM, HBM],
+                out_specs=[VMEM] * 2,
+                out_shape=block_shapes,
+                name="joint_blocks",
+                **pair_streaming,
+            )(facts, after(attended, before), end_rows, weight, in_hbm(end_weight))
+            comes, blocks = lax.optimization_barrier((joint_arrived, blocks))
+            before = up, down = added(blocks, comes)
+            joint_arrived = exchanged(up, down, 1, step)
+    arrived = [arrived, joint_arrived]
     projected, gate = pl.pallas_call(
-        functools.partial(own_kernel, spans),
-        in_specs=[SMEM, VMEM, HBM, HBM],
+        functools.partial(own_kernel, spans, ranks),
+        in_specs=[SMEM, VMEM, VMEM, HBM, HBM, HBM],
         out_specs=[VMEM, VMEM],
         out_shape=[jax.ShapeDtypeStruct((block, model), bf16), jax.ShapeDtypeStruct((1, model), f32)],
         scratch_shapes=[
-            pltpu.VMEM((everything, width, tile), bf16),
+            pltpu.VMEM((tiles, width, tile), bf16),
+            pltpu.VMEM((tiles, 2 * width, tile), bf16),
             pltpu.VMEM((8, model), f32),
-            pltpu.SemaphoreType.DMA((everything + 1,)),
+            pltpu.SemaphoreType.DMA((tiles + 1,)),
+            pltpu.SemaphoreType.DMA((2 * tiles,)),
         ],
         compiler_params=PARAMS,
-        cost_estimate=taking(5.0),
+        cost_estimate=taking(7.0),
         name="own",
-    )(facts, after(attended, before), weight, in_hbm(gate_table))
-
-    finished = []
-    for chunk in range(chunks - 1):
-        there = slice(chunk * columns, (chunk + 1) * columns)
-        summed = sum(part.astype(f32) for part in (projected[:, there], *arrived[chunk]))
-        finished.append((summed * gate[:, there]).astype(bf16))
+    )(facts, after(attended, before), end_rows, weight, in_hbm(end_weight), in_hbm(gate_table))
+
+    summed = sum(part.astype(f32) for part in (projected[:, :columns], *arrived[0]))
+    finished = (summed * gate[:, :columns]).astype(bf16)
     pieces = 2
     return pl.pallas_call(
         final_kernel,
@@ -469,7 +591,7 @@
         compiler_params=PARAMS,
         cost_estimate=taking(2.7),
         name="final",
-    )(jnp.concatenate(finished, axis=1), projected, gate, *arrived[-1])
+    )(finished, projected, gate, *arrived[1])
 
 
 def solution(mesh):

time: 103 us -> 154 us (1.50)
  Pallas kernels: 34.2 us -> 58.2 us
  between operations: 0.57 us -> 13.8 us
  waiting for transfers between devices: 26 us -> 37.1 us
  starting transfers between devices: 38 us -> 39.9 us
    pallas_call x1, Pallas kernels: 1.7 us -> 19.6 us  [body(): pl.pallas_call(functools.partial(split_kernel, spans, ranks), in_specs=[S...]
    all_gather x0 -> x1, waiting for transfers between devices: none -> 12.8 us  [body(): lax.all_gather(after(end_piece, sent), ('group', 'span'), axis=0, tiled=T...]
    ppermute x5, waiting for transfers between devices: 10.8 us -> 2.89 us  [shifted(): lax.ppermute(block, axis, [(i, i + distance) for i in range(count) if 0 <...]
    ppermute x10 -> x11, waiting for transfers between devices: 15.2 us -> 21.4 us  [the longest x1 12 us: body(): end_early = lax.ppermute(early_rows, 'tensor', ends)]
    pallas_call x6 -> x5, Pallas kernels: 16.9 us -> 22.8 us  [the longest x1 8.28 us: body(): pl.pallas_call(functools.partial(own_kernel, spans, ranks), in_specs=[SME...]
    ppermute x5, starting transfers between devices: 10 us -> 13.1 us  [shifted(): lax.ppermute(block, axis, [(i, i + distance) for i in range(count) if 0 <...]
    ppermute x10 -> x11, starting transfers between devices: 27.5 us -> 26.4 us  [the longest x3 12.7 us: exchanged(): lax.ppermute(up, 'tensor', [(i, i + 1) for i in reached])]
  transfers between devices with their start and end apart: 17 -> 19, of which waited for: 7 -> 4; matrix products, arithmetic and copies ran while one was open for 2% -> 2% of each run, Pallas kernels for 33% -> 37%
where the time goes in v11:
time: 154 us; the launch traced here: 153 us
  Pallas kernels  58.2 us (38%)
  starting transfers between devices  39.9 us (26%)
  waiting for transfers between devices  37.1 us (24%)
  between operations  13.8 us (9%)
  other arithmetic  2.94 us (2%)
    pallas_call x1, Pallas kernels, body(): pl.pallas_call(functools.partial(split_kernel, spans, ranks), in_specs=[S...  19.6 us
    ppermute x5, starting transfers between devices, shifted(): lax.ppermute(block, axis, [(i, i + distance) for i in range(count) if 0 <...  13.1 us
    all_gather x1, waiting for transfers between devices, body(): lax.all_gather(after(end_piece, sent), ('group', 'span'), axis=0, tiled=T...  12.8 us
    ppermute x3, starting transfers between devices, exchanged(): lax.ppermute(up, 'tensor', [(i, i + 1) for i in reached])  12.7 us
    ppermute x1, waiting for transfers between devices, body(): end_early = lax.ppermute(early_rows, 'tensor', ends)  12 us
    ppermute x3, waiting for transfers between devices, exchanged(): lax.ppermute(down, 'tensor', [(last - i, last - i - 1) for i in reached])  9.36 us
    pallas_call x2, Pallas kernels, local(): pl.pallas_call(functools.partial(local_kernel, spans, ranks, part), in_sp...  9.04 us
    pallas_call x1, Pallas kernels, body(): pl.pallas_call(functools.partial(own_kernel, spans, ranks), in_specs=[SME...  8.28 us
  transfers between devices with their start and end apart: 19, of which 4 were waited for; matrix products, arithmetic and copies ran while one was open for 2% of the time, Pallas kernels for 37%

profile of v11, /device:TPU:14, one launch (start us, length us, event | category | flops | bytes accessed | tf_op | source)
XLA Modules:
  0.0 152.9 jit_solution(9019906674920331439)
XLA Ops:
  6.5 0.0 collective-permute-start.3
  6.5 0.5 collective-permute-start
  7.1 0.7 pad_add_fusion.facts
  7.8 0.0 copy-start.2
  7.8 19.6 %split.1 = (bf16[96,768]{1,0:T(8,128)(2,1)S(1)}, bf16[192,768]{1,0:T(8,128)(2,1)S(1)}, bf16[96,768]{1,0:T(8,128)(2,1)S(1)}, bf16[96,3072]{1,0:T(8,128)(2,1)}) custom-call(s32[6,4]{1,0:T(8,128)S(1)} %pad_add_fusion.facts, bf16[384,768]{1,0:T(8,128)(2,1)} %query.5, bf16[768,6144]{1,0:T(8,128)(2,1)} %weight.9), custom_call_target="tpu_custom_call" | custom-call | bytes 6273000 | tf_op jit(solution)/shard_map/split/pallas_call | solution.py:413
  27.4 0.0 collective-permute-done.3.key_beside
  27.4 1.3 collective-permute-start.9
  28.7 2.4 %collective-permute-start.4 = (bf16[96,768]{1,0:T(8,128)(2,1)S(1)}, bf16[96,768]{1,0:T(8,128)(2,1)S(1)}, u32[]{:S(2)}, u32[]{:S(2)}) collective-permute-start(bf16[96,768]{1,0:T(8,128)(2,1)S(1)} %get-tuple-element.54), channel_id=1, source_target_pairs={{8,0},{12,4},{9,1},{13,5},{10,2},{14,6},{11,3},{15,7},{24,16},{28,... | collective-permute-start | bytes 442376 | tf_op jit(solution)/shard_map/ppermute | solution.py:32
  31.1 1.3 collective-permute-start.1
  32.5 2.9 %collective-permute-done.4.refs_0_ = bf16[96,768]{1,0:T(8,128)(2,1)S(1)} collective-permute-done((bf16[96,768]{1,0:T(8,128)(2,1)S(1)}, bf16[96,768]{1,0:T(8,128)(2,1)S(1)}, u32[]{:S(2)}, u32[]{:S(2)}) %collective-permute-start.4) | collective-permute-done | bytes 147488 | tf_op jit(solution)/shard_map/ppermute | solution.py:32
  35.3 0.6 served.2
  36.0 1.3 collective-permute-start.5
  37.3 6.8 %collective-permute-start.2 = (bf16[96,768]{1,0:T(8,128)(2,1)S(1)}, bf16[96,768]{1,0:T(8,128)(2,1)S(1)}, u32[]{:S(2)}, u32[]{:S(2)}) collective-permute-start(bf16[96,768]{1,0:T(8,128)(2,1)S(1)} %get-tuple-element.52), channel_id=1, source_target_pairs={{8,0},{12,4},{9,1},{13,5},{10,2},{14,6},{11,3},{15,7},{24,16},{28,... | collective-permute-start | bytes 442376 | tf_op jit(solution)/shard_map/ppermute | solution.py:32
  44.0 4.2 %local.2 = (f32[96,768]{1,0:T(8,128)S(1)}, f32[96,128]{1,0:T(8,128)S(1)}) custom-call(s32[6,4]{1,0:T(8,128)S(1)} %pad_add_fusion.facts, bf16[384,768]{1,0:T(8,128)(2,1)} %query.5, bf16[384,768]{1,0:T(8,128)(2,1)} %key.7, bf16[384,768]{1,0:T(8,128)(2,1)} %value.7, bf16[384,768]{1,0:T(8,128)(2,1)S(1)} %collective-permute-done.3.key_beside, ...), custom_call_target="tpu_custom_call" | custom-call | bytes 14760000 | tf_op jit(solution)/shard_map/local/pallas_call | solution.py:435
  48.3 0.0 copy-start.1
  48.3 0.0 copy-start.3
  48.4 1.0 opening.1
  49.3 0.8 copy-done.4
  50.1 0.0 all-gather.2.cloned.1.call-update
  50.2 1.3 collective-permute-start.8
  51.5 0.6 served.3
  52.1 1.3 collective-permute-start.7
  53.4 1.3 collective-permute-start.6
  54.7 4.8 %local.3 = (f32[288,768]{1,0:T(8,128)S(1)}, f32[288,128]{1,0:T(8,128)S(1)}) custom-call(s32[6,4]{1,0:T(8,128)S(1)} %pad_add_fusion.facts, bf16[384,768]{1,0:T(8,128)(2,1)} %query.5, bf16[384,768]{1,0:T(8,128)(2,1)} %key.7, bf16[384,768]{1,0:T(8,128)(2,1)} %value.7, bf16[384,768]{1,0:T(8,128)(2,1)S(1)} %collective-permute-done.3.key_beside, ...), custom_call_target="tpu_custom_call" | custom-call | bytes 14760000 | tf_op jit(solution)/shard_map/local/pallas_call | solution.py:435
  59.5 12.0 %collective-permute-done.6.end_rows = bf16[96,768]{1,0:T(8,128)(2,1)S(1)} collective-permute-done((bf16[96,768]{1,0:T(8,128)(2,1)S(1)}, bf16[96,768]{1,0:T(8,128)(2,1)S(1)}, u32[]{:S(2)}, u32[]{:S(2)}) %collective-permute-start.6) | collective-permute-done | bytes 147488 | tf_op jit(solution)/shard_map/ppermute | solution.py:491
  71.5 4.4 %merged_blocks.1 = (bf16[384,768]{1,0:T(8,128)(2,1)S(1)}, bf16[96,3072]{1,0:T(8,128)(2,1)S(1)}, bf16[96,3072]{1,0:T(8,128)(2,1)S(1)}) custom-call(s32[6,4]{1,0:T(8,128)S(1)} %pad_add_fusion.facts, f32[96,768]{1,0:T(8,128)S(1)} %get-tuple-element.56.refs_0_, f32[96,128]{1,0:T(8,128)S(1)} %get-tuple-element.57.refs_1_, ...), custom_call_target="tpu_custom_call" | custom-call | bytes 11070000 | tf_op jit(solution)/shard_map/merged_blocks/pallas_call | solution.py:499
  75.9 1.3 fusion.1
  77.2 1.3 collective-permute-start.12
  78.5 4.5 %collective-permute-start.11 = (bf16[96,3072]{1,0:T(8,128)(2,1)}, bf16[96,3072]{1,0:T(8,128)(2,1)S(1)}, u32[]{:S(2)}, u32[]{:S(2)}) collective-permute-start(bf16[96,3072]{1,0:T(8,128)(2,1)} %get-tuple-element.96), channel_id=1, source_target_pairs={{0,1},{1,2},{4,5},{5,6},{8,9},{9,10},{12,13},{13,14},{16,17},{17,1... | collective-permute-start | bytes 1769480 | tf_op jit(solution)/shard_map/ppermute | solution.py:511
  83.1 1.3 collective-permute-start.13
  84.4 12.8 %all-gather.2.cloned.1.call-done.end_weight = bf16[768,3072]{1,0:T(8,128)(2,1)} async-done(((bf16[96,3072]{1,0:T(8,128)(2,1)}), bf16[768,3072]{1,0:T(8,128)(2,1)}) %all-gather.2.cloned.1.call-update) | async-done | bytes 4718608 | tf_op jit(solution)/shard_map/all_gather | solution.py:492
  97.2 5.0 %joint_opening.1 = bf16[96,3072]{1,0:T(8,128)(2,1)S(1)} custom-call(s32[6,4]{1,0:T(8,128)S(1)} %pad_add_fusion.facts, bf16[96,768]{1,0:T(8,128)(2,1)S(1)} %get-tuple-element.72.rows, bf16[96,768]{1,0:T(8,128)(2,1)S(1)} %collective-permute-done.6.end_rows, bf16[768,6144]{1,0:T(8,128)(2,1)} %weight.9, bf16[768,3072]{1,0:T(8,128)(2,1)} %all-gather.2.cloned.1.call-done.end_weight), custom_call_target="tpu_custom_call" | custom-call | bytes 11070000 | tf_op jit(solution)/shard_map/joint_opening/pallas_call | solution.py:538
  102.2 3.4 %collective-permute-start.10 = (bf16[96,3072]{1,0:T(8,128)(2,1)S(1)}, bf16[96,3072]{1,0:T(8,128)(2,1)S(1)}, u32[]{:S(2)}, u32[]{:S(2)}) collective-permute-start(bf16[96,3072]{1,0:T(8,128)(2,1)S(1)} %joint_opening.1), channel_id=1, source_target_pairs={{1,2},{2,1},{5,6},{6,5},{9,10},{10,9},{13,14},{14,13},{17,18},{18,... | collective-permute-start | bytes 1769480 | tf_op jit(solution)/shard_map/ppermute | solution.py:546
  105.6 3.5 %blocks.1 = (bf16[96,3072]{1,0:T(8,128)(2,1)S(1)}, bf16[96,3072]{1,0:T(8,128)(2,1)S(1)}) custom-call(s32[6,4]{1,0:T(8,128)S(1)} %pad_add_fusion.facts, bf16[384,768]{1,0:T(8,128)(2,1)S(1)} %get-tuple-element.90.attended, bf16[768,6144]{1,0:T(8,128)(2,1)} %weight.9), custom_call_target="tpu_custom_call" | custom-call | bytes 11070000 | tf_op jit(solution)/shard_map/blocks/pallas_call | solution.py:525
  109.2 0.1 add_convert_fusion.2
  109.3 1.9 %collective-permute-start.15 = (bf16[96,3072]{1,0:T(8,128)(2,1)S(1)}, bf16[96,3072]{1,0:T(8,128)(2,1)S(1)}, u32[]{:S(2)}, u32[]{:S(2)}) collective-permute-start(bf16[96,3072]{1,0:T(8,128)(2,1)S(1)} %add_convert_fusion.2), channel_id=1, source_target_pairs={{3,2},{2,1},{1,0},{7,6},{6,5},{5,4},{11,10},{10,9},{9,8},{15,14},{... | collective-permute-start | bytes 1769480 | tf_op jit(solution)/shard_map/ppermute | solution.py:512
  111.2 0.1 add_convert_fusion.3
  111.4 3.9 %collective-permute-start.14 = (bf16[96,3072]{1,0:T(8,128)(2,1)S(1)}, bf16[96,3072]{1,0:T(8,128)(2,1)S(1)}, u32[]{:S(2)}, u32[]{:S(2)}) collective-permute-start(bf16[96,3072]{1,0:T(8,128)(2,1)S(1)} %add_convert_fusion.3), channel_id=1, source_target_pairs={{0,1},{1,2},{2,3},{4,5},{5,6},{6,7},{8,9},{9,10},{10,11},{12,13},{... | collective-permute-start | bytes 1769480 | tf_op jit(solution)/shard_map/ppermute | solution.py:511
  115.3 5.1 %joint_blocks.1 = (bf16[96,3072]{1,0:T(8,128)(2,1)S(1)}, bf16[96,3072]{1,0:T(8,128)(2,1)S(1)}) custom-call(s32[6,4]{1,0:T(8,128)S(1)} %pad_add_fusion.facts, bf16[384,768]{1,0:T(8,128)(2,1)S(1)} %get-tuple-element.90.attended, bf16[192,768]{1,0:T(8,128)(2,1)S(1)} %collective-permute-done.13.end_rows, bf16[768,6144]{1,0:T(8,128)(2,1)} %weight.9, ...), custom_call_target="tpu_custom_call" | custom-call | bytes 11070000 | tf_op jit(solution)/shard_map/joint_blocks/pallas_call | solution.py:549
  120.4 0.1 broadcast_select_fusion
  120.5 0.1 add_convert_fusion
  120.7 1.9 %collective-permute-start.17 = (bf16[96,3072]{1,0:T(8,128)(2,1)S(1)}, bf16[96,3072]{1,0:T(8,128)(2,1)S(1)}, u32[]{:S(2)}, u32[]{:S(2)}) collective-permute-start(bf16[96,3072]{1,0:T(8,128)(2,1)S(1)} %add_convert_fusion), channel_id=1, source_target_pairs={{2,1},{1,0},{6,5},{5,4},{10,9},{9,8},{14,13},{13,12},{18,17},{17,1... | collective-permute-start | bytes 1769480 | tf_op jit(solution)/shard_map/ppermute | solution.py:512
  122.6 0.1 add_convert_fusion.1
  122.7 4.2 %collective-permute-start.16 = (bf16[96,3072]{1,0:T(8,128)(2,1)S(1)}, bf16[96,3072]{1,0:T(8,128)(2,1)S(1)}, u32[]{:S(2)}, u32[]{:S(2)}) collective-permute-start(bf16[96,3072]{1,0:T(8,128)(2,1)S(1)} %add_convert_fusion.1), channel_id=1, source_target_pairs={{1,2},{2,3},{5,6},{6,7},{9,10},{10,11},{13,14},{14,15},{17,18},{18... | collective-permute-start | bytes 1769480 | tf_op jit(solution)/shard_map/ppermute | solution.py:511
  127.0 8.3 %own.1 = (bf16[96,6144]{1,0:T(8,128)(2,1)S(1)}, f32[1,6144]{1,0:T(1,128)S(1)}) custom-call(s32[6,4]{1,0:T(8,128)S(1)} %pad_add_fusion.facts, bf16[384,768]{1,0:T(8,128)(2,1)S(1)} %get-tuple-element.90.attended, bf16[192,768]{1,0:T(8,128)(2,1)S(1)} %collective-permute-done.13.end_rows, bf16[768,6144]{1,0:T(8,128)(2,1)} %weight.9, ...), custom_call_target="tpu_custom_call" | custom-call | bytes 25830000 | tf_op jit(solution)/shard_map/own/pallas_call | solution.py:561
  135.3 0.3 multiply_convert_fusion.done
  135.5 9.4 %collective-permute-done.17.down = bf16[96,3072]{1,0:T(8,128)(2,1)S(1)} collective-permute-done((bf16[96,3072]{1,0:T(8,128)(2,1)S(1)}, bf16[96,3072]{1,0:T(8,128)(2,1)S(1)}, u32[]{:S(2)}, u32[]{:S(2)}) %collective-permute-start.17) | collective-permute-done | bytes 589856 | tf_op jit(solution)/shard_map/ppermute | solution.py:512
  144.9 1.1 final.1
  (24 shorter events, 0.1 us)
Async XLA Ops:
  6.5 90.7 %all-gather.2.cloned.1.call-start = ((), (), s32[]{:S(2)}) async-start(), calls=%async_computation | async-start | bytes 5308416 | tf_op jit(solution)/shard_map/all_gather | solution.py:492
  6.5 20.9 %collective-permute-start.3 = (bf16[384,768]{1,0:T(8,128)(2,1)}, bf16[384,768]{1,0:T(8,128)(2,1)S(1)}, u32[]{:S(2)}, u32[]{:S(2)}) collective-permute-start(bf16[384,768]{1,0:T(8,128)(2,1)} %key.7), channel_id=1, source_target_pairs={{0,4},{4,0},{8,12},{12,8},{1,5},{5,1},{9,13},{13,9},{2,6},{6,2},{1... | collective-permute-start | bytes 1769480 | tf_op jit(solution)/shard_map/ppermute | solution.py:427
  6.5 24.6 %collective-permute-start = (bf16[384,768]{1,0:T(8,128)(2,1)}, bf16[384,768]{1,0:T(8,128)(2,1)S(1)}, u32[]{:S(2)}, u32[]{:S(2)}) collective-permute-start(bf16[384,768]{1,0:T(8,128)(2,1)} %value.7), channel_id=1, source_target_pairs={{0,4},{4,0},{8,12},{12,8},{1,5},{5,1},{9,13},{13,9},{2,6},{6,2},{1... | collective-permute-start | bytes 1769480 | tf_op jit(solution)/shard_map/ppermute | solution.py:428
  7.8 27.6 %copy-start = (bf16[384,768]{1,0:T(8,128)(2,1)S(1)}, bf16[384,768]{1,0:T(8,128)(2,1)}, u32[]{:S(2)}) copy-start(bf16[384,768]{1,0:T(8,128)(2,1)} %key.7) | copy-start | bytes 1769476
  7.8 27.6 %copy-start.2 = (bf16[384,768]{1,0:T(8,128)(2,1)S(1)}, bf16[384,768]{1,0:T(8,128)(2,1)}, u32[]{:S(2)}) copy-start(bf16[384,768]{1,0:T(8,128)(2,1)} %value.7) | copy-start | bytes 1769476
  27.4 22.7 %collective-permute-start.9 = (bf16[96,3072]{1,0:T(8,128)(2,1)}, bf16[96,3072]{1,0:T(8,128)(2,1)}, u32[]{:S(2)}, u32[]{:S(2)}) collective-permute-start(bf16[96,3072]{1,0:T(8,128)(2,1)} %get-tuple-element.74), channel_id=1, source_target_pairs={{0,1},{3,2},{4,5},{7,6},{8,9},{11,10},{12,13},{15,14},{16,17},{19,... | collective-permute-start | bytes 1769480 | tf_op jit(solution)/shard_map/ppermute | solution.py:460
  28.7 6.6 %collective-permute-start.4 = (bf16[96,768]{1,0:T(8,128)(2,1)S(1)}, bf16[96,768]{1,0:T(8,128)(2,1)S(1)}, u32[]{:S(2)}, u32[]{:S(2)}) collective-permute-start(bf16[96,768]{1,0:T(8,128)(2,1)S(1)} %get-tuple-element.54), channel_id=1, source_target_pairs={{8,0},{12,4},{9,1},{13,5},{10,2},{14,6},{11,3},{15,7},{24,16},{28,... | collective-permute-start | bytes 442376 | tf_op jit(solution)/shard_map/ppermute | solution.py:32
  31.1 17.2 %collective-permute-start.1 = (bf16[192,768]{1,0:T(8,128)(2,1)S(1)}, bf16[192,768]{1,0:T(8,128)(2,1)S(1)}, u32[]{:S(2)}, u32[]{:S(2)}) collective-permute-start(bf16[192,768]{1,0:T(8,128)(2,1)S(1)} %get-tuple-element.51), channel_id=1, source_target_pairs={{8,0},{12,4},{9,1},{13,5},{10,2},{14,6},{11,3},{15,7},{24,16},{28,... | collective-permute-start | bytes 884744 | tf_op jit(solution)/shard_map/ppermute | solution.py:32
  36.0 12.4 %collective-permute-start.5 = (bf16[96,896]{1,0:T(8,128)(2,1)S(1)}, bf16[96,896]{1,0:T(8,128)(2,1)S(1)}, u32[]{:S(2)}, u32[]{:S(2)}) collective-permute-start(bf16[96,896]{1,0:T(8,128)(2,1)S(1)} %served.2), channel_id=1, source_target_pairs={{0,8},{4,12},{1,9},{5,13},{2,10},{6,14},{3,11},{7,15},{16,24},{20,... | collective-permute-start | bytes 516104 | tf_op jit(solution)/shard_map/ppermute | solution.py:32
  37.3 11.0 %collective-permute-start.2 = (bf16[96,768]{1,0:T(8,128)(2,1)S(1)}, bf16[96,768]{1,0:T(8,128)(2,1)S(1)}, u32[]{:S(2)}, u32[]{:S(2)}) collective-permute-start(bf16[96,768]{1,0:T(8,128)(2,1)S(1)} %get-tuple-element.52), channel_id=1, source_target_pairs={{8,0},{12,4},{9,1},{13,5},{10,2},{14,6},{11,3},{15,7},{24,16},{28,... | collective-permute-start | bytes 442376 | tf_op jit(solution)/shard_map/ppermute | solution.py:32
  48.3 3.1 %copy-start.1 = (bf16[384,768]{1,0:T(8,128)(2,1)S(1)}, bf16[384,768]{1,0:T(8,128)(2,1)}, u32[]{:S(2)}) copy-start(bf16[384,768]{1,0:T(8,128)(2,1)} %key.7) | copy-start | bytes 1769476
  48.3 3.1 %copy-start.3 = (bf16[384,768]{1,0:T(8,128)(2,1)S(1)}, bf16[384,768]{1,0:T(8,128)(2,1)}, u32[]{:S(2)}) copy-start(bf16[384,768]{1,0:T(8,128)(2,1)} %value.7) | copy-start | bytes 1769476
  49.3 0.8 copy-start.4
  50.2 25.7 %collective-permute-start.8 = (bf16[96,3072]{1,0:T(8,128)(2,1)}, bf16[96,3072]{1,0:T(8,128)(2,1)S(1)}, u32[]{:S(2)}, u32[]{:S(2)}) collective-permute-start(bf16[96,3072]{1,0:T(8,128)(2,1)} %copy-done.4), channel_id=1, source_target_pairs={{0,1},{3,2},{4,5},{7,6},{8,9},{11,10},{12,13},{15,14},{16,17},{19,... | collective-permute-start | bytes 1769480 | tf_op jit(solution)/shard_map/ppermute | solution.py:490
  52.1 19.4 %collective-permute-start.7 = (bf16[288,896]{1,0:T(8,128)(2,1)S(1)}, bf16[288,896]{1,0:T(8,128)(2,1)S(1)}, u32[]{:S(2)}, u32[]{:S(2)}) collective-permute-start(bf16[288,896]{1,0:T(8,128)(2,1)S(1)} %served.3), channel_id=1, source_target_pairs={{0,8},{4,12},{1,9},{5,13},{2,10},{6,14},{3,11},{7,15},{16,24},{20,... | collective-permute-start | bytes 1548296 | tf_op jit(solution)/shard_map/ppermute | solution.py:32
  53.4 18.1 %collective-permute-start.6 = (bf16[96,768]{1,0:T(8,128)(2,1)S(1)}, bf16[96,768]{1,0:T(8,128)(2,1)S(1)}, u32[]{:S(2)}, u32[]{:S(2)}) collective-permute-start(bf16[96,768]{1,0:T(8,128)(2,1)S(1)} %get-tuple-element.72.rows), channel_id=1, source_target_pairs={{0,1},{3,2},{4,5},{7,6},{8,9},{11,10},{12,13},{15,14},{16,17},{19,... | collective-permute-start | bytes 442376 | tf_op jit(solution)/shard_map/ppermute | solution.py:491
  77.2 31.9 %collective-permute-start.12 = (bf16[96,3072]{1,0:T(8,128)(2,1)}, bf16[96,3072]{1,0:T(8,128)(2,1)S(1)}, u32[]{:S(2)}, u32[]{:S(2)}) collective-permute-start(bf16[96,3072]{1,0:T(8,128)(2,1)} %get-tuple-element.95), channel_id=1, source_target_pairs={{3,2},{2,1},{7,6},{6,5},{11,10},{10,9},{15,14},{14,13},{19,18},{18... | collective-permute-start | bytes 1769480 | tf_op jit(solution)/shard_map/ppermute | solution.py:512
  78.5 30.7 %collective-permute-start.11 = (bf16[96,3072]{1,0:T(8,128)(2,1)}, bf16[96,3072]{1,0:T(8,128)(2,1)S(1)}, u32[]{:S(2)}, u32[]{:S(2)}) collective-permute-start(bf16[96,3072]{1,0:T(8,128)(2,1)} %get-tuple-element.96), channel_id=1, source_target_pairs={{0,1},{1,2},{4,5},{5,6},{8,9},{9,10},{12,13},{13,14},{16,17},{17,1... | collective-permute-start | bytes 1769480 | tf_op jit(solution)/shard_map/ppermute | solution.py:511
  83.1 32.2 %collective-permute-start.13 = (bf16[192,768]{1,0:T(8,128)(2,1)S(1)}, bf16[192,768]{1,0:T(8,128)(2,1)S(1)}, u32[]{:S(2)}, u32[]{:S(2)}) collective-permute-start(bf16[192,768]{1,0:T(8,128)(2,1)S(1)} %slice.9), channel_id=1, source_target_pairs={{0,1},{3,2},{4,5},{7,6},{8,9},{11,10},{12,13},{15,14},{16,17},{19,... | collective-permute-start | bytes 884744 | tf_op jit(solution)/shard_map/ppermute | solution.py:537
  102.2 18.2 %collective-permute-start.10 = (bf16[96,3072]{1,0:T(8,128)(2,1)S(1)}, bf16[96,3072]{1,0:T(8,128)(2,1)S(1)}, u32[]{:S(2)}, u32[]{:S(2)}) collective-permute-start(bf16[96,3072]{1,0:T(8,128)(2,1)S(1)} %joint_opening.1), channel_id=1, source_target_pairs={{1,2},{2,1},{5,6},{6,5},{9,10},{10,9},{13,14},{14,13},{17,18},{18,... | collective-permute-start | bytes 1769480 | tf_op jit(solution)/shard_map/ppermute | solution.py:546
  109.3 25.9 %collective-permute-start.15 = (bf16[96,3072]{1,0:T(8,128)(2,1)S(1)}, bf16[96,3072]{1,0:T(8,128)(2,1)S(1)}, u32[]{:S(2)}, u32[]{:S(2)}) collective-permute-start(bf16[96,3072]{1,0:T(8,128)(2,1)S(1)} %add_convert_fusion.2), channel_id=1, source_target_pairs={{3,2},{2,1},{1,0},{7,6},{6,5},{5,4},{11,10},{10,9},{9,8},{15,14},{... | collective-permute-start | bytes 1769480 | tf_op jit(solution)/shard_map/ppermute | solution.py:512
  111.4 23.9 %collective-permute-start.14 = (bf16[96,3072]{1,0:T(8,128)(2,1)S(1)}, bf16[96,3072]{1,0:T(8,128)(2,1)S(1)}, u32[]{:S(2)}, u32[]{:S(2)}) collective-permute-start(bf16[96,3072]{1,0:T(8,128)(2,1)S(1)} %add_convert_fusion.3), channel_id=1, source_target_pairs={{0,1},{1,2},{2,3},{4,5},{5,6},{6,7},{8,9},{9,10},{10,11},{12,13},{... | collective-permute-start | bytes 1769480 | tf_op jit(solution)/shard_map/ppermute | solution.py:511
  120.7 24.2 %collective-permute-start.17 = (bf16[96,3072]{1,0:T(8,128)(2,1)S(1)}, bf16[96,3072]{1,0:T(8,128)(2,1)S(1)}, u32[]{:S(2)}, u32[]{:S(2)}) collective-permute-start(bf16[96,3072]{1,0:T(8,128)(2,1)S(1)} %add_convert_fusion), channel_id=1, source_target_pairs={{2,1},{1,0},{6,5},{5,4},{10,9},{9,8},{14,13},{13,12},{18,17},{17,1... | collective-permute-start | bytes 1769480 | tf_op jit(solution)/shard_map/ppermute | solution.py:512
  122.7 22.2 %collective-permute-start.16 = (bf16[96,3072]{1,0:T(8,128)(2,1)S(1)}, bf16[96,3072]{1,0:T(8,128)(2,1)S(1)}, u32[]{:S(2)}, u32[]{:S(2)}) collective-permute-start(bf16[96,3072]{1,0:T(8,128)(2,1)S(1)} %add_convert_fusion.1), channel_id=1, source_target_pairs={{1,2},{2,3},{5,6},{6,7},{9,10},{10,11},{13,14},{14,15},{17,18},{18... | collective-permute-start | bytes 1769480 | tf_op jit(solution)/shard_map/ppermute | solution.py:511
Sparse Core Ops, SparseCore 0:
  50.3 46.8 all-gather.1

commit v12 on v10

--- a/solution.py
+++ b/solution.py
@@ -41,13 +41,21 @@
     scale = LOG2E * HD ** (-0.5)
     lane = lax.broadcasted_iota(jnp.int32, (rows, LANES), 1)
     packed = jnp.zeros((rows, LANES), jnp.float32)
-    for head in range(width // HD):
+
+    def scored(head):
         columns = head_columns(head)
-        mine = query[:, columns]
-        scores = [
-            lax.dot_general(mine, key[:, columns], (((1,), (1,)), ((), ())), preferred_element_type=jnp.float32)
+        return [
+            lax.dot_general(
+                query[:, columns], key[:, columns], (((1,), (1,)), ((), ())), preferred_element_type=jnp.float32
+            )
             for key in keys
         ]
+
+    heads = width // HD
+    later = scored(0)
+    for head in range(heads):
+        columns = head_columns(head)
+        scores, later = later, scored(head + 1) if head + 1 < heads else None
         tops = [jnp.max(block, axis=-1, keepdims=True) * scale for block in scores]
         top = functools.reduce(
             jnp.maximum, [one if flag is None else jnp.where(flag, one, HIDDEN) for one, flag in zip(tops, flags)]
@@ -92,25 +100,44 @@
     return (early, block), (late, rows - block)
 
 
-def split_kernel(spans, ranks, facts, query, *refs):
-    here = Facts(facts, spans)
+def split_kernel(ranks, part, place, query, *refs):
     *targets, semaphores = refs
 
-    @pl.when(here.span > 1)
+    @pl.when(place[0] > 1)
     def _():
-        (early, _), (late, _) = parts_of(here.rank, ranks, query.shape[0])
-        starts = (early, late, pl.multiple_of(late + targets[1].shape[0], 16))
-        copies = [
-            copied(query.at[pl.ds(start, target.shape[0])], target, semaphores.at[index])
-            for index, (start, target) in enumerate(zip(starts, targets))
-        ]
+        start, _ = parts_of(place[1], ranks, query.shape[0])[part]
+        copies = []
+        for index, target in enumerate(targets):
+            size = target.shape[0]
+            copies.append(copied(query.at[pl.ds(pl.multiple_of(start, 16), size)], target, semaphores.at[index]))
+            start = start + size
         for copy in copies:
             copy.wait()
 
 
-def local_kernel(spans, ranks, part, facts, query, key, value, key_beside, value_beside, result, sums, *scratch):
+def local_kernel(spans, ranks, part, who, facts, query, key, value, key_beside, value_beside, *refs):
     here = Facts(facts, spans)
-    query_, key_, value_, key_beside_, value_beside_, semaphores = scratch
+    if who is None:
+        attend_here(here, ranks, part, query, key, value, key_beside, value_beside, *refs)
+        return
+
+    mine = here.span > 1 if who == "askers" else here.span < 2
+
+    @pl.when(mine)
+    def _():
+        attend_here(here, ranks, part, query, key, value, key_beside, value_beside, *refs)
+
+    *before, result, sums = refs[:-6]
+    if before:
+
+        @pl.when(jnp.logical_not(mine))
+        def _():
+            result[...] = before[0][...]
+            sums[...] = before[1][...]
+
+
+def attend_here(here, ranks, part, query, key, value, key_beside, value_beside, *refs):
+    result, sums, query_, key_, value_, key_beside_, value_beside_, semaphores = refs[-8:]
     start, size = parts_of(here.rank, ranks, query.shape[0])[part]
     copies = [
         copied(source, target, semaphores.at[index])
@@ -307,16 +334,21 @@
     facts = jnp.concatenate([visible, place[None, :], levels[None, :]], axis=0)
 
     third = (rows - block) // 48 * 16
-    query_early, *query_late = pl.pallas_call(
-        functools.partial(split_kernel, spans, ranks),
-        in_specs=[SMEM, HBM],
-        out_specs=[VMEM] * 3,
-        out_shape=[jax.ShapeDtypeStruct((part, width), bf16) for part in (block, rows - block - third, third)],
-        scratch_shapes=[pltpu.SemaphoreType.DMA((3,))],
-        compiler_params=PARAMS,
-        cost_estimate=taking(1.7),
-        name="split",
-    )(facts, in_hbm(queries))
+    here = jnp.stack([span, rank]).astype(jnp.int32)
+
+    def split(part, place, sizes):
+        return pl.pallas_call(
+            functools.partial(split_kernel, ranks, part),
+            in_specs=[SMEM, HBM],
+            out_specs=[VMEM] * len(sizes),
+            out_shape=[jax.ShapeDtypeStruct((size, width), bf16) for size in sizes],
+            scratch_shapes=[pltpu.SemaphoreType.DMA((len(sizes),))],
+            compiler_params=PARAMS,
+            cost_estimate=taking(1.0),
+            name="split",
+        )(place, in_hbm(queries))
+
+    query_early, = split(0, here, [block])
     distances = list(range(2, spans, 2))
     asked_early = [shifted(query_early, "span", -distance) for distance in distances]
     swap = [(i, i + 1 - 2 * (i % 2)) for i in range(spans)]
@@ -326,11 +358,11 @@
     def after(value, *others):
         return lax.optimization_barrier((value, others))[0]
 
-    def local(part, facts):
+    def local(part, facts, who=None, before=()):
         size = (block, rows - block)[part]
-        return pl.pallas_call(
-            functools.partial(local_kernel, spans, ranks, part),
-            in_specs=[SMEM, HBM, HBM, HBM, ANY, ANY],
+        return list(pl.pallas_call(
+            functools.partial(local_kernel, spans, ranks, part, who),
+            in_specs=[SMEM, HBM, HBM, HBM, ANY, ANY] + [VMEM] * len(before),
             out_specs=[VMEM] * 2,
             out_shape=[jax.ShapeDtypeStruct((size, width), f32), jax.ShapeDtypeStruct((size, LANES), f32)],
             scratch_shapes=[pltpu.VMEM((size, width), bf16)] + [pltpu.VMEM((rows, width), bf16)] * 4
@@ -338,7 +370,7 @@
             compiler_params=PARAMS,
             cost_estimate=taking(4.0),
             name="local",
-        )(facts, in_hbm(queries), in_hbm(keys), in_hbm(values), key_beside, value_beside)
+        )(facts, in_hbm(queries), in_hbm(keys), in_hbm(values), key_beside, value_beside, *before))
 
     def served(asked, distance):
         return pl.pallas_call(
@@ -352,11 +384,12 @@
             name="served",
         )(facts, keys, values, key_beside, value_beside, *asked)
 
-    early = list(local(0, facts))
-    query_late = after(query_late, early)
-    asked_early = after(asked_early, early)
+    early = local(0, facts, "others")
+    query_late = split(1, after(here, early), [rows - block - third, third])
     asked_late = [[shifted(query, "span", -distance) for query in query_late] for distance in distances]
-    early += [shifted(served([q], d), "span", d) for q, d in zip(asked_early, distances)]
+    out_early = [served([q], d) for q, d in zip(after(asked_early, early), distances)]
+    early = local(0, after(facts, out_early), "askers", early)
+    early += [shifted(o, "span", d) for o, d in zip(out_early, distances)]
 
     chunks = 2
     columns = model // chunks
@@ -372,9 +405,9 @@
             out_specs=VMEM,
             out_shape=jax.ShapeDtypeStruct((block, columns), bf16),
             scratch_shapes=[
-                pltpu.VMEM((tiles, width, tile), bf16),
+                pltpu.VMEM((2 * tiles, width, tile // 2), bf16),
                 pltpu.VMEM((block, width), bf16),
-                pltpu.SemaphoreType.DMA((tiles,)),
+                pltpu.SemaphoreType.DMA((2 * tiles,)),
             ],
             compiler_params=PARAMS,
             cost_estimate=taking(3.4),
@@ -388,7 +421,7 @@
     for chunk in range(1, chunks):
         sent = opening(chunk, after(facts, out_late))
         arrived.append([lax.ppermute(sent, "tensor", ends)])
-    late = list(local(1, after(facts, sent)))
+    late = local(1, after(facts, sent))
     late += [shifted(o, "span", d) for o, d in zip(out_late, distances)]
 
     streaming = dict(

time: 103 us -> 104 us (level)
  starting transfers between devices: 38 us -> 40.4 us
  waiting for transfers between devices: 26 us -> 24.2 us
    ppermute x5, waiting for transfers between devices: 10.8 us -> 6.94 us  [shifted(): lax.ppermute(block, axis, [(i, i + distance) for i in range(count) if 0 <...]
    ppermute x4, waiting for transfers between devices: 7.98 us -> 11.3 us  [body(): lax.ppermute(up, 'tensor', [(i, i + 1) for i in range(step + 1)])]
    ppermute x4, waiting for transfers between devices: 7.21 us -> 4.54 us  [body(): lax.ppermute(down, 'tensor', [(last - i, last - i - 1) for i in range(ste...]
    ppermute x5, starting transfers between devices: 10 us -> 11.7 us  [shifted(): lax.ppermute(block, axis, [(i, i + distance) for i in range(count) if 0 <...]
    ppermute x1, waiting for transfers between devices: 0.01 us -> 1.38 us  [body(): arrived.append([lax.ppermute(sent, 'tensor', ends)])]
    pallas_call x3 -> x5, Pallas kernels: 10.7 us -> 11.4 us  [the longest x3 8.36 us: local(): pl.pallas_call(functools.partial(local_kernel, spans, ranks, part, who),...]
where the time goes in v12:
time: 104 us; the launch traced here: 102 us
  starting transfers between devices  40.4 us (39%)
  Pallas kernels  34.9 us (34%)
  waiting for transfers between devices  24.2 us (23%)
  other arithmetic  2.22 us (2%)
    ppermute x4, starting transfers between devices, body(): lax.ppermute(up, 'tensor', [(i, i + 1) for i in range(step + 1)])  19 us
    ppermute x5, starting transfers between devices, shifted(): lax.ppermute(block, axis, [(i, i + distance) for i in range(count) if 0 <...  11.7 us
    ppermute x4, waiting for transfers between devices, body(): lax.ppermute(up, 'tensor', [(i, i + 1) for i in range(step + 1)])  11.3 us
    pallas_call x3, Pallas kernels, blocks_of(): pl.pallas_call(functools.partial(blocks_kernel, spans, ranks, chunk * col...  10.6 us
    pallas_call x3, Pallas kernels, local(): pl.pallas_call(functools.partial(local_kernel, spans, ranks, part, who),...  8.36 us
    ppermute x5, waiting for transfers between devices, shifted(): lax.ppermute(block, axis, [(i, i + distance) for i in range(count) if 0 <...  6.94 us
    ppermute x4, starting transfers between devices, body(): lax.ppermute(down, 'tensor', [(last - i, last - i - 1) for i in range(ste...  6.43 us
    pallas_call x1, Pallas kernels, body(): pl.pallas_call(functools.partial(own_kernel, spans), in_specs=[SMEM, VMEM...  5.05 us
  transfers between devices with their start and end apart: 17, of which 7 were waited for; matrix products, arithmetic and copies ran while one was open for 2% of the time, Pallas kernels for 33%

profile of v12, /device:TPU:14, one launch (start us, length us, event | category | flops | bytes accessed | tf_op | source)
XLA Modules:
  0.0 102.4 jit_solution(18254265178926684580)
XLA Ops:
  0.0 0.5 collective-permute-start.1
  0.5 0.1 pad_add_fusion.1.place
  0.6 1.5 %split.2 = bf16[96,768]{1,0:T(8,128)(2,1)S(1)} custom-call(s32[2]{0:T(128)S(1)} %pad_add_fusion.1.place, bf16[384,768]{1,0:T(8,128)(2,1)} %query.9), custom_call_target="tpu_custom_call" | custom-call | bytes 3690000 | tf_op jit(solution)/shard_map/split/pallas_call | solution.py:340
  2.1 1.5 %collective-permute-start.2 = (bf16[96,768]{1,0:T(8,128)(2,1)S(1)}, bf16[96,768]{1,0:T(8,128)(2,1)S(1)}, u32[]{:S(2)}, u32[]{:S(2)}) collective-permute-start(bf16[96,768]{1,0:T(8,128)(2,1)S(1)} %split.2), channel_id=1, source_target_pairs={{8,0},{12,4},{9,1},{13,5},{10,2},{14,6},{11,3},{15,7},{24,16},{28,... | collective-permute-start | bytes 442376 | tf_op jit(solution)/shard_map/ppermute | solution.py:32
  3.6 0.7 pad_add_fusion.facts
  4.3 0.7 local.3
  5.0 1.6 %split.3 = (bf16[192,768]{1,0:T(8,128)(2,1)S(1)}, bf16[96,768]{1,0:T(8,128)(2,1)S(1)}) custom-call(s32[2]{0:T(128)S(1)} %pad_add_fusion.1.place, bf16[384,768]{1,0:T(8,128)(2,1)} %query.9), custom_call_target="tpu_custom_call" | custom-call | bytes 3690000 | tf_op jit(solution)/shard_map/split/pallas_call | solution.py:340
  6.6 3.1 %collective-permute-start.4 = (bf16[192,768]{1,0:T(8,128)(2,1)S(1)}, bf16[192,768]{1,0:T(8,128)(2,1)S(1)}, u32[]{:S(2)}, u32[]{:S(2)}) collective-permute-start(bf16[192,768]{1,0:T(8,128)(2,1)S(1)} %get-tuple-element.56), channel_id=1, source_target_pairs={{8,0},{12,4},{9,1},{13,5},{10,2},{14,6},{11,3},{15,7},{24,16},{28,... | collective-permute-start | bytes 884744 | tf_op jit(solution)/shard_map/ppermute | solution.py:32
  9.7 0.6 served.2
  10.3 1.3 %collective-permute-start.3 = (bf16[96,896]{1,0:T(8,128)(2,1)S(1)}, bf16[96,896]{1,0:T(8,128)(2,1)S(1)}, u32[]{:S(2)}, u32[]{:S(2)}) collective-permute-start(bf16[96,896]{1,0:T(8,128)(2,1)S(1)} %served.2), channel_id=1, source_target_pairs={{0,8},{4,12},{1,9},{5,13},{2,10},{6,14},{3,11},{7,15},{16,24},{20,... | collective-permute-start | bytes 516104 | tf_op jit(solution)/shard_map/ppermute | solution.py:32
  11.6 4.6 %collective-permute-start.5 = (bf16[96,768]{1,0:T(8,128)(2,1)S(1)}, bf16[96,768]{1,0:T(8,128)(2,1)S(1)}, u32[]{:S(2)}, u32[]{:S(2)}) collective-permute-start(bf16[96,768]{1,0:T(8,128)(2,1)S(1)} %get-tuple-element.57), channel_id=1, source_target_pairs={{8,0},{12,4},{9,1},{13,5},{10,2},{14,6},{11,3},{15,7},{24,16},{28,... | collective-permute-start | bytes 442376 | tf_op jit(solution)/shard_map/ppermute | solution.py:32
  16.2 3.4 %local.4 = (f32[96,768]{1,0:T(8,128)S(1)}, f32[96,128]{1,0:T(8,128)S(1)}) custom-call(s32[6,4]{1,0:T(8,128)S(1)} %pad_add_fusion.facts, bf16[384,768]{1,0:T(8,128)(2,1)} %query.9, bf16[384,768]{1,0:T(8,128)(2,1)} %key.9, bf16[384,768]{1,0:T(8,128)(2,1)} %value.9, bf16[384,768]{1,0:T(8,128)(2,1)S(1)} %collective-permute-done.key_beside, ...), custom_call_target="tpu_custom_call" | custom-call | bytes 14760000 | tf_op jit(solution)/shard_map/local/pallas_call | solution.py:363
  19.6 0.0 copy-start.3
  19.6 0.7 opening.2
  20.3 1.3 %collective-permute-start.8 = (bf16[96,3072]{1,0:T(8,128)(2,1)S(1)}, bf16[96,3072]{1,0:T(8,128)(2,1)S(1)}, u32[]{:S(2)}, u32[]{:S(2)}) collective-permute-start(bf16[96,3072]{1,0:T(8,128)(2,1)S(1)} %opening.2), channel_id=1, source_target_pairs={{0,1},{3,2},{4,5},{7,6},{8,9},{11,10},{12,13},{15,14},{16,17},{19,... | collective-permute-start | bytes 1769480 | tf_op jit(solution)/shard_map/ppermute | solution.py:419
  21.6 0.6 served.3
  22.3 1.3 %collective-permute-start.6 = (bf16[288,896]{1,0:T(8,128)(2,1)S(1)}, bf16[288,896]{1,0:T(8,128)(2,1)S(1)}, u32[]{:S(2)}, u32[]{:S(2)}) collective-permute-start(bf16[288,896]{1,0:T(8,128)(2,1)S(1)} %served.3), channel_id=1, source_target_pairs={{0,8},{4,12},{1,9},{5,13},{2,10},{6,14},{3,11},{7,15},{16,24},{20,... | collective-permute-start | bytes 1548296 | tf_op jit(solution)/shard_map/ppermute | solution.py:32
  23.6 0.7 opening.3
  24.2 1.5 %collective-permute-start.7 = (bf16[96,3072]{1,0:T(8,128)(2,1)S(1)}, bf16[96,3072]{1,0:T(8,128)(2,1)S(1)}, u32[]{:S(2)}, u32[]{:S(2)}) collective-permute-start(bf16[96,3072]{1,0:T(8,128)(2,1)S(1)} %opening.3), channel_id=1, source_target_pairs={{0,1},{3,2},{4,5},{7,6},{8,9},{11,10},{12,13},{15,14},{16,17},{19,... | collective-permute-start | bytes 1769480 | tf_op jit(solution)/shard_map/ppermute | solution.py:423
  25.7 4.3 %local.5 = (f32[288,768]{1,0:T(8,128)S(1)}, f32[288,128]{1,0:T(8,128)S(1)}) custom-call(s32[6,4]{1,0:T(8,128)S(1)} %pad_add_fusion.facts, bf16[384,768]{1,0:T(8,128)(2,1)} %query.9, bf16[384,768]{1,0:T(8,128)(2,1)} %key.9, bf16[384,768]{1,0:T(8,128)(2,1)} %value.9, bf16[384,768]{1,0:T(8,128)(2,1)S(1)} %collective-permute-done.key_beside, ...), custom_call_target="tpu_custom_call" | custom-call | bytes 14760000 | tf_op jit(solution)/shard_map/local/pallas_call | solution.py:363
  30.0 6.9 %collective-permute-done.6.refs_5_ = bf16[288,896]{1,0:T(8,128)(2,1)S(1)} collective-permute-done((bf16[288,896]{1,0:T(8,128)(2,1)S(1)}, bf16[288,896]{1,0:T(8,128)(2,1)S(1)}, u32[]{:S(2)}, u32[]{:S(2)}) %collective-permute-start.6) | collective-permute-done | bytes 516128 | tf_op jit(solution)/shard_map/ppermute | solution.py:32
  37.0 4.3 %merged_blocks.1 = (bf16[384,768]{1,0:T(8,128)(2,1)S(1)}, bf16[96,3072]{1,0:T(8,128)(2,1)S(1)}, bf16[96,3072]{1,0:T(8,128)(2,1)S(1)}) custom-call(s32[6,4]{1,0:T(8,128)S(1)} %pad_add_fusion.facts, f32[96,768]{1,0:T(8,128)S(1)} %get-tuple-element.53.refs_0_, f32[96,128]{1,0:T(8,128)S(1)} %get-tuple-element.54.refs_1_, ...), custom_call_target="tpu_custom_call" | custom-call | bytes 11070000 | tf_op jit(solution)/shard_map/merged_blocks/pallas_call | solution.py:434
  41.3 0.3 fusion.1
  41.6 1.3 %collective-permute-start.12 = (bf16[96,3072]{1,0:T(8,128)(2,1)S(1)}, bf16[96,3072]{1,0:T(8,128)(2,1)S(1)}, u32[]{:S(2)}, u32[]{:S(2)}) collective-permute-start(bf16[96,3072]{1,0:T(8,128)(2,1)S(1)} %get-tuple-element.95), channel_id=1, source_target_pairs={{3,2},{2,1},{7,6},{6,5},{11,10},{10,9},{15,14},{14,13},{19,18},{18... | collective-permute-start | bytes 1769480 | tf_op jit(solution)/shard_map/ppermute | solution.py:468
  42.9 4.6 %collective-permute-start.11 = (bf16[96,3072]{1,0:T(8,128)(2,1)S(1)}, bf16[96,3072]{1,0:T(8,128)(2,1)S(1)}, u32[]{:S(2)}, u32[]{:S(2)}) collective-permute-start(bf16[96,3072]{1,0:T(8,128)(2,1)S(1)} %get-tuple-element.96), channel_id=1, source_target_pairs={{0,1},{1,2},{4,5},{5,6},{8,9},{9,10},{12,13},{13,14},{16,17},{17,1... | collective-permute-start | bytes 1769480 | tf_op jit(solution)/shard_map/ppermute | solution.py:467
  47.4 3.3 %blocks.3 = (bf16[96,3072]{1,0:T(8,128)(2,1)S(1)}, bf16[96,3072]{1,0:T(8,128)(2,1)S(1)}) custom-call(s32[6,4]{1,0:T(8,128)S(1)} %pad_add_fusion.facts, bf16[384,768]{1,0:T(8,128)(2,1)S(1)} %get-tuple-element.90.attended, bf16[768,6144]{1,0:T(8,128)(2,1)} %weight.7), custom_call_target="tpu_custom_call" | custom-call | bytes 11070000 | tf_op jit(solution)/shard_map/blocks/pallas_call | solution.py:444
  50.7 1.4 %collective-permute-done.7 = bf16[96,3072]{1,0:T(8,128)(2,1)S(1)} collective-permute-done((bf16[96,3072]{1,0:T(8,128)(2,1)S(1)}, bf16[96,3072]{1,0:T(8,128)(2,1)S(1)}, u32[]{:S(2)}, u32[]{:S(2)}) %collective-permute-start.7) | collective-permute-done | bytes 589856 | tf_op jit(solution)/shard_map/ppermute | solution.py:423
  52.1 0.3 fusion.3
  52.4 1.3 %collective-permute-start.10 = (bf16[96,3072]{1,0:T(8,128)(2,1)S(1)}, bf16[96,3072]{1,0:T(8,128)(2,1)S(1)}, u32[]{:S(2)}, u32[]{:S(2)}) collective-permute-start(bf16[96,3072]{1,0:T(8,128)(2,1)S(1)} %get-tuple-element.93), channel_id=1, source_target_pairs={{3,2},{2,1},{7,6},{6,5},{11,10},{10,9},{15,14},{14,13},{19,18},{18... | collective-permute-start | bytes 1769480 | tf_op jit(solution)/shard_map/ppermute | solution.py:468
  53.7 5.2 %collective-permute-start.9 = (bf16[96,3072]{1,0:T(8,128)(2,1)S(1)}, bf16[96,3072]{1,0:T(8,128)(2,1)S(1)}, u32[]{:S(2)}, u32[]{:S(2)}) collective-permute-start(bf16[96,3072]{1,0:T(8,128)(2,1)S(1)} %get-tuple-element.94), channel_id=1, source_target_pairs={{0,1},{1,2},{4,5},{5,6},{8,9},{9,10},{12,13},{13,14},{16,17},{17,1... | collective-permute-start | bytes 1769480 | tf_op jit(solution)/shard_map/ppermute | solution.py:467
  59.0 3.5 %blocks.4 = (bf16[96,3072]{1,0:T(8,128)(2,1)S(1)}, bf16[96,3072]{1,0:T(8,128)(2,1)S(1)}) custom-call(s32[6,4]{1,0:T(8,128)S(1)} %pad_add_fusion.facts, bf16[384,768]{1,0:T(8,128)(2,1)S(1)} %get-tuple-element.90.attended, bf16[768,6144]{1,0:T(8,128)(2,1)} %weight.7), custom_call_target="tpu_custom_call" | custom-call | bytes 11070000 | tf_op jit(solution)/shard_map/blocks/pallas_call | solution.py:444
  62.5 2.3 %collective-permute-done.11 = bf16[96,3072]{1,0:T(8,128)(2,1)S(1)} collective-permute-done((bf16[96,3072]{1,0:T(8,128)(2,1)S(1)}, bf16[96,3072]{1,0:T(8,128)(2,1)S(1)}, u32[]{:S(2)}, u32[]{:S(2)}) %collective-permute-start.11) | collective-permute-done | bytes 589856 | tf_op jit(solution)/shard_map/ppermute | solution.py:467
  64.8 0.1 add_convert_fusion.2
  64.9 1.9 %collective-permute-start.14 = (bf16[96,3072]{1,0:T(8,128)(2,1)S(1)}, bf16[96,3072]{1,0:T(8,128)(2,1)S(1)}, u32[]{:S(2)}, u32[]{:S(2)}) collective-permute-start(bf16[96,3072]{1,0:T(8,128)(2,1)S(1)} %add_convert_fusion.2), channel_id=1, source_target_pairs={{3,2},{2,1},{1,0},{7,6},{6,5},{5,4},{11,10},{10,9},{9,8},{15,14},{... | collective-permute-start | bytes 1769480 | tf_op jit(solution)/shard_map/ppermute | solution.py:468
  66.9 0.1 add_convert_fusion.3
  67.0 4.6 %collective-permute-start.13 = (bf16[96,3072]{1,0:T(8,128)(2,1)S(1)}, bf16[96,3072]{1,0:T(8,128)(2,1)S(1)}, u32[]{:S(2)}, u32[]{:S(2)}) collective-permute-start(bf16[96,3072]{1,0:T(8,128)(2,1)S(1)} %add_convert_fusion.3), channel_id=1, source_target_pairs={{0,1},{1,2},{2,3},{4,5},{5,6},{6,7},{8,9},{9,10},{10,11},{12,13},{... | collective-permute-start | bytes 1769480 | tf_op jit(solution)/shard_map/ppermute | solution.py:467
  71.6 3.7 %blocks.5 = (bf16[96,3072]{1,0:T(8,128)(2,1)S(1)}, bf16[96,3072]{1,0:T(8,128)(2,1)S(1)}) custom-call(s32[6,4]{1,0:T(8,128)S(1)} %pad_add_fusion.facts, bf16[384,768]{1,0:T(8,128)(2,1)S(1)} %get-tuple-element.90.attended, bf16[768,6144]{1,0:T(8,128)(2,1)} %weight.7), custom_call_target="tpu_custom_call" | custom-call | bytes 11070000 | tf_op jit(solution)/shard_map/blocks/pallas_call | solution.py:444
  75.4 2.0 %collective-permute-done.9 = bf16[96,3072]{1,0:T(8,128)(2,1)S(1)} collective-permute-done((bf16[96,3072]{1,0:T(8,128)(2,1)S(1)}, bf16[96,3072]{1,0:T(8,128)(2,1)S(1)}, u32[]{:S(2)}, u32[]{:S(2)}) %collective-permute-start.9) | collective-permute-done | bytes 589856 | tf_op jit(solution)/shard_map/ppermute | solution.py:467
  77.4 0.2 add_convert_fusion
  77.6 1.9 %collective-permute-start.16 = (bf16[96,3072]{1,0:T(8,128)(2,1)S(1)}, bf16[96,3072]{1,0:T(8,128)(2,1)S(1)}, u32[]{:S(2)}, u32[]{:S(2)}) collective-permute-start(bf16[96,3072]{1,0:T(8,128)(2,1)S(1)} %add_convert_fusion), channel_id=1, source_target_pairs={{3,2},{2,1},{1,0},{7,6},{6,5},{5,4},{11,10},{10,9},{9,8},{15,14},{... | collective-permute-start | bytes 1769480 | tf_op jit(solution)/shard_map/ppermute | solution.py:468
  79.5 0.1 add_convert_fusion.1
  79.7 4.6 %collective-permute-start.15 = (bf16[96,3072]{1,0:T(8,128)(2,1)S(1)}, bf16[96,3072]{1,0:T(8,128)(2,1)S(1)}, u32[]{:S(2)}, u32[]{:S(2)}) collective-permute-start(bf16[96,3072]{1,0:T(8,128)(2,1)S(1)} %add_convert_fusion.1), channel_id=1, source_target_pairs={{0,1},{1,2},{2,3},{4,5},{5,6},{6,7},{8,9},{9,10},{10,11},{12,13},{... | collective-permute-start | bytes 1769480 | tf_op jit(solution)/shard_map/ppermute | solution.py:467
  84.3 5.1 %own.1 = (bf16[96,6144]{1,0:T(8,128)(2,1)S(1)}, f32[1,6144]{1,0:T(1,128)S(1)}) custom-call(s32[6,4]{1,0:T(8,128)S(1)} %pad_add_fusion.facts, bf16[384,768]{1,0:T(8,128)(2,1)S(1)} %get-tuple-element.90.attended, bf16[768,6144]{1,0:T(8,128)(2,1)} %weight.7, f32[64,6144]{1,0:T(8,128)} %gate_table.1), custom_call_target="tpu_custom_call" | custom-call | bytes 18450000 | tf_op jit(solution)/shard_map/own/pallas_call | solution.py:471
  89.4 0.7 collective-permute-done.13
  90.1 0.3 multiply_convert_fusion.done
  90.3 4.5 %collective-permute-done.16.down = bf16[96,3072]{1,0:T(8,128)(2,1)S(1)} collective-permute-done((bf16[96,3072]{1,0:T(8,128)(2,1)S(1)}, bf16[96,3072]{1,0:T(8,128)(2,1)S(1)}, u32[]{:S(2)}, u32[]{:S(2)}) %collective-permute-start.16) | collective-permute-done | bytes 589856 | tf_op jit(solution)/shard_map/ppermute | solution.py:468
  94.8 6.3 %collective-permute-done.15.up = bf16[96,3072]{1,0:T(8,128)(2,1)S(1)} collective-permute-done((bf16[96,3072]{1,0:T(8,128)(2,1)S(1)}, bf16[96,3072]{1,0:T(8,128)(2,1)S(1)}, u32[]{:S(2)}, u32[]{:S(2)}) %collective-permute-start.15) | collective-permute-done | bytes 589856 | tf_op jit(solution)/shard_map/ppermute | solution.py:467
  101.1 1.1 %final.1 = bf16[96,6144]{1,0:T(8,128)(2,1)} custom-call(bf16[96,3072]{1,0:T(8,128)(2,1)S(1)} %multiply_convert_fusion.done, bf16[96,6144]{1,0:T(8,128)(2,1)S(1)} %get-tuple-element.91.projected, f32[1,6144]{1,0:T(1,128)S(1)} %get-tuple-element.92.gate, bf16[96,3072]{1,0:T(8,128)(2,1)S(1)} %collective-permute-done.15.up, ...), custom_call_target="tpu_custom_call" | custom-call | bytes 9963000 | tf_op jit(solution)/shard_map/final/pallas_call | solution.py:492
  (20 shorter events, 0.1 us)
Async XLA Ops:
  0.0 4.3 %collective-permute-start = (bf16[384,768]{1,0:T(8,128)(2,1)}, bf16[384,768]{1,0:T(8,128)(2,1)S(1)}, u32[]{:S(2)}, u32[]{:S(2)}) collective-permute-start(bf16[384,768]{1,0:T(8,128)(2,1)} %key.9), channel_id=1, source_target_pairs={{0,4},{4,0},{8,12},{12,8},{1,5},{5,1},{9,13},{13,9},{2,6},{6,2},{1... | collective-permute-start | bytes 1769480 | tf_op jit(solution)/shard_map/ppermute | solution.py:355
  0.0 4.3 %collective-permute-start.1 = (bf16[384,768]{1,0:T(8,128)(2,1)}, bf16[384,768]{1,0:T(8,128)(2,1)S(1)}, u32[]{:S(2)}, u32[]{:S(2)}) collective-permute-start(bf16[384,768]{1,0:T(8,128)(2,1)} %value.9), channel_id=1, source_target_pairs={{0,4},{4,0},{8,12},{12,8},{1,5},{5,1},{9,13},{13,9},{2,6},{6,2},{1... | collective-permute-start | bytes 1769480 | tf_op jit(solution)/shard_map/ppermute | solution.py:356
  2.1 7.6 %collective-permute-start.2 = (bf16[96,768]{1,0:T(8,128)(2,1)S(1)}, bf16[96,768]{1,0:T(8,128)(2,1)S(1)}, u32[]{:S(2)}, u32[]{:S(2)}) collective-permute-start(bf16[96,768]{1,0:T(8,128)(2,1)S(1)} %split.2), channel_id=1, source_target_pairs={{8,0},{12,4},{9,1},{13,5},{10,2},{14,6},{11,3},{15,7},{24,16},{28,... | collective-permute-start | bytes 442376 | tf_op jit(solution)/shard_map/ppermute | solution.py:32
  4.3 5.3 %copy-start = (bf16[384,768]{1,0:T(8,128)(2,1)S(1)}, bf16[384,768]{1,0:T(8,128)(2,1)}, u32[]{:S(2)}) copy-start(bf16[384,768]{1,0:T(8,128)(2,1)} %key.9) | copy-start | bytes 1769476
  4.3 5.4 %copy-start.2 = (bf16[384,768]{1,0:T(8,128)(2,1)S(1)}, bf16[384,768]{1,0:T(8,128)(2,1)}, u32[]{:S(2)}) copy-start(bf16[384,768]{1,0:T(8,128)(2,1)} %value.9) | copy-start | bytes 1769476
  6.6 15.0 %collective-permute-start.4 = (bf16[192,768]{1,0:T(8,128)(2,1)S(1)}, bf16[192,768]{1,0:T(8,128)(2,1)S(1)}, u32[]{:S(2)}, u32[]{:S(2)}) collective-permute-start(bf16[192,768]{1,0:T(8,128)(2,1)S(1)} %get-tuple-element.56), channel_id=1, source_target_pairs={{8,0},{12,4},{9,1},{13,5},{10,2},{14,6},{11,3},{15,7},{24,16},{28,... | collective-permute-start | bytes 884744 | tf_op jit(solution)/shard_map/ppermute | solution.py:32
  10.3 9.3 %collective-permute-start.3 = (bf16[96,896]{1,0:T(8,128)(2,1)S(1)}, bf16[96,896]{1,0:T(8,128)(2,1)S(1)}, u32[]{:S(2)}, u32[]{:S(2)}) collective-permute-start(bf16[96,896]{1,0:T(8,128)(2,1)S(1)} %served.2), channel_id=1, source_target_pairs={{0,8},{4,12},{1,9},{5,13},{2,10},{6,14},{3,11},{7,15},{16,24},{20,... | collective-permute-start | bytes 516104 | tf_op jit(solution)/shard_map/ppermute | solution.py:32
  11.6 10.0 %collective-permute-start.5 = (bf16[96,768]{1,0:T(8,128)(2,1)S(1)}, bf16[96,768]{1,0:T(8,128)(2,1)S(1)}, u32[]{:S(2)}, u32[]{:S(2)}) collective-permute-start(bf16[96,768]{1,0:T(8,128)(2,1)S(1)} %get-tuple-element.57), channel_id=1, source_target_pairs={{8,0},{12,4},{9,1},{13,5},{10,2},{14,6},{11,3},{15,7},{24,16},{28,... | collective-permute-start | bytes 442376 | tf_op jit(solution)/shard_map/ppermute | solution.py:32
  19.6 2.0 %copy-start.1 = (bf16[384,768]{1,0:T(8,128)(2,1)S(1)}, bf16[384,768]{1,0:T(8,128)(2,1)}, u32[]{:S(2)}) copy-start(bf16[384,768]{1,0:T(8,128)(2,1)} %key.9) | copy-start | bytes 1769476
  19.6 2.0 %copy-start.3 = (bf16[384,768]{1,0:T(8,128)(2,1)S(1)}, bf16[384,768]{1,0:T(8,128)(2,1)}, u32[]{:S(2)}) copy-start(bf16[384,768]{1,0:T(8,128)(2,1)} %value.9) | copy-start | bytes 1769476
  20.3 21.0 %collective-permute-start.8 = (bf16[96,3072]{1,0:T(8,128)(2,1)S(1)}, bf16[96,3072]{1,0:T(8,128)(2,1)S(1)}, u32[]{:S(2)}, u32[]{:S(2)}) collective-permute-start(bf16[96,3072]{1,0:T(8,128)(2,1)S(1)} %opening.2), channel_id=1, source_target_pairs={{0,1},{3,2},{4,5},{7,6},{8,9},{11,10},{12,13},{15,14},{16,17},{19,... | collective-permute-start | bytes 1769480 | tf_op jit(solution)/shard_map/ppermute | solution.py:419
  22.3 14.7 %collective-permute-start.6 = (bf16[288,896]{1,0:T(8,128)(2,1)S(1)}, bf16[288,896]{1,0:T(8,128)(2,1)S(1)}, u32[]{:S(2)}, u32[]{:S(2)}) collective-permute-start(bf16[288,896]{1,0:T(8,128)(2,1)S(1)} %served.3), channel_id=1, source_target_pairs={{0,8},{4,12},{1,9},{5,13},{2,10},{6,14},{3,11},{7,15},{16,24},{20,... | collective-permute-start | bytes 1548296 | tf_op jit(solution)/shard_map/ppermute | solution.py:32
  24.2 27.9 %collective-permute-start.7 = (bf16[96,3072]{1,0:T(8,128)(2,1)S(1)}, bf16[96,3072]{1,0:T(8,128)(2,1)S(1)}, u32[]{:S(2)}, u32[]{:S(2)}) collective-permute-start(bf16[96,3072]{1,0:T(8,128)(2,1)S(1)} %opening.3), channel_id=1, source_target_pairs={{0,1},{3,2},{4,5},{7,6},{8,9},{11,10},{12,13},{15,14},{16,17},{19,... | collective-permute-start | bytes 1769480 | tf_op jit(solution)/shard_map/ppermute | solution.py:423
  41.6 20.9 %collective-permute-start.12 = (bf16[96,3072]{1,0:T(8,128)(2,1)S(1)}, bf16[96,3072]{1,0:T(8,128)(2,1)S(1)}, u32[]{:S(2)}, u32[]{:S(2)}) collective-permute-start(bf16[96,3072]{1,0:T(8,128)(2,1)S(1)} %get-tuple-element.95), channel_id=1, source_target_pairs={{3,2},{2,1},{7,6},{6,5},{11,10},{10,9},{15,14},{14,13},{19,18},{18... | collective-permute-start | bytes 1769480 | tf_op jit(solution)/shard_map/ppermute | solution.py:468
  42.9 21.9 %collective-permute-start.11 = (bf16[96,3072]{1,0:T(8,128)(2,1)S(1)}, bf16[96,3072]{1,0:T(8,128)(2,1)S(1)}, u32[]{:S(2)}, u32[]{:S(2)}) collective-permute-start(bf16[96,3072]{1,0:T(8,128)(2,1)S(1)} %get-tuple-element.96), channel_id=1, source_target_pairs={{0,1},{1,2},{4,5},{5,6},{8,9},{9,10},{12,13},{13,14},{16,17},{17,1... | collective-permute-start | bytes 1769480 | tf_op jit(solution)/shard_map/ppermute | solution.py:467
  52.4 22.9 %collective-permute-start.10 = (bf16[96,3072]{1,0:T(8,128)(2,1)S(1)}, bf16[96,3072]{1,0:T(8,128)(2,1)S(1)}, u32[]{:S(2)}, u32[]{:S(2)}) collective-permute-start(bf16[96,3072]{1,0:T(8,128)(2,1)S(1)} %get-tuple-element.93), channel_id=1, source_target_pairs={{3,2},{2,1},{7,6},{6,5},{11,10},{10,9},{15,14},{14,13},{19,18},{18... | collective-permute-start | bytes 1769480 | tf_op jit(solution)/shard_map/ppermute | solution.py:468
  53.7 23.7 %collective-permute-start.9 = (bf16[96,3072]{1,0:T(8,128)(2,1)S(1)}, bf16[96,3072]{1,0:T(8,128)(2,1)S(1)}, u32[]{:S(2)}, u32[]{:S(2)}) collective-permute-start(bf16[96,3072]{1,0:T(8,128)(2,1)S(1)} %get-tuple-element.94), channel_id=1, source_target_pairs={{0,1},{1,2},{4,5},{5,6},{8,9},{9,10},{12,13},{13,14},{16,17},{17,1... | collective-permute-start | bytes 1769480 | tf_op jit(solution)/shard_map/ppermute | solution.py:467
  64.9 24.4 %collective-permute-start.14 = (bf16[96,3072]{1,0:T(8,128)(2,1)S(1)}, bf16[96,3072]{1,0:T(8,128)(2,1)S(1)}, u32[]{:S(2)}, u32[]{:S(2)}) collective-permute-start(bf16[96,3072]{1,0:T(8,128)(2,1)S(1)} %add_convert_fusion.2), channel_id=1, source_target_pairs={{3,2},{2,1},{1,0},{7,6},{6,5},{5,4},{11,10},{10,9},{9,8},{15,14},{... | collective-permute-start | bytes 1769480 | tf_op jit(solution)/shard_map/ppermute | solution.py:468
  67.0 23.0 %collective-permute-start.13 = (bf16[96,3072]{1,0:T(8,128)(2,1)S(1)}, bf16[96,3072]{1,0:T(8,128)(2,1)S(1)}, u32[]{:S(2)}, u32[]{:S(2)}) collective-permute-start(bf16[96,3072]{1,0:T(8,128)(2,1)S(1)} %add_convert_fusion.3), channel_id=1, source_target_pairs={{0,1},{1,2},{2,3},{4,5},{5,6},{6,7},{8,9},{9,10},{10,11},{12,13},{... | collective-permute-start | bytes 1769480 | tf_op jit(solution)/shard_map/ppermute | solution.py:467
  77.6 17.3 %collective-permute-start.16 = (bf16[96,3072]{1,0:T(8,128)(2,1)S(1)}, bf16[96,3072]{1,0:T(8,128)(2,1)S(1)}, u32[]{:S(2)}, u32[]{:S(2)}) collective-permute-start(bf16[96,3072]{1,0:T(8,128)(2,1)S(1)} %add_convert_fusion), channel_id=1, source_target_pairs={{3,2},{2,1},{1,0},{7,6},{6,5},{5,4},{11,10},{10,9},{9,8},{15,14},{... | collective-permute-start | bytes 1769480 | tf_op jit(solution)/shard_map/ppermute | solution.py:468
  79.7 21.4 %collective-permute-start.15 = (bf16[96,3072]{1,0:T(8,128)(2,1)S(1)}, bf16[96,3072]{1,0:T(8,128)(2,1)S(1)}, u32[]{:S(2)}, u32[]{:S(2)}) collective-permute-start(bf16[96,3072]{1,0:T(8,128)(2,1)S(1)} %add_convert_fusion.1), channel_id=1, source_target_pairs={{0,1},{1,2},{2,3},{4,5},{5,6},{6,7},{8,9},{9,10},{10,11},{12,13},{... | collective-permute-start | bytes 1769480 | tf_op jit(solution)/shard_map/ppermute | solution.py:467

commit v13 on v10

--- a/solution.py
+++ b/solution.py
@@ -41,13 +41,21 @@
     scale = LOG2E * HD ** (-0.5)
     lane = lax.broadcasted_iota(jnp.int32, (rows, LANES), 1)
     packed = jnp.zeros((rows, LANES), jnp.float32)
-    for head in range(width // HD):
+
+    def scored(head):
         columns = head_columns(head)
-        mine = query[:, columns]
-        scores = [
-            lax.dot_general(mine, key[:, columns], (((1,), (1,)), ((), ())), preferred_element_type=jnp.float32)
+        return [
+            lax.dot_general(
+                query[:, columns], key[:, columns], (((1,), (1,)), ((), ())), preferred_element_type=jnp.float32
+            )
             for key in keys
         ]
+
+    heads = width // HD
+    later = scored(0)
+    for head in range(heads):
+        columns = head_columns(head)
+        scores, later = later, scored(head + 1) if head + 1 < heads else None
         tops = [jnp.max(block, axis=-1, keepdims=True) * scale for block in scores]
         top = functools.reduce(
             jnp.maximum, [one if flag is None else jnp.where(flag, one, HIDDEN) for one, flag in zip(tops, flags)]
@@ -92,13 +100,12 @@
     return (early, block), (late, rows - block)
 
 
-def split_kernel(spans, ranks, facts, query, *refs):
-    here = Facts(facts, spans)
+def split_kernel(ranks, place, query, *refs):
     *targets, semaphores = refs
 
-    @pl.when(here.span > 1)
+    @pl.when(place[0] > 1)
     def _():
-        (early, _), (late, _) = parts_of(here.rank, ranks, query.shape[0])
+        (early, _), (late, _) = parts_of(place[1], ranks, query.shape[0])
         starts = (early, late, pl.multiple_of(late + targets[1].shape[0], 16))
         copies = [
             copied(query.at[pl.ds(start, target.shape[0])], target, semaphores.at[index])
@@ -308,7 +315,7 @@
 
     third = (rows - block) // 48 * 16
     query_early, *query_late = pl.pallas_call(
-        functools.partial(split_kernel, spans, ranks),
+        functools.partial(split_kernel, ranks),
         in_specs=[SMEM, HBM],
         out_specs=[VMEM] * 3,
         out_shape=[jax.ShapeDtypeStruct((part, width), bf16) for part in (block, rows - block - third, third)],
@@ -316,7 +323,7 @@
         compiler_params=PARAMS,
         cost_estimate=taking(1.7),
         name="split",
-    )(facts, in_hbm(queries))
+    )(jnp.stack([span, rank]).astype(jnp.int32), in_hbm(queries))
     distances = list(range(2, spans, 2))
     asked_early = [shifted(query_early, "span", -distance) for distance in distances]
     swap = [(i, i + 1 - 2 * (i % 2)) for i in range(spans)]
@@ -372,9 +379,9 @@
             out_specs=VMEM,
             out_shape=jax.ShapeDtypeStruct((block, columns), bf16),
             scratch_shapes=[
-                pltpu.VMEM((tiles, width, tile), bf16),
+                pltpu.VMEM((2, width, columns // 2), bf16),
                 pltpu.VMEM((block, width), bf16),
-                pltpu.SemaphoreType.DMA((tiles,)),
+                pltpu.SemaphoreType.DMA((2,)),
             ],
             compiler_params=PARAMS,
             cost_estimate=taking(3.4),

time: 103 us -> 102 us (level)
  Pallas kernels: 34.2 us -> 32.7 us
  waiting for transfers between devices: 26 us -> 27.1 us
    pallas_call x2, Pallas kernels: 9.05 us -> 7.71 us  [local(): pl.pallas_call(functools.partial(local_kernel, spans, ranks, part), in_sp...]
    ppermute x4, waiting for transfers between devices: 7.98 us -> 9.17 us  [body(): lax.ppermute(up, 'tensor', [(i, i + 1) for i in range(step + 1)])]
  transfers between devices with their start and end apart: 17 -> 17, of which waited for: 7 -> 7; matrix products, arithmetic and copies ran while one was open for 2% -> 2% of each run, Pallas kernels for 33% -> 32%
where the time goes in v13:
time: 102 us; the launch traced here: 100 us
  starting transfers between devices  37.7 us (37%)
  Pallas kernels  32.7 us (32%)
  waiting for transfers between devices  27.1 us (27%)
  other arithmetic  2.14 us (2%)
    ppermute x4, starting transfers between devices, body(): lax.ppermute(up, 'tensor', [(i, i + 1) for i in range(step + 1)])  18.3 us
    ppermute x5, waiting for transfers between devices, shifted(): lax.ppermute(block, axis, [(i, i + distance) for i in range(count) if 0 <...  11.1 us
    pallas_call x3, Pallas kernels, blocks_of(): pl.pallas_call(functools.partial(blocks_kernel, spans, ranks, chunk * col...  10.3 us
    ppermute x5, starting transfers between devices, shifted(): lax.ppermute(block, axis, [(i, i + distance) for i in range(count) if 0 <...  9.81 us
    ppermute x4, waiting for transfers between devices, body(): lax.ppermute(up, 'tensor', [(i, i + 1) for i in range(step + 1)])  9.17 us
    pallas_call x2, Pallas kernels, local(): pl.pallas_call(functools.partial(local_kernel, spans, ranks, part), in_sp...  7.71 us
    ppermute x4, waiting for transfers between devices, body(): lax.ppermute(down, 'tensor', [(last - i, last - i - 1) for i in range(ste...  6.81 us
    ppermute x4, starting transfers between devices, body(): lax.ppermute(down, 'tensor', [(last - i, last - i - 1) for i in range(ste...  6.43 us
  transfers between devices with their start and end apart: 17, of which 7 were waited for; matrix products, arithmetic and copies ran while one was open for 2% of the time, Pallas kernels for 32%

profile of v13, /device:TPU:14, one launch (start us, length us, event | category | flops | bytes accessed | tf_op | source)
XLA Modules:
  0.0 100.2 jit_solution(13577202777995886677)
XLA Ops:
  0.0 0.5 collective-permute-start.1
  0.5 0.1 pad_add_fusion.1.place
  0.6 1.6 %split.1 = (bf16[96,768]{1,0:T(8,128)(2,1)S(1)}, bf16[192,768]{1,0:T(8,128)(2,1)S(1)}, bf16[96,768]{1,0:T(8,128)(2,1)S(1)}) custom-call(s32[2]{0:T(128)S(1)} %pad_add_fusion.1.place, bf16[384,768]{1,0:T(8,128)(2,1)} %query.5), custom_call_target="tpu_custom_call" | custom-call | bytes 6273000 | tf_op jit(solution)/shard_map/split/pallas_call | solution.py:317
  2.2 1.4 %collective-permute-start.2 = (bf16[96,768]{1,0:T(8,128)(2,1)S(1)}, bf16[96,768]{1,0:T(8,128)(2,1)S(1)}, u32[]{:S(2)}, u32[]{:S(2)}) collective-permute-start(bf16[96,768]{1,0:T(8,128)(2,1)S(1)} %get-tuple-element.50), channel_id=1, source_target_pairs={{8,0},{12,4},{9,1},{13,5},{10,2},{14,6},{11,3},{15,7},{24,16},{28,... | collective-permute-start | bytes 442376 | tf_op jit(solution)/shard_map/ppermute | solution.py:32
  3.6 0.7 pad_add_fusion.facts
  4.3 0.0 copy-start.1
  4.4 0.0 collective-permute-done.1.value_beside
  4.4 3.4 %local.2 = (f32[96,768]{1,0:T(8,128)S(1)}, f32[96,128]{1,0:T(8,128)S(1)}) custom-call(s32[6,4]{1,0:T(8,128)S(1)} %pad_add_fusion.facts, bf16[384,768]{1,0:T(8,128)(2,1)} %query.5, bf16[384,768]{1,0:T(8,128)(2,1)} %key.7, bf16[384,768]{1,0:T(8,128)(2,1)} %value.7, bf16[384,768]{1,0:T(8,128)(2,1)S(1)} %collective-permute-done.key_beside, ...), custom_call_target="tpu_custom_call" | custom-call | bytes 14760000 | tf_op jit(solution)/shard_map/local/pallas_call | solution.py:338
  7.8 1.3 %collective-permute-start.4 = (bf16[192,768]{1,0:T(8,128)(2,1)S(1)}, bf16[192,768]{1,0:T(8,128)(2,1)S(1)}, u32[]{:S(2)}, u32[]{:S(2)}) collective-permute-start(bf16[192,768]{1,0:T(8,128)(2,1)S(1)} %get-tuple-element.54), channel_id=1, source_target_pairs={{8,0},{12,4},{9,1},{13,5},{10,2},{14,6},{11,3},{15,7},{24,16},{28,... | collective-permute-start | bytes 884744 | tf_op jit(solution)/shard_map/ppermute | solution.py:32
  9.1 0.6 served.2
  9.7 1.3 %collective-permute-start.3 = (bf16[96,896]{1,0:T(8,128)(2,1)S(1)}, bf16[96,896]{1,0:T(8,128)(2,1)S(1)}, u32[]{:S(2)}, u32[]{:S(2)}) collective-permute-start(bf16[96,896]{1,0:T(8,128)(2,1)S(1)} %served.2), channel_id=1, source_target_pairs={{0,8},{4,12},{1,9},{5,13},{2,10},{6,14},{3,11},{7,15},{16,24},{20,... | collective-permute-start | bytes 516104 | tf_op jit(solution)/shard_map/ppermute | solution.py:32
  11.0 4.6 %collective-permute-start.5 = (bf16[96,768]{1,0:T(8,128)(2,1)S(1)}, bf16[96,768]{1,0:T(8,128)(2,1)S(1)}, u32[]{:S(2)}, u32[]{:S(2)}) collective-permute-start(bf16[96,768]{1,0:T(8,128)(2,1)S(1)} %get-tuple-element.55), channel_id=1, source_target_pairs={{8,0},{12,4},{9,1},{13,5},{10,2},{14,6},{11,3},{15,7},{24,16},{28,... | collective-permute-start | bytes 442376 | tf_op jit(solution)/shard_map/ppermute | solution.py:32
  15.6 2.3 %collective-permute-done.3.refs_2_ = bf16[96,896]{1,0:T(8,128)(2,1)S(1)} collective-permute-done((bf16[96,896]{1,0:T(8,128)(2,1)S(1)}, bf16[96,896]{1,0:T(8,128)(2,1)S(1)}, u32[]{:S(2)}, u32[]{:S(2)}) %collective-permute-start.3) | collective-permute-done | bytes 172064 | tf_op jit(solution)/shard_map/ppermute | solution.py:32
  17.9 0.6 opening.2
  18.5 1.3 %collective-permute-start.8 = (bf16[96,3072]{1,0:T(8,128)(2,1)S(1)}, bf16[96,3072]{1,0:T(8,128)(2,1)S(1)}, u32[]{:S(2)}, u32[]{:S(2)}) collective-permute-start(bf16[96,3072]{1,0:T(8,128)(2,1)S(1)} %opening.2), channel_id=1, source_target_pairs={{0,1},{3,2},{4,5},{7,6},{8,9},{11,10},{12,13},{15,14},{16,17},{19,... | collective-permute-start | bytes 1769480 | tf_op jit(solution)/shard_map/ppermute | solution.py:393
  19.8 0.0 collective-permute-done.5.refs_1_
  19.8 0.6 served.3
  20.4 1.3 %collective-permute-start.6 = (bf16[288,896]{1,0:T(8,128)(2,1)S(1)}, bf16[288,896]{1,0:T(8,128)(2,1)S(1)}, u32[]{:S(2)}, u32[]{:S(2)}) collective-permute-start(bf16[288,896]{1,0:T(8,128)(2,1)S(1)} %served.3), channel_id=1, source_target_pairs={{0,8},{4,12},{1,9},{5,13},{2,10},{6,14},{3,11},{7,15},{16,24},{20,... | collective-permute-start | bytes 1548296 | tf_op jit(solution)/shard_map/ppermute | solution.py:32
  21.7 0.6 opening.3
  22.4 1.3 %collective-permute-start.7 = (bf16[96,3072]{1,0:T(8,128)(2,1)S(1)}, bf16[96,3072]{1,0:T(8,128)(2,1)S(1)}, u32[]{:S(2)}, u32[]{:S(2)}) collective-permute-start(bf16[96,3072]{1,0:T(8,128)(2,1)S(1)} %opening.3), channel_id=1, source_target_pairs={{0,1},{3,2},{4,5},{7,6},{8,9},{11,10},{12,13},{15,14},{16,17},{19,... | collective-permute-start | bytes 1769480 | tf_op jit(solution)/shard_map/ppermute | solution.py:397
  23.7 4.3 %local.3 = (f32[288,768]{1,0:T(8,128)S(1)}, f32[288,128]{1,0:T(8,128)S(1)}) custom-call(s32[6,4]{1,0:T(8,128)S(1)} %pad_add_fusion.facts, bf16[384,768]{1,0:T(8,128)(2,1)} %query.5, bf16[384,768]{1,0:T(8,128)(2,1)} %key.7, bf16[384,768]{1,0:T(8,128)(2,1)} %value.7, bf16[384,768]{1,0:T(8,128)(2,1)S(1)} %collective-permute-done.key_beside, ...), custom_call_target="tpu_custom_call" | custom-call | bytes 14760000 | tf_op jit(solution)/shard_map/local/pallas_call | solution.py:338
  28.0 8.8 %collective-permute-done.6.refs_5_ = bf16[288,896]{1,0:T(8,128)(2,1)S(1)} collective-permute-done((bf16[288,896]{1,0:T(8,128)(2,1)S(1)}, bf16[288,896]{1,0:T(8,128)(2,1)S(1)}, u32[]{:S(2)}, u32[]{:S(2)}) %collective-permute-start.6) | collective-permute-done | bytes 516128 | tf_op jit(solution)/shard_map/ppermute | solution.py:32
  36.8 4.4 %merged_blocks.1 = (bf16[384,768]{1,0:T(8,128)(2,1)S(1)}, bf16[96,3072]{1,0:T(8,128)(2,1)S(1)}, bf16[96,3072]{1,0:T(8,128)(2,1)S(1)}) custom-call(s32[6,4]{1,0:T(8,128)S(1)} %pad_add_fusion.facts, f32[96,768]{1,0:T(8,128)S(1)} %get-tuple-element.48.refs_0_, f32[96,128]{1,0:T(8,128)S(1)} %get-tuple-element.49.refs_1_, ...), custom_call_target="tpu_custom_call" | custom-call | bytes 11070000 | tf_op jit(solution)/shard_map/merged_blocks/pallas_call | solution.py:408
  41.3 0.2 fusion.1
  41.5 1.3 %collective-permute-start.12 = (bf16[96,3072]{1,0:T(8,128)(2,1)S(1)}, bf16[96,3072]{1,0:T(8,128)(2,1)S(1)}, u32[]{:S(2)}, u32[]{:S(2)}) collective-permute-start(bf16[96,3072]{1,0:T(8,128)(2,1)S(1)} %get-tuple-element.93), channel_id=1, source_target_pairs={{3,2},{2,1},{7,6},{6,5},{11,10},{10,9},{15,14},{14,13},{19,18},{18... | collective-permute-start | bytes 1769480 | tf_op jit(solution)/shard_map/ppermute | solution.py:442
  42.8 4.6 %collective-permute-start.11 = (bf16[96,3072]{1,0:T(8,128)(2,1)S(1)}, bf16[96,3072]{1,0:T(8,128)(2,1)S(1)}, u32[]{:S(2)}, u32[]{:S(2)}) collective-permute-start(bf16[96,3072]{1,0:T(8,128)(2,1)S(1)} %get-tuple-element.94), channel_id=1, source_target_pairs={{0,1},{1,2},{4,5},{5,6},{8,9},{9,10},{12,13},{13,14},{16,17},{17,1... | collective-permute-start | bytes 1769480 | tf_op jit(solution)/shard_map/ppermute | solution.py:441
  47.4 3.3 %blocks.3 = (bf16[96,3072]{1,0:T(8,128)(2,1)S(1)}, bf16[96,3072]{1,0:T(8,128)(2,1)S(1)}) custom-call(s32[6,4]{1,0:T(8,128)S(1)} %pad_add_fusion.facts, bf16[384,768]{1,0:T(8,128)(2,1)S(1)} %get-tuple-element.88.attended, bf16[768,6144]{1,0:T(8,128)(2,1)} %weight.7), custom_call_target="tpu_custom_call" | custom-call | bytes 11070000 | tf_op jit(solution)/shard_map/blocks/pallas_call | solution.py:418
  50.7 0.3 fusion.3
  51.0 1.3 %collective-permute-start.10 = (bf16[96,3072]{1,0:T(8,128)(2,1)S(1)}, bf16[96,3072]{1,0:T(8,128)(2,1)S(1)}, u32[]{:S(2)}, u32[]{:S(2)}) collective-permute-start(bf16[96,3072]{1,0:T(8,128)(2,1)S(1)} %get-tuple-element.91), channel_id=1, source_target_pairs={{3,2},{2,1},{7,6},{6,5},{11,10},{10,9},{15,14},{14,13},{19,18},{18... | collective-permute-start | bytes 1769480 | tf_op jit(solution)/shard_map/ppermute | solution.py:442
  52.3 4.6 %collective-permute-start.9 = (bf16[96,3072]{1,0:T(8,128)(2,1)S(1)}, bf16[96,3072]{1,0:T(8,128)(2,1)S(1)}, u32[]{:S(2)}, u32[]{:S(2)}) collective-permute-start(bf16[96,3072]{1,0:T(8,128)(2,1)S(1)} %get-tuple-element.92), channel_id=1, source_target_pairs={{0,1},{1,2},{4,5},{5,6},{8,9},{9,10},{12,13},{13,14},{16,17},{17,1... | collective-permute-start | bytes 1769480 | tf_op jit(solution)/shard_map/ppermute | solution.py:441
  56.9 3.5 %blocks.4 = (bf16[96,3072]{1,0:T(8,128)(2,1)S(1)}, bf16[96,3072]{1,0:T(8,128)(2,1)S(1)}) custom-call(s32[6,4]{1,0:T(8,128)S(1)} %pad_add_fusion.facts, bf16[384,768]{1,0:T(8,128)(2,1)S(1)} %get-tuple-element.88.attended, bf16[768,6144]{1,0:T(8,128)(2,1)} %weight.7), custom_call_target="tpu_custom_call" | custom-call | bytes 11070000 | tf_op jit(solution)/shard_map/blocks/pallas_call | solution.py:418
  60.4 2.3 %collective-permute-done.11 = bf16[96,3072]{1,0:T(8,128)(2,1)S(1)} collective-permute-done((bf16[96,3072]{1,0:T(8,128)(2,1)S(1)}, bf16[96,3072]{1,0:T(8,128)(2,1)S(1)}, u32[]{:S(2)}, u32[]{:S(2)}) %collective-permute-start.11) | collective-permute-done | bytes 589856 | tf_op jit(solution)/shard_map/ppermute | solution.py:441
  62.7 0.1 add_convert_fusion.2
  62.9 1.9 %collective-permute-start.14 = (bf16[96,3072]{1,0:T(8,128)(2,1)S(1)}, bf16[96,3072]{1,0:T(8,128)(2,1)S(1)}, u32[]{:S(2)}, u32[]{:S(2)}) collective-permute-start(bf16[96,3072]{1,0:T(8,128)(2,1)S(1)} %add_convert_fusion.2), channel_id=1, source_target_pairs={{3,2},{2,1},{1,0},{7,6},{6,5},{5,4},{11,10},{10,9},{9,8},{15,14},{... | collective-permute-start | bytes 1769480 | tf_op jit(solution)/shard_map/ppermute | solution.py:442
  64.8 0.2 add_convert_fusion.3
  65.0 4.6 %collective-permute-start.13 = (bf16[96,3072]{1,0:T(8,128)(2,1)S(1)}, bf16[96,3072]{1,0:T(8,128)(2,1)S(1)}, u32[]{:S(2)}, u32[]{:S(2)}) collective-permute-start(bf16[96,3072]{1,0:T(8,128)(2,1)S(1)} %add_convert_fusion.3), channel_id=1, source_target_pairs={{0,1},{1,2},{2,3},{4,5},{5,6},{6,7},{8,9},{9,10},{10,11},{12,13},{... | collective-permute-start | bytes 1769480 | tf_op jit(solution)/shard_map/ppermute | solution.py:441
  69.6 3.5 %blocks.5 = (bf16[96,3072]{1,0:T(8,128)(2,1)S(1)}, bf16[96,3072]{1,0:T(8,128)(2,1)S(1)}) custom-call(s32[6,4]{1,0:T(8,128)S(1)} %pad_add_fusion.facts, bf16[384,768]{1,0:T(8,128)(2,1)S(1)} %get-tuple-element.88.attended, bf16[768,6144]{1,0:T(8,128)(2,1)} %weight.7), custom_call_target="tpu_custom_call" | custom-call | bytes 11070000 | tf_op jit(solution)/shard_map/blocks/pallas_call | solution.py:418
  73.1 2.2 %collective-permute-done.9 = bf16[96,3072]{1,0:T(8,128)(2,1)S(1)} collective-permute-done((bf16[96,3072]{1,0:T(8,128)(2,1)S(1)}, bf16[96,3072]{1,0:T(8,128)(2,1)S(1)}, u32[]{:S(2)}, u32[]{:S(2)}) %collective-permute-start.9) | collective-permute-done | bytes 589856 | tf_op jit(solution)/shard_map/ppermute | solution.py:441
  75.4 0.2 add_convert_fusion
  75.5 1.9 %collective-permute-start.16 = (bf16[96,3072]{1,0:T(8,128)(2,1)S(1)}, bf16[96,3072]{1,0:T(8,128)(2,1)S(1)}, u32[]{:S(2)}, u32[]{:S(2)}) collective-permute-start(bf16[96,3072]{1,0:T(8,128)(2,1)S(1)} %add_convert_fusion), channel_id=1, source_target_pairs={{3,2},{2,1},{1,0},{7,6},{6,5},{5,4},{11,10},{10,9},{9,8},{15,14},{... | collective-permute-start | bytes 1769480 | tf_op jit(solution)/shard_map/ppermute | solution.py:442
  77.4 0.1 add_convert_fusion.1
  77.6 4.6 %collective-permute-start.15 = (bf16[96,3072]{1,0:T(8,128)(2,1)S(1)}, bf16[96,3072]{1,0:T(8,128)(2,1)S(1)}, u32[]{:S(2)}, u32[]{:S(2)}) collective-permute-start(bf16[96,3072]{1,0:T(8,128)(2,1)S(1)} %add_convert_fusion.1), channel_id=1, source_target_pairs={{0,1},{1,2},{2,3},{4,5},{5,6},{6,7},{8,9},{9,10},{10,11},{12,13},{... | collective-permute-start | bytes 1769480 | tf_op jit(solution)/shard_map/ppermute | solution.py:441
  82.2 5.1 %own.1 = (bf16[96,6144]{1,0:T(8,128)(2,1)S(1)}, f32[1,6144]{1,0:T(1,128)S(1)}) custom-call(s32[6,4]{1,0:T(8,128)S(1)} %pad_add_fusion.facts, bf16[384,768]{1,0:T(8,128)(2,1)S(1)} %get-tuple-element.88.attended, bf16[768,6144]{1,0:T(8,128)(2,1)} %weight.7, f32[64,6144]{1,0:T(8,128)} %gate_table.1), custom_call_target="tpu_custom_call" | custom-call | bytes 18450000 | tf_op jit(solution)/shard_map/own/pallas_call | solution.py:445
  87.3 0.7 collective-permute-done.13
  88.0 0.3 multiply_convert_fusion.done
  88.3 6.8 %collective-permute-done.16.down = bf16[96,3072]{1,0:T(8,128)(2,1)S(1)} collective-permute-done((bf16[96,3072]{1,0:T(8,128)(2,1)S(1)}, bf16[96,3072]{1,0:T(8,128)(2,1)S(1)}, u32[]{:S(2)}, u32[]{:S(2)}) %collective-permute-start.16) | collective-permute-done | bytes 589856 | tf_op jit(solution)/shard_map/ppermute | solution.py:442
  95.1 3.9 %collective-permute-done.15.up = bf16[96,3072]{1,0:T(8,128)(2,1)S(1)} collective-permute-done((bf16[96,3072]{1,0:T(8,128)(2,1)S(1)}, bf16[96,3072]{1,0:T(8,128)(2,1)S(1)}, u32[]{:S(2)}, u32[]{:S(2)}) %collective-permute-start.15) | collective-permute-done | bytes 589856 | tf_op jit(solution)/shard_map/ppermute | solution.py:441
  99.0 1.1 %final.1 = bf16[96,6144]{1,0:T(8,128)(2,1)} custom-call(bf16[96,3072]{1,0:T(8,128)(2,1)S(1)} %multiply_convert_fusion.done, bf16[96,6144]{1,0:T(8,128)(2,1)S(1)} %get-tuple-element.89.projected, f32[1,6144]{1,0:T(1,128)S(1)} %get-tuple-element.90.gate, bf16[96,3072]{1,0:T(8,128)(2,1)S(1)} %collective-permute-done.15.up, ...), custom_call_target="tpu_custom_call" | custom-call | bytes 9963000 | tf_op jit(solution)/shard_map/final/pallas_call | solution.py:466
  (14 shorter events, 0.0 us)
Async XLA Ops:
  0.0 4.3 %collective-permute-start = (bf16[384,768]{1,0:T(8,128)(2,1)}, bf16[384,768]{1,0:T(8,128)(2,1)S(1)}, u32[]{:S(2)}, u32[]{:S(2)}) collective-permute-start(bf16[384,768]{1,0:T(8,128)(2,1)} %key.7), channel_id=1, source_target_pairs={{0,4},{4,0},{8,12},{12,8},{1,5},{5,1},{9,13},{13,9},{2,6},{6,2},{1... | collective-permute-start | bytes 1769480 | tf_op jit(solution)/shard_map/ppermute | solution.py:330
  0.0 4.4 %collective-permute-start.1 = (bf16[384,768]{1,0:T(8,128)(2,1)}, bf16[384,768]{1,0:T(8,128)(2,1)S(1)}, u32[]{:S(2)}, u32[]{:S(2)}) collective-permute-start(bf16[384,768]{1,0:T(8,128)(2,1)} %value.7), channel_id=1, source_target_pairs={{0,4},{4,0},{8,12},{12,8},{1,5},{5,1},{9,13},{13,9},{2,6},{6,2},{1... | collective-permute-start | bytes 1769480 | tf_op jit(solution)/shard_map/ppermute | solution.py:331
  2.2 6.9 %collective-permute-start.2 = (bf16[96,768]{1,0:T(8,128)(2,1)S(1)}, bf16[96,768]{1,0:T(8,128)(2,1)S(1)}, u32[]{:S(2)}, u32[]{:S(2)}) collective-permute-start(bf16[96,768]{1,0:T(8,128)(2,1)S(1)} %get-tuple-element.50), channel_id=1, source_target_pairs={{8,0},{12,4},{9,1},{13,5},{10,2},{14,6},{11,3},{15,7},{24,16},{28,... | collective-permute-start | bytes 442376 | tf_op jit(solution)/shard_map/ppermute | solution.py:32
  4.3 4.8 %copy-start = (bf16[384,768]{1,0:T(8,128)(2,1)S(1)}, bf16[384,768]{1,0:T(8,128)(2,1)}, u32[]{:S(2)}) copy-start(bf16[384,768]{1,0:T(8,128)(2,1)} %key.7) | copy-start | bytes 1769476
  4.3 4.8 %copy-start.1 = (bf16[384,768]{1,0:T(8,128)(2,1)S(1)}, bf16[384,768]{1,0:T(8,128)(2,1)}, u32[]{:S(2)}) copy-start(bf16[384,768]{1,0:T(8,128)(2,1)} %value.7) | copy-start | bytes 1769476
  7.8 12.0 %collective-permute-start.4 = (bf16[192,768]{1,0:T(8,128)(2,1)S(1)}, bf16[192,768]{1,0:T(8,128)(2,1)S(1)}, u32[]{:S(2)}, u32[]{:S(2)}) collective-permute-start(bf16[192,768]{1,0:T(8,128)(2,1)S(1)} %get-tuple-element.54), channel_id=1, source_target_pairs={{8,0},{12,4},{9,1},{13,5},{10,2},{14,6},{11,3},{15,7},{24,16},{28,... | collective-permute-start | bytes 884744 | tf_op jit(solution)/shard_map/ppermute | solution.py:32
  9.7 8.1 %collective-permute-start.3 = (bf16[96,896]{1,0:T(8,128)(2,1)S(1)}, bf16[96,896]{1,0:T(8,128)(2,1)S(1)}, u32[]{:S(2)}, u32[]{:S(2)}) collective-permute-start(bf16[96,896]{1,0:T(8,128)(2,1)S(1)} %served.2), channel_id=1, source_target_pairs={{0,8},{4,12},{1,9},{5,13},{2,10},{6,14},{3,11},{7,15},{16,24},{20,... | collective-permute-start | bytes 516104 | tf_op jit(solution)/shard_map/ppermute | solution.py:32
  11.0 8.8 %collective-permute-start.5 = (bf16[96,768]{1,0:T(8,128)(2,1)S(1)}, bf16[96,768]{1,0:T(8,128)(2,1)S(1)}, u32[]{:S(2)}, u32[]{:S(2)}) collective-permute-start(bf16[96,768]{1,0:T(8,128)(2,1)S(1)} %get-tuple-element.55), channel_id=1, source_target_pairs={{8,0},{12,4},{9,1},{13,5},{10,2},{14,6},{11,3},{15,7},{24,16},{28,... | collective-permute-start | bytes 442376 | tf_op jit(solution)/shard_map/ppermute | solution.py:32
  18.5 22.8 %collective-permute-start.8 = (bf16[96,3072]{1,0:T(8,128)(2,1)S(1)}, bf16[96,3072]{1,0:T(8,128)(2,1)S(1)}, u32[]{:S(2)}, u32[]{:S(2)}) collective-permute-start(bf16[96,3072]{1,0:T(8,128)(2,1)S(1)} %opening.2), channel_id=1, source_target_pairs={{0,1},{3,2},{4,5},{7,6},{8,9},{11,10},{12,13},{15,14},{16,17},{19,... | collective-permute-start | bytes 1769480 | tf_op jit(solution)/shard_map/ppermute | solution.py:393
  20.4 16.4 %collective-permute-start.6 = (bf16[288,896]{1,0:T(8,128)(2,1)S(1)}, bf16[288,896]{1,0:T(8,128)(2,1)S(1)}, u32[]{:S(2)}, u32[]{:S(2)}) collective-permute-start(bf16[288,896]{1,0:T(8,128)(2,1)S(1)} %served.3), channel_id=1, source_target_pairs={{0,8},{4,12},{1,9},{5,13},{2,10},{6,14},{3,11},{7,15},{16,24},{20,... | collective-permute-start | bytes 1548296 | tf_op jit(solution)/shard_map/ppermute | solution.py:32
  22.4 28.4 %collective-permute-start.7 = (bf16[96,3072]{1,0:T(8,128)(2,1)S(1)}, bf16[96,3072]{1,0:T(8,128)(2,1)S(1)}, u32[]{:S(2)}, u32[]{:S(2)}) collective-permute-start(bf16[96,3072]{1,0:T(8,128)(2,1)S(1)} %opening.3), channel_id=1, source_target_pairs={{0,1},{3,2},{4,5},{7,6},{8,9},{11,10},{12,13},{15,14},{16,17},{19,... | collective-permute-start | bytes 1769480 | tf_op jit(solution)/shard_map/ppermute | solution.py:397
  41.5 18.8 %collective-permute-start.12 = (bf16[96,3072]{1,0:T(8,128)(2,1)S(1)}, bf16[96,3072]{1,0:T(8,128)(2,1)S(1)}, u32[]{:S(2)}, u32[]{:S(2)}) collective-permute-start(bf16[96,3072]{1,0:T(8,128)(2,1)S(1)} %get-tuple-element.93), channel_id=1, source_target_pairs={{3,2},{2,1},{7,6},{6,5},{11,10},{10,9},{15,14},{14,13},{19,18},{18... | collective-permute-start | bytes 1769480 | tf_op jit(solution)/shard_map/ppermute | solution.py:442
  42.8 19.9 %collective-permute-start.11 = (bf16[96,3072]{1,0:T(8,128)(2,1)S(1)}, bf16[96,3072]{1,0:T(8,128)(2,1)S(1)}, u32[]{:S(2)}, u32[]{:S(2)}) collective-permute-start(bf16[96,3072]{1,0:T(8,128)(2,1)S(1)} %get-tuple-element.94), channel_id=1, source_target_pairs={{0,1},{1,2},{4,5},{5,6},{8,9},{9,10},{12,13},{13,14},{16,17},{17,1... | collective-permute-start | bytes 1769480 | tf_op jit(solution)/shard_map/ppermute | solution.py:441
  51.0 22.1 %collective-permute-start.10 = (bf16[96,3072]{1,0:T(8,128)(2,1)S(1)}, bf16[96,3072]{1,0:T(8,128)(2,1)S(1)}, u32[]{:S(2)}, u32[]{:S(2)}) collective-permute-start(bf16[96,3072]{1,0:T(8,128)(2,1)S(1)} %get-tuple-element.91), channel_id=1, source_target_pairs={{3,2},{2,1},{7,6},{6,5},{11,10},{10,9},{15,14},{14,13},{19,18},{18... | collective-permute-start | bytes 1769480 | tf_op jit(solution)/shard_map/ppermute | solution.py:442
  52.3 23.1 %collective-permute-start.9 = (bf16[96,3072]{1,0:T(8,128)(2,1)S(1)}, bf16[96,3072]{1,0:T(8,128)(2,1)S(1)}, u32[]{:S(2)}, u32[]{:S(2)}) collective-permute-start(bf16[96,3072]{1,0:T(8,128)(2,1)S(1)} %get-tuple-element.92), channel_id=1, source_target_pairs={{0,1},{1,2},{4,5},{5,6},{8,9},{9,10},{12,13},{13,14},{16,17},{17,1... | collective-permute-start | bytes 1769480 | tf_op jit(solution)/shard_map/ppermute | solution.py:441
  62.9 24.4 %collective-permute-start.14 = (bf16[96,3072]{1,0:T(8,128)(2,1)S(1)}, bf16[96,3072]{1,0:T(8,128)(2,1)S(1)}, u32[]{:S(2)}, u32[]{:S(2)}) collective-permute-start(bf16[96,3072]{1,0:T(8,128)(2,1)S(1)} %add_convert_fusion.2), channel_id=1, source_target_pairs={{3,2},{2,1},{1,0},{7,6},{6,5},{5,4},{11,10},{10,9},{9,8},{15,14},{... | collective-permute-start | bytes 1769480 | tf_op jit(solution)/shard_map/ppermute | solution.py:442
  65.0 23.0 %collective-permute-start.13 = (bf16[96,3072]{1,0:T(8,128)(2,1)S(1)}, bf16[96,3072]{1,0:T(8,128)(2,1)S(1)}, u32[]{:S(2)}, u32[]{:S(2)}) collective-permute-start(bf16[96,3072]{1,0:T(8,128)(2,1)S(1)} %add_convert_fusion.3), channel_id=1, source_target_pairs={{0,1},{1,2},{2,3},{4,5},{5,6},{6,7},{8,9},{9,10},{10,11},{12,13},{... | collective-permute-start | bytes 1769480 | tf_op jit(solution)/shard_map/ppermute | solution.py:441
  75.5 19.5 %collective-permute-start.16 = (bf16[96,3072]{1,0:T(8,128)(2,1)S(1)}, bf16[96,3072]{1,0:T(8,128)(2,1)S(1)}, u32[]{:S(2)}, u32[]{:S(2)}) collective-permute-start(bf16[96,3072]{1,0:T(8,128)(2,1)S(1)} %add_convert_fusion), channel_id=1, source_target_pairs={{3,2},{2,1},{1,0},{7,6},{6,5},{5,4},{11,10},{10,9},{9,8},{15,14},{... | collective-permute-start | bytes 1769480 | tf_op jit(solution)/shard_map/ppermute | solution.py:442
  77.6 21.4 %collective-permute-start.15 = (bf16[96,3072]{1,0:T(8,128)(2,1)S(1)}, bf16[96,3072]{1,0:T(8,128)(2,1)S(1)}, u32[]{:S(2)}, u32[]{:S(2)}) collective-permute-start(bf16[96,3072]{1,0:T(8,128)(2,1)S(1)} %add_convert_fusion.1), channel_id=1, source_target_pairs={{0,1},{1,2},{2,3},{4,5},{5,6},{6,7},{8,9},{9,10},{10,11},{12,13},{... | collective-permute-start | bytes 1769480 | tf_op jit(solution)/shard_map/ppermute | solution.py:441

commit v14 on v13

--- a/solution.py
+++ b/solution.py
@@ -100,19 +100,28 @@
     return (early, block), (late, rows - block)
 
 
-def split_kernel(ranks, place, query, *refs):
-    *targets, semaphores = refs
+def split_kernel(ranks, place, query, weight, *refs):
+    *targets, piece, semaphores = refs
+    (early, _), (late, _) = parts_of(place[1], ranks, query.shape[0])
+    starts = (early, late, late + targets[1].shape[0])
+    size, columns = piece.shape
+    first = pl.multiple_of(jnp.minimum(place[2] * size, weight.shape[0] - size), 16)
+    taken = copied(
+        weight.at[pl.ds(first, size), pl.ds(weight.shape[1] - columns, columns)], piece, semaphores.at[len(targets)]
+    )
 
     @pl.when(place[0] > 1)
     def _():
-        (early, _), (late, _) = parts_of(place[1], ranks, query.shape[0])
-        starts = (early, late, pl.multiple_of(late + targets[1].shape[0], 16))
         copies = [
-            copied(query.at[pl.ds(start, target.shape[0])], target, semaphores.at[index])
+            copied(
+                query.at[pl.ds(pl.multiple_of(start, 16), target.shape[0])], target, semaphores.at[index]
+            )
             for index, (start, target) in enumerate(zip(starts, targets))
         ]
         for copy in copies:
             copy.wait()
+
+    taken.wait()
 
 
 def local_kernel(spans, ranks, part, facts, query, key, value, key_beside, value_beside, result, sums, *scratch):
@@ -244,8 +253,9 @@
 
 def merged_blocks_kernel(spans, ranks, distances, facts, *refs):
     each = 2 + len(distances)
-    parts, (weight, attended, *results) = (refs[:each], refs[each:2 * each]), refs[2 * each:]
+    parts, (weight, attended, end_rows, *results) = (refs[:each], refs[each:2 * each]), refs[2 * each:]
     here = Facts(facts, spans)
+    block = end_rows.shape[0]
     work = project_blocks(ranks, 0, here, 1, attended, weight, *results)
     next(work)
     for (start, size), (own, own_sum, *served) in zip(parts_of(here.rank, ranks, attended.shape[0]), parts):
@@ -255,6 +265,8 @@
             attended[there, columns] = part
 
         merge(here.span, distances, own, own_sum, served, write)
+    inward = jnp.where(here.rank == 0, 1, ranks - 2)
+    end_rows[...] = attended[pl.ds(pl.multiple_of(inward * block, block), block), :]
     for _ in work:
         pass
 
@@ -264,19 +276,49 @@
         pass
 
 
-def own_kernel(spans, facts, attended, weight, gate_table, result, gate, tiles, gates, semaphores):
+def is_inner(rank, ranks):
+    return jnp.logical_or(rank == 1, rank == ranks - 2)
+
+
+def streamed_pairs(weight, first, end_weight, tiles, semaphores):
+    count, depth, tile = tiles.shape
+    width = depth // 2
+    copies = []
+    for index in range(count):
+        columns = pl.ds(first + index * tile, tile)
+        copies.append((
+            copied(weight.at[:, columns], tiles.at[index, pl.ds(0, width)], semaphores.at[2 * index]),
+            copied(
+                end_weight.at[:, pl.ds(index * tile, tile)], tiles.at[index, pl.ds(width, width)],
+                semaphores.at[2 * index + 1],
+            ),
+        ))
+    return copies
+
+
+def own_kernel(spans, ranks, facts, attended, end_rows, weight, end_weight, gate_table, result, gate,
+               tiles, pairs, gates, semaphores, pair_semaphores):
     here = Facts(facts, spans)
-    block = result.shape[0]
+    block, width = result.shape[0], attended.shape[1]
     count, _, tile = tiles.shape
+    columns = count * tile
     level = here.level()
     above = pl.multiple_of(level // 8 * 8, 8)
     gate_copy = copied(gate_table.at[pl.ds(above, 8)], gates, semaphores.at[count])
     copies = streamed(weight, 0, tiles, semaphores)
-    start = pl.multiple_of(here.rank * block, block)
+    pair_copies = streamed_pairs(weight, columns, end_weight, pairs, pair_semaphores)
+    mine = attended[pl.ds(pl.multiple_of(here.rank * block, block), block), :]
+    other = jnp.where(is_inner(here.rank, ranks), end_rows[...], jnp.zeros((block, width), jnp.bfloat16))
     for index, copy in enumerate(copies):
         copy.wait()
-        product = jnp.dot(attended[pl.ds(start, block), :], tiles[index], preferred_element_type=jnp.float32)
+        product = jnp.dot(mine, tiles[index], preferred_element_type=jnp.float32)
         result[:, index * tile:(index + 1) * tile] = product.astype(jnp.bfloat16)
+    both = jnp.concatenate([mine, other], axis=1)
+    for index, pair in enumerate(pair_copies):
+        for copy in pair:
+            copy.wait()
+        product = jnp.dot(both, pairs[index], preferred_element_type=jnp.float32)
+        result[:, columns + index * tile:columns + (index + 1) * tile] = product.astype(jnp.bfloat16)
     gate_copy.wait()
     gate[...] = gates[pl.ds(lax.rem(level, 8), 1), :]
 
@@ -314,16 +356,21 @@
     facts = jnp.concatenate([visible, place[None, :], levels[None, :]], axis=0)
 
     third = (rows - block) // 48 * 16
-    query_early, *query_late = pl.pallas_call(
+    columns = model // 2
+    plane = lax.axis_size("group") * spans
+    pieces = -(-width // (16 * plane)) * 16
+    here = jnp.stack([span, rank, lax.axis_index("group") * spans + span]).astype(jnp.int32)
+    query_early, *query_late, piece = pl.pallas_call(
         functools.partial(split_kernel, ranks),
-        in_specs=[SMEM, HBM],
-        out_specs=[VMEM] * 3,
-        out_shape=[jax.ShapeDtypeStruct((part, width), bf16) for part in (block, rows - block - third, third)],
-        scratch_shapes=[pltpu.SemaphoreType.DMA((3,))],
+        in_specs=[SMEM, HBM, HBM],
+        out_specs=[VMEM] * 4,
+        out_shape=[jax.ShapeDtypeStruct((part, width), bf16) for part in (block, rows - block - third, third)]
+        + [jax.ShapeDtypeStruct((pieces, columns), bf16)],
+        scratch_shapes=[pltpu.SemaphoreType.DMA((4,))],
         compiler_params=PARAMS,
         cost_estimate=taking(1.7),
         name="split",
-    )(jnp.stack([span, rank]).astype(jnp.int32), in_hbm(queries))
+    )(here, in_hbm(queries), in_hbm(out_weight))
     distances = list(range(2, spans, 2))
     asked_early = [shifted(query_early, "span", -distance) for distance in distances]
     swap = [(i, i + 1 - 2 * (i % 2)) for i in range(spans)]
@@ -361,12 +408,12 @@
 
     early = list(local(0, facts))
     query_late = after(query_late, early)
+    end_piece = lax.ppermute(after(piece, key_beside), "tensor", [(0, 1), (ranks - 1, ranks - 2)])
     asked_early = after(asked_early, early)
     asked_late = [[shifted(query, "span", -distance) for query in query_late] for distance in distances]
     early += [shifted(served([q], d), "span", d) for q, d in zip(asked_early, distances)]
 
     chunks = 2
-    columns = model // chunks
     tiles = 4
     tile = columns // tiles
     last = ranks - 1
@@ -391,7 +438,7 @@
     ends = [(0, 1), (last, last - 1)]
     sent = opening(0, facts)
     arrived = [[lax.ppermute(sent, "tensor", ends)]]
-    out_late = [served(q, d) for q, d in zip(after(asked_late, sent), distances)]
+    out_late = [served(q, d) for q, d in zip(after(asked_late, sent, end_piece), distances)]
     for chunk in range(1, chunks):
         sent = opening(chunk, after(facts, out_late))
         arrived.append([lax.ppermute(sent, "tensor", ends)])
@@ -405,14 +452,17 @@
     )
     attended_shape = jax.ShapeDtypeStruct((rows, width), bf16)
     block_shapes = [jax.ShapeDtypeStruct((block, columns), bf16)] * 2
-    attended, *merged = pl.pallas_call(
+    attended, end_rows, *merged = pl.pallas_call(
         functools.partial(merged_blocks_kernel, spans, ranks, distances),
         in_specs=[SMEM] + [VMEM] * (4 + 2 * len(distances)) + [HBM],
-        out_specs=[VMEM] * 3,
-        out_shape=[attended_shape] + block_shapes,
+        out_specs=[VMEM] * 4,
+        out_shape=[attended_shape, jax.ShapeDtypeStruct((block, width), bf16)] + block_shapes,
         name="merged_blocks",
         **streaming,
     )(facts, *early, *late, weight)
+
+    end_rows = lax.ppermute(end_rows, "tensor", ends)
+    end_weight = lax.all_gather(after(end_piece, attended), ("group", "span"), axis=0, tiled=True)[:width]
 
     def blocks_of(step, chunk, attended):
         return pl.pallas_call(
@@ -430,32 +480,34 @@
             if step == 1 and chunk == 0:
                 blocks = merged
             else:
-                blocks = blocks_of(step, chunk, after(attended, before))
+                blocks = blocks_of(step, chunk, after(attended, before, *[end_rows] * (step > 1)))
             comes, blocks = lax.optimization_barrier((arrived[chunk], blocks))
             up, down = [
                 (mine.astype(f32) + come.astype(f32)).astype(bf16)
                 for mine, come in zip(blocks, (comes[0], comes[-1]))
             ]
             before = (up, down)
+            senders = range(1 if (step, chunk) == (last - 1, 1) else 0, step + 1)
             arrived[chunk] = [
-                lax.ppermute(up, "tensor", [(i, i + 1) for i in range(step + 1)]),
-                lax.ppermute(down, "tensor", [(last - i, last - i - 1) for i in range(step + 1)]),
+                lax.ppermute(up, "tensor", [(i, i + 1) for i in senders]),
+                lax.ppermute(down, "tensor", [(last - i, last - i - 1) for i in senders]),
             ]
-    everything = chunks * tiles
     projected, gate = pl.pallas_call(
-        functools.partial(own_kernel, spans),
-        in_specs=[SMEM, VMEM, HBM, HBM],
+        functools.partial(own_kernel, spans, ranks),
+        in_specs=[SMEM, VMEM, VMEM, HBM, HBM, HBM],
         out_specs=[VMEM, VMEM],
         out_shape=[jax.ShapeDtypeStruct((block, model), bf16), jax.ShapeDtypeStruct((1, model), f32)],
         scratch_shapes=[
-            pltpu.VMEM((everything, width, tile), bf16),
+            pltpu.VMEM((tiles, width, tile), bf16),
+            pltpu.VMEM((tiles, 2 * width, tile), bf16),
             pltpu.VMEM((8, model), f32),
-            pltpu.SemaphoreType.DMA((everything + 1,)),
+            pltpu.SemaphoreType.DMA((tiles + 1,)),
+            pltpu.SemaphoreType.DMA((2 * tiles,)),
         ],
         compiler_params=PARAMS,
-        cost_estimate=taking(5.0),
+        cost_estimate=taking(7.0),
         name="own",
-    )(facts, after(attended, before), weight, in_hbm(gate_table))
+    )(facts, after(attended, before), end_rows, weight, in_hbm(end_weight), in_hbm(gate_table))
 
     finished = []
     for chunk in range(chunks - 1):

time: 102 us -> 142 us (1.39)
  waiting for transfers between devices: 27.1 us -> 42.1 us
  between operations: 0.55 us -> 13.8 us
  local copies, waits for them, and re-layouts: 0.01 us -> 3.92 us
  Pallas kernels: 32.7 us -> 36.3 us
  other arithmetic: 2.14 us -> 5.24 us
    ppermute x1, waiting for transfers between devices: 0.01 us -> 15.8 us  [body(): arrived = [[lax.ppermute(sent, 'tensor', ends)]]]
    ppermute x8 -> x10, waiting for transfers between devices: 16 us -> 10.8 us  [the longest x1 10.7 us: body(): end_rows = lax.ppermute(end_rows, 'tensor', ends)]
    unnamed x4 -> x20, local copies, waits for them, and re-layouts: 0.01 us -> 3.92 us
    pallas_call x1, Pallas kernels: 5.05 us -> 8.28 us  [body(): pl.pallas_call(functools.partial(own_kernel, spans, ranks), in_specs=[SME...]
    convert_element_type x6, other arithmetic: 1.09 us -> 3.65 us  [body(): (mine.astype(f32) + come.astype(f32)).astype(bf16)]
    ppermute x5, waiting for transfers between devices: 11.1 us -> 13.4 us  [shifted(): lax.ppermute(block, axis, [(i, i + distance) for i in range(count) if 0 <...]
    ppermute x1, waiting for transfers between devices: 0.01 us -> 1.98 us  [body(): arrived.append([lax.ppermute(sent, 'tensor', ends)])]
    ppermute x8 -> x10, starting transfers between devices: 24.8 us -> 25 us  [the longest x4 14.7 us: body(): lax.ppermute(up, 'tensor', [(i, i + 1) for i in senders])]
  transfers between devices with their start and end apart: 17 -> 20, of which waited for: 7 -> 7; matrix products, arithmetic and copies ran while one was open for 2% -> 4% of each run, Pallas kernels for 32% -> 22%
where the time goes in v14:
time: 142 us; the launch traced here: 140 us
  waiting for transfers between devices  42.1 us (30%)
  starting transfers between devices  38.8 us (27%)
  Pallas kernels  36.3 us (26%)
  between operations  13.8 us (10%)
  other arithmetic  5.24 us (4%)
  local copies, waits for them, and re-layouts  3.92 us (3%)
    ppermute x1, waiting for transfers between devices, body(): arrived = [[lax.ppermute(sent, 'tensor', ends)]]  15.8 us
    ppermute x4, starting transfers between devices, body(): lax.ppermute(up, 'tensor', [(i, i + 1) for i in senders])  14.7 us
    ppermute x5, waiting for transfers between devices, shifted(): lax.ppermute(block, axis, [(i, i + distance) for i in range(count) if 0 <...  13.4 us
    pallas_call x3, Pallas kernels, blocks_of(): pl.pallas_call(functools.partial(blocks_kernel, spans, ranks, chunk * col...  11.1 us
    ppermute x5, starting transfers between devices, shifted(): lax.ppermute(block, axis, [(i, i + distance) for i in range(count) if 0 <...  10.7 us
    ppermute x1, waiting for transfers between devices, body(): end_rows = lax.ppermute(end_rows, 'tensor', ends)  10.7 us
    pallas_call x1, Pallas kernels, body(): pl.pallas_call(functools.partial(own_kernel, spans, ranks), in_specs=[SME...  8.28 us
    ppermute x4, starting transfers between devices, body(): lax.ppermute(down, 'tensor', [(last - i, last - i - 1) for i in senders])  7.8 us
  transfers between devices with their start and end apart: 20, of which 7 were waited for; matrix products, arithmetic and copies ran while one was open for 4% of the time, Pallas kernels for 22%

profile of v14, /device:TPU:14, one launch (start us, length us, event | category | flops | bytes accessed | tf_op | source)
XLA Modules:
  0.0 140.3 jit_solution(4148246689515112168)
XLA Ops:
  6.5 0.5 collective-permute-start.1
  7.1 1.8 %split.1 = (bf16[96,768]{1,0:T(8,128)(2,1)S(1)}, bf16[192,768]{1,0:T(8,128)(2,1)S(1)}, bf16[96,768]{1,0:T(8,128)(2,1)S(1)}, bf16[96,3072]{1,0:T(8,128)(2,1)S(1)}) custom-call(s32[3]{0:T(128)S(1)} %pad_add_fusion.1.place, bf16[384,768]{1,0:T(8,128)(2,1)} %query.5, bf16[768,6144]{1,0:T(8,128)(2,1)} %weight.9), custom_call_target="tpu_custom_call" | custom-call | bytes 6273000 | tf_op jit(solution)/shard_map/split/pallas_call | solution.py:363
  9.0 1.3 collective-permute-start.6
  10.3 2.3 %collective-permute-start.2 = (bf16[96,768]{1,0:T(8,128)(2,1)S(1)}, bf16[96,768]{1,0:T(8,128)(2,1)S(1)}, u32[]{:S(2)}, u32[]{:S(2)}) collective-permute-start(bf16[96,768]{1,0:T(8,128)(2,1)S(1)} %get-tuple-element.54), channel_id=1, source_target_pairs={{8,0},{12,4},{9,1},{13,5},{10,2},{14,6},{11,3},{15,7},{24,16},{28,... | collective-permute-start | bytes 442376 | tf_op jit(solution)/shard_map/ppermute | solution.py:32
  12.6 3.4 %local.2 = (f32[96,768]{1,0:T(8,128)S(1)}, f32[96,128]{1,0:T(8,128)S(1)}) custom-call(s32[6,4]{1,0:T(8,128)S(1)} %pad_add_fusion.facts, bf16[384,768]{1,0:T(8,128)(2,1)} %query.5, bf16[384,768]{1,0:T(8,128)(2,1)} %key.7, bf16[384,768]{1,0:T(8,128)(2,1)} %value.7, bf16[384,768]{1,0:T(8,128)(2,1)S(1)} %collective-permute-done.key_beside, ...), custom_call_target="tpu_custom_call" | custom-call | bytes 14760000 | tf_op jit(solution)/shard_map/local/pallas_call | solution.py:385
  16.0 1.3 collective-permute-start.4
  17.4 0.6 served.2
  18.0 1.3 collective-permute-start.3
  19.3 4.6 %collective-permute-start.5 = (bf16[96,768]{1,0:T(8,128)(2,1)S(1)}, bf16[96,768]{1,0:T(8,128)(2,1)S(1)}, u32[]{:S(2)}, u32[]{:S(2)}) collective-permute-start(bf16[96,768]{1,0:T(8,128)(2,1)S(1)} %get-tuple-element.59), channel_id=1, source_target_pairs={{8,0},{12,4},{9,1},{13,5},{10,2},{14,6},{11,3},{15,7},{24,16},{28,... | collective-permute-start | bytes 442376 | tf_op jit(solution)/shard_map/ppermute | solution.py:32
  23.9 2.1 %collective-permute-done.3.refs_2_ = bf16[96,896]{1,0:T(8,128)(2,1)S(1)} collective-permute-done((bf16[96,896]{1,0:T(8,128)(2,1)S(1)}, bf16[96,896]{1,0:T(8,128)(2,1)S(1)}, u32[]{:S(2)}, u32[]{:S(2)}) %collective-permute-start.3) | collective-permute-done | bytes 172064 | tf_op jit(solution)/shard_map/ppermute | solution.py:32
  26.0 0.6 opening.2
  26.6 0.4 collective-permute-done.5.refs_1_
  27.0 0.6 copy-done.4
  27.6 0.7 copy-done.2
  28.3 1.0 copy-done.3
  29.3 0.9 copy-done.5
  30.2 0.6 served.3
  30.8 1.3 collective-permute-start.7
  32.1 0.6 opening.3
  32.8 4.3 %local.3 = (f32[288,768]{1,0:T(8,128)S(1)}, f32[288,128]{1,0:T(8,128)S(1)}) custom-call(s32[6,4]{1,0:T(8,128)S(1)} %pad_add_fusion.facts, bf16[384,768]{1,0:T(8,128)(2,1)} %query.5, bf16[384,768]{1,0:T(8,128)(2,1)} %key.7, bf16[384,768]{1,0:T(8,128)(2,1)} %value.7, bf16[384,768]{1,0:T(8,128)(2,1)S(1)} %collective-permute-done.key_beside, ...), custom_call_target="tpu_custom_call" | custom-call | bytes 14760000 | tf_op jit(solution)/shard_map/local/pallas_call | solution.py:385
  37.1 10.9 %collective-permute-done.7.refs_5_ = bf16[288,896]{1,0:T(8,128)(2,1)S(1)} collective-permute-done((bf16[288,896]{1,0:T(8,128)(2,1)S(1)}, bf16[288,896]{1,0:T(8,128)(2,1)S(1)}, u32[]{:S(2)}, u32[]{:S(2)}) %collective-permute-start.7) | collective-permute-done | bytes 516128 | tf_op jit(solution)/shard_map/ppermute | solution.py:32
  48.0 3.9 %merged_blocks.1 = (bf16[384,768]{1,0:T(8,128)(2,1)S(1)}, bf16[96,768]{1,0:T(8,128)(2,1)S(1)}, bf16[96,3072]{1,0:T(8,128)(2,1)S(1)}, bf16[96,3072]{1,0:T(8,128)(2,1)S(1)}) custom-call(s32[6,4]{1,0:T(8,128)S(1)} %pad_add_fusion.facts, f32[96,768]{1,0:T(8,128)S(1)} %get-tuple-element.52.refs_0_, f32[96,128]{1,0:T(8,128)S(1)} %get-tuple-element.53.refs_1_, ...), custom_call_target="tpu_custom_call" | custom-call | bytes 11070000 | tf_op jit(solution)/shard_map/merged_blocks/pallas_call | solution.py:455
  51.9 0.7 copy-done.6
  52.6 1.3 collective-permute-start.9
  53.9 1.3 collective-permute-start.8
  55.2 15.8 %collective-permute-done.9 = bf16[96,3072]{1,0:T(8,128)(2,1)S(1)} collective-permute-done((bf16[96,3072]{1,0:T(8,128)(2,1)S(1)}, bf16[96,3072]{1,0:T(8,128)(2,1)S(1)}, u32[]{:S(2)}, u32[]{:S(2)}) %collective-permute-start.9) | collective-permute-done | bytes 589856 | tf_op jit(solution)/shard_map/ppermute | solution.py:440
  71.0 0.3 fusion.1
  71.3 3.5 %collective-permute-start.12 = (bf16[96,3072]{1,0:T(8,128)(2,1)S(1)}, bf16[96,3072]{1,0:T(8,128)(2,1)S(1)}, u32[]{:S(2)}, u32[]{:S(2)}) collective-permute-start(bf16[96,3072]{1,0:T(8,128)(2,1)S(1)} %get-tuple-element.102), channel_id=1, source_target_pairs={{0,1},{1,2},{4,5},{5,6},{8,9},{9,10},{12,13},{13,14},{16,17},{17,1... | collective-permute-start | bytes 1769480 | tf_op jit(solution)/shard_map/ppermute | solution.py:492
  74.8 1.4 %collective-permute-start.13 = (bf16[96,3072]{1,0:T(8,128)(2,1)S(1)}, bf16[96,3072]{1,0:T(8,128)(2,1)S(1)}, u32[]{:S(2)}, u32[]{:S(2)}) collective-permute-start(bf16[96,3072]{1,0:T(8,128)(2,1)S(1)} %get-tuple-element.101), channel_id=1, source_target_pairs={{3,2},{2,1},{7,6},{6,5},{11,10},{10,9},{15,14},{14,13},{19,18},{18... | collective-permute-start | bytes 1769480 | tf_op jit(solution)/shard_map/ppermute | solution.py:493
  76.3 4.1 %blocks.3 = (bf16[96,3072]{1,0:T(8,128)(2,1)S(1)}, bf16[96,3072]{1,0:T(8,128)(2,1)S(1)}) custom-call(s32[6,4]{1,0:T(8,128)S(1)} %pad_add_fusion.facts, bf16[384,768]{1,0:T(8,128)(2,1)S(1)} %get-tuple-element.95.attended, bf16[768,6144]{1,0:T(8,128)(2,1)} %weight.9), custom_call_target="tpu_custom_call" | custom-call | bytes 11070000 | tf_op jit(solution)/shard_map/blocks/pallas_call | solution.py:468
  80.4 1.3 collective-permute-start.14
  81.7 2.0 %collective-permute-done.8 = bf16[96,3072]{1,0:T(8,128)(2,1)S(1)} collective-permute-done((bf16[96,3072]{1,0:T(8,128)(2,1)S(1)}, bf16[96,3072]{1,0:T(8,128)(2,1)S(1)}, u32[]{:S(2)}, u32[]{:S(2)}) %collective-permute-start.8) | collective-permute-done | bytes 589856 | tf_op jit(solution)/shard_map/ppermute | solution.py:444
  83.6 0.3 fusion.3
  83.9 3.5 %collective-permute-start.10 = (bf16[96,3072]{1,0:T(8,128)(2,1)S(1)}, bf16[96,3072]{1,0:T(8,128)(2,1)S(1)}, u32[]{:S(2)}, u32[]{:S(2)}) collective-permute-start(bf16[96,3072]{1,0:T(8,128)(2,1)S(1)} %get-tuple-element.100), channel_id=1, source_target_pairs={{0,1},{1,2},{4,5},{5,6},{8,9},{9,10},{12,13},{13,14},{16,17},{17,1... | collective-permute-start | bytes 1769480 | tf_op jit(solution)/shard_map/ppermute | solution.py:492
  87.4 1.3 collective-permute-start.11
  88.7 10.7 %collective-permute-done.14.end_rows = bf16[96,768]{1,0:T(8,128)(2,1)S(1)} collective-permute-done((bf16[96,768]{1,0:T(8,128)(2,1)S(1)}, bf16[96,768]{1,0:T(8,128)(2,1)S(1)}, u32[]{:S(2)}, u32[]{:S(2)}) %collective-permute-start.14) | collective-permute-done | bytes 147488 | tf_op jit(solution)/shard_map/ppermute | solution.py:464
  99.4 3.5 %blocks.4 = (bf16[96,3072]{1,0:T(8,128)(2,1)S(1)}, bf16[96,3072]{1,0:T(8,128)(2,1)S(1)}) custom-call(s32[6,4]{1,0:T(8,128)S(1)} %pad_add_fusion.facts, bf16[384,768]{1,0:T(8,128)(2,1)S(1)} %get-tuple-element.95.attended, bf16[768,6144]{1,0:T(8,128)(2,1)} %weight.9), custom_call_target="tpu_custom_call" | custom-call | bytes 11070000 | tf_op jit(solution)/shard_map/blocks/pallas_call | solution.py:468
  103.0 1.0 add_convert_fusion.3
  103.9 3.5 %collective-permute-start.15 = (bf16[96,3072]{1,0:T(8,128)(2,1)}, bf16[96,3072]{1,0:T(8,128)(2,1)}, u32[]{:S(2)}, u32[]{:S(2)}) collective-permute-start(bf16[96,3072]{1,0:T(8,128)(2,1)} %add_convert_fusion.3), channel_id=1, source_target_pairs={{0,1},{1,2},{2,3},{4,5},{5,6},{6,7},{8,9},{9,10},{10,11},{12,13},{... | collective-permute-start | bytes 1769480 | tf_op jit(solution)/shard_map/ppermute | solution.py:492
  107.4 1.0 add_convert_fusion.2
  108.4 3.2 %collective-permute-start.16 = (bf16[96,3072]{1,0:T(8,128)(2,1)}, bf16[96,3072]{1,0:T(8,128)(2,1)}, u32[]{:S(2)}, u32[]{:S(2)}) collective-permute-start(bf16[96,3072]{1,0:T(8,128)(2,1)} %add_convert_fusion.2), channel_id=1, source_target_pairs={{3,2},{2,1},{1,0},{7,6},{6,5},{5,4},{11,10},{10,9},{9,8},{15,14},{... | collective-permute-start | bytes 1769480 | tf_op jit(solution)/shard_map/ppermute | solution.py:493
  111.6 3.5 %blocks.5 = (bf16[96,3072]{1,0:T(8,128)(2,1)S(1)}, bf16[96,3072]{1,0:T(8,128)(2,1)S(1)}) custom-call(s32[6,4]{1,0:T(8,128)S(1)} %pad_add_fusion.facts, bf16[384,768]{1,0:T(8,128)(2,1)S(1)} %get-tuple-element.95.attended, bf16[768,6144]{1,0:T(8,128)(2,1)} %weight.9), custom_call_target="tpu_custom_call" | custom-call | bytes 11070000 | tf_op jit(solution)/shard_map/blocks/pallas_call | solution.py:468
  115.3 1.9 %collective-permute-start.18 = (bf16[96,3072]{1,0:T(8,128)(2,1)S(1)}, bf16[96,3072]{1,0:T(8,128)(2,1)S(1)}, u32[]{:S(2)}, u32[]{:S(2)}) collective-permute-start(bf16[96,3072]{1,0:T(8,128)(2,1)S(1)} %add_convert_fusion), channel_id=1, source_target_pairs={{2,1},{1,0},{6,5},{5,4},{10,9},{9,8},{14,13},{13,12},{18,17},{17,1... | collective-permute-start | bytes 1769480 | tf_op jit(solution)/shard_map/ppermute | solution.py:493
  117.2 1.0 add_convert_fusion.1
  118.2 4.2 %collective-permute-start.17 = (bf16[96,3072]{1,0:T(8,128)(2,1)}, bf16[96,3072]{1,0:T(8,128)(2,1)S(1)}, u32[]{:S(2)}, u32[]{:S(2)}) collective-permute-start(bf16[96,3072]{1,0:T(8,128)(2,1)} %add_convert_fusion.1), channel_id=1, source_target_pairs={{1,2},{2,3},{5,6},{6,7},{9,10},{10,11},{13,14},{14,15},{17,18},{18... | collective-permute-start | bytes 1769480 | tf_op jit(solution)/shard_map/ppermute | solution.py:492
  122.4 8.3 %own.1 = (bf16[96,6144]{1,0:T(8,128)(2,1)S(1)}, f32[1,6144]{1,0:T(1,128)S(1)}) custom-call(s32[6,4]{1,0:T(8,128)S(1)} %pad_add_fusion.facts, bf16[384,768]{1,0:T(8,128)(2,1)S(1)} %get-tuple-element.95.attended, bf16[96,768]{1,0:T(8,128)(2,1)S(1)} %collective-permute-done.14.end_rows, bf16[768,6144]{1,0:T(8,128)(2,1)} %weight.9, ...), custom_call_target="tpu_custom_call" | custom-call | bytes 25830000 | tf_op jit(solution)/shard_map/own/pallas_call | solution.py:495
  130.7 1.5 %multiply_convert_fusion.done = bf16[96,3072]{1,0:T(8,128)(2,1)S(1)} fusion(bf16[96,3072]{1,0:T(8,128)(2,1)} %collective-permute-done.16, bf16[96,3072]{1,0:T(8,128)(2,1)} %collective-permute-done.15, f32[3072]{0:T(1024)S(1)} %bitcast.5, bf16[96,6144]{1,0:T(8,128)(2,1)S(1)} %get-tuple-element.97.projected), kind=kLoop, calls=%fused_computation.8 | loop fusion | flops 2064384 | bytes 2371584 | tf_op jit(solution)/shard_map/convert_element_type | solution.py:516
  132.4 1.1 final.1
  (37 shorter events, 0.5 us)
Async XLA Ops:
  6.5 115.9 %all-gather.2.cloned.1.call-start = ((), (), s32[]{:S(2)}) async-start(), calls=%async_computation | async-start | bytes 5308416 | tf_op jit(solution)/shard_map/all_gather | solution.py:465
  6.5 2.4 %collective-permute-start = (bf16[384,768]{1,0:T(8,128)(2,1)}, bf16[384,768]{1,0:T(8,128)(2,1)S(1)}, u32[]{:S(2)}, u32[]{:S(2)}) collective-permute-start(bf16[384,768]{1,0:T(8,128)(2,1)} %key.7), channel_id=1, source_target_pairs={{0,4},{4,0},{8,12},{12,8},{1,5},{5,1},{9,13},{13,9},{2,6},{6,2},{1... | collective-permute-start | bytes 1769480 | tf_op jit(solution)/shard_map/ppermute | solution.py:377
  6.5 6.1 %collective-permute-start.1 = (bf16[384,768]{1,0:T(8,128)(2,1)}, bf16[384,768]{1,0:T(8,128)(2,1)S(1)}, u32[]{:S(2)}, u32[]{:S(2)}) collective-permute-start(bf16[384,768]{1,0:T(8,128)(2,1)} %value.7), channel_id=1, source_target_pairs={{0,4},{4,0},{8,12},{12,8},{1,5},{5,1},{9,13},{13,9},{2,6},{6,2},{1... | collective-permute-start | bytes 1769480 | tf_op jit(solution)/shard_map/ppermute | solution.py:378
  7.1 5.4 %copy-start.8 = (s32[4,4]{1,0:T(4,128)S(1)}, s32[4,4]{1,0:T(4,128)}, u32[]{:S(2)}) copy-start(s32[4,4]{1,0:T(4,128)} %param.13) | copy-start | bytes 196
  7.1 5.4 %copy-start.9 = (s32[4]{0:T(128)S(1)}, s32[4]{0:T(128)}, u32[]{:S(2)}) copy-start(s32[4]{0:T(128)} %param.12) | copy-start | bytes 52
  9.0 19.4 %collective-permute-start.6 = (bf16[96,3072]{1,0:T(8,128)(2,1)S(1)}, bf16[96,3072]{1,0:T(8,128)(2,1)}, u32[]{:S(2)}, u32[]{:S(2)}) collective-permute-start(bf16[96,3072]{1,0:T(8,128)(2,1)S(1)} %get-tuple-element.61), channel_id=1, source_target_pairs={{0,1},{3,2},{4,5},{7,6},{8,9},{11,10},{12,13},{15,14},{16,17},{19,... | collective-permute-start | bytes 1769480 | tf_op jit(solution)/shard_map/ppermute | solution.py:411
  10.3 7.1 %collective-permute-start.2 = (bf16[96,768]{1,0:T(8,128)(2,1)S(1)}, bf16[96,768]{1,0:T(8,128)(2,1)S(1)}, u32[]{:S(2)}, u32[]{:S(2)}) collective-permute-start(bf16[96,768]{1,0:T(8,128)(2,1)S(1)} %get-tuple-element.54), channel_id=1, source_target_pairs={{8,0},{12,4},{9,1},{13,5},{10,2},{14,6},{11,3},{15,7},{24,16},{28,... | collective-permute-start | bytes 442376 | tf_op jit(solution)/shard_map/ppermute | solution.py:32
  12.6 4.8 %copy-start = (bf16[384,768]{1,0:T(8,128)(2,1)S(1)}, bf16[384,768]{1,0:T(8,128)(2,1)}, u32[]{:S(2)}) copy-start(bf16[384,768]{1,0:T(8,128)(2,1)} %key.7) | copy-start | bytes 1769476
  12.6 4.8 %copy-start.1 = (bf16[384,768]{1,0:T(8,128)(2,1)S(1)}, bf16[384,768]{1,0:T(8,128)(2,1)}, u32[]{:S(2)}) copy-start(bf16[384,768]{1,0:T(8,128)(2,1)} %value.7) | copy-start | bytes 1769476
  16.0 11.6 %collective-permute-start.4 = (bf16[192,768]{1,0:T(8,128)(2,1)S(1)}, bf16[192,768]{1,0:T(8,128)(2,1)S(1)}, u32[]{:S(2)}, u32[]{:S(2)}) collective-permute-start(bf16[192,768]{1,0:T(8,128)(2,1)S(1)} %get-tuple-element.58), channel_id=1, source_target_pairs={{8,0},{12,4},{9,1},{13,5},{10,2},{14,6},{11,3},{15,7},{24,16},{28,... | collective-permute-start | bytes 884744 | tf_op jit(solution)/shard_map/ppermute | solution.py:32
  18.0 8.0 %collective-permute-start.3 = (bf16[96,896]{1,0:T(8,128)(2,1)S(1)}, bf16[96,896]{1,0:T(8,128)(2,1)S(1)}, u32[]{:S(2)}, u32[]{:S(2)}) collective-permute-start(bf16[96,896]{1,0:T(8,128)(2,1)S(1)} %served.2), channel_id=1, source_target_pairs={{0,8},{4,12},{1,9},{5,13},{2,10},{6,14},{3,11},{7,15},{16,24},{20,... | collective-permute-start | bytes 516104 | tf_op jit(solution)/shard_map/ppermute | solution.py:32
  19.3 7.7 %collective-permute-start.5 = (bf16[96,768]{1,0:T(8,128)(2,1)S(1)}, bf16[96,768]{1,0:T(8,128)(2,1)S(1)}, u32[]{:S(2)}, u32[]{:S(2)}) collective-permute-start(bf16[96,768]{1,0:T(8,128)(2,1)S(1)} %get-tuple-element.59), channel_id=1, source_target_pairs={{8,0},{12,4},{9,1},{13,5},{10,2},{14,6},{11,3},{15,7},{24,16},{28,... | collective-permute-start | bytes 442376 | tf_op jit(solution)/shard_map/ppermute | solution.py:32
  27.0 0.7 copy-start.4
  27.6 0.7 copy-start.2
  28.3 1.0 copy-start.3
  29.3 0.9 copy-start.5
  30.8 17.2 %collective-permute-start.7 = (bf16[288,896]{1,0:T(8,128)(2,1)S(1)}, bf16[288,896]{1,0:T(8,128)(2,1)S(1)}, u32[]{:S(2)}, u32[]{:S(2)}) collective-permute-start(bf16[288,896]{1,0:T(8,128)(2,1)S(1)} %served.3), channel_id=1, source_target_pairs={{0,8},{4,12},{1,9},{5,13},{2,10},{6,14},{3,11},{7,15},{16,24},{20,... | collective-permute-start | bytes 1548296 | tf_op jit(solution)/shard_map/ppermute | solution.py:32
  51.9 0.7 copy-start.6
  52.6 18.4 %collective-permute-start.9 = (bf16[96,3072]{1,0:T(8,128)(2,1)S(1)}, bf16[96,3072]{1,0:T(8,128)(2,1)S(1)}, u32[]{:S(2)}, u32[]{:S(2)}) collective-permute-start(bf16[96,3072]{1,0:T(8,128)(2,1)S(1)} %opening.2), channel_id=1, source_target_pairs={{0,1},{3,2},{4,5},{7,6},{8,9},{11,10},{12,13},{15,14},{16,17},{19,... | collective-permute-start | bytes 1769480 | tf_op jit(solution)/shard_map/ppermute | solution.py:440
  53.9 29.8 %collective-permute-start.8 = (bf16[96,3072]{1,0:T(8,128)(2,1)S(1)}, bf16[96,3072]{1,0:T(8,128)(2,1)S(1)}, u32[]{:S(2)}, u32[]{:S(2)}) collective-permute-start(bf16[96,3072]{1,0:T(8,128)(2,1)S(1)} %opening.3), channel_id=1, source_target_pairs={{0,1},{3,2},{4,5},{7,6},{8,9},{11,10},{12,13},{15,14},{16,17},{19,... | collective-permute-start | bytes 1769480 | tf_op jit(solution)/shard_map/ppermute | solution.py:444
  71.3 31.7 %collective-permute-start.12 = (bf16[96,3072]{1,0:T(8,128)(2,1)S(1)}, bf16[96,3072]{1,0:T(8,128)(2,1)S(1)}, u32[]{:S(2)}, u32[]{:S(2)}) collective-permute-start(bf16[96,3072]{1,0:T(8,128)(2,1)S(1)} %get-tuple-element.102), channel_id=1, source_target_pairs={{0,1},{1,2},{4,5},{5,6},{8,9},{9,10},{12,13},{13,14},{16,17},{17,1... | collective-permute-start | bytes 1769480 | tf_op jit(solution)/shard_map/ppermute | solution.py:492
  74.8 5.6 %copy-start.7 = (bf16[96,768]{1,0:T(8,128)(2,1)S(1)}, bf16[96,768]{1,0:T(8,128)(2,1)}, u32[]{:S(2)}) copy-start(bf16[96,768]{1,0:T(8,128)(2,1)} %copy-done.6) | copy-start | bytes 442372
  74.8 28.2 %collective-permute-start.13 = (bf16[96,3072]{1,0:T(8,128)(2,1)S(1)}, bf16[96,3072]{1,0:T(8,128)(2,1)S(1)}, u32[]{:S(2)}, u32[]{:S(2)}) collective-permute-start(bf16[96,3072]{1,0:T(8,128)(2,1)S(1)} %get-tuple-element.101), channel_id=1, source_target_pairs={{3,2},{2,1},{7,6},{6,5},{11,10},{10,9},{15,14},{14,13},{19,18},{18... | collective-permute-start | bytes 1769480 | tf_op jit(solution)/shard_map/ppermute | solution.py:493
  80.4 19.1 %collective-permute-start.14 = (bf16[96,768]{1,0:T(8,128)(2,1)S(1)}, bf16[96,768]{1,0:T(8,128)(2,1)S(1)}, u32[]{:S(2)}, u32[]{:S(2)}) collective-permute-start(bf16[96,768]{1,0:T(8,128)(2,1)S(1)} %copy-done.7), channel_id=1, source_target_pairs={{0,1},{3,2},{4,5},{7,6},{8,9},{11,10},{12,13},{15,14},{16,17},{19,... | collective-permute-start | bytes 442376 | tf_op jit(solution)/shard_map/ppermute | solution.py:464
  83.9 31.1 %collective-permute-start.10 = (bf16[96,3072]{1,0:T(8,128)(2,1)S(1)}, bf16[96,3072]{1,0:T(8,128)(2,1)S(1)}, u32[]{:S(2)}, u32[]{:S(2)}) collective-permute-start(bf16[96,3072]{1,0:T(8,128)(2,1)S(1)} %get-tuple-element.100), channel_id=1, source_target_pairs={{0,1},{1,2},{4,5},{5,6},{8,9},{9,10},{12,13},{13,14},{16,17},{17,1... | collective-permute-start | bytes 1769480 | tf_op jit(solution)/shard_map/ppermute | solution.py:492
  87.4 27.6 %collective-permute-start.11 = (bf16[96,3072]{1,0:T(8,128)(2,1)S(1)}, bf16[96,3072]{1,0:T(8,128)(2,1)S(1)}, u32[]{:S(2)}, u32[]{:S(2)}) collective-permute-start(bf16[96,3072]{1,0:T(8,128)(2,1)S(1)} %get-tuple-element.99), channel_id=1, source_target_pairs={{3,2},{2,1},{7,6},{6,5},{11,10},{10,9},{15,14},{14,13},{19,18},{18... | collective-permute-start | bytes 1769480 | tf_op jit(solution)/shard_map/ppermute | solution.py:493
  103.9 26.8 %collective-permute-start.15 = (bf16[96,3072]{1,0:T(8,128)(2,1)}, bf16[96,3072]{1,0:T(8,128)(2,1)}, u32[]{:S(2)}, u32[]{:S(2)}) collective-permute-start(bf16[96,3072]{1,0:T(8,128)(2,1)} %add_convert_fusion.3), channel_id=1, source_target_pairs={{0,1},{1,2},{2,3},{4,5},{5,6},{6,7},{8,9},{9,10},{10,11},{12,13},{... | collective-permute-start | bytes 1769480 | tf_op jit(solution)/shard_map/ppermute | solution.py:492
  108.4 22.3 %collective-permute-start.16 = (bf16[96,3072]{1,0:T(8,128)(2,1)}, bf16[96,3072]{1,0:T(8,128)(2,1)}, u32[]{:S(2)}, u32[]{:S(2)}) collective-permute-start(bf16[96,3072]{1,0:T(8,128)(2,1)} %add_convert_fusion.2), channel_id=1, source_target_pairs={{3,2},{2,1},{1,0},{7,6},{6,5},{5,4},{11,10},{10,9},{9,8},{15,14},{... | collective-permute-start | bytes 1769480 | tf_op jit(solution)/shard_map/ppermute | solution.py:493
  115.3 17.1 %collective-permute-start.18 = (bf16[96,3072]{1,0:T(8,128)(2,1)S(1)}, bf16[96,3072]{1,0:T(8,128)(2,1)S(1)}, u32[]{:S(2)}, u32[]{:S(2)}) collective-permute-start(bf16[96,3072]{1,0:T(8,128)(2,1)S(1)} %add_convert_fusion), channel_id=1, source_target_pairs={{2,1},{1,0},{6,5},{5,4},{10,9},{9,8},{14,13},{13,12},{18,17},{17,1... | collective-permute-start | bytes 1769480 | tf_op jit(solution)/shard_map/ppermute | solution.py:493
  118.2 14.2 %collective-permute-start.17 = (bf16[96,3072]{1,0:T(8,128)(2,1)}, bf16[96,3072]{1,0:T(8,128)(2,1)S(1)}, u32[]{:S(2)}, u32[]{:S(2)}) collective-permute-start(bf16[96,3072]{1,0:T(8,128)(2,1)} %add_convert_fusion.1), channel_id=1, source_target_pairs={{1,2},{2,3},{5,6},{6,7},{9,10},{10,11},{13,14},{14,15},{17,18},{18... | collective-permute-start | bytes 1769480 | tf_op jit(solution)/shard_map/ppermute | solution.py:492
Sparse Core Ops, SparseCore 0:
  52.7 40.4 all-gather.1

commit v15 on v13

--- a/solution.py
+++ b/solution.py
@@ -191,22 +191,32 @@
     ]
 
 
-def opening_kernel(spans, ranks, distances, first, facts, *refs):
+def fetch_kernel(weight, tiles, semaphores):
+    for copy in streamed(weight, 0, tiles, semaphores):
+        copy.wait()
+
+
+def opening_kernel(ranks, distances, spans, first, facts, *refs):
     own, own_sum, *served = refs[:2 + len(distances)]
-    weight, result, tiles, rows, semaphores = refs[2 + len(distances):]
+    weight, result, *scratch = refs[2 + len(distances):]
+    rows = scratch[-1]
     here = Facts(facts, spans)
-    tile = tiles.shape[2]
 
     @pl.when(jnp.logical_or(here.rank == 0, here.rank == ranks - 1))
     def _():
-        copies = streamed(weight, first, tiles, semaphores)
+        tiles, copies = weight, [None] * weight.shape[0]
+        if first:
+            tiles, semaphores, _ = scratch
+            copies = streamed(weight, first, tiles, semaphores)
 
         def write(columns, part):
             rows[:, columns] = part
 
         merge(here.span, distances, own, own_sum, served, write)
+        tile = tiles.shape[2]
         for index, copy in enumerate(copies):
-            copy.wait()
+            if copy is not None:
+                copy.wait()
             product = jnp.dot(rows[...], tiles[index], preferred_element_type=jnp.float32)
             result[:, index * tile:(index + 1) * tile] = product.astype(jnp.bfloat16)
 
@@ -363,7 +373,8 @@
     query_late = after(query_late, early)
     asked_early = after(asked_early, early)
     asked_late = [[shifted(query, "span", -distance) for query in query_late] for distance in distances]
-    early += [shifted(served([q], d), "span", d) for q, d in zip(asked_early, distances)]
+    out_early = [served([q], d) for q, d in zip(asked_early, distances)]
+    early += [shifted(o, "span", d) for o, d in zip(out_early, distances)]
 
     chunks = 2
     columns = model // chunks
@@ -372,21 +383,35 @@
     last = ranks - 1
     weight = in_hbm(out_weight)
 
+    tile_shape = (tiles, width, tile)
+    streaming = dict(
+        scratch_shapes=[pltpu.VMEM(tile_shape, bf16), pltpu.SemaphoreType.DMA((tiles,))],
+        compiler_params=PARAMS,
+        cost_estimate=taking(3.0),
+    )
+    fetched = pl.pallas_call(
+        fetch_kernel,
+        in_specs=[HBM],
+        out_specs=VMEM,
+        out_shape=jax.ShapeDtypeStruct(tile_shape, bf16),
+        scratch_shapes=[pltpu.SemaphoreType.DMA((tiles,))],
+        compiler_params=PARAMS,
+        cost_estimate=taking(2.4),
+        name="fetch",
+    )(in_hbm(after(out_weight, out_early)))
+
     def opening(chunk, facts):
+        scratch = streaming["scratch_shapes"] if chunk else []
         return pl.pallas_call(
-            functools.partial(opening_kernel, spans, ranks, distances, chunk * columns),
-            in_specs=[SMEM] + [VMEM] * (2 + len(distances)) + [HBM],
+            functools.partial(opening_kernel, ranks, distances, spans, chunk * columns),
+            in_specs=[SMEM] + [VMEM] * (2 + len(distances)) + [HBM if chunk else VMEM],
             out_specs=VMEM,
             out_shape=jax.ShapeDtypeStruct((block, columns), bf16),
-            scratch_shapes=[
-                pltpu.VMEM((2, width, columns // 2), bf16),
-                pltpu.VMEM((block, width), bf16),
-                pltpu.SemaphoreType.DMA((2,)),
-            ],
+            scratch_shapes=scratch + [pltpu.VMEM((block, width), bf16)],
             compiler_params=PARAMS,
             cost_estimate=taking(3.4),
             name="opening",
-        )(facts, *early, weight)
+        )(facts, *early, weight if chunk else fetched)
 
     ends = [(0, 1), (last, last - 1)]
     sent = opening(0, facts)
@@ -398,11 +423,6 @@
     late = list(local(1, after(facts, sent)))
     late += [shifted(o, "span", d) for o, d in zip(out_late, distances)]
 
-    streaming = dict(
-        scratch_shapes=[pltpu.VMEM((tiles, width, tile), bf16), pltpu.SemaphoreType.DMA((tiles,))],
-        compiler_params=PARAMS,
-        cost_estimate=taking(3.0),
-    )
     attended_shape = jax.ShapeDtypeStruct((rows, width), bf16)
     block_shapes = [jax.ShapeDtypeStruct((block, columns), bf16)] * 2
     attended, *merged = pl.pallas_call(

time: 102 us -> 101 us (level)
  Pallas kernels: 32.7 us -> 35.1 us
  waiting for transfers between devices: 27.1 us -> 25.5 us
  starting transfers between devices: 37.7 us -> 36.3 us
    pallas_call x2 -> x3, Pallas kernels: 1.25 us -> 3.65 us  [the longest x1 2.39 us: body(): pl.pallas_call(fetch_kernel, in_specs=[HBM], out_specs=VMEM, out_shape=ja...]
    ppermute x5, waiting for transfers between devices: 11.1 us -> 8.71 us  [shifted(): lax.ppermute(block, axis, [(i, i + distance) for i in range(count) if 0 <...]
    ppermute x4, starting transfers between devices: 18.3 us -> 16.9 us  [body(): lax.ppermute(up, 'tensor', [(i, i + 1) for i in range(step + 1)])]
    ppermute x4, waiting for transfers between devices: 6.81 us -> 7.99 us  [body(): lax.ppermute(down, 'tensor', [(last - i, last - i - 1) for i in range(ste...]
  transfers between devices with their start and end apart: 17 -> 17, of which waited for: 7 -> 7; matrix products, arithmetic and copies ran while one was open for 2% -> 2% of each run, Pallas kernels for 32% -> 34%
where the time goes in v15:
time: 101 us; the launch traced here: 99.6 us
  starting transfers between devices  36.3 us (36%)
  Pallas kernels  35.1 us (35%)
  waiting for transfers between devices  25.5 us (25%)
  other arithmetic  2.14 us (2%)
    ppermute x4, starting transfers between devices, body(): lax.ppermute(up, 'tensor', [(i, i + 1) for i in range(step + 1)])  16.9 us
    pallas_call x3, Pallas kernels, blocks_of(): pl.pallas_call(functools.partial(blocks_kernel, spans, ranks, chunk * col...  10.3 us
    ppermute x5, starting transfers between devices, shifted(): lax.ppermute(block, axis, [(i, i + distance) for i in range(count) if 0 <...  9.81 us
    ppermute x4, waiting for transfers between devices, body(): lax.ppermute(up, 'tensor', [(i, i + 1) for i in range(step + 1)])  8.8 us
    ppermute x5, waiting for transfers between devices, shifted(): lax.ppermute(block, axis, [(i, i + distance) for i in range(count) if 0 <...  8.71 us
    ppermute x4, waiting for transfers between devices, body(): lax.ppermute(down, 'tensor', [(last - i, last - i - 1) for i in range(ste...  7.99 us
    pallas_call x2, Pallas kernels, local(): pl.pallas_call(functools.partial(local_kernel, spans, ranks, part), in_sp...  7.7 us
    ppermute x4, starting transfers between devices, body(): lax.ppermute(down, 'tensor', [(last - i, last - i - 1) for i in range(ste...  6.43 us
  transfers between devices with their start and end apart: 17, of which 7 were waited for; matrix products, arithmetic and copies ran while one was open for 2% of the time, Pallas kernels for 34%

profile of v15, /device:TPU:14, one launch (start us, length us, event | category | flops | bytes accessed | tf_op | source)
XLA Modules:
  0.0 99.6 jit_solution(10697195977868552648)
XLA Ops:
  0.0 0.5 collective-permute-start.1
  0.5 0.1 pad_add_fusion.1.place
  0.6 1.6 %split.1 = (bf16[96,768]{1,0:T(8,128)(2,1)S(1)}, bf16[192,768]{1,0:T(8,128)(2,1)S(1)}, bf16[96,768]{1,0:T(8,128)(2,1)S(1)}) custom-call(s32[2]{0:T(128)S(1)} %pad_add_fusion.1.place, bf16[384,768]{1,0:T(8,128)(2,1)} %query.5), custom_call_target="tpu_custom_call" | custom-call | bytes 6273000 | tf_op jit(solution)/shard_map/split/pallas_call | solution.py:327
  2.2 1.4 %collective-permute-start.2 = (bf16[96,768]{1,0:T(8,128)(2,1)S(1)}, bf16[96,768]{1,0:T(8,128)(2,1)S(1)}, u32[]{:S(2)}, u32[]{:S(2)}) collective-permute-start(bf16[96,768]{1,0:T(8,128)(2,1)S(1)} %get-tuple-element.51), channel_id=1, source_target_pairs={{8,0},{12,4},{9,1},{13,5},{10,2},{14,6},{11,3},{15,7},{24,16},{28,... | collective-permute-start | bytes 442376 | tf_op jit(solution)/shard_map/ppermute | solution.py:32
  3.6 0.7 pad_add_fusion.facts
  4.3 0.0 copy-start.1
  4.3 0.0 collective-permute-done.key_beside
  4.4 3.4 %local.2 = (f32[96,768]{1,0:T(8,128)S(1)}, f32[96,128]{1,0:T(8,128)S(1)}) custom-call(s32[6,4]{1,0:T(8,128)S(1)} %pad_add_fusion.facts, bf16[384,768]{1,0:T(8,128)(2,1)} %query.5, bf16[384,768]{1,0:T(8,128)(2,1)} %key.7, bf16[384,768]{1,0:T(8,128)(2,1)} %value.7, bf16[384,768]{1,0:T(8,128)(2,1)S(1)} %collective-permute-done.key_beside, ...), custom_call_target="tpu_custom_call" | custom-call | bytes 14760000 | tf_op jit(solution)/shard_map/local/pallas_call | solution.py:348
  7.8 1.3 %collective-permute-start.4 = (bf16[192,768]{1,0:T(8,128)(2,1)S(1)}, bf16[192,768]{1,0:T(8,128)(2,1)S(1)}, u32[]{:S(2)}, u32[]{:S(2)}) collective-permute-start(bf16[192,768]{1,0:T(8,128)(2,1)S(1)} %get-tuple-element.55), channel_id=1, source_target_pairs={{8,0},{12,4},{9,1},{13,5},{10,2},{14,6},{11,3},{15,7},{24,16},{28,... | collective-permute-start | bytes 884744 | tf_op jit(solution)/shard_map/ppermute | solution.py:32
  9.1 0.6 served.2
  9.7 1.3 %collective-permute-start.3 = (bf16[96,896]{1,0:T(8,128)(2,1)S(1)}, bf16[96,896]{1,0:T(8,128)(2,1)S(1)}, u32[]{:S(2)}, u32[]{:S(2)}) collective-permute-start(bf16[96,896]{1,0:T(8,128)(2,1)S(1)} %served.2), channel_id=1, source_target_pairs={{0,8},{4,12},{1,9},{5,13},{2,10},{6,14},{3,11},{7,15},{16,24},{20,... | collective-permute-start | bytes 516104 | tf_op jit(solution)/shard_map/ppermute | solution.py:32
  11.0 4.6 %collective-permute-start.5 = (bf16[96,768]{1,0:T(8,128)(2,1)S(1)}, bf16[96,768]{1,0:T(8,128)(2,1)S(1)}, u32[]{:S(2)}, u32[]{:S(2)}) collective-permute-start(bf16[96,768]{1,0:T(8,128)(2,1)S(1)} %get-tuple-element.56), channel_id=1, source_target_pairs={{8,0},{12,4},{9,1},{13,5},{10,2},{14,6},{11,3},{15,7},{24,16},{28,... | collective-permute-start | bytes 442376 | tf_op jit(solution)/shard_map/ppermute | solution.py:32
  15.6 2.4 %fetch.1.refs_3_ = bf16[4,768,768]{2,1,0:T(8,128)(2,1)S(1)} custom-call(bf16[768,6144]{1,0:T(8,128)(2,1)} %weight.8), custom_call_target="tpu_custom_call" | custom-call | bytes 8856000 | tf_op jit(solution)/shard_map/fetch/pallas_call | solution.py:392
  18.0 0.6 opening.2
  18.6 1.3 %collective-permute-start.8 = (bf16[96,3072]{1,0:T(8,128)(2,1)S(1)}, bf16[96,3072]{1,0:T(8,128)(2,1)S(1)}, u32[]{:S(2)}, u32[]{:S(2)}) collective-permute-start(bf16[96,3072]{1,0:T(8,128)(2,1)S(1)} %opening.2), channel_id=1, source_target_pairs={{0,1},{3,2},{4,5},{7,6},{8,9},{11,10},{12,13},{15,14},{16,17},{19,... | collective-permute-start | bytes 1769480 | tf_op jit(solution)/shard_map/ppermute | solution.py:418
  20.0 0.6 served.3
  20.6 1.3 %collective-permute-start.6 = (bf16[288,896]{1,0:T(8,128)(2,1)S(1)}, bf16[288,896]{1,0:T(8,128)(2,1)S(1)}, u32[]{:S(2)}, u32[]{:S(2)}) collective-permute-start(bf16[288,896]{1,0:T(8,128)(2,1)S(1)} %served.3), channel_id=1, source_target_pairs={{0,8},{4,12},{1,9},{5,13},{2,10},{6,14},{3,11},{7,15},{16,24},{20,... | collective-permute-start | bytes 1548296 | tf_op jit(solution)/shard_map/ppermute | solution.py:32
  21.9 0.6 opening.3
  22.5 1.3 %collective-permute-start.7 = (bf16[96,3072]{1,0:T(8,128)(2,1)S(1)}, bf16[96,3072]{1,0:T(8,128)(2,1)S(1)}, u32[]{:S(2)}, u32[]{:S(2)}) collective-permute-start(bf16[96,3072]{1,0:T(8,128)(2,1)S(1)} %opening.3), channel_id=1, source_target_pairs={{0,1},{3,2},{4,5},{7,6},{8,9},{11,10},{12,13},{15,14},{16,17},{19,... | collective-permute-start | bytes 1769480 | tf_op jit(solution)/shard_map/ppermute | solution.py:422
  23.8 4.3 %local.3 = (f32[288,768]{1,0:T(8,128)S(1)}, f32[288,128]{1,0:T(8,128)S(1)}) custom-call(s32[6,4]{1,0:T(8,128)S(1)} %pad_add_fusion.facts, bf16[384,768]{1,0:T(8,128)(2,1)} %query.5, bf16[384,768]{1,0:T(8,128)(2,1)} %key.7, bf16[384,768]{1,0:T(8,128)(2,1)} %value.7, bf16[384,768]{1,0:T(8,128)(2,1)S(1)} %collective-permute-done.key_beside, ...), custom_call_target="tpu_custom_call" | custom-call | bytes 14760000 | tf_op jit(solution)/shard_map/local/pallas_call | solution.py:348
  28.1 8.7 %collective-permute-done.6.refs_5_ = bf16[288,896]{1,0:T(8,128)(2,1)S(1)} collective-permute-done((bf16[288,896]{1,0:T(8,128)(2,1)S(1)}, bf16[288,896]{1,0:T(8,128)(2,1)S(1)}, u32[]{:S(2)}, u32[]{:S(2)}) %collective-permute-start.6) | collective-permute-done | bytes 516128 | tf_op jit(solution)/shard_map/ppermute | solution.py:32
  36.8 4.4 %merged_blocks.1 = (bf16[384,768]{1,0:T(8,128)(2,1)S(1)}, bf16[96,3072]{1,0:T(8,128)(2,1)S(1)}, bf16[96,3072]{1,0:T(8,128)(2,1)S(1)}) custom-call(s32[6,4]{1,0:T(8,128)S(1)} %pad_add_fusion.facts, f32[96,768]{1,0:T(8,128)S(1)} %get-tuple-element.49.refs_0_, f32[96,128]{1,0:T(8,128)S(1)} %get-tuple-element.50.refs_1_, ...), custom_call_target="tpu_custom_call" | custom-call | bytes 11070000 | tf_op jit(solution)/shard_map/merged_blocks/pallas_call | solution.py:428
  41.3 0.2 fusion.1
  41.5 1.3 %collective-permute-start.12 = (bf16[96,3072]{1,0:T(8,128)(2,1)S(1)}, bf16[96,3072]{1,0:T(8,128)(2,1)S(1)}, u32[]{:S(2)}, u32[]{:S(2)}) collective-permute-start(bf16[96,3072]{1,0:T(8,128)(2,1)S(1)} %get-tuple-element.95), channel_id=1, source_target_pairs={{3,2},{2,1},{7,6},{6,5},{11,10},{10,9},{15,14},{14,13},{19,18},{18... | collective-permute-start | bytes 1769480 | tf_op jit(solution)/shard_map/ppermute | solution.py:462
  42.8 4.6 %collective-permute-start.11 = (bf16[96,3072]{1,0:T(8,128)(2,1)S(1)}, bf16[96,3072]{1,0:T(8,128)(2,1)S(1)}, u32[]{:S(2)}, u32[]{:S(2)}) collective-permute-start(bf16[96,3072]{1,0:T(8,128)(2,1)S(1)} %get-tuple-element.96), channel_id=1, source_target_pairs={{0,1},{1,2},{4,5},{5,6},{8,9},{9,10},{12,13},{13,14},{16,17},{17,1... | collective-permute-start | bytes 1769480 | tf_op jit(solution)/shard_map/ppermute | solution.py:461
  47.4 3.3 %blocks.3 = (bf16[96,3072]{1,0:T(8,128)(2,1)S(1)}, bf16[96,3072]{1,0:T(8,128)(2,1)S(1)}) custom-call(s32[6,4]{1,0:T(8,128)S(1)} %pad_add_fusion.facts, bf16[384,768]{1,0:T(8,128)(2,1)S(1)} %get-tuple-element.90.attended, bf16[768,6144]{1,0:T(8,128)(2,1)} %weight.8), custom_call_target="tpu_custom_call" | custom-call | bytes 11070000 | tf_op jit(solution)/shard_map/blocks/pallas_call | solution.py:438
  50.7 0.3 fusion.3
  51.0 1.3 %collective-permute-start.10 = (bf16[96,3072]{1,0:T(8,128)(2,1)S(1)}, bf16[96,3072]{1,0:T(8,128)(2,1)S(1)}, u32[]{:S(2)}, u32[]{:S(2)}) collective-permute-start(bf16[96,3072]{1,0:T(8,128)(2,1)S(1)} %get-tuple-element.93), channel_id=1, source_target_pairs={{3,2},{2,1},{7,6},{6,5},{11,10},{10,9},{15,14},{14,13},{19,18},{18... | collective-permute-start | bytes 1769480 | tf_op jit(solution)/shard_map/ppermute | solution.py:462
  52.3 4.6 %collective-permute-start.9 = (bf16[96,3072]{1,0:T(8,128)(2,1)S(1)}, bf16[96,3072]{1,0:T(8,128)(2,1)S(1)}, u32[]{:S(2)}, u32[]{:S(2)}) collective-permute-start(bf16[96,3072]{1,0:T(8,128)(2,1)S(1)} %get-tuple-element.94), channel_id=1, source_target_pairs={{0,1},{1,2},{4,5},{5,6},{8,9},{9,10},{12,13},{13,14},{16,17},{17,1... | collective-permute-start | bytes 1769480 | tf_op jit(solution)/shard_map/ppermute | solution.py:461
  56.8 3.5 %blocks.4 = (bf16[96,3072]{1,0:T(8,128)(2,1)S(1)}, bf16[96,3072]{1,0:T(8,128)(2,1)S(1)}) custom-call(s32[6,4]{1,0:T(8,128)S(1)} %pad_add_fusion.facts, bf16[384,768]{1,0:T(8,128)(2,1)S(1)} %get-tuple-element.90.attended, bf16[768,6144]{1,0:T(8,128)(2,1)} %weight.8), custom_call_target="tpu_custom_call" | custom-call | bytes 11070000 | tf_op jit(solution)/shard_map/blocks/pallas_call | solution.py:438
  60.4 1.7 %collective-permute-done.11 = bf16[96,3072]{1,0:T(8,128)(2,1)S(1)} collective-permute-done((bf16[96,3072]{1,0:T(8,128)(2,1)S(1)}, bf16[96,3072]{1,0:T(8,128)(2,1)S(1)}, u32[]{:S(2)}, u32[]{:S(2)}) %collective-permute-start.11) | collective-permute-done | bytes 589856 | tf_op jit(solution)/shard_map/ppermute | solution.py:461
  62.1 0.1 add_convert_fusion.2
  62.2 1.9 %collective-permute-start.14 = (bf16[96,3072]{1,0:T(8,128)(2,1)S(1)}, bf16[96,3072]{1,0:T(8,128)(2,1)S(1)}, u32[]{:S(2)}, u32[]{:S(2)}) collective-permute-start(bf16[96,3072]{1,0:T(8,128)(2,1)S(1)} %add_convert_fusion.2), channel_id=1, source_target_pairs={{3,2},{2,1},{1,0},{7,6},{6,5},{5,4},{11,10},{10,9},{9,8},{15,14},{... | collective-permute-start | bytes 1769480 | tf_op jit(solution)/shard_map/ppermute | solution.py:462
  64.2 0.2 add_convert_fusion.3
  64.3 3.9 %collective-permute-start.13 = (bf16[96,3072]{1,0:T(8,128)(2,1)S(1)}, bf16[96,3072]{1,0:T(8,128)(2,1)S(1)}, u32[]{:S(2)}, u32[]{:S(2)}) collective-permute-start(bf16[96,3072]{1,0:T(8,128)(2,1)S(1)} %add_convert_fusion.3), channel_id=1, source_target_pairs={{0,1},{1,2},{2,3},{4,5},{5,6},{6,7},{8,9},{9,10},{10,11},{12,13},{... | collective-permute-start | bytes 1769480 | tf_op jit(solution)/shard_map/ppermute | solution.py:461
  68.2 3.5 %blocks.5 = (bf16[96,3072]{1,0:T(8,128)(2,1)S(1)}, bf16[96,3072]{1,0:T(8,128)(2,1)S(1)}) custom-call(s32[6,4]{1,0:T(8,128)S(1)} %pad_add_fusion.facts, bf16[384,768]{1,0:T(8,128)(2,1)S(1)} %get-tuple-element.90.attended, bf16[768,6144]{1,0:T(8,128)(2,1)} %weight.8), custom_call_target="tpu_custom_call" | custom-call | bytes 11070000 | tf_op jit(solution)/shard_map/blocks/pallas_call | solution.py:438
  71.8 0.6 collective-permute-done.10
  72.3 2.4 %collective-permute-done.9 = bf16[96,3072]{1,0:T(8,128)(2,1)S(1)} collective-permute-done((bf16[96,3072]{1,0:T(8,128)(2,1)S(1)}, bf16[96,3072]{1,0:T(8,128)(2,1)S(1)}, u32[]{:S(2)}, u32[]{:S(2)}) %collective-permute-start.9) | collective-permute-done | bytes 589856 | tf_op jit(solution)/shard_map/ppermute | solution.py:461
  74.7 0.2 add_convert_fusion
  74.9 1.9 %collective-permute-start.16 = (bf16[96,3072]{1,0:T(8,128)(2,1)S(1)}, bf16[96,3072]{1,0:T(8,128)(2,1)S(1)}, u32[]{:S(2)}, u32[]{:S(2)}) collective-permute-start(bf16[96,3072]{1,0:T(8,128)(2,1)S(1)} %add_convert_fusion), channel_id=1, source_target_pairs={{3,2},{2,1},{1,0},{7,6},{6,5},{5,4},{11,10},{10,9},{9,8},{15,14},{... | collective-permute-start | bytes 1769480 | tf_op jit(solution)/shard_map/ppermute | solution.py:462
  76.8 0.1 add_convert_fusion.1
  77.0 3.9 %collective-permute-start.15 = (bf16[96,3072]{1,0:T(8,128)(2,1)S(1)}, bf16[96,3072]{1,0:T(8,128)(2,1)S(1)}, u32[]{:S(2)}, u32[]{:S(2)}) collective-permute-start(bf16[96,3072]{1,0:T(8,128)(2,1)S(1)} %add_convert_fusion.1), channel_id=1, source_target_pairs={{0,1},{1,2},{2,3},{4,5},{5,6},{6,7},{8,9},{9,10},{10,11},{12,13},{... | collective-permute-start | bytes 1769480 | tf_op jit(solution)/shard_map/ppermute | solution.py:461
  80.9 5.1 %own.1 = (bf16[96,6144]{1,0:T(8,128)(2,1)S(1)}, f32[1,6144]{1,0:T(1,128)S(1)}) custom-call(s32[6,4]{1,0:T(8,128)S(1)} %pad_add_fusion.facts, bf16[384,768]{1,0:T(8,128)(2,1)S(1)} %get-tuple-element.90.attended, bf16[768,6144]{1,0:T(8,128)(2,1)} %weight.8, f32[64,6144]{1,0:T(8,128)} %gate_table.1), custom_call_target="tpu_custom_call" | custom-call | bytes 18450000 | tf_op jit(solution)/shard_map/own/pallas_call | solution.py:465
  86.0 1.4 %collective-permute-done.13 = bf16[96,3072]{1,0:T(8,128)(2,1)S(1)} collective-permute-done((bf16[96,3072]{1,0:T(8,128)(2,1)S(1)}, bf16[96,3072]{1,0:T(8,128)(2,1)S(1)}, u32[]{:S(2)}, u32[]{:S(2)}) %collective-permute-start.13) | collective-permute-done | bytes 589856 | tf_op jit(solution)/shard_map/ppermute | solution.py:461
  87.4 0.3 multiply_convert_fusion.done
  87.6 7.4 %collective-permute-done.16.down = bf16[96,3072]{1,0:T(8,128)(2,1)S(1)} collective-permute-done((bf16[96,3072]{1,0:T(8,128)(2,1)S(1)}, bf16[96,3072]{1,0:T(8,128)(2,1)S(1)}, u32[]{:S(2)}, u32[]{:S(2)}) %collective-permute-start.16) | collective-permute-done | bytes 589856 | tf_op jit(solution)/shard_map/ppermute | solution.py:462
  95.0 3.3 %collective-permute-done.15.up = bf16[96,3072]{1,0:T(8,128)(2,1)S(1)} collective-permute-done((bf16[96,3072]{1,0:T(8,128)(2,1)S(1)}, bf16[96,3072]{1,0:T(8,128)(2,1)S(1)}, u32[]{:S(2)}, u32[]{:S(2)}) %collective-permute-start.15) | collective-permute-done | bytes 589856 | tf_op jit(solution)/shard_map/ppermute | solution.py:461
  98.3 1.1 %final.1 = bf16[96,6144]{1,0:T(8,128)(2,1)} custom-call(bf16[96,3072]{1,0:T(8,128)(2,1)S(1)} %multiply_convert_fusion.done, bf16[96,6144]{1,0:T(8,128)(2,1)S(1)} %get-tuple-element.91.projected, f32[1,6144]{1,0:T(1,128)S(1)} %get-tuple-element.92.gate, bf16[96,3072]{1,0:T(8,128)(2,1)S(1)} %collective-permute-done.15.up, ...), custom_call_target="tpu_custom_call" | custom-call | bytes 9963000 | tf_op jit(solution)/shard_map/final/pallas_call | solution.py:486
  (15 shorter events, 0.0 us)
Async XLA Ops:
  0.0 4.3 %collective-permute-start = (bf16[384,768]{1,0:T(8,128)(2,1)}, bf16[384,768]{1,0:T(8,128)(2,1)S(1)}, u32[]{:S(2)}, u32[]{:S(2)}) collective-permute-start(bf16[384,768]{1,0:T(8,128)(2,1)} %key.7), channel_id=1, source_target_pairs={{0,4},{4,0},{8,12},{12,8},{1,5},{5,1},{9,13},{13,9},{2,6},{6,2},{1... | collective-permute-start | bytes 1769480 | tf_op jit(solution)/shard_map/ppermute | solution.py:340
  0.0 4.4 %collective-permute-start.1 = (bf16[384,768]{1,0:T(8,128)(2,1)}, bf16[384,768]{1,0:T(8,128)(2,1)S(1)}, u32[]{:S(2)}, u32[]{:S(2)}) collective-permute-start(bf16[384,768]{1,0:T(8,128)(2,1)} %value.7), channel_id=1, source_target_pairs={{0,4},{4,0},{8,12},{12,8},{1,5},{5,1},{9,13},{13,9},{2,6},{6,2},{1... | collective-permute-start | bytes 1769480 | tf_op jit(solution)/shard_map/ppermute | solution.py:341
  2.2 6.9 %collective-permute-start.2 = (bf16[96,768]{1,0:T(8,128)(2,1)S(1)}, bf16[96,768]{1,0:T(8,128)(2,1)S(1)}, u32[]{:S(2)}, u32[]{:S(2)}) collective-permute-start(bf16[96,768]{1,0:T(8,128)(2,1)S(1)} %get-tuple-element.51), channel_id=1, source_target_pairs={{8,0},{12,4},{9,1},{13,5},{10,2},{14,6},{11,3},{15,7},{24,16},{28,... | collective-permute-start | bytes 442376 | tf_op jit(solution)/shard_map/ppermute | solution.py:32
  4.3 4.8 %copy-start = (bf16[384,768]{1,0:T(8,128)(2,1)S(1)}, bf16[384,768]{1,0:T(8,128)(2,1)}, u32[]{:S(2)}) copy-start(bf16[384,768]{1,0:T(8,128)(2,1)} %key.7) | copy-start | bytes 1769476
  4.3 4.8 %copy-start.1 = (bf16[384,768]{1,0:T(8,128)(2,1)S(1)}, bf16[384,768]{1,0:T(8,128)(2,1)}, u32[]{:S(2)}) copy-start(bf16[384,768]{1,0:T(8,128)(2,1)} %value.7) | copy-start | bytes 1769476
  7.8 12.2 %collective-permute-start.4 = (bf16[192,768]{1,0:T(8,128)(2,1)S(1)}, bf16[192,768]{1,0:T(8,128)(2,1)S(1)}, u32[]{:S(2)}, u32[]{:S(2)}) collective-permute-start(bf16[192,768]{1,0:T(8,128)(2,1)S(1)} %get-tuple-element.55), channel_id=1, source_target_pairs={{8,0},{12,4},{9,1},{13,5},{10,2},{14,6},{11,3},{15,7},{24,16},{28,... | collective-permute-start | bytes 884744 | tf_op jit(solution)/shard_map/ppermute | solution.py:32
  9.7 8.3 %collective-permute-start.3 = (bf16[96,896]{1,0:T(8,128)(2,1)S(1)}, bf16[96,896]{1,0:T(8,128)(2,1)S(1)}, u32[]{:S(2)}, u32[]{:S(2)}) collective-permute-start(bf16[96,896]{1,0:T(8,128)(2,1)S(1)} %served.2), channel_id=1, source_target_pairs={{0,8},{4,12},{1,9},{5,13},{2,10},{6,14},{3,11},{7,15},{16,24},{20,... | collective-permute-start | bytes 516104 | tf_op jit(solution)/shard_map/ppermute | solution.py:32
  11.0 8.9 %collective-permute-start.5 = (bf16[96,768]{1,0:T(8,128)(2,1)S(1)}, bf16[96,768]{1,0:T(8,128)(2,1)S(1)}, u32[]{:S(2)}, u32[]{:S(2)}) collective-permute-start(bf16[96,768]{1,0:T(8,128)(2,1)S(1)} %get-tuple-element.56), channel_id=1, source_target_pairs={{8,0},{12,4},{9,1},{13,5},{10,2},{14,6},{11,3},{15,7},{24,16},{28,... | collective-permute-start | bytes 442376 | tf_op jit(solution)/shard_map/ppermute | solution.py:32
  18.6 22.6 %collective-permute-start.8 = (bf16[96,3072]{1,0:T(8,128)(2,1)S(1)}, bf16[96,3072]{1,0:T(8,128)(2,1)S(1)}, u32[]{:S(2)}, u32[]{:S(2)}) collective-permute-start(bf16[96,3072]{1,0:T(8,128)(2,1)S(1)} %opening.2), channel_id=1, source_target_pairs={{0,1},{3,2},{4,5},{7,6},{8,9},{11,10},{12,13},{15,14},{16,17},{19,... | collective-permute-start | bytes 1769480 | tf_op jit(solution)/shard_map/ppermute | solution.py:418
  20.6 16.3 %collective-permute-start.6 = (bf16[288,896]{1,0:T(8,128)(2,1)S(1)}, bf16[288,896]{1,0:T(8,128)(2,1)S(1)}, u32[]{:S(2)}, u32[]{:S(2)}) collective-permute-start(bf16[288,896]{1,0:T(8,128)(2,1)S(1)} %served.3), channel_id=1, source_target_pairs={{0,8},{4,12},{1,9},{5,13},{2,10},{6,14},{3,11},{7,15},{16,24},{20,... | collective-permute-start | bytes 1548296 | tf_op jit(solution)/shard_map/ppermute | solution.py:32
  22.5 28.2 %collective-permute-start.7 = (bf16[96,3072]{1,0:T(8,128)(2,1)S(1)}, bf16[96,3072]{1,0:T(8,128)(2,1)S(1)}, u32[]{:S(2)}, u32[]{:S(2)}) collective-permute-start(bf16[96,3072]{1,0:T(8,128)(2,1)S(1)} %opening.3), channel_id=1, source_target_pairs={{0,1},{3,2},{4,5},{7,6},{8,9},{11,10},{12,13},{15,14},{16,17},{19,... | collective-permute-start | bytes 1769480 | tf_op jit(solution)/shard_map/ppermute | solution.py:422
  41.5 18.8 %collective-permute-start.12 = (bf16[96,3072]{1,0:T(8,128)(2,1)S(1)}, bf16[96,3072]{1,0:T(8,128)(2,1)S(1)}, u32[]{:S(2)}, u32[]{:S(2)}) collective-permute-start(bf16[96,3072]{1,0:T(8,128)(2,1)S(1)} %get-tuple-element.95), channel_id=1, source_target_pairs={{3,2},{2,1},{7,6},{6,5},{11,10},{10,9},{15,14},{14,13},{19,18},{18... | collective-permute-start | bytes 1769480 | tf_op jit(solution)/shard_map/ppermute | solution.py:462
  42.8 19.3 %collective-permute-start.11 = (bf16[96,3072]{1,0:T(8,128)(2,1)S(1)}, bf16[96,3072]{1,0:T(8,128)(2,1)S(1)}, u32[]{:S(2)}, u32[]{:S(2)}) collective-permute-start(bf16[96,3072]{1,0:T(8,128)(2,1)S(1)} %get-tuple-element.96), channel_id=1, source_target_pairs={{0,1},{1,2},{4,5},{5,6},{8,9},{9,10},{12,13},{13,14},{16,17},{17,1... | collective-permute-start | bytes 1769480 | tf_op jit(solution)/shard_map/ppermute | solution.py:461
  51.0 21.3 %collective-permute-start.10 = (bf16[96,3072]{1,0:T(8,128)(2,1)S(1)}, bf16[96,3072]{1,0:T(8,128)(2,1)S(1)}, u32[]{:S(2)}, u32[]{:S(2)}) collective-permute-start(bf16[96,3072]{1,0:T(8,128)(2,1)S(1)} %get-tuple-element.93), channel_id=1, source_target_pairs={{3,2},{2,1},{7,6},{6,5},{11,10},{10,9},{15,14},{14,13},{19,18},{18... | collective-permute-start | bytes 1769480 | tf_op jit(solution)/shard_map/ppermute | solution.py:462
  52.3 22.4 %collective-permute-start.9 = (bf16[96,3072]{1,0:T(8,128)(2,1)S(1)}, bf16[96,3072]{1,0:T(8,128)(2,1)S(1)}, u32[]{:S(2)}, u32[]{:S(2)}) collective-permute-start(bf16[96,3072]{1,0:T(8,128)(2,1)S(1)} %get-tuple-element.94), channel_id=1, source_target_pairs={{0,1},{1,2},{4,5},{5,6},{8,9},{9,10},{12,13},{13,14},{16,17},{17,1... | collective-permute-start | bytes 1769480 | tf_op jit(solution)/shard_map/ppermute | solution.py:461
  62.2 23.7 %collective-permute-start.14 = (bf16[96,3072]{1,0:T(8,128)(2,1)S(1)}, bf16[96,3072]{1,0:T(8,128)(2,1)S(1)}, u32[]{:S(2)}, u32[]{:S(2)}) collective-permute-start(bf16[96,3072]{1,0:T(8,128)(2,1)S(1)} %add_convert_fusion.2), channel_id=1, source_target_pairs={{3,2},{2,1},{1,0},{7,6},{6,5},{5,4},{11,10},{10,9},{9,8},{15,14},{... | collective-permute-start | bytes 1769480 | tf_op jit(solution)/shard_map/ppermute | solution.py:462
  64.3 23.0 %collective-permute-start.13 = (bf16[96,3072]{1,0:T(8,128)(2,1)S(1)}, bf16[96,3072]{1,0:T(8,128)(2,1)S(1)}, u32[]{:S(2)}, u32[]{:S(2)}) collective-permute-start(bf16[96,3072]{1,0:T(8,128)(2,1)S(1)} %add_convert_fusion.3), channel_id=1, source_target_pairs={{0,1},{1,2},{2,3},{4,5},{5,6},{6,7},{8,9},{9,10},{10,11},{12,13},{... | collective-permute-start | bytes 1769480 | tf_op jit(solution)/shard_map/ppermute | solution.py:461
  74.9 20.2 %collective-permute-start.16 = (bf16[96,3072]{1,0:T(8,128)(2,1)S(1)}, bf16[96,3072]{1,0:T(8,128)(2,1)S(1)}, u32[]{:S(2)}, u32[]{:S(2)}) collective-permute-start(bf16[96,3072]{1,0:T(8,128)(2,1)S(1)} %add_convert_fusion), channel_id=1, source_target_pairs={{3,2},{2,1},{1,0},{7,6},{6,5},{5,4},{11,10},{10,9},{9,8},{15,14},{... | collective-permute-start | bytes 1769480 | tf_op jit(solution)/shard_map/ppermute | solution.py:462
  77.0 21.4 %collective-permute-start.15 = (bf16[96,3072]{1,0:T(8,128)(2,1)S(1)}, bf16[96,3072]{1,0:T(8,128)(2,1)S(1)}, u32[]{:S(2)}, u32[]{:S(2)}) collective-permute-start(bf16[96,3072]{1,0:T(8,128)(2,1)S(1)} %add_convert_fusion.1), channel_id=1, source_target_pairs={{0,1},{1,2},{2,3},{4,5},{5,6},{6,7},{8,9},{9,10},{10,11},{12,13},{... | collective-permute-start | bytes 1769480 | tf_op jit(solution)/shard_map/ppermute | solution.py:461

commit v16 on v15

--- a/solution.py
+++ b/solution.py
@@ -74,16 +74,12 @@
 
 
 class Facts:
-    def __init__(self, ref, spans):
-        self.ref, self.spans = ref, spans
-        self.span, self.rank = ref[spans, 0], ref[spans, 1]
+    def __init__(self, place, visible):
+        self.span, self.rank, self.visible = place[0], place[1], visible
         self.beside = self.span + 1 - 2 * lax.rem(self.span, 2)
 
     def sees(self, asker, span):
-        return self.ref[asker, span] > 0
-
-    def level(self):
-        return self.ref[self.spans + 1, self.span]
+        return self.visible[asker, span] > 0
 
 
 def copied(source, target, semaphore):
@@ -115,8 +111,8 @@
             copy.wait()
 
 
-def local_kernel(spans, ranks, part, facts, query, key, value, key_beside, value_beside, result, sums, *scratch):
-    here = Facts(facts, spans)
+def local_kernel(ranks, part, place, visible, query, key, value, key_beside, value_beside, result, sums, *scratch):
+    here = Facts(place, visible)
     query_, key_, value_, key_beside_, value_beside_, semaphores = scratch
     start, size = parts_of(here.rank, ranks, query.shape[0])[part]
     copies = [
@@ -136,8 +132,8 @@
     sums[...] = attend(query_, [key_, key_beside_], [value_, value_beside_], flags, write)
 
 
-def served_kernel(distance, spans, facts, key, value, key_beside, value_beside, *refs):
-    here = Facts(facts, spans)
+def served_kernel(distance, spans, place, visible, key, value, key_beside, value_beside, *refs):
+    here = Facts(place, visible)
 
     @pl.when(here.span + distance < spans)
     def _():
@@ -191,18 +187,19 @@
     ]
 
 
-def fetch_kernel(weight, tiles, semaphores):
-    for copy in streamed(weight, 0, tiles, semaphores):
-        copy.wait()
-
-
-def opening_kernel(ranks, distances, spans, first, facts, *refs):
+def fetch_kernel(ranks, place, weight, tiles, semaphores):
+    @pl.when(jnp.logical_or(place[1] == 0, place[1] == ranks - 1))
+    def _():
+        for copy in streamed(weight, 0, tiles, semaphores):
+            copy.wait()
+
+
+def opening_kernel(ranks, distances, first, place, *refs):
     own, own_sum, *served = refs[:2 + len(distances)]
     weight, result, *scratch = refs[2 + len(distances):]
     rows = scratch[-1]
-    here = Facts(facts, spans)
-
-    @pl.when(jnp.logical_or(here.rank == 0, here.rank == ranks - 1))
+
+    @pl.when(jnp.logical_or(place[1] == 0, place[1] == ranks - 1))
     def _():
         tiles, copies = weight, [None] * weight.shape[0]
         if first:
@@ -212,7 +209,7 @@
         def write(columns, part):
             rows[:, columns] = part
 
-        merge(here.span, distances, own, own_sum, served, write)
+        merge(place[0], distances, own, own_sum, served, write)
         tile = tiles.shape[2]
         for index, copy in enumerate(copies):
             if copy is not None:
@@ -221,8 +218,7 @@
             result[:, index * tile:(index + 1) * tile] = product.astype(jnp.bfloat16)
 
 
-def project_blocks(ranks, first, facts, step, attended, weight, up, down, tiles, semaphores):
-    rank = facts.rank
+def project_blocks(ranks, first, rank, step, attended, weight, up, down, tiles, semaphores):
     last = ranks - 1
     tile = tiles.shape[2]
     block = up.shape[0]
@@ -252,37 +248,35 @@
             down[:, there] = one
 
 
-def merged_blocks_kernel(spans, ranks, distances, facts, *refs):
+def merged_blocks_kernel(ranks, distances, place, *refs):
     each = 2 + len(distances)
     parts, (weight, attended, *results) = (refs[:each], refs[each:2 * each]), refs[2 * each:]
-    here = Facts(facts, spans)
-    work = project_blocks(ranks, 0, here, 1, attended, weight, *results)
+    work = project_blocks(ranks, 0, place[1], 1, attended, weight, *results)
     next(work)
-    for (start, size), (own, own_sum, *served) in zip(parts_of(here.rank, ranks, attended.shape[0]), parts):
+    for (start, size), (own, own_sum, *served) in zip(parts_of(place[1], ranks, attended.shape[0]), parts):
         there = pl.ds(start, size)
 
         def write(columns, part):
             attended[there, columns] = part
 
-        merge(here.span, distances, own, own_sum, served, write)
+        merge(place[0], distances, own, own_sum, served, write)
     for _ in work:
         pass
 
 
-def blocks_kernel(spans, ranks, first, step, facts, attended, weight, *results):
-    for _ in project_blocks(ranks, first, Facts(facts, spans), step, attended, weight, *results):
+def blocks_kernel(ranks, first, step, place, attended, weight, *results):
+    for _ in project_blocks(ranks, first, place[1], step, attended, weight, *results):
         pass
 
 
-def own_kernel(spans, facts, attended, weight, gate_table, result, gate, tiles, gates, semaphores):
-    here = Facts(facts, spans)
+def own_kernel(place, levels, attended, weight, gate_table, result, gate, tiles, gates, semaphores):
     block = result.shape[0]
     count, _, tile = tiles.shape
-    level = here.level()
+    level = levels[place[0]]
     above = pl.multiple_of(level // 8 * 8, 8)
     gate_copy = copied(gate_table.at[pl.ds(above, 8)], gates, semaphores.at[count])
     copies = streamed(weight, 0, tiles, semaphores)
-    start = pl.multiple_of(here.rank * block, block)
+    start = pl.multiple_of(place[1] * block, block)
     for index, copy in enumerate(copies):
         copy.wait()
         product = jnp.dot(attended[pl.ds(start, block), :], tiles[index], preferred_element_type=jnp.float32)
@@ -319,10 +313,7 @@
     rank = lax.axis_index("tensor")
     block = rows // ranks
     bf16, f32 = jnp.bfloat16, jnp.float32
-    numbers = jnp.arange(spans, dtype=jnp.int32)
-    place = jnp.where(numbers == 0, span, jnp.where(numbers == 1, rank, 0)).astype(jnp.int32)
-    facts = jnp.concatenate([visible, place[None, :], levels[None, :]], axis=0)
-
+    place = jnp.stack([span, rank]).astype(jnp.int32)
     third = (rows - block) // 48 * 16
     query_early, *query_late = pl.pallas_call(
         functools.partial(split_kernel, ranks),
@@ -333,7 +324,7 @@
         compiler_params=PARAMS,
         cost_estimate=taking(1.7),
         name="split",
-    )(jnp.stack([span, rank]).astype(jnp.int32), in_hbm(queries))
+    )(place, in_hbm(queries))
     distances = list(range(2, spans, 2))
     asked_early = [shifted(query_early, "span", -distance) for distance in distances]
     swap = [(i, i + 1 - 2 * (i % 2)) for i in range(spans)]
@@ -343,11 +334,11 @@
     def after(value, *others):
         return lax.optimization_barrier((value, others))[0]
 
-    def local(part, facts):
+    def local(part, place):
         size = (block, rows - block)[part]
         return pl.pallas_call(
-            functools.partial(local_kernel, spans, ranks, part),
-            in_specs=[SMEM, HBM, HBM, HBM, ANY, ANY],
+            functools.partial(local_kernel, ranks, part),
+            in_specs=[SMEM, SMEM, HBM, HBM, HBM, ANY, ANY],
             out_specs=[VMEM] * 2,
             out_shape=[jax.ShapeDtypeStruct((size, width), f32), jax.ShapeDtypeStruct((size, LANES), f32)],
             scratch_shapes=[pltpu.VMEM((size, width), bf16)] + [pltpu.VMEM((rows, width), bf16)] * 4
@@ -355,21 +346,21 @@
             compiler_params=PARAMS,
             cost_estimate=taking(4.0),
             name="local",
-        )(facts, in_hbm(queries), in_hbm(keys), in_hbm(values), key_beside, value_beside)
+        )(place, visible, in_hbm(queries), in_hbm(keys), in_hbm(values), key_beside, value_beside)
 
     def served(asked, distance):
         return pl.pallas_call(
             functools.partial(served_kernel, distance, spans),
-            in_specs=[SMEM] + [VMEM] * (4 + len(asked)),
+            in_specs=[SMEM, SMEM] + [VMEM] * (4 + len(asked)),
             out_specs=VMEM,
             out_shape=jax.ShapeDtypeStruct((sum(part.shape[0] for part in asked), width + LANES), bf16),
             scratch_shapes=[pltpu.VMEM((sum(part.shape[0] for part in asked), width), bf16)],
             compiler_params=PARAMS,
             cost_estimate=taking(3.3),
             name="served",
-        )(facts, keys, values, key_beside, value_beside, *asked)
-
-    early = list(local(0, facts))
+        )(place, visible, keys, values, key_beside, value_beside, *asked)
+
+    early = list(local(0, place))
     query_late = after(query_late, early)
     asked_early = after(asked_early, early)
     asked_late = [[shifted(query, "span", -distance) for query in query_late] for distance in distances]
@@ -390,20 +381,20 @@
         cost_estimate=taking(3.0),
     )
     fetched = pl.pallas_call(
-        fetch_kernel,
-        in_specs=[HBM],
+        functools.partial(fetch_kernel, ranks),
+        in_specs=[SMEM, HBM],
         out_specs=VMEM,
         out_shape=jax.ShapeDtypeStruct(tile_shape, bf16),
         scratch_shapes=[pltpu.SemaphoreType.DMA((tiles,))],
         compiler_params=PARAMS,
         cost_estimate=taking(2.4),
         name="fetch",
-    )(in_hbm(after(out_weight, out_early)))
-
-    def opening(chunk, facts):
+    )(after(place, out_early), weight)
+
+    def opening(chunk, place):
         scratch = streaming["scratch_shapes"] if chunk else []
         return pl.pallas_call(
-            functools.partial(opening_kernel, ranks, distances, spans, chunk * columns),
+            functools.partial(opening_kernel, ranks, distances, chunk * columns),
             in_specs=[SMEM] + [VMEM] * (2 + len(distances)) + [HBM if chunk else VMEM],
             out_specs=VMEM,
             out_shape=jax.ShapeDtypeStruct((block, columns), bf16),
@@ -411,38 +402,38 @@
             compiler_params=PARAMS,
             cost_estimate=taking(3.4),
             name="opening",
-        )(facts, *early, weight if chunk else fetched)
+        )(place, *early, weight if chunk else fetched)
 
     ends = [(0, 1), (last, last - 1)]
-    sent = opening(0, facts)
+    sent = opening(0, place)
     arrived = [[lax.ppermute(sent, "tensor", ends)]]
     out_late = [served(q, d) for q, d in zip(after(asked_late, sent), distances)]
     for chunk in range(1, chunks):
-        sent = opening(chunk, after(facts, out_late))
+        sent = opening(chunk, after(place, out_late))
         arrived.append([lax.ppermute(sent, "tensor", ends)])
-    late = list(local(1, after(facts, sent)))
+    late = list(local(1, after(place, sent)))
     late += [shifted(o, "span", d) for o, d in zip(out_late, distances)]
 
     attended_shape = jax.ShapeDtypeStruct((rows, width), bf16)
     block_shapes = [jax.ShapeDtypeStruct((block, columns), bf16)] * 2
     attended, *merged = pl.pallas_call(
-        functools.partial(merged_blocks_kernel, spans, ranks, distances),
+        functools.partial(merged_blocks_kernel, ranks, distances),
         in_specs=[SMEM] + [VMEM] * (4 + 2 * len(distances)) + [HBM],
         out_specs=[VMEM] * 3,
         out_shape=[attended_shape] + block_shapes,
         name="merged_blocks",
         **streaming,
-    )(facts, *early, *late, weight)
+    )(place, *early, *late, weight)
 
     def blocks_of(step, chunk, attended):
         return pl.pallas_call(
-            functools.partial(blocks_kernel, spans, ranks, chunk * columns, step),
+            functools.partial(blocks_kernel, ranks, chunk * columns, step),
             in_specs=[SMEM, VMEM, HBM],
             out_specs=[VMEM] * 2,
             out_shape=block_shapes,
             name="blocks",
             **streaming,
-        )(facts, attended, weight)
+        )(place, attended, weight)
 
     before = attended
     for step in range(1, last):
@@ -463,8 +454,8 @@
             ]
     everything = chunks * tiles
     projected, gate = pl.pallas_call(
-        functools.partial(own_kernel, spans),
-        in_specs=[SMEM, VMEM, HBM, HBM],
+        own_kernel,
+        in_specs=[SMEM, SMEM, VMEM, HBM, HBM],
         out_specs=[VMEM, VMEM],
         out_shape=[jax.ShapeDtypeStruct((block, model), bf16), jax.ShapeDtypeStruct((1, model), f32)],
         scratch_shapes=[
@@ -475,7 +466,7 @@
         compiler_params=PARAMS,
         cost_estimate=taking(5.0),
         name="own",
-    )(facts, after(attended, before), weight, in_hbm(gate_table))
+    )(place, levels, after(attended, before), weight, in_hbm(gate_table))
 
     finished = []
     for chunk in range(chunks - 1):

time: 101 us -> 101 us (level)
  Pallas kernels: 35.1 us -> 32.8 us
  starting transfers between devices: 36.3 us -> 37.7 us
    pallas_call x10, Pallas kernels: 31.1 us -> 28.9 us  [the longest x3 10.2 us: blocks_of(): pl.pallas_call(functools.partial(blocks_kernel, ranks, chunk * columns, s...]
    ppermute x5, waiting for transfers between devices: 8.71 us -> 10.5 us  [shifted(): lax.ppermute(block, axis, [(i, i + distance) for i in range(count) if 0 <...]
  transfers between devices with their start and end apart: 17 -> 17, of which waited for: 7 -> 8; matrix products, arithmetic and copies ran while one was open for 2% -> 1% of each run, Pallas kernels for 34% -> 32%
where the time goes in v16:
time: 101 us; the launch traced here: 99.7 us
  starting transfers between devices  37.7 us (37%)
  Pallas kernels  32.8 us (32%)
  waiting for transfers between devices  26.5 us (26%)
  other arithmetic  1.42 us (1%)
    ppermute x4, starting transfers between devices, body(): lax.ppermute(up, 'tensor', [(i, i + 1) for i in range(step + 1)])  17.9 us
    ppermute x5, waiting for transfers between devices, shifted(): lax.ppermute(block, axis, [(i, i + distance) for i in range(count) if 0 <...  10.5 us
    ppermute x5, starting transfers between devices, shifted(): lax.ppermute(block, axis, [(i, i + distance) for i in range(count) if 0 <...  10.3 us
    pallas_call x3, Pallas kernels, blocks_of(): pl.pallas_call(functools.partial(blocks_kernel, ranks, chunk * columns, s...  10.2 us
    ppermute x4, waiting for transfers between devices, body(): lax.ppermute(up, 'tensor', [(i, i + 1) for i in range(step + 1)])  8.26 us
    ppermute x4, waiting for transfers between devices, body(): lax.ppermute(down, 'tensor', [(last - i, last - i - 1) for i in range(ste...  7.69 us
    pallas_call x2, Pallas kernels, local(): pl.pallas_call(functools.partial(local_kernel, ranks, part), in_specs=[SM...  7.65 us
    ppermute x4, starting transfers between devices, body(): lax.ppermute(down, 'tensor', [(last - i, last - i - 1) for i in range(ste...  6.43 us
  transfers between devices with their start and end apart: 17, of which 8 were waited for; matrix products, arithmetic and copies ran while one was open for 1% of the time, Pallas kernels for 32%

profile of v16, /device:TPU:14, one launch (start us, length us, event | category | flops | bytes accessed | tf_op | source)
XLA Modules:
  0.0 99.7 jit_solution(611644614288919331)
XLA Ops:
  0.0 0.5 collective-permute-start.1
  0.5 0.1 pad_add_fusion.place
  0.6 1.6 %split.1 = (bf16[96,768]{1,0:T(8,128)(2,1)S(1)}, bf16[192,768]{1,0:T(8,128)(2,1)S(1)}, bf16[96,768]{1,0:T(8,128)(2,1)S(1)}) custom-call(s32[2]{0:T(128)S(1)} %pad_add_fusion.place, bf16[384,768]{1,0:T(8,128)(2,1)} %query.5), custom_call_target="tpu_custom_call" | custom-call | bytes 6273000 | tf_op jit(solution)/shard_map/split/pallas_call | solution.py:318
  2.3 1.5 %collective-permute-start.2 = (bf16[96,768]{1,0:T(8,128)(2,1)S(1)}, bf16[96,768]{1,0:T(8,128)(2,1)S(1)}, u32[]{:S(2)}, u32[]{:S(2)}) collective-permute-start(bf16[96,768]{1,0:T(8,128)(2,1)S(1)} %get-tuple-element.51), channel_id=1, source_target_pairs={{8,0},{12,4},{9,1},{13,5},{10,2},{14,6},{11,3},{15,7},{24,16},{28,... | collective-permute-start | bytes 442376 | tf_op jit(solution)/shard_map/ppermute | solution.py:32
  3.8 0.7 copy-done.2
  4.5 3.4 %local.2 = (f32[96,768]{1,0:T(8,128)S(1)}, f32[96,128]{1,0:T(8,128)S(1)}) custom-call(s32[2]{0:T(128)S(1)} %pad_add_fusion.place, s32[4,4]{1,0:T(4,128)S(1)} %copy-done.2, bf16[384,768]{1,0:T(8,128)(2,1)} %query.5, bf16[384,768]{1,0:T(8,128)(2,1)} %key.7, bf16[384,768]{1,0:T(8,128)(2,1)} %value.7, bf16[384,768]{1,0:T(8,128)(2,1)S(1)} %collective-permute-done.key_beside, ...), custom_call_target="tpu_custom_call" | custom-call | bytes 14760000 | tf_op jit(solution)/shard_map/local/pallas_call | solution.py:339
  7.8 1.7 %collective-permute-start.4 = (bf16[192,768]{1,0:T(8,128)(2,1)S(1)}, bf16[192,768]{1,0:T(8,128)(2,1)S(1)}, u32[]{:S(2)}, u32[]{:S(2)}) collective-permute-start(bf16[192,768]{1,0:T(8,128)(2,1)S(1)} %get-tuple-element.55), channel_id=1, source_target_pairs={{8,0},{12,4},{9,1},{13,5},{10,2},{14,6},{11,3},{15,7},{24,16},{28,... | collective-permute-start | bytes 884744 | tf_op jit(solution)/shard_map/ppermute | solution.py:32
  9.6 0.6 served.2
  10.2 1.3 %collective-permute-start.3 = (bf16[96,896]{1,0:T(8,128)(2,1)S(1)}, bf16[96,896]{1,0:T(8,128)(2,1)S(1)}, u32[]{:S(2)}, u32[]{:S(2)}) collective-permute-start(bf16[96,896]{1,0:T(8,128)(2,1)S(1)} %served.2), channel_id=1, source_target_pairs={{0,8},{4,12},{1,9},{5,13},{2,10},{6,14},{3,11},{7,15},{16,24},{20,... | collective-permute-start | bytes 516104 | tf_op jit(solution)/shard_map/ppermute | solution.py:32
  11.5 4.6 %collective-permute-start.5 = (bf16[96,768]{1,0:T(8,128)(2,1)S(1)}, bf16[96,768]{1,0:T(8,128)(2,1)S(1)}, u32[]{:S(2)}, u32[]{:S(2)}) collective-permute-start(bf16[96,768]{1,0:T(8,128)(2,1)S(1)} %get-tuple-element.56), channel_id=1, source_target_pairs={{8,0},{12,4},{9,1},{13,5},{10,2},{14,6},{11,3},{15,7},{24,16},{28,... | collective-permute-start | bytes 442376 | tf_op jit(solution)/shard_map/ppermute | solution.py:32
  16.0 0.6 fetch.1.refs_3_
  16.6 1.6 %collective-permute-done.3.refs_2_ = bf16[96,896]{1,0:T(8,128)(2,1)S(1)} collective-permute-done((bf16[96,896]{1,0:T(8,128)(2,1)S(1)}, bf16[96,896]{1,0:T(8,128)(2,1)S(1)}, u32[]{:S(2)}, u32[]{:S(2)}) %collective-permute-start.3) | collective-permute-done | bytes 172064 | tf_op jit(solution)/shard_map/ppermute | solution.py:32
  18.2 0.5 opening.2
  18.8 1.3 %collective-permute-start.8 = (bf16[96,3072]{1,0:T(8,128)(2,1)S(1)}, bf16[96,3072]{1,0:T(8,128)(2,1)S(1)}, u32[]{:S(2)}, u32[]{:S(2)}) collective-permute-start(bf16[96,3072]{1,0:T(8,128)(2,1)S(1)} %opening.2), channel_id=1, source_target_pairs={{0,1},{3,2},{4,5},{7,6},{8,9},{11,10},{12,13},{15,14},{16,17},{19,... | collective-permute-start | bytes 1769480 | tf_op jit(solution)/shard_map/ppermute | solution.py:409
  20.1 0.6 served.3
  20.7 1.3 %collective-permute-start.6 = (bf16[288,896]{1,0:T(8,128)(2,1)S(1)}, bf16[288,896]{1,0:T(8,128)(2,1)S(1)}, u32[]{:S(2)}, u32[]{:S(2)}) collective-permute-start(bf16[288,896]{1,0:T(8,128)(2,1)S(1)} %served.3), channel_id=1, source_target_pairs={{0,8},{4,12},{1,9},{5,13},{2,10},{6,14},{3,11},{7,15},{16,24},{20,... | collective-permute-start | bytes 1548296 | tf_op jit(solution)/shard_map/ppermute | solution.py:32
  22.0 0.6 opening.3
  22.6 1.3 %collective-permute-start.7 = (bf16[96,3072]{1,0:T(8,128)(2,1)S(1)}, bf16[96,3072]{1,0:T(8,128)(2,1)S(1)}, u32[]{:S(2)}, u32[]{:S(2)}) collective-permute-start(bf16[96,3072]{1,0:T(8,128)(2,1)S(1)} %opening.3), channel_id=1, source_target_pairs={{0,1},{3,2},{4,5},{7,6},{8,9},{11,10},{12,13},{15,14},{16,17},{19,... | collective-permute-start | bytes 1769480 | tf_op jit(solution)/shard_map/ppermute | solution.py:413
  23.9 4.3 %local.3 = (f32[288,768]{1,0:T(8,128)S(1)}, f32[288,128]{1,0:T(8,128)S(1)}) custom-call(s32[2]{0:T(128)S(1)} %pad_add_fusion.place, s32[4,4]{1,0:T(4,128)S(1)} %copy-done.2, bf16[384,768]{1,0:T(8,128)(2,1)} %query.5, bf16[384,768]{1,0:T(8,128)(2,1)} %key.7, bf16[384,768]{1,0:T(8,128)(2,1)} %value.7, bf16[384,768]{1,0:T(8,128)(2,1)S(1)} %collective-permute-done.key_beside, ...), custom_call_target="tpu_custom_call" | custom-call | bytes 14760000 | tf_op jit(solution)/shard_map/local/pallas_call | solution.py:339
  28.1 9.0 %collective-permute-done.6.refs_5_ = bf16[288,896]{1,0:T(8,128)(2,1)S(1)} collective-permute-done((bf16[288,896]{1,0:T(8,128)(2,1)S(1)}, bf16[288,896]{1,0:T(8,128)(2,1)S(1)}, u32[]{:S(2)}, u32[]{:S(2)}) %collective-permute-start.6) | collective-permute-done | bytes 516128 | tf_op jit(solution)/shard_map/ppermute | solution.py:32
  37.1 4.3 %merged_blocks.1 = (bf16[384,768]{1,0:T(8,128)(2,1)S(1)}, bf16[96,3072]{1,0:T(8,128)(2,1)S(1)}, bf16[96,3072]{1,0:T(8,128)(2,1)S(1)}) custom-call(s32[2]{0:T(128)S(1)} %pad_add_fusion.place, f32[96,768]{1,0:T(8,128)S(1)} %get-tuple-element.49.refs_0_, f32[96,128]{1,0:T(8,128)S(1)} %get-tuple-element.50.refs_1_, ...), custom_call_target="tpu_custom_call" | custom-call | bytes 11070000 | tf_op jit(solution)/shard_map/merged_blocks/pallas_call | solution.py:419
  41.5 0.2 fusion.1
  41.7 1.3 %collective-permute-start.12 = (bf16[96,3072]{1,0:T(8,128)(2,1)S(1)}, bf16[96,3072]{1,0:T(8,128)(2,1)S(1)}, u32[]{:S(2)}, u32[]{:S(2)}) collective-permute-start(bf16[96,3072]{1,0:T(8,128)(2,1)S(1)} %get-tuple-element.95), channel_id=1, source_target_pairs={{3,2},{2,1},{7,6},{6,5},{11,10},{10,9},{15,14},{14,13},{19,18},{18... | collective-permute-start | bytes 1769480 | tf_op jit(solution)/shard_map/ppermute | solution.py:453
  43.0 4.6 %collective-permute-start.11 = (bf16[96,3072]{1,0:T(8,128)(2,1)S(1)}, bf16[96,3072]{1,0:T(8,128)(2,1)S(1)}, u32[]{:S(2)}, u32[]{:S(2)}) collective-permute-start(bf16[96,3072]{1,0:T(8,128)(2,1)S(1)} %get-tuple-element.96), channel_id=1, source_target_pairs={{0,1},{1,2},{4,5},{5,6},{8,9},{9,10},{12,13},{13,14},{16,17},{17,1... | collective-permute-start | bytes 1769480 | tf_op jit(solution)/shard_map/ppermute | solution.py:452
  47.6 3.3 %blocks.3 = (bf16[96,3072]{1,0:T(8,128)(2,1)S(1)}, bf16[96,3072]{1,0:T(8,128)(2,1)S(1)}) custom-call(s32[2]{0:T(128)S(1)} %pad_add_fusion.place, bf16[384,768]{1,0:T(8,128)(2,1)S(1)} %get-tuple-element.90.attended, bf16[768,6144]{1,0:T(8,128)(2,1)} %weight.9), custom_call_target="tpu_custom_call" | custom-call | bytes 11070000 | tf_op jit(solution)/shard_map/blocks/pallas_call | solution.py:429
  50.9 0.2 fusion.3
  51.1 1.3 %collective-permute-start.10 = (bf16[96,3072]{1,0:T(8,128)(2,1)S(1)}, bf16[96,3072]{1,0:T(8,128)(2,1)S(1)}, u32[]{:S(2)}, u32[]{:S(2)}) collective-permute-start(bf16[96,3072]{1,0:T(8,128)(2,1)S(1)} %get-tuple-element.93), channel_id=1, source_target_pairs={{3,2},{2,1},{7,6},{6,5},{11,10},{10,9},{15,14},{14,13},{19,18},{18... | collective-permute-start | bytes 1769480 | tf_op jit(solution)/shard_map/ppermute | solution.py:453
  52.4 4.6 %collective-permute-start.9 = (bf16[96,3072]{1,0:T(8,128)(2,1)S(1)}, bf16[96,3072]{1,0:T(8,128)(2,1)S(1)}, u32[]{:S(2)}, u32[]{:S(2)}) collective-permute-start(bf16[96,3072]{1,0:T(8,128)(2,1)S(1)} %get-tuple-element.94), channel_id=1, source_target_pairs={{0,1},{1,2},{4,5},{5,6},{8,9},{9,10},{12,13},{13,14},{16,17},{17,1... | collective-permute-start | bytes 1769480 | tf_op jit(solution)/shard_map/ppermute | solution.py:452
  57.0 3.4 %blocks.4 = (bf16[96,3072]{1,0:T(8,128)(2,1)S(1)}, bf16[96,3072]{1,0:T(8,128)(2,1)S(1)}) custom-call(s32[2]{0:T(128)S(1)} %pad_add_fusion.place, bf16[384,768]{1,0:T(8,128)(2,1)S(1)} %get-tuple-element.90.attended, bf16[768,6144]{1,0:T(8,128)(2,1)} %weight.9), custom_call_target="tpu_custom_call" | custom-call | bytes 11070000 | tf_op jit(solution)/shard_map/blocks/pallas_call | solution.py:429
  60.4 1.7 %collective-permute-done.11 = bf16[96,3072]{1,0:T(8,128)(2,1)S(1)} collective-permute-done((bf16[96,3072]{1,0:T(8,128)(2,1)S(1)}, bf16[96,3072]{1,0:T(8,128)(2,1)S(1)}, u32[]{:S(2)}, u32[]{:S(2)}) %collective-permute-start.11) | collective-permute-done | bytes 589856 | tf_op jit(solution)/shard_map/ppermute | solution.py:452
  62.2 0.2 add_convert_fusion.2
  62.4 1.9 %collective-permute-start.14 = (bf16[96,3072]{1,0:T(8,128)(2,1)S(1)}, bf16[96,3072]{1,0:T(8,128)(2,1)S(1)}, u32[]{:S(2)}, u32[]{:S(2)}) collective-permute-start(bf16[96,3072]{1,0:T(8,128)(2,1)S(1)} %add_convert_fusion.2), channel_id=1, source_target_pairs={{3,2},{2,1},{1,0},{7,6},{6,5},{5,4},{11,10},{10,9},{9,8},{15,14},{... | collective-permute-start | bytes 1769480 | tf_op jit(solution)/shard_map/ppermute | solution.py:453
  64.3 0.1 add_convert_fusion.3
  64.4 4.4 %collective-permute-start.13 = (bf16[96,3072]{1,0:T(8,128)(2,1)S(1)}, bf16[96,3072]{1,0:T(8,128)(2,1)S(1)}, u32[]{:S(2)}, u32[]{:S(2)}) collective-permute-start(bf16[96,3072]{1,0:T(8,128)(2,1)S(1)} %add_convert_fusion.3), channel_id=1, source_target_pairs={{0,1},{1,2},{2,3},{4,5},{5,6},{6,7},{8,9},{9,10},{10,11},{12,13},{... | collective-permute-start | bytes 1769480 | tf_op jit(solution)/shard_map/ppermute | solution.py:452
  68.8 3.4 %blocks.5 = (bf16[96,3072]{1,0:T(8,128)(2,1)S(1)}, bf16[96,3072]{1,0:T(8,128)(2,1)S(1)}) custom-call(s32[2]{0:T(128)S(1)} %pad_add_fusion.place, bf16[384,768]{1,0:T(8,128)(2,1)S(1)} %get-tuple-element.90.attended, bf16[768,6144]{1,0:T(8,128)(2,1)} %weight.9), custom_call_target="tpu_custom_call" | custom-call | bytes 11070000 | tf_op jit(solution)/shard_map/blocks/pallas_call | solution.py:429
  72.3 0.2 collective-permute-done.10
  72.5 2.3 %collective-permute-done.9 = bf16[96,3072]{1,0:T(8,128)(2,1)S(1)} collective-permute-done((bf16[96,3072]{1,0:T(8,128)(2,1)S(1)}, bf16[96,3072]{1,0:T(8,128)(2,1)S(1)}, u32[]{:S(2)}, u32[]{:S(2)}) %collective-permute-start.9) | collective-permute-done | bytes 589856 | tf_op jit(solution)/shard_map/ppermute | solution.py:452
  74.8 0.1 add_convert_fusion
  75.0 0.0 copy-start.3
  75.0 1.9 %collective-permute-start.16 = (bf16[96,3072]{1,0:T(8,128)(2,1)S(1)}, bf16[96,3072]{1,0:T(8,128)(2,1)S(1)}, u32[]{:S(2)}, u32[]{:S(2)}) collective-permute-start(bf16[96,3072]{1,0:T(8,128)(2,1)S(1)} %add_convert_fusion), channel_id=1, source_target_pairs={{3,2},{2,1},{1,0},{7,6},{6,5},{5,4},{11,10},{10,9},{9,8},{15,14},{... | collective-permute-start | bytes 1769480 | tf_op jit(solution)/shard_map/ppermute | solution.py:453
  76.9 0.1 add_convert_fusion.1
  77.1 4.4 %collective-permute-start.15 = (bf16[96,3072]{1,0:T(8,128)(2,1)S(1)}, bf16[96,3072]{1,0:T(8,128)(2,1)S(1)}, u32[]{:S(2)}, u32[]{:S(2)}) collective-permute-start(bf16[96,3072]{1,0:T(8,128)(2,1)S(1)} %add_convert_fusion.1), channel_id=1, source_target_pairs={{0,1},{1,2},{2,3},{4,5},{5,6},{6,7},{8,9},{9,10},{10,11},{12,13},{... | collective-permute-start | bytes 1769480 | tf_op jit(solution)/shard_map/ppermute | solution.py:452
  81.5 5.0 %own.1 = (bf16[96,6144]{1,0:T(8,128)(2,1)S(1)}, f32[1,6144]{1,0:T(1,128)S(1)}) custom-call(s32[2]{0:T(128)S(1)} %pad_add_fusion.place, s32[4]{0:T(128)S(1)} %copy-done.3, bf16[384,768]{1,0:T(8,128)(2,1)S(1)} %get-tuple-element.90.attended, bf16[768,6144]{1,0:T(8,128)(2,1)} %weight.9, f32[64,6144]{1,0:T(8,128)} %gate_table.1), custom_call_target="tpu_custom_call" | custom-call | bytes 18450000 | tf_op jit(solution)/shard_map/own/pallas_call | solution.py:456
  86.5 1.0 collective-permute-done.13
  87.5 0.3 multiply_convert_fusion.done
  87.7 7.5 %collective-permute-done.16.down = bf16[96,3072]{1,0:T(8,128)(2,1)S(1)} collective-permute-done((bf16[96,3072]{1,0:T(8,128)(2,1)S(1)}, bf16[96,3072]{1,0:T(8,128)(2,1)S(1)}, u32[]{:S(2)}, u32[]{:S(2)}) %collective-permute-start.16) | collective-permute-done | bytes 589856 | tf_op jit(solution)/shard_map/ppermute | solution.py:453
  95.2 3.3 %collective-permute-done.15.up = bf16[96,3072]{1,0:T(8,128)(2,1)S(1)} collective-permute-done((bf16[96,3072]{1,0:T(8,128)(2,1)S(1)}, bf16[96,3072]{1,0:T(8,128)(2,1)S(1)}, u32[]{:S(2)}, u32[]{:S(2)}) %collective-permute-start.15) | collective-permute-done | bytes 589856 | tf_op jit(solution)/shard_map/ppermute | solution.py:452
  98.4 1.1 %final.1 = bf16[96,6144]{1,0:T(8,128)(2,1)} custom-call(bf16[96,3072]{1,0:T(8,128)(2,1)S(1)} %multiply_convert_fusion.done, bf16[96,6144]{1,0:T(8,128)(2,1)S(1)} %get-tuple-element.91.projected, f32[1,6144]{1,0:T(1,128)S(1)} %get-tuple-element.92.gate, bf16[96,3072]{1,0:T(8,128)(2,1)S(1)} %collective-permute-done.15.up, ...), custom_call_target="tpu_custom_call" | custom-call | bytes 9963000 | tf_op jit(solution)/shard_map/final/pallas_call | solution.py:477
  (17 shorter events, 0.0 us)
Async XLA Ops:
  0.0 3.8 %collective-permute-start = (bf16[384,768]{1,0:T(8,128)(2,1)}, bf16[384,768]{1,0:T(8,128)(2,1)S(1)}, u32[]{:S(2)}, u32[]{:S(2)}) collective-permute-start(bf16[384,768]{1,0:T(8,128)(2,1)} %key.7), channel_id=1, source_target_pairs={{0,4},{4,0},{8,12},{12,8},{1,5},{5,1},{9,13},{13,9},{2,6},{6,2},{1... | collective-permute-start | bytes 1769480 | tf_op jit(solution)/shard_map/ppermute | solution.py:331
  0.0 3.8 %collective-permute-start.1 = (bf16[384,768]{1,0:T(8,128)(2,1)}, bf16[384,768]{1,0:T(8,128)(2,1)S(1)}, u32[]{:S(2)}, u32[]{:S(2)}) collective-permute-start(bf16[384,768]{1,0:T(8,128)(2,1)} %value.7), channel_id=1, source_target_pairs={{0,4},{4,0},{8,12},{12,8},{1,5},{5,1},{9,13},{13,9},{2,6},{6,2},{1... | collective-permute-start | bytes 1769480 | tf_op jit(solution)/shard_map/ppermute | solution.py:332
  2.2 7.3 %copy-start = (bf16[384,768]{1,0:T(8,128)(2,1)S(1)}, bf16[384,768]{1,0:T(8,128)(2,1)}, u32[]{:S(2)}) copy-start(bf16[384,768]{1,0:T(8,128)(2,1)} %key.7) | copy-start | bytes 1769476
  2.2 7.3 %copy-start.1 = (bf16[384,768]{1,0:T(8,128)(2,1)S(1)}, bf16[384,768]{1,0:T(8,128)(2,1)}, u32[]{:S(2)}) copy-start(bf16[384,768]{1,0:T(8,128)(2,1)} %value.7) | copy-start | bytes 1769476
  2.3 7.3 %collective-permute-start.2 = (bf16[96,768]{1,0:T(8,128)(2,1)S(1)}, bf16[96,768]{1,0:T(8,128)(2,1)S(1)}, u32[]{:S(2)}, u32[]{:S(2)}) collective-permute-start(bf16[96,768]{1,0:T(8,128)(2,1)S(1)} %get-tuple-element.51), channel_id=1, source_target_pairs={{8,0},{12,4},{9,1},{13,5},{10,2},{14,6},{11,3},{15,7},{24,16},{28,... | collective-permute-start | bytes 442376 | tf_op jit(solution)/shard_map/ppermute | solution.py:32
  3.8 0.7 copy-start.2
  7.8 12.2 %collective-permute-start.4 = (bf16[192,768]{1,0:T(8,128)(2,1)S(1)}, bf16[192,768]{1,0:T(8,128)(2,1)S(1)}, u32[]{:S(2)}, u32[]{:S(2)}) collective-permute-start(bf16[192,768]{1,0:T(8,128)(2,1)S(1)} %get-tuple-element.55), channel_id=1, source_target_pairs={{8,0},{12,4},{9,1},{13,5},{10,2},{14,6},{11,3},{15,7},{24,16},{28,... | collective-permute-start | bytes 884744 | tf_op jit(solution)/shard_map/ppermute | solution.py:32
  10.2 8.0 %collective-permute-start.3 = (bf16[96,896]{1,0:T(8,128)(2,1)S(1)}, bf16[96,896]{1,0:T(8,128)(2,1)S(1)}, u32[]{:S(2)}, u32[]{:S(2)}) collective-permute-start(bf16[96,896]{1,0:T(8,128)(2,1)S(1)} %served.2), channel_id=1, source_target_pairs={{0,8},{4,12},{1,9},{5,13},{2,10},{6,14},{3,11},{7,15},{16,24},{20,... | collective-permute-start | bytes 516104 | tf_op jit(solution)/shard_map/ppermute | solution.py:32
  11.5 8.6 %collective-permute-start.5 = (bf16[96,768]{1,0:T(8,128)(2,1)S(1)}, bf16[96,768]{1,0:T(8,128)(2,1)S(1)}, u32[]{:S(2)}, u32[]{:S(2)}) collective-permute-start(bf16[96,768]{1,0:T(8,128)(2,1)S(1)} %get-tuple-element.56), channel_id=1, source_target_pairs={{8,0},{12,4},{9,1},{13,5},{10,2},{14,6},{11,3},{15,7},{24,16},{28,... | collective-permute-start | bytes 442376 | tf_op jit(solution)/shard_map/ppermute | solution.py:32
  18.8 22.7 %collective-permute-start.8 = (bf16[96,3072]{1,0:T(8,128)(2,1)S(1)}, bf16[96,3072]{1,0:T(8,128)(2,1)S(1)}, u32[]{:S(2)}, u32[]{:S(2)}) collective-permute-start(bf16[96,3072]{1,0:T(8,128)(2,1)S(1)} %opening.2), channel_id=1, source_target_pairs={{0,1},{3,2},{4,5},{7,6},{8,9},{11,10},{12,13},{15,14},{16,17},{19,... | collective-permute-start | bytes 1769480 | tf_op jit(solution)/shard_map/ppermute | solution.py:409
  20.7 16.5 %collective-permute-start.6 = (bf16[288,896]{1,0:T(8,128)(2,1)S(1)}, bf16[288,896]{1,0:T(8,128)(2,1)S(1)}, u32[]{:S(2)}, u32[]{:S(2)}) collective-permute-start(bf16[288,896]{1,0:T(8,128)(2,1)S(1)} %served.3), channel_id=1, source_target_pairs={{0,8},{4,12},{1,9},{5,13},{2,10},{6,14},{3,11},{7,15},{16,24},{20,... | collective-permute-start | bytes 1548296 | tf_op jit(solution)/shard_map/ppermute | solution.py:32
  22.6 28.3 %collective-permute-start.7 = (bf16[96,3072]{1,0:T(8,128)(2,1)S(1)}, bf16[96,3072]{1,0:T(8,128)(2,1)S(1)}, u32[]{:S(2)}, u32[]{:S(2)}) collective-permute-start(bf16[96,3072]{1,0:T(8,128)(2,1)S(1)} %opening.3), channel_id=1, source_target_pairs={{0,1},{3,2},{4,5},{7,6},{8,9},{11,10},{12,13},{15,14},{16,17},{19,... | collective-permute-start | bytes 1769480 | tf_op jit(solution)/shard_map/ppermute | solution.py:413
  41.7 18.7 %collective-permute-start.12 = (bf16[96,3072]{1,0:T(8,128)(2,1)S(1)}, bf16[96,3072]{1,0:T(8,128)(2,1)S(1)}, u32[]{:S(2)}, u32[]{:S(2)}) collective-permute-start(bf16[96,3072]{1,0:T(8,128)(2,1)S(1)} %get-tuple-element.95), channel_id=1, source_target_pairs={{3,2},{2,1},{7,6},{6,5},{11,10},{10,9},{15,14},{14,13},{19,18},{18... | collective-permute-start | bytes 1769480 | tf_op jit(solution)/shard_map/ppermute | solution.py:453
  43.0 19.2 %collective-permute-start.11 = (bf16[96,3072]{1,0:T(8,128)(2,1)S(1)}, bf16[96,3072]{1,0:T(8,128)(2,1)S(1)}, u32[]{:S(2)}, u32[]{:S(2)}) collective-permute-start(bf16[96,3072]{1,0:T(8,128)(2,1)S(1)} %get-tuple-element.96), channel_id=1, source_target_pairs={{0,1},{1,2},{4,5},{5,6},{8,9},{9,10},{12,13},{13,14},{16,17},{17,1... | collective-permute-start | bytes 1769480 | tf_op jit(solution)/shard_map/ppermute | solution.py:452
  51.1 21.4 %collective-permute-start.10 = (bf16[96,3072]{1,0:T(8,128)(2,1)S(1)}, bf16[96,3072]{1,0:T(8,128)(2,1)S(1)}, u32[]{:S(2)}, u32[]{:S(2)}) collective-permute-start(bf16[96,3072]{1,0:T(8,128)(2,1)S(1)} %get-tuple-element.93), channel_id=1, source_target_pairs={{3,2},{2,1},{7,6},{6,5},{11,10},{10,9},{15,14},{14,13},{19,18},{18... | collective-permute-start | bytes 1769480 | tf_op jit(solution)/shard_map/ppermute | solution.py:453
  52.4 22.4 %collective-permute-start.9 = (bf16[96,3072]{1,0:T(8,128)(2,1)S(1)}, bf16[96,3072]{1,0:T(8,128)(2,1)S(1)}, u32[]{:S(2)}, u32[]{:S(2)}) collective-permute-start(bf16[96,3072]{1,0:T(8,128)(2,1)S(1)} %get-tuple-element.94), channel_id=1, source_target_pairs={{0,1},{1,2},{4,5},{5,6},{8,9},{9,10},{12,13},{13,14},{16,17},{17,1... | collective-permute-start | bytes 1769480 | tf_op jit(solution)/shard_map/ppermute | solution.py:452
  62.4 24.2 %collective-permute-start.14 = (bf16[96,3072]{1,0:T(8,128)(2,1)S(1)}, bf16[96,3072]{1,0:T(8,128)(2,1)S(1)}, u32[]{:S(2)}, u32[]{:S(2)}) collective-permute-start(bf16[96,3072]{1,0:T(8,128)(2,1)S(1)} %add_convert_fusion.2), channel_id=1, source_target_pairs={{3,2},{2,1},{1,0},{7,6},{6,5},{5,4},{11,10},{10,9},{9,8},{15,14},{... | collective-permute-start | bytes 1769480 | tf_op jit(solution)/shard_map/ppermute | solution.py:453
  64.4 23.0 %collective-permute-start.13 = (bf16[96,3072]{1,0:T(8,128)(2,1)S(1)}, bf16[96,3072]{1,0:T(8,128)(2,1)S(1)}, u32[]{:S(2)}, u32[]{:S(2)}) collective-permute-start(bf16[96,3072]{1,0:T(8,128)(2,1)S(1)} %add_convert_fusion.3), channel_id=1, source_target_pairs={{0,1},{1,2},{2,3},{4,5},{5,6},{6,7},{8,9},{9,10},{10,11},{12,13},{... | collective-permute-start | bytes 1769480 | tf_op jit(solution)/shard_map/ppermute | solution.py:452
  75.0 6.5 %copy-start.3 = (s32[4]{0:T(128)S(1)}, s32[4]{0:T(128)}, u32[]{:S(2)}) copy-start(s32[4]{0:T(128)} %levels.1) | copy-start | bytes 52
  75.0 20.2 %collective-permute-start.16 = (bf16[96,3072]{1,0:T(8,128)(2,1)S(1)}, bf16[96,3072]{1,0:T(8,128)(2,1)S(1)}, u32[]{:S(2)}, u32[]{:S(2)}) collective-permute-start(bf16[96,3072]{1,0:T(8,128)(2,1)S(1)} %add_convert_fusion), channel_id=1, source_target_pairs={{3,2},{2,1},{1,0},{7,6},{6,5},{5,4},{11,10},{10,9},{9,8},{15,14},{... | collective-permute-start | bytes 1769480 | tf_op jit(solution)/shard_map/ppermute | solution.py:453
  77.1 21.4 %collective-permute-start.15 = (bf16[96,3072]{1,0:T(8,128)(2,1)S(1)}, bf16[96,3072]{1,0:T(8,128)(2,1)S(1)}, u32[]{:S(2)}, u32[]{:S(2)}) collective-permute-start(bf16[96,3072]{1,0:T(8,128)(2,1)S(1)} %add_convert_fusion.1), channel_id=1, source_target_pairs={{0,1},{1,2},{2,3},{4,5},{5,6},{6,7},{8,9},{9,10},{10,11},{12,13},{... | collective-permute-start | bytes 1769480 | tf_op jit(solution)/shard_map/ppermute | solution.py:452

commit v17 on v15

--- a/solution.py
+++ b/solution.py
@@ -115,9 +115,28 @@
             copy.wait()
 
 
-def local_kernel(spans, ranks, part, facts, query, key, value, key_beside, value_beside, result, sums, *scratch):
+def local_kernel(spans, ranks, part, who, facts, query, key, value, key_beside, value_beside, *refs):
     here = Facts(facts, spans)
-    query_, key_, value_, key_beside_, value_beside_, semaphores = scratch
+    if who is None:
+        attend_here(here, ranks, part, query, key, value, key_beside, value_beside, *refs)
+        return
+    mine = here.span > 1 if who == "askers" else here.span < 2
+
+    @pl.when(mine)
+    def _():
+        attend_here(here, ranks, part, query, key, value, key_beside, value_beside, *refs)
+
+    *before, result, sums = refs[:-6]
+    if before:
+
+        @pl.when(jnp.logical_not(mine))
+        def _():
+            result[...] = before[0][...]
+            sums[...] = before[1][...]
+
+
+def attend_here(here, ranks, part, query, key, value, key_beside, value_beside, *refs):
+    result, sums, query_, key_, value_, key_beside_, value_beside_, semaphores = refs[-8:]
     start, size = parts_of(here.rank, ranks, query.shape[0])[part]
     copies = [
         copied(source, target, semaphores.at[index])
@@ -198,27 +217,29 @@
 
 def opening_kernel(ranks, distances, spans, first, facts, *refs):
     own, own_sum, *served = refs[:2 + len(distances)]
-    weight, result, *scratch = refs[2 + len(distances):]
+    weight, *fetched, result = refs[2 + len(distances):-3]
+    scratch = refs[-3:]
+    fetched = fetched[0] if fetched else None
     rows = scratch[-1]
     here = Facts(facts, spans)
 
     @pl.when(jnp.logical_or(here.rank == 0, here.rank == ranks - 1))
     def _():
-        tiles, copies = weight, [None] * weight.shape[0]
-        if first:
-            tiles, semaphores, _ = scratch
-            copies = streamed(weight, first, tiles, semaphores)
+        tiles, semaphores, _ = scratch
+        tile = tiles.shape[2]
+        parts = [] if fetched is None else [(None, fetched, index) for index in range(fetched.shape[0])]
+        copies = streamed(weight, first + len(parts) * tile, tiles, semaphores)
+        parts += [(copy, tiles, index) for index, copy in enumerate(copies)]
 
         def write(columns, part):
             rows[:, columns] = part
 
         merge(here.span, distances, own, own_sum, served, write)
-        tile = tiles.shape[2]
-        for index, copy in enumerate(copies):
+        for at, (copy, held, index) in enumerate(parts):
             if copy is not None:
                 copy.wait()
-            product = jnp.dot(rows[...], tiles[index], preferred_element_type=jnp.float32)
-            result[:, index * tile:(index + 1) * tile] = product.astype(jnp.bfloat16)
+            product = jnp.dot(rows[...], held[index], preferred_element_type=jnp.float32)
+            result[:, at * tile:(at + 1) * tile] = product.astype(jnp.bfloat16)
 
 
 def project_blocks(ranks, first, facts, step, attended, weight, up, down, tiles, semaphores):
@@ -334,6 +355,7 @@
         cost_estimate=taking(1.7),
         name="split",
     )(jnp.stack([span, rank]).astype(jnp.int32), in_hbm(queries))
+    query_late = list(query_late)
     distances = list(range(2, spans, 2))
     asked_early = [shifted(query_early, "span", -distance) for distance in distances]
     swap = [(i, i + 1 - 2 * (i % 2)) for i in range(spans)]
@@ -343,11 +365,11 @@
     def after(value, *others):
         return lax.optimization_barrier((value, others))[0]
 
-    def local(part, facts):
+    def local(part, facts, who=None, before=()):
         size = (block, rows - block)[part]
-        return pl.pallas_call(
-            functools.partial(local_kernel, spans, ranks, part),
-            in_specs=[SMEM, HBM, HBM, HBM, ANY, ANY],
+        return list(pl.pallas_call(
+            functools.partial(local_kernel, spans, ranks, part, who),
+            in_specs=[SMEM, HBM, HBM, HBM, ANY, ANY] + [VMEM] * len(before),
             out_specs=[VMEM] * 2,
             out_shape=[jax.ShapeDtypeStruct((size, width), f32), jax.ShapeDtypeStruct((size, LANES), f32)],
             scratch_shapes=[pltpu.VMEM((size, width), bf16)] + [pltpu.VMEM((rows, width), bf16)] * 4
@@ -355,7 +377,7 @@
             compiler_params=PARAMS,
             cost_estimate=taking(4.0),
             name="local",
-        )(facts, in_hbm(queries), in_hbm(keys), in_hbm(values), key_beside, value_beside)
+        )(facts, in_hbm(queries), in_hbm(keys), in_hbm(values), key_beside, value_beside, *before))
 
     def served(asked, distance):
         return pl.pallas_call(
@@ -369,11 +391,13 @@
             name="served",
         )(facts, keys, values, key_beside, value_beside, *asked)
 
-    early = list(local(0, facts))
-    query_late = after(query_late, early)
+    early = local(0, facts, "others")
+    query_late[0] = after(query_late[0], early)
     asked_early = after(asked_early, early)
+    out_early = [served([q], d) for q, d in zip(asked_early, distances)]
+    early = local(0, after(facts, out_early), "askers", early)
+    query_late[1] = after(query_late[1], early)
     asked_late = [[shifted(query, "span", -distance) for query in query_late] for distance in distances]
-    out_early = [served([q], d) for q, d in zip(asked_early, distances)]
     early += [shifted(o, "span", d) for o, d in zip(out_early, distances)]
 
     chunks = 2
@@ -393,25 +417,30 @@
         fetch_kernel,
         in_specs=[HBM],
         out_specs=VMEM,
-        out_shape=jax.ShapeDtypeStruct(tile_shape, bf16),
-        scratch_shapes=[pltpu.SemaphoreType.DMA((tiles,))],
+        out_shape=jax.ShapeDtypeStruct((tiles // 2, width, tile), bf16),
+        scratch_shapes=[pltpu.SemaphoreType.DMA((tiles // 2,))],
         compiler_params=PARAMS,
-        cost_estimate=taking(2.4),
+        cost_estimate=taking(1.5),
         name="fetch",
-    )(in_hbm(after(out_weight, out_early)))
+    )(in_hbm(after(out_weight, early[:2])))
 
     def opening(chunk, facts):
-        scratch = streaming["scratch_shapes"] if chunk else []
+        fetches = [] if chunk else [fetched]
+        streams = tiles if chunk else tiles - tiles // 2
         return pl.pallas_call(
             functools.partial(opening_kernel, ranks, distances, spans, chunk * columns),
-            in_specs=[SMEM] + [VMEM] * (2 + len(distances)) + [HBM if chunk else VMEM],
+            in_specs=[SMEM] + [VMEM] * (2 + len(distances)) + [HBM] + [VMEM] * len(fetches),
             out_specs=VMEM,
             out_shape=jax.ShapeDtypeStruct((block, columns), bf16),
-            scratch_shapes=scratch + [pltpu.VMEM((block, width), bf16)],
+            scratch_shapes=[
+                pltpu.VMEM((streams, width, tile), bf16),
+                pltpu.SemaphoreType.DMA((streams,)),
+                pltpu.VMEM((block, width), bf16),
+            ],
             compiler_params=PARAMS,
             cost_estimate=taking(3.4),
             name="opening",
-        )(facts, *early, weight if chunk else fetched)
+        )(facts, *early, weight, *fetches)
 
     ends = [(0, 1), (last, last - 1)]
     sent = opening(0, facts)
@@ -420,7 +449,7 @@
     for chunk in range(1, chunks):
         sent = opening(chunk, after(facts, out_late))
         arrived.append([lax.ppermute(sent, "tensor", ends)])
-    late = list(local(1, after(facts, sent)))
+    late = local(1, after(facts, sent))
     late += [shifted(o, "span", d) for o, d in zip(out_late, distances)]
 
     attended_shape = jax.ShapeDtypeStruct((rows, width), bf16)

time: 101 us -> 102 us (level)
  starting transfers between devices: 36.3 us -> 38 us
  waiting for transfers between devices: 25.5 us -> 24.4 us
    ppermute x4, waiting for transfers between devices: 7.99 us -> 5.92 us  [body(): lax.ppermute(down, 'tensor', [(last - i, last - i - 1) for i in range(ste...]
    ppermute x4, starting transfers between devices: 16.9 us -> 18.7 us  [body(): lax.ppermute(up, 'tensor', [(i, i + 1) for i in range(step + 1)])]
    ppermute x4, waiting for transfers between devices: 8.8 us -> 10.2 us  [body(): lax.ppermute(up, 'tensor', [(i, i + 1) for i in range(step + 1)])]
    pallas_call x2 -> x3, Pallas kernels: 7.7 us -> 8.35 us  [local(): pl.pallas_call(functools.partial(local_kernel, spans, ranks, part, who),...]
  transfers between devices with their start and end apart: 17 -> 17, of which waited for: 7 -> 6; matrix products, arithmetic and copies ran while one was open for 2% -> 2% of each run, Pallas kernels for 34% -> 34%
where the time goes in v17:
time: 102 us; the launch traced here: 100 us
  starting transfers between devices  38 us (37%)
  Pallas kernels  34.9 us (34%)
  waiting for transfers between devices  24.4 us (24%)
  other arithmetic  2.19 us (2%)
    ppermute x4, starting transfers between devices, body(): lax.ppermute(up, 'tensor', [(i, i + 1) for i in range(step + 1)])  18.7 us
    pallas_call x3, Pallas kernels, blocks_of(): pl.pallas_call(functools.partial(blocks_kernel, spans, ranks, chunk * col...  10.3 us
    ppermute x4, waiting for transfers between devices, body(): lax.ppermute(up, 'tensor', [(i, i + 1) for i in range(step + 1)])  10.2 us
    ppermute x5, starting transfers between devices, shifted(): lax.ppermute(block, axis, [(i, i + distance) for i in range(count) if 0 <...  9.83 us
    pallas_call x3, Pallas kernels, local(): pl.pallas_call(functools.partial(local_kernel, spans, ranks, part, who),...  8.35 us
    ppermute x5, waiting for transfers between devices, shifted(): lax.ppermute(block, axis, [(i, i + distance) for i in range(count) if 0 <...  8.27 us
    ppermute x4, starting transfers between devices, body(): lax.ppermute(down, 'tensor', [(last - i, last - i - 1) for i in range(ste...  6.43 us
    ppermute x4, waiting for transfers between devices, body(): lax.ppermute(down, 'tensor', [(last - i, last - i - 1) for i in range(ste...  5.92 us
  transfers between devices with their start and end apart: 17, of which 6 were waited for; matrix products, arithmetic and copies ran while one was open for 2% of the time, Pallas kernels for 34%

profile of v17, /device:TPU:14, one launch (start us, length us, event | category | flops | bytes accessed | tf_op | source)
XLA Modules:
  0.0 100.1 jit_solution(14717783627848335298)
XLA Ops:
  0.0 0.5 collective-permute-start.1
  0.5 0.1 pad_add_fusion.1.place
  0.6 1.6 %split.1 = (bf16[96,768]{1,0:T(8,128)(2,1)S(1)}, bf16[192,768]{1,0:T(8,128)(2,1)S(1)}, bf16[96,768]{1,0:T(8,128)(2,1)S(1)}) custom-call(s32[2]{0:T(128)S(1)} %pad_add_fusion.1.place, bf16[384,768]{1,0:T(8,128)(2,1)} %query.7), custom_call_target="tpu_custom_call" | custom-call | bytes 6273000 | tf_op jit(solution)/shard_map/split/pallas_call | solution.py:348
  2.2 1.4 %collective-permute-start.2 = (bf16[96,768]{1,0:T(8,128)(2,1)S(1)}, bf16[96,768]{1,0:T(8,128)(2,1)S(1)}, u32[]{:S(2)}, u32[]{:S(2)}) collective-permute-start(bf16[96,768]{1,0:T(8,128)(2,1)S(1)} %get-tuple-element.52), channel_id=1, source_target_pairs={{8,0},{12,4},{9,1},{13,5},{10,2},{14,6},{11,3},{15,7},{24,16},{28,... | collective-permute-start | bytes 442376 | tf_op jit(solution)/shard_map/ppermute | solution.py:32
  3.6 0.7 pad_add_fusion.facts
  4.3 0.0 copy-start.2
  4.4 0.7 local.3
  5.0 4.0 %collective-permute-start.4 = (bf16[192,768]{1,0:T(8,128)(2,1)S(1)}, bf16[192,768]{1,0:T(8,128)(2,1)S(1)}, u32[]{:S(2)}, u32[]{:S(2)}) collective-permute-start(bf16[192,768]{1,0:T(8,128)(2,1)S(1)} %get-tuple-element.60), channel_id=1, source_target_pairs={{8,0},{12,4},{9,1},{13,5},{10,2},{14,6},{11,3},{15,7},{24,16},{28,... | collective-permute-start | bytes 884744 | tf_op jit(solution)/shard_map/ppermute | solution.py:32
  9.1 0.6 served.2
  9.7 1.3 %collective-permute-start.3 = (bf16[96,896]{1,0:T(8,128)(2,1)S(1)}, bf16[96,896]{1,0:T(8,128)(2,1)S(1)}, u32[]{:S(2)}, u32[]{:S(2)}) collective-permute-start(bf16[96,896]{1,0:T(8,128)(2,1)S(1)} %served.2), channel_id=1, source_target_pairs={{0,8},{4,12},{1,9},{5,13},{2,10},{6,14},{3,11},{7,15},{16,24},{20,... | collective-permute-start | bytes 516104 | tf_op jit(solution)/shard_map/ppermute | solution.py:32
  11.0 3.4 %local.4 = (f32[96,768]{1,0:T(8,128)S(1)}, f32[96,128]{1,0:T(8,128)S(1)}) custom-call(s32[6,4]{1,0:T(8,128)S(1)} %pad_add_fusion.facts, bf16[384,768]{1,0:T(8,128)(2,1)} %query.7, bf16[384,768]{1,0:T(8,128)(2,1)} %key.9, bf16[384,768]{1,0:T(8,128)(2,1)} %value.9, bf16[384,768]{1,0:T(8,128)(2,1)S(1)} %collective-permute-done.key_beside, ...), custom_call_target="tpu_custom_call" | custom-call | bytes 14760000 | tf_op jit(solution)/shard_map/local/pallas_call | solution.py:370
  14.4 1.8 %collective-permute-start.5 = (bf16[96,768]{1,0:T(8,128)(2,1)S(1)}, bf16[96,768]{1,0:T(8,128)(2,1)S(1)}, u32[]{:S(2)}, u32[]{:S(2)}) collective-permute-start(bf16[96,768]{1,0:T(8,128)(2,1)S(1)} %get-tuple-element.62), channel_id=1, source_target_pairs={{8,0},{12,4},{9,1},{13,5},{10,2},{14,6},{11,3},{15,7},{24,16},{28,... | collective-permute-start | bytes 442376 | tf_op jit(solution)/shard_map/ppermute | solution.py:32
  16.3 1.7 %fetch.1.refs_4_ = bf16[2,768,768]{2,1,0:T(8,128)(2,1)S(1)} custom-call(bf16[768,6144]{1,0:T(8,128)(2,1)} %weight.8), custom_call_target="tpu_custom_call" | custom-call | bytes 5535000 | tf_op jit(solution)/shard_map/fetch/pallas_call | solution.py:416
  17.9 0.0 copy-start.1
  18.0 0.6 opening.2
  18.6 1.3 %collective-permute-start.8 = (bf16[96,3072]{1,0:T(8,128)(2,1)S(1)}, bf16[96,3072]{1,0:T(8,128)(2,1)S(1)}, u32[]{:S(2)}, u32[]{:S(2)}) collective-permute-start(bf16[96,3072]{1,0:T(8,128)(2,1)S(1)} %opening.2), channel_id=1, source_target_pairs={{0,1},{3,2},{4,5},{7,6},{8,9},{11,10},{12,13},{15,14},{16,17},{19,... | collective-permute-start | bytes 1769480 | tf_op jit(solution)/shard_map/ppermute | solution.py:447
  20.0 0.6 served.3
  20.6 1.3 %collective-permute-start.6 = (bf16[288,896]{1,0:T(8,128)(2,1)S(1)}, bf16[288,896]{1,0:T(8,128)(2,1)S(1)}, u32[]{:S(2)}, u32[]{:S(2)}) collective-permute-start(bf16[288,896]{1,0:T(8,128)(2,1)S(1)} %served.3), channel_id=1, source_target_pairs={{0,8},{4,12},{1,9},{5,13},{2,10},{6,14},{3,11},{7,15},{16,24},{20,... | collective-permute-start | bytes 1548296 | tf_op jit(solution)/shard_map/ppermute | solution.py:32
  21.9 0.6 opening.3
  22.5 1.3 %collective-permute-start.7 = (bf16[96,3072]{1,0:T(8,128)(2,1)S(1)}, bf16[96,3072]{1,0:T(8,128)(2,1)S(1)}, u32[]{:S(2)}, u32[]{:S(2)}) collective-permute-start(bf16[96,3072]{1,0:T(8,128)(2,1)S(1)} %opening.3), channel_id=1, source_target_pairs={{0,1},{3,2},{4,5},{7,6},{8,9},{11,10},{12,13},{15,14},{16,17},{19,... | collective-permute-start | bytes 1769480 | tf_op jit(solution)/shard_map/ppermute | solution.py:451
  23.8 4.3 %local.5 = (f32[288,768]{1,0:T(8,128)S(1)}, f32[288,128]{1,0:T(8,128)S(1)}) custom-call(s32[6,4]{1,0:T(8,128)S(1)} %pad_add_fusion.facts, bf16[384,768]{1,0:T(8,128)(2,1)} %query.7, bf16[384,768]{1,0:T(8,128)(2,1)} %key.9, bf16[384,768]{1,0:T(8,128)(2,1)} %value.9, bf16[384,768]{1,0:T(8,128)(2,1)S(1)} %collective-permute-done.key_beside, ...), custom_call_target="tpu_custom_call" | custom-call | bytes 14760000 | tf_op jit(solution)/shard_map/local/pallas_call | solution.py:370
  28.1 8.3 %collective-permute-done.6.refs_5_ = bf16[288,896]{1,0:T(8,128)(2,1)S(1)} collective-permute-done((bf16[288,896]{1,0:T(8,128)(2,1)S(1)}, bf16[288,896]{1,0:T(8,128)(2,1)S(1)}, u32[]{:S(2)}, u32[]{:S(2)}) %collective-permute-start.6) | collective-permute-done | bytes 516128 | tf_op jit(solution)/shard_map/ppermute | solution.py:32
  36.4 4.3 %merged_blocks.1 = (bf16[384,768]{1,0:T(8,128)(2,1)S(1)}, bf16[96,3072]{1,0:T(8,128)(2,1)S(1)}, bf16[96,3072]{1,0:T(8,128)(2,1)S(1)}) custom-call(s32[6,4]{1,0:T(8,128)S(1)} %pad_add_fusion.facts, f32[96,768]{1,0:T(8,128)S(1)} %get-tuple-element.57.refs_0_, f32[96,128]{1,0:T(8,128)S(1)} %get-tuple-element.58.refs_1_, ...), custom_call_target="tpu_custom_call" | custom-call | bytes 11070000 | tf_op jit(solution)/shard_map/merged_blocks/pallas_call | solution.py:457
  40.7 0.3 fusion.1
  41.0 1.3 %collective-permute-start.12 = (bf16[96,3072]{1,0:T(8,128)(2,1)S(1)}, bf16[96,3072]{1,0:T(8,128)(2,1)S(1)}, u32[]{:S(2)}, u32[]{:S(2)}) collective-permute-start(bf16[96,3072]{1,0:T(8,128)(2,1)S(1)} %get-tuple-element.101), channel_id=1, source_target_pairs={{3,2},{2,1},{7,6},{6,5},{11,10},{10,9},{15,14},{14,13},{19,18},{18... | collective-permute-start | bytes 1769480 | tf_op jit(solution)/shard_map/ppermute | solution.py:491
  42.3 4.6 %collective-permute-start.11 = (bf16[96,3072]{1,0:T(8,128)(2,1)S(1)}, bf16[96,3072]{1,0:T(8,128)(2,1)S(1)}, u32[]{:S(2)}, u32[]{:S(2)}) collective-permute-start(bf16[96,3072]{1,0:T(8,128)(2,1)S(1)} %get-tuple-element.102), channel_id=1, source_target_pairs={{0,1},{1,2},{4,5},{5,6},{8,9},{9,10},{12,13},{13,14},{16,17},{17,1... | collective-permute-start | bytes 1769480 | tf_op jit(solution)/shard_map/ppermute | solution.py:490
  46.9 3.3 %blocks.3 = (bf16[96,3072]{1,0:T(8,128)(2,1)S(1)}, bf16[96,3072]{1,0:T(8,128)(2,1)S(1)}) custom-call(s32[6,4]{1,0:T(8,128)S(1)} %pad_add_fusion.facts, bf16[384,768]{1,0:T(8,128)(2,1)S(1)} %get-tuple-element.96.attended, bf16[768,6144]{1,0:T(8,128)(2,1)} %weight.8), custom_call_target="tpu_custom_call" | custom-call | bytes 11070000 | tf_op jit(solution)/shard_map/blocks/pallas_call | solution.py:467
  50.2 0.3 fusion.3
  50.5 1.3 %collective-permute-start.10 = (bf16[96,3072]{1,0:T(8,128)(2,1)S(1)}, bf16[96,3072]{1,0:T(8,128)(2,1)S(1)}, u32[]{:S(2)}, u32[]{:S(2)}) collective-permute-start(bf16[96,3072]{1,0:T(8,128)(2,1)S(1)} %get-tuple-element.99), channel_id=1, source_target_pairs={{3,2},{2,1},{7,6},{6,5},{11,10},{10,9},{15,14},{14,13},{19,18},{18... | collective-permute-start | bytes 1769480 | tf_op jit(solution)/shard_map/ppermute | solution.py:491
  51.8 4.9 %collective-permute-start.9 = (bf16[96,3072]{1,0:T(8,128)(2,1)S(1)}, bf16[96,3072]{1,0:T(8,128)(2,1)S(1)}, u32[]{:S(2)}, u32[]{:S(2)}) collective-permute-start(bf16[96,3072]{1,0:T(8,128)(2,1)S(1)} %get-tuple-element.100), channel_id=1, source_target_pairs={{0,1},{1,2},{4,5},{5,6},{8,9},{9,10},{12,13},{13,14},{16,17},{17,1... | collective-permute-start | bytes 1769480 | tf_op jit(solution)/shard_map/ppermute | solution.py:490
  56.7 3.5 %blocks.4 = (bf16[96,3072]{1,0:T(8,128)(2,1)S(1)}, bf16[96,3072]{1,0:T(8,128)(2,1)S(1)}) custom-call(s32[6,4]{1,0:T(8,128)S(1)} %pad_add_fusion.facts, bf16[384,768]{1,0:T(8,128)(2,1)S(1)} %get-tuple-element.96.attended, bf16[768,6144]{1,0:T(8,128)(2,1)} %weight.8), custom_call_target="tpu_custom_call" | custom-call | bytes 11070000 | tf_op jit(solution)/shard_map/blocks/pallas_call | solution.py:467
  60.2 2.3 %collective-permute-done.11 = bf16[96,3072]{1,0:T(8,128)(2,1)S(1)} collective-permute-done((bf16[96,3072]{1,0:T(8,128)(2,1)S(1)}, bf16[96,3072]{1,0:T(8,128)(2,1)S(1)}, u32[]{:S(2)}, u32[]{:S(2)}) %collective-permute-start.11) | collective-permute-done | bytes 589856 | tf_op jit(solution)/shard_map/ppermute | solution.py:490
  62.5 0.1 add_convert_fusion.2
  62.6 1.9 %collective-permute-start.14 = (bf16[96,3072]{1,0:T(8,128)(2,1)S(1)}, bf16[96,3072]{1,0:T(8,128)(2,1)S(1)}, u32[]{:S(2)}, u32[]{:S(2)}) collective-permute-start(bf16[96,3072]{1,0:T(8,128)(2,1)S(1)} %add_convert_fusion.2), channel_id=1, source_target_pairs={{3,2},{2,1},{1,0},{7,6},{6,5},{5,4},{11,10},{10,9},{9,8},{15,14},{... | collective-permute-start | bytes 1769480 | tf_op jit(solution)/shard_map/ppermute | solution.py:491
  64.6 0.2 add_convert_fusion.3
  64.7 4.6 %collective-permute-start.13 = (bf16[96,3072]{1,0:T(8,128)(2,1)S(1)}, bf16[96,3072]{1,0:T(8,128)(2,1)S(1)}, u32[]{:S(2)}, u32[]{:S(2)}) collective-permute-start(bf16[96,3072]{1,0:T(8,128)(2,1)S(1)} %add_convert_fusion.3), channel_id=1, source_target_pairs={{0,1},{1,2},{2,3},{4,5},{5,6},{6,7},{8,9},{9,10},{10,11},{12,13},{... | collective-permute-start | bytes 1769480 | tf_op jit(solution)/shard_map/ppermute | solution.py:490
  69.4 3.5 %blocks.5 = (bf16[96,3072]{1,0:T(8,128)(2,1)S(1)}, bf16[96,3072]{1,0:T(8,128)(2,1)S(1)}) custom-call(s32[6,4]{1,0:T(8,128)S(1)} %pad_add_fusion.facts, bf16[384,768]{1,0:T(8,128)(2,1)S(1)} %get-tuple-element.96.attended, bf16[768,6144]{1,0:T(8,128)(2,1)} %weight.8), custom_call_target="tpu_custom_call" | custom-call | bytes 11070000 | tf_op jit(solution)/shard_map/blocks/pallas_call | solution.py:467
  72.9 2.3 %collective-permute-done.9 = bf16[96,3072]{1,0:T(8,128)(2,1)S(1)} collective-permute-done((bf16[96,3072]{1,0:T(8,128)(2,1)S(1)}, bf16[96,3072]{1,0:T(8,128)(2,1)S(1)}, u32[]{:S(2)}, u32[]{:S(2)}) %collective-permute-start.9) | collective-permute-done | bytes 589856 | tf_op jit(solution)/shard_map/ppermute | solution.py:490
  75.1 0.2 add_convert_fusion
  75.3 1.9 %collective-permute-start.16 = (bf16[96,3072]{1,0:T(8,128)(2,1)S(1)}, bf16[96,3072]{1,0:T(8,128)(2,1)S(1)}, u32[]{:S(2)}, u32[]{:S(2)}) collective-permute-start(bf16[96,3072]{1,0:T(8,128)(2,1)S(1)} %add_convert_fusion), channel_id=1, source_target_pairs={{3,2},{2,1},{1,0},{7,6},{6,5},{5,4},{11,10},{10,9},{9,8},{15,14},{... | collective-permute-start | bytes 1769480 | tf_op jit(solution)/shard_map/ppermute | solution.py:491
  77.2 0.1 add_convert_fusion.1
  77.4 4.6 %collective-permute-start.15 = (bf16[96,3072]{1,0:T(8,128)(2,1)S(1)}, bf16[96,3072]{1,0:T(8,128)(2,1)S(1)}, u32[]{:S(2)}, u32[]{:S(2)}) collective-permute-start(bf16[96,3072]{1,0:T(8,128)(2,1)S(1)} %add_convert_fusion.1), channel_id=1, source_target_pairs={{0,1},{1,2},{2,3},{4,5},{5,6},{6,7},{8,9},{9,10},{10,11},{12,13},{... | collective-permute-start | bytes 1769480 | tf_op jit(solution)/shard_map/ppermute | solution.py:490
  82.0 5.1 %own.1 = (bf16[96,6144]{1,0:T(8,128)(2,1)S(1)}, f32[1,6144]{1,0:T(1,128)S(1)}) custom-call(s32[6,4]{1,0:T(8,128)S(1)} %pad_add_fusion.facts, bf16[384,768]{1,0:T(8,128)(2,1)S(1)} %get-tuple-element.96.attended, bf16[768,6144]{1,0:T(8,128)(2,1)} %weight.8, f32[64,6144]{1,0:T(8,128)} %gate_table.1), custom_call_target="tpu_custom_call" | custom-call | bytes 18450000 | tf_op jit(solution)/shard_map/own/pallas_call | solution.py:494
  87.1 0.7 collective-permute-done.13
  87.8 0.3 multiply_convert_fusion.done
  88.0 5.9 %collective-permute-done.16.down = bf16[96,3072]{1,0:T(8,128)(2,1)S(1)} collective-permute-done((bf16[96,3072]{1,0:T(8,128)(2,1)S(1)}, bf16[96,3072]{1,0:T(8,128)(2,1)S(1)}, u32[]{:S(2)}, u32[]{:S(2)}) %collective-permute-start.16) | collective-permute-done | bytes 589856 | tf_op jit(solution)/shard_map/ppermute | solution.py:491
  93.9 4.9 %collective-permute-done.15.up = bf16[96,3072]{1,0:T(8,128)(2,1)S(1)} collective-permute-done((bf16[96,3072]{1,0:T(8,128)(2,1)S(1)}, bf16[96,3072]{1,0:T(8,128)(2,1)S(1)}, u32[]{:S(2)}, u32[]{:S(2)}) %collective-permute-start.15) | collective-permute-done | bytes 589856 | tf_op jit(solution)/shard_map/ppermute | solution.py:490
  98.8 1.1 %final.1 = bf16[96,6144]{1,0:T(8,128)(2,1)} custom-call(bf16[96,3072]{1,0:T(8,128)(2,1)S(1)} %multiply_convert_fusion.done, bf16[96,6144]{1,0:T(8,128)(2,1)S(1)} %get-tuple-element.97.projected, f32[1,6144]{1,0:T(1,128)S(1)} %get-tuple-element.98.gate, bf16[96,3072]{1,0:T(8,128)(2,1)S(1)} %collective-permute-done.15.up, ...), custom_call_target="tpu_custom_call" | custom-call | bytes 9963000 | tf_op jit(solution)/shard_map/final/pallas_call | solution.py:515
  (20 shorter events, 0.1 us)
Async XLA Ops:
  0.0 4.3 %collective-permute-start = (bf16[384,768]{1,0:T(8,128)(2,1)}, bf16[384,768]{1,0:T(8,128)(2,1)S(1)}, u32[]{:S(2)}, u32[]{:S(2)}) collective-permute-start(bf16[384,768]{1,0:T(8,128)(2,1)} %key.9), channel_id=1, source_target_pairs={{0,4},{4,0},{8,12},{12,8},{1,5},{5,1},{9,13},{13,9},{2,6},{6,2},{1... | collective-permute-start | bytes 1769480 | tf_op jit(solution)/shard_map/ppermute | solution.py:362
  0.0 4.4 %collective-permute-start.1 = (bf16[384,768]{1,0:T(8,128)(2,1)}, bf16[384,768]{1,0:T(8,128)(2,1)S(1)}, u32[]{:S(2)}, u32[]{:S(2)}) collective-permute-start(bf16[384,768]{1,0:T(8,128)(2,1)} %value.9), channel_id=1, source_target_pairs={{0,4},{4,0},{8,12},{12,8},{1,5},{5,1},{9,13},{13,9},{2,6},{6,2},{1... | collective-permute-start | bytes 1769480 | tf_op jit(solution)/shard_map/ppermute | solution.py:363
  2.2 6.8 %collective-permute-start.2 = (bf16[96,768]{1,0:T(8,128)(2,1)S(1)}, bf16[96,768]{1,0:T(8,128)(2,1)S(1)}, u32[]{:S(2)}, u32[]{:S(2)}) collective-permute-start(bf16[96,768]{1,0:T(8,128)(2,1)S(1)} %get-tuple-element.52), channel_id=1, source_target_pairs={{8,0},{12,4},{9,1},{13,5},{10,2},{14,6},{11,3},{15,7},{24,16},{28,... | collective-permute-start | bytes 442376 | tf_op jit(solution)/shard_map/ppermute | solution.py:32
  4.3 4.8 %copy-start = (bf16[384,768]{1,0:T(8,128)(2,1)S(1)}, bf16[384,768]{1,0:T(8,128)(2,1)}, u32[]{:S(2)}) copy-start(bf16[384,768]{1,0:T(8,128)(2,1)} %key.9) | copy-start | bytes 1769476
  4.3 4.8 %copy-start.2 = (bf16[384,768]{1,0:T(8,128)(2,1)S(1)}, bf16[384,768]{1,0:T(8,128)(2,1)}, u32[]{:S(2)}) copy-start(bf16[384,768]{1,0:T(8,128)(2,1)} %value.9) | copy-start | bytes 1769476
  5.0 14.9 %collective-permute-start.4 = (bf16[192,768]{1,0:T(8,128)(2,1)S(1)}, bf16[192,768]{1,0:T(8,128)(2,1)S(1)}, u32[]{:S(2)}, u32[]{:S(2)}) collective-permute-start(bf16[192,768]{1,0:T(8,128)(2,1)S(1)} %get-tuple-element.60), channel_id=1, source_target_pairs={{8,0},{12,4},{9,1},{13,5},{10,2},{14,6},{11,3},{15,7},{24,16},{28,... | collective-permute-start | bytes 884744 | tf_op jit(solution)/shard_map/ppermute | solution.py:32
  9.7 8.2 %collective-permute-start.3 = (bf16[96,896]{1,0:T(8,128)(2,1)S(1)}, bf16[96,896]{1,0:T(8,128)(2,1)S(1)}, u32[]{:S(2)}, u32[]{:S(2)}) collective-permute-start(bf16[96,896]{1,0:T(8,128)(2,1)S(1)} %served.2), channel_id=1, source_target_pairs={{0,8},{4,12},{1,9},{5,13},{2,10},{6,14},{3,11},{7,15},{16,24},{20,... | collective-permute-start | bytes 516104 | tf_op jit(solution)/shard_map/ppermute | solution.py:32
  14.4 5.5 %collective-permute-start.5 = (bf16[96,768]{1,0:T(8,128)(2,1)S(1)}, bf16[96,768]{1,0:T(8,128)(2,1)S(1)}, u32[]{:S(2)}, u32[]{:S(2)}) collective-permute-start(bf16[96,768]{1,0:T(8,128)(2,1)S(1)} %get-tuple-element.62), channel_id=1, source_target_pairs={{8,0},{12,4},{9,1},{13,5},{10,2},{14,6},{11,3},{15,7},{24,16},{28,... | collective-permute-start | bytes 442376 | tf_op jit(solution)/shard_map/ppermute | solution.py:32
  17.9 2.0 %copy-start.1 = (bf16[384,768]{1,0:T(8,128)(2,1)S(1)}, bf16[384,768]{1,0:T(8,128)(2,1)}, u32[]{:S(2)}) copy-start(bf16[384,768]{1,0:T(8,128)(2,1)} %key.9) | copy-start | bytes 1769476
  18.0 2.0 %copy-start.3 = (bf16[384,768]{1,0:T(8,128)(2,1)S(1)}, bf16[384,768]{1,0:T(8,128)(2,1)}, u32[]{:S(2)}) copy-start(bf16[384,768]{1,0:T(8,128)(2,1)} %value.9) | copy-start | bytes 1769476
  18.6 22.1 %collective-permute-start.8 = (bf16[96,3072]{1,0:T(8,128)(2,1)S(1)}, bf16[96,3072]{1,0:T(8,128)(2,1)S(1)}, u32[]{:S(2)}, u32[]{:S(2)}) collective-permute-start(bf16[96,3072]{1,0:T(8,128)(2,1)S(1)} %opening.2), channel_id=1, source_target_pairs={{0,1},{3,2},{4,5},{7,6},{8,9},{11,10},{12,13},{15,14},{16,17},{19,... | collective-permute-start | bytes 1769480 | tf_op jit(solution)/shard_map/ppermute | solution.py:447
  20.6 15.8 %collective-permute-start.6 = (bf16[288,896]{1,0:T(8,128)(2,1)S(1)}, bf16[288,896]{1,0:T(8,128)(2,1)S(1)}, u32[]{:S(2)}, u32[]{:S(2)}) collective-permute-start(bf16[288,896]{1,0:T(8,128)(2,1)S(1)} %served.3), channel_id=1, source_target_pairs={{0,8},{4,12},{1,9},{5,13},{2,10},{6,14},{3,11},{7,15},{16,24},{20,... | collective-permute-start | bytes 1548296 | tf_op jit(solution)/shard_map/ppermute | solution.py:32
  22.5 27.7 %collective-permute-start.7 = (bf16[96,3072]{1,0:T(8,128)(2,1)S(1)}, bf16[96,3072]{1,0:T(8,128)(2,1)S(1)}, u32[]{:S(2)}, u32[]{:S(2)}) collective-permute-start(bf16[96,3072]{1,0:T(8,128)(2,1)S(1)} %opening.3), channel_id=1, source_target_pairs={{0,1},{3,2},{4,5},{7,6},{8,9},{11,10},{12,13},{15,14},{16,17},{19,... | collective-permute-start | bytes 1769480 | tf_op jit(solution)/shard_map/ppermute | solution.py:451
  41.0 19.2 %collective-permute-start.12 = (bf16[96,3072]{1,0:T(8,128)(2,1)S(1)}, bf16[96,3072]{1,0:T(8,128)(2,1)S(1)}, u32[]{:S(2)}, u32[]{:S(2)}) collective-permute-start(bf16[96,3072]{1,0:T(8,128)(2,1)S(1)} %get-tuple-element.101), channel_id=1, source_target_pairs={{3,2},{2,1},{7,6},{6,5},{11,10},{10,9},{15,14},{14,13},{19,18},{18... | collective-permute-start | bytes 1769480 | tf_op jit(solution)/shard_map/ppermute | solution.py:491
  42.3 20.2 %collective-permute-start.11 = (bf16[96,3072]{1,0:T(8,128)(2,1)S(1)}, bf16[96,3072]{1,0:T(8,128)(2,1)S(1)}, u32[]{:S(2)}, u32[]{:S(2)}) collective-permute-start(bf16[96,3072]{1,0:T(8,128)(2,1)S(1)} %get-tuple-element.102), channel_id=1, source_target_pairs={{0,1},{1,2},{4,5},{5,6},{8,9},{9,10},{12,13},{13,14},{16,17},{17,1... | collective-permute-start | bytes 1769480 | tf_op jit(solution)/shard_map/ppermute | solution.py:490
  50.5 22.4 %collective-permute-start.10 = (bf16[96,3072]{1,0:T(8,128)(2,1)S(1)}, bf16[96,3072]{1,0:T(8,128)(2,1)S(1)}, u32[]{:S(2)}, u32[]{:S(2)}) collective-permute-start(bf16[96,3072]{1,0:T(8,128)(2,1)S(1)} %get-tuple-element.99), channel_id=1, source_target_pairs={{3,2},{2,1},{7,6},{6,5},{11,10},{10,9},{15,14},{14,13},{19,18},{18... | collective-permute-start | bytes 1769480 | tf_op jit(solution)/shard_map/ppermute | solution.py:491
  51.8 23.4 %collective-permute-start.9 = (bf16[96,3072]{1,0:T(8,128)(2,1)S(1)}, bf16[96,3072]{1,0:T(8,128)(2,1)S(1)}, u32[]{:S(2)}, u32[]{:S(2)}) collective-permute-start(bf16[96,3072]{1,0:T(8,128)(2,1)S(1)} %get-tuple-element.100), channel_id=1, source_target_pairs={{0,1},{1,2},{4,5},{5,6},{8,9},{9,10},{12,13},{13,14},{16,17},{17,1... | collective-permute-start | bytes 1769480 | tf_op jit(solution)/shard_map/ppermute | solution.py:490
  62.6 24.4 %collective-permute-start.14 = (bf16[96,3072]{1,0:T(8,128)(2,1)S(1)}, bf16[96,3072]{1,0:T(8,128)(2,1)S(1)}, u32[]{:S(2)}, u32[]{:S(2)}) collective-permute-start(bf16[96,3072]{1,0:T(8,128)(2,1)S(1)} %add_convert_fusion.2), channel_id=1, source_target_pairs={{3,2},{2,1},{1,0},{7,6},{6,5},{5,4},{11,10},{10,9},{9,8},{15,14},{... | collective-permute-start | bytes 1769480 | tf_op jit(solution)/shard_map/ppermute | solution.py:491
  64.7 23.0 %collective-permute-start.13 = (bf16[96,3072]{1,0:T(8,128)(2,1)S(1)}, bf16[96,3072]{1,0:T(8,128)(2,1)S(1)}, u32[]{:S(2)}, u32[]{:S(2)}) collective-permute-start(bf16[96,3072]{1,0:T(8,128)(2,1)S(1)} %add_convert_fusion.3), channel_id=1, source_target_pairs={{0,1},{1,2},{2,3},{4,5},{5,6},{6,7},{8,9},{9,10},{10,11},{12,13},{... | collective-permute-start | bytes 1769480 | tf_op jit(solution)/shard_map/ppermute | solution.py:490
  75.3 18.6 %collective-permute-start.16 = (bf16[96,3072]{1,0:T(8,128)(2,1)S(1)}, bf16[96,3072]{1,0:T(8,128)(2,1)S(1)}, u32[]{:S(2)}, u32[]{:S(2)}) collective-permute-start(bf16[96,3072]{1,0:T(8,128)(2,1)S(1)} %add_convert_fusion), channel_id=1, source_target_pairs={{3,2},{2,1},{1,0},{7,6},{6,5},{5,4},{11,10},{10,9},{9,8},{15,14},{... | collective-permute-start | bytes 1769480 | tf_op jit(solution)/shard_map/ppermute | solution.py:491
  77.4 21.5 %collective-permute-start.15 = (bf16[96,3072]{1,0:T(8,128)(2,1)S(1)}, bf16[96,3072]{1,0:T(8,128)(2,1)S(1)}, u32[]{:S(2)}, u32[]{:S(2)}) collective-permute-start(bf16[96,3072]{1,0:T(8,128)(2,1)S(1)} %add_convert_fusion.1), channel_id=1, source_target_pairs={{0,1},{1,2},{2,3},{4,5},{5,6},{6,7},{8,9},{9,10},{10,11},{12,13},{... | collective-permute-start | bytes 1769480 | tf_op jit(solution)/shard_map/ppermute | solution.py:490

commit v18 on v16

--- a/solution.py
+++ b/solution.py
@@ -96,8 +96,9 @@
     return (early, block), (late, rows - block)
 
 
-def split_kernel(ranks, place, query, *refs):
-    *targets, semaphores = refs
+def split_kernel(ranks, place, query, visible, *refs):
+    *targets, seen, semaphores = refs
+    scalars = copied(visible, seen, semaphores.at[len(targets)])
 
     @pl.when(place[0] > 1)
     def _():
@@ -109,6 +110,8 @@
         ]
         for copy in copies:
             copy.wait()
+
+    scalars.wait()
 
 
 def local_kernel(ranks, part, place, visible, query, key, value, key_beside, value_beside, result, sums, *scratch):
@@ -187,11 +190,9 @@
     ]
 
 
-def fetch_kernel(ranks, place, weight, tiles, semaphores):
-    @pl.when(jnp.logical_or(place[1] == 0, place[1] == ranks - 1))
-    def _():
-        for copy in streamed(weight, 0, tiles, semaphores):
-            copy.wait()
+def fetch_kernel(weight, tiles, semaphores):
+    for copy in streamed(weight, 0, tiles, semaphores):
+        copy.wait()
 
 
 def opening_kernel(ranks, distances, first, place, *refs):
@@ -315,16 +316,17 @@
     bf16, f32 = jnp.bfloat16, jnp.float32
     place = jnp.stack([span, rank]).astype(jnp.int32)
     third = (rows - block) // 48 * 16
-    query_early, *query_late = pl.pallas_call(
+    query_early, *query_late, seen = pl.pallas_call(
         functools.partial(split_kernel, ranks),
-        in_specs=[SMEM, HBM],
-        out_specs=[VMEM] * 3,
-        out_shape=[jax.ShapeDtypeStruct((part, width), bf16) for part in (block, rows - block - third, third)],
-        scratch_shapes=[pltpu.SemaphoreType.DMA((3,))],
+        in_specs=[SMEM, HBM, HBM],
+        out_specs=[VMEM] * 3 + [SMEM],
+        out_shape=[jax.ShapeDtypeStruct((part, width), bf16) for part in (block, rows - block - third, third)]
+        + [jax.ShapeDtypeStruct(visible.shape, visible.dtype)],
+        scratch_shapes=[pltpu.SemaphoreType.DMA((4,))],
         compiler_params=PARAMS,
         cost_estimate=taking(1.7),
         name="split",
-    )(place, in_hbm(queries))
+    )(place, in_hbm(queries), in_hbm(visible))
     distances = list(range(2, spans, 2))
     asked_early = [shifted(query_early, "span", -distance) for distance in distances]
     swap = [(i, i + 1 - 2 * (i % 2)) for i in range(spans)]
@@ -346,7 +348,7 @@
             compiler_params=PARAMS,
             cost_estimate=taking(4.0),
             name="local",
-        )(place, visible, in_hbm(queries), in_hbm(keys), in_hbm(values), key_beside, value_beside)
+        )(place, seen, in_hbm(queries), in_hbm(keys), in_hbm(values), key_beside, value_beside)
 
     def served(asked, distance):
         return pl.pallas_call(
@@ -358,7 +360,7 @@
             compiler_params=PARAMS,
             cost_estimate=taking(3.3),
             name="served",
-        )(place, visible, keys, values, key_beside, value_beside, *asked)
+        )(place, seen, keys, values, key_beside, value_beside, *asked)
 
     early = list(local(0, place))
     query_late = after(query_late, early)
@@ -381,15 +383,15 @@
         cost_estimate=taking(3.0),
     )
     fetched = pl.pallas_call(
-        functools.partial(fetch_kernel, ranks),
-        in_specs=[SMEM, HBM],
+        fetch_kernel,
+        in_specs=[HBM],
         out_specs=VMEM,
         out_shape=jax.ShapeDtypeStruct(tile_shape, bf16),
         scratch_shapes=[pltpu.SemaphoreType.DMA((tiles,))],
         compiler_params=PARAMS,
         cost_estimate=taking(2.4),
         name="fetch",
-    )(after(place, out_early), weight)
+    )(in_hbm(after(out_weight, out_early)))
 
     def opening(chunk, place):
         scratch = streaming["scratch_shapes"] if chunk else []

time: 101 us -> 101 us (level)
  Pallas kernels: 32.8 us -> 35.2 us
    ppermute x5, waiting for transfers between devices: 10.5 us -> 8.45 us  [shifted(): lax.ppermute(block, axis, [(i, i + distance) for i in range(count) if 0 <...]
    ppermute x4, waiting for transfers between devices: 8.26 us -> 10.3 us  [body(): lax.ppermute(up, 'tensor', [(i, i + 1) for i in range(step + 1)])]
    pallas_call x1, Pallas kernels: 0.59 us -> 2.39 us  [body(): pl.pallas_call(fetch_kernel, in_specs=[HBM], out_specs=VMEM, out_shape=ja...]
  transfers between devices with their start and end apart: 17 -> 17, of which waited for: 8 -> 7; matrix products, arithmetic and copies ran while one was open for 1% -> 1% of each run, Pallas kernels for 32% -> 34%
where the time goes in v18:
time: 101 us; the launch traced here: 99.8 us
  starting transfers between devices  36.9 us (37%)
  Pallas kernels  35.2 us (35%)
  waiting for transfers between devices  25.7 us (25%)
  other arithmetic  1.42 us (1%)
    ppermute x4, starting transfers between devices, body(): lax.ppermute(up, 'tensor', [(i, i + 1) for i in range(step + 1)])  16.9 us
    ppermute x5, starting transfers between devices, shifted(): lax.ppermute(block, axis, [(i, i + distance) for i in range(count) if 0 <...  10.5 us
    ppermute x4, waiting for transfers between devices, body(): lax.ppermute(up, 'tensor', [(i, i + 1) for i in range(step + 1)])  10.3 us
    pallas_call x3, Pallas kernels, blocks_of(): pl.pallas_call(functools.partial(blocks_kernel, ranks, chunk * columns, s...  10.2 us
    ppermute x5, waiting for transfers between devices, shifted(): lax.ppermute(block, axis, [(i, i + distance) for i in range(count) if 0 <...  8.45 us
    pallas_call x2, Pallas kernels, local(): pl.pallas_call(functools.partial(local_kernel, ranks, part), in_specs=[SM...  7.64 us
    ppermute x4, waiting for transfers between devices, body(): lax.ppermute(down, 'tensor', [(last - i, last - i - 1) for i in range(ste...  6.95 us
    ppermute x4, starting transfers between devices, body(): lax.ppermute(down, 'tensor', [(last - i, last - i - 1) for i in range(ste...  6.43 us
  transfers between devices with their start and end apart: 17, of which 7 were waited for; matrix products, arithmetic and copies ran while one was open for 1% of the time, Pallas kernels for 34%

profile of v18, /device:TPU:14, one launch (start us, length us, event | category | flops | bytes accessed | tf_op | source)
XLA Modules:
  0.0 99.8 jit_solution(15483741085289973728)
XLA Ops:
  0.0 0.5 collective-permute-start.1
  0.5 0.1 pad_add_fusion.place
  0.6 2.3 %split.1 = (bf16[96,768]{1,0:T(8,128)(2,1)S(1)}, bf16[192,768]{1,0:T(8,128)(2,1)S(1)}, bf16[96,768]{1,0:T(8,128)(2,1)S(1)}, s32[4,4]{1,0:T(4,128)S(1)}) custom-call(s32[2]{0:T(128)S(1)} %pad_add_fusion.place, bf16[384,768]{1,0:T(8,128)(2,1)} %query.5, s32[4,4]{1,0:T(4,128)} %visible.1), custom_call_target="tpu_custom_call" | custom-call | bytes 6273000 | tf_op jit(solution)/shard_map/split/pallas_call | solution.py:319
  2.9 2.0 %collective-permute-start.2 = (bf16[96,768]{1,0:T(8,128)(2,1)S(1)}, bf16[96,768]{1,0:T(8,128)(2,1)S(1)}, u32[]{:S(2)}, u32[]{:S(2)}) collective-permute-start(bf16[96,768]{1,0:T(8,128)(2,1)S(1)} %get-tuple-element.53), channel_id=1, source_target_pairs={{8,0},{12,4},{9,1},{13,5},{10,2},{14,6},{11,3},{15,7},{24,16},{28,... | collective-permute-start | bytes 442376 | tf_op jit(solution)/shard_map/ppermute | solution.py:32
  4.9 0.0 copy-start
  4.9 0.0 copy-start.1
  4.9 3.4 %local.2 = (f32[96,768]{1,0:T(8,128)S(1)}, f32[96,128]{1,0:T(8,128)S(1)}) custom-call(s32[2]{0:T(128)S(1)} %pad_add_fusion.place, s32[4,4]{1,0:T(4,128)S(1)} %get-tuple-element.50.visible, bf16[384,768]{1,0:T(8,128)(2,1)} %query.5, bf16[384,768]{1,0:T(8,128)(2,1)} %key.7, bf16[384,768]{1,0:T(8,128)(2,1)} %value.7, ...), custom_call_target="tpu_custom_call" | custom-call | bytes 14760000 | tf_op jit(solution)/shard_map/local/pallas_call | solution.py:341
  8.3 1.3 %collective-permute-start.4 = (bf16[192,768]{1,0:T(8,128)(2,1)S(1)}, bf16[192,768]{1,0:T(8,128)(2,1)S(1)}, u32[]{:S(2)}, u32[]{:S(2)}) collective-permute-start(bf16[192,768]{1,0:T(8,128)(2,1)S(1)} %get-tuple-element.57), channel_id=1, source_target_pairs={{8,0},{12,4},{9,1},{13,5},{10,2},{14,6},{11,3},{15,7},{24,16},{28,... | collective-permute-start | bytes 884744 | tf_op jit(solution)/shard_map/ppermute | solution.py:32
  9.7 0.6 served.2
  10.3 1.3 %collective-permute-start.3 = (bf16[96,896]{1,0:T(8,128)(2,1)S(1)}, bf16[96,896]{1,0:T(8,128)(2,1)S(1)}, u32[]{:S(2)}, u32[]{:S(2)}) collective-permute-start(bf16[96,896]{1,0:T(8,128)(2,1)S(1)} %served.2), channel_id=1, source_target_pairs={{0,8},{4,12},{1,9},{5,13},{2,10},{6,14},{3,11},{7,15},{16,24},{20,... | collective-permute-start | bytes 516104 | tf_op jit(solution)/shard_map/ppermute | solution.py:32
  11.6 4.6 %collective-permute-start.5 = (bf16[96,768]{1,0:T(8,128)(2,1)S(1)}, bf16[96,768]{1,0:T(8,128)(2,1)S(1)}, u32[]{:S(2)}, u32[]{:S(2)}) collective-permute-start(bf16[96,768]{1,0:T(8,128)(2,1)S(1)} %get-tuple-element.58), channel_id=1, source_target_pairs={{8,0},{12,4},{9,1},{13,5},{10,2},{14,6},{11,3},{15,7},{24,16},{28,... | collective-permute-start | bytes 442376 | tf_op jit(solution)/shard_map/ppermute | solution.py:32
  16.1 2.4 %fetch.1.refs_3_ = bf16[4,768,768]{2,1,0:T(8,128)(2,1)S(1)} custom-call(bf16[768,6144]{1,0:T(8,128)(2,1)} %weight.8), custom_call_target="tpu_custom_call" | custom-call | bytes 8856000 | tf_op jit(solution)/shard_map/fetch/pallas_call | solution.py:385
  18.5 0.6 opening.2
  19.1 1.3 %collective-permute-start.8 = (bf16[96,3072]{1,0:T(8,128)(2,1)S(1)}, bf16[96,3072]{1,0:T(8,128)(2,1)S(1)}, u32[]{:S(2)}, u32[]{:S(2)}) collective-permute-start(bf16[96,3072]{1,0:T(8,128)(2,1)S(1)} %opening.2), channel_id=1, source_target_pairs={{0,1},{3,2},{4,5},{7,6},{8,9},{11,10},{12,13},{15,14},{16,17},{19,... | collective-permute-start | bytes 1769480 | tf_op jit(solution)/shard_map/ppermute | solution.py:411
  20.4 0.6 served.3
  21.0 1.3 %collective-permute-start.6 = (bf16[288,896]{1,0:T(8,128)(2,1)S(1)}, bf16[288,896]{1,0:T(8,128)(2,1)S(1)}, u32[]{:S(2)}, u32[]{:S(2)}) collective-permute-start(bf16[288,896]{1,0:T(8,128)(2,1)S(1)} %served.3), channel_id=1, source_target_pairs={{0,8},{4,12},{1,9},{5,13},{2,10},{6,14},{3,11},{7,15},{16,24},{20,... | collective-permute-start | bytes 1548296 | tf_op jit(solution)/shard_map/ppermute | solution.py:32
  22.3 0.6 opening.3
  22.9 1.3 %collective-permute-start.7 = (bf16[96,3072]{1,0:T(8,128)(2,1)S(1)}, bf16[96,3072]{1,0:T(8,128)(2,1)S(1)}, u32[]{:S(2)}, u32[]{:S(2)}) collective-permute-start(bf16[96,3072]{1,0:T(8,128)(2,1)S(1)} %opening.3), channel_id=1, source_target_pairs={{0,1},{3,2},{4,5},{7,6},{8,9},{11,10},{12,13},{15,14},{16,17},{19,... | collective-permute-start | bytes 1769480 | tf_op jit(solution)/shard_map/ppermute | solution.py:415
  24.2 4.3 %local.3 = (f32[288,768]{1,0:T(8,128)S(1)}, f32[288,128]{1,0:T(8,128)S(1)}) custom-call(s32[2]{0:T(128)S(1)} %pad_add_fusion.place, s32[4,4]{1,0:T(4,128)S(1)} %get-tuple-element.50.visible, bf16[384,768]{1,0:T(8,128)(2,1)} %query.5, bf16[384,768]{1,0:T(8,128)(2,1)} %key.7, bf16[384,768]{1,0:T(8,128)(2,1)} %value.7, ...), custom_call_target="tpu_custom_call" | custom-call | bytes 14760000 | tf_op jit(solution)/shard_map/local/pallas_call | solution.py:341
  28.5 8.4 %collective-permute-done.6.refs_5_ = bf16[288,896]{1,0:T(8,128)(2,1)S(1)} collective-permute-done((bf16[288,896]{1,0:T(8,128)(2,1)S(1)}, bf16[288,896]{1,0:T(8,128)(2,1)S(1)}, u32[]{:S(2)}, u32[]{:S(2)}) %collective-permute-start.6) | collective-permute-done | bytes 516128 | tf_op jit(solution)/shard_map/ppermute | solution.py:32
  36.9 4.3 %merged_blocks.1 = (bf16[384,768]{1,0:T(8,128)(2,1)S(1)}, bf16[96,3072]{1,0:T(8,128)(2,1)S(1)}, bf16[96,3072]{1,0:T(8,128)(2,1)S(1)}) custom-call(s32[2]{0:T(128)S(1)} %pad_add_fusion.place, f32[96,768]{1,0:T(8,128)S(1)} %get-tuple-element.51.refs_0_, f32[96,128]{1,0:T(8,128)S(1)} %get-tuple-element.52.refs_1_, ...), custom_call_target="tpu_custom_call" | custom-call | bytes 11070000 | tf_op jit(solution)/shard_map/merged_blocks/pallas_call | solution.py:421
  41.3 0.2 fusion.1
  41.5 1.3 %collective-permute-start.12 = (bf16[96,3072]{1,0:T(8,128)(2,1)S(1)}, bf16[96,3072]{1,0:T(8,128)(2,1)S(1)}, u32[]{:S(2)}, u32[]{:S(2)}) collective-permute-start(bf16[96,3072]{1,0:T(8,128)(2,1)S(1)} %get-tuple-element.97), channel_id=1, source_target_pairs={{3,2},{2,1},{7,6},{6,5},{11,10},{10,9},{15,14},{14,13},{19,18},{18... | collective-permute-start | bytes 1769480 | tf_op jit(solution)/shard_map/ppermute | solution.py:455
  42.8 4.6 %collective-permute-start.11 = (bf16[96,3072]{1,0:T(8,128)(2,1)S(1)}, bf16[96,3072]{1,0:T(8,128)(2,1)S(1)}, u32[]{:S(2)}, u32[]{:S(2)}) collective-permute-start(bf16[96,3072]{1,0:T(8,128)(2,1)S(1)} %get-tuple-element.98), channel_id=1, source_target_pairs={{0,1},{1,2},{4,5},{5,6},{8,9},{9,10},{12,13},{13,14},{16,17},{17,1... | collective-permute-start | bytes 1769480 | tf_op jit(solution)/shard_map/ppermute | solution.py:454
  47.4 3.3 %blocks.3 = (bf16[96,3072]{1,0:T(8,128)(2,1)S(1)}, bf16[96,3072]{1,0:T(8,128)(2,1)S(1)}) custom-call(s32[2]{0:T(128)S(1)} %pad_add_fusion.place, bf16[384,768]{1,0:T(8,128)(2,1)S(1)} %get-tuple-element.92.attended, bf16[768,6144]{1,0:T(8,128)(2,1)} %weight.8), custom_call_target="tpu_custom_call" | custom-call | bytes 11070000 | tf_op jit(solution)/shard_map/blocks/pallas_call | solution.py:431
  50.7 0.2 fusion.3
  50.9 1.3 %collective-permute-start.10 = (bf16[96,3072]{1,0:T(8,128)(2,1)S(1)}, bf16[96,3072]{1,0:T(8,128)(2,1)S(1)}, u32[]{:S(2)}, u32[]{:S(2)}) collective-permute-start(bf16[96,3072]{1,0:T(8,128)(2,1)S(1)} %get-tuple-element.95), channel_id=1, source_target_pairs={{3,2},{2,1},{7,6},{6,5},{11,10},{10,9},{15,14},{14,13},{19,18},{18... | collective-permute-start | bytes 1769480 | tf_op jit(solution)/shard_map/ppermute | solution.py:455
  52.2 4.6 %collective-permute-start.9 = (bf16[96,3072]{1,0:T(8,128)(2,1)S(1)}, bf16[96,3072]{1,0:T(8,128)(2,1)S(1)}, u32[]{:S(2)}, u32[]{:S(2)}) collective-permute-start(bf16[96,3072]{1,0:T(8,128)(2,1)S(1)} %get-tuple-element.96), channel_id=1, source_target_pairs={{0,1},{1,2},{4,5},{5,6},{8,9},{9,10},{12,13},{13,14},{16,17},{17,1... | collective-permute-start | bytes 1769480 | tf_op jit(solution)/shard_map/ppermute | solution.py:454
  56.8 3.4 %blocks.4 = (bf16[96,3072]{1,0:T(8,128)(2,1)S(1)}, bf16[96,3072]{1,0:T(8,128)(2,1)S(1)}) custom-call(s32[2]{0:T(128)S(1)} %pad_add_fusion.place, bf16[384,768]{1,0:T(8,128)(2,1)S(1)} %get-tuple-element.92.attended, bf16[768,6144]{1,0:T(8,128)(2,1)} %weight.8), custom_call_target="tpu_custom_call" | custom-call | bytes 11070000 | tf_op jit(solution)/shard_map/blocks/pallas_call | solution.py:431
  60.3 2.3 %collective-permute-done.11 = bf16[96,3072]{1,0:T(8,128)(2,1)S(1)} collective-permute-done((bf16[96,3072]{1,0:T(8,128)(2,1)S(1)}, bf16[96,3072]{1,0:T(8,128)(2,1)S(1)}, u32[]{:S(2)}, u32[]{:S(2)}) %collective-permute-start.11) | collective-permute-done | bytes 589856 | tf_op jit(solution)/shard_map/ppermute | solution.py:454
  62.5 0.2 add_convert_fusion.2
  62.7 1.9 %collective-permute-start.14 = (bf16[96,3072]{1,0:T(8,128)(2,1)S(1)}, bf16[96,3072]{1,0:T(8,128)(2,1)S(1)}, u32[]{:S(2)}, u32[]{:S(2)}) collective-permute-start(bf16[96,3072]{1,0:T(8,128)(2,1)S(1)} %add_convert_fusion.2), channel_id=1, source_target_pairs={{3,2},{2,1},{1,0},{7,6},{6,5},{5,4},{11,10},{10,9},{9,8},{15,14},{... | collective-permute-start | bytes 1769480 | tf_op jit(solution)/shard_map/ppermute | solution.py:455
  64.6 0.1 add_convert_fusion.3
  64.8 3.9 %collective-permute-start.13 = (bf16[96,3072]{1,0:T(8,128)(2,1)S(1)}, bf16[96,3072]{1,0:T(8,128)(2,1)S(1)}, u32[]{:S(2)}, u32[]{:S(2)}) collective-permute-start(bf16[96,3072]{1,0:T(8,128)(2,1)S(1)} %add_convert_fusion.3), channel_id=1, source_target_pairs={{0,1},{1,2},{2,3},{4,5},{5,6},{6,7},{8,9},{9,10},{10,11},{12,13},{... | collective-permute-start | bytes 1769480 | tf_op jit(solution)/shard_map/ppermute | solution.py:454
  68.7 3.4 %blocks.5 = (bf16[96,3072]{1,0:T(8,128)(2,1)S(1)}, bf16[96,3072]{1,0:T(8,128)(2,1)S(1)}) custom-call(s32[2]{0:T(128)S(1)} %pad_add_fusion.place, bf16[384,768]{1,0:T(8,128)(2,1)S(1)} %get-tuple-element.92.attended, bf16[768,6144]{1,0:T(8,128)(2,1)} %weight.8), custom_call_target="tpu_custom_call" | custom-call | bytes 11070000 | tf_op jit(solution)/shard_map/blocks/pallas_call | solution.py:431
  72.2 0.2 collective-permute-done.10
  72.3 2.8 %collective-permute-done.9 = bf16[96,3072]{1,0:T(8,128)(2,1)S(1)} collective-permute-done((bf16[96,3072]{1,0:T(8,128)(2,1)S(1)}, bf16[96,3072]{1,0:T(8,128)(2,1)S(1)}, u32[]{:S(2)}, u32[]{:S(2)}) %collective-permute-start.9) | collective-permute-done | bytes 589856 | tf_op jit(solution)/shard_map/ppermute | solution.py:454
  75.2 0.1 add_convert_fusion
  75.3 0.0 copy-start.2
  75.3 1.9 %collective-permute-start.16 = (bf16[96,3072]{1,0:T(8,128)(2,1)S(1)}, bf16[96,3072]{1,0:T(8,128)(2,1)S(1)}, u32[]{:S(2)}, u32[]{:S(2)}) collective-permute-start(bf16[96,3072]{1,0:T(8,128)(2,1)S(1)} %add_convert_fusion), channel_id=1, source_target_pairs={{3,2},{2,1},{1,0},{7,6},{6,5},{5,4},{11,10},{10,9},{9,8},{15,14},{... | collective-permute-start | bytes 1769480 | tf_op jit(solution)/shard_map/ppermute | solution.py:455
  77.3 0.1 add_convert_fusion.1
  77.4 3.9 %collective-permute-start.15 = (bf16[96,3072]{1,0:T(8,128)(2,1)S(1)}, bf16[96,3072]{1,0:T(8,128)(2,1)S(1)}, u32[]{:S(2)}, u32[]{:S(2)}) collective-permute-start(bf16[96,3072]{1,0:T(8,128)(2,1)S(1)} %add_convert_fusion.1), channel_id=1, source_target_pairs={{0,1},{1,2},{2,3},{4,5},{5,6},{6,7},{8,9},{9,10},{10,11},{12,13},{... | collective-permute-start | bytes 1769480 | tf_op jit(solution)/shard_map/ppermute | solution.py:454
  81.4 5.0 %own.1 = (bf16[96,6144]{1,0:T(8,128)(2,1)S(1)}, f32[1,6144]{1,0:T(1,128)S(1)}) custom-call(s32[2]{0:T(128)S(1)} %pad_add_fusion.place, s32[4]{0:T(128)S(1)} %copy-done.2, bf16[384,768]{1,0:T(8,128)(2,1)S(1)} %get-tuple-element.92.attended, bf16[768,6144]{1,0:T(8,128)(2,1)} %weight.8, f32[64,6144]{1,0:T(8,128)} %gate_table.1), custom_call_target="tpu_custom_call" | custom-call | bytes 18450000 | tf_op jit(solution)/shard_map/own/pallas_call | solution.py:458
  86.4 1.4 %collective-permute-done.13 = bf16[96,3072]{1,0:T(8,128)(2,1)S(1)} collective-permute-done((bf16[96,3072]{1,0:T(8,128)(2,1)S(1)}, bf16[96,3072]{1,0:T(8,128)(2,1)S(1)}, u32[]{:S(2)}, u32[]{:S(2)}) %collective-permute-start.13) | collective-permute-done | bytes 589856 | tf_op jit(solution)/shard_map/ppermute | solution.py:454
  87.8 0.3 multiply_convert_fusion.done
  88.1 6.8 %collective-permute-done.16.down = bf16[96,3072]{1,0:T(8,128)(2,1)S(1)} collective-permute-done((bf16[96,3072]{1,0:T(8,128)(2,1)S(1)}, bf16[96,3072]{1,0:T(8,128)(2,1)S(1)}, u32[]{:S(2)}, u32[]{:S(2)}) %collective-permute-start.16) | collective-permute-done | bytes 589856 | tf_op jit(solution)/shard_map/ppermute | solution.py:455
  94.8 3.7 %collective-permute-done.15.up = bf16[96,3072]{1,0:T(8,128)(2,1)S(1)} collective-permute-done((bf16[96,3072]{1,0:T(8,128)(2,1)S(1)}, bf16[96,3072]{1,0:T(8,128)(2,1)S(1)}, u32[]{:S(2)}, u32[]{:S(2)}) %collective-permute-start.15) | collective-permute-done | bytes 589856 | tf_op jit(solution)/shard_map/ppermute | solution.py:454
  98.6 1.1 %final.1 = bf16[96,6144]{1,0:T(8,128)(2,1)} custom-call(bf16[96,3072]{1,0:T(8,128)(2,1)S(1)} %multiply_convert_fusion.done, bf16[96,6144]{1,0:T(8,128)(2,1)S(1)} %get-tuple-element.93.projected, f32[1,6144]{1,0:T(1,128)S(1)} %get-tuple-element.94.gate, bf16[96,3072]{1,0:T(8,128)(2,1)S(1)} %collective-permute-done.15.up, ...), custom_call_target="tpu_custom_call" | custom-call | bytes 9963000 | tf_op jit(solution)/shard_map/final/pallas_call | solution.py:479
  (15 shorter events, 0.0 us)
Async XLA Ops:
  0.0 4.9 %collective-permute-start = (bf16[384,768]{1,0:T(8,128)(2,1)}, bf16[384,768]{1,0:T(8,128)(2,1)S(1)}, u32[]{:S(2)}, u32[]{:S(2)}) collective-permute-start(bf16[384,768]{1,0:T(8,128)(2,1)} %key.7), channel_id=1, source_target_pairs={{0,4},{4,0},{8,12},{12,8},{1,5},{5,1},{9,13},{13,9},{2,6},{6,2},{1... | collective-permute-start | bytes 1769480 | tf_op jit(solution)/shard_map/ppermute | solution.py:333
  0.0 4.9 %collective-permute-start.1 = (bf16[384,768]{1,0:T(8,128)(2,1)}, bf16[384,768]{1,0:T(8,128)(2,1)S(1)}, u32[]{:S(2)}, u32[]{:S(2)}) collective-permute-start(bf16[384,768]{1,0:T(8,128)(2,1)} %value.7), channel_id=1, source_target_pairs={{0,4},{4,0},{8,12},{12,8},{1,5},{5,1},{9,13},{13,9},{2,6},{6,2},{1... | collective-permute-start | bytes 1769480 | tf_op jit(solution)/shard_map/ppermute | solution.py:334
  2.9 6.8 %collective-permute-start.2 = (bf16[96,768]{1,0:T(8,128)(2,1)S(1)}, bf16[96,768]{1,0:T(8,128)(2,1)S(1)}, u32[]{:S(2)}, u32[]{:S(2)}) collective-permute-start(bf16[96,768]{1,0:T(8,128)(2,1)S(1)} %get-tuple-element.53), channel_id=1, source_target_pairs={{8,0},{12,4},{9,1},{13,5},{10,2},{14,6},{11,3},{15,7},{24,16},{28,... | collective-permute-start | bytes 442376 | tf_op jit(solution)/shard_map/ppermute | solution.py:32
  4.9 4.7 %copy-start = (bf16[384,768]{1,0:T(8,128)(2,1)S(1)}, bf16[384,768]{1,0:T(8,128)(2,1)}, u32[]{:S(2)}) copy-start(bf16[384,768]{1,0:T(8,128)(2,1)} %key.7) | copy-start | bytes 1769476
  4.9 4.7 %copy-start.1 = (bf16[384,768]{1,0:T(8,128)(2,1)S(1)}, bf16[384,768]{1,0:T(8,128)(2,1)}, u32[]{:S(2)}) copy-start(bf16[384,768]{1,0:T(8,128)(2,1)} %value.7) | copy-start | bytes 1769476
  8.3 12.1 %collective-permute-start.4 = (bf16[192,768]{1,0:T(8,128)(2,1)S(1)}, bf16[192,768]{1,0:T(8,128)(2,1)S(1)}, u32[]{:S(2)}, u32[]{:S(2)}) collective-permute-start(bf16[192,768]{1,0:T(8,128)(2,1)S(1)} %get-tuple-element.57), channel_id=1, source_target_pairs={{8,0},{12,4},{9,1},{13,5},{10,2},{14,6},{11,3},{15,7},{24,16},{28,... | collective-permute-start | bytes 884744 | tf_op jit(solution)/shard_map/ppermute | solution.py:32
  10.3 8.3 %collective-permute-start.3 = (bf16[96,896]{1,0:T(8,128)(2,1)S(1)}, bf16[96,896]{1,0:T(8,128)(2,1)S(1)}, u32[]{:S(2)}, u32[]{:S(2)}) collective-permute-start(bf16[96,896]{1,0:T(8,128)(2,1)S(1)} %served.2), channel_id=1, source_target_pairs={{0,8},{4,12},{1,9},{5,13},{2,10},{6,14},{3,11},{7,15},{16,24},{20,... | collective-permute-start | bytes 516104 | tf_op jit(solution)/shard_map/ppermute | solution.py:32
  11.6 8.8 %collective-permute-start.5 = (bf16[96,768]{1,0:T(8,128)(2,1)S(1)}, bf16[96,768]{1,0:T(8,128)(2,1)S(1)}, u32[]{:S(2)}, u32[]{:S(2)}) collective-permute-start(bf16[96,768]{1,0:T(8,128)(2,1)S(1)} %get-tuple-element.58), channel_id=1, source_target_pairs={{8,0},{12,4},{9,1},{13,5},{10,2},{14,6},{11,3},{15,7},{24,16},{28,... | collective-permute-start | bytes 442376 | tf_op jit(solution)/shard_map/ppermute | solution.py:32
  19.1 22.2 %collective-permute-start.8 = (bf16[96,3072]{1,0:T(8,128)(2,1)S(1)}, bf16[96,3072]{1,0:T(8,128)(2,1)S(1)}, u32[]{:S(2)}, u32[]{:S(2)}) collective-permute-start(bf16[96,3072]{1,0:T(8,128)(2,1)S(1)} %opening.2), channel_id=1, source_target_pairs={{0,1},{3,2},{4,5},{7,6},{8,9},{11,10},{12,13},{15,14},{16,17},{19,... | collective-permute-start | bytes 1769480 | tf_op jit(solution)/shard_map/ppermute | solution.py:411
  21.0 15.9 %collective-permute-start.6 = (bf16[288,896]{1,0:T(8,128)(2,1)S(1)}, bf16[288,896]{1,0:T(8,128)(2,1)S(1)}, u32[]{:S(2)}, u32[]{:S(2)}) collective-permute-start(bf16[288,896]{1,0:T(8,128)(2,1)S(1)} %served.3), channel_id=1, source_target_pairs={{0,8},{4,12},{1,9},{5,13},{2,10},{6,14},{3,11},{7,15},{16,24},{20,... | collective-permute-start | bytes 1548296 | tf_op jit(solution)/shard_map/ppermute | solution.py:32
  22.9 27.8 %collective-permute-start.7 = (bf16[96,3072]{1,0:T(8,128)(2,1)S(1)}, bf16[96,3072]{1,0:T(8,128)(2,1)S(1)}, u32[]{:S(2)}, u32[]{:S(2)}) collective-permute-start(bf16[96,3072]{1,0:T(8,128)(2,1)S(1)} %opening.3), channel_id=1, source_target_pairs={{0,1},{3,2},{4,5},{7,6},{8,9},{11,10},{12,13},{15,14},{16,17},{19,... | collective-permute-start | bytes 1769480 | tf_op jit(solution)/shard_map/ppermute | solution.py:415
  41.5 18.7 %collective-permute-start.12 = (bf16[96,3072]{1,0:T(8,128)(2,1)S(1)}, bf16[96,3072]{1,0:T(8,128)(2,1)S(1)}, u32[]{:S(2)}, u32[]{:S(2)}) collective-permute-start(bf16[96,3072]{1,0:T(8,128)(2,1)S(1)} %get-tuple-element.97), channel_id=1, source_target_pairs={{3,2},{2,1},{7,6},{6,5},{11,10},{10,9},{15,14},{14,13},{19,18},{18... | collective-permute-start | bytes 1769480 | tf_op jit(solution)/shard_map/ppermute | solution.py:455
  42.8 19.7 %collective-permute-start.11 = (bf16[96,3072]{1,0:T(8,128)(2,1)S(1)}, bf16[96,3072]{1,0:T(8,128)(2,1)S(1)}, u32[]{:S(2)}, u32[]{:S(2)}) collective-permute-start(bf16[96,3072]{1,0:T(8,128)(2,1)S(1)} %get-tuple-element.98), channel_id=1, source_target_pairs={{0,1},{1,2},{4,5},{5,6},{8,9},{9,10},{12,13},{13,14},{16,17},{17,1... | collective-permute-start | bytes 1769480 | tf_op jit(solution)/shard_map/ppermute | solution.py:454
  50.9 21.4 %collective-permute-start.10 = (bf16[96,3072]{1,0:T(8,128)(2,1)S(1)}, bf16[96,3072]{1,0:T(8,128)(2,1)S(1)}, u32[]{:S(2)}, u32[]{:S(2)}) collective-permute-start(bf16[96,3072]{1,0:T(8,128)(2,1)S(1)} %get-tuple-element.95), channel_id=1, source_target_pairs={{3,2},{2,1},{7,6},{6,5},{11,10},{10,9},{15,14},{14,13},{19,18},{18... | collective-permute-start | bytes 1769480 | tf_op jit(solution)/shard_map/ppermute | solution.py:455
  52.2 22.9 %collective-permute-start.9 = (bf16[96,3072]{1,0:T(8,128)(2,1)S(1)}, bf16[96,3072]{1,0:T(8,128)(2,1)S(1)}, u32[]{:S(2)}, u32[]{:S(2)}) collective-permute-start(bf16[96,3072]{1,0:T(8,128)(2,1)S(1)} %get-tuple-element.96), channel_id=1, source_target_pairs={{0,1},{1,2},{4,5},{5,6},{8,9},{9,10},{12,13},{13,14},{16,17},{17,1... | collective-permute-start | bytes 1769480 | tf_op jit(solution)/shard_map/ppermute | solution.py:454
  62.7 23.7 %collective-permute-start.14 = (bf16[96,3072]{1,0:T(8,128)(2,1)S(1)}, bf16[96,3072]{1,0:T(8,128)(2,1)S(1)}, u32[]{:S(2)}, u32[]{:S(2)}) collective-permute-start(bf16[96,3072]{1,0:T(8,128)(2,1)S(1)} %add_convert_fusion.2), channel_id=1, source_target_pairs={{3,2},{2,1},{1,0},{7,6},{6,5},{5,4},{11,10},{10,9},{9,8},{15,14},{... | collective-permute-start | bytes 1769480 | tf_op jit(solution)/shard_map/ppermute | solution.py:455
  64.8 23.0 %collective-permute-start.13 = (bf16[96,3072]{1,0:T(8,128)(2,1)S(1)}, bf16[96,3072]{1,0:T(8,128)(2,1)S(1)}, u32[]{:S(2)}, u32[]{:S(2)}) collective-permute-start(bf16[96,3072]{1,0:T(8,128)(2,1)S(1)} %add_convert_fusion.3), channel_id=1, source_target_pairs={{0,1},{1,2},{2,3},{4,5},{5,6},{6,7},{8,9},{9,10},{10,11},{12,13},{... | collective-permute-start | bytes 1769480 | tf_op jit(solution)/shard_map/ppermute | solution.py:454
  75.3 6.0 %copy-start.2 = (s32[4]{0:T(128)S(1)}, s32[4]{0:T(128)}, u32[]{:S(2)}) copy-start(s32[4]{0:T(128)} %levels.1) | copy-start | bytes 52
  75.3 19.5 %collective-permute-start.16 = (bf16[96,3072]{1,0:T(8,128)(2,1)S(1)}, bf16[96,3072]{1,0:T(8,128)(2,1)S(1)}, u32[]{:S(2)}, u32[]{:S(2)}) collective-permute-start(bf16[96,3072]{1,0:T(8,128)(2,1)S(1)} %add_convert_fusion), channel_id=1, source_target_pairs={{3,2},{2,1},{1,0},{7,6},{6,5},{5,4},{11,10},{10,9},{9,8},{15,14},{... | collective-permute-start | bytes 1769480 | tf_op jit(solution)/shard_map/ppermute | solution.py:455
  77.4 21.2 %collective-permute-start.15 = (bf16[96,3072]{1,0:T(8,128)(2,1)S(1)}, bf16[96,3072]{1,0:T(8,128)(2,1)S(1)}, u32[]{:S(2)}, u32[]{:S(2)}) collective-permute-start(bf16[96,3072]{1,0:T(8,128)(2,1)S(1)} %add_convert_fusion.1), channel_id=1, source_target_pairs={{0,1},{1,2},{2,3},{4,5},{5,6},{6,7},{8,9},{9,10},{10,11},{12,13},{... | collective-permute-start | bytes 1769480 | tf_op jit(solution)/shard_map/ppermute | solution.py:454

commit v19 on v16

--- a/solution.py
+++ b/solution.py
@@ -36,7 +36,7 @@
     return slice(head * HD, (head + 1) * HD)
 
 
-def attend(query, keys, values, flags, write):
+def attend(query, keys, values, flags, write, arrive=None):
     rows, width = query.shape
     scale = LOG2E * HD ** (-0.5)
     lane = lax.broadcasted_iota(jnp.int32, (rows, LANES), 1)
@@ -53,6 +53,8 @@
 
     heads = width // HD
     later = scored(0)
+    if arrive is not None:
+        arrive()
     for head in range(heads):
         columns = head_columns(head)
         scores, later = later, scored(head + 1) if head + 1 < heads else None
@@ -73,13 +75,15 @@
     return packed
 
 
-class Facts:
-    def __init__(self, place, visible):
-        self.span, self.rank, self.visible = place[0], place[1], visible
-        self.beside = self.span + 1 - 2 * lax.rem(self.span, 2)
-
-    def sees(self, asker, span):
-        return self.visible[asker, span] > 0
+def seen_by(visible, asker, span):
+    table = visible[...]
+    row, column = (lax.broadcasted_iota(jnp.int32, table.shape, axis) for axis in (0, 1))
+    here = jnp.logical_and(row == asker, column == span)
+    return jnp.max(jnp.where(here, table, 0).astype(jnp.float32), axis=(0, 1), keepdims=True) > 0.0
+
+
+def beside_of(span):
+    return span + 1 - 2 * lax.rem(span, 2)
 
 
 def copied(source, target, semaphore):
@@ -111,34 +115,38 @@
             copy.wait()
 
 
-def local_kernel(ranks, part, place, visible, query, key, value, key_beside, value_beside, result, sums, *scratch):
-    here = Facts(place, visible)
+def local_kernel(ranks, part, place, visible, query, key, value, key_beside, value_beside,
+                 result, sums, seen, *scratch):
     query_, key_, value_, key_beside_, value_beside_, semaphores = scratch
-    start, size = parts_of(here.rank, ranks, query.shape[0])[part]
+    start, size = parts_of(place[1], ranks, query.shape[0])[part]
     copies = [
         copied(source, target, semaphores.at[index])
         for index, (source, target) in enumerate((
-            (query.at[pl.ds(start, size)], query_),
+            (visible, seen), (query.at[pl.ds(start, size)], query_),
             (key, key_), (key_beside, key_beside_), (value, value_), (value_beside, value_beside_),
         ))
     ]
-    for copy in copies:
+    for copy in copies[:4]:
         copy.wait()
+
+    def arrive():
+        for copy in copies[4:]:
+            copy.wait()
 
     def write(columns, block):
         result[:, columns] = block
 
-    flags = [None, here.sees(here.span, here.beside)]
-    sums[...] = attend(query_, [key_, key_beside_], [value_, value_beside_], flags, write)
+    flags = [None, seen_by(seen, place[0], beside_of(place[0]))]
+    sums[...] = attend(query_, [key_, key_beside_], [value_, value_beside_], flags, write, arrive)
 
 
 def served_kernel(distance, spans, place, visible, key, value, key_beside, value_beside, *refs):
-    here = Facts(place, visible)
-
-    @pl.when(here.span + distance < spans)
+    span = place[0]
+
+    @pl.when(span + distance < spans)
     def _():
-        asker = jnp.minimum(here.span + distance, spans - 1)
-        flags = [here.sees(asker, here.span), here.sees(asker, here.beside)]
+        asker = jnp.minimum(span + distance, spans - 1)
+        flags = [seen_by(visible, asker, span), seen_by(visible, asker, beside_of(span))]
         *queries, result, query = refs
         at = 0
         for part in queries:
@@ -187,11 +195,9 @@
     ]
 
 
-def fetch_kernel(ranks, place, weight, tiles, semaphores):
-    @pl.when(jnp.logical_or(place[1] == 0, place[1] == ranks - 1))
-    def _():
-        for copy in streamed(weight, 0, tiles, semaphores):
-            copy.wait()
+def fetch_kernel(weight, tiles, semaphores):
+    for copy in streamed(weight, 0, tiles, semaphores):
+        copy.wait()
 
 
 def opening_kernel(ranks, distances, first, place, *refs):
@@ -338,29 +344,33 @@
         size = (block, rows - block)[part]
         return pl.pallas_call(
             functools.partial(local_kernel, ranks, part),
-            in_specs=[SMEM, SMEM, HBM, HBM, HBM, ANY, ANY],
-            out_specs=[VMEM] * 2,
-            out_shape=[jax.ShapeDtypeStruct((size, width), f32), jax.ShapeDtypeStruct((size, LANES), f32)],
+            in_specs=[SMEM, HBM, HBM, HBM, HBM, ANY, ANY],
+            out_specs=[VMEM] * 3,
+            out_shape=[
+                jax.ShapeDtypeStruct((size, width), f32),
+                jax.ShapeDtypeStruct((size, LANES), f32),
+                jax.ShapeDtypeStruct(visible.shape, visible.dtype),
+            ],
             scratch_shapes=[pltpu.VMEM((size, width), bf16)] + [pltpu.VMEM((rows, width), bf16)] * 4
-            + [pltpu.SemaphoreType.DMA((5,))],
+            + [pltpu.SemaphoreType.DMA((6,))],
             compiler_params=PARAMS,
             cost_estimate=taking(4.0),
             name="local",
-        )(place, visible, in_hbm(queries), in_hbm(keys), in_hbm(values), key_beside, value_beside)
+        )(place, in_hbm(visible), in_hbm(queries), in_hbm(keys), in_hbm(values), key_beside, value_beside)
 
     def served(asked, distance):
         return pl.pallas_call(
             functools.partial(served_kernel, distance, spans),
-            in_specs=[SMEM, SMEM] + [VMEM] * (4 + len(asked)),
+            in_specs=[SMEM] + [VMEM] * (5 + len(asked)),
             out_specs=VMEM,
             out_shape=jax.ShapeDtypeStruct((sum(part.shape[0] for part in asked), width + LANES), bf16),
             scratch_shapes=[pltpu.VMEM((sum(part.shape[0] for part in asked), width), bf16)],
             compiler_params=PARAMS,
             cost_estimate=taking(3.3),
             name="served",
-        )(place, visible, keys, values, key_beside, value_beside, *asked)
-
-    early = list(local(0, place))
+        )(place, seen, keys, values, key_beside, value_beside, *asked)
+
+    *early, seen = local(0, place)
     query_late = after(query_late, early)
     asked_early = after(asked_early, early)
     asked_late = [[shifted(query, "span", -distance) for query in query_late] for distance in distances]
@@ -381,15 +391,15 @@
         cost_estimate=taking(3.0),
     )
     fetched = pl.pallas_call(
-        functools.partial(fetch_kernel, ranks),
-        in_specs=[SMEM, HBM],
+        fetch_kernel,
+        in_specs=[HBM],
         out_specs=VMEM,
         out_shape=jax.ShapeDtypeStruct(tile_shape, bf16),
         scratch_shapes=[pltpu.SemaphoreType.DMA((tiles,))],
         compiler_params=PARAMS,
         cost_estimate=taking(2.4),
         name="fetch",
-    )(after(place, out_early), weight)
+    )(in_hbm(after(out_weight, out_early)))
 
     def opening(chunk, place):
         scratch = streaming["scratch_shapes"] if chunk else []
@@ -411,7 +421,7 @@
     for chunk in range(1, chunks):
         sent = opening(chunk, after(place, out_late))
         arrived.append([lax.ppermute(sent, "tensor", ends)])
-    late = list(local(1, after(place, sent)))
+    *late, _ = local(1, after(place, sent))
     late += [shifted(o, "span", d) for o, d in zip(out_late, distances)]
 
     attended_shape = jax.ShapeDtypeStruct((rows, width), bf16)

time: 101 us -> 99.9 us (0.989)
  Pallas kernels: 32.8 us -> 34.3 us
    pallas_call x1, Pallas kernels: 0.59 us -> 2.39 us  [body(): pl.pallas_call(fetch_kernel, in_specs=[HBM], out_specs=VMEM, out_shape=ja...]
    ppermute x5, waiting for transfers between devices: 10.5 us -> 8.81 us  [shifted(): lax.ppermute(block, axis, [(i, i + distance) for i in range(count) if 0 <...]
    ppermute x4, waiting for transfers between devices: 8.26 us -> 9.46 us  [body(): lax.ppermute(up, 'tensor', [(i, i + 1) for i in range(step + 1)])]
  transfers between devices with their start and end apart: 17 -> 17, of which waited for: 8 -> 7; matrix products, arithmetic and copies ran while one was open for 1% -> 1% of each run, Pallas kernels for 32% -> 34%
where the time goes in v19:
time: 99.9 us; the launch traced here: 99 us
  starting transfers between devices  36.8 us (37%)
  Pallas kernels  34.3 us (34%)
  waiting for transfers between devices  25.9 us (26%)
  other arithmetic  1.42 us (1%)
    ppermute x4, starting transfers between devices, body(): lax.ppermute(up, 'tensor', [(i, i + 1) for i in range(step + 1)])  16.9 us
    ppermute x5, starting transfers between devices, shifted(): lax.ppermute(block, axis, [(i, i + distance) for i in range(count) if 0 <...  10.3 us
    pallas_call x3, Pallas kernels, blocks_of(): pl.pallas_call(functools.partial(blocks_kernel, ranks, chunk * columns, s...  10.2 us
    ppermute x4, waiting for transfers between devices, body(): lax.ppermute(up, 'tensor', [(i, i + 1) for i in range(step + 1)])  9.46 us
    ppermute x5, waiting for transfers between devices, shifted(): lax.ppermute(block, axis, [(i, i + distance) for i in range(count) if 0 <...  8.81 us
    ppermute x4, waiting for transfers between devices, body(): lax.ppermute(down, 'tensor', [(last - i, last - i - 1) for i in range(ste...  7.64 us
    pallas_call x2, Pallas kernels, local(): pl.pallas_call(functools.partial(local_kernel, ranks, part), in_specs=[SM...  7.44 us
    ppermute x4, starting transfers between devices, body(): lax.ppermute(down, 'tensor', [(last - i, last - i - 1) for i in range(ste...  6.43 us
  transfers between devices with their start and end apart: 17, of which 7 were waited for; matrix products, arithmetic and copies ran while one was open for 1% of the time, Pallas kernels for 34%

profile of v19, /device:TPU:14, one launch (start us, length us, event | category | flops | bytes accessed | tf_op | source)
XLA Modules:
  0.0 99.0 jit_solution(7355329868485909362)
XLA Ops:
  0.0 0.5 collective-permute-start.1
  0.5 0.1 pad_add_fusion.place
  0.6 1.6 %split.1 = (bf16[96,768]{1,0:T(8,128)(2,1)S(1)}, bf16[192,768]{1,0:T(8,128)(2,1)S(1)}, bf16[96,768]{1,0:T(8,128)(2,1)S(1)}) custom-call(s32[2]{0:T(128)S(1)} %pad_add_fusion.place, bf16[384,768]{1,0:T(8,128)(2,1)} %query.5), custom_call_target="tpu_custom_call" | custom-call | bytes 6273000 | tf_op jit(solution)/shard_map/split/pallas_call | solution.py:324
  2.2 0.0 copy-start
  2.2 0.0 copy-start.1
  2.3 1.5 %collective-permute-start.2 = (bf16[96,768]{1,0:T(8,128)(2,1)S(1)}, bf16[96,768]{1,0:T(8,128)(2,1)S(1)}, u32[]{:S(2)}, u32[]{:S(2)}) collective-permute-start(bf16[96,768]{1,0:T(8,128)(2,1)S(1)} %get-tuple-element.53), channel_id=1, source_target_pairs={{8,0},{12,4},{9,1},{13,5},{10,2},{14,6},{11,3},{15,7},{24,16},{28,... | collective-permute-start | bytes 442376 | tf_op jit(solution)/shard_map/ppermute | solution.py:32
  3.8 3.2 %local.2 = (f32[96,768]{1,0:T(8,128)S(1)}, f32[96,128]{1,0:T(8,128)S(1)}, s32[4,4]{1,0:T(4,128)S(1)}) custom-call(s32[2]{0:T(128)S(1)} %pad_add_fusion.place, s32[4,4]{1,0:T(4,128)} %visible.3, bf16[384,768]{1,0:T(8,128)(2,1)} %query.5, bf16[384,768]{1,0:T(8,128)(2,1)} %key.7, bf16[384,768]{1,0:T(8,128)(2,1)} %value.7, ...), custom_call_target="tpu_custom_call" | custom-call | bytes 14760000 | tf_op jit(solution)/shard_map/local/pallas_call | solution.py:345
  7.0 1.7 %collective-permute-start.4 = (bf16[192,768]{1,0:T(8,128)(2,1)S(1)}, bf16[192,768]{1,0:T(8,128)(2,1)S(1)}, u32[]{:S(2)}, u32[]{:S(2)}) collective-permute-start(bf16[192,768]{1,0:T(8,128)(2,1)S(1)} %get-tuple-element.57), channel_id=1, source_target_pairs={{8,0},{12,4},{9,1},{13,5},{10,2},{14,6},{11,3},{15,7},{24,16},{28,... | collective-permute-start | bytes 884744 | tf_op jit(solution)/shard_map/ppermute | solution.py:32
  8.8 0.6 served.2
  9.3 1.3 %collective-permute-start.3 = (bf16[96,896]{1,0:T(8,128)(2,1)S(1)}, bf16[96,896]{1,0:T(8,128)(2,1)S(1)}, u32[]{:S(2)}, u32[]{:S(2)}) collective-permute-start(bf16[96,896]{1,0:T(8,128)(2,1)S(1)} %served.2), channel_id=1, source_target_pairs={{0,8},{4,12},{1,9},{5,13},{2,10},{6,14},{3,11},{7,15},{16,24},{20,... | collective-permute-start | bytes 516104 | tf_op jit(solution)/shard_map/ppermute | solution.py:32
  10.6 4.6 %collective-permute-start.5 = (bf16[96,768]{1,0:T(8,128)(2,1)S(1)}, bf16[96,768]{1,0:T(8,128)(2,1)S(1)}, u32[]{:S(2)}, u32[]{:S(2)}) collective-permute-start(bf16[96,768]{1,0:T(8,128)(2,1)S(1)} %get-tuple-element.58), channel_id=1, source_target_pairs={{8,0},{12,4},{9,1},{13,5},{10,2},{14,6},{11,3},{15,7},{24,16},{28,... | collective-permute-start | bytes 442376 | tf_op jit(solution)/shard_map/ppermute | solution.py:32
  15.2 2.4 %fetch.1.refs_3_ = bf16[4,768,768]{2,1,0:T(8,128)(2,1)S(1)} custom-call(bf16[768,6144]{1,0:T(8,128)(2,1)} %weight.8), custom_call_target="tpu_custom_call" | custom-call | bytes 8856000 | tf_op jit(solution)/shard_map/fetch/pallas_call | solution.py:393
  17.6 0.6 opening.2
  18.2 1.3 %collective-permute-start.8 = (bf16[96,3072]{1,0:T(8,128)(2,1)S(1)}, bf16[96,3072]{1,0:T(8,128)(2,1)S(1)}, u32[]{:S(2)}, u32[]{:S(2)}) collective-permute-start(bf16[96,3072]{1,0:T(8,128)(2,1)S(1)} %opening.2), channel_id=1, source_target_pairs={{0,1},{3,2},{4,5},{7,6},{8,9},{11,10},{12,13},{15,14},{16,17},{19,... | collective-permute-start | bytes 1769480 | tf_op jit(solution)/shard_map/ppermute | solution.py:419
  19.5 0.6 served.3
  20.0 1.3 %collective-permute-start.6 = (bf16[288,896]{1,0:T(8,128)(2,1)S(1)}, bf16[288,896]{1,0:T(8,128)(2,1)S(1)}, u32[]{:S(2)}, u32[]{:S(2)}) collective-permute-start(bf16[288,896]{1,0:T(8,128)(2,1)S(1)} %served.3), channel_id=1, source_target_pairs={{0,8},{4,12},{1,9},{5,13},{2,10},{6,14},{3,11},{7,15},{16,24},{20,... | collective-permute-start | bytes 1548296 | tf_op jit(solution)/shard_map/ppermute | solution.py:32
  21.3 0.6 opening.3
  21.9 1.3 %collective-permute-start.7 = (bf16[96,3072]{1,0:T(8,128)(2,1)S(1)}, bf16[96,3072]{1,0:T(8,128)(2,1)S(1)}, u32[]{:S(2)}, u32[]{:S(2)}) collective-permute-start(bf16[96,3072]{1,0:T(8,128)(2,1)S(1)} %opening.3), channel_id=1, source_target_pairs={{0,1},{3,2},{4,5},{7,6},{8,9},{11,10},{12,13},{15,14},{16,17},{19,... | collective-permute-start | bytes 1769480 | tf_op jit(solution)/shard_map/ppermute | solution.py:423
  23.2 4.2 %local.3 = (f32[288,768]{1,0:T(8,128)S(1)}, f32[288,128]{1,0:T(8,128)S(1)}, s32[4,4]{1,0:T(4,128)}) custom-call(s32[2]{0:T(128)S(1)} %pad_add_fusion.place, s32[4,4]{1,0:T(4,128)} %visible.3, bf16[384,768]{1,0:T(8,128)(2,1)} %query.5, bf16[384,768]{1,0:T(8,128)(2,1)} %key.7, bf16[384,768]{1,0:T(8,128)(2,1)} %value.7, ...), custom_call_target="tpu_custom_call" | custom-call | bytes 14760000 | tf_op jit(solution)/shard_map/local/pallas_call | solution.py:345
  27.5 8.8 %collective-permute-done.6.refs_5_ = bf16[288,896]{1,0:T(8,128)(2,1)S(1)} collective-permute-done((bf16[288,896]{1,0:T(8,128)(2,1)S(1)}, bf16[288,896]{1,0:T(8,128)(2,1)S(1)}, u32[]{:S(2)}, u32[]{:S(2)}) %collective-permute-start.6) | collective-permute-done | bytes 516128 | tf_op jit(solution)/shard_map/ppermute | solution.py:32
  36.2 4.3 %merged_blocks.1 = (bf16[384,768]{1,0:T(8,128)(2,1)S(1)}, bf16[96,3072]{1,0:T(8,128)(2,1)S(1)}, bf16[96,3072]{1,0:T(8,128)(2,1)S(1)}) custom-call(s32[2]{0:T(128)S(1)} %pad_add_fusion.place, f32[96,768]{1,0:T(8,128)S(1)} %get-tuple-element.50.refs_0_, f32[96,128]{1,0:T(8,128)S(1)} %get-tuple-element.51.refs_1_, ...), custom_call_target="tpu_custom_call" | custom-call | bytes 11070000 | tf_op jit(solution)/shard_map/merged_blocks/pallas_call | solution.py:429
  40.6 0.2 fusion.1
  40.9 1.3 %collective-permute-start.12 = (bf16[96,3072]{1,0:T(8,128)(2,1)S(1)}, bf16[96,3072]{1,0:T(8,128)(2,1)S(1)}, u32[]{:S(2)}, u32[]{:S(2)}) collective-permute-start(bf16[96,3072]{1,0:T(8,128)(2,1)S(1)} %get-tuple-element.97), channel_id=1, source_target_pairs={{3,2},{2,1},{7,6},{6,5},{11,10},{10,9},{15,14},{14,13},{19,18},{18... | collective-permute-start | bytes 1769480 | tf_op jit(solution)/shard_map/ppermute | solution.py:463
  42.2 4.6 %collective-permute-start.11 = (bf16[96,3072]{1,0:T(8,128)(2,1)S(1)}, bf16[96,3072]{1,0:T(8,128)(2,1)S(1)}, u32[]{:S(2)}, u32[]{:S(2)}) collective-permute-start(bf16[96,3072]{1,0:T(8,128)(2,1)S(1)} %get-tuple-element.98), channel_id=1, source_target_pairs={{0,1},{1,2},{4,5},{5,6},{8,9},{9,10},{12,13},{13,14},{16,17},{17,1... | collective-permute-start | bytes 1769480 | tf_op jit(solution)/shard_map/ppermute | solution.py:462
  46.7 3.3 %blocks.3 = (bf16[96,3072]{1,0:T(8,128)(2,1)S(1)}, bf16[96,3072]{1,0:T(8,128)(2,1)S(1)}) custom-call(s32[2]{0:T(128)S(1)} %pad_add_fusion.place, bf16[384,768]{1,0:T(8,128)(2,1)S(1)} %get-tuple-element.92.attended, bf16[768,6144]{1,0:T(8,128)(2,1)} %weight.8), custom_call_target="tpu_custom_call" | custom-call | bytes 11070000 | tf_op jit(solution)/shard_map/blocks/pallas_call | solution.py:439
  50.0 0.2 fusion.3
  50.3 1.3 %collective-permute-start.10 = (bf16[96,3072]{1,0:T(8,128)(2,1)S(1)}, bf16[96,3072]{1,0:T(8,128)(2,1)S(1)}, u32[]{:S(2)}, u32[]{:S(2)}) collective-permute-start(bf16[96,3072]{1,0:T(8,128)(2,1)S(1)} %get-tuple-element.95), channel_id=1, source_target_pairs={{3,2},{2,1},{7,6},{6,5},{11,10},{10,9},{15,14},{14,13},{19,18},{18... | collective-permute-start | bytes 1769480 | tf_op jit(solution)/shard_map/ppermute | solution.py:463
  51.6 4.6 %collective-permute-start.9 = (bf16[96,3072]{1,0:T(8,128)(2,1)S(1)}, bf16[96,3072]{1,0:T(8,128)(2,1)S(1)}, u32[]{:S(2)}, u32[]{:S(2)}) collective-permute-start(bf16[96,3072]{1,0:T(8,128)(2,1)S(1)} %get-tuple-element.96), channel_id=1, source_target_pairs={{0,1},{1,2},{4,5},{5,6},{8,9},{9,10},{12,13},{13,14},{16,17},{17,1... | collective-permute-start | bytes 1769480 | tf_op jit(solution)/shard_map/ppermute | solution.py:462
  56.1 3.4 %blocks.4 = (bf16[96,3072]{1,0:T(8,128)(2,1)S(1)}, bf16[96,3072]{1,0:T(8,128)(2,1)S(1)}) custom-call(s32[2]{0:T(128)S(1)} %pad_add_fusion.place, bf16[384,768]{1,0:T(8,128)(2,1)S(1)} %get-tuple-element.92.attended, bf16[768,6144]{1,0:T(8,128)(2,1)} %weight.8), custom_call_target="tpu_custom_call" | custom-call | bytes 11070000 | tf_op jit(solution)/shard_map/blocks/pallas_call | solution.py:439
  59.6 2.0 %collective-permute-done.11 = bf16[96,3072]{1,0:T(8,128)(2,1)S(1)} collective-permute-done((bf16[96,3072]{1,0:T(8,128)(2,1)S(1)}, bf16[96,3072]{1,0:T(8,128)(2,1)S(1)}, u32[]{:S(2)}, u32[]{:S(2)}) %collective-permute-start.11) | collective-permute-done | bytes 589856 | tf_op jit(solution)/shard_map/ppermute | solution.py:462
  61.6 0.2 add_convert_fusion.2
  61.8 1.9 %collective-permute-start.14 = (bf16[96,3072]{1,0:T(8,128)(2,1)S(1)}, bf16[96,3072]{1,0:T(8,128)(2,1)S(1)}, u32[]{:S(2)}, u32[]{:S(2)}) collective-permute-start(bf16[96,3072]{1,0:T(8,128)(2,1)S(1)} %add_convert_fusion.2), channel_id=1, source_target_pairs={{3,2},{2,1},{1,0},{7,6},{6,5},{5,4},{11,10},{10,9},{9,8},{15,14},{... | collective-permute-start | bytes 1769480 | tf_op jit(solution)/shard_map/ppermute | solution.py:463
  63.7 0.1 add_convert_fusion.3
  63.8 3.9 %collective-permute-start.13 = (bf16[96,3072]{1,0:T(8,128)(2,1)S(1)}, bf16[96,3072]{1,0:T(8,128)(2,1)S(1)}, u32[]{:S(2)}, u32[]{:S(2)}) collective-permute-start(bf16[96,3072]{1,0:T(8,128)(2,1)S(1)} %add_convert_fusion.3), channel_id=1, source_target_pairs={{0,1},{1,2},{2,3},{4,5},{5,6},{6,7},{8,9},{9,10},{10,11},{12,13},{... | collective-permute-start | bytes 1769480 | tf_op jit(solution)/shard_map/ppermute | solution.py:462
  67.8 3.4 %blocks.5 = (bf16[96,3072]{1,0:T(8,128)(2,1)S(1)}, bf16[96,3072]{1,0:T(8,128)(2,1)S(1)}) custom-call(s32[2]{0:T(128)S(1)} %pad_add_fusion.place, bf16[384,768]{1,0:T(8,128)(2,1)S(1)} %get-tuple-element.92.attended, bf16[768,6144]{1,0:T(8,128)(2,1)} %weight.8), custom_call_target="tpu_custom_call" | custom-call | bytes 11070000 | tf_op jit(solution)/shard_map/blocks/pallas_call | solution.py:439
  71.2 0.4 collective-permute-done.10
  71.7 2.6 %collective-permute-done.9 = bf16[96,3072]{1,0:T(8,128)(2,1)S(1)} collective-permute-done((bf16[96,3072]{1,0:T(8,128)(2,1)S(1)}, bf16[96,3072]{1,0:T(8,128)(2,1)S(1)}, u32[]{:S(2)}, u32[]{:S(2)}) %collective-permute-start.9) | collective-permute-done | bytes 589856 | tf_op jit(solution)/shard_map/ppermute | solution.py:462
  74.2 0.1 add_convert_fusion
  74.4 0.0 copy-start.2
  74.4 1.9 %collective-permute-start.16 = (bf16[96,3072]{1,0:T(8,128)(2,1)S(1)}, bf16[96,3072]{1,0:T(8,128)(2,1)S(1)}, u32[]{:S(2)}, u32[]{:S(2)}) collective-permute-start(bf16[96,3072]{1,0:T(8,128)(2,1)S(1)} %add_convert_fusion), channel_id=1, source_target_pairs={{3,2},{2,1},{1,0},{7,6},{6,5},{5,4},{11,10},{10,9},{9,8},{15,14},{... | collective-permute-start | bytes 1769480 | tf_op jit(solution)/shard_map/ppermute | solution.py:463
  76.3 0.1 add_convert_fusion.1
  76.5 3.9 %collective-permute-start.15 = (bf16[96,3072]{1,0:T(8,128)(2,1)S(1)}, bf16[96,3072]{1,0:T(8,128)(2,1)S(1)}, u32[]{:S(2)}, u32[]{:S(2)}) collective-permute-start(bf16[96,3072]{1,0:T(8,128)(2,1)S(1)} %add_convert_fusion.1), channel_id=1, source_target_pairs={{0,1},{1,2},{2,3},{4,5},{5,6},{6,7},{8,9},{9,10},{10,11},{12,13},{... | collective-permute-start | bytes 1769480 | tf_op jit(solution)/shard_map/ppermute | solution.py:462
  80.4 5.0 %own.1 = (bf16[96,6144]{1,0:T(8,128)(2,1)S(1)}, f32[1,6144]{1,0:T(1,128)S(1)}) custom-call(s32[2]{0:T(128)S(1)} %pad_add_fusion.place, s32[4]{0:T(128)S(1)} %copy-done.2, bf16[384,768]{1,0:T(8,128)(2,1)S(1)} %get-tuple-element.92.attended, bf16[768,6144]{1,0:T(8,128)(2,1)} %weight.8, f32[64,6144]{1,0:T(8,128)} %gate_table.1), custom_call_target="tpu_custom_call" | custom-call | bytes 18450000 | tf_op jit(solution)/shard_map/own/pallas_call | solution.py:466
  85.5 1.4 %collective-permute-done.13 = bf16[96,3072]{1,0:T(8,128)(2,1)S(1)} collective-permute-done((bf16[96,3072]{1,0:T(8,128)(2,1)S(1)}, bf16[96,3072]{1,0:T(8,128)(2,1)S(1)}, u32[]{:S(2)}, u32[]{:S(2)}) %collective-permute-start.13) | collective-permute-done | bytes 589856 | tf_op jit(solution)/shard_map/ppermute | solution.py:462
  86.9 0.3 multiply_convert_fusion.done
  87.1 7.2 %collective-permute-done.16.down = bf16[96,3072]{1,0:T(8,128)(2,1)S(1)} collective-permute-done((bf16[96,3072]{1,0:T(8,128)(2,1)S(1)}, bf16[96,3072]{1,0:T(8,128)(2,1)S(1)}, u32[]{:S(2)}, u32[]{:S(2)}) %collective-permute-start.16) | collective-permute-done | bytes 589856 | tf_op jit(solution)/shard_map/ppermute | solution.py:463
  94.3 3.4 %collective-permute-done.15.up = bf16[96,3072]{1,0:T(8,128)(2,1)S(1)} collective-permute-done((bf16[96,3072]{1,0:T(8,128)(2,1)S(1)}, bf16[96,3072]{1,0:T(8,128)(2,1)S(1)}, u32[]{:S(2)}, u32[]{:S(2)}) %collective-permute-start.15) | collective-permute-done | bytes 589856 | tf_op jit(solution)/shard_map/ppermute | solution.py:462
  97.8 1.1 %final.1 = bf16[96,6144]{1,0:T(8,128)(2,1)} custom-call(bf16[96,3072]{1,0:T(8,128)(2,1)S(1)} %multiply_convert_fusion.done, bf16[96,6144]{1,0:T(8,128)(2,1)S(1)} %get-tuple-element.93.projected, f32[1,6144]{1,0:T(1,128)S(1)} %get-tuple-element.94.gate, bf16[96,3072]{1,0:T(8,128)(2,1)S(1)} %collective-permute-done.15.up, ...), custom_call_target="tpu_custom_call" | custom-call | bytes 9963000 | tf_op jit(solution)/shard_map/final/pallas_call | solution.py:487
  (15 shorter events, 0.0 us)
Async XLA Ops:
  0.0 3.8 %collective-permute-start = (bf16[384,768]{1,0:T(8,128)(2,1)}, bf16[384,768]{1,0:T(8,128)(2,1)S(1)}, u32[]{:S(2)}, u32[]{:S(2)}) collective-permute-start(bf16[384,768]{1,0:T(8,128)(2,1)} %key.7), channel_id=1, source_target_pairs={{0,4},{4,0},{8,12},{12,8},{1,5},{5,1},{9,13},{13,9},{2,6},{6,2},{1... | collective-permute-start | bytes 1769480 | tf_op jit(solution)/shard_map/ppermute | solution.py:337
  0.0 3.8 %collective-permute-start.1 = (bf16[384,768]{1,0:T(8,128)(2,1)}, bf16[384,768]{1,0:T(8,128)(2,1)S(1)}, u32[]{:S(2)}, u32[]{:S(2)}) collective-permute-start(bf16[384,768]{1,0:T(8,128)(2,1)} %value.7), channel_id=1, source_target_pairs={{0,4},{4,0},{8,12},{12,8},{1,5},{5,1},{9,13},{13,9},{2,6},{6,2},{1... | collective-permute-start | bytes 1769480 | tf_op jit(solution)/shard_map/ppermute | solution.py:338
  2.2 6.5 %copy-start = (bf16[384,768]{1,0:T(8,128)(2,1)S(1)}, bf16[384,768]{1,0:T(8,128)(2,1)}, u32[]{:S(2)}) copy-start(bf16[384,768]{1,0:T(8,128)(2,1)} %key.7) | copy-start | bytes 1769476
  2.2 6.5 %copy-start.1 = (bf16[384,768]{1,0:T(8,128)(2,1)S(1)}, bf16[384,768]{1,0:T(8,128)(2,1)}, u32[]{:S(2)}) copy-start(bf16[384,768]{1,0:T(8,128)(2,1)} %value.7) | copy-start | bytes 1769476
  2.3 6.5 %collective-permute-start.2 = (bf16[96,768]{1,0:T(8,128)(2,1)S(1)}, bf16[96,768]{1,0:T(8,128)(2,1)S(1)}, u32[]{:S(2)}, u32[]{:S(2)}) collective-permute-start(bf16[96,768]{1,0:T(8,128)(2,1)S(1)} %get-tuple-element.53), channel_id=1, source_target_pairs={{8,0},{12,4},{9,1},{13,5},{10,2},{14,6},{11,3},{15,7},{24,16},{28,... | collective-permute-start | bytes 442376 | tf_op jit(solution)/shard_map/ppermute | solution.py:32
  7.0 12.5 %collective-permute-start.4 = (bf16[192,768]{1,0:T(8,128)(2,1)S(1)}, bf16[192,768]{1,0:T(8,128)(2,1)S(1)}, u32[]{:S(2)}, u32[]{:S(2)}) collective-permute-start(bf16[192,768]{1,0:T(8,128)(2,1)S(1)} %get-tuple-element.57), channel_id=1, source_target_pairs={{8,0},{12,4},{9,1},{13,5},{10,2},{14,6},{11,3},{15,7},{24,16},{28,... | collective-permute-start | bytes 884744 | tf_op jit(solution)/shard_map/ppermute | solution.py:32
  9.3 8.3 %collective-permute-start.3 = (bf16[96,896]{1,0:T(8,128)(2,1)S(1)}, bf16[96,896]{1,0:T(8,128)(2,1)S(1)}, u32[]{:S(2)}, u32[]{:S(2)}) collective-permute-start(bf16[96,896]{1,0:T(8,128)(2,1)S(1)} %served.2), channel_id=1, source_target_pairs={{0,8},{4,12},{1,9},{5,13},{2,10},{6,14},{3,11},{7,15},{16,24},{20,... | collective-permute-start | bytes 516104 | tf_op jit(solution)/shard_map/ppermute | solution.py:32
  10.6 8.8 %collective-permute-start.5 = (bf16[96,768]{1,0:T(8,128)(2,1)S(1)}, bf16[96,768]{1,0:T(8,128)(2,1)S(1)}, u32[]{:S(2)}, u32[]{:S(2)}) collective-permute-start(bf16[96,768]{1,0:T(8,128)(2,1)S(1)} %get-tuple-element.58), channel_id=1, source_target_pairs={{8,0},{12,4},{9,1},{13,5},{10,2},{14,6},{11,3},{15,7},{24,16},{28,... | collective-permute-start | bytes 442376 | tf_op jit(solution)/shard_map/ppermute | solution.py:32
  18.2 22.4 %collective-permute-start.8 = (bf16[96,3072]{1,0:T(8,128)(2,1)S(1)}, bf16[96,3072]{1,0:T(8,128)(2,1)S(1)}, u32[]{:S(2)}, u32[]{:S(2)}) collective-permute-start(bf16[96,3072]{1,0:T(8,128)(2,1)S(1)} %opening.2), channel_id=1, source_target_pairs={{0,1},{3,2},{4,5},{7,6},{8,9},{11,10},{12,13},{15,14},{16,17},{19,... | collective-permute-start | bytes 1769480 | tf_op jit(solution)/shard_map/ppermute | solution.py:419
  20.0 16.2 %collective-permute-start.6 = (bf16[288,896]{1,0:T(8,128)(2,1)S(1)}, bf16[288,896]{1,0:T(8,128)(2,1)S(1)}, u32[]{:S(2)}, u32[]{:S(2)}) collective-permute-start(bf16[288,896]{1,0:T(8,128)(2,1)S(1)} %served.3), channel_id=1, source_target_pairs={{0,8},{4,12},{1,9},{5,13},{2,10},{6,14},{3,11},{7,15},{16,24},{20,... | collective-permute-start | bytes 1548296 | tf_op jit(solution)/shard_map/ppermute | solution.py:32
  21.9 28.1 %collective-permute-start.7 = (bf16[96,3072]{1,0:T(8,128)(2,1)S(1)}, bf16[96,3072]{1,0:T(8,128)(2,1)S(1)}, u32[]{:S(2)}, u32[]{:S(2)}) collective-permute-start(bf16[96,3072]{1,0:T(8,128)(2,1)S(1)} %opening.3), channel_id=1, source_target_pairs={{0,1},{3,2},{4,5},{7,6},{8,9},{11,10},{12,13},{15,14},{16,17},{19,... | collective-permute-start | bytes 1769480 | tf_op jit(solution)/shard_map/ppermute | solution.py:423
  40.9 18.7 %collective-permute-start.12 = (bf16[96,3072]{1,0:T(8,128)(2,1)S(1)}, bf16[96,3072]{1,0:T(8,128)(2,1)S(1)}, u32[]{:S(2)}, u32[]{:S(2)}) collective-permute-start(bf16[96,3072]{1,0:T(8,128)(2,1)S(1)} %get-tuple-element.97), channel_id=1, source_target_pairs={{3,2},{2,1},{7,6},{6,5},{11,10},{10,9},{15,14},{14,13},{19,18},{18... | collective-permute-start | bytes 1769480 | tf_op jit(solution)/shard_map/ppermute | solution.py:463
  42.2 19.4 %collective-permute-start.11 = (bf16[96,3072]{1,0:T(8,128)(2,1)S(1)}, bf16[96,3072]{1,0:T(8,128)(2,1)S(1)}, u32[]{:S(2)}, u32[]{:S(2)}) collective-permute-start(bf16[96,3072]{1,0:T(8,128)(2,1)S(1)} %get-tuple-element.98), channel_id=1, source_target_pairs={{0,1},{1,2},{4,5},{5,6},{8,9},{9,10},{12,13},{13,14},{16,17},{17,1... | collective-permute-start | bytes 1769480 | tf_op jit(solution)/shard_map/ppermute | solution.py:462
  50.3 21.4 %collective-permute-start.10 = (bf16[96,3072]{1,0:T(8,128)(2,1)S(1)}, bf16[96,3072]{1,0:T(8,128)(2,1)S(1)}, u32[]{:S(2)}, u32[]{:S(2)}) collective-permute-start(bf16[96,3072]{1,0:T(8,128)(2,1)S(1)} %get-tuple-element.95), channel_id=1, source_target_pairs={{3,2},{2,1},{7,6},{6,5},{11,10},{10,9},{15,14},{14,13},{19,18},{18... | collective-permute-start | bytes 1769480 | tf_op jit(solution)/shard_map/ppermute | solution.py:463
  51.6 22.7 %collective-permute-start.9 = (bf16[96,3072]{1,0:T(8,128)(2,1)S(1)}, bf16[96,3072]{1,0:T(8,128)(2,1)S(1)}, u32[]{:S(2)}, u32[]{:S(2)}) collective-permute-start(bf16[96,3072]{1,0:T(8,128)(2,1)S(1)} %get-tuple-element.96), channel_id=1, source_target_pairs={{0,1},{1,2},{4,5},{5,6},{8,9},{9,10},{12,13},{13,14},{16,17},{17,1... | collective-permute-start | bytes 1769480 | tf_op jit(solution)/shard_map/ppermute | solution.py:462
  61.8 23.7 %collective-permute-start.14 = (bf16[96,3072]{1,0:T(8,128)(2,1)S(1)}, bf16[96,3072]{1,0:T(8,128)(2,1)S(1)}, u32[]{:S(2)}, u32[]{:S(2)}) collective-permute-start(bf16[96,3072]{1,0:T(8,128)(2,1)S(1)} %add_convert_fusion.2), channel_id=1, source_target_pairs={{3,2},{2,1},{1,0},{7,6},{6,5},{5,4},{11,10},{10,9},{9,8},{15,14},{... | collective-permute-start | bytes 1769480 | tf_op jit(solution)/shard_map/ppermute | solution.py:463
  63.8 23.0 %collective-permute-start.13 = (bf16[96,3072]{1,0:T(8,128)(2,1)S(1)}, bf16[96,3072]{1,0:T(8,128)(2,1)S(1)}, u32[]{:S(2)}, u32[]{:S(2)}) collective-permute-start(bf16[96,3072]{1,0:T(8,128)(2,1)S(1)} %add_convert_fusion.3), channel_id=1, source_target_pairs={{0,1},{1,2},{2,3},{4,5},{5,6},{6,7},{8,9},{9,10},{10,11},{12,13},{... | collective-permute-start | bytes 1769480 | tf_op jit(solution)/shard_map/ppermute | solution.py:462
  74.4 6.0 %copy-start.2 = (s32[4]{0:T(128)S(1)}, s32[4]{0:T(128)}, u32[]{:S(2)}) copy-start(s32[4]{0:T(128)} %levels.1) | copy-start | bytes 52
  74.4 19.9 %collective-permute-start.16 = (bf16[96,3072]{1,0:T(8,128)(2,1)S(1)}, bf16[96,3072]{1,0:T(8,128)(2,1)S(1)}, u32[]{:S(2)}, u32[]{:S(2)}) collective-permute-start(bf16[96,3072]{1,0:T(8,128)(2,1)S(1)} %add_convert_fusion), channel_id=1, source_target_pairs={{3,2},{2,1},{1,0},{7,6},{6,5},{5,4},{11,10},{10,9},{9,8},{15,14},{... | collective-permute-start | bytes 1769480 | tf_op jit(solution)/shard_map/ppermute | solution.py:463
  76.5 21.3 %collective-permute-start.15 = (bf16[96,3072]{1,0:T(8,128)(2,1)S(1)}, bf16[96,3072]{1,0:T(8,128)(2,1)S(1)}, u32[]{:S(2)}, u32[]{:S(2)}) collective-permute-start(bf16[96,3072]{1,0:T(8,128)(2,1)S(1)} %add_convert_fusion.1), channel_id=1, source_target_pairs={{0,1},{1,2},{2,3},{4,5},{5,6},{6,7},{8,9},{9,10},{10,11},{12,13},{... | collective-permute-start | bytes 1769480 | tf_op jit(solution)/shard_map/ppermute | solution.py:462

commit v20 on v19

--- a/solution.py
+++ b/solution.py
@@ -195,9 +195,13 @@
     ]
 
 
-def fetch_kernel(weight, tiles, semaphores):
-    for copy in streamed(weight, 0, tiles, semaphores):
-        copy.wait()
+def fetch_kernel(askers, place, weight, *refs):
+    tiles, semaphores = refs[-2:]
+
+    @pl.when(place[0] > 1 if askers else place[0] < 2)
+    def _():
+        for copy in streamed(weight, 0, tiles, semaphores):
+            copy.wait()
 
 
 def opening_kernel(ranks, distances, first, place, *refs):
@@ -373,10 +377,6 @@
     *early, seen = local(0, place)
     query_late = after(query_late, early)
     asked_early = after(asked_early, early)
-    asked_late = [[shifted(query, "span", -distance) for query in query_late] for distance in distances]
-    out_early = [served([q], d) for q, d in zip(asked_early, distances)]
-    early += [shifted(o, "span", d) for o, d in zip(out_early, distances)]
-
     chunks = 2
     columns = model // chunks
     tiles = 4
@@ -390,16 +390,26 @@
         compiler_params=PARAMS,
         cost_estimate=taking(3.0),
     )
-    fetched = pl.pallas_call(
-        fetch_kernel,
-        in_specs=[HBM],
-        out_specs=VMEM,
-        out_shape=jax.ShapeDtypeStruct(tile_shape, bf16),
-        scratch_shapes=[pltpu.SemaphoreType.DMA((tiles,))],
-        compiler_params=PARAMS,
-        cost_estimate=taking(2.4),
-        name="fetch",
-    )(in_hbm(after(out_weight, out_early)))
+
+    def fetch(askers, place, *before):
+        return pl.pallas_call(
+            functools.partial(fetch_kernel, askers),
+            in_specs=[SMEM, HBM] + [VMEM] * len(before),
+            out_specs=VMEM,
+            out_shape=jax.ShapeDtypeStruct(tile_shape, bf16),
+            input_output_aliases={2: 0} if before else {},
+            scratch_shapes=[pltpu.SemaphoreType.DMA((tiles,))],
+            compiler_params=PARAMS,
+            cost_estimate=taking(2.4),
+            name="fetch",
+        )(place, weight, *before)
+
+    out_early = [served([q], d) for q, d in zip(asked_early, distances)]
+    early += [shifted(o, "span", d) for o, d in zip(out_early, distances)]
+    fetched = fetch(True, after(place, out_early))
+    query_late = [query_late[0], after(query_late[1], fetched)]
+    asked_late = [[shifted(query, "span", -distance) for query in query_late] for distance in distances]
+    fetched = fetch(False, place, fetched)
 
     def opening(chunk, place):
         scratch = streaming["scratch_shapes"] if chunk else []

time: 99.9 us -> 100 us (level)
  starting transfers between devices: 36.8 us -> 34.5 us
  Pallas kernels: 34.3 us -> 35.4 us
    ppermute x5, starting transfers between devices: 10.3 us -> 7.99 us  [shifted(): lax.ppermute(block, axis, [(i, i + distance) for i in range(count) if 0 <...]
    pallas_call x1 -> x2, Pallas kernels: 2.39 us -> 3.52 us  [fetch(): pl.pallas_call(functools.partial(fetch_kernel, askers), in_specs=[SMEM, H...]
  transfers between devices with their start and end apart: 17 -> 17, of which waited for: 7 -> 8; matrix products, arithmetic and copies ran while one was open for 1% -> 1% of each run, Pallas kernels for 34% -> 35%
where the time goes in v20:
time: 100 us; the launch traced here: 98.5 us
  Pallas kernels  35.4 us (35%)
  starting transfers between devices  34.5 us (34%)
  waiting for transfers between devices  26.6 us (27%)
  other arithmetic  1.42 us (1%)
    ppermute x4, starting transfers between devices, body(): lax.ppermute(up, 'tensor', [(i, i + 1) for i in range(step + 1)])  16.9 us
    pallas_call x3, Pallas kernels, blocks_of(): pl.pallas_call(functools.partial(blocks_kernel, ranks, chunk * columns, s...  10.2 us
    ppermute x5, waiting for transfers between devices, shifted(): lax.ppermute(block, axis, [(i, i + distance) for i in range(count) if 0 <...  9.78 us
    ppermute x4, waiting for transfers between devices, body(): lax.ppermute(up, 'tensor', [(i, i + 1) for i in range(step + 1)])  9.53 us
    ppermute x5, starting transfers between devices, shifted(): lax.ppermute(block, axis, [(i, i + distance) for i in range(count) if 0 <...  7.99 us
    pallas_call x2, Pallas kernels, local(): pl.pallas_call(functools.partial(local_kernel, ranks, part), in_specs=[SM...  7.44 us
    ppermute x4, waiting for transfers between devices, body(): lax.ppermute(down, 'tensor', [(last - i, last - i - 1) for i in range(ste...  7.26 us
    ppermute x4, starting transfers between devices, body(): lax.ppermute(down, 'tensor', [(last - i, last - i - 1) for i in range(ste...  6.43 us
  transfers between devices with their start and end apart: 17, of which 8 were waited for; matrix products, arithmetic and copies ran while one was open for 1% of the time, Pallas kernels for 35%

profile of v20, /device:TPU:14, one launch (start us, length us, event | category | flops | bytes accessed | tf_op | source)
XLA Modules:
  0.0 98.5 jit_solution(9983918643831964579)
XLA Ops:
  0.0 0.5 collective-permute-start.1
  0.5 0.1 pad_add_fusion.place
  0.6 1.6 %split.1 = (bf16[96,768]{1,0:T(8,128)(2,1)S(1)}, bf16[192,768]{1,0:T(8,128)(2,1)S(1)}, bf16[96,768]{1,0:T(8,128)(2,1)S(1)}) custom-call(s32[2]{0:T(128)S(1)} %pad_add_fusion.place, bf16[384,768]{1,0:T(8,128)(2,1)} %query.5), custom_call_target="tpu_custom_call" | custom-call | bytes 6273000 | tf_op jit(solution)/shard_map/split/pallas_call | solution.py:328
  2.2 0.0 copy-start
  2.3 1.5 %collective-permute-start.2 = (bf16[96,768]{1,0:T(8,128)(2,1)S(1)}, bf16[96,768]{1,0:T(8,128)(2,1)S(1)}, u32[]{:S(2)}, u32[]{:S(2)}) collective-permute-start(bf16[96,768]{1,0:T(8,128)(2,1)S(1)} %get-tuple-element.54), channel_id=1, source_target_pairs={{8,0},{12,4},{9,1},{13,5},{10,2},{14,6},{11,3},{15,7},{24,16},{28,... | collective-permute-start | bytes 442376 | tf_op jit(solution)/shard_map/ppermute | solution.py:32
  3.8 3.2 %local.2 = (f32[96,768]{1,0:T(8,128)S(1)}, f32[96,128]{1,0:T(8,128)S(1)}, s32[4,4]{1,0:T(4,128)S(1)}) custom-call(s32[2]{0:T(128)S(1)} %pad_add_fusion.place, s32[4,4]{1,0:T(4,128)} %visible.3, bf16[384,768]{1,0:T(8,128)(2,1)} %query.5, bf16[384,768]{1,0:T(8,128)(2,1)} %key.7, bf16[384,768]{1,0:T(8,128)(2,1)} %value.7, ...), custom_call_target="tpu_custom_call" | custom-call | bytes 14760000 | tf_op jit(solution)/shard_map/local/pallas_call | solution.py:349
  7.0 1.7 %collective-permute-start.4 = (bf16[192,768]{1,0:T(8,128)(2,1)S(1)}, bf16[192,768]{1,0:T(8,128)(2,1)S(1)}, u32[]{:S(2)}, u32[]{:S(2)}) collective-permute-start(bf16[192,768]{1,0:T(8,128)(2,1)S(1)} %get-tuple-element.58), channel_id=1, source_target_pairs={{8,0},{12,4},{9,1},{13,5},{10,2},{14,6},{11,3},{15,7},{24,16},{28,... | collective-permute-start | bytes 884744 | tf_op jit(solution)/shard_map/ppermute | solution.py:32
  8.8 0.6 served.2
  9.3 1.3 %collective-permute-start.3 = (bf16[96,896]{1,0:T(8,128)(2,1)S(1)}, bf16[96,896]{1,0:T(8,128)(2,1)S(1)}, u32[]{:S(2)}, u32[]{:S(2)}) collective-permute-start(bf16[96,896]{1,0:T(8,128)(2,1)S(1)} %served.2), channel_id=1, source_target_pairs={{0,8},{4,12},{1,9},{5,13},{2,10},{6,14},{3,11},{7,15},{16,24},{20,... | collective-permute-start | bytes 516104 | tf_op jit(solution)/shard_map/ppermute | solution.py:32
  10.6 2.9 %fetch.2.refs_0_ = bf16[4,768,768]{2,1,0:T(8,128)(2,1)S(1)} custom-call(s32[2]{0:T(128)S(1)} %pad_add_fusion.place, bf16[768,6144]{1,0:T(8,128)(2,1)} %weight.11), custom_call_target="tpu_custom_call" | custom-call | bytes 8856000 | tf_op jit(solution)/shard_map/fetch/pallas_call | solution.py:395
  13.6 2.2 %collective-permute-start.5 = (bf16[96,768]{1,0:T(8,128)(2,1)S(1)}, bf16[96,768]{1,0:T(8,128)(2,1)S(1)}, u32[]{:S(2)}, u32[]{:S(2)}) collective-permute-start(bf16[96,768]{1,0:T(8,128)(2,1)S(1)} %get-tuple-element.61), channel_id=1, source_target_pairs={{8,0},{12,4},{9,1},{13,5},{10,2},{14,6},{11,3},{15,7},{24,16},{28,... | collective-permute-start | bytes 442376 | tf_op jit(solution)/shard_map/ppermute | solution.py:32
  15.8 0.6 fetch.3.refs_3_
  16.4 1.0 collective-permute-done.3.refs_2_
  17.4 0.5 opening.2
  17.9 1.3 %collective-permute-start.8 = (bf16[96,3072]{1,0:T(8,128)(2,1)S(1)}, bf16[96,3072]{1,0:T(8,128)(2,1)S(1)}, u32[]{:S(2)}, u32[]{:S(2)}) collective-permute-start(bf16[96,3072]{1,0:T(8,128)(2,1)S(1)} %opening.2), channel_id=1, source_target_pairs={{0,1},{3,2},{4,5},{7,6},{8,9},{11,10},{12,13},{15,14},{16,17},{19,... | collective-permute-start | bytes 1769480 | tf_op jit(solution)/shard_map/ppermute | solution.py:429
  19.2 0.6 served.3
  19.8 1.3 %collective-permute-start.6 = (bf16[288,896]{1,0:T(8,128)(2,1)S(1)}, bf16[288,896]{1,0:T(8,128)(2,1)S(1)}, u32[]{:S(2)}, u32[]{:S(2)}) collective-permute-start(bf16[288,896]{1,0:T(8,128)(2,1)S(1)} %served.3), channel_id=1, source_target_pairs={{0,8},{4,12},{1,9},{5,13},{2,10},{6,14},{3,11},{7,15},{16,24},{20,... | collective-permute-start | bytes 1548296 | tf_op jit(solution)/shard_map/ppermute | solution.py:32
  21.1 0.6 opening.3
  21.7 1.3 %collective-permute-start.7 = (bf16[96,3072]{1,0:T(8,128)(2,1)S(1)}, bf16[96,3072]{1,0:T(8,128)(2,1)S(1)}, u32[]{:S(2)}, u32[]{:S(2)}) collective-permute-start(bf16[96,3072]{1,0:T(8,128)(2,1)S(1)} %opening.3), channel_id=1, source_target_pairs={{0,1},{3,2},{4,5},{7,6},{8,9},{11,10},{12,13},{15,14},{16,17},{19,... | collective-permute-start | bytes 1769480 | tf_op jit(solution)/shard_map/ppermute | solution.py:433
  23.0 4.2 %local.3 = (f32[288,768]{1,0:T(8,128)S(1)}, f32[288,128]{1,0:T(8,128)S(1)}, s32[4,4]{1,0:T(4,128)}) custom-call(s32[2]{0:T(128)S(1)} %pad_add_fusion.place, s32[4,4]{1,0:T(4,128)} %visible.3, bf16[384,768]{1,0:T(8,128)(2,1)} %query.5, bf16[384,768]{1,0:T(8,128)(2,1)} %key.7, bf16[384,768]{1,0:T(8,128)(2,1)} %value.7, ...), custom_call_target="tpu_custom_call" | custom-call | bytes 14760000 | tf_op jit(solution)/shard_map/local/pallas_call | solution.py:349
  27.2 8.8 %collective-permute-done.6.refs_5_ = bf16[288,896]{1,0:T(8,128)(2,1)S(1)} collective-permute-done((bf16[288,896]{1,0:T(8,128)(2,1)S(1)}, bf16[288,896]{1,0:T(8,128)(2,1)S(1)}, u32[]{:S(2)}, u32[]{:S(2)}) %collective-permute-start.6) | collective-permute-done | bytes 516128 | tf_op jit(solution)/shard_map/ppermute | solution.py:32
  36.0 4.3 %merged_blocks.1 = (bf16[384,768]{1,0:T(8,128)(2,1)S(1)}, bf16[96,3072]{1,0:T(8,128)(2,1)S(1)}, bf16[96,3072]{1,0:T(8,128)(2,1)S(1)}) custom-call(s32[2]{0:T(128)S(1)} %pad_add_fusion.place, f32[96,768]{1,0:T(8,128)S(1)} %get-tuple-element.51.refs_0_, f32[96,128]{1,0:T(8,128)S(1)} %get-tuple-element.52.refs_1_, ...), custom_call_target="tpu_custom_call" | custom-call | bytes 11070000 | tf_op jit(solution)/shard_map/merged_blocks/pallas_call | solution.py:439
  40.4 0.3 fusion.1
  40.6 1.3 %collective-permute-start.12 = (bf16[96,3072]{1,0:T(8,128)(2,1)S(1)}, bf16[96,3072]{1,0:T(8,128)(2,1)S(1)}, u32[]{:S(2)}, u32[]{:S(2)}) collective-permute-start(bf16[96,3072]{1,0:T(8,128)(2,1)S(1)} %get-tuple-element.99), channel_id=1, source_target_pairs={{3,2},{2,1},{7,6},{6,5},{11,10},{10,9},{15,14},{14,13},{19,18},{18... | collective-permute-start | bytes 1769480 | tf_op jit(solution)/shard_map/ppermute | solution.py:473
  41.9 4.6 %collective-permute-start.11 = (bf16[96,3072]{1,0:T(8,128)(2,1)S(1)}, bf16[96,3072]{1,0:T(8,128)(2,1)S(1)}, u32[]{:S(2)}, u32[]{:S(2)}) collective-permute-start(bf16[96,3072]{1,0:T(8,128)(2,1)S(1)} %get-tuple-element.100), channel_id=1, source_target_pairs={{0,1},{1,2},{4,5},{5,6},{8,9},{9,10},{12,13},{13,14},{16,17},{17,1... | collective-permute-start | bytes 1769480 | tf_op jit(solution)/shard_map/ppermute | solution.py:472
  46.5 3.3 %blocks.3 = (bf16[96,3072]{1,0:T(8,128)(2,1)S(1)}, bf16[96,3072]{1,0:T(8,128)(2,1)S(1)}) custom-call(s32[2]{0:T(128)S(1)} %pad_add_fusion.place, bf16[384,768]{1,0:T(8,128)(2,1)S(1)} %get-tuple-element.94.attended, bf16[768,6144]{1,0:T(8,128)(2,1)} %weight.11), custom_call_target="tpu_custom_call" | custom-call | bytes 11070000 | tf_op jit(solution)/shard_map/blocks/pallas_call | solution.py:449
  49.8 0.2 fusion.3
  50.0 1.3 %collective-permute-start.10 = (bf16[96,3072]{1,0:T(8,128)(2,1)S(1)}, bf16[96,3072]{1,0:T(8,128)(2,1)S(1)}, u32[]{:S(2)}, u32[]{:S(2)}) collective-permute-start(bf16[96,3072]{1,0:T(8,128)(2,1)S(1)} %get-tuple-element.97), channel_id=1, source_target_pairs={{3,2},{2,1},{7,6},{6,5},{11,10},{10,9},{15,14},{14,13},{19,18},{18... | collective-permute-start | bytes 1769480 | tf_op jit(solution)/shard_map/ppermute | solution.py:473
  51.3 4.6 %collective-permute-start.9 = (bf16[96,3072]{1,0:T(8,128)(2,1)S(1)}, bf16[96,3072]{1,0:T(8,128)(2,1)S(1)}, u32[]{:S(2)}, u32[]{:S(2)}) collective-permute-start(bf16[96,3072]{1,0:T(8,128)(2,1)S(1)} %get-tuple-element.98), channel_id=1, source_target_pairs={{0,1},{1,2},{4,5},{5,6},{8,9},{9,10},{12,13},{13,14},{16,17},{17,1... | collective-permute-start | bytes 1769480 | tf_op jit(solution)/shard_map/ppermute | solution.py:472
  55.9 3.4 %blocks.4 = (bf16[96,3072]{1,0:T(8,128)(2,1)S(1)}, bf16[96,3072]{1,0:T(8,128)(2,1)S(1)}) custom-call(s32[2]{0:T(128)S(1)} %pad_add_fusion.place, bf16[384,768]{1,0:T(8,128)(2,1)S(1)} %get-tuple-element.94.attended, bf16[768,6144]{1,0:T(8,128)(2,1)} %weight.11), custom_call_target="tpu_custom_call" | custom-call | bytes 11070000 | tf_op jit(solution)/shard_map/blocks/pallas_call | solution.py:449
  59.3 2.0 %collective-permute-done.11 = bf16[96,3072]{1,0:T(8,128)(2,1)S(1)} collective-permute-done((bf16[96,3072]{1,0:T(8,128)(2,1)S(1)}, bf16[96,3072]{1,0:T(8,128)(2,1)S(1)}, u32[]{:S(2)}, u32[]{:S(2)}) %collective-permute-start.11) | collective-permute-done | bytes 589856 | tf_op jit(solution)/shard_map/ppermute | solution.py:472
  61.4 0.2 add_convert_fusion.2
  61.5 1.9 %collective-permute-start.14 = (bf16[96,3072]{1,0:T(8,128)(2,1)S(1)}, bf16[96,3072]{1,0:T(8,128)(2,1)S(1)}, u32[]{:S(2)}, u32[]{:S(2)}) collective-permute-start(bf16[96,3072]{1,0:T(8,128)(2,1)S(1)} %add_convert_fusion.2), channel_id=1, source_target_pairs={{3,2},{2,1},{1,0},{7,6},{6,5},{5,4},{11,10},{10,9},{9,8},{15,14},{... | collective-permute-start | bytes 1769480 | tf_op jit(solution)/shard_map/ppermute | solution.py:473
  63.4 0.1 add_convert_fusion.3
  63.6 3.9 %collective-permute-start.13 = (bf16[96,3072]{1,0:T(8,128)(2,1)S(1)}, bf16[96,3072]{1,0:T(8,128)(2,1)S(1)}, u32[]{:S(2)}, u32[]{:S(2)}) collective-permute-start(bf16[96,3072]{1,0:T(8,128)(2,1)S(1)} %add_convert_fusion.3), channel_id=1, source_target_pairs={{0,1},{1,2},{2,3},{4,5},{5,6},{6,7},{8,9},{9,10},{10,11},{12,13},{... | collective-permute-start | bytes 1769480 | tf_op jit(solution)/shard_map/ppermute | solution.py:472
  67.5 3.4 %blocks.5 = (bf16[96,3072]{1,0:T(8,128)(2,1)S(1)}, bf16[96,3072]{1,0:T(8,128)(2,1)S(1)}) custom-call(s32[2]{0:T(128)S(1)} %pad_add_fusion.place, bf16[384,768]{1,0:T(8,128)(2,1)S(1)} %get-tuple-element.94.attended, bf16[768,6144]{1,0:T(8,128)(2,1)} %weight.11), custom_call_target="tpu_custom_call" | custom-call | bytes 11070000 | tf_op jit(solution)/shard_map/blocks/pallas_call | solution.py:449
  71.0 0.4 collective-permute-done.10
  71.4 2.6 %collective-permute-done.9 = bf16[96,3072]{1,0:T(8,128)(2,1)S(1)} collective-permute-done((bf16[96,3072]{1,0:T(8,128)(2,1)S(1)}, bf16[96,3072]{1,0:T(8,128)(2,1)S(1)}, u32[]{:S(2)}, u32[]{:S(2)}) %collective-permute-start.9) | collective-permute-done | bytes 589856 | tf_op jit(solution)/shard_map/ppermute | solution.py:472
  74.0 0.1 add_convert_fusion
  74.2 1.9 %collective-permute-start.16 = (bf16[96,3072]{1,0:T(8,128)(2,1)S(1)}, bf16[96,3072]{1,0:T(8,128)(2,1)S(1)}, u32[]{:S(2)}, u32[]{:S(2)}) collective-permute-start(bf16[96,3072]{1,0:T(8,128)(2,1)S(1)} %add_convert_fusion), channel_id=1, source_target_pairs={{3,2},{2,1},{1,0},{7,6},{6,5},{5,4},{11,10},{10,9},{9,8},{15,14},{... | collective-permute-start | bytes 1769480 | tf_op jit(solution)/shard_map/ppermute | solution.py:473
  76.1 0.1 add_convert_fusion.1
  76.2 3.9 %collective-permute-start.15 = (bf16[96,3072]{1,0:T(8,128)(2,1)S(1)}, bf16[96,3072]{1,0:T(8,128)(2,1)S(1)}, u32[]{:S(2)}, u32[]{:S(2)}) collective-permute-start(bf16[96,3072]{1,0:T(8,128)(2,1)S(1)} %add_convert_fusion.1), channel_id=1, source_target_pairs={{0,1},{1,2},{2,3},{4,5},{5,6},{6,7},{8,9},{9,10},{10,11},{12,13},{... | collective-permute-start | bytes 1769480 | tf_op jit(solution)/shard_map/ppermute | solution.py:472
  80.2 5.0 %own.1 = (bf16[96,6144]{1,0:T(8,128)(2,1)S(1)}, f32[1,6144]{1,0:T(1,128)S(1)}) custom-call(s32[2]{0:T(128)S(1)} %pad_add_fusion.place, s32[4]{0:T(128)S(1)} %copy-done.2, bf16[384,768]{1,0:T(8,128)(2,1)S(1)} %get-tuple-element.94.attended, bf16[768,6144]{1,0:T(8,128)(2,1)} %weight.11, f32[64,6144]{1,0:T(8,128)} %gate_table.1), custom_call_target="tpu_custom_call" | custom-call | bytes 18450000 | tf_op jit(solution)/shard_map/own/pallas_call | solution.py:476
  85.2 1.4 %collective-permute-done.13 = bf16[96,3072]{1,0:T(8,128)(2,1)S(1)} collective-permute-done((bf16[96,3072]{1,0:T(8,128)(2,1)S(1)}, bf16[96,3072]{1,0:T(8,128)(2,1)S(1)}, u32[]{:S(2)}, u32[]{:S(2)}) %collective-permute-start.13) | collective-permute-done | bytes 589856 | tf_op jit(solution)/shard_map/ppermute | solution.py:472
  86.6 0.3 multiply_convert_fusion.done
  86.9 6.8 %collective-permute-done.16.down = bf16[96,3072]{1,0:T(8,128)(2,1)S(1)} collective-permute-done((bf16[96,3072]{1,0:T(8,128)(2,1)S(1)}, bf16[96,3072]{1,0:T(8,128)(2,1)S(1)}, u32[]{:S(2)}, u32[]{:S(2)}) %collective-permute-start.16) | collective-permute-done | bytes 589856 | tf_op jit(solution)/shard_map/ppermute | solution.py:473
  93.7 3.5 %collective-permute-done.15.up = bf16[96,3072]{1,0:T(8,128)(2,1)S(1)} collective-permute-done((bf16[96,3072]{1,0:T(8,128)(2,1)S(1)}, bf16[96,3072]{1,0:T(8,128)(2,1)S(1)}, u32[]{:S(2)}, u32[]{:S(2)}) %collective-permute-start.15) | collective-permute-done | bytes 589856 | tf_op jit(solution)/shard_map/ppermute | solution.py:472
  97.2 1.1 %final.1 = bf16[96,6144]{1,0:T(8,128)(2,1)} custom-call(bf16[96,3072]{1,0:T(8,128)(2,1)S(1)} %multiply_convert_fusion.done, bf16[96,6144]{1,0:T(8,128)(2,1)S(1)} %get-tuple-element.95.projected, f32[1,6144]{1,0:T(1,128)S(1)} %get-tuple-element.96.gate, bf16[96,3072]{1,0:T(8,128)(2,1)S(1)} %collective-permute-done.15.up, ...), custom_call_target="tpu_custom_call" | custom-call | bytes 9963000 | tf_op jit(solution)/shard_map/final/pallas_call | solution.py:497
  (16 shorter events, 0.0 us)
Async XLA Ops:
  0.0 3.8 %collective-permute-start = (bf16[384,768]{1,0:T(8,128)(2,1)}, bf16[384,768]{1,0:T(8,128)(2,1)S(1)}, u32[]{:S(2)}, u32[]{:S(2)}) collective-permute-start(bf16[384,768]{1,0:T(8,128)(2,1)} %key.7), channel_id=1, source_target_pairs={{0,4},{4,0},{8,12},{12,8},{1,5},{5,1},{9,13},{13,9},{2,6},{6,2},{1... | collective-permute-start | bytes 1769480 | tf_op jit(solution)/shard_map/ppermute | solution.py:341
  0.0 3.8 %collective-permute-start.1 = (bf16[384,768]{1,0:T(8,128)(2,1)}, bf16[384,768]{1,0:T(8,128)(2,1)S(1)}, u32[]{:S(2)}, u32[]{:S(2)}) collective-permute-start(bf16[384,768]{1,0:T(8,128)(2,1)} %value.7), channel_id=1, source_target_pairs={{0,4},{4,0},{8,12},{12,8},{1,5},{5,1},{9,13},{13,9},{2,6},{6,2},{1... | collective-permute-start | bytes 1769480 | tf_op jit(solution)/shard_map/ppermute | solution.py:342
  2.2 6.5 %copy-start = (bf16[384,768]{1,0:T(8,128)(2,1)S(1)}, bf16[384,768]{1,0:T(8,128)(2,1)}, u32[]{:S(2)}) copy-start(bf16[384,768]{1,0:T(8,128)(2,1)} %key.7) | copy-start | bytes 1769476
  2.2 6.5 %copy-start.1 = (bf16[384,768]{1,0:T(8,128)(2,1)S(1)}, bf16[384,768]{1,0:T(8,128)(2,1)}, u32[]{:S(2)}) copy-start(bf16[384,768]{1,0:T(8,128)(2,1)} %value.7) | copy-start | bytes 1769476
  2.3 6.5 %collective-permute-start.2 = (bf16[96,768]{1,0:T(8,128)(2,1)S(1)}, bf16[96,768]{1,0:T(8,128)(2,1)S(1)}, u32[]{:S(2)}, u32[]{:S(2)}) collective-permute-start(bf16[96,768]{1,0:T(8,128)(2,1)S(1)} %get-tuple-element.54), channel_id=1, source_target_pairs={{8,0},{12,4},{9,1},{13,5},{10,2},{14,6},{11,3},{15,7},{24,16},{28,... | collective-permute-start | bytes 442376 | tf_op jit(solution)/shard_map/ppermute | solution.py:32
  7.0 12.2 %collective-permute-start.4 = (bf16[192,768]{1,0:T(8,128)(2,1)S(1)}, bf16[192,768]{1,0:T(8,128)(2,1)S(1)}, u32[]{:S(2)}, u32[]{:S(2)}) collective-permute-start(bf16[192,768]{1,0:T(8,128)(2,1)S(1)} %get-tuple-element.58), channel_id=1, source_target_pairs={{8,0},{12,4},{9,1},{13,5},{10,2},{14,6},{11,3},{15,7},{24,16},{28,... | collective-permute-start | bytes 884744 | tf_op jit(solution)/shard_map/ppermute | solution.py:32
  9.3 8.0 %collective-permute-start.3 = (bf16[96,896]{1,0:T(8,128)(2,1)S(1)}, bf16[96,896]{1,0:T(8,128)(2,1)S(1)}, u32[]{:S(2)}, u32[]{:S(2)}) collective-permute-start(bf16[96,896]{1,0:T(8,128)(2,1)S(1)} %served.2), channel_id=1, source_target_pairs={{0,8},{4,12},{1,9},{5,13},{2,10},{6,14},{3,11},{7,15},{16,24},{20,... | collective-permute-start | bytes 516104 | tf_op jit(solution)/shard_map/ppermute | solution.py:32
  13.6 5.7 %collective-permute-start.5 = (bf16[96,768]{1,0:T(8,128)(2,1)S(1)}, bf16[96,768]{1,0:T(8,128)(2,1)S(1)}, u32[]{:S(2)}, u32[]{:S(2)}) collective-permute-start(bf16[96,768]{1,0:T(8,128)(2,1)S(1)} %get-tuple-element.61), channel_id=1, source_target_pairs={{8,0},{12,4},{9,1},{13,5},{10,2},{14,6},{11,3},{15,7},{24,16},{28,... | collective-permute-start | bytes 442376 | tf_op jit(solution)/shard_map/ppermute | solution.py:32
  17.9 22.4 %collective-permute-start.8 = (bf16[96,3072]{1,0:T(8,128)(2,1)S(1)}, bf16[96,3072]{1,0:T(8,128)(2,1)S(1)}, u32[]{:S(2)}, u32[]{:S(2)}) collective-permute-start(bf16[96,3072]{1,0:T(8,128)(2,1)S(1)} %opening.2), channel_id=1, source_target_pairs={{0,1},{3,2},{4,5},{7,6},{8,9},{11,10},{12,13},{15,14},{16,17},{19,... | collective-permute-start | bytes 1769480 | tf_op jit(solution)/shard_map/ppermute | solution.py:429
  19.8 16.2 %collective-permute-start.6 = (bf16[288,896]{1,0:T(8,128)(2,1)S(1)}, bf16[288,896]{1,0:T(8,128)(2,1)S(1)}, u32[]{:S(2)}, u32[]{:S(2)}) collective-permute-start(bf16[288,896]{1,0:T(8,128)(2,1)S(1)} %served.3), channel_id=1, source_target_pairs={{0,8},{4,12},{1,9},{5,13},{2,10},{6,14},{3,11},{7,15},{16,24},{20,... | collective-permute-start | bytes 1548296 | tf_op jit(solution)/shard_map/ppermute | solution.py:32
  21.7 28.1 %collective-permute-start.7 = (bf16[96,3072]{1,0:T(8,128)(2,1)S(1)}, bf16[96,3072]{1,0:T(8,128)(2,1)S(1)}, u32[]{:S(2)}, u32[]{:S(2)}) collective-permute-start(bf16[96,3072]{1,0:T(8,128)(2,1)S(1)} %opening.3), channel_id=1, source_target_pairs={{0,1},{3,2},{4,5},{7,6},{8,9},{11,10},{12,13},{15,14},{16,17},{19,... | collective-permute-start | bytes 1769480 | tf_op jit(solution)/shard_map/ppermute | solution.py:433
  40.6 18.7 %collective-permute-start.12 = (bf16[96,3072]{1,0:T(8,128)(2,1)S(1)}, bf16[96,3072]{1,0:T(8,128)(2,1)S(1)}, u32[]{:S(2)}, u32[]{:S(2)}) collective-permute-start(bf16[96,3072]{1,0:T(8,128)(2,1)S(1)} %get-tuple-element.99), channel_id=1, source_target_pairs={{3,2},{2,1},{7,6},{6,5},{11,10},{10,9},{15,14},{14,13},{19,18},{18... | collective-permute-start | bytes 1769480 | tf_op jit(solution)/shard_map/ppermute | solution.py:473
  41.9 19.4 %collective-permute-start.11 = (bf16[96,3072]{1,0:T(8,128)(2,1)S(1)}, bf16[96,3072]{1,0:T(8,128)(2,1)S(1)}, u32[]{:S(2)}, u32[]{:S(2)}) collective-permute-start(bf16[96,3072]{1,0:T(8,128)(2,1)S(1)} %get-tuple-element.100), channel_id=1, source_target_pairs={{0,1},{1,2},{4,5},{5,6},{8,9},{9,10},{12,13},{13,14},{16,17},{17,1... | collective-permute-start | bytes 1769480 | tf_op jit(solution)/shard_map/ppermute | solution.py:472
  50.0 21.4 %collective-permute-start.10 = (bf16[96,3072]{1,0:T(8,128)(2,1)S(1)}, bf16[96,3072]{1,0:T(8,128)(2,1)S(1)}, u32[]{:S(2)}, u32[]{:S(2)}) collective-permute-start(bf16[96,3072]{1,0:T(8,128)(2,1)S(1)} %get-tuple-element.97), channel_id=1, source_target_pairs={{3,2},{2,1},{7,6},{6,5},{11,10},{10,9},{15,14},{14,13},{19,18},{18... | collective-permute-start | bytes 1769480 | tf_op jit(solution)/shard_map/ppermute | solution.py:473
  51.3 22.7 %collective-permute-start.9 = (bf16[96,3072]{1,0:T(8,128)(2,1)S(1)}, bf16[96,3072]{1,0:T(8,128)(2,1)S(1)}, u32[]{:S(2)}, u32[]{:S(2)}) collective-permute-start(bf16[96,3072]{1,0:T(8,128)(2,1)S(1)} %get-tuple-element.98), channel_id=1, source_target_pairs={{0,1},{1,2},{4,5},{5,6},{8,9},{9,10},{12,13},{13,14},{16,17},{17,1... | collective-permute-start | bytes 1769480 | tf_op jit(solution)/shard_map/ppermute | solution.py:472
  61.5 23.7 %collective-permute-start.14 = (bf16[96,3072]{1,0:T(8,128)(2,1)S(1)}, bf16[96,3072]{1,0:T(8,128)(2,1)S(1)}, u32[]{:S(2)}, u32[]{:S(2)}) collective-permute-start(bf16[96,3072]{1,0:T(8,128)(2,1)S(1)} %add_convert_fusion.2), channel_id=1, source_target_pairs={{3,2},{2,1},{1,0},{7,6},{6,5},{5,4},{11,10},{10,9},{9,8},{15,14},{... | collective-permute-start | bytes 1769480 | tf_op jit(solution)/shard_map/ppermute | solution.py:473
  63.6 23.0 %collective-permute-start.13 = (bf16[96,3072]{1,0:T(8,128)(2,1)S(1)}, bf16[96,3072]{1,0:T(8,128)(2,1)S(1)}, u32[]{:S(2)}, u32[]{:S(2)}) collective-permute-start(bf16[96,3072]{1,0:T(8,128)(2,1)S(1)} %add_convert_fusion.3), channel_id=1, source_target_pairs={{0,1},{1,2},{2,3},{4,5},{5,6},{6,7},{8,9},{9,10},{10,11},{12,13},{... | collective-permute-start | bytes 1769480 | tf_op jit(solution)/shard_map/ppermute | solution.py:472
  74.1 6.0 %copy-start.2 = (s32[4]{0:T(128)S(1)}, s32[4]{0:T(128)}, u32[]{:S(2)}) copy-start(s32[4]{0:T(128)} %levels.1) | copy-start | bytes 52
  74.2 19.5 %collective-permute-start.16 = (bf16[96,3072]{1,0:T(8,128)(2,1)S(1)}, bf16[96,3072]{1,0:T(8,128)(2,1)S(1)}, u32[]{:S(2)}, u32[]{:S(2)}) collective-permute-start(bf16[96,3072]{1,0:T(8,128)(2,1)S(1)} %add_convert_fusion), channel_id=1, source_target_pairs={{3,2},{2,1},{1,0},{7,6},{6,5},{5,4},{11,10},{10,9},{9,8},{15,14},{... | collective-permute-start | bytes 1769480 | tf_op jit(solution)/shard_map/ppermute | solution.py:473
  76.2 21.0 %collective-permute-start.15 = (bf16[96,3072]{1,0:T(8,128)(2,1)S(1)}, bf16[96,3072]{1,0:T(8,128)(2,1)S(1)}, u32[]{:S(2)}, u32[]{:S(2)}) collective-permute-start(bf16[96,3072]{1,0:T(8,128)(2,1)S(1)} %add_convert_fusion.1), channel_id=1, source_target_pairs={{0,1},{1,2},{2,3},{4,5},{5,6},{6,7},{8,9},{9,10},{10,11},{12,13},{... | collective-permute-start | bytes 1769480 | tf_op jit(solution)/shard_map/ppermute | solution.py:472

commit v21 on v20

--- a/solution.py
+++ b/solution.py
@@ -86,6 +86,10 @@
     return span + 1 - 2 * lax.rem(span, 2)
 
 
+def place_here():
+    return lax.axis_index("span"), lax.axis_index("tensor")
+
+
 def copied(source, target, semaphore):
     copy = pltpu.make_async_copy(source, target, semaphore)
     copy.start()
@@ -100,8 +104,9 @@
     return (early, block), (late, rows - block)
 
 
-def split_kernel(ranks, place, query, *refs):
+def split_kernel(ranks, query, *refs):
     *targets, semaphores = refs
+    place = place_here()
 
     @pl.when(place[0] > 1)
     def _():
@@ -115,9 +120,10 @@
             copy.wait()
 
 
-def local_kernel(ranks, part, place, visible, query, key, value, key_beside, value_beside,
+def local_kernel(ranks, part, visible, query, key, value, key_beside, value_beside,
                  result, sums, seen, *scratch):
     query_, key_, value_, key_beside_, value_beside_, semaphores = scratch
+    place = place_here()
     start, size = parts_of(place[1], ranks, query.shape[0])[part]
     copies = [
         copied(source, target, semaphores.at[index])
@@ -140,8 +146,8 @@
     sums[...] = attend(query_, [key_, key_beside_], [value_, value_beside_], flags, write, arrive)
 
 
-def served_kernel(distance, spans, place, visible, key, value, key_beside, value_beside, *refs):
-    span = place[0]
+def served_kernel(distance, spans, visible, key, value, key_beside, value_beside, *refs):
+    span, _ = place_here()
 
     @pl.when(span + distance < spans)
     def _():
@@ -195,19 +201,21 @@
     ]
 
 
-def fetch_kernel(askers, place, weight, *refs):
+def fetch_kernel(askers, weight, *refs):
     tiles, semaphores = refs[-2:]
-
-    @pl.when(place[0] > 1 if askers else place[0] < 2)
+    span, _ = place_here()
+
+    @pl.when(span > 1 if askers else span < 2)
     def _():
         for copy in streamed(weight, 0, tiles, semaphores):
             copy.wait()
 
 
-def opening_kernel(ranks, distances, first, place, *refs):
+def opening_kernel(ranks, distances, first, *refs):
     own, own_sum, *served = refs[:2 + len(distances)]
     weight, result, *scratch = refs[2 + len(distances):]
     rows = scratch[-1]
+    place = place_here()
 
     @pl.when(jnp.logical_or(place[1] == 0, place[1] == ranks - 1))
     def _():
@@ -327,14 +335,14 @@
     third = (rows - block) // 48 * 16
     query_early, *query_late = pl.pallas_call(
         functools.partial(split_kernel, ranks),
-        in_specs=[SMEM, HBM],
+        in_specs=[HBM],
         out_specs=[VMEM] * 3,
         out_shape=[jax.ShapeDtypeStruct((part, width), bf16) for part in (block, rows - block - third, third)],
         scratch_shapes=[pltpu.SemaphoreType.DMA((3,))],
         compiler_params=PARAMS,
         cost_estimate=taking(1.7),
         name="split",
-    )(place, in_hbm(queries))
+    )(in_hbm(queries))
     distances = list(range(2, spans, 2))
     asked_early = [shifted(query_early, "span", -distance) for distance in distances]
     swap = [(i, i + 1 - 2 * (i % 2)) for i in range(spans)]
@@ -344,11 +352,11 @@
     def after(value, *others):
         return lax.optimization_barrier((value, others))[0]
 
-    def local(part, place):
+    def local(part, queries):
         size = (block, rows - block)[part]
         return pl.pallas_call(
             functools.partial(local_kernel, ranks, part),
-            in_specs=[SMEM, HBM, HBM, HBM, HBM, ANY, ANY],
+            in_specs=[HBM, HBM, HBM, HBM, ANY, ANY],
             out_specs=[VMEM] * 3,
             out_shape=[
                 jax.ShapeDtypeStruct((size, width), f32),
@@ -360,21 +368,21 @@
             compiler_params=PARAMS,
             cost_estimate=taking(4.0),
             name="local",
-        )(place, in_hbm(visible), in_hbm(queries), in_hbm(keys), in_hbm(values), key_beside, value_beside)
+        )(in_hbm(visible), in_hbm(queries), in_hbm(keys), in_hbm(values), key_beside, value_beside)
 
     def served(asked, distance):
         return pl.pallas_call(
             functools.partial(served_kernel, distance, spans),
-            in_specs=[SMEM] + [VMEM] * (5 + len(asked)),
+            in_specs=[VMEM] * (5 + len(asked)),
             out_specs=VMEM,
             out_shape=jax.ShapeDtypeStruct((sum(part.shape[0] for part in asked), width + LANES), bf16),
             scratch_shapes=[pltpu.VMEM((sum(part.shape[0] for part in asked), width), bf16)],
             compiler_params=PARAMS,
             cost_estimate=taking(3.3),
             name="served",
-        )(place, seen, keys, values, key_beside, value_beside, *asked)
-
-    *early, seen = local(0, place)
+        )(seen, keys, values, key_beside, value_beside, *asked)
+
+    *early, seen = local(0, queries)
     query_late = after(query_late, early)
     asked_early = after(asked_early, early)
     chunks = 2
@@ -391,47 +399,47 @@
         cost_estimate=taking(3.0),
     )
 
-    def fetch(askers, place, *before):
+    def fetch(askers, weight, *before):
         return pl.pallas_call(
             functools.partial(fetch_kernel, askers),
-            in_specs=[SMEM, HBM] + [VMEM] * len(before),
+            in_specs=[HBM] + [VMEM] * len(before),
             out_specs=VMEM,
             out_shape=jax.ShapeDtypeStruct(tile_shape, bf16),
-            input_output_aliases={2: 0} if before else {},
+            input_output_aliases={1: 0} if before else {},
             scratch_shapes=[pltpu.SemaphoreType.DMA((tiles,))],
             compiler_params=PARAMS,
             cost_estimate=taking(2.4),
             name="fetch",
-        )(place, weight, *before)
+        )(in_hbm(weight), *before)
 
     out_early = [served([q], d) for q, d in zip(asked_early, distances)]
     early += [shifted(o, "span", d) for o, d in zip(out_early, distances)]
-    fetched = fetch(True, after(place, out_early))
+    fetched = fetch(True, after(out_weight, out_early))
     query_late = [query_late[0], after(query_late[1], fetched)]
     asked_late = [[shifted(query, "span", -distance) for query in query_late] for distance in distances]
-    fetched = fetch(False, place, fetched)
-
-    def opening(chunk, place):
+    fetched = fetch(False, out_weight, fetched)
+
+    def opening(chunk, weight):
         scratch = streaming["scratch_shapes"] if chunk else []
         return pl.pallas_call(
             functools.partial(opening_kernel, ranks, distances, chunk * columns),
-            in_specs=[SMEM] + [VMEM] * (2 + len(distances)) + [HBM if chunk else VMEM],
+            in_specs=[VMEM] * (2 + len(distances)) + [HBM if chunk else VMEM],
             out_specs=VMEM,
             out_shape=jax.ShapeDtypeStruct((block, columns), bf16),
             scratch_shapes=scratch + [pltpu.VMEM((block, width), bf16)],
             compiler_params=PARAMS,
             cost_estimate=taking(3.4),
             name="opening",
-        )(place, *early, weight if chunk else fetched)
+        )(*early, in_hbm(weight) if chunk else fetched)
 
     ends = [(0, 1), (last, last - 1)]
-    sent = opening(0, place)
+    sent = opening(0, out_weight)
     arrived = [[lax.ppermute(sent, "tensor", ends)]]
     out_late = [served(q, d) for q, d in zip(after(asked_late, sent), distances)]
     for chunk in range(1, chunks):
-        sent = opening(chunk, after(place, out_late))
+        sent = opening(chunk, after(out_weight, out_late))
         arrived.append([lax.ppermute(sent, "tensor", ends)])
-    *late, _ = local(1, after(place, sent))
+    *late, _ = local(1, after(queries, sent))
     late += [shifted(o, "span", d) for o, d in zip(out_late, distances)]
 
     attended_shape = jax.ShapeDtypeStruct((rows, width), bf16)

time: 100 us -> 101 us (1.010)
  waiting for transfers between devices: 26.6 us -> 31.2 us
  Pallas kernels: 35.4 us -> 31.3 us
  other arithmetic: 1.42 us -> 2.49 us
    ppermute x4, waiting for transfers between devices: 7.26 us -> 17.5 us  [body(): lax.ppermute(down, 'tensor', [(last - i, last - i - 1) for i in range(ste...]
    ppermute x4, waiting for transfers between devices: 9.53 us -> 0.01 us  [body(): lax.ppermute(up, 'tensor', [(i, i + 1) for i in range(step + 1)])]
    ppermute x5, waiting for transfers between devices: 9.78 us -> 13.6 us  [shifted(): lax.ppermute(block, axis, [(i, i + distance) for i in range(count) if 0 <...]
    pallas_call x5, Pallas kernels: 12.6 us -> 9.92 us  [the longest x2 6.37 us: local(): pl.pallas_call(functools.partial(local_kernel, ranks, part), in_specs=[HB...]
    ppermute x4, starting transfers between devices: 16.9 us -> 14.5 us  [body(): lax.ppermute(up, 'tensor', [(i, i + 1) for i in range(step + 1)])]
    ppermute x4, starting transfers between devices: 6.43 us -> 8.46 us  [body(): lax.ppermute(down, 'tensor', [(last - i, last - i - 1) for i in range(ste...]
    pallas_call x2, Pallas kernels: 1.13 us -> 0.04 us  [opening(): pl.pallas_call(functools.partial(opening_kernel, ranks, distances, chunk...]
    convert_element_type x6, other arithmetic: 1.09 us -> 2.15 us  [body(): (mine.astype(f32) + come.astype(f32)).astype(bf16)]
  transfers between devices with their start and end apart: 17 -> 17, of which waited for: 8 -> 7; matrix products, arithmetic and copies ran while one was open for 1% -> 2% of each run, Pallas kernels for 35% -> 30%
where the time goes in v21:
time: 101 us; the launch traced here: 100 us
  starting transfers between devices  34.6 us (34%)
  Pallas kernels  31.3 us (31%)
  waiting for transfers between devices  31.2 us (31%)
  other arithmetic  2.49 us (2%)
    ppermute x4, waiting for transfers between devices, body(): lax.ppermute(down, 'tensor', [(last - i, last - i - 1) for i in range(ste...  17.5 us
    ppermute x4, starting transfers between devices, body(): lax.ppermute(up, 'tensor', [(i, i + 1) for i in range(step + 1)])  14.5 us
    ppermute x5, waiting for transfers between devices, shifted(): lax.ppermute(block, axis, [(i, i + distance) for i in range(count) if 0 <...  13.6 us
    pallas_call x3, Pallas kernels, blocks_of(): pl.pallas_call(functools.partial(blocks_kernel, ranks, chunk * columns, s...  10.2 us
    ppermute x5, starting transfers between devices, shifted(): lax.ppermute(block, axis, [(i, i + distance) for i in range(count) if 0 <...  8.6 us
    ppermute x4, starting transfers between devices, body(): lax.ppermute(down, 'tensor', [(last - i, last - i - 1) for i in range(ste...  8.46 us
    pallas_call x2, Pallas kernels, local(): pl.pallas_call(functools.partial(local_kernel, ranks, part), in_specs=[HB...  6.37 us
    pallas_call x1, Pallas kernels, body(): pl.pallas_call(own_kernel, in_specs=[SMEM, SMEM, VMEM, HBM, HBM], out_spe...  4.99 us
  transfers between devices with their start and end apart: 17, of which 7 were waited for; matrix products, arithmetic and copies ran while one was open for 2% of the time, Pallas kernels for 30%

profile of v21, /device:TPU:14, one launch (start us, length us, event | category | flops | bytes accessed | tf_op | source)
XLA Modules:
  0.0 100.2 jit_solution(15534459773213968864)
XLA Ops:
  0.0 0.5 collective-permute-start.1
  0.5 1.1 %split.1 = (bf16[96,768]{1,0:T(8,128)(2,1)S(1)}, bf16[192,768]{1,0:T(8,128)(2,1)S(1)}, bf16[96,768]{1,0:T(8,128)(2,1)S(1)}) custom-call(bf16[384,768]{1,0:T(8,128)(2,1)} %query.4), custom_call_target="tpu_custom_call" | custom-call | bytes 6273000 | tf_op jit(solution)/shard_map/split/pallas_call | solution.py:336
  1.6 0.0 copy-start
  1.6 0.0 copy-start.1
  1.6 1.5 %collective-permute-start.2 = (bf16[96,768]{1,0:T(8,128)(2,1)S(1)}, bf16[96,768]{1,0:T(8,128)(2,1)S(1)}, u32[]{:S(2)}, u32[]{:S(2)}) collective-permute-start(bf16[96,768]{1,0:T(8,128)(2,1)S(1)} %get-tuple-element.54), channel_id=1, source_target_pairs={{8,0},{12,4},{9,1},{13,5},{10,2},{14,6},{11,3},{15,7},{24,16},{28,... | collective-permute-start | bytes 442376 | tf_op jit(solution)/shard_map/ppermute | solution.py:32
  3.1 0.0 collective-permute-done.key_beside
  3.1 0.0 collective-permute-done.1.value_beside
  3.1 2.7 %local.2 = (f32[96,768]{1,0:T(8,128)S(1)}, f32[96,128]{1,0:T(8,128)S(1)}, s32[4,4]{1,0:T(4,128)S(1)}) custom-call(s32[4,4]{1,0:T(4,128)} %visible.3, bf16[384,768]{1,0:T(8,128)(2,1)} %query.4, bf16[384,768]{1,0:T(8,128)(2,1)} %key.7, bf16[384,768]{1,0:T(8,128)(2,1)} %value.7, bf16[384,768]{1,0:T(8,128)(2,1)S(1)} %collective-permute-done.key_beside, ...), custom_call_target="tpu_custom_call" | custom-call | bytes 14760000 | tf_op jit(solution)/shard_map/local/pallas_call | solution.py:357
  5.9 2.3 %collective-permute-start.4 = (bf16[192,768]{1,0:T(8,128)(2,1)S(1)}, bf16[192,768]{1,0:T(8,128)(2,1)S(1)}, u32[]{:S(2)}, u32[]{:S(2)}) collective-permute-start(bf16[192,768]{1,0:T(8,128)(2,1)S(1)} %get-tuple-element.58), channel_id=1, source_target_pairs={{8,0},{12,4},{9,1},{13,5},{10,2},{14,6},{11,3},{15,7},{24,16},{28,... | collective-permute-start | bytes 884744 | tf_op jit(solution)/shard_map/ppermute | solution.py:32
  8.3 1.3 %collective-permute-start.3 = (bf16[96,896]{1,0:T(8,128)(2,1)S(1)}, bf16[96,896]{1,0:T(8,128)(2,1)S(1)}, u32[]{:S(2)}, u32[]{:S(2)}) collective-permute-start(bf16[96,896]{1,0:T(8,128)(2,1)S(1)} %served.2), channel_id=1, source_target_pairs={{0,8},{4,12},{1,9},{5,13},{2,10},{6,14},{3,11},{7,15},{16,24},{20,... | collective-permute-start | bytes 516104 | tf_op jit(solution)/shard_map/ppermute | solution.py:32
  9.6 2.4 %fetch.2.refs_0_ = bf16[4,768,768]{2,1,0:T(8,128)(2,1)S(1)} custom-call(bf16[768,6144]{1,0:T(8,128)(2,1)} %weight.10), custom_call_target="tpu_custom_call" | custom-call | bytes 8856000 | tf_op jit(solution)/shard_map/fetch/pallas_call | solution.py:403
  12.0 2.2 %collective-permute-start.5 = (bf16[96,768]{1,0:T(8,128)(2,1)S(1)}, bf16[96,768]{1,0:T(8,128)(2,1)S(1)}, u32[]{:S(2)}, u32[]{:S(2)}) collective-permute-start(bf16[96,768]{1,0:T(8,128)(2,1)S(1)} %get-tuple-element.61), channel_id=1, source_target_pairs={{8,0},{12,4},{9,1},{13,5},{10,2},{14,6},{11,3},{15,7},{24,16},{28,... | collective-permute-start | bytes 442376 | tf_op jit(solution)/shard_map/ppermute | solution.py:32
  14.2 0.1 fetch.3.refs_3_
  14.2 2.0 %collective-permute-done.3.refs_2_ = bf16[96,896]{1,0:T(8,128)(2,1)S(1)} collective-permute-done((bf16[96,896]{1,0:T(8,128)(2,1)S(1)}, bf16[96,896]{1,0:T(8,128)(2,1)S(1)}, u32[]{:S(2)}, u32[]{:S(2)}) %collective-permute-start.3) | collective-permute-done | bytes 172064 | tf_op jit(solution)/shard_map/ppermute | solution.py:32
  16.3 1.3 %collective-permute-start.8 = (bf16[96,3072]{1,0:T(8,128)(2,1)S(1)}, bf16[96,3072]{1,0:T(8,128)(2,1)}, u32[]{:S(2)}, u32[]{:S(2)}) collective-permute-start(bf16[96,3072]{1,0:T(8,128)(2,1)S(1)} %opening.2), channel_id=1, source_target_pairs={{0,1},{3,2},{4,5},{7,6},{8,9},{11,10},{12,13},{15,14},{16,17},{19,... | collective-permute-start | bytes 1769480 | tf_op jit(solution)/shard_map/ppermute | solution.py:437
  17.6 0.3 collective-permute-done.5.refs_1_
  17.9 0.8 served.3
  18.7 1.3 %collective-permute-start.6 = (bf16[288,896]{1,0:T(8,128)(2,1)}, bf16[288,896]{1,0:T(8,128)(2,1)S(1)}, u32[]{:S(2)}, u32[]{:S(2)}) collective-permute-start(bf16[288,896]{1,0:T(8,128)(2,1)} %served.3), channel_id=1, source_target_pairs={{0,8},{4,12},{1,9},{5,13},{2,10},{6,14},{3,11},{7,15},{16,24},{20,... | collective-permute-start | bytes 1548296 | tf_op jit(solution)/shard_map/ppermute | solution.py:32
  20.0 0.1 pad_add_fusion.place
  20.1 1.3 %collective-permute-start.7 = (bf16[96,3072]{1,0:T(8,128)(2,1)S(1)}, bf16[96,3072]{1,0:T(8,128)(2,1)S(1)}, u32[]{:S(2)}, u32[]{:S(2)}) collective-permute-start(bf16[96,3072]{1,0:T(8,128)(2,1)S(1)} %opening.3), channel_id=1, source_target_pairs={{0,1},{3,2},{4,5},{7,6},{8,9},{11,10},{12,13},{15,14},{16,17},{19,... | collective-permute-start | bytes 1769480 | tf_op jit(solution)/shard_map/ppermute | solution.py:441
  21.4 3.7 %local.3 = (f32[288,768]{1,0:T(8,128)S(1)}, f32[288,128]{1,0:T(8,128)S(1)}, s32[4,4]{1,0:T(4,128)}) custom-call(s32[4,4]{1,0:T(4,128)} %visible.3, bf16[384,768]{1,0:T(8,128)(2,1)} %query.4, bf16[384,768]{1,0:T(8,128)(2,1)} %key.7, bf16[384,768]{1,0:T(8,128)(2,1)} %value.7, bf16[384,768]{1,0:T(8,128)(2,1)S(1)} %collective-permute-done.key_beside, ...), custom_call_target="tpu_custom_call" | custom-call | bytes 14760000 | tf_op jit(solution)/shard_map/local/pallas_call | solution.py:357
  25.1 11.3 %collective-permute-done.6.refs_5_ = bf16[288,896]{1,0:T(8,128)(2,1)S(1)} collective-permute-done((bf16[288,896]{1,0:T(8,128)(2,1)}, bf16[288,896]{1,0:T(8,128)(2,1)S(1)}, u32[]{:S(2)}, u32[]{:S(2)}) %collective-permute-start.6) | collective-permute-done | bytes 516128 | tf_op jit(solution)/shard_map/ppermute | solution.py:32
  36.3 4.3 %merged_blocks.1 = (bf16[384,768]{1,0:T(8,128)(2,1)S(1)}, bf16[96,3072]{1,0:T(8,128)(2,1)S(1)}, bf16[96,3072]{1,0:T(8,128)(2,1)S(1)}) custom-call(s32[2]{0:T(128)S(1)} %pad_add_fusion.place, f32[96,768]{1,0:T(8,128)S(1)} %get-tuple-element.51.refs_0_, f32[96,128]{1,0:T(8,128)S(1)} %get-tuple-element.52.refs_1_, ...), custom_call_target="tpu_custom_call" | custom-call | bytes 11070000 | tf_op jit(solution)/shard_map/merged_blocks/pallas_call | solution.py:447
  40.7 1.3 %fusion.1 = (bf16[96,3072]{1,0:T(8,128)(2,1)S(1)}, bf16[96,3072]{1,0:T(8,128)(2,1)S(1)}) fusion(bf16[96,3072]{1,0:T(8,128)(2,1)} %collective-permute-done.8, bf16[96,3072]{1,0:T(8,128)(2,1)S(1)} %get-tuple-element.73, bf16[96,3072]{1,0:T(8,128)(2,1)S(1)} %get-tuple-element.71), kind=kLoop, calls=%fused_computation.5 | loop fusion | flops 2064384 | bytes 2949120 | tf_op jit(solution)/shard_map/convert_element_type | solution.py:475
  42.0 3.5 %collective-permute-start.11 = (bf16[96,3072]{1,0:T(8,128)(2,1)S(1)}, bf16[96,3072]{1,0:T(8,128)(2,1)S(1)}, u32[]{:S(2)}, u32[]{:S(2)}) collective-permute-start(bf16[96,3072]{1,0:T(8,128)(2,1)S(1)} %get-tuple-element.100), channel_id=1, source_target_pairs={{0,1},{1,2},{4,5},{5,6},{8,9},{9,10},{12,13},{13,14},{16,17},{17,1... | collective-permute-start | bytes 1769480 | tf_op jit(solution)/shard_map/ppermute | solution.py:480
  45.5 1.3 %collective-permute-start.12 = (bf16[96,3072]{1,0:T(8,128)(2,1)S(1)}, bf16[96,3072]{1,0:T(8,128)(2,1)S(1)}, u32[]{:S(2)}, u32[]{:S(2)}) collective-permute-start(bf16[96,3072]{1,0:T(8,128)(2,1)S(1)} %get-tuple-element.99), channel_id=1, source_target_pairs={{3,2},{2,1},{7,6},{6,5},{11,10},{10,9},{15,14},{14,13},{19,18},{18... | collective-permute-start | bytes 1769480 | tf_op jit(solution)/shard_map/ppermute | solution.py:481
  46.8 3.3 %blocks.3 = (bf16[96,3072]{1,0:T(8,128)(2,1)S(1)}, bf16[96,3072]{1,0:T(8,128)(2,1)S(1)}) custom-call(s32[2]{0:T(128)S(1)} %pad_add_fusion.place, bf16[384,768]{1,0:T(8,128)(2,1)S(1)} %get-tuple-element.94.attended, bf16[768,6144]{1,0:T(8,128)(2,1)} %weight.10), custom_call_target="tpu_custom_call" | custom-call | bytes 11070000 | tf_op jit(solution)/shard_map/blocks/pallas_call | solution.py:457
  50.1 0.2 fusion.3
  50.3 1.3 %collective-permute-start.10 = (bf16[96,3072]{1,0:T(8,128)(2,1)S(1)}, bf16[96,3072]{1,0:T(8,128)(2,1)S(1)}, u32[]{:S(2)}, u32[]{:S(2)}) collective-permute-start(bf16[96,3072]{1,0:T(8,128)(2,1)S(1)} %get-tuple-element.97), channel_id=1, source_target_pairs={{3,2},{2,1},{7,6},{6,5},{11,10},{10,9},{15,14},{14,13},{19,18},{18... | collective-permute-start | bytes 1769480 | tf_op jit(solution)/shard_map/ppermute | solution.py:481
  51.6 5.2 %collective-permute-start.9 = (bf16[96,3072]{1,0:T(8,128)(2,1)S(1)}, bf16[96,3072]{1,0:T(8,128)(2,1)S(1)}, u32[]{:S(2)}, u32[]{:S(2)}) collective-permute-start(bf16[96,3072]{1,0:T(8,128)(2,1)S(1)} %get-tuple-element.98), channel_id=1, source_target_pairs={{0,1},{1,2},{4,5},{5,6},{8,9},{9,10},{12,13},{13,14},{16,17},{17,1... | collective-permute-start | bytes 1769480 | tf_op jit(solution)/shard_map/ppermute | solution.py:480
  56.8 3.4 %blocks.4 = (bf16[96,3072]{1,0:T(8,128)(2,1)S(1)}, bf16[96,3072]{1,0:T(8,128)(2,1)S(1)}) custom-call(s32[2]{0:T(128)S(1)} %pad_add_fusion.place, bf16[384,768]{1,0:T(8,128)(2,1)S(1)} %get-tuple-element.94.attended, bf16[768,6144]{1,0:T(8,128)(2,1)} %weight.10), custom_call_target="tpu_custom_call" | custom-call | bytes 11070000 | tf_op jit(solution)/shard_map/blocks/pallas_call | solution.py:457
  60.3 3.4 %collective-permute-done.12 = bf16[96,3072]{1,0:T(8,128)(2,1)S(1)} collective-permute-done((bf16[96,3072]{1,0:T(8,128)(2,1)S(1)}, bf16[96,3072]{1,0:T(8,128)(2,1)S(1)}, u32[]{:S(2)}, u32[]{:S(2)}) %collective-permute-start.12) | collective-permute-done | bytes 589856 | tf_op jit(solution)/shard_map/ppermute | solution.py:481
  63.6 0.2 add_convert_fusion.3
  63.8 1.9 %collective-permute-start.13 = (bf16[96,3072]{1,0:T(8,128)(2,1)S(1)}, bf16[96,3072]{1,0:T(8,128)(2,1)S(1)}, u32[]{:S(2)}, u32[]{:S(2)}) collective-permute-start(bf16[96,3072]{1,0:T(8,128)(2,1)S(1)} %add_convert_fusion.3), channel_id=1, source_target_pairs={{0,1},{1,2},{2,3},{4,5},{5,6},{6,7},{8,9},{9,10},{10,11},{12,13},{... | collective-permute-start | bytes 1769480 | tf_op jit(solution)/shard_map/ppermute | solution.py:480
  65.7 0.1 add_convert_fusion.2
  65.9 4.0 %collective-permute-start.14 = (bf16[96,3072]{1,0:T(8,128)(2,1)S(1)}, bf16[96,3072]{1,0:T(8,128)(2,1)S(1)}, u32[]{:S(2)}, u32[]{:S(2)}) collective-permute-start(bf16[96,3072]{1,0:T(8,128)(2,1)S(1)} %add_convert_fusion.2), channel_id=1, source_target_pairs={{3,2},{2,1},{1,0},{7,6},{6,5},{5,4},{11,10},{10,9},{9,8},{15,14},{... | collective-permute-start | bytes 1769480 | tf_op jit(solution)/shard_map/ppermute | solution.py:481
  69.8 3.4 %blocks.5 = (bf16[96,3072]{1,0:T(8,128)(2,1)S(1)}, bf16[96,3072]{1,0:T(8,128)(2,1)S(1)}) custom-call(s32[2]{0:T(128)S(1)} %pad_add_fusion.place, bf16[384,768]{1,0:T(8,128)(2,1)S(1)} %get-tuple-element.94.attended, bf16[768,6144]{1,0:T(8,128)(2,1)} %weight.10), custom_call_target="tpu_custom_call" | custom-call | bytes 11070000 | tf_op jit(solution)/shard_map/blocks/pallas_call | solution.py:457
  73.3 3.0 %collective-permute-done.10 = bf16[96,3072]{1,0:T(8,128)(2,1)S(1)} collective-permute-done((bf16[96,3072]{1,0:T(8,128)(2,1)S(1)}, bf16[96,3072]{1,0:T(8,128)(2,1)S(1)}, u32[]{:S(2)}, u32[]{:S(2)}) %collective-permute-start.10) | collective-permute-done | bytes 589856 | tf_op jit(solution)/shard_map/ppermute | solution.py:481
  76.3 0.1 add_convert_fusion
  76.4 0.0 copy-start.2
  76.4 1.9 %collective-permute-start.16 = (bf16[96,3072]{1,0:T(8,128)(2,1)S(1)}, bf16[96,3072]{1,0:T(8,128)(2,1)S(1)}, u32[]{:S(2)}, u32[]{:S(2)}) collective-permute-start(bf16[96,3072]{1,0:T(8,128)(2,1)S(1)} %add_convert_fusion), channel_id=1, source_target_pairs={{3,2},{2,1},{1,0},{7,6},{6,5},{5,4},{11,10},{10,9},{9,8},{15,14},{... | collective-permute-start | bytes 1769480 | tf_op jit(solution)/shard_map/ppermute | solution.py:481
  78.4 0.1 add_convert_fusion.1
  78.5 3.9 %collective-permute-start.15 = (bf16[96,3072]{1,0:T(8,128)(2,1)S(1)}, bf16[96,3072]{1,0:T(8,128)(2,1)S(1)}, u32[]{:S(2)}, u32[]{:S(2)}) collective-permute-start(bf16[96,3072]{1,0:T(8,128)(2,1)S(1)} %add_convert_fusion.1), channel_id=1, source_target_pairs={{0,1},{1,2},{2,3},{4,5},{5,6},{6,7},{8,9},{9,10},{10,11},{12,13},{... | collective-permute-start | bytes 1769480 | tf_op jit(solution)/shard_map/ppermute | solution.py:480
  82.5 5.0 %own.1 = (bf16[96,6144]{1,0:T(8,128)(2,1)S(1)}, f32[1,6144]{1,0:T(1,128)S(1)}) custom-call(s32[2]{0:T(128)S(1)} %pad_add_fusion.place, s32[4]{0:T(128)S(1)} %copy-done.2, bf16[384,768]{1,0:T(8,128)(2,1)S(1)} %get-tuple-element.94.attended, bf16[768,6144]{1,0:T(8,128)(2,1)} %weight.10, f32[64,6144]{1,0:T(8,128)} %gate_table.1), custom_call_target="tpu_custom_call" | custom-call | bytes 18450000 | tf_op jit(solution)/shard_map/own/pallas_call | solution.py:484
  87.5 1.4 %collective-permute-done.14 = bf16[96,3072]{1,0:T(8,128)(2,1)S(1)} collective-permute-done((bf16[96,3072]{1,0:T(8,128)(2,1)S(1)}, bf16[96,3072]{1,0:T(8,128)(2,1)S(1)}, u32[]{:S(2)}, u32[]{:S(2)}) %collective-permute-start.14) | collective-permute-done | bytes 589856 | tf_op jit(solution)/shard_map/ppermute | solution.py:481
  88.9 0.3 multiply_convert_fusion.done
  89.2 9.7 %collective-permute-done.16.down = bf16[96,3072]{1,0:T(8,128)(2,1)S(1)} collective-permute-done((bf16[96,3072]{1,0:T(8,128)(2,1)S(1)}, bf16[96,3072]{1,0:T(8,128)(2,1)S(1)}, u32[]{:S(2)}, u32[]{:S(2)}) %collective-permute-start.16) | collective-permute-done | bytes 589856 | tf_op jit(solution)/shard_map/ppermute | solution.py:481
  98.9 1.1 %final.1 = bf16[96,6144]{1,0:T(8,128)(2,1)} custom-call(bf16[96,3072]{1,0:T(8,128)(2,1)S(1)} %multiply_convert_fusion.done, bf16[96,6144]{1,0:T(8,128)(2,1)S(1)} %get-tuple-element.95.projected, f32[1,6144]{1,0:T(1,128)S(1)} %get-tuple-element.96.gate, bf16[96,3072]{1,0:T(8,128)(2,1)S(1)} %collective-permute-done.15.up, ...), custom_call_target="tpu_custom_call" | custom-call | bytes 9963000 | tf_op jit(solution)/shard_map/final/pallas_call | solution.py:505
  (16 shorter events, 0.1 us)
Async XLA Ops:
  0.0 3.1 %collective-permute-start = (bf16[384,768]{1,0:T(8,128)(2,1)}, bf16[384,768]{1,0:T(8,128)(2,1)S(1)}, u32[]{:S(2)}, u32[]{:S(2)}) collective-permute-start(bf16[384,768]{1,0:T(8,128)(2,1)} %key.7), channel_id=1, source_target_pairs={{0,4},{4,0},{8,12},{12,8},{1,5},{5,1},{9,13},{13,9},{2,6},{6,2},{1... | collective-permute-start | bytes 1769480 | tf_op jit(solution)/shard_map/ppermute | solution.py:349
  0.0 3.1 %collective-permute-start.1 = (bf16[384,768]{1,0:T(8,128)(2,1)}, bf16[384,768]{1,0:T(8,128)(2,1)S(1)}, u32[]{:S(2)}, u32[]{:S(2)}) collective-permute-start(bf16[384,768]{1,0:T(8,128)(2,1)} %value.7), channel_id=1, source_target_pairs={{0,4},{4,0},{8,12},{12,8},{1,5},{5,1},{9,13},{13,9},{2,6},{6,2},{1... | collective-permute-start | bytes 1769480 | tf_op jit(solution)/shard_map/ppermute | solution.py:350
  1.6 6.6 %copy-start = (bf16[384,768]{1,0:T(8,128)(2,1)S(1)}, bf16[384,768]{1,0:T(8,128)(2,1)}, u32[]{:S(2)}) copy-start(bf16[384,768]{1,0:T(8,128)(2,1)} %key.7) | copy-start | bytes 1769476
  1.6 6.6 %copy-start.1 = (bf16[384,768]{1,0:T(8,128)(2,1)S(1)}, bf16[384,768]{1,0:T(8,128)(2,1)}, u32[]{:S(2)}) copy-start(bf16[384,768]{1,0:T(8,128)(2,1)} %value.7) | copy-start | bytes 1769476
  1.6 6.6 %collective-permute-start.2 = (bf16[96,768]{1,0:T(8,128)(2,1)S(1)}, bf16[96,768]{1,0:T(8,128)(2,1)S(1)}, u32[]{:S(2)}, u32[]{:S(2)}) collective-permute-start(bf16[96,768]{1,0:T(8,128)(2,1)S(1)} %get-tuple-element.54), channel_id=1, source_target_pairs={{8,0},{12,4},{9,1},{13,5},{10,2},{14,6},{11,3},{15,7},{24,16},{28,... | collective-permute-start | bytes 442376 | tf_op jit(solution)/shard_map/ppermute | solution.py:32
  5.9 12.0 %collective-permute-start.4 = (bf16[192,768]{1,0:T(8,128)(2,1)S(1)}, bf16[192,768]{1,0:T(8,128)(2,1)S(1)}, u32[]{:S(2)}, u32[]{:S(2)}) collective-permute-start(bf16[192,768]{1,0:T(8,128)(2,1)S(1)} %get-tuple-element.58), channel_id=1, source_target_pairs={{8,0},{12,4},{9,1},{13,5},{10,2},{14,6},{11,3},{15,7},{24,16},{28,... | collective-permute-start | bytes 884744 | tf_op jit(solution)/shard_map/ppermute | solution.py:32
  8.3 8.0 %collective-permute-start.3 = (bf16[96,896]{1,0:T(8,128)(2,1)S(1)}, bf16[96,896]{1,0:T(8,128)(2,1)S(1)}, u32[]{:S(2)}, u32[]{:S(2)}) collective-permute-start(bf16[96,896]{1,0:T(8,128)(2,1)S(1)} %served.2), channel_id=1, source_target_pairs={{0,8},{4,12},{1,9},{5,13},{2,10},{6,14},{3,11},{7,15},{16,24},{20,... | collective-permute-start | bytes 516104 | tf_op jit(solution)/shard_map/ppermute | solution.py:32
  12.0 5.9 %collective-permute-start.5 = (bf16[96,768]{1,0:T(8,128)(2,1)S(1)}, bf16[96,768]{1,0:T(8,128)(2,1)S(1)}, u32[]{:S(2)}, u32[]{:S(2)}) collective-permute-start(bf16[96,768]{1,0:T(8,128)(2,1)S(1)} %get-tuple-element.61), channel_id=1, source_target_pairs={{8,0},{12,4},{9,1},{13,5},{10,2},{14,6},{11,3},{15,7},{24,16},{28,... | collective-permute-start | bytes 442376 | tf_op jit(solution)/shard_map/ppermute | solution.py:32
  16.3 24.4 %collective-permute-start.8 = (bf16[96,3072]{1,0:T(8,128)(2,1)S(1)}, bf16[96,3072]{1,0:T(8,128)(2,1)}, u32[]{:S(2)}, u32[]{:S(2)}) collective-permute-start(bf16[96,3072]{1,0:T(8,128)(2,1)S(1)} %opening.2), channel_id=1, source_target_pairs={{0,1},{3,2},{4,5},{7,6},{8,9},{11,10},{12,13},{15,14},{16,17},{19,... | collective-permute-start | bytes 1769480 | tf_op jit(solution)/shard_map/ppermute | solution.py:437
  18.7 17.7 %collective-permute-start.6 = (bf16[288,896]{1,0:T(8,128)(2,1)}, bf16[288,896]{1,0:T(8,128)(2,1)S(1)}, u32[]{:S(2)}, u32[]{:S(2)}) collective-permute-start(bf16[288,896]{1,0:T(8,128)(2,1)} %served.3), channel_id=1, source_target_pairs={{0,8},{4,12},{1,9},{5,13},{2,10},{6,14},{3,11},{7,15},{16,24},{20,... | collective-permute-start | bytes 1548296 | tf_op jit(solution)/shard_map/ppermute | solution.py:32
  20.1 30.0 %collective-permute-start.7 = (bf16[96,3072]{1,0:T(8,128)(2,1)S(1)}, bf16[96,3072]{1,0:T(8,128)(2,1)S(1)}, u32[]{:S(2)}, u32[]{:S(2)}) collective-permute-start(bf16[96,3072]{1,0:T(8,128)(2,1)S(1)} %opening.3), channel_id=1, source_target_pairs={{0,1},{3,2},{4,5},{7,6},{8,9},{11,10},{12,13},{15,14},{16,17},{19,... | collective-permute-start | bytes 1769480 | tf_op jit(solution)/shard_map/ppermute | solution.py:441
  42.0 18.3 %collective-permute-start.11 = (bf16[96,3072]{1,0:T(8,128)(2,1)S(1)}, bf16[96,3072]{1,0:T(8,128)(2,1)S(1)}, u32[]{:S(2)}, u32[]{:S(2)}) collective-permute-start(bf16[96,3072]{1,0:T(8,128)(2,1)S(1)} %get-tuple-element.100), channel_id=1, source_target_pairs={{0,1},{1,2},{4,5},{5,6},{8,9},{9,10},{12,13},{13,14},{16,17},{17,1... | collective-permute-start | bytes 1769480 | tf_op jit(solution)/shard_map/ppermute | solution.py:480
  45.5 18.2 %collective-permute-start.12 = (bf16[96,3072]{1,0:T(8,128)(2,1)S(1)}, bf16[96,3072]{1,0:T(8,128)(2,1)S(1)}, u32[]{:S(2)}, u32[]{:S(2)}) collective-permute-start(bf16[96,3072]{1,0:T(8,128)(2,1)S(1)} %get-tuple-element.99), channel_id=1, source_target_pairs={{3,2},{2,1},{7,6},{6,5},{11,10},{10,9},{15,14},{14,13},{19,18},{18... | collective-permute-start | bytes 1769480 | tf_op jit(solution)/shard_map/ppermute | solution.py:481
  50.3 26.0 %collective-permute-start.10 = (bf16[96,3072]{1,0:T(8,128)(2,1)S(1)}, bf16[96,3072]{1,0:T(8,128)(2,1)S(1)}, u32[]{:S(2)}, u32[]{:S(2)}) collective-permute-start(bf16[96,3072]{1,0:T(8,128)(2,1)S(1)} %get-tuple-element.97), channel_id=1, source_target_pairs={{3,2},{2,1},{7,6},{6,5},{11,10},{10,9},{15,14},{14,13},{19,18},{18... | collective-permute-start | bytes 1769480 | tf_op jit(solution)/shard_map/ppermute | solution.py:481
  51.6 24.7 %collective-permute-start.9 = (bf16[96,3072]{1,0:T(8,128)(2,1)S(1)}, bf16[96,3072]{1,0:T(8,128)(2,1)S(1)}, u32[]{:S(2)}, u32[]{:S(2)}) collective-permute-start(bf16[96,3072]{1,0:T(8,128)(2,1)S(1)} %get-tuple-element.98), channel_id=1, source_target_pairs={{0,1},{1,2},{4,5},{5,6},{8,9},{9,10},{12,13},{13,14},{16,17},{17,1... | collective-permute-start | bytes 1769480 | tf_op jit(solution)/shard_map/ppermute | solution.py:480
  63.8 23.7 %collective-permute-start.13 = (bf16[96,3072]{1,0:T(8,128)(2,1)S(1)}, bf16[96,3072]{1,0:T(8,128)(2,1)S(1)}, u32[]{:S(2)}, u32[]{:S(2)}) collective-permute-start(bf16[96,3072]{1,0:T(8,128)(2,1)S(1)} %add_convert_fusion.3), channel_id=1, source_target_pairs={{0,1},{1,2},{2,3},{4,5},{5,6},{6,7},{8,9},{9,10},{10,11},{12,13},{... | collective-permute-start | bytes 1769480 | tf_op jit(solution)/shard_map/ppermute | solution.py:480
  65.9 23.0 %collective-permute-start.14 = (bf16[96,3072]{1,0:T(8,128)(2,1)S(1)}, bf16[96,3072]{1,0:T(8,128)(2,1)S(1)}, u32[]{:S(2)}, u32[]{:S(2)}) collective-permute-start(bf16[96,3072]{1,0:T(8,128)(2,1)S(1)} %add_convert_fusion.2), channel_id=1, source_target_pairs={{3,2},{2,1},{1,0},{7,6},{6,5},{5,4},{11,10},{10,9},{9,8},{15,14},{... | collective-permute-start | bytes 1769480 | tf_op jit(solution)/shard_map/ppermute | solution.py:481
  76.4 6.0 %copy-start.2 = (s32[4]{0:T(128)S(1)}, s32[4]{0:T(128)}, u32[]{:S(2)}) copy-start(s32[4]{0:T(128)} %levels.1) | copy-start | bytes 52
  76.4 22.5 %collective-permute-start.16 = (bf16[96,3072]{1,0:T(8,128)(2,1)S(1)}, bf16[96,3072]{1,0:T(8,128)(2,1)S(1)}, u32[]{:S(2)}, u32[]{:S(2)}) collective-permute-start(bf16[96,3072]{1,0:T(8,128)(2,1)S(1)} %add_convert_fusion), channel_id=1, source_target_pairs={{3,2},{2,1},{1,0},{7,6},{6,5},{5,4},{11,10},{10,9},{9,8},{15,14},{... | collective-permute-start | bytes 1769480 | tf_op jit(solution)/shard_map/ppermute | solution.py:481
  78.5 20.4 %collective-permute-start.15 = (bf16[96,3072]{1,0:T(8,128)(2,1)S(1)}, bf16[96,3072]{1,0:T(8,128)(2,1)S(1)}, u32[]{:S(2)}, u32[]{:S(2)}) collective-permute-start(bf16[96,3072]{1,0:T(8,128)(2,1)S(1)} %add_convert_fusion.1), channel_id=1, source_target_pairs={{0,1},{1,2},{2,3},{4,5},{5,6},{6,7},{8,9},{9,10},{10,11},{12,13},{... | collective-permute-start | bytes 1769480 | tf_op jit(solution)/shard_map/ppermute | solution.py:480

commit v22 on v21

--- a/solution.py
+++ b/solution.py
@@ -471,10 +471,12 @@
             else:
                 blocks = blocks_of(step, chunk, after(attended, before))
             comes, blocks = lax.optimization_barrier((arrived[chunk], blocks))
-            up, down = [
-                (mine.astype(f32) + come.astype(f32)).astype(bf16)
-                for mine, come in zip(blocks, (comes[0], comes[-1]))
-            ]
+            if step == 1 and chunk == 0:
+                down = (blocks[1].astype(f32) + comes[-1].astype(f32)).astype(bf16)
+                up = (after(blocks[0], down).astype(f32) + comes[0].astype(f32)).astype(bf16)
+            else:
+                up = (blocks[0].astype(f32) + comes[0].astype(f32)).astype(bf16)
+                down = (after(blocks[1], up).astype(f32) + comes[-1].astype(f32)).astype(bf16)
             before = (up, down)
             arrived[chunk] = [
                 lax.ppermute(up, "tensor", [(i, i + 1) for i in range(step + 1)]),

time: 101 us -> 101 us (level)
  waiting for transfers between devices: 31.2 us -> 27.9 us
  starting transfers between devices: 34.6 us -> 36 us
  other arithmetic: 2.49 us -> 3.66 us
    ppermute x4, waiting for transfers between devices: 17.5 us -> 7.36 us  [body(): lax.ppermute(down, 'tensor', [(last - i, last - i - 1) for i in range(ste...]
    ppermute x4, waiting for transfers between devices: 0.01 us -> 6.86 us  [body(): lax.ppermute(up, 'tensor', [(i, i + 1) for i in range(step + 1)])]
    ppermute x4, starting transfers between devices: 14.5 us -> 17.9 us  [body(): lax.ppermute(up, 'tensor', [(i, i + 1) for i in range(step + 1)])]
    ppermute x4, starting transfers between devices: 8.46 us -> 6.43 us  [body(): lax.ppermute(down, 'tensor', [(last - i, last - i - 1) for i in range(ste...]
    convert_element_type x6 -> x8, other arithmetic: 2.15 us -> 3.32 us  [the longest x1 1.22 us: body(): down = (blocks[1].astype(f32) + comes[-1].astype(f32)).astype(bf16)]
  transfers between devices with their start and end apart: 17 -> 17, of which waited for: 7 -> 8; matrix products, arithmetic and copies ran while one was open for 2% -> 4% of each run, Pallas kernels for 30% -> 30%
where the time goes in v22:
time: 101 us; the launch traced here: 99.4 us
  starting transfers between devices  36 us (36%)
  Pallas kernels  31.3 us (31%)
  waiting for transfers between devices  27.9 us (28%)
  other arithmetic  3.66 us (4%)
    ppermute x4, starting transfers between devices, body(): lax.ppermute(up, 'tensor', [(i, i + 1) for i in range(step + 1)])  17.9 us
    ppermute x5, waiting for transfers between devices, shifted(): lax.ppermute(block, axis, [(i, i + distance) for i in range(count) if 0 <...  13.6 us
    pallas_call x3, Pallas kernels, blocks_of(): pl.pallas_call(functools.partial(blocks_kernel, ranks, chunk * columns, s...  10.2 us
    ppermute x5, starting transfers between devices, shifted(): lax.ppermute(block, axis, [(i, i + distance) for i in range(count) if 0 <...  8.6 us
    ppermute x4, waiting for transfers between devices, body(): lax.ppermute(down, 'tensor', [(last - i, last - i - 1) for i in range(ste...  7.36 us
    ppermute x4, waiting for transfers between devices, body(): lax.ppermute(up, 'tensor', [(i, i + 1) for i in range(step + 1)])  6.86 us
    ppermute x4, starting transfers between devices, body(): lax.ppermute(down, 'tensor', [(last - i, last - i - 1) for i in range(ste...  6.43 us
    pallas_call x2, Pallas kernels, local(): pl.pallas_call(functools.partial(local_kernel, ranks, part), in_specs=[HB...  6.37 us
  transfers between devices with their start and end apart: 17, of which 8 were waited for; matrix products, arithmetic and copies ran while one was open for 4% of the time, Pallas kernels for 30%

profile of v22, /device:TPU:14, one launch (start us, length us, event | category | flops | bytes accessed | tf_op | source)
XLA Modules:
  0.0 99.4 jit_solution(12830239552885598802)
XLA Ops:
  0.0 0.5 collective-permute-start.1
  0.5 1.1 %split.1 = (bf16[96,768]{1,0:T(8,128)(2,1)S(1)}, bf16[192,768]{1,0:T(8,128)(2,1)S(1)}, bf16[96,768]{1,0:T(8,128)(2,1)S(1)}) custom-call(bf16[384,768]{1,0:T(8,128)(2,1)} %query.4), custom_call_target="tpu_custom_call" | custom-call | bytes 6273000 | tf_op jit(solution)/shard_map/split/pallas_call | solution.py:336
  1.6 0.0 copy-start
  1.6 0.0 copy-start.1
  1.6 1.5 %collective-permute-start.2 = (bf16[96,768]{1,0:T(8,128)(2,1)S(1)}, bf16[96,768]{1,0:T(8,128)(2,1)S(1)}, u32[]{:S(2)}, u32[]{:S(2)}) collective-permute-start(bf16[96,768]{1,0:T(8,128)(2,1)S(1)} %get-tuple-element.58), channel_id=1, source_target_pairs={{8,0},{12,4},{9,1},{13,5},{10,2},{14,6},{11,3},{15,7},{24,16},{28,... | collective-permute-start | bytes 442376 | tf_op jit(solution)/shard_map/ppermute | solution.py:32
  3.1 2.7 %local.2 = (f32[96,768]{1,0:T(8,128)S(1)}, f32[96,128]{1,0:T(8,128)S(1)}, s32[4,4]{1,0:T(4,128)S(1)}) custom-call(s32[4,4]{1,0:T(4,128)} %visible.3, bf16[384,768]{1,0:T(8,128)(2,1)} %query.4, bf16[384,768]{1,0:T(8,128)(2,1)} %key.7, bf16[384,768]{1,0:T(8,128)(2,1)} %value.7, bf16[384,768]{1,0:T(8,128)(2,1)S(1)} %collective-permute-done.key_beside, ...), custom_call_target="tpu_custom_call" | custom-call | bytes 14760000 | tf_op jit(solution)/shard_map/local/pallas_call | solution.py:357
  5.9 2.3 %collective-permute-start.4 = (bf16[192,768]{1,0:T(8,128)(2,1)S(1)}, bf16[192,768]{1,0:T(8,128)(2,1)S(1)}, u32[]{:S(2)}, u32[]{:S(2)}) collective-permute-start(bf16[192,768]{1,0:T(8,128)(2,1)S(1)} %get-tuple-element.62), channel_id=1, source_target_pairs={{8,0},{12,4},{9,1},{13,5},{10,2},{14,6},{11,3},{15,7},{24,16},{28,... | collective-permute-start | bytes 884744 | tf_op jit(solution)/shard_map/ppermute | solution.py:32
  8.3 1.3 %collective-permute-start.3 = (bf16[96,896]{1,0:T(8,128)(2,1)S(1)}, bf16[96,896]{1,0:T(8,128)(2,1)S(1)}, u32[]{:S(2)}, u32[]{:S(2)}) collective-permute-start(bf16[96,896]{1,0:T(8,128)(2,1)S(1)} %served.2), channel_id=1, source_target_pairs={{0,8},{4,12},{1,9},{5,13},{2,10},{6,14},{3,11},{7,15},{16,24},{20,... | collective-permute-start | bytes 516104 | tf_op jit(solution)/shard_map/ppermute | solution.py:32
  9.6 2.4 %fetch.2.refs_0_ = bf16[4,768,768]{2,1,0:T(8,128)(2,1)S(1)} custom-call(bf16[768,6144]{1,0:T(8,128)(2,1)} %weight.10), custom_call_target="tpu_custom_call" | custom-call | bytes 8856000 | tf_op jit(solution)/shard_map/fetch/pallas_call | solution.py:403
  12.0 2.2 %collective-permute-start.5 = (bf16[96,768]{1,0:T(8,128)(2,1)S(1)}, bf16[96,768]{1,0:T(8,128)(2,1)S(1)}, u32[]{:S(2)}, u32[]{:S(2)}) collective-permute-start(bf16[96,768]{1,0:T(8,128)(2,1)S(1)} %get-tuple-element.65), channel_id=1, source_target_pairs={{8,0},{12,4},{9,1},{13,5},{10,2},{14,6},{11,3},{15,7},{24,16},{28,... | collective-permute-start | bytes 442376 | tf_op jit(solution)/shard_map/ppermute | solution.py:32
  14.2 0.1 fetch.3.refs_3_
  14.2 2.0 %collective-permute-done.3.refs_2_ = bf16[96,896]{1,0:T(8,128)(2,1)S(1)} collective-permute-done((bf16[96,896]{1,0:T(8,128)(2,1)S(1)}, bf16[96,896]{1,0:T(8,128)(2,1)S(1)}, u32[]{:S(2)}, u32[]{:S(2)}) %collective-permute-start.3) | collective-permute-done | bytes 172064 | tf_op jit(solution)/shard_map/ppermute | solution.py:32
  16.3 1.3 %collective-permute-start.8 = (bf16[96,3072]{1,0:T(8,128)(2,1)S(1)}, bf16[96,3072]{1,0:T(8,128)(2,1)}, u32[]{:S(2)}, u32[]{:S(2)}) collective-permute-start(bf16[96,3072]{1,0:T(8,128)(2,1)S(1)} %opening.2), channel_id=1, source_target_pairs={{0,1},{3,2},{4,5},{7,6},{8,9},{11,10},{12,13},{15,14},{16,17},{19,... | collective-permute-start | bytes 1769480 | tf_op jit(solution)/shard_map/ppermute | solution.py:437
  17.6 0.3 collective-permute-done.5.refs_1_
  17.9 0.8 served.3
  18.7 1.3 %collective-permute-start.6 = (bf16[288,896]{1,0:T(8,128)(2,1)}, bf16[288,896]{1,0:T(8,128)(2,1)S(1)}, u32[]{:S(2)}, u32[]{:S(2)}) collective-permute-start(bf16[288,896]{1,0:T(8,128)(2,1)} %served.3), channel_id=1, source_target_pairs={{0,8},{4,12},{1,9},{5,13},{2,10},{6,14},{3,11},{7,15},{16,24},{20,... | collective-permute-start | bytes 1548296 | tf_op jit(solution)/shard_map/ppermute | solution.py:32
  20.0 0.1 pad_add_fusion.place
  20.1 1.3 %collective-permute-start.7 = (bf16[96,3072]{1,0:T(8,128)(2,1)S(1)}, bf16[96,3072]{1,0:T(8,128)(2,1)S(1)}, u32[]{:S(2)}, u32[]{:S(2)}) collective-permute-start(bf16[96,3072]{1,0:T(8,128)(2,1)S(1)} %opening.3), channel_id=1, source_target_pairs={{0,1},{3,2},{4,5},{7,6},{8,9},{11,10},{12,13},{15,14},{16,17},{19,... | collective-permute-start | bytes 1769480 | tf_op jit(solution)/shard_map/ppermute | solution.py:441
  21.4 3.7 %local.3 = (f32[288,768]{1,0:T(8,128)S(1)}, f32[288,128]{1,0:T(8,128)S(1)}, s32[4,4]{1,0:T(4,128)}) custom-call(s32[4,4]{1,0:T(4,128)} %visible.3, bf16[384,768]{1,0:T(8,128)(2,1)} %query.4, bf16[384,768]{1,0:T(8,128)(2,1)} %key.7, bf16[384,768]{1,0:T(8,128)(2,1)} %value.7, bf16[384,768]{1,0:T(8,128)(2,1)S(1)} %collective-permute-done.key_beside, ...), custom_call_target="tpu_custom_call" | custom-call | bytes 14760000 | tf_op jit(solution)/shard_map/local/pallas_call | solution.py:357
  25.1 11.3 %collective-permute-done.6.refs_5_ = bf16[288,896]{1,0:T(8,128)(2,1)S(1)} collective-permute-done((bf16[288,896]{1,0:T(8,128)(2,1)}, bf16[288,896]{1,0:T(8,128)(2,1)S(1)}, u32[]{:S(2)}, u32[]{:S(2)}) %collective-permute-start.6) | collective-permute-done | bytes 516128 | tf_op jit(solution)/shard_map/ppermute | solution.py:32
  36.3 4.3 %merged_blocks.1 = (bf16[384,768]{1,0:T(8,128)(2,1)S(1)}, bf16[96,3072]{1,0:T(8,128)(2,1)S(1)}, bf16[96,3072]{1,0:T(8,128)(2,1)S(1)}) custom-call(s32[2]{0:T(128)S(1)} %pad_add_fusion.place, f32[96,768]{1,0:T(8,128)S(1)} %get-tuple-element.55.refs_0_, f32[96,128]{1,0:T(8,128)S(1)} %get-tuple-element.56.refs_1_, ...), custom_call_target="tpu_custom_call" | custom-call | bytes 11070000 | tf_op jit(solution)/shard_map/merged_blocks/pallas_call | solution.py:447
  40.7 1.2 %fusion = bf16[96,3072]{1,0:T(8,128)(2,1)S(1)} fusion(bf16[96,3072]{1,0:T(8,128)(2,1)} %collective-permute-done.8, bf16[96,3072]{1,0:T(8,128)(2,1)S(1)} %get-tuple-element.76), kind=kLoop, calls=%fused_computation.4 | loop fusion | flops 1179648 | bytes 1769472 | tf_op jit(solution)/shard_map/convert_element_type | solution.py:475
  41.9 1.3 %collective-permute-start.12 = (bf16[96,3072]{1,0:T(8,128)(2,1)S(1)}, bf16[96,3072]{1,0:T(8,128)(2,1)S(1)}, u32[]{:S(2)}, u32[]{:S(2)}) collective-permute-start(bf16[96,3072]{1,0:T(8,128)(2,1)S(1)} %fusion), channel_id=1, source_target_pairs={{3,2},{2,1},{7,6},{6,5},{11,10},{10,9},{15,14},{14,13},{19,18},{18... | collective-permute-start | bytes 1769480 | tf_op jit(solution)/shard_map/ppermute | solution.py:483
  43.2 1.2 %fusion.1 = bf16[96,3072]{1,0:T(8,128)(2,1)S(1)} fusion(bf16[96,3072]{1,0:T(8,128)(2,1)} %collective-permute-done.8, bf16[96,3072]{1,0:T(8,128)(2,1)S(1)} %get-tuple-element.78), kind=kLoop, calls=%fused_computation.5 | loop fusion | flops 1179648 | bytes 1769472 | tf_op jit(solution)/shard_map/convert_element_type | solution.py:476
  44.4 4.6 %collective-permute-start.11 = (bf16[96,3072]{1,0:T(8,128)(2,1)S(1)}, bf16[96,3072]{1,0:T(8,128)(2,1)S(1)}, u32[]{:S(2)}, u32[]{:S(2)}) collective-permute-start(bf16[96,3072]{1,0:T(8,128)(2,1)S(1)} %fusion.1), channel_id=1, source_target_pairs={{0,1},{1,2},{4,5},{5,6},{8,9},{9,10},{12,13},{13,14},{16,17},{17,1... | collective-permute-start | bytes 1769480 | tf_op jit(solution)/shard_map/ppermute | solution.py:482
  49.0 3.3 %blocks.3 = (bf16[96,3072]{1,0:T(8,128)(2,1)S(1)}, bf16[96,3072]{1,0:T(8,128)(2,1)S(1)}) custom-call(s32[2]{0:T(128)S(1)} %pad_add_fusion.place, bf16[384,768]{1,0:T(8,128)(2,1)S(1)} %get-tuple-element.102.attended, bf16[768,6144]{1,0:T(8,128)(2,1)} %weight.10), custom_call_target="tpu_custom_call" | custom-call | bytes 11070000 | tf_op jit(solution)/shard_map/blocks/pallas_call | solution.py:457
  52.3 0.2 fusion.2
  52.4 0.2 fusion.3
  52.6 1.3 %collective-permute-start.10 = (bf16[96,3072]{1,0:T(8,128)(2,1)S(1)}, bf16[96,3072]{1,0:T(8,128)(2,1)S(1)}, u32[]{:S(2)}, u32[]{:S(2)}) collective-permute-start(bf16[96,3072]{1,0:T(8,128)(2,1)S(1)} %fusion.3), channel_id=1, source_target_pairs={{3,2},{2,1},{7,6},{6,5},{11,10},{10,9},{15,14},{14,13},{19,18},{18... | collective-permute-start | bytes 1769480 | tf_op jit(solution)/shard_map/ppermute | solution.py:483
  53.9 4.6 %collective-permute-start.9 = (bf16[96,3072]{1,0:T(8,128)(2,1)S(1)}, bf16[96,3072]{1,0:T(8,128)(2,1)S(1)}, u32[]{:S(2)}, u32[]{:S(2)}) collective-permute-start(bf16[96,3072]{1,0:T(8,128)(2,1)S(1)} %fusion.2), channel_id=1, source_target_pairs={{0,1},{1,2},{4,5},{5,6},{8,9},{9,10},{12,13},{13,14},{16,17},{17,1... | collective-permute-start | bytes 1769480 | tf_op jit(solution)/shard_map/ppermute | solution.py:482
  58.5 3.4 %blocks.4 = (bf16[96,3072]{1,0:T(8,128)(2,1)S(1)}, bf16[96,3072]{1,0:T(8,128)(2,1)S(1)}) custom-call(s32[2]{0:T(128)S(1)} %pad_add_fusion.place, bf16[384,768]{1,0:T(8,128)(2,1)S(1)} %get-tuple-element.102.attended, bf16[768,6144]{1,0:T(8,128)(2,1)} %weight.10), custom_call_target="tpu_custom_call" | custom-call | bytes 11070000 | tf_op jit(solution)/shard_map/blocks/pallas_call | solution.py:457
  61.9 0.8 collective-permute-done.11
  62.8 0.1 add_convert_fusion.3
  62.9 0.1 add_convert_fusion.2
  63.1 1.9 %collective-permute-start.14 = (bf16[96,3072]{1,0:T(8,128)(2,1)S(1)}, bf16[96,3072]{1,0:T(8,128)(2,1)S(1)}, u32[]{:S(2)}, u32[]{:S(2)}) collective-permute-start(bf16[96,3072]{1,0:T(8,128)(2,1)S(1)} %add_convert_fusion.2), channel_id=1, source_target_pairs={{3,2},{2,1},{1,0},{7,6},{6,5},{5,4},{11,10},{10,9},{9,8},{15,14},{... | collective-permute-start | bytes 1769480 | tf_op jit(solution)/shard_map/ppermute | solution.py:483
  65.0 4.4 %collective-permute-start.13 = (bf16[96,3072]{1,0:T(8,128)(2,1)S(1)}, bf16[96,3072]{1,0:T(8,128)(2,1)S(1)}, u32[]{:S(2)}, u32[]{:S(2)}) collective-permute-start(bf16[96,3072]{1,0:T(8,128)(2,1)S(1)} %add_convert_fusion.3), channel_id=1, source_target_pairs={{0,1},{1,2},{2,3},{4,5},{5,6},{6,7},{8,9},{9,10},{10,11},{12,13},{... | collective-permute-start | bytes 1769480 | tf_op jit(solution)/shard_map/ppermute | solution.py:482
  69.4 3.4 %blocks.5 = (bf16[96,3072]{1,0:T(8,128)(2,1)S(1)}, bf16[96,3072]{1,0:T(8,128)(2,1)S(1)}) custom-call(s32[2]{0:T(128)S(1)} %pad_add_fusion.place, bf16[384,768]{1,0:T(8,128)(2,1)S(1)} %get-tuple-element.102.attended, bf16[768,6144]{1,0:T(8,128)(2,1)} %weight.10), custom_call_target="tpu_custom_call" | custom-call | bytes 11070000 | tf_op jit(solution)/shard_map/blocks/pallas_call | solution.py:457
  72.9 2.5 %collective-permute-done.9 = bf16[96,3072]{1,0:T(8,128)(2,1)S(1)} collective-permute-done((bf16[96,3072]{1,0:T(8,128)(2,1)S(1)}, bf16[96,3072]{1,0:T(8,128)(2,1)S(1)}, u32[]{:S(2)}, u32[]{:S(2)}) %collective-permute-start.9) | collective-permute-done | bytes 589856 | tf_op jit(solution)/shard_map/ppermute | solution.py:482
  75.4 0.2 add_convert_fusion.1
  75.6 0.1 add_convert_fusion
  75.7 1.9 %collective-permute-start.16 = (bf16[96,3072]{1,0:T(8,128)(2,1)S(1)}, bf16[96,3072]{1,0:T(8,128)(2,1)S(1)}, u32[]{:S(2)}, u32[]{:S(2)}) collective-permute-start(bf16[96,3072]{1,0:T(8,128)(2,1)S(1)} %add_convert_fusion), channel_id=1, source_target_pairs={{3,2},{2,1},{1,0},{7,6},{6,5},{5,4},{11,10},{10,9},{9,8},{15,14},{... | collective-permute-start | bytes 1769480 | tf_op jit(solution)/shard_map/ppermute | solution.py:483
  77.7 4.4 %collective-permute-start.15 = (bf16[96,3072]{1,0:T(8,128)(2,1)S(1)}, bf16[96,3072]{1,0:T(8,128)(2,1)S(1)}, u32[]{:S(2)}, u32[]{:S(2)}) collective-permute-start(bf16[96,3072]{1,0:T(8,128)(2,1)S(1)} %add_convert_fusion.1), channel_id=1, source_target_pairs={{0,1},{1,2},{2,3},{4,5},{5,6},{6,7},{8,9},{9,10},{10,11},{12,13},{... | collective-permute-start | bytes 1769480 | tf_op jit(solution)/shard_map/ppermute | solution.py:482
  82.1 5.0 %own.1 = (bf16[96,6144]{1,0:T(8,128)(2,1)S(1)}, f32[1,6144]{1,0:T(1,128)S(1)}) custom-call(s32[2]{0:T(128)S(1)} %pad_add_fusion.place, s32[4]{0:T(128)S(1)} %copy-done.2, bf16[384,768]{1,0:T(8,128)(2,1)S(1)} %get-tuple-element.102.attended, bf16[768,6144]{1,0:T(8,128)(2,1)} %weight.10, f32[64,6144]{1,0:T(8,128)} %gate_table.1), custom_call_target="tpu_custom_call" | custom-call | bytes 18450000 | tf_op jit(solution)/shard_map/own/pallas_call | solution.py:486
  87.1 1.0 collective-permute-done.13
  88.0 0.3 multiply_convert_fusion.done
  88.3 7.3 %collective-permute-done.16.down = bf16[96,3072]{1,0:T(8,128)(2,1)S(1)} collective-permute-done((bf16[96,3072]{1,0:T(8,128)(2,1)S(1)}, bf16[96,3072]{1,0:T(8,128)(2,1)S(1)}, u32[]{:S(2)}, u32[]{:S(2)}) %collective-permute-start.16) | collective-permute-done | bytes 589856 | tf_op jit(solution)/shard_map/ppermute | solution.py:483
  95.6 2.5 %collective-permute-done.15.up = bf16[96,3072]{1,0:T(8,128)(2,1)S(1)} collective-permute-done((bf16[96,3072]{1,0:T(8,128)(2,1)S(1)}, bf16[96,3072]{1,0:T(8,128)(2,1)S(1)}, u32[]{:S(2)}, u32[]{:S(2)}) %collective-permute-start.15) | collective-permute-done | bytes 589856 | tf_op jit(solution)/shard_map/ppermute | solution.py:482
  98.2 1.1 %final.1 = bf16[96,6144]{1,0:T(8,128)(2,1)} custom-call(bf16[96,3072]{1,0:T(8,128)(2,1)S(1)} %multiply_convert_fusion.done, bf16[96,6144]{1,0:T(8,128)(2,1)S(1)} %get-tuple-element.103.projected, f32[1,6144]{1,0:T(1,128)S(1)} %get-tuple-element.104.gate, bf16[96,3072]{1,0:T(8,128)(2,1)S(1)} %collective-permute-done.15.up, ...), custom_call_target="tpu_custom_call" | custom-call | bytes 9963000 | tf_op jit(solution)/shard_map/final/pallas_call | solution.py:507
  (18 shorter events, 0.1 us)
Async XLA Ops:
  0.0 3.1 %collective-permute-start = (bf16[384,768]{1,0:T(8,128)(2,1)}, bf16[384,768]{1,0:T(8,128)(2,1)S(1)}, u32[]{:S(2)}, u32[]{:S(2)}) collective-permute-start(bf16[384,768]{1,0:T(8,128)(2,1)} %key.7), channel_id=1, source_target_pairs={{0,4},{4,0},{8,12},{12,8},{1,5},{5,1},{9,13},{13,9},{2,6},{6,2},{1... | collective-permute-start | bytes 1769480 | tf_op jit(solution)/shard_map/ppermute | solution.py:349
  0.0 3.1 %collective-permute-start.1 = (bf16[384,768]{1,0:T(8,128)(2,1)}, bf16[384,768]{1,0:T(8,128)(2,1)S(1)}, u32[]{:S(2)}, u32[]{:S(2)}) collective-permute-start(bf16[384,768]{1,0:T(8,128)(2,1)} %value.7), channel_id=1, source_target_pairs={{0,4},{4,0},{8,12},{12,8},{1,5},{5,1},{9,13},{13,9},{2,6},{6,2},{1... | collective-permute-start | bytes 1769480 | tf_op jit(solution)/shard_map/ppermute | solution.py:350
  1.6 6.6 %copy-start = (bf16[384,768]{1,0:T(8,128)(2,1)S(1)}, bf16[384,768]{1,0:T(8,128)(2,1)}, u32[]{:S(2)}) copy-start(bf16[384,768]{1,0:T(8,128)(2,1)} %key.7) | copy-start | bytes 1769476
  1.6 6.6 %copy-start.1 = (bf16[384,768]{1,0:T(8,128)(2,1)S(1)}, bf16[384,768]{1,0:T(8,128)(2,1)}, u32[]{:S(2)}) copy-start(bf16[384,768]{1,0:T(8,128)(2,1)} %value.7) | copy-start | bytes 1769476
  1.6 6.6 %collective-permute-start.2 = (bf16[96,768]{1,0:T(8,128)(2,1)S(1)}, bf16[96,768]{1,0:T(8,128)(2,1)S(1)}, u32[]{:S(2)}, u32[]{:S(2)}) collective-permute-start(bf16[96,768]{1,0:T(8,128)(2,1)S(1)} %get-tuple-element.58), channel_id=1, source_target_pairs={{8,0},{12,4},{9,1},{13,5},{10,2},{14,6},{11,3},{15,7},{24,16},{28,... | collective-permute-start | bytes 442376 | tf_op jit(solution)/shard_map/ppermute | solution.py:32
  5.9 12.0 %collective-permute-start.4 = (bf16[192,768]{1,0:T(8,128)(2,1)S(1)}, bf16[192,768]{1,0:T(8,128)(2,1)S(1)}, u32[]{:S(2)}, u32[]{:S(2)}) collective-permute-start(bf16[192,768]{1,0:T(8,128)(2,1)S(1)} %get-tuple-element.62), channel_id=1, source_target_pairs={{8,0},{12,4},{9,1},{13,5},{10,2},{14,6},{11,3},{15,7},{24,16},{28,... | collective-permute-start | bytes 884744 | tf_op jit(solution)/shard_map/ppermute | solution.py:32
  8.3 8.0 %collective-permute-start.3 = (bf16[96,896]{1,0:T(8,128)(2,1)S(1)}, bf16[96,896]{1,0:T(8,128)(2,1)S(1)}, u32[]{:S(2)}, u32[]{:S(2)}) collective-permute-start(bf16[96,896]{1,0:T(8,128)(2,1)S(1)} %served.2), channel_id=1, source_target_pairs={{0,8},{4,12},{1,9},{5,13},{2,10},{6,14},{3,11},{7,15},{16,24},{20,... | collective-permute-start | bytes 516104 | tf_op jit(solution)/shard_map/ppermute | solution.py:32
  12.0 5.9 %collective-permute-start.5 = (bf16[96,768]{1,0:T(8,128)(2,1)S(1)}, bf16[96,768]{1,0:T(8,128)(2,1)S(1)}, u32[]{:S(2)}, u32[]{:S(2)}) collective-permute-start(bf16[96,768]{1,0:T(8,128)(2,1)S(1)} %get-tuple-element.65), channel_id=1, source_target_pairs={{8,0},{12,4},{9,1},{13,5},{10,2},{14,6},{11,3},{15,7},{24,16},{28,... | collective-permute-start | bytes 442376 | tf_op jit(solution)/shard_map/ppermute | solution.py:32
  16.3 24.4 %collective-permute-start.8 = (bf16[96,3072]{1,0:T(8,128)(2,1)S(1)}, bf16[96,3072]{1,0:T(8,128)(2,1)}, u32[]{:S(2)}, u32[]{:S(2)}) collective-permute-start(bf16[96,3072]{1,0:T(8,128)(2,1)S(1)} %opening.2), channel_id=1, source_target_pairs={{0,1},{3,2},{4,5},{7,6},{8,9},{11,10},{12,13},{15,14},{16,17},{19,... | collective-permute-start | bytes 1769480 | tf_op jit(solution)/shard_map/ppermute | solution.py:437
  18.7 17.7 %collective-permute-start.6 = (bf16[288,896]{1,0:T(8,128)(2,1)}, bf16[288,896]{1,0:T(8,128)(2,1)S(1)}, u32[]{:S(2)}, u32[]{:S(2)}) collective-permute-start(bf16[288,896]{1,0:T(8,128)(2,1)} %served.3), channel_id=1, source_target_pairs={{0,8},{4,12},{1,9},{5,13},{2,10},{6,14},{3,11},{7,15},{16,24},{20,... | collective-permute-start | bytes 1548296 | tf_op jit(solution)/shard_map/ppermute | solution.py:32
  20.1 32.2 %collective-permute-start.7 = (bf16[96,3072]{1,0:T(8,128)(2,1)S(1)}, bf16[96,3072]{1,0:T(8,128)(2,1)S(1)}, u32[]{:S(2)}, u32[]{:S(2)}) collective-permute-start(bf16[96,3072]{1,0:T(8,128)(2,1)S(1)} %opening.3), channel_id=1, source_target_pairs={{0,1},{3,2},{4,5},{7,6},{8,9},{11,10},{12,13},{15,14},{16,17},{19,... | collective-permute-start | bytes 1769480 | tf_op jit(solution)/shard_map/ppermute | solution.py:441
  41.9 20.8 %collective-permute-start.12 = (bf16[96,3072]{1,0:T(8,128)(2,1)S(1)}, bf16[96,3072]{1,0:T(8,128)(2,1)S(1)}, u32[]{:S(2)}, u32[]{:S(2)}) collective-permute-start(bf16[96,3072]{1,0:T(8,128)(2,1)S(1)} %fusion), channel_id=1, source_target_pairs={{3,2},{2,1},{7,6},{6,5},{11,10},{10,9},{15,14},{14,13},{19,18},{18... | collective-permute-start | bytes 1769480 | tf_op jit(solution)/shard_map/ppermute | solution.py:483
  44.4 18.3 %collective-permute-start.11 = (bf16[96,3072]{1,0:T(8,128)(2,1)S(1)}, bf16[96,3072]{1,0:T(8,128)(2,1)S(1)}, u32[]{:S(2)}, u32[]{:S(2)}) collective-permute-start(bf16[96,3072]{1,0:T(8,128)(2,1)S(1)} %fusion.1), channel_id=1, source_target_pairs={{0,1},{1,2},{4,5},{5,6},{8,9},{9,10},{12,13},{13,14},{16,17},{17,1... | collective-permute-start | bytes 1769480 | tf_op jit(solution)/shard_map/ppermute | solution.py:482
  52.6 20.2 %collective-permute-start.10 = (bf16[96,3072]{1,0:T(8,128)(2,1)S(1)}, bf16[96,3072]{1,0:T(8,128)(2,1)S(1)}, u32[]{:S(2)}, u32[]{:S(2)}) collective-permute-start(bf16[96,3072]{1,0:T(8,128)(2,1)S(1)} %fusion.3), channel_id=1, source_target_pairs={{3,2},{2,1},{7,6},{6,5},{11,10},{10,9},{15,14},{14,13},{19,18},{18... | collective-permute-start | bytes 1769480 | tf_op jit(solution)/shard_map/ppermute | solution.py:483
  53.9 21.5 %collective-permute-start.9 = (bf16[96,3072]{1,0:T(8,128)(2,1)S(1)}, bf16[96,3072]{1,0:T(8,128)(2,1)S(1)}, u32[]{:S(2)}, u32[]{:S(2)}) collective-permute-start(bf16[96,3072]{1,0:T(8,128)(2,1)S(1)} %fusion.2), channel_id=1, source_target_pairs={{0,1},{1,2},{4,5},{5,6},{8,9},{9,10},{12,13},{13,14},{16,17},{17,1... | collective-permute-start | bytes 1769480 | tf_op jit(solution)/shard_map/ppermute | solution.py:482
  63.1 24.0 %collective-permute-start.14 = (bf16[96,3072]{1,0:T(8,128)(2,1)S(1)}, bf16[96,3072]{1,0:T(8,128)(2,1)S(1)}, u32[]{:S(2)}, u32[]{:S(2)}) collective-permute-start(bf16[96,3072]{1,0:T(8,128)(2,1)S(1)} %add_convert_fusion.2), channel_id=1, source_target_pairs={{3,2},{2,1},{1,0},{7,6},{6,5},{5,4},{11,10},{10,9},{9,8},{15,14},{... | collective-permute-start | bytes 1769480 | tf_op jit(solution)/shard_map/ppermute | solution.py:483
  65.0 23.0 %collective-permute-start.13 = (bf16[96,3072]{1,0:T(8,128)(2,1)S(1)}, bf16[96,3072]{1,0:T(8,128)(2,1)S(1)}, u32[]{:S(2)}, u32[]{:S(2)}) collective-permute-start(bf16[96,3072]{1,0:T(8,128)(2,1)S(1)} %add_convert_fusion.3), channel_id=1, source_target_pairs={{0,1},{1,2},{2,3},{4,5},{5,6},{6,7},{8,9},{9,10},{10,11},{12,13},{... | collective-permute-start | bytes 1769480 | tf_op jit(solution)/shard_map/ppermute | solution.py:482
  75.6 6.5 %copy-start.2 = (s32[4]{0:T(128)S(1)}, s32[4]{0:T(128)}, u32[]{:S(2)}) copy-start(s32[4]{0:T(128)} %levels.1) | copy-start | bytes 52
  75.7 19.9 %collective-permute-start.16 = (bf16[96,3072]{1,0:T(8,128)(2,1)S(1)}, bf16[96,3072]{1,0:T(8,128)(2,1)S(1)}, u32[]{:S(2)}, u32[]{:S(2)}) collective-permute-start(bf16[96,3072]{1,0:T(8,128)(2,1)S(1)} %add_convert_fusion), channel_id=1, source_target_pairs={{3,2},{2,1},{1,0},{7,6},{6,5},{5,4},{11,10},{10,9},{9,8},{15,14},{... | collective-permute-start | bytes 1769480 | tf_op jit(solution)/shard_map/ppermute | solution.py:483
  77.7 20.5 %collective-permute-start.15 = (bf16[96,3072]{1,0:T(8,128)(2,1)S(1)}, bf16[96,3072]{1,0:T(8,128)(2,1)S(1)}, u32[]{:S(2)}, u32[]{:S(2)}) collective-permute-start(bf16[96,3072]{1,0:T(8,128)(2,1)S(1)} %add_convert_fusion.1), channel_id=1, source_target_pairs={{0,1},{1,2},{2,3},{4,5},{5,6},{6,7},{8,9},{9,10},{10,11},{12,13},{... | collective-permute-start | bytes 1769480 | tf_op jit(solution)/shard_map/ppermute | solution.py:482

commit v23 on v21

--- a/solution.py
+++ b/solution.py
@@ -201,14 +201,9 @@
     ]
 
 
-def fetch_kernel(askers, weight, *refs):
-    tiles, semaphores = refs[-2:]
-    span, _ = place_here()
-
-    @pl.when(span > 1 if askers else span < 2)
-    def _():
-        for copy in streamed(weight, 0, tiles, semaphores):
-            copy.wait()
+def fetch_kernel(weight, tiles, semaphores):
+    for copy in streamed(weight, 0, tiles, semaphores):
+        copy.wait()
 
 
 def opening_kernel(ranks, distances, first, *refs):
@@ -385,6 +380,10 @@
     *early, seen = local(0, queries)
     query_late = after(query_late, early)
     asked_early = after(asked_early, early)
+    asked_late = [[shifted(query, "span", -distance) for query in query_late] for distance in distances]
+    out_early = [served([q], d) for q, d in zip(asked_early, distances)]
+    early += [shifted(o, "span", d) for o, d in zip(out_early, distances)]
+
     chunks = 2
     columns = model // chunks
     tiles = 4
@@ -398,26 +397,16 @@
         compiler_params=PARAMS,
         cost_estimate=taking(3.0),
     )
-
-    def fetch(askers, weight, *before):
-        return pl.pallas_call(
-            functools.partial(fetch_kernel, askers),
-            in_specs=[HBM] + [VMEM] * len(before),
-            out_specs=VMEM,
-            out_shape=jax.ShapeDtypeStruct(tile_shape, bf16),
-            input_output_aliases={1: 0} if before else {},
-            scratch_shapes=[pltpu.SemaphoreType.DMA((tiles,))],
-            compiler_params=PARAMS,
-            cost_estimate=taking(2.4),
-            name="fetch",
-        )(in_hbm(weight), *before)
-
-    out_early = [served([q], d) for q, d in zip(asked_early, distances)]
-    early += [shifted(o, "span", d) for o, d in zip(out_early, distances)]
-    fetched = fetch(True, after(out_weight, out_early))
-    query_late = [query_late[0], after(query_late[1], fetched)]
-    asked_late = [[shifted(query, "span", -distance) for query in query_late] for distance in distances]
-    fetched = fetch(False, out_weight, fetched)
+    fetched = pl.pallas_call(
+        fetch_kernel,
+        in_specs=[HBM],
+        out_specs=VMEM,
+        out_shape=jax.ShapeDtypeStruct(tile_shape, bf16),
+        scratch_shapes=[pltpu.SemaphoreType.DMA((tiles,))],
+        compiler_params=PARAMS,
+        cost_estimate=taking(2.4),
+        name="fetch",
+    )(in_hbm(after(out_weight, out_early)))
 
     def opening(chunk, weight):
         scratch = streaming["scratch_shapes"] if chunk else []

time: 101 us -> 101 us (level)
  starting transfers between devices: 34.6 us -> 37 us
  waiting for transfers between devices: 31.2 us -> 28.9 us
    ppermute x5, starting transfers between devices: 8.6 us -> 10.9 us  [shifted(): lax.ppermute(block, axis, [(i, i + distance) for i in range(count) if 0 <...]
    ppermute x5, waiting for transfers between devices: 13.6 us -> 11.3 us  [shifted(): lax.ppermute(block, axis, [(i, i + distance) for i in range(count) if 0 <...]
    pallas_call x2 -> x1, Pallas kernels: 2.46 us -> 2.39 us  [body(): pl.pallas_call(fetch_kernel, in_specs=[HBM], out_specs=VMEM, out_shape=ja...]
  transfers between devices with their start and end apart: 17 -> 17, of which waited for: 7 -> 5; matrix products, arithmetic and copies ran while one was open for 2% -> 2% of each run, Pallas kernels for 30% -> 30%
where the time goes in v23:
time: 101 us; the launch traced here: 100 us
  starting transfers between devices  37 us (37%)
  Pallas kernels  31.3 us (31%)
  waiting for transfers between devices  28.9 us (29%)
  other arithmetic  2.49 us (2%)
    ppermute x4, waiting for transfers between devices, body(): lax.ppermute(down, 'tensor', [(last - i, last - i - 1) for i in range(ste...  17.5 us
    ppermute x4, starting transfers between devices, body(): lax.ppermute(up, 'tensor', [(i, i + 1) for i in range(step + 1)])  14.5 us
    ppermute x5, waiting for transfers between devices, shifted(): lax.ppermute(block, axis, [(i, i + distance) for i in range(count) if 0 <...  11.3 us
    ppermute x5, starting transfers between devices, shifted(): lax.ppermute(block, axis, [(i, i + distance) for i in range(count) if 0 <...  10.9 us
    pallas_call x3, Pallas kernels, blocks_of(): pl.pallas_call(functools.partial(blocks_kernel, ranks, chunk * columns, s...  10.2 us
    ppermute x4, starting transfers between devices, body(): lax.ppermute(down, 'tensor', [(last - i, last - i - 1) for i in range(ste...  8.46 us
    pallas_call x2, Pallas kernels, local(): pl.pallas_call(functools.partial(local_kernel, ranks, part), in_specs=[HB...  6.37 us
    pallas_call x1, Pallas kernels, body(): pl.pallas_call(own_kernel, in_specs=[SMEM, SMEM, VMEM, HBM, HBM], out_spe...  4.99 us
  transfers between devices with their start and end apart: 17, of which 5 were waited for; matrix products, arithmetic and copies ran while one was open for 2% of the time, Pallas kernels for 30%

profile of v23, /device:TPU:14, one launch (start us, length us, event | category | flops | bytes accessed | tf_op | source)
XLA Modules:
  0.0 100.2 jit_solution(7369580628804591029)
XLA Ops:
  0.0 0.5 collective-permute-start.1
  0.5 1.1 %split.1 = (bf16[96,768]{1,0:T(8,128)(2,1)S(1)}, bf16[192,768]{1,0:T(8,128)(2,1)S(1)}, bf16[96,768]{1,0:T(8,128)(2,1)S(1)}) custom-call(bf16[384,768]{1,0:T(8,128)(2,1)} %query.4), custom_call_target="tpu_custom_call" | custom-call | bytes 6273000 | tf_op jit(solution)/shard_map/split/pallas_call | solution.py:331
  1.6 0.0 copy-start
  1.6 0.0 copy-start.1
  1.6 1.5 %collective-permute-start.2 = (bf16[96,768]{1,0:T(8,128)(2,1)S(1)}, bf16[96,768]{1,0:T(8,128)(2,1)S(1)}, u32[]{:S(2)}, u32[]{:S(2)}) collective-permute-start(bf16[96,768]{1,0:T(8,128)(2,1)S(1)} %get-tuple-element.53), channel_id=1, source_target_pairs={{8,0},{12,4},{9,1},{13,5},{10,2},{14,6},{11,3},{15,7},{24,16},{28,... | collective-permute-start | bytes 442376 | tf_op jit(solution)/shard_map/ppermute | solution.py:32
  3.1 0.0 collective-permute-done.key_beside
  3.1 0.0 collective-permute-done.1.value_beside
  3.1 2.7 %local.2 = (f32[96,768]{1,0:T(8,128)S(1)}, f32[96,128]{1,0:T(8,128)S(1)}, s32[4,4]{1,0:T(4,128)S(1)}) custom-call(s32[4,4]{1,0:T(4,128)} %visible.3, bf16[384,768]{1,0:T(8,128)(2,1)} %query.4, bf16[384,768]{1,0:T(8,128)(2,1)} %key.7, bf16[384,768]{1,0:T(8,128)(2,1)} %value.7, bf16[384,768]{1,0:T(8,128)(2,1)S(1)} %collective-permute-done.key_beside, ...), custom_call_target="tpu_custom_call" | custom-call | bytes 14760000 | tf_op jit(solution)/shard_map/local/pallas_call | solution.py:352
  5.9 2.3 %collective-permute-start.4 = (bf16[192,768]{1,0:T(8,128)(2,1)S(1)}, bf16[192,768]{1,0:T(8,128)(2,1)S(1)}, u32[]{:S(2)}, u32[]{:S(2)}) collective-permute-start(bf16[192,768]{1,0:T(8,128)(2,1)S(1)} %get-tuple-element.57), channel_id=1, source_target_pairs={{8,0},{12,4},{9,1},{13,5},{10,2},{14,6},{11,3},{15,7},{24,16},{28,... | collective-permute-start | bytes 884744 | tf_op jit(solution)/shard_map/ppermute | solution.py:32
  8.2 0.0 collective-permute-done.2.refs_0_
  8.3 1.3 %collective-permute-start.3 = (bf16[96,896]{1,0:T(8,128)(2,1)S(1)}, bf16[96,896]{1,0:T(8,128)(2,1)S(1)}, u32[]{:S(2)}, u32[]{:S(2)}) collective-permute-start(bf16[96,896]{1,0:T(8,128)(2,1)S(1)} %served.2), channel_id=1, source_target_pairs={{0,8},{4,12},{1,9},{5,13},{2,10},{6,14},{3,11},{7,15},{16,24},{20,... | collective-permute-start | bytes 516104 | tf_op jit(solution)/shard_map/ppermute | solution.py:32
  9.6 4.6 %collective-permute-start.5 = (bf16[96,768]{1,0:T(8,128)(2,1)S(1)}, bf16[96,768]{1,0:T(8,128)(2,1)S(1)}, u32[]{:S(2)}, u32[]{:S(2)}) collective-permute-start(bf16[96,768]{1,0:T(8,128)(2,1)S(1)} %get-tuple-element.58), channel_id=1, source_target_pairs={{8,0},{12,4},{9,1},{13,5},{10,2},{14,6},{11,3},{15,7},{24,16},{28,... | collective-permute-start | bytes 442376 | tf_op jit(solution)/shard_map/ppermute | solution.py:32
  14.1 2.4 %fetch.1.refs_3_ = bf16[4,768,768]{2,1,0:T(8,128)(2,1)S(1)} custom-call(bf16[768,6144]{1,0:T(8,128)(2,1)} %weight.8), custom_call_target="tpu_custom_call" | custom-call | bytes 8856000 | tf_op jit(solution)/shard_map/fetch/pallas_call | solution.py:400
  16.5 0.0 collective-permute-done.3.refs_2_
  16.6 1.3 %collective-permute-start.8 = (bf16[96,3072]{1,0:T(8,128)(2,1)S(1)}, bf16[96,3072]{1,0:T(8,128)(2,1)}, u32[]{:S(2)}, u32[]{:S(2)}) collective-permute-start(bf16[96,3072]{1,0:T(8,128)(2,1)S(1)} %opening.2), channel_id=1, source_target_pairs={{0,1},{3,2},{4,5},{7,6},{8,9},{11,10},{12,13},{15,14},{16,17},{19,... | collective-permute-start | bytes 1769480 | tf_op jit(solution)/shard_map/ppermute | solution.py:426
  17.9 0.0 collective-permute-done.5.refs_1_
  17.9 0.8 served.3
  18.7 1.3 %collective-permute-start.6 = (bf16[288,896]{1,0:T(8,128)(2,1)}, bf16[288,896]{1,0:T(8,128)(2,1)S(1)}, u32[]{:S(2)}, u32[]{:S(2)}) collective-permute-start(bf16[288,896]{1,0:T(8,128)(2,1)} %served.3), channel_id=1, source_target_pairs={{0,8},{4,12},{1,9},{5,13},{2,10},{6,14},{3,11},{7,15},{16,24},{20,... | collective-permute-start | bytes 1548296 | tf_op jit(solution)/shard_map/ppermute | solution.py:32
  20.0 0.1 pad_add_fusion.place
  20.1 1.3 %collective-permute-start.7 = (bf16[96,3072]{1,0:T(8,128)(2,1)S(1)}, bf16[96,3072]{1,0:T(8,128)(2,1)S(1)}, u32[]{:S(2)}, u32[]{:S(2)}) collective-permute-start(bf16[96,3072]{1,0:T(8,128)(2,1)S(1)} %opening.3), channel_id=1, source_target_pairs={{0,1},{3,2},{4,5},{7,6},{8,9},{11,10},{12,13},{15,14},{16,17},{19,... | collective-permute-start | bytes 1769480 | tf_op jit(solution)/shard_map/ppermute | solution.py:430
  21.4 3.7 %local.3 = (f32[288,768]{1,0:T(8,128)S(1)}, f32[288,128]{1,0:T(8,128)S(1)}, s32[4,4]{1,0:T(4,128)}) custom-call(s32[4,4]{1,0:T(4,128)} %visible.3, bf16[384,768]{1,0:T(8,128)(2,1)} %query.4, bf16[384,768]{1,0:T(8,128)(2,1)} %key.7, bf16[384,768]{1,0:T(8,128)(2,1)} %value.7, bf16[384,768]{1,0:T(8,128)(2,1)S(1)} %collective-permute-done.key_beside, ...), custom_call_target="tpu_custom_call" | custom-call | bytes 14760000 | tf_op jit(solution)/shard_map/local/pallas_call | solution.py:352
  25.1 11.3 %collective-permute-done.6.refs_5_ = bf16[288,896]{1,0:T(8,128)(2,1)S(1)} collective-permute-done((bf16[288,896]{1,0:T(8,128)(2,1)}, bf16[288,896]{1,0:T(8,128)(2,1)S(1)}, u32[]{:S(2)}, u32[]{:S(2)}) %collective-permute-start.6) | collective-permute-done | bytes 516128 | tf_op jit(solution)/shard_map/ppermute | solution.py:32
  36.4 4.3 %merged_blocks.1 = (bf16[384,768]{1,0:T(8,128)(2,1)S(1)}, bf16[96,3072]{1,0:T(8,128)(2,1)S(1)}, bf16[96,3072]{1,0:T(8,128)(2,1)S(1)}) custom-call(s32[2]{0:T(128)S(1)} %pad_add_fusion.place, f32[96,768]{1,0:T(8,128)S(1)} %get-tuple-element.50.refs_0_, f32[96,128]{1,0:T(8,128)S(1)} %get-tuple-element.51.refs_1_, ...), custom_call_target="tpu_custom_call" | custom-call | bytes 11070000 | tf_op jit(solution)/shard_map/merged_blocks/pallas_call | solution.py:436
  40.7 1.3 %fusion.1 = (bf16[96,3072]{1,0:T(8,128)(2,1)S(1)}, bf16[96,3072]{1,0:T(8,128)(2,1)S(1)}) fusion(bf16[96,3072]{1,0:T(8,128)(2,1)} %collective-permute-done.8, bf16[96,3072]{1,0:T(8,128)(2,1)S(1)} %get-tuple-element.71, bf16[96,3072]{1,0:T(8,128)(2,1)S(1)} %get-tuple-element.69), kind=kLoop, calls=%fused_computation.5 | loop fusion | flops 2064384 | bytes 2949120 | tf_op jit(solution)/shard_map/convert_element_type | solution.py:464
  42.0 3.5 %collective-permute-start.11 = (bf16[96,3072]{1,0:T(8,128)(2,1)S(1)}, bf16[96,3072]{1,0:T(8,128)(2,1)S(1)}, u32[]{:S(2)}, u32[]{:S(2)}) collective-permute-start(bf16[96,3072]{1,0:T(8,128)(2,1)S(1)} %get-tuple-element.98), channel_id=1, source_target_pairs={{0,1},{1,2},{4,5},{5,6},{8,9},{9,10},{12,13},{13,14},{16,17},{17,1... | collective-permute-start | bytes 1769480 | tf_op jit(solution)/shard_map/ppermute | solution.py:469
  45.5 1.3 %collective-permute-start.12 = (bf16[96,3072]{1,0:T(8,128)(2,1)S(1)}, bf16[96,3072]{1,0:T(8,128)(2,1)S(1)}, u32[]{:S(2)}, u32[]{:S(2)}) collective-permute-start(bf16[96,3072]{1,0:T(8,128)(2,1)S(1)} %get-tuple-element.97), channel_id=1, source_target_pairs={{3,2},{2,1},{7,6},{6,5},{11,10},{10,9},{15,14},{14,13},{19,18},{18... | collective-permute-start | bytes 1769480 | tf_op jit(solution)/shard_map/ppermute | solution.py:470
  46.8 3.3 %blocks.3 = (bf16[96,3072]{1,0:T(8,128)(2,1)S(1)}, bf16[96,3072]{1,0:T(8,128)(2,1)S(1)}) custom-call(s32[2]{0:T(128)S(1)} %pad_add_fusion.place, bf16[384,768]{1,0:T(8,128)(2,1)S(1)} %get-tuple-element.92.attended, bf16[768,6144]{1,0:T(8,128)(2,1)} %weight.8), custom_call_target="tpu_custom_call" | custom-call | bytes 11070000 | tf_op jit(solution)/shard_map/blocks/pallas_call | solution.py:446
  50.1 0.2 fusion.3
  50.3 1.3 %collective-permute-start.10 = (bf16[96,3072]{1,0:T(8,128)(2,1)S(1)}, bf16[96,3072]{1,0:T(8,128)(2,1)S(1)}, u32[]{:S(2)}, u32[]{:S(2)}) collective-permute-start(bf16[96,3072]{1,0:T(8,128)(2,1)S(1)} %get-tuple-element.95), channel_id=1, source_target_pairs={{3,2},{2,1},{7,6},{6,5},{11,10},{10,9},{15,14},{14,13},{19,18},{18... | collective-permute-start | bytes 1769480 | tf_op jit(solution)/shard_map/ppermute | solution.py:470
  51.6 5.2 %collective-permute-start.9 = (bf16[96,3072]{1,0:T(8,128)(2,1)S(1)}, bf16[96,3072]{1,0:T(8,128)(2,1)S(1)}, u32[]{:S(2)}, u32[]{:S(2)}) collective-permute-start(bf16[96,3072]{1,0:T(8,128)(2,1)S(1)} %get-tuple-element.96), channel_id=1, source_target_pairs={{0,1},{1,2},{4,5},{5,6},{8,9},{9,10},{12,13},{13,14},{16,17},{17,1... | collective-permute-start | bytes 1769480 | tf_op jit(solution)/shard_map/ppermute | solution.py:469
  56.8 3.4 %blocks.4 = (bf16[96,3072]{1,0:T(8,128)(2,1)S(1)}, bf16[96,3072]{1,0:T(8,128)(2,1)S(1)}) custom-call(s32[2]{0:T(128)S(1)} %pad_add_fusion.place, bf16[384,768]{1,0:T(8,128)(2,1)S(1)} %get-tuple-element.92.attended, bf16[768,6144]{1,0:T(8,128)(2,1)} %weight.8), custom_call_target="tpu_custom_call" | custom-call | bytes 11070000 | tf_op jit(solution)/shard_map/blocks/pallas_call | solution.py:446
  60.3 3.4 %collective-permute-done.12 = bf16[96,3072]{1,0:T(8,128)(2,1)S(1)} collective-permute-done((bf16[96,3072]{1,0:T(8,128)(2,1)S(1)}, bf16[96,3072]{1,0:T(8,128)(2,1)S(1)}, u32[]{:S(2)}, u32[]{:S(2)}) %collective-permute-start.12) | collective-permute-done | bytes 589856 | tf_op jit(solution)/shard_map/ppermute | solution.py:470
  63.6 0.2 add_convert_fusion.3
  63.8 1.9 %collective-permute-start.13 = (bf16[96,3072]{1,0:T(8,128)(2,1)S(1)}, bf16[96,3072]{1,0:T(8,128)(2,1)S(1)}, u32[]{:S(2)}, u32[]{:S(2)}) collective-permute-start(bf16[96,3072]{1,0:T(8,128)(2,1)S(1)} %add_convert_fusion.3), channel_id=1, source_target_pairs={{0,1},{1,2},{2,3},{4,5},{5,6},{6,7},{8,9},{9,10},{10,11},{12,13},{... | collective-permute-start | bytes 1769480 | tf_op jit(solution)/shard_map/ppermute | solution.py:469
  65.7 0.1 add_convert_fusion.2
  65.9 4.0 %collective-permute-start.14 = (bf16[96,3072]{1,0:T(8,128)(2,1)S(1)}, bf16[96,3072]{1,0:T(8,128)(2,1)S(1)}, u32[]{:S(2)}, u32[]{:S(2)}) collective-permute-start(bf16[96,3072]{1,0:T(8,128)(2,1)S(1)} %add_convert_fusion.2), channel_id=1, source_target_pairs={{3,2},{2,1},{1,0},{7,6},{6,5},{5,4},{11,10},{10,9},{9,8},{15,14},{... | collective-permute-start | bytes 1769480 | tf_op jit(solution)/shard_map/ppermute | solution.py:470
  69.9 3.4 %blocks.5 = (bf16[96,3072]{1,0:T(8,128)(2,1)S(1)}, bf16[96,3072]{1,0:T(8,128)(2,1)S(1)}) custom-call(s32[2]{0:T(128)S(1)} %pad_add_fusion.place, bf16[384,768]{1,0:T(8,128)(2,1)S(1)} %get-tuple-element.92.attended, bf16[768,6144]{1,0:T(8,128)(2,1)} %weight.8), custom_call_target="tpu_custom_call" | custom-call | bytes 11070000 | tf_op jit(solution)/shard_map/blocks/pallas_call | solution.py:446
  73.3 3.0 %collective-permute-done.10 = bf16[96,3072]{1,0:T(8,128)(2,1)S(1)} collective-permute-done((bf16[96,3072]{1,0:T(8,128)(2,1)S(1)}, bf16[96,3072]{1,0:T(8,128)(2,1)S(1)}, u32[]{:S(2)}, u32[]{:S(2)}) %collective-permute-start.10) | collective-permute-done | bytes 589856 | tf_op jit(solution)/shard_map/ppermute | solution.py:470
  76.3 0.1 add_convert_fusion
  76.4 0.0 copy-start.2
  76.5 1.9 %collective-permute-start.16 = (bf16[96,3072]{1,0:T(8,128)(2,1)S(1)}, bf16[96,3072]{1,0:T(8,128)(2,1)S(1)}, u32[]{:S(2)}, u32[]{:S(2)}) collective-permute-start(bf16[96,3072]{1,0:T(8,128)(2,1)S(1)} %add_convert_fusion), channel_id=1, source_target_pairs={{3,2},{2,1},{1,0},{7,6},{6,5},{5,4},{11,10},{10,9},{9,8},{15,14},{... | collective-permute-start | bytes 1769480 | tf_op jit(solution)/shard_map/ppermute | solution.py:470
  78.4 0.1 add_convert_fusion.1
  78.5 3.9 %collective-permute-start.15 = (bf16[96,3072]{1,0:T(8,128)(2,1)S(1)}, bf16[96,3072]{1,0:T(8,128)(2,1)S(1)}, u32[]{:S(2)}, u32[]{:S(2)}) collective-permute-start(bf16[96,3072]{1,0:T(8,128)(2,1)S(1)} %add_convert_fusion.1), channel_id=1, source_target_pairs={{0,1},{1,2},{2,3},{4,5},{5,6},{6,7},{8,9},{9,10},{10,11},{12,13},{... | collective-permute-start | bytes 1769480 | tf_op jit(solution)/shard_map/ppermute | solution.py:469
  82.5 5.0 %own.1 = (bf16[96,6144]{1,0:T(8,128)(2,1)S(1)}, f32[1,6144]{1,0:T(1,128)S(1)}) custom-call(s32[2]{0:T(128)S(1)} %pad_add_fusion.place, s32[4]{0:T(128)S(1)} %copy-done.2, bf16[384,768]{1,0:T(8,128)(2,1)S(1)} %get-tuple-element.92.attended, bf16[768,6144]{1,0:T(8,128)(2,1)} %weight.8, f32[64,6144]{1,0:T(8,128)} %gate_table.1), custom_call_target="tpu_custom_call" | custom-call | bytes 18450000 | tf_op jit(solution)/shard_map/own/pallas_call | solution.py:473
  87.5 1.4 %collective-permute-done.14 = bf16[96,3072]{1,0:T(8,128)(2,1)S(1)} collective-permute-done((bf16[96,3072]{1,0:T(8,128)(2,1)S(1)}, bf16[96,3072]{1,0:T(8,128)(2,1)S(1)}, u32[]{:S(2)}, u32[]{:S(2)}) %collective-permute-start.14) | collective-permute-done | bytes 589856 | tf_op jit(solution)/shard_map/ppermute | solution.py:470
  88.9 0.3 multiply_convert_fusion.done
  89.2 9.8 %collective-permute-done.16.down = bf16[96,3072]{1,0:T(8,128)(2,1)S(1)} collective-permute-done((bf16[96,3072]{1,0:T(8,128)(2,1)S(1)}, bf16[96,3072]{1,0:T(8,128)(2,1)S(1)}, u32[]{:S(2)}, u32[]{:S(2)}) %collective-permute-start.16) | collective-permute-done | bytes 589856 | tf_op jit(solution)/shard_map/ppermute | solution.py:470
  98.9 1.1 %final.1 = bf16[96,6144]{1,0:T(8,128)(2,1)} custom-call(bf16[96,3072]{1,0:T(8,128)(2,1)S(1)} %multiply_convert_fusion.done, bf16[96,6144]{1,0:T(8,128)(2,1)S(1)} %get-tuple-element.93.projected, f32[1,6144]{1,0:T(1,128)S(1)} %get-tuple-element.94.gate, bf16[96,3072]{1,0:T(8,128)(2,1)S(1)} %collective-permute-done.15.up, ...), custom_call_target="tpu_custom_call" | custom-call | bytes 9963000 | tf_op jit(solution)/shard_map/final/pallas_call | solution.py:494
  (15 shorter events, 0.1 us)
Async XLA Ops:
  0.0 3.1 %collective-permute-start = (bf16[384,768]{1,0:T(8,128)(2,1)}, bf16[384,768]{1,0:T(8,128)(2,1)S(1)}, u32[]{:S(2)}, u32[]{:S(2)}) collective-permute-start(bf16[384,768]{1,0:T(8,128)(2,1)} %key.7), channel_id=1, source_target_pairs={{0,4},{4,0},{8,12},{12,8},{1,5},{5,1},{9,13},{13,9},{2,6},{6,2},{1... | collective-permute-start | bytes 1769480 | tf_op jit(solution)/shard_map/ppermute | solution.py:344
  0.0 3.1 %collective-permute-start.1 = (bf16[384,768]{1,0:T(8,128)(2,1)}, bf16[384,768]{1,0:T(8,128)(2,1)S(1)}, u32[]{:S(2)}, u32[]{:S(2)}) collective-permute-start(bf16[384,768]{1,0:T(8,128)(2,1)} %value.7), channel_id=1, source_target_pairs={{0,4},{4,0},{8,12},{12,8},{1,5},{5,1},{9,13},{13,9},{2,6},{6,2},{1... | collective-permute-start | bytes 1769480 | tf_op jit(solution)/shard_map/ppermute | solution.py:345
  1.6 6.6 %copy-start = (bf16[384,768]{1,0:T(8,128)(2,1)S(1)}, bf16[384,768]{1,0:T(8,128)(2,1)}, u32[]{:S(2)}) copy-start(bf16[384,768]{1,0:T(8,128)(2,1)} %key.7) | copy-start | bytes 1769476
  1.6 6.6 %copy-start.1 = (bf16[384,768]{1,0:T(8,128)(2,1)S(1)}, bf16[384,768]{1,0:T(8,128)(2,1)}, u32[]{:S(2)}) copy-start(bf16[384,768]{1,0:T(8,128)(2,1)} %value.7) | copy-start | bytes 1769476
  1.6 6.6 %collective-permute-start.2 = (bf16[96,768]{1,0:T(8,128)(2,1)S(1)}, bf16[96,768]{1,0:T(8,128)(2,1)S(1)}, u32[]{:S(2)}, u32[]{:S(2)}) collective-permute-start(bf16[96,768]{1,0:T(8,128)(2,1)S(1)} %get-tuple-element.53), channel_id=1, source_target_pairs={{8,0},{12,4},{9,1},{13,5},{10,2},{14,6},{11,3},{15,7},{24,16},{28,... | collective-permute-start | bytes 442376 | tf_op jit(solution)/shard_map/ppermute | solution.py:32
  5.9 12.0 %collective-permute-start.4 = (bf16[192,768]{1,0:T(8,128)(2,1)S(1)}, bf16[192,768]{1,0:T(8,128)(2,1)S(1)}, u32[]{:S(2)}, u32[]{:S(2)}) collective-permute-start(bf16[192,768]{1,0:T(8,128)(2,1)S(1)} %get-tuple-element.57), channel_id=1, source_target_pairs={{8,0},{12,4},{9,1},{13,5},{10,2},{14,6},{11,3},{15,7},{24,16},{28,... | collective-permute-start | bytes 884744 | tf_op jit(solution)/shard_map/ppermute | solution.py:32
  8.3 8.3 %collective-permute-start.3 = (bf16[96,896]{1,0:T(8,128)(2,1)S(1)}, bf16[96,896]{1,0:T(8,128)(2,1)S(1)}, u32[]{:S(2)}, u32[]{:S(2)}) collective-permute-start(bf16[96,896]{1,0:T(8,128)(2,1)S(1)} %served.2), channel_id=1, source_target_pairs={{0,8},{4,12},{1,9},{5,13},{2,10},{6,14},{3,11},{7,15},{16,24},{20,... | collective-permute-start | bytes 516104 | tf_op jit(solution)/shard_map/ppermute | solution.py:32
  9.6 8.3 %collective-permute-start.5 = (bf16[96,768]{1,0:T(8,128)(2,1)S(1)}, bf16[96,768]{1,0:T(8,128)(2,1)S(1)}, u32[]{:S(2)}, u32[]{:S(2)}) collective-permute-start(bf16[96,768]{1,0:T(8,128)(2,1)S(1)} %get-tuple-element.58), channel_id=1, source_target_pairs={{8,0},{12,4},{9,1},{13,5},{10,2},{14,6},{11,3},{15,7},{24,16},{28,... | collective-permute-start | bytes 442376 | tf_op jit(solution)/shard_map/ppermute | solution.py:32
  16.6 24.1 %collective-permute-start.8 = (bf16[96,3072]{1,0:T(8,128)(2,1)S(1)}, bf16[96,3072]{1,0:T(8,128)(2,1)}, u32[]{:S(2)}, u32[]{:S(2)}) collective-permute-start(bf16[96,3072]{1,0:T(8,128)(2,1)S(1)} %opening.2), channel_id=1, source_target_pairs={{0,1},{3,2},{4,5},{7,6},{8,9},{11,10},{12,13},{15,14},{16,17},{19,... | collective-permute-start | bytes 1769480 | tf_op jit(solution)/shard_map/ppermute | solution.py:426
  18.7 17.7 %collective-permute-start.6 = (bf16[288,896]{1,0:T(8,128)(2,1)}, bf16[288,896]{1,0:T(8,128)(2,1)S(1)}, u32[]{:S(2)}, u32[]{:S(2)}) collective-permute-start(bf16[288,896]{1,0:T(8,128)(2,1)} %served.3), channel_id=1, source_target_pairs={{0,8},{4,12},{1,9},{5,13},{2,10},{6,14},{3,11},{7,15},{16,24},{20,... | collective-permute-start | bytes 1548296 | tf_op jit(solution)/shard_map/ppermute | solution.py:32
  20.1 30.0 %collective-permute-start.7 = (bf16[96,3072]{1,0:T(8,128)(2,1)S(1)}, bf16[96,3072]{1,0:T(8,128)(2,1)S(1)}, u32[]{:S(2)}, u32[]{:S(2)}) collective-permute-start(bf16[96,3072]{1,0:T(8,128)(2,1)S(1)} %opening.3), channel_id=1, source_target_pairs={{0,1},{3,2},{4,5},{7,6},{8,9},{11,10},{12,13},{15,14},{16,17},{19,... | collective-permute-start | bytes 1769480 | tf_op jit(solution)/shard_map/ppermute | solution.py:430
  42.0 18.3 %collective-permute-start.11 = (bf16[96,3072]{1,0:T(8,128)(2,1)S(1)}, bf16[96,3072]{1,0:T(8,128)(2,1)S(1)}, u32[]{:S(2)}, u32[]{:S(2)}) collective-permute-start(bf16[96,3072]{1,0:T(8,128)(2,1)S(1)} %get-tuple-element.98), channel_id=1, source_target_pairs={{0,1},{1,2},{4,5},{5,6},{8,9},{9,10},{12,13},{13,14},{16,17},{17,1... | collective-permute-start | bytes 1769480 | tf_op jit(solution)/shard_map/ppermute | solution.py:469
  45.5 18.2 %collective-permute-start.12 = (bf16[96,3072]{1,0:T(8,128)(2,1)S(1)}, bf16[96,3072]{1,0:T(8,128)(2,1)S(1)}, u32[]{:S(2)}, u32[]{:S(2)}) collective-permute-start(bf16[96,3072]{1,0:T(8,128)(2,1)S(1)} %get-tuple-element.97), channel_id=1, source_target_pairs={{3,2},{2,1},{7,6},{6,5},{11,10},{10,9},{15,14},{14,13},{19,18},{18... | collective-permute-start | bytes 1769480 | tf_op jit(solution)/shard_map/ppermute | solution.py:470
  50.3 26.0 %collective-permute-start.10 = (bf16[96,3072]{1,0:T(8,128)(2,1)S(1)}, bf16[96,3072]{1,0:T(8,128)(2,1)S(1)}, u32[]{:S(2)}, u32[]{:S(2)}) collective-permute-start(bf16[96,3072]{1,0:T(8,128)(2,1)S(1)} %get-tuple-element.95), channel_id=1, source_target_pairs={{3,2},{2,1},{7,6},{6,5},{11,10},{10,9},{15,14},{14,13},{19,18},{18... | collective-permute-start | bytes 1769480 | tf_op jit(solution)/shard_map/ppermute | solution.py:470
  51.6 24.7 %collective-permute-start.9 = (bf16[96,3072]{1,0:T(8,128)(2,1)S(1)}, bf16[96,3072]{1,0:T(8,128)(2,1)S(1)}, u32[]{:S(2)}, u32[]{:S(2)}) collective-permute-start(bf16[96,3072]{1,0:T(8,128)(2,1)S(1)} %get-tuple-element.96), channel_id=1, source_target_pairs={{0,1},{1,2},{4,5},{5,6},{8,9},{9,10},{12,13},{13,14},{16,17},{17,1... | collective-permute-start | bytes 1769480 | tf_op jit(solution)/shard_map/ppermute | solution.py:469
  63.8 23.7 %collective-permute-start.13 = (bf16[96,3072]{1,0:T(8,128)(2,1)S(1)}, bf16[96,3072]{1,0:T(8,128)(2,1)S(1)}, u32[]{:S(2)}, u32[]{:S(2)}) collective-permute-start(bf16[96,3072]{1,0:T(8,128)(2,1)S(1)} %add_convert_fusion.3), channel_id=1, source_target_pairs={{0,1},{1,2},{2,3},{4,5},{5,6},{6,7},{8,9},{9,10},{10,11},{12,13},{... | collective-permute-start | bytes 1769480 | tf_op jit(solution)/shard_map/ppermute | solution.py:469
  65.9 23.0 %collective-permute-start.14 = (bf16[96,3072]{1,0:T(8,128)(2,1)S(1)}, bf16[96,3072]{1,0:T(8,128)(2,1)S(1)}, u32[]{:S(2)}, u32[]{:S(2)}) collective-permute-start(bf16[96,3072]{1,0:T(8,128)(2,1)S(1)} %add_convert_fusion.2), channel_id=1, source_target_pairs={{3,2},{2,1},{1,0},{7,6},{6,5},{5,4},{11,10},{10,9},{9,8},{15,14},{... | collective-permute-start | bytes 1769480 | tf_op jit(solution)/shard_map/ppermute | solution.py:470
  76.4 6.0 %copy-start.2 = (s32[4]{0:T(128)S(1)}, s32[4]{0:T(128)}, u32[]{:S(2)}) copy-start(s32[4]{0:T(128)} %levels.1) | copy-start | bytes 52
  76.5 22.5 %collective-permute-start.16 = (bf16[96,3072]{1,0:T(8,128)(2,1)S(1)}, bf16[96,3072]{1,0:T(8,128)(2,1)S(1)}, u32[]{:S(2)}, u32[]{:S(2)}) collective-permute-start(bf16[96,3072]{1,0:T(8,128)(2,1)S(1)} %add_convert_fusion), channel_id=1, source_target_pairs={{3,2},{2,1},{1,0},{7,6},{6,5},{5,4},{11,10},{10,9},{9,8},{15,14},{... | collective-permute-start | bytes 1769480 | tf_op jit(solution)/shard_map/ppermute | solution.py:470
  78.5 20.4 %collective-permute-start.15 = (bf16[96,3072]{1,0:T(8,128)(2,1)S(1)}, bf16[96,3072]{1,0:T(8,128)(2,1)S(1)}, u32[]{:S(2)}, u32[]{:S(2)}) collective-permute-start(bf16[96,3072]{1,0:T(8,128)(2,1)S(1)} %add_convert_fusion.1), channel_id=1, source_target_pairs={{0,1},{1,2},{2,3},{4,5},{5,6},{6,7},{8,9},{9,10},{10,11},{12,13},{... | collective-permute-start | bytes 1769480 | tf_op jit(solution)/shard_map/ppermute | solution.py:469
